TPU v7x, 32 devices: a whole 2x2x4 slice. The times are simulated.
32 devices in a mesh: role: 4 (over y, x), pairs: 8 (over z, core).
Axes of the slice: x: 2, y: 2, z: 4, core: 2. Of those that a mesh axis runs over, the one named last changes fastest.
Arguments:
- three_index: bfloat16 [16, 1024, 512], P('pairs'), may hold values from -6 to 6
- coeff: bfloat16 [32, 512, 256], P('pairs'), may hold values from -6 to 6
- amps: bfloat16 [32, 256, 256], P('pairs'), may hold values from -4 to 4
- eps_virt: float32 [32, 256], P('pairs'), may hold values from 0.3 to 3
- eps_occ: float32 [16], replicated, may hold values from -1.5 to -0.3
- nvirt: int32 [32], P('pairs'), may hold values from 64 to 256, as said below
- pair_occ: int32 [32, 2], P('pairs'), may hold values from 0 to 15, as said below
- partners: int32 [32, 8], P('pairs'), may hold values from 0 to 31, as said below
- coupling: float32 [32, 8], P('pairs'), may hold values from -1 to 1
- pair_owner: int32 [32], P('pairs'), may hold values from 1 to 3, as said below
Outputs:
- amps_out: bfloat16 [64, 256, 256], P(('role', 'pairs'))
- dressed_out: bfloat16 [64, 512, 256], P(('role', 'pairs'))
Inputs may be any that keep to these rules, and one draw needn't show every extreme that they name: `nvirt`: each block of 4 consecutive pairs has one pair with all 256 virtuals. `pair_occ`: for pair k in block c = k // 4, the first orbital is one of the 2 orbitals numbered from 2 * c, and the second is one of the 6 orbitals numbered cyclically from 2 * (c - 1) modulo 16. Pair k's partners are distinct pairs of its own block of 4 pairs and the blocks just before and after it, cyclically modulo 32. `pair_owner`: in each block of 4 consecutive pairs, each of the roles 1 to 3 holds one or two pairs and exactly one role holds two.
All inputs are finite; a program needn't handle non-finite values.
Results may differ from a plain program's by a relative error of at most 0.012.
Values may be sent and summed in bfloat16 or wider, within the bound.
No kernel may reach another device: no remote copies, remote signals or barrier semaphores. Data moves between devices by JAX's collectives and lax.ppermute only.
A program may use at most 64 MiB of HBM per device.

v0:
```python
import math

import jax
import jax.numpy as jnp
from jax import lax
from jax.sharding import PartitionSpec as P

PARTNERS = 8
ITERS = 2
SLOTS = 2


def extended(cells, sides, width):
    for axis, dim in sides:
        count = lax.axis_size(axis)
        head = lax.slice_in_dim(cells, 0, width, axis=dim)
        tail = lax.slice_in_dim(cells, cells.shape[dim] - width, cells.shape[dim], axis=dim)
        cells = jnp.concatenate(
            [
                lax.ppermute(tail, axis, [(i, (i + 1) % count) for i in range(count)]),
                cells,
                lax.ppermute(head, axis, [((i + 1) % count, i) for i in range(count)]),
            ],
            axis=dim,
        )
    return cells


def local(
    three_index, coeff, amps, eps_virt, eps_occ, nvirt, pair_occ, partners, coupling, pair_owner
):
    column_count = lax.axis_size("pairs")
    role_index = lax.axis_index("role")
    column = lax.axis_index("pairs")
    occ_block = three_index.shape[0]
    width_aux = three_index.shape[1]
    pair_block = coeff.shape[0]
    width_pao = coeff.shape[1]
    width_virt = coeff.shape[2]
    slot_count = SLOTS
    pao_scale = 1.0 / math.sqrt(width_pao)
    aux_scale = 1.0 / math.sqrt(width_aux)
    virt_scale = 1.0 / math.sqrt(width_virt)
    occ_local = jnp.mod(pair_occ - (column - 1) * occ_block, occ_block * column_count)
    partner_local = jnp.mod(partners - (column - 1) * pair_block, pair_block * column_count)
    positions = jnp.arange(pair_block, dtype=jnp.int32)
    same_owner = (pair_owner[:, None] == pair_owner[None, :]).astype(jnp.int32)
    earlier = (positions[None, :] < positions[:, None]).astype(jnp.int32)
    pair_ranks = jnp.sum(same_owner * earlier, axis=1)
    gathered_at = pair_owner * slot_count + pair_ranks
    owned_here = pair_owner == role_index
    slot_ids = jnp.arange(slot_count, dtype=jnp.int32)
    slot_hits = (owned_here[None, :] & (pair_ranks[None, :] == slot_ids[:, None])).astype(jnp.int32)
    slot_pair = jnp.sum(slot_hits * positions[None, :], axis=1)
    slot_valid = (jnp.sum(slot_hits, axis=1) > 0).astype(jnp.float32)
    virtuals = jnp.arange(width_virt, dtype=jnp.int32)
    blocks = extended(three_index, (("pairs", 0),), occ_block)

    def transform_rows(orbitals_all, first_ids, second_ids):

        def one_pair(packed):
            orbitals, first_at, second_at = packed
            first_half = (
                jnp.dot(blocks[first_at], orbitals, preferred_element_type=jnp.float32) * pao_scale
            ).astype(jnp.bfloat16)
            second_half = (
                jnp.dot(blocks[second_at], orbitals, preferred_element_type=jnp.float32) * pao_scale
            ).astype(jnp.bfloat16)
            return (
                jnp.einsum("qa,qb->ab", first_half, second_half, preferred_element_type=jnp.float32)
                * aux_scale
            )

        return lax.map(one_pair, (orbitals_all, first_ids, second_ids))

    near_orbitals = extended(coeff, (("pairs", 0),), pair_block)

    def slot_intersections():

        def slot_one_slot(slot_at):
            pair_at = slot_pair[slot_at]
            partner_orb = near_orbitals[partner_local[pair_at]]
            return (
                jnp.einsum(
                    "mb,kmc->kbc", coeff[pair_at], partner_orb, preferred_element_type=jnp.float32
                )
                * (1.0 / width_pao)
            ).astype(jnp.bfloat16)

        return lax.map(slot_one_slot, slot_ids)

    intersections = lax.cond(
        role_index > 0,
        slot_intersections,
        lambda: jnp.zeros((slot_count, PARTNERS, width_virt, width_virt), jnp.bfloat16),
    )

    def refresh(slot_ints, amp_pairs, near_amps):

        def refresh_one_slot(slot_at):
            pair_at = slot_pair[slot_at]
            intersection = intersections[slot_at]
            partner_amp = near_amps[partner_local[pair_at]]
            middle = jnp.einsum(
                "kbc,kcd->kbd", intersection, partner_amp, preferred_element_type=jnp.float32
            ).astype(jnp.bfloat16)
            partner_terms = jnp.einsum(
                "kbd,ked->kbe", middle, intersection, preferred_element_type=jnp.float32
            )
            coupled = jnp.sum(coupling[pair_at][:, None, None] * partner_terms, axis=0)
            occ_shift = eps_occ[pair_occ[pair_at, 0]] + eps_occ[pair_occ[pair_at, 1]]
            energy = eps_virt[pair_at][:, None] + eps_virt[pair_at][None, :] - occ_shift
            own_amp = amp_pairs[pair_at].astype(jnp.float32)
            fresh_amp = own_amp - (
                slot_ints[slot_at].astype(jnp.float32) + energy * own_amp + coupled
            ) / (energy + 1.0)
            keep_rows = (virtuals < nvirt[pair_at]).astype(jnp.float32) * slot_valid[slot_at]
            fresh_amp = (fresh_amp * keep_rows[:, None] * keep_rows[None, :]).astype(jnp.bfloat16)
            dressed = (
                (
                    coeff[pair_at].astype(jnp.float32)
                    + jnp.dot(coeff[pair_at], fresh_amp, preferred_element_type=jnp.float32)
                    * virt_scale
                )
                * slot_valid[slot_at]
            ).astype(jnp.bfloat16)
            return (fresh_amp, dressed)

        return lax.map(refresh_one_slot, slot_ids)

    zero_amp = jnp.zeros((slot_count, width_virt, width_virt), jnp.bfloat16)
    zero_orb = jnp.zeros((slot_count, width_pao, width_virt), jnp.bfloat16)
    amp_pairs = amps
    slot_amps = zero_amp
    slot_orbs = jnp.take(coeff, slot_pair, axis=0)
    for iteration in range(ITERS):
        slot_orbs_now = slot_orbs
        slot_occ = jnp.take(occ_local, slot_pair, axis=0)
        slot_ints = lax.cond(
            role_index > 0,
            lambda: transform_rows(slot_orbs_now, slot_occ[:, 0], slot_occ[:, 1]).astype(
                jnp.bfloat16
            ),
            lambda: jnp.zeros((slot_count, width_virt, width_virt), jnp.bfloat16),
        )
        near_amps = extended(amp_pairs, (("pairs", 0),), pair_block)
        slot_amps, slot_orbs = lax.cond(
            role_index > 0,
            lambda: refresh(slot_ints, amp_pairs, near_amps),
            lambda: (zero_amp, zero_orb),
        )
        if iteration + 1 < ITERS:
            every_amp = lax.all_gather(slot_amps, "role", axis=0, tiled=True)
            amp_pairs = jnp.take(every_amp, gathered_at, axis=0)
    return (slot_amps, slot_orbs)


def solution(mesh):
    in_specs = (
        P("pairs", None, None),
        P("pairs", None, None),
        P("pairs", None, None),
        P("pairs", None),
        P(),
        P("pairs"),
        P("pairs", None),
        P("pairs", None),
        P("pairs", None),
        P("pairs"),
    )
    out_specs = (P(("role", "pairs"), None, None), P(("role", "pairs"), None, None))
    return jax.shard_map(local, mesh=mesh, in_specs=in_specs, out_specs=out_specs, check_vma=False)
```

profile of v0, /device:TPU:2, one launch (start us, length us, event | category | flops | bytes accessed | tf_op | source)
XLA Modules:
  0.0 293.4 jit_solution(3364630825413588847)
XLA Ops:
  7.3 3.5 %collective-permute-start.1 = (bf16[2,1024,512]{2,1,0:T(8,128)(2,1)}, bf16[2,1024,512]{2,1,0:T(8,128)(2,1)}, u32[]{:S(2)}, u32[]{:S(2)}) collective-permute-start(bf16[2,1024,512]{2,1,0:T(8,128)(2,1)} %param.32), channel_id=1, source_target_pairs={{1,0},{2,1},{3,2},{4,3},{5,4},{6,5},{7,6},{0,7},{9,8},{10,9},{11,1... | collective-permute-start | bytes 6291464 | tf_op jit(solution)/shard_map/ppermute | solution.py:22
  10.8 3.5 %collective-permute-start.3 = (bf16[4,512,256]{2,1,0:T(8,128)(2,1)}, bf16[4,512,256]{2,1,0:T(8,128)(2,1)}, u32[]{:S(2)}, u32[]{:S(2)}) collective-permute-start(bf16[4,512,256]{2,1,0:T(8,128)(2,1)} %param.33), channel_id=1, source_target_pairs={{1,0},{2,1},{3,2},{4,3},{5,4},{6,5},{7,6},{0,7},{9,8},{10,9},{11,1... | collective-permute-start | bytes 3145736 | tf_op jit(solution)/shard_map/ppermute | solution.py:22
  14.4 0.9 select_reduce_fusion
  15.3 0.7 compare_and_fusion.2
  16.1 0.8 copy.29
  16.9 68.4 %collective-permute-done.4 = bf16[4,256,256]{2,1,0:T(8,128)(2,1)S(1)} collective-permute-done((bf16[4,256,256]{2,1,0:T(8,128)(2,1)}, bf16[4,256,256]{2,1,0:T(8,128)(2,1)S(1)}, u32[]{:S(2)}, u32[]{:S(2)}) %collective-permute-start.4) | collective-permute-done | bytes 524320 | tf_op jit(solution)/shard_map/ppermute | solution.py:20
  85.9 0.7 add_select_fusion
  86.6 5.7 %collective-permute-done.5 = bf16[4,256,256]{2,1,0:T(8,128)(2,1)S(1)} collective-permute-done((bf16[4,256,256]{2,1,0:T(8,128)(2,1)}, bf16[4,256,256]{2,1,0:T(8,128)(2,1)S(1)}, u32[]{:S(2)}, u32[]{:S(2)}) %collective-permute-start.5) | collective-permute-done | bytes 524320 | tf_op jit(solution)/shard_map/ppermute | solution.py:22
  92.3 2.4 pad_maximum_fusion.1
  94.7 1.0 copy-done.2
  95.7 2.0 pad_maximum_fusion
  97.7 21.0 %conditional.6 = (bf16[2,8,256,256]{2,3,1,0:T(8,128)(2,1)}) conditional(s32[]{:T(128)} %convert_element_type.97, () %tuple.73, (s32[2]{0:T(128)S(1)}, s32[2]{0:T(128)S(1)}, s32[4,8]{1,0:T(4,128)S(1)}, bf16[12,512,256]{2,1,0:T(8,128)(2,1)S(1)}, bf16[4,512,256]{2,1,0:T(8,128)(2,1)}) %tuple.74), branch_computations={%region_2.3_spmd, %region_3.6_spmd} | conditional | flops 537920512 | bytes 7607225 | solution.py:92
  97.8 21.0 %while.55 = (s32[]{:T(128)}, bf16[2,8,256,256]{2,3,1,0:T(8,128)(2,1)}, s32[2]{0:T(128)S(1)}, s32[2]{0:T(128)S(1)}, s32[4,8]{1,0:T(4,128)S(1)}, /*index=5*/bf16[1...) while((s32[]{:T(128)}, ...), condition=%wide.region_5.5_spmd, body=%wide.region_4.4_spmd.sunk | while | flops 537920512 | bytes 7607121 | solution.py:90
  102.9 2.0 gather_fusion.2
  104.9 3.4 %fusion.176 = bf16[2,8,256,256]{2,3,1,0:T(8,128)(2,1)} fusion(bf16[2,8,256,256]{2,3,1,0:T(8,128)(2,1)} %get-tuple-element.1294, s32[]{:T(128)} %get-tuple-element.1293, bf16[8,512,256]{2,1,0:T(8,128)(2,1)} %gather_fusion.2, bf16[4,512,256]{2,1,0:T(8,128)(2,1)} %get-tuple-element.1310, s32[]{:T(128)S(6)} %select_n.212), kind=kOutput, calls=%fused_computation.50.clone.1 | convolution fusion | flops 537919488 | bytes 3408388 | tf_op jit(solution)/shard_map/cond/branch_1_fun/while/body/eval_jaxpr/mb,kmc->kbc/dot_general | solution.py:84
  113.4 2.0 gather_fusion.2
  115.4 3.3 %fusion.176 = bf16[2,8,256,256]{2,3,1,0:T(8,128)(2,1)} fusion(bf16[2,8,256,256]{2,3,1,0:T(8,128)(2,1)} %get-tuple-element.1294, s32[]{:T(128)} %get-tuple-element.1293, bf16[8,512,256]{2,1,0:T(8,128)(2,1)} %gather_fusion.2, bf16[4,512,256]{2,1,0:T(8,128)(2,1)} %get-tuple-element.1310, s32[]{:T(128)S(6)} %select_n.212), kind=kOutput, calls=%fused_computation.50.clone.1 | convolution fusion | flops 537919488 | bytes 3408388 | tf_op jit(solution)/shard_map/cond/branch_1_fun/while/body/eval_jaxpr/mb,kmc->kbc/dot_general | solution.py:84
  118.7 1.9 constant_dynamic-update-slice_fusion.4
  121.1 1.7 constant_dynamic-update-slice_fusion.2
  122.9 2.7 copy-done.3
  125.6 22.4 %conditional.5 = (bf16[2,256,256]{2,1,0:T(8,128)(2,1)}) conditional(s32[]{:T(128)} %convert_element_type.97, () %tuple.71, (s32[2]{0:T(128)S(1)}, s32[2]{0:T(128)S(1)}, bf16[4,512,256]{2,1,0:T(8,128)(2,1)}, s32[2,2]{1,0:T(2,128)S(1)}, bf16[6,1024,512]{2,1,0:T(8,128)(2,1)S(1)}) %tuple.72), branch_computations={%region_6.8_spmd, %region_7.11_spmd} | conditional | flops 672465920 | bytes 31201192 | solution.py:139
  125.6 2.6 copy-done.4
  128.2 1.8 gather_fusion.3
  130.3 17.7 %while.56 = (s32[]{:T(128)}, bf16[2,256,256]{2,1,0:T(8,128)(2,1)}, s32[2]{0:T(128)S(1)}, bf16[6,1024,512]{2,1,0:T(8,128)(2,1)}, bf16[2,512,256]{2,1,0:T(8,128)(2...) while((s32[]{:T(128)}, bf16[2,256,256]{2,1,0:T(8,128)(2,1)}, s32[2]{0:T(128)S(1)}, ...), condition=%wide.region_9.10_spmd, body=%wide.region_8.9_spmd.sunk | while | flops 672202752 | bytes 3933889 | solution.py:74
  132.6 1.7 fusion.182
  136.5 2.6 fusion.183
  141.4 1.7 fusion.182
  145.3 2.6 fusion.183
  148.0 43.4 %conditional.7 = (bf16[2,256,256]{2,1,0:T(8,128)(2,1)}, bf16[2,512,256]{2,1,0:T(8,128)(2,1)}) conditional(s32[]{:T(128)} %convert_element_type.97, () %tuple.70, (s32[2]{0:T(128)S(1)}, s32[2]{0:T(128)S(1)}, bf16[4,256,256]{2,1,0:T(8,128)(2,1)}, bf16[2,256,256]{2,1,0:T(8,128)(2,1)}, f32[4,256]{1,0:T(4,128)S(1)}, /*index=5*/s32[4,2]{0,1:T(2,128)S(1)}, ...), branch_computations={%region_11.13_spmd, %region_12.17_spmd} | conditional | flops 606995968 | bytes 7226249 | solution.py:147
  148.1 43.4 %while.58 = (s32[]{:T(128)}, bf16[2,256,256]{2,1,0:T(8,128)(2,1)}, bf16[2,512,256]{2,1,0:T(8,128)(2,1)}, s32[2]{0:T(128)S(1)}, s32[2]{0:T(128)S(1)}, /*index=5*/...) while((s32[]{:T(128)}, bf16[2,256,256]{2,1,0:T(8,128)(2,1)}, ...), condition=%wide.region_15.16_spmd, body=%wide.region_13.15_spmd.sunk | while | flops 606995968 | bytes 7226041 | solution.py:129
  153.7 2.4 multiply_reduce_fusion.5
  156.1 0.7 constant_dynamic-slice_fusion.17
  160.7 0.7 fusion.171
  163.3 0.7 dynamic_slice.322
  164.0 1.3 compare_select_fusion.13
  165.3 1.8 constant_dynamic-update-slice_fusion.8
  167.2 2.7 fusion.172
  175.4 2.3 multiply_reduce_fusion.5
  177.7 0.7 constant_dynamic-slice_fusion.17
  182.3 0.7 fusion.171
  185.0 0.7 dynamic_slice.322
  185.6 1.3 compare_select_fusion.13
  187.0 1.9 constant_dynamic-update-slice_fusion.8
  188.8 2.7 fusion.172
  191.5 28.0 %all-gather.2.cloned.1.call-done = bf16[8,256,256]{2,1,0:T(8,128)(2,1)} async-done(((bf16[2,256,256]{2,1,0:T(8,128)(2,1)}), bf16[8,256,256]{2,1,0:T(8,128)(2,1)}) %all-gather.2.cloned.1.call-update) | async-done | bytes 1048592 | tf_op jit(solution)/shard_map/all_gather | solution.py:153
  219.5 1.8 gather_fusion.4
  221.5 3.5 %collective-permute-start.7 = (bf16[4,256,256]{2,1,0:T(8,128)(2,1)S(1)}, bf16[4,256,256]{2,1,0:T(8,128)(2,1)S(1)}, u32[]{:S(2)}, u32[]{:S(2)}) collective-permute-start(bf16[4,256,256]{2,1,0:T(8,128)(2,1)S(1)} %broadcast_select_fusion.1), channel_id=1, source_target_pairs={{1,0},{2,1},{3,2},{4,3},{5,4},{6,5},{7,6},{0,7},{9,8},{10,9},{11,1... | collective-permute-start | bytes 1572872 | tf_op jit(solution)/shard_map/ppermute | solution.py:22
  225.1 18.7 %conditional.8 = (bf16[2,256,256]{2,1,0:T(8,128)(2,1)}) conditional(s32[]{:T(128)} %convert_element_type.97, () %tuple.76, (s32[2,2]{1,0:T(2,128)S(1)}, bf16[6,1024,512]{2,1,0:T(8,128)(2,1)}, bf16[2,512,256]{2,1,0:T(8,128)(2,1)}) %tuple.186), branch_computations={%region_16.18_spmd, %region_17.21_spmd} | conditional | flops 672202752 | bytes 3934041 | solution.py:139
  225.2 18.5 %while.57 = (s32[]{:T(128)}, bf16[2,256,256]{2,1,0:T(8,128)(2,1)}, s32[2]{0:T(128)S(1)}, bf16[6,1024,512]{2,1,0:T(8,128)(2,1)}, bf16[2,512,256]{2,1,0:T(8,128)(2...) while((s32[]{:T(128)}, bf16[2,256,256]{2,1,0:T(8,128)(2,1)}, s32[2]{0:T(128)S(1)}, ...), condition=%wide.region_19.20_spmd, body=%wide.region_18.19_spmd.sunk | while | flops 672202752 | bytes 3933889 | solution.py:74
  227.6 1.7 fusion.162
  231.8 2.7 fusion.163
  236.9 1.7 fusion.162
  241.0 2.7 fusion.163
  243.9 42.7 %conditional.9 = (bf16[2,256,256]{2,1,0:T(8,128)(2,1)}, bf16[2,512,256]{2,1,0:T(8,128)(2,1)}) conditional(s32[]{:T(128)} %convert_element_type.97, () %tuple.69, (s32[2]{0:T(128)S(1)}, s32[2]{0:T(128)S(1)}, bf16[4,256,256]{2,1,0:T(8,128)(2,1)S(1)}, bf16[2,256,256]{2,1,0:T(8,128)(2,1)}, f32[4,256]{1,0:T(4,128)S(1)}, ...), branch_computations={%region_20.22_spmd, %region_21.26_spmd} | conditional | flops 606995968 | bytes 7226249 | solution.py:147
  244.0 42.6 %while.59 = (s32[]{:T(128)}, bf16[2,256,256]{2,1,0:T(8,128)(2,1)}, bf16[2,512,256]{2,1,0:T(8,128)(2,1)}, s32[2]{0:T(128)S(1)}, s32[2]{0:T(128)S(1)}, /*index=5*/...) while((s32[]{:T(128)}, bf16[2,256,256]{2,1,0:T(8,128)(2,1)}, ...), condition=%wide.region_24.25_spmd, body=%wide.region_22.24_spmd.sunk | while | flops 606995968 | bytes 7226041 | solution.py:129
  249.5 2.4 multiply_reduce_fusion.4
  256.3 0.7 fusion.155
  259.6 1.3 compare_select_fusion.12
  260.9 1.8 constant_dynamic-update-slice_fusion.7
  262.7 2.6 fusion.156
  270.9 2.3 multiply_reduce_fusion.4
  280.9 1.3 compare_select_fusion.12
  282.2 1.8 constant_dynamic-update-slice_fusion.7
  284.0 2.6 fusion.156
  (116 shorter events, 22.7 us)
Async XLA Ops:
  7.2 212.4 %all-gather.2.cloned.1.call-start = ((), (), s32[]{:S(2)}) async-start(), calls=%async_computation | async-start | bytes 1310720 | tf_op jit(solution)/shard_map/all_gather | solution.py:153
  7.2 111.5 %collective-permute-start = (bf16[2,1024,512]{2,1,0:T(8,128)(2,1)}, bf16[2,1024,512]{2,1,0:T(8,128)(2,1)}, u32[]{:S(2)}, u32[]{:S(2)}) collective-permute-start(bf16[2,1024,512]{2,1,0:T(8,128)(2,1)} %param.32), channel_id=1, source_target_pairs={{0,1},{1,2},{2,3},{3,4},{4,5},{5,6},{6,7},{7,0},{8,9},{9,10},{10,1... | collective-permute-start | bytes 6291464 | tf_op jit(solution)/shard_map/ppermute | solution.py:20
  7.3 113.8 %collective-permute-start.1 = (bf16[2,1024,512]{2,1,0:T(8,128)(2,1)}, bf16[2,1024,512]{2,1,0:T(8,128)(2,1)}, u32[]{:S(2)}, u32[]{:S(2)}) collective-permute-start(bf16[2,1024,512]{2,1,0:T(8,128)(2,1)} %param.32), channel_id=1, source_target_pairs={{1,0},{2,1},{3,2},{4,3},{5,4},{6,5},{7,6},{0,7},{9,8},{10,9},{11,1... | collective-permute-start | bytes 6291464 | tf_op jit(solution)/shard_map/ppermute | solution.py:22
  10.8 83.9 %collective-permute-start.2 = (bf16[4,512,256]{2,1,0:T(8,128)(2,1)}, bf16[4,512,256]{2,1,0:T(8,128)(2,1)S(1)}, u32[]{:S(2)}, u32[]{:S(2)}) collective-permute-start(bf16[4,512,256]{2,1,0:T(8,128)(2,1)} %param.33), channel_id=1, source_target_pairs={{0,1},{1,2},{2,3},{3,4},{4,5},{5,6},{6,7},{7,0},{8,9},{9,10},{10,1... | collective-permute-start | bytes 3145736 | tf_op jit(solution)/shard_map/ppermute | solution.py:20
  10.8 84.9 %collective-permute-start.3 = (bf16[4,512,256]{2,1,0:T(8,128)(2,1)}, bf16[4,512,256]{2,1,0:T(8,128)(2,1)}, u32[]{:S(2)}, u32[]{:S(2)}) collective-permute-start(bf16[4,512,256]{2,1,0:T(8,128)(2,1)} %param.33), channel_id=1, source_target_pairs={{1,0},{2,1},{3,2},{4,3},{5,4},{6,5},{7,6},{0,7},{9,8},{10,9},{11,1... | collective-permute-start | bytes 3145736 | tf_op jit(solution)/shard_map/ppermute | solution.py:22
  14.3 70.9 %collective-permute-start.4 = (bf16[4,256,256]{2,1,0:T(8,128)(2,1)}, bf16[4,256,256]{2,1,0:T(8,128)(2,1)S(1)}, u32[]{:S(2)}, u32[]{:S(2)}) collective-permute-start(bf16[4,256,256]{2,1,0:T(8,128)(2,1)} %param.34), channel_id=1, source_target_pairs={{0,1},{1,2},{2,3},{3,4},{4,5},{5,6},{6,7},{7,0},{8,9},{9,10},{10,1... | collective-permute-start | bytes 1572872 | tf_op jit(solution)/shard_map/ppermute | solution.py:20
  85.3 7.0 %collective-permute-start.5 = (bf16[4,256,256]{2,1,0:T(8,128)(2,1)}, bf16[4,256,256]{2,1,0:T(8,128)(2,1)S(1)}, u32[]{:S(2)}, u32[]{:S(2)}) collective-permute-start(bf16[4,256,256]{2,1,0:T(8,128)(2,1)} %param.34), channel_id=1, source_target_pairs={{1,0},{2,1},{3,2},{4,3},{5,4},{6,5},{7,6},{0,7},{9,8},{10,9},{11,1... | collective-permute-start | bytes 1572872 | tf_op jit(solution)/shard_map/ppermute | solution.py:22
  94.7 1.0 copy-start.2
  118.7 2.2 copy-start.1
  122.8 2.8 copy-start.3
  122.9 25.1 %copy-start = (bf16[12,256,256]{2,1,0:T(8,128)(2,1)S(1)}, bf16[12,256,256]{2,1,0:T(8,128)(2,1)}, u32[]{:S(2)}) copy-start(bf16[12,256,256]{2,1,0:T(8,128)(2,1)} %pad_maximum_fusion.1) | copy-start | bytes 4718596
  122.9 25.1 %copy-start.5 = (f32[16]{0:T(128)S(1)}, f32[16]{0:T(128)}, u32[]{:S(2)}) copy-start(f32[16]{0:T(128)} %param.36) | copy-start | bytes 196
  122.9 25.1 %copy-start.6 = (s32[4,2]{0,1:T(2,128)S(1)}, s32[4,2]{0,1:T(2,128)}, u32[]{:S(2)}) copy-start(s32[4,2]{0,1:T(2,128)} %param.38) | copy-start | bytes 100
  122.9 25.1 %copy-start.7 = (f32[4,256]{1,0:T(4,128)S(1)}, f32[4,256]{1,0:T(4,128)}, u32[]{:S(2)}) copy-start(f32[4,256]{1,0:T(4,128)} %param.35) | copy-start | bytes 12292
  122.9 25.1 %copy-start.8 = (f32[4,8]{1,0:T(4,128)S(1)}, f32[4,8]{1,0:T(4,128)}, u32[]{:S(2)}) copy-start(f32[4,8]{1,0:T(4,128)} %param.40) | copy-start | bytes 388
  122.9 25.1 %copy-start.9 = (s32[4]{0:T(128)S(1)}, s32[4]{0:T(128)}, u32[]{:S(2)}) copy-start(s32[4]{0:T(128)} %param.37) | copy-start | bytes 52
  125.6 2.6 copy-start.4
  221.5 22.3 %collective-permute-start.6 = (bf16[4,256,256]{2,1,0:T(8,128)(2,1)S(1)}, bf16[4,256,256]{2,1,0:T(8,128)(2,1)S(1)}, u32[]{:S(2)}, u32[]{:S(2)}) collective-permute-start(bf16[4,256,256]{2,1,0:T(8,128)(2,1)S(1)} %broadcast_select_fusion.1), channel_id=1, source_target_pairs={{0,1},{1,2},{2,3},{3,4},{4,5},{5,6},{6,7},{7,0},{8,9},{9,10},{10,1... | collective-permute-start | bytes 1572872 | tf_op jit(solution)/shard_map/ppermute | solution.py:20
  221.5 22.2 %collective-permute-start.7 = (bf16[4,256,256]{2,1,0:T(8,128)(2,1)S(1)}, bf16[4,256,256]{2,1,0:T(8,128)(2,1)S(1)}, u32[]{:S(2)}, u32[]{:S(2)}) collective-permute-start(bf16[4,256,256]{2,1,0:T(8,128)(2,1)S(1)} %broadcast_select_fusion.1), channel_id=1, source_target_pairs={{1,0},{2,1},{3,2},{4,3},{5,4},{6,5},{7,6},{0,7},{9,8},{10,9},{11,1... | collective-permute-start | bytes 1572872 | tf_op jit(solution)/shard_map/ppermute | solution.py:22
Sparse Core Ops, SparseCore 0:
  191.6 27.8 all-gather.1
where the time goes:
time: 295 us; the launch traced here: 293 us
  waiting for transfers between devices  102 us (35%)
  loops' own time  57.6 us (20%)
  local copies, waits for them, and re-layouts  44.7 us (15%)
  matrix products  44 us (15%)
  other arithmetic  20 us (7%)
  between operations  14.3 us (5%)
  starting transfers between devices  10.8 us (4%)
    ppermute x4, waiting for transfers between devices, extended(): lax.ppermute(tail, axis, [(i, (i + 1) % count) for i in range(count)])  68.4 us
    another operation x2, loops' own time, refresh(): return lax.map(refresh_one_slot, slot_ids)  35.6 us
    all_gather x1, waiting for transfers between devices, local(): every_amp = lax.all_gather(slot_amps, 'role', axis=0, tiled=True)  28 us
    another operation x2, loops' own time, transform_rows(): return lax.map(one_pair, (orbitals_all, first_ids, second_ids))  14.1 us
    dot_general x4, matrix products, one_pair(): jnp.einsum('qa,qb->ab', first_half, second_half, preferred_element_type=j...  10.6 us
    ppermute x4, starting transfers between devices, extended(): lax.ppermute(head, axis, [((i + 1) % count, i) for i in range(count)])  10.6 us
    dot_general x4, matrix products, refresh_one_slot(): jnp.dot(coeff[pair_at], fresh_amp, preferred_element_type=jnp.float32)  10.5 us
    dot_general x4, matrix products, refresh_one_slot(): jnp.einsum('kbd,ked->kbe', middle, intersection, preferred_element_type=j...  9.41 us
  transfers between devices with their start and end apart: 9, of which 3 were waited for; matrix products, arithmetic and copies ran while one was open for 12% of the time, Pallas kernels for 0%

commit v1 on v0

v1 whole, which is shorter than its diff:
```python
import math

import jax
import jax.numpy as jnp
from jax import lax
from jax.experimental import pallas as pl
from jax.experimental.pallas import tpu as pltpu
from jax.sharding import PartitionSpec as P

F32 = jnp.float32
BF16 = jnp.bfloat16
NN = ((1,), (0,))
NT = ((1,), (1,))

VMEM = pl.BlockSpec(memory_space=pltpu.VMEM)
SMEM = pl.BlockSpec(memory_space=pltpu.SMEM)
ANY = pl.BlockSpec(memory_space=pl.ANY)

MINE, EXTRA, OWNER, FIRST, SECOND, NV_MINE, NV_EXTRA, ROLE_PAIR = 0, 1, 2, 3, 4, 5, 6, 7


def mxu(a, b, dims):
    return lax.dot_general(a, b, (dims, ((), ())), preferred_element_type=F32)


def call(body, ins, outs, args, scratch=(), flops=0):
    moved = sum(a.size * a.dtype.itemsize for a in args)
    return pl.pallas_call(
        body,
        in_specs=ins,
        out_specs=[spec for spec, _, _ in outs],
        out_shape=[jax.ShapeDtypeStruct(shape, dtype) for _, shape, dtype in outs],
        scratch_shapes=list(scratch),
        cost_estimate=pl.CostEstimate(flops=flops, bytes_accessed=moved, transcendentals=0),
        compiler_params=pltpu.CompilerParams(vmem_limit_bytes=48 * 1024 * 1024),
    )(*args)


def pair_of_role(owner_ref, role, pairs):
    chosen = jnp.int32(0)
    for p in range(pairs):
        earlier = jnp.int32(0)
        for o in range(p):
            earlier += (owner_ref[o] == owner_ref[p]).astype(jnp.int32)
        hit = jnp.where(role > 0, (owner_ref[p] == role) & (earlier == 0), earlier == 1)
        chosen = jnp.where(hit, p, chosen)
    return chosen


def local(
    three_index, coeff, amps, eps_virt, eps_occ, nvirt, pair_occ, partners, coupling, pair_owner
):
    columns = lax.axis_size("pairs")
    roles = lax.axis_size("role")
    occ_block, aux, pao = three_index.shape
    pairs, _, virt = coeff.shape
    partner_count = partners.shape[1]
    slots = 2
    assert roles == pairs
    tile = min(256, aux)
    pao_scale = 1.0 / math.sqrt(pao)
    aux_scale = 1.0 / math.sqrt(aux)
    virt_scale = 1.0 / math.sqrt(virt)
    square = (virt, virt)

    def shift(x, by):
        return lax.ppermute(x, "pairs", [(i, (i + by) % columns) for i in range(columns)])

    def swap(x, by, skip=()):
        return lax.ppermute(
            x, "role", [(i, i ^ by) for i in range(roles) if i ^ by not in skip]
        )

    def pick_body(owner_ref, coeff_ref, out_ref, sem):
        mine = pair_of_role(owner_ref, lax.axis_index("role"), pairs)
        copy = pltpu.make_async_copy(coeff_ref.at[mine], out_ref, sem)
        copy.start()
        copy.wait()

    (x_mine,) = call(
        pick_body,
        [SMEM, ANY],
        [(ANY, (pao, virt), BF16)],
        (pair_owner, coeff),
        scratch=[pltpu.SemaphoreType.DMA],
    )
    x_left = shift(x_mine, 1)
    x_right = shift(x_mine, -1)

    def plan_body(
        owner_ref, occ_ref, partner_ref, coupling_ref, eps_ref, nvirt_ref,
        to_left, to_right, ints, floats, extra_w,
    ):
        role = lax.axis_index("role")
        column = lax.axis_index("pairs")
        mine = pair_of_role(owner_ref, role, pairs)
        extra = pair_of_role(owner_ref, jnp.int32(0), pairs)
        ints[MINE] = mine
        ints[EXTRA] = extra
        ints[OWNER] = owner_ref[extra]
        for s in range(roles):
            ints[ROLE_PAIR + s] = pair_of_role(owner_ref, jnp.int32(s), pairs)
        ints[NV_MINE] = nvirt_ref[mine]
        ints[NV_EXTRA] = nvirt_ref[extra]
        ints[FIRST] = occ_ref[mine, 0] - column * occ_block
        occ_all = occ_block * columns
        second = lax.rem(occ_ref[mine, 1] - (column - 1) * occ_block + occ_all, occ_all)
        ints[SECOND] = second
        floats[pairs] = eps_ref[occ_ref[mine, 0]] + eps_ref[occ_ref[mine, 1]]
        floats[pairs + 1] = eps_ref[occ_ref[extra, 0]] + eps_ref[occ_ref[extra, 1]]
        for q in range(pairs):
            to_left[q] = jnp.float32(0)
            to_right[q] = jnp.float32(0)
            floats[q] = jnp.float32(0)
        for q in range(3 * pairs):
            extra_w[q] = jnp.float32(0)
        pair_all = pairs * columns

        def near(p, k):
            return lax.rem(partner_ref[p, k] - (column - 1) * pairs + pair_all, pair_all)

        for k in range(partner_count):
            at, weight = near(mine, k), coupling_ref[mine, k]

            @pl.when(at < pairs)
            def _():
                to_left[at] += weight

            @pl.when((at >= pairs) & (at < 2 * pairs))
            def _():
                floats[at - pairs] += weight

            @pl.when(at >= 2 * pairs)
            def _():
                to_right[at - 2 * pairs] += weight

            extra_w[near(extra, k)] += coupling_ref[extra, k]
        to_left[pairs] = jnp.minimum(second, occ_block - 1).astype(F32)
        to_right[pairs] = jnp.maximum(second - 2 * occ_block, 0).astype(F32)
        to_left[pairs + 1] = mine.astype(F32)
        to_right[pairs + 1] = mine.astype(F32)

    meta = (SMEM, (pairs + 2,), F32)
    to_left, to_right, ints, floats, extra_w = call(
        plan_body,
        [SMEM] * 6,
        [
            meta,
            meta,
            (SMEM, (ROLE_PAIR + roles,), jnp.int32),
            (SMEM, (pairs + 2,), F32),
            (SMEM, (3 * pairs,), F32),
        ],
        (pair_owner, pair_occ, partners, coupling, eps_occ, nvirt),
    )
    of_left = shift(to_right, 1)
    of_right = shift(to_left, -1)

    def overlaps(x, coeff_ref, out_ref):
        turned = x.T
        for q in range(pairs):
            s = mxu(turned, coeff_ref[q], NN) * (1.0 / pao)
            out_ref[q] = s.astype(BF16)

    def coupled(s_ref, parts):
        total = None
        for at, weight, amp in parts:
            s = s_ref[at]
            middle = mxu(s, amp, NN).astype(BF16)
            term = weight * mxu(middle, s, NT)
            total = term if total is None else total + term
        return total

    def own_body(
        ints, floats, three_ref, coeff_ref, amps_ref, eps_ref,
        first_ref, second_ref, s_ref, c_ref, gain_ref, gain_extra_ref,
    ):
        mine = ints[MINE]
        x = coeff_ref[mine]
        turned = x.T
        first = ints[FIRST]
        second = jnp.clip(ints[SECOND] - occ_block, 0, occ_block - 1)
        for at in range(0, aux, tile):
            rows = pl.ds(at, tile)
            first_ref[:, rows] = (mxu(turned, three_ref[first, rows, :], NT) * pao_scale).astype(BF16)
            second_ref[rows, :] = (mxu(three_ref[second, rows, :], x, NN) * pao_scale).astype(BF16)
        overlaps(x, coeff_ref, s_ref)
        c_ref[...] = coupled(s_ref, [(q, floats[q], amps_ref[q]) for q in range(pairs)])

        def gain(pair, count, shift_at):
            row = jnp.broadcast_to(eps_ref[pl.ds(pair, 1), :], square)
            energy = row + row.T - floats[shift_at]
            inside = (lax.broadcasted_iota(jnp.int32, square, 0) < count) & (
                lax.broadcasted_iota(jnp.int32, square, 1) < count
            )
            return jnp.where(inside, 1.0 / (energy + 1.0), 0.0)

        gain_ref[...] = gain(mine, ints[NV_MINE], pairs)
        gain_extra_ref[...] = gain(ints[EXTRA], ints[NV_EXTRA], pairs + 1)

    all_s = (VMEM, (pairs, virt, virt), BF16)
    first_t, second_own, s_own, c_own, gain, gain_extra = call(
        own_body,
        [SMEM, SMEM, VMEM, VMEM, VMEM, VMEM],
        [
            (VMEM, (virt, aux), BF16),
            (VMEM, (aux, virt), BF16),
            all_s,
            (VMEM, square, F32),
            (VMEM, square, F32),
            (VMEM, square, F32),
        ],
        (ints, floats, three_index, coeff, amps, eps_virt),
        flops=2 * virt * (2 * aux * pao + pairs * virt * (pao + 2 * virt)),
    )

    def half_body(of_left, of_right, three_ref, xl_ref, xr_ref, yl_ref, yr_ref):
        for of, x_ref, y_ref in ((of_left, xl_ref, yl_ref), (of_right, xr_ref, yr_ref)):
            at_occ = of[pairs].astype(jnp.int32)
            for at in range(0, aux, tile):
                rows = pl.ds(at, tile)
                y_ref[rows, :] = (mxu(three_ref[at_occ, rows, :], x_ref[...], NN) * pao_scale).astype(BF16)

    half = (VMEM, (aux, virt), BF16)
    y_left, y_right = call(
        half_body,
        [SMEM, SMEM, VMEM, VMEM, VMEM],
        [half, half],
        (of_left, of_right, three_index, x_left, x_right),
        flops=4 * aux * pao * virt,
    )
    y_from_right = shift(y_left, -1)
    y_from_left = shift(y_right, 1)

    def near_body(of_left, of_right, coeff_ref, amps_ref, xl_ref, xr_ref, sl_ref, sr_ref, cl_ref, cr_ref):
        for of, x_ref, s_ref, c_ref in (
            (of_left, xl_ref, sl_ref, cl_ref),
            (of_right, xr_ref, sr_ref, cr_ref),
        ):
            overlaps(x_ref[...], coeff_ref, s_ref)
            c_ref[...] = coupled(
                s_ref, [(q, of[q], amps_ref[q]) for q in range(pairs)]
            ).astype(BF16)

    sq_b = (VMEM, square, BF16)
    sq_f = (VMEM, square, F32)
    s_left, s_right, c_left, c_right = call(
        near_body,
        [SMEM, SMEM, VMEM, VMEM, VMEM, VMEM],
        [all_s, all_s, sq_b, sq_b],
        (of_left, of_right, coeff, amps, x_left, x_right),
        flops=4 * pairs * virt * virt * (pao + 2 * virt),
    )
    c_from_right = shift(c_left, -1)
    c_from_left = shift(c_right, 1)

    def first_body(
        ints, first_ref, own_ref, left_ref, right_ref, amps_ref, c_ref, cl_ref, cr_ref, gain_ref,
        amp_ref, k_ref, held, sem,
    ):
        second = ints[SECOND]

        def take(source):
            copy = pltpu.make_async_copy(source, held, sem)
            copy.start()
            copy.wait()

        @pl.when(second < occ_block)
        def _():
            take(left_ref)

        @pl.when((second >= occ_block) & (second < 2 * occ_block))
        def _():
            take(own_ref)

        @pl.when(second >= 2 * occ_block)
        def _():
            take(right_ref)

        k = mxu(first_ref[...], held[...], NN) * aux_scale
        k_ref[...] = k
        c = c_ref[...] + cl_ref[...].astype(F32) + cr_ref[...].astype(F32)
        old = amps_ref[ints[MINE]].astype(F32)
        amp_ref[...] = (gain_ref[...] * (old - k - c)).astype(BF16)

    amp, k_first = call(
        first_body,
        [SMEM, VMEM, ANY, ANY, ANY, VMEM, VMEM, VMEM, VMEM, VMEM],
        [sq_b, sq_f],
        (
            ints, first_t, second_own, y_from_left, y_from_right,
            amps, c_own, c_from_left, c_from_right, gain,
        ),
        scratch=[pltpu.VMEM((aux, virt), BF16), pltpu.SemaphoreType.DMA],
        flops=2 * aux * virt * virt,
    )

    amp_roles = [amp] + [swap(amp, m) for m in range(1, roles)]
    amp_left = shift(amp, 1)
    amp_right = shift(amp, -1)

    def second_body(amp_ref, k_ref, out_ref):
        amp = amp_ref[...]
        k = k_ref[...]
        right = k + mxu(k.astype(BF16), amp, NN) * virt_scale
        both = right + mxu(amp.T, right.astype(BF16), NN) * virt_scale
        out_ref[...] = amp.astype(F32) - both

    (rest,) = call(
        second_body, [VMEM, VMEM], [sq_f], (amp, k_first), flops=4 * virt * virt * virt
    )

    def extra_body(
        ints, extra_w, of_left, of_right, so_ref, sl_ref, sr_ref, ao_ref, al_ref, ar_ref, rest_ref, out_ref
    ):
        extra = ints[EXTRA]
        left = of_left[pairs + 1].astype(jnp.int32)
        right = of_right[pairs + 1].astype(jnp.int32)
        total = jnp.where(lax.axis_index("role") == 0, rest_ref[...], 0.0)
        for s_ref, amp_ref, at in (
            (sl_ref, al_ref, left),
            (so_ref, ao_ref, pairs + ints[MINE]),
            (sr_ref, ar_ref, 2 * pairs + right),
        ):
            s = s_ref[extra]
            middle = mxu(amp_ref[...], s, NN).astype(BF16)
            total -= extra_w[at] * mxu(s.T, middle, NN)
        out_ref[...] = total.astype(BF16)

    (extra_part,) = call(
        extra_body,
        [SMEM] * 4 + [VMEM] * 7,
        [sq_b],
        (
            ints, extra_w, of_left, of_right, s_own, s_left, s_right,
            amp, amp_left, amp_right, rest,
        ),
        flops=12 * virt * virt * virt,
    )
    extra_parts = [extra_part] + [swap(extra_part, m, skip=(0,)) for m in range(1, roles)]

    def column_parts(ints, weight, amp_refs):
        role = lax.axis_index("role")
        parts = []
        for m in range(roles):
            at = ints[ROLE_PAIR + (role ^ m)]
            parts.append((at, weight[at], amp_refs[m][...]))
        return parts

    def again_body(ints, of_left, of_right, sl_ref, sr_ref, a0, a1, a2, a3, cl_ref, cr_ref):
        amp_refs = (a0, a1, a2, a3)
        for of, s_ref, c_ref in ((of_left, sl_ref, cl_ref), (of_right, sr_ref, cr_ref)):
            c_ref[...] = coupled(s_ref, column_parts(ints, of, amp_refs)).astype(BF16)

    c_left, c_right = call(
        again_body,
        [SMEM] * 3 + [VMEM] * 6,
        [sq_b, sq_b],
        (ints, of_left, of_right, s_left, s_right, *amp_roles),
        flops=8 * pairs * virt * virt * virt,
    )
    c_from_right = shift(c_left, -1)
    c_from_left = shift(c_right, 1)

    def own_again_body(ints, floats, s_ref, a0, a1, a2, a3, rest_ref, out_ref):
        c = coupled(s_ref, column_parts(ints, floats, (a0, a1, a2, a3)))
        out_ref[...] = rest_ref[...] - c

    (rest,) = call(
        own_again_body,
        [SMEM] * 2 + [VMEM] * 6,
        [sq_f],
        (ints, floats, s_own, *amp_roles, rest),
        flops=4 * pairs * virt * virt * virt,
    )

    def last_body(
        ints, coeff_ref, gain_ref, gain_extra_ref, rest_ref, cl_ref, cr_ref, e0, e1, e2, e3,
        amp_ref, orb_ref,
    ):
        role = lax.axis_index("role")

        def store(slot, amp, pair):
            amp = amp.astype(BF16)
            amp_ref[slot] = amp
            x = coeff_ref[pair]
            orb_ref[slot] = (x.astype(F32) + mxu(x, amp, NN) * virt_scale).astype(BF16)

        def clear(slot):
            amp_ref[slot] = jnp.zeros(square, BF16)
            orb_ref[slot] = jnp.zeros((pao, virt), BF16)

        has_extra = role == ints[OWNER]

        @pl.when(has_extra)
        def _():
            total = sum(e[...].astype(F32) for e in (e0, e1, e2, e3))
            store(1, gain_extra_ref[...] * total, ints[EXTRA])

        @pl.when(jnp.logical_not(has_extra))
        def _():
            clear(1)

        @pl.when(role > 0)
        def _():
            total = rest_ref[...] - cl_ref[...].astype(F32) - cr_ref[...].astype(F32)
            store(0, gain_ref[...] * total, ints[MINE])

        @pl.when(role == 0)
        def _():
            clear(0)

    amps_out, dressed_out = call(
        last_body,
        [SMEM] + [VMEM] * 10,
        [(VMEM, (slots, virt, virt), BF16), (VMEM, (slots, pao, virt), BF16)],
        (ints, coeff, gain, gain_extra, rest, c_from_left, c_from_right, *extra_parts),
        flops=4 * pao * virt * virt,
    )
    return amps_out, dressed_out


def solution(mesh):
    in_specs = (
        P("pairs", None, None),
        P("pairs", None, None),
        P("pairs", None, None),
        P("pairs", None),
        P(),
        P("pairs"),
        P("pairs", None),
        P("pairs", None),
        P("pairs", None),
        P("pairs"),
    )
    out_specs = (P(("role", "pairs"), None, None), P(("role", "pairs"), None, None))
    return jax.shard_map(local, mesh=mesh, in_specs=in_specs, out_specs=out_specs, check_vma=False)
```

time: 295 us -> 67.1 us (0.23)
  the two profiles are of different devices: /device:TPU:2 before, /device:TPU:0 now
where the time goes in v1:
time: 67.1 us; the launch traced here: 66.7 us
  starting transfers between devices  31.7 us (47%)
  Pallas kernels  13.6 us (20%)
  waiting for transfers between devices  13 us (19%)
  local copies, waits for them, and re-layouts  7.58 us (11%)
  between operations  0.87 us (1%)
    ppermute x12, starting transfers between devices, shift(): lax.ppermute(x, 'pairs', [(i, (i + by) % columns) for i in range(columns)])  19.5 us
    pallas_call x11, Pallas kernels, call(): pl.pallas_call(body, in_specs=ins, out_specs=[spec for spec, _, _ in outs...  13.6 us
    ppermute x12, waiting for transfers between devices, shift(): lax.ppermute(x, 'pairs', [(i, (i + by) % columns) for i in range(columns)])  13 us
    ppermute x6, starting transfers between devices, swap(): lax.ppermute(x, 'role', [(i, i ^ by) for i in range(roles) if i ^ by not...  12.2 us
    unnamed x25, local copies, waits for them, and re-layouts  7.58 us
  transfers between devices with their start and end apart: 18, of which 5 were waited for; matrix products, arithmetic and copies ran while one was open for 1% of the time, Pallas kernels for 14%

profile of v1, /device:TPU:0, one launch (start us, length us, event | category | flops | bytes accessed | tf_op | source)
XLA Modules:
  0.0 66.7 jit_solution(5656054266480732814)
XLA Ops:
  0.6 0.0 copy-start
  0.6 1.2 %copy-done = bf16[4,512,256]{2,1,0:T(8,128)(2,1)S(1)} copy-done((bf16[4,512,256]{2,1,0:T(8,128)(2,1)S(1)}, bf16[4,512,256]{2,1,0:T(8,128)(2,1)}, u32[]{:S(2)}) %copy-start) | copy-done | bytes 1048600
  1.9 0.0 copy-start.5
  1.9 0.7 copy-done.5
  2.5 0.6 shard_map.115
  3.1 4.5 %collective-permute-start.3 = (bf16[512,256]{1,0:T(8,128)(2,1)S(1)}, bf16[512,256]{1,0:T(8,128)(2,1)S(1)}, u32[]{:S(2)}, u32[]{:S(2)}) collective-permute-start(bf16[512,256]{1,0:T(8,128)(2,1)S(1)} %shard_map.115), channel_id=1, source_target_pairs={{0,7},{1,0},{2,1},{3,2},{4,3},{5,4},{6,5},{7,6},{8,15},{9,8},{10,9... | collective-permute-start | bytes 786440 | tf_op jit(solution)/shard_map/ppermute | solution.py:67
  7.7 0.0 collective-permute-start.2
  7.7 0.8 %copy.12.occ_ref = s32[4,2]{1,0:T(4,128)S(1)} copy(s32[4,2]{0,1:T(2,128)} %param.16) | data formatting | bytes 64 | tf_op args[6]
  8.4 0.7 copy-done.6
  9.1 0.7 %copy-done.7 = s32[4,8]{1,0:T(4,128)S(1)} copy-done((s32[4,8]{1,0:T(4,128)S(1)}, s32[4,8]{1,0:T(4,128)}, u32[]{:S(2)}) %copy-start.7) | copy-done | bytes 152
  9.8 0.7 %copy-done.8 = f32[4,8]{1,0:T(4,128)S(1)} copy-done((f32[4,8]{1,0:T(4,128)S(1)}, f32[4,8]{1,0:T(4,128)}, u32[]{:S(2)}) %copy-start.8) | copy-done | bytes 152
  10.4 0.7 copy-done.9
  11.1 0.7 copy-done.10
  11.8 1.5 %shard_map.113 = (f32[6]{0:T(128)S(1)}, f32[6]{0:T(128)S(1)}, s32[11]{0:T(128)S(1)}, f32[6]{0:T(128)S(1)}, f32[12]{0:T(128)S(1)}) custom-call(s32[4]{0:T(128)S(1)} %copy-done.6, s32[4,2]{1,0:T(4,128)S(1)} %copy.12.occ_ref, s32[4,8]{1,0:T(4,128)S(1)} %copy-done.7, f32[4,8]{1,0:T(4,128)S(1)} %copy-done.8, f32[16]{0:T(128)S(1)} %copy-done.9, s32[4]{0:T(128)S(1)} %copy-done.10), custom_call_target="tpu_custom_call" | custom-call | bytes 384 | tf_op jit(solution)/shard_map/pallas_call | solution.py:28
  13.2 0.1 collective-permute-start
  13.3 3.6 %collective-permute-start.1 = (f32[6]{0:T(128)S(1)}, f32[6]{0:T(128)S(1)}, u32[]{:S(2)}, u32[]{:S(2)}) collective-permute-start(f32[6]{0:T(128)S(1)} %get-tuple-element.31), channel_id=1, source_target_pairs={{0,7},{1,0},{2,1},{3,2},{4,3},{5,4},{6,5},{7,6},{8,15},{9,8},{10,9... | collective-permute-start | bytes 80 | tf_op jit(solution)/shard_map/ppermute | solution.py:67
  16.9 1.2 %collective-permute-done.of_left = f32[6]{0:T(128)S(1)} collective-permute-done((f32[6]{0:T(128)S(1)}, f32[6]{0:T(128)S(1)}, u32[]{:S(2)}, u32[]{:S(2)}) %collective-permute-start) | collective-permute-done | bytes 56 | tf_op jit(solution)/shard_map/ppermute | solution.py:67
  18.1 0.1 collective-permute-done.1.of_right
  18.2 0.0 collective-permute-done.3.xr_ref
  18.2 0.0 collective-permute-done.2.xl_ref
  18.2 1.6 %copy-done.2 = bf16[2,1024,512]{2,1,0:T(8,128)(2,1)S(1)} copy-done((bf16[2,1024,512]{2,1,0:T(8,128)(2,1)S(1)}, bf16[2,1024,512]{2,1,0:T(8,128)(2,1)}, u32[]{:S(2)}) %copy-start.2) | copy-done | bytes 2097176
  19.8 1.2 %shard_map.116 = (bf16[1024,256]{1,0:T(8,128)(2,1)S(1)}, bf16[1024,256]{1,0:T(8,128)(2,1)S(1)}) custom-call(f32[6]{0:T(128)S(1)} %collective-permute-done.of_left, f32[6]{0:T(128)S(1)} %collective-permute-done.1.of_right, bf16[2,1024,512]{2,1,0:T(8,128)(2,1)S(1)} %copy-done.2, bf16[512,256]{1,0:T(8,128)(2,1)S(1)} %collective-permute-done.2.xl_ref, ...), custom_call_target="tpu_custom_call" | custom-call | flops 536870912 | bytes 2621488 | tf_op jit(solution)/shard_map/pallas_call | solution.py:28
  21.0 0.0 copy-start.3
  21.1 0.0 copy-start.11
  21.1 0.1 collective-permute-start.4
  21.1 3.5 %collective-permute-start.5 = (bf16[1024,256]{1,0:T(8,128)(2,1)S(1)}, bf16[1024,256]{1,0:T(8,128)(2,1)S(1)}, u32[]{:S(2)}, u32[]{:S(2)}) collective-permute-start(bf16[1024,256]{1,0:T(8,128)(2,1)S(1)} %get-tuple-element.33), channel_id=1, source_target_pairs={{0,7},{1,0},{2,1},{3,2},{4,3},{5,4},{6,5},{7,6},{8,15},{9,8},{10,9... | collective-permute-start | bytes 1572872 | tf_op jit(solution)/shard_map/ppermute | solution.py:67
  24.7 0.0 copy-done.1
  24.7 0.0 copy-done.4
  24.7 1.9 %shard_map.117 = (bf16[4,256,256]{2,1,0:T(8,128)(2,1)S(1)}, bf16[4,256,256]{2,1,0:T(8,128)(2,1)S(1)}, bf16[256,256]{1,0:T(8,128)(2,1)S(1)}, bf16[256,256]{1,0:T(8,128)(2,1)S(1)}) custom-call(f32[6]{0:T(128)S(1)} %collective-permute-done.of_left, f32[6]{0:T(128)S(1)} %collective-permute-done.1.of_right, bf16[4,512,256]{2,1,0:T(8,128)(2,1)S(1)} %copy-done.1, ...), custom_call_target="tpu_custom_call" | custom-call | flops 1073741824 | bytes 2097200 | tf_op jit(solution)/shard_map/pallas_call | solution.py:28
  26.6 0.1 collective-permute-start.6
  26.7 3.5 %collective-permute-start.7 = (bf16[256,256]{1,0:T(8,128)(2,1)S(1)}, bf16[256,256]{1,0:T(8,128)(2,1)S(1)}, u32[]{:S(2)}, u32[]{:S(2)}) collective-permute-start(bf16[256,256]{1,0:T(8,128)(2,1)S(1)} %get-tuple-element.36), channel_id=1, source_target_pairs={{0,7},{1,0},{2,1},{3,2},{4,3},{5,4},{6,5},{7,6},{8,15},{9,8},{10,9... | collective-permute-start | bytes 393224 | tf_op jit(solution)/shard_map/ppermute | solution.py:67
  30.2 0.0 copy-done.3
  30.2 0.0 copy-done.11
  30.2 1.9 %shard_map.114 = (bf16[256,1024]{1,0:T(8,128)(2,1)S(1)}, bf16[1024,256]{1,0:T(8,128)(2,1)S(1)}, bf16[4,256,256]{2,1,0:T(8,128)(2,1)S(1)}, f32[256,256]{1,0:T(8,1...) custom-call(s32[11]{0:T(128)S(1)} %get-tuple-element.23.ints, f32[6]{0:T(128)S(1)} %get-tuple-element.24.floats, ...), custom_call_target="tpu_custom_call" | custom-call | flops 1073741824 | bytes 3674180 | tf_op jit(solution)/shard_map/pallas_call | solution.py:28
  32.2 7.2 %collective-permute-done.6.cl_ref = bf16[256,256]{1,0:T(8,128)(2,1)S(1)} collective-permute-done((bf16[256,256]{1,0:T(8,128)(2,1)S(1)}, bf16[256,256]{1,0:T(8,128)(2,1)S(1)}, u32[]{:S(2)}, u32[]{:S(2)}) %collective-permute-start.6) | collective-permute-done | bytes 131104 | tf_op jit(solution)/shard_map/ppermute | solution.py:67
  39.4 0.0 collective-permute-done.7.cr_ref
  39.4 0.0 collective-permute-done.4.left_ref
  39.4 0.0 collective-permute-done.5.right_ref
  39.4 0.9 %shard_map.118 = (bf16[256,256]{1,0:T(8,128)(2,1)S(1)}, f32[256,256]{1,0:T(8,128)S(1)}) custom-call(s32[11]{0:T(128)S(1)} %get-tuple-element.23.ints, bf16[256,1024]{1,0:T(8,128)(2,1)S(1)} %get-tuple-element.28.first_ref, bf16[1024,256]{1,0:T(8,128)(2,1)S(1)} %get-tuple-element.29.own_ref, bf16[1024,256]{1,0:T(8,128)(2,1)S(1)} %collective-permute-done.4.left_ref, ...), custom_call_target="tpu_custom_call" | custom-call | flops 134217728 | bytes 3407916 | tf_op jit(solution)/shard_map/pallas_call | solution.py:28
  40.3 0.1 collective-permute-start.14
  40.4 0.5 collective-permute-start.13
  40.9 2.4 %collective-permute-start.10 = (bf16[256,256]{1,0:T(8,128)(2,1)S(1)}, bf16[256,256]{1,0:T(8,128)(2,1)S(1)}, u32[]{:S(2)}, u32[]{:S(2)}) collective-permute-start(bf16[256,256]{1,0:T(8,128)(2,1)S(1)} %get-tuple-element.37.amp_ref.a0.ao_ref), channel_id=1, source_target_pairs={{0,24},{8,16},{16,8},{24,0},{1,25},{9,17},{17,9},{25,1},{2,26},{10... | collective-permute-start | bytes 393224 | tf_op jit(solution)/shard_map/ppermute | solution.py:70
  43.3 0.5 collective-permute-start.9
  43.9 0.5 collective-permute-start.8
  44.4 0.4 shard_map.119.rest_ref
  44.8 0.0 collective-permute-done.14.ar_ref
  44.8 1.9 %collective-permute-done.13.al_ref = bf16[256,256]{1,0:T(8,128)(2,1)S(1)} collective-permute-done((bf16[256,256]{1,0:T(8,128)(2,1)S(1)}, bf16[256,256]{1,0:T(8,128)(2,1)S(1)}, u32[]{:S(2)}, u32[]{:S(2)}) %collective-permute-start.13) | collective-permute-done | bytes 131104 | tf_op jit(solution)/shard_map/ppermute | solution.py:67
  46.7 1.1 %shard_map.122.e0 = bf16[256,256]{1,0:T(8,128)(2,1)S(1)} custom-call(s32[11]{0:T(128)S(1)} %get-tuple-element.23.ints, f32[12]{0:T(128)S(1)} %get-tuple-element.43.extra_w, f32[6]{0:T(128)S(1)} %collective-permute-done.of_left, f32[6]{0:T(128)S(1)} %collective-permute-done.1.of_right, bf16[4,256,256]{2,1,0:T(8,128)(2,1)S(1)} %get-tuple-element.27.s_ref.so_ref, ...), custom_call_target="tpu_custom_call" | custom-call | flops 201326592 | bytes 2228364 | tf_op jit(solution)/shard_map/pallas_call | solution.py:28
  47.9 4.4 %collective-permute-start.17 = (bf16[256,256]{1,0:T(8,128)(2,1)S(1)}, bf16[256,256]{1,0:T(8,128)(2,1)S(1)}, u32[]{:S(2)}, u32[]{:S(2)}) collective-permute-start(bf16[256,256]{1,0:T(8,128)(2,1)S(1)} %shard_map.122.e0), channel_id=1, source_target_pairs={{0,24},{8,16},{16,8},{1,25},{9,17},{17,9},{2,26},{10,18},{18,10},{... | collective-permute-start | bytes 393224 | tf_op jit(solution)/shard_map/ppermute | solution.py:70
  52.2 2.4 %collective-permute-start.16 = (bf16[256,256]{1,0:T(8,128)(2,1)S(1)}, bf16[256,256]{1,0:T(8,128)(2,1)S(1)}, u32[]{:S(2)}, u32[]{:S(2)}) collective-permute-start(bf16[256,256]{1,0:T(8,128)(2,1)S(1)} %shard_map.122.e0), channel_id=1, source_target_pairs={{0,16},{8,24},{24,8},{1,17},{9,25},{25,9},{2,18},{10,26},{26,10},{... | collective-permute-start | bytes 393224 | tf_op jit(solution)/shard_map/ppermute | solution.py:70
  54.6 0.0 collective-permute-done.10.a3
  54.7 1.9 %collective-permute-start.15 = (bf16[256,256]{1,0:T(8,128)(2,1)S(1)}, bf16[256,256]{1,0:T(8,128)(2,1)S(1)}, u32[]{:S(2)}, u32[]{:S(2)}) collective-permute-start(bf16[256,256]{1,0:T(8,128)(2,1)S(1)} %shard_map.122.e0), channel_id=1, source_target_pairs={{0,8},{16,24},{24,16},{1,9},{17,25},{25,17},{2,10},{18,26},{26,18}... | collective-permute-start | bytes 393224 | tf_op jit(solution)/shard_map/ppermute | solution.py:70
  56.6 0.0 collective-permute-done.9.a2
  56.6 0.0 collective-permute-done.8.a1
  56.6 1.4 %shard_map.121 = (bf16[256,256]{1,0:T(8,128)(2,1)S(1)}, bf16[256,256]{1,0:T(8,128)(2,1)S(1)}) custom-call(s32[11]{0:T(128)S(1)} %get-tuple-element.23.ints, f32[6]{0:T(128)S(1)} %collective-permute-done.of_left, f32[6]{0:T(128)S(1)} %collective-permute-done.1.of_right, bf16[4,256,256]{2,1,0:T(8,128)(2,1)S(1)} %get-tuple-element.39.sl_ref, ...), custom_call_target="tpu_custom_call" | custom-call | flops 536870912 | bytes 1572956 | tf_op jit(solution)/shard_map/pallas_call | solution.py:28
  58.0 0.1 collective-permute-start.11
  58.1 3.5 %collective-permute-start.12 = (bf16[256,256]{1,0:T(8,128)(2,1)S(1)}, bf16[256,256]{1,0:T(8,128)(2,1)S(1)}, u32[]{:S(2)}, u32[]{:S(2)}) collective-permute-start(bf16[256,256]{1,0:T(8,128)(2,1)S(1)} %get-tuple-element.42), channel_id=1, source_target_pairs={{0,7},{1,0},{2,1},{3,2},{4,3},{5,4},{6,5},{7,6},{8,15},{9,8},{10,9... | collective-permute-start | bytes 393224 | tf_op jit(solution)/shard_map/ppermute | solution.py:67
  61.6 1.1 %shard_map.120.rest_ref = f32[256,256]{1,0:T(8,128)S(1)} custom-call(s32[11]{0:T(128)S(1)} %get-tuple-element.23.ints, f32[6]{0:T(128)S(1)} %get-tuple-element.24.floats, bf16[4,256,256]{2,1,0:T(8,128)(2,1)S(1)} %get-tuple-element.27.s_ref.so_ref, bf16[256,256]{1,0:T(8,128)(2,1)S(1)} %get-tuple-element.37.amp_ref.a0.ao_ref, ...), custom_call_target="tpu_custom_call" | custom-call | flops 268435456 | bytes 1310788 | tf_op jit(solution)/shard_map/pallas_call | solution.py:28
  62.7 0.0 collective-permute-done.17.e3
  62.7 0.0 collective-permute-done.16.e2
  62.7 0.0 collective-permute-done.15.e1
  62.7 2.5 %collective-permute-done.11.cl_ref = bf16[256,256]{1,0:T(8,128)(2,1)S(1)} collective-permute-done((bf16[256,256]{1,0:T(8,128)(2,1)S(1)}, bf16[256,256]{1,0:T(8,128)(2,1)S(1)}, u32[]{:S(2)}, u32[]{:S(2)}) %collective-permute-start.11) | collective-permute-done | bytes 131104 | tf_op jit(solution)/shard_map/ppermute | solution.py:67
  65.3 0.0 collective-permute-done.12.cr_ref
  65.3 1.5 %shard_map.123 = (bf16[2,256,256]{2,1,0:T(8,128)(2,1)}, bf16[2,512,256]{2,1,0:T(8,128)(2,1)}) custom-call(s32[11]{0:T(128)S(1)} %get-tuple-element.23.ints, bf16[4,512,256]{2,1,0:T(8,128)(2,1)S(1)} %copy-done.1, f32[256,256]{1,0:T(8,128)S(1)} %get-tuple-element.25.gain_ref, f32[256,256]{1,0:T(8,128)S(1)} %get-tuple-element.26.gain_extra_ref, ...), custom_call_target="tpu_custom_call" | custom-call | flops 134217728 | bytes 2621484 | tf_op jit(solution)/shard_map/pallas_call | solution.py:28
  (8 shorter events, 0.0 us)
Async XLA Ops:
  0.6 1.2 %copy-start = (bf16[4,512,256]{2,1,0:T(8,128)(2,1)S(1)}, bf16[4,512,256]{2,1,0:T(8,128)(2,1)}, u32[]{:S(2)}) copy-start(bf16[4,512,256]{2,1,0:T(8,128)(2,1)} %coeff_ref.7) | copy-start | bytes 3145732
  1.9 0.7 copy-start.5
  2.5 22.2 %copy-start.1 = (bf16[4,512,256]{2,1,0:T(8,128)(2,1)S(1)}, bf16[4,512,256]{2,1,0:T(8,128)(2,1)}, u32[]{:S(2)}) copy-start(bf16[4,512,256]{2,1,0:T(8,128)(2,1)} %coeff_ref.7) | copy-start | bytes 3145732
  3.1 15.1 %collective-permute-start.3 = (bf16[512,256]{1,0:T(8,128)(2,1)S(1)}, bf16[512,256]{1,0:T(8,128)(2,1)S(1)}, u32[]{:S(2)}, u32[]{:S(2)}) collective-permute-start(bf16[512,256]{1,0:T(8,128)(2,1)S(1)} %shard_map.115), channel_id=1, source_target_pairs={{0,7},{1,0},{2,1},{3,2},{4,3},{5,4},{6,5},{7,6},{8,15},{9,8},{10,9... | collective-permute-start | bytes 786440 | tf_op jit(solution)/shard_map/ppermute | solution.py:67
  7.7 10.5 %collective-permute-start.2 = (bf16[512,256]{1,0:T(8,128)(2,1)S(1)}, bf16[512,256]{1,0:T(8,128)(2,1)S(1)}, u32[]{:S(2)}, u32[]{:S(2)}) collective-permute-start(bf16[512,256]{1,0:T(8,128)(2,1)S(1)} %shard_map.115), channel_id=1, source_target_pairs={{0,1},{1,2},{2,3},{3,4},{4,5},{5,6},{6,7},{7,0},{8,9},{9,10},{10,1... | collective-permute-start | bytes 786440 | tf_op jit(solution)/shard_map/ppermute | solution.py:67
  8.4 0.7 copy-start.6
  9.1 0.7 %copy-start.7 = (s32[4,8]{1,0:T(4,128)S(1)}, s32[4,8]{1,0:T(4,128)}, u32[]{:S(2)}) copy-start(s32[4,8]{1,0:T(4,128)} %partner_ref.1) | copy-start | bytes 388
  9.8 0.7 %copy-start.8 = (f32[4,8]{1,0:T(4,128)S(1)}, f32[4,8]{1,0:T(4,128)}, u32[]{:S(2)}) copy-start(f32[4,8]{1,0:T(4,128)} %coupling_ref.1) | copy-start | bytes 388
  10.4 0.7 copy-start.9
  11.1 0.7 copy-start.10
  13.2 4.8 %collective-permute-start = (f32[6]{0:T(128)S(1)}, f32[6]{0:T(128)S(1)}, u32[]{:S(2)}, u32[]{:S(2)}) collective-permute-start(f32[6]{0:T(128)S(1)} %get-tuple-element.30), channel_id=1, source_target_pairs={{0,1},{1,2},{2,3},{3,4},{4,5},{5,6},{6,7},{7,0},{8,9},{9,10},{10,1... | collective-permute-start | bytes 80 | tf_op jit(solution)/shard_map/ppermute | solution.py:67
  13.3 4.9 %collective-permute-start.1 = (f32[6]{0:T(128)S(1)}, f32[6]{0:T(128)S(1)}, u32[]{:S(2)}, u32[]{:S(2)}) collective-permute-start(f32[6]{0:T(128)S(1)} %get-tuple-element.31), channel_id=1, source_target_pairs={{0,7},{1,0},{2,1},{3,2},{4,3},{5,4},{6,5},{7,6},{8,15},{9,8},{10,9... | collective-permute-start | bytes 80 | tf_op jit(solution)/shard_map/ppermute | solution.py:67
  18.2 1.6 %copy-start.2 = (bf16[2,1024,512]{2,1,0:T(8,128)(2,1)S(1)}, bf16[2,1024,512]{2,1,0:T(8,128)(2,1)}, u32[]{:S(2)}) copy-start(bf16[2,1024,512]{2,1,0:T(8,128)(2,1)} %three_ref.3) | copy-start | bytes 6291460
  19.8 4.9 %copy-start.4 = (bf16[4,256,256]{2,1,0:T(8,128)(2,1)S(1)}, bf16[4,256,256]{2,1,0:T(8,128)(2,1)}, u32[]{:S(2)}) copy-start(bf16[4,256,256]{2,1,0:T(8,128)(2,1)} %amps_ref.5) | copy-start | bytes 1572868
  21.0 9.2 %copy-start.3 = (bf16[2,1024,512]{2,1,0:T(8,128)(2,1)S(1)}, bf16[2,1024,512]{2,1,0:T(8,128)(2,1)}, u32[]{:S(2)}) copy-start(bf16[2,1024,512]{2,1,0:T(8,128)(2,1)} %three_ref.3) | copy-start | bytes 6291460
  21.1 9.2 %copy-start.11 = (f32[4,256]{1,0:T(4,128)S(1)}, f32[4,256]{1,0:T(4,128)}, u32[]{:S(2)}) copy-start(f32[4,256]{1,0:T(4,128)} %eps_ref.3) | copy-start | bytes 12292
  21.1 18.3 %collective-permute-start.4 = (bf16[1024,256]{1,0:T(8,128)(2,1)S(1)}, bf16[1024,256]{1,0:T(8,128)(2,1)S(1)}, u32[]{:S(2)}, u32[]{:S(2)}) collective-permute-start(bf16[1024,256]{1,0:T(8,128)(2,1)S(1)} %get-tuple-element.32), channel_id=1, source_target_pairs={{0,1},{1,2},{2,3},{3,4},{4,5},{5,6},{6,7},{7,0},{8,9},{9,10},{10,1... | collective-permute-start | bytes 1572872 | tf_op jit(solution)/shard_map/ppermute | solution.py:67
  21.1 18.3 %collective-permute-start.5 = (bf16[1024,256]{1,0:T(8,128)(2,1)S(1)}, bf16[1024,256]{1,0:T(8,128)(2,1)S(1)}, u32[]{:S(2)}, u32[]{:S(2)}) collective-permute-start(bf16[1024,256]{1,0:T(8,128)(2,1)S(1)} %get-tuple-element.33), channel_id=1, source_target_pairs={{0,7},{1,0},{2,1},{3,2},{4,3},{5,4},{6,5},{7,6},{8,15},{9,8},{10,9... | collective-permute-start | bytes 1572872 | tf_op jit(solution)/shard_map/ppermute | solution.py:67
  26.6 12.8 %collective-permute-start.6 = (bf16[256,256]{1,0:T(8,128)(2,1)S(1)}, bf16[256,256]{1,0:T(8,128)(2,1)S(1)}, u32[]{:S(2)}, u32[]{:S(2)}) collective-permute-start(bf16[256,256]{1,0:T(8,128)(2,1)S(1)} %get-tuple-element.35), channel_id=1, source_target_pairs={{0,1},{1,2},{2,3},{3,4},{4,5},{5,6},{6,7},{7,0},{8,9},{9,10},{10,1... | collective-permute-start | bytes 393224 | tf_op jit(solution)/shard_map/ppermute | solution.py:67
  26.7 12.7 %collective-permute-start.7 = (bf16[256,256]{1,0:T(8,128)(2,1)S(1)}, bf16[256,256]{1,0:T(8,128)(2,1)S(1)}, u32[]{:S(2)}, u32[]{:S(2)}) collective-permute-start(bf16[256,256]{1,0:T(8,128)(2,1)S(1)} %get-tuple-element.36), channel_id=1, source_target_pairs={{0,7},{1,0},{2,1},{3,2},{4,3},{5,4},{6,5},{7,6},{8,15},{9,8},{10,9... | collective-permute-start | bytes 393224 | tf_op jit(solution)/shard_map/ppermute | solution.py:67
  40.3 4.5 %collective-permute-start.14 = (bf16[256,256]{1,0:T(8,128)(2,1)S(1)}, bf16[256,256]{1,0:T(8,128)(2,1)S(1)}, u32[]{:S(2)}, u32[]{:S(2)}) collective-permute-start(bf16[256,256]{1,0:T(8,128)(2,1)S(1)} %get-tuple-element.37.amp_ref.a0.ao_ref), channel_id=1, source_target_pairs={{0,7},{1,0},{2,1},{3,2},{4,3},{5,4},{6,5},{7,6},{8,15},{9,8},{10,9... | collective-permute-start | bytes 393224 | tf_op jit(solution)/shard_map/ppermute | solution.py:67
  40.4 6.3 %collective-permute-start.13 = (bf16[256,256]{1,0:T(8,128)(2,1)S(1)}, bf16[256,256]{1,0:T(8,128)(2,1)S(1)}, u32[]{:S(2)}, u32[]{:S(2)}) collective-permute-start(bf16[256,256]{1,0:T(8,128)(2,1)S(1)} %get-tuple-element.37.amp_ref.a0.ao_ref), channel_id=1, source_target_pairs={{0,1},{1,2},{2,3},{3,4},{4,5},{5,6},{6,7},{7,0},{8,9},{9,10},{10,1... | collective-permute-start | bytes 393224 | tf_op jit(solution)/shard_map/ppermute | solution.py:67
  40.9 13.7 %collective-permute-start.10 = (bf16[256,256]{1,0:T(8,128)(2,1)S(1)}, bf16[256,256]{1,0:T(8,128)(2,1)S(1)}, u32[]{:S(2)}, u32[]{:S(2)}) collective-permute-start(bf16[256,256]{1,0:T(8,128)(2,1)S(1)} %get-tuple-element.37.amp_ref.a0.ao_ref), channel_id=1, source_target_pairs={{0,24},{8,16},{16,8},{24,0},{1,25},{9,17},{17,9},{25,1},{2,26},{10... | collective-permute-start | bytes 393224 | tf_op jit(solution)/shard_map/ppermute | solution.py:70
  43.3 13.3 %collective-permute-start.9 = (bf16[256,256]{1,0:T(8,128)(2,1)S(1)}, bf16[256,256]{1,0:T(8,128)(2,1)S(1)}, u32[]{:S(2)}, u32[]{:S(2)}) collective-permute-start(bf16[256,256]{1,0:T(8,128)(2,1)S(1)} %get-tuple-element.37.amp_ref.a0.ao_ref), channel_id=1, source_target_pairs={{0,16},{8,24},{16,0},{24,8},{1,17},{9,25},{17,1},{25,9},{2,18},{10... | collective-permute-start | bytes 393224 | tf_op jit(solution)/shard_map/ppermute | solution.py:70
  43.9 12.8 %collective-permute-start.8 = (bf16[256,256]{1,0:T(8,128)(2,1)S(1)}, bf16[256,256]{1,0:T(8,128)(2,1)S(1)}, u32[]{:S(2)}, u32[]{:S(2)}) collective-permute-start(bf16[256,256]{1,0:T(8,128)(2,1)S(1)} %get-tuple-element.37.amp_ref.a0.ao_ref), channel_id=1, source_target_pairs={{0,8},{8,0},{16,24},{24,16},{1,9},{9,1},{17,25},{25,17},{2,10},{10... | collective-permute-start | bytes 393224 | tf_op jit(solution)/shard_map/ppermute | solution.py:70
  47.9 14.8 %collective-permute-start.17 = (bf16[256,256]{1,0:T(8,128)(2,1)S(1)}, bf16[256,256]{1,0:T(8,128)(2,1)S(1)}, u32[]{:S(2)}, u32[]{:S(2)}) collective-permute-start(bf16[256,256]{1,0:T(8,128)(2,1)S(1)} %shard_map.122.e0), channel_id=1, source_target_pairs={{0,24},{8,16},{16,8},{1,25},{9,17},{17,9},{2,26},{10,18},{18,10},{... | collective-permute-start | bytes 393224 | tf_op jit(solution)/shard_map/ppermute | solution.py:70
  52.2 10.5 %collective-permute-start.16 = (bf16[256,256]{1,0:T(8,128)(2,1)S(1)}, bf16[256,256]{1,0:T(8,128)(2,1)S(1)}, u32[]{:S(2)}, u32[]{:S(2)}) collective-permute-start(bf16[256,256]{1,0:T(8,128)(2,1)S(1)} %shard_map.122.e0), channel_id=1, source_target_pairs={{0,16},{8,24},{24,8},{1,17},{9,25},{25,9},{2,18},{10,26},{26,10},{... | collective-permute-start | bytes 393224 | tf_op jit(solution)/shard_map/ppermute | solution.py:70
  54.7 8.1 %collective-permute-start.15 = (bf16[256,256]{1,0:T(8,128)(2,1)S(1)}, bf16[256,256]{1,0:T(8,128)(2,1)S(1)}, u32[]{:S(2)}, u32[]{:S(2)}) collective-permute-start(bf16[256,256]{1,0:T(8,128)(2,1)S(1)} %shard_map.122.e0), channel_id=1, source_target_pairs={{0,8},{16,24},{24,16},{1,9},{17,25},{25,17},{2,10},{18,26},{26,18}... | collective-permute-start | bytes 393224 | tf_op jit(solution)/shard_map/ppermute | solution.py:70
  58.0 7.2 %collective-permute-start.11 = (bf16[256,256]{1,0:T(8,128)(2,1)S(1)}, bf16[256,256]{1,0:T(8,128)(2,1)S(1)}, u32[]{:S(2)}, u32[]{:S(2)}) collective-permute-start(bf16[256,256]{1,0:T(8,128)(2,1)S(1)} %get-tuple-element.41), channel_id=1, source_target_pairs={{0,1},{1,2},{2,3},{3,4},{4,5},{5,6},{6,7},{7,0},{8,9},{9,10},{10,1... | collective-permute-start | bytes 393224 | tf_op jit(solution)/shard_map/ppermute | solution.py:67
  58.1 7.2 %collective-permute-start.12 = (bf16[256,256]{1,0:T(8,128)(2,1)S(1)}, bf16[256,256]{1,0:T(8,128)(2,1)S(1)}, u32[]{:S(2)}, u32[]{:S(2)}) collective-permute-start(bf16[256,256]{1,0:T(8,128)(2,1)S(1)} %get-tuple-element.42), channel_id=1, source_target_pairs={{0,7},{1,0},{2,1},{3,2},{4,3},{5,4},{6,5},{7,6},{8,15},{9,8},{10,9... | collective-permute-start | bytes 393224 | tf_op jit(solution)/shard_map/ppermute | solution.py:67

commit v2 on v1

v2 whole, which is shorter than its diff:
```python
import math

import jax
import jax.numpy as jnp
from jax import lax
from jax.experimental import pallas as pl
from jax.experimental.pallas import tpu as pltpu
from jax.sharding import PartitionSpec as P

F32 = jnp.float32
BF16 = jnp.bfloat16
I32 = jnp.int32
NN = ((1,), (0,))
NT = ((1,), (1,))

VMEM = pl.BlockSpec(memory_space=pltpu.VMEM)
SMEM = pl.BlockSpec(memory_space=pltpu.SMEM)
ANY = pl.BlockSpec(memory_space=pl.ANY)
HBM = pl.BlockSpec(memory_space=pltpu.HBM)

MINE, EXTRA, OWNER, FIRST, SECOND, WHOSE, NV_MINE, NV_EXTRA, ROLE_PAIR = range(9)


def mxu(a, b, dims):
    return lax.dot_general(a, b, (dims, ((), ())), preferred_element_type=F32)


def call(body, ins, outs, args, scratch=(), flops=0, vmem=48):
    moved = sum(a.size * a.dtype.itemsize for a in args)
    return pl.pallas_call(
        body,
        in_specs=ins,
        out_specs=[spec for spec, _, _ in outs],
        out_shape=[jax.ShapeDtypeStruct(shape, dtype) for _, shape, dtype in outs],
        scratch_shapes=list(scratch),
        cost_estimate=pl.CostEstimate(flops=flops, bytes_accessed=moved, transcendentals=0),
        compiler_params=pltpu.CompilerParams(vmem_limit_bytes=vmem * 1024 * 1024),
    )(*args)


def local(
    three_index, coeff, amps, eps_virt, eps_occ, nvirt, pair_occ, partners, coupling, pair_owner
):
    columns = lax.axis_size("pairs")
    roles = lax.axis_size("role")
    occ_block, aux, pao = three_index.shape
    pairs, _, virt = coeff.shape
    partner_count = partners.shape[1]
    slots = 2
    assert roles == pairs and columns % 2 == 0
    tile = min(256, aux)
    pao_scale = 1.0 / math.sqrt(pao)
    aux_scale = 1.0 / math.sqrt(aux)
    virt_scale = 1.0 / math.sqrt(virt)
    square = (virt, virt)
    sq_b = (VMEM, square, BF16)
    sq_f = (VMEM, square, F32)
    two_b = (VMEM, (2, virt, virt), BF16)
    all_s = (VMEM, (pairs, virt, virt), BF16)
    orb = (VMEM, (pao, virt), BF16)

    def inner(x):
        return lax.ppermute(x, "pairs", [(i, i ^ 1) for i in range(columns)])

    def outer(x):
        return lax.ppermute(
            x, "pairs", [(i, (i + (1 if i % 2 else -1)) % columns) for i in range(columns)]
        )

    def swap(x, by):
        return lax.ppermute(x, "role", [(i, i ^ by) for i in range(roles)])

    weights = 2 * pairs

    def plan_body(
        owner_hbm, occ_hbm, partner_hbm, coupling_hbm, eps_hbm, nvirt_hbm, coeff_hbm,
        mine_ref, extra_ref, to_inner, to_outer, ints, floats,
        owner_ref, occ_ref, partner_ref, coupling_ref, eps_ref, nvirt_ref, near_w, sems,
    ):
        small = [
            pltpu.make_async_copy(source, target, sems.at[at])
            for at, (source, target) in enumerate(
                (
                    (owner_hbm, owner_ref),
                    (occ_hbm, occ_ref),
                    (partner_hbm, partner_ref),
                    (coupling_hbm, coupling_ref),
                    (eps_hbm, eps_ref),
                    (nvirt_hbm, nvirt_ref),
                )
            )
        ]
        for copy in small:
            copy.start()
        role = lax.axis_index("role")
        column = lax.axis_index("pairs")
        small[0].wait()
        of_role = [jnp.int32(0)] * roles
        for p in range(pairs):
            earlier = jnp.int32(0)
            for o in range(p):
                earlier += (owner_ref[o] == owner_ref[p]).astype(I32)
            for s in range(roles):
                hit = (earlier == 0) & (owner_ref[p] == s) if s else earlier == 1
                of_role[s] = jnp.where(hit, p, of_role[s])
        extra = of_role[0]
        mine = extra
        for s in range(1, roles):
            mine = jnp.where(role == s, of_role[s], mine)
        large = [
            pltpu.make_async_copy(coeff_hbm.at[mine], mine_ref, sems.at[6]),
            pltpu.make_async_copy(coeff_hbm.at[extra], extra_ref, sems.at[7]),
        ]
        for copy in large:
            copy.start()
        for copy in small[1:]:
            copy.wait()
        ints[MINE] = mine
        ints[EXTRA] = extra
        ints[OWNER] = owner_ref[extra]
        for s in range(roles):
            ints[ROLE_PAIR + s] = of_role[s]
        ints[NV_MINE] = nvirt_ref[mine]
        ints[NV_EXTRA] = nvirt_ref[extra]
        ints[FIRST] = occ_ref[0, mine] - column * occ_block
        odd = lax.rem(column, 2) == 1
        inner_at = jnp.where(odd, 0, 2)
        outer_at = 2 - inner_at
        occ_all = occ_block * columns
        second = lax.rem(occ_ref[1, mine] - (column - 1) * occ_block + occ_all, occ_all)
        block = (second >= occ_block).astype(I32) + (second >= 2 * occ_block).astype(I32)
        ints[SECOND] = second - block * occ_block
        ints[WHOSE] = jnp.where(block == 1, 0, jnp.where(block == inner_at, 1, 2))
        floats[weights] = eps_ref[occ_ref[0, mine]] + eps_ref[occ_ref[1, mine]]
        floats[weights + 1] = eps_ref[occ_ref[0, extra]] + eps_ref[occ_ref[1, extra]]
        pair_all = pairs * columns
        for which, pair in enumerate((mine, extra)):
            for q in range(3 * pairs):
                near_w[q] = jnp.float32(0)
            for k in range(partner_count):
                at = lax.rem(partner_ref[pair, k] - (column - 1) * pairs + pair_all, pair_all)
                near_w[at] += coupling_ref[pair, k]
            for q in range(pairs):
                to = which * pairs + q
                to_inner[to] = near_w[inner_at * pairs + q]
                floats[to] = near_w[pairs + q]
                to_outer[to] = near_w[outer_at * pairs + q]
        to_inner[weights] = ints[SECOND].astype(F32)
        to_outer[weights] = ints[SECOND].astype(F32)
        for copy in large:
            copy.wait()

    meta = (SMEM, (weights + 1,), F32)
    x_mine, x_extra, to_inner, to_outer, ints, floats = call(
        plan_body,
        [HBM] * 7,
        [
            (ANY, (pao, virt), BF16),
            (ANY, (pao, virt), BF16),
            meta,
            meta,
            (SMEM, (ROLE_PAIR + roles,), I32),
            (SMEM, (weights + 2,), F32),
        ],
        (pair_owner, pair_occ.T, partners, coupling, eps_occ, nvirt, coeff),
        scratch=[
            pltpu.SMEM(pair_owner.shape, I32),
            pltpu.SMEM(pair_occ.shape[::-1], I32),
            pltpu.SMEM(partners.shape, I32),
            pltpu.SMEM(coupling.shape, F32),
            pltpu.SMEM(eps_occ.shape, F32),
            pltpu.SMEM(nvirt.shape, I32),
            pltpu.SMEM((3 * pairs,), F32),
            pltpu.SemaphoreType.DMA((8,)),
        ],
        vmem=60,
    )
    x_out = outer(x_mine)
    of_out = outer(to_outer)
    x_in = inner(x_mine)
    of_in = inner(to_inner)
    x_extra_in = inner(x_extra)

    def overlaps(x, coeff_ref, out_ref):
        turned = x.T
        for q in range(pairs):
            s = mxu(turned, coeff_ref[q], NN) * (1.0 / pao)
            out_ref[q] = s.astype(BF16)

    def coupled(s_ref, parts):
        total = None
        for at, weight, amp in parts:
            s = s_ref[at]
            middle = mxu(s, amp, NN).astype(BF16)
            term = weight * mxu(middle, s, NT)
            total = term if total is None else total + term
        return total

    def half_into(y_ref, three_ref, at_occ, x):
        for at in range(0, aux, tile):
            rows = pl.ds(at, tile)
            y_ref[rows, :] = (mxu(three_ref[at_occ, rows, :], x, NN) * pao_scale).astype(BF16)

    def own_body(
        ints, floats, three_ref, coeff_ref, amps_ref, eps_ref,
        first_ref, second_ref, s_ref, se_ref, c_ref, gain_ref, gain_extra_ref,
    ):
        mine = ints[MINE]
        x = coeff_ref[mine]
        turned = x.T
        first = ints[FIRST]
        for at in range(0, aux, tile):
            rows = pl.ds(at, tile)
            first_ref[:, rows] = (mxu(turned, three_ref[first, rows, :], NT) * pao_scale).astype(BF16)
        half_into(second_ref, three_ref, ints[SECOND], x)
        overlaps(x, coeff_ref, s_ref)
        overlaps(coeff_ref[ints[EXTRA]], coeff_ref, se_ref)
        c_ref[...] = coupled(s_ref, [(q, floats[q], amps_ref[q]) for q in range(pairs)])

        def gain(pair, count, shift_at):
            row = jnp.broadcast_to(eps_ref[pl.ds(pair, 1), :], square)
            energy = row + row.T - floats[shift_at]
            inside = (lax.broadcasted_iota(I32, square, 0) < count) & (
                lax.broadcasted_iota(I32, square, 1) < count
            )
            return jnp.where(inside, 1.0 / (energy + 1.0), 0.0)

        gain_ref[...] = gain(mine, ints[NV_MINE], weights)
        gain_extra_ref[...] = gain(ints[EXTRA], ints[NV_EXTRA], weights + 1)

    half = (VMEM, (aux, virt), BF16)
    first_t, second_own, s_own, se_own, c_own, gain, gain_extra = call(
        own_body,
        [SMEM, SMEM, VMEM, VMEM, VMEM, VMEM],
        [(VMEM, (virt, aux), BF16), half, all_s, all_s, sq_f, sq_f, sq_f],
        (ints, floats, three_index, coeff, amps, eps_virt),
        flops=2 * virt * (2 * aux * pao + pairs * virt * (2 * pao + 2 * virt)),
    )

    def inner_body(of, three_ref, coeff_ref, amps_ref, x_ref, xe_ref, y_ref, s_ref, se_ref, c_ref):
        half_into(y_ref, three_ref, of[weights].astype(I32), x_ref[...])
        overlaps(x_ref[...], coeff_ref, s_ref)
        overlaps(xe_ref[...], coeff_ref, se_ref)
        c = coupled(s_ref, [(q, of[q], amps_ref[q]) for q in range(pairs)])
        c_ref[...] = c.astype(BF16)

    y_in, s_in, se_in, c_in = call(
        inner_body,
        [SMEM] + [VMEM] * 5,
        [half, all_s, all_s, sq_b],
        (of_in, three_index, coeff, amps, x_in, x_extra_in),
        flops=2 * virt * (aux * pao + pairs * virt * (2 * pao + 2 * virt)),
    )
    y_from_in = inner(y_in)
    c_from_in = inner(c_in)

    def outer_half_body(of, three_ref, x_ref, own_ref, in_ref, y_ref):
        half_into(y_ref, three_ref, of[weights].astype(I32), x_ref[...])

    (y_out,) = call(
        outer_half_body,
        [SMEM, VMEM, VMEM, ANY, ANY],
        [half],
        (of_out, three_index, x_out, first_t, y_in),
        flops=2 * aux * pao * virt,
    )
    y_from_out = outer(y_out)

    def outer_body(of, coeff_ref, amps_ref, x_ref, s_ref, c_ref):
        overlaps(x_ref[...], coeff_ref, s_ref)
        c = coupled(s_ref, [(q, of[q], amps_ref[q]) for q in range(pairs)])
        c_ref[...] = c.astype(BF16)

    s_out, c_out = call(
        outer_body,
        [SMEM, VMEM, VMEM, VMEM],
        [all_s, sq_b],
        (of_out, coeff, amps, x_out),
        flops=2 * pairs * virt * virt * (pao + 2 * virt),
    )
    c_from_out = outer(c_out)

    x_sent, _ = lax.optimization_barrier((x_out, y_out))
    x_extras = [lax.ppermute(x_sent, "role", [(0, s)]) for s in range(1, roles)]

    def first_body(
        ints, first_ref, own_ref, in_ref, out_ref, amps_ref, c_ref, ci_ref, co_ref, gain_ref,
        amp_ref, k_ref, held, sem,
    ):
        for whose, source in enumerate((own_ref, in_ref, out_ref)):

            @pl.when(ints[WHOSE] == whose)
            def _():
                copy = pltpu.make_async_copy(source, held, sem)
                copy.start()
                copy.wait()

        k = mxu(first_ref[...], held[...], NN) * aux_scale
        k_ref[...] = k
        c = c_ref[...] + ci_ref[...].astype(F32) + co_ref[...].astype(F32)
        old = amps_ref[ints[MINE]].astype(F32)
        amp_ref[...] = (gain_ref[...] * (old - k - c)).astype(BF16)

    amp, k_first = call(
        first_body,
        [SMEM, VMEM, ANY, ANY, ANY, VMEM, VMEM, VMEM, VMEM, VMEM],
        [sq_b, sq_f],
        (
            ints, first_t, second_own, y_from_in, y_from_out,
            amps, c_own, c_from_in, c_from_out, gain,
        ),
        scratch=[pltpu.VMEM((aux, virt), BF16), pltpu.SemaphoreType.DMA],
        flops=2 * aux * virt * virt,
    )
    amp_roles = [amp] + [swap(amp, m) for m in range(1, roles)]

    def second_body(amp_ref, k_ref, out_ref, out_b_ref):
        amp = amp_ref[...]
        k = k_ref[...]
        right = k + mxu(k.astype(BF16), amp, NN) * virt_scale
        both = right + mxu(amp.T, right.astype(BF16), NN) * virt_scale
        rest = amp.astype(F32) - both
        out_ref[...] = rest
        out_b_ref[...] = rest.astype(BF16)

    rest, rest_b = call(
        second_body, [VMEM, VMEM], [sq_f, sq_b], (amp, k_first), flops=4 * virt * virt * virt
    )
    rests = [lax.ppermute(rest_b, "role", [(0, s)]) for s in range(1, roles)]

    def outer_extra_body(s_near_ref, coeff_ref, after_ref, *refs):
        x_refs, s_ref = refs[:-1], refs[-1]
        role = lax.axis_index("role")

        @pl.when(role == 0)
        def _():
            s_ref[...] = s_near_ref[...]

        for s in range(1, roles):

            @pl.when(role == s)
            def _():
                overlaps(x_refs[s - 1][...], coeff_ref, s_ref)

    (se_out,) = call(
        outer_extra_body,
        [VMEM, VMEM, ANY] + [VMEM] * (roles - 1),
        [all_s],
        (s_out, coeff, rest, *x_extras),
        flops=2 * pairs * virt * virt * pao,
    )

    def parts_of(ints, weight_ref, first_weight, amp_refs):
        role = lax.axis_index("role")
        parts = []
        for m in range(roles):
            at = ints[ROLE_PAIR + (role ^ m)]
            parts.append((at, weight_ref[first_weight + at], amp_refs[m][...]))
        return parts

    def near_again_body(ints, of, s_ref, se_ref, *refs):
        amp_refs, c_ref = refs[:roles], refs[roles]
        c_ref[0] = coupled(s_ref, parts_of(ints, of, 0, amp_refs)).astype(BF16)
        c_ref[1] = coupled(se_ref, parts_of(ints, of, pairs, amp_refs)).astype(BF16)

    def near_again(of, s, se):
        (c,) = call(
            near_again_body,
            [SMEM, SMEM] + [VMEM] * (2 + roles),
            [two_b],
            (ints, of, s, se, *amp_roles),
            flops=8 * pairs * virt * virt * virt,
        )
        return c

    cc_from_out = outer(near_again(of_out, s_out, se_out))
    cc_from_in = inner(near_again(of_in, s_in, se_in))

    def own_again_body(ints, floats, s_ref, se_ref, rest_ref, *refs):
        amp_refs, rest_refs, (out_ref, out_extra_ref) = (
            refs[:roles], refs[roles : 2 * roles - 1], refs[2 * roles - 1 :],
        )
        out_ref[...] = rest_ref[...] - coupled(s_ref, parts_of(ints, floats, 0, amp_refs))
        role = lax.axis_index("role")
        total = -coupled(se_ref, parts_of(ints, floats, pairs, amp_refs))
        for s in range(1, roles):
            total += jnp.where(role == s, rest_refs[s - 1][...].astype(F32), 0.0)
        out_extra_ref[...] = total

    rest, rest_extra = call(
        own_again_body,
        [SMEM] * 2 + [VMEM] * (3 + 2 * roles - 1),
        [sq_f, sq_f],
        (ints, floats, s_own, se_own, rest, *amp_roles, *rests),
        flops=8 * pairs * virt * virt * virt,
    )

    def last_body(
        ints, coeff_ref, gain_ref, gain_extra_ref, rest_ref, rest_extra_ref, ci_ref, co_ref, amp_ref, orb_ref
    ):
        role = lax.axis_index("role")

        def store(slot, here, gain, rest, pair):
            @pl.when(here)
            def _():
                c = ci_ref[slot].astype(F32) + co_ref[slot].astype(F32)
                amp = (gain[...] * (rest[...] - c)).astype(BF16)
                amp_ref[slot] = amp
                x = coeff_ref[pair]
                orb_ref[slot] = (x.astype(F32) + mxu(x, amp, NN) * virt_scale).astype(BF16)

            @pl.when(jnp.logical_not(here))
            def _():
                amp_ref[slot] = jnp.zeros(square, BF16)
                orb_ref[slot] = jnp.zeros((pao, virt), BF16)

        store(0, role > 0, gain_ref, rest_ref, ints[MINE])
        store(1, role == ints[OWNER], gain_extra_ref, rest_extra_ref, ints[EXTRA])

    amps_out, dressed_out = call(
        last_body,
        [SMEM] + [VMEM] * 7,
        [(VMEM, (slots, virt, virt), BF16), (VMEM, (slots, pao, virt), BF16)],
        (ints, coeff, gain, gain_extra, rest, rest_extra, cc_from_in, cc_from_out),
        flops=4 * pao * virt * virt,
    )
    return amps_out, dressed_out


def solution(mesh):
    in_specs = (
        P("pairs", None, None),
        P("pairs", None, None),
        P("pairs", None, None),
        P("pairs", None),
        P(),
        P("pairs"),
        P("pairs", None),
        P("pairs", None),
        P("pairs", None),
        P("pairs"),
    )
    out_specs = (P(("role", "pairs"), None, None), P(("role", "pairs"), None, None))
    return jax.shard_map(local, mesh=mesh, in_specs=in_specs, out_specs=out_specs, check_vma=False)
```

time: 67.1 us -> 85.4 us (1.27)
  Pallas kernels: 13.6 us -> 33 us
  local copies, waits for them, and re-layouts: 7.58 us -> 4.18 us
  waiting for transfers between devices: 13 us -> 15.8 us
    pallas_call x11 -> x12, Pallas kernels: 13.6 us -> 33 us  [call(): pl.pallas_call(body, in_specs=ins, out_specs=[spec for spec, _, _ in outs...]
    unnamed x25 -> x20, local copies, waits for them, and re-layouts: 7.58 us -> 4.18 us
    ppermute x18 -> x20, waiting for transfers between devices: 13 us -> 15.8 us  [the longest x5 8.99 us: outer(): lax.ppermute(x, 'pairs', [(i, (i + (1 if i % 2 else -1)) % columns) for i...]
    ppermute x18 -> x20, starting transfers between devices: 31.7 us -> 31 us  [the longest x5 11.4 us: outer(): lax.ppermute(x, 'pairs', [(i, (i + (1 if i % 2 else -1)) % columns) for i...]
  transfers between devices with their start and end apart: 18 -> 20, of which waited for: 5 -> 5; matrix products, arithmetic and copies ran while one was open for 1% -> 0% of each run, Pallas kernels for 14% -> 14%
where the time goes in v2:
time: 85.4 us; the launch traced here: 85 us
  Pallas kernels  33 us (39%)
  starting transfers between devices  31 us (36%)
  waiting for transfers between devices  15.8 us (19%)
  local copies, waits for them, and re-layouts  4.18 us (5%)
  between operations  0.96 us (1%)
    pallas_call x12, Pallas kernels, call(): pl.pallas_call(body, in_specs=ins, out_specs=[spec for spec, _, _ in outs...  33 us
    ppermute x5, starting transfers between devices, outer(): lax.ppermute(x, 'pairs', [(i, (i + (1 if i % 2 else -1)) % columns) for i...  11.4 us
    ppermute x3, starting transfers between devices, local(): x_extras = [lax.ppermute(x_sent, 'role', [(0, s)]) for s in range(1, roles)]  9.06 us
    ppermute x5, waiting for transfers between devices, outer(): lax.ppermute(x, 'pairs', [(i, (i + (1 if i % 2 else -1)) % columns) for i...  8.99 us
    ppermute x3, starting transfers between devices, local(): rests = [lax.ppermute(rest_b, 'role', [(0, s)]) for s in range(1, roles)]  6.32 us
    unnamed x20, local copies, waits for them, and re-layouts  4.18 us
    ppermute x3, starting transfers between devices, swap(): return lax.ppermute(x, 'role', [(i, i ^ by) for i in range(roles)])  3.53 us
    ppermute x3, waiting for transfers between devices, swap(): return lax.ppermute(x, 'role', [(i, i ^ by) for i in range(roles)])  2.74 us
  transfers between devices with their start and end apart: 20, of which 5 were waited for; matrix products, arithmetic and copies ran while one was open for 0% of the time, Pallas kernels for 14%

profile of v2, /device:TPU:0, one launch (start us, length us, event | category | flops | bytes accessed | tf_op | source)
XLA Modules:
  0.0 85.0 jit_solution(3641396482187067681)
XLA Ops:
  0.6 18.3 %shard_map.113 = (bf16[512,256]{1,0:T(8,128)(2,1)}, bf16[512,256]{1,0:T(8,128)(2,1)}, f32[9]{0:T(128)}, f32[9]{0:T(128)}, s32[12]{0:T(128)}, /*index=5*/f32[10]{0:T(128)}) custom-call(s32[4]{0:T(128)} %owner_hbm.1, s32[2,4]{1,0:T(2,128)} %bitcast.1, s32[4,8]{1,0:T(4,128)} %partner_hbm.1, f32[4,8]{1,0:T(4,128)} %coupling_hbm.1, f32[16]{0:T(128)} %eps_hbm.1, ...), custom_call_target="tpu_custom_call" | custom-call | bytes 1048960 | tf_op jit(solution)/shard_map/pallas_call | solution.py:30
  18.9 0.5 collective-permute-start.1
  19.4 0.1 collective-permute-start.2
  19.5 4.7 %collective-permute-start.5 = (bf16[512,256]{1,0:T(8,128)(2,1)}, bf16[512,256]{1,0:T(8,128)(2,1)S(1)}, u32[]{:S(2)}, u32[]{:S(2)}) collective-permute-start(bf16[512,256]{1,0:T(8,128)(2,1)} %get-tuple-element.37), channel_id=1, source_target_pairs={{0,7},{1,2},{2,1},{3,4},{4,3},{5,6},{6,5},{7,0},{8,15},{9,10},{10,... | collective-permute-start | bytes 786440 | tf_op jit(solution)/shard_map/ppermute | solution.py:66
  24.2 0.0 collective-permute-start
  24.2 0.6 collective-permute-start.4
  24.8 1.2 %copy-done = bf16[4,512,256]{2,1,0:T(8,128)(2,1)S(1)} copy-done((bf16[4,512,256]{2,1,0:T(8,128)(2,1)S(1)}, bf16[4,512,256]{2,1,0:T(8,128)(2,1)}, u32[]{:S(2)}) %copy-start) | copy-done | bytes 1048600
  26.0 1.0 %copy-done.3 = bf16[4,256,256]{2,1,0:T(8,128)(2,1)S(1)} copy-done((bf16[4,256,256]{2,1,0:T(8,128)(2,1)S(1)}, bf16[4,256,256]{2,1,0:T(8,128)(2,1)}, u32[]{:S(2)}) %copy-start.3) | copy-done | bytes 524312
  27.1 0.6 copy-done.5
  27.7 0.6 copy-done.7
  28.3 0.7 copy-done.9
  29.0 3.5 %shard_map.114 = (bf16[256,1024]{1,0:T(8,128)(2,1)S(1)}, bf16[1024,256]{1,0:T(8,128)(2,1)S(1)}, bf16[4,256,256]{2,1,0:T(8,128)(2,1)S(1)}, bf16[4,256,256]{2,1,0:...) custom-call(s32[12]{0:T(128)S(1)} %copy-done.5, f32[10]{0:T(128)S(1)} %copy-done.7, ...), custom_call_target="tpu_custom_call" | custom-call | flops 1342177280 | bytes 3674200 | tf_op jit(solution)/shard_map/pallas_call | solution.py:30
  32.4 0.0 collective-permute-done.of
  32.4 0.0 collective-permute-done.1.x_ref
  32.4 0.0 collective-permute-done.2.xe_ref
  32.5 0.0 copy-done.2
  32.5 1.9 %shard_map.115 = (bf16[1024,256]{1,0:T(8,128)(2,1)S(1)}, bf16[4,256,256]{2,1,0:T(8,128)(2,1)S(1)}, bf16[4,256,256]{2,1,0:T(8,128)(2,1)S(1)}, bf16[256,256]{1,0:T(8,128)(2,1)S(1)}) custom-call(f32[9]{0:T(128)S(1)} %collective-permute-done.of, bf16[2,1024,512]{2,1,0:T(8,128)(2,1)S(1)} %copy-done.2, bf16[4,512,256]{2,1,0:T(8,128)(2,1)S(1)} %copy-done, ...), custom_call_target="tpu_custom_call" | custom-call | flops 1073741824 | bytes 4194340 | tf_op jit(solution)/shard_map/pallas_call | solution.py:30
  34.4 0.0 copy-start.1
  34.4 0.0 copy-start.4
  34.4 0.1 collective-permute-start.3
  34.5 0.0 collective-permute-done.4.of
  34.5 0.0 collective-permute-done.5.x_ref
  34.5 0.0 copy-start.6
  34.5 1.0 %shard_map.116 = bf16[1024,256]{1,0:T(8,128)(2,1)S(1)} custom-call(f32[9]{0:T(128)S(1)} %collective-permute-done.4.of, bf16[2,1024,512]{2,1,0:T(8,128)(2,1)S(1)} %copy-done.2, bf16[512,256]{1,0:T(8,128)(2,1)S(1)} %collective-permute-done.5.x_ref, bf16[256,1024]{1,0:T(8,128)(2,1)S(1)} %get-tuple-element.34.own_ref.first_ref, ...), custom_call_target="tpu_custom_call" | custom-call | flops 268435456 | bytes 3407908 | tf_op jit(solution)/shard_map/pallas_call | solution.py:30
  35.5 3.0 %collective-permute-start.6 = (bf16[1024,256]{1,0:T(8,128)(2,1)S(1)}, bf16[1024,256]{1,0:T(8,128)(2,1)S(1)}, u32[]{:S(2)}, u32[]{:S(2)}) collective-permute-start(bf16[1024,256]{1,0:T(8,128)(2,1)S(1)} %shard_map.116), channel_id=1, source_target_pairs={{0,7},{1,2},{2,1},{3,4},{4,3},{5,6},{6,5},{7,0},{8,15},{9,10},{10,... | collective-permute-start | bytes 1572872 | tf_op jit(solution)/shard_map/ppermute | solution.py:66
  38.6 0.0 collective-permute-start.7
  38.6 0.0 copy-done.1
  38.6 0.0 copy-done.4
  38.6 1.4 %shard_map.117 = (bf16[4,256,256]{2,1,0:T(8,128)(2,1)S(1)}, bf16[256,256]{1,0:T(8,128)(2,1)S(1)}) custom-call(f32[9]{0:T(128)S(1)} %collective-permute-done.4.of, bf16[4,512,256]{2,1,0:T(8,128)(2,1)S(1)} %copy-done.1, bf16[4,256,256]{2,1,0:T(8,128)(2,1)S(1)} %copy-done.4, bf16[512,256]{1,0:T(8,128)(2,1)S(1)} %collective-permute-done.5.x_ref), custom_call_target="tpu_custom_call" | custom-call | flops 536870912 | bytes 1835044 | tf_op jit(solution)/shard_map/pallas_call | solution.py:30
  40.0 0.6 collective-permute-start.8
  40.6 3.4 %collective-permute-start.16 = (bf16[512,256]{1,0:T(8,128)(2,1)S(1)}, bf16[512,256]{1,0:T(8,128)(2,1)S(1)}, u32[]{:S(2)}, u32[]{:S(2)}) collective-permute-start(bf16[512,256]{1,0:T(8,128)(2,1)S(1)} %collective-permute-done.5.x_ref), channel_id=1, source_target_pairs={{0,8},{1,9},{2,10},{3,11},{4,12},{5,13},{6,14},{7,15}} | collective-permute-start | bytes 786440 | tf_op jit(solution)/shard_map/ppermute | solution.py:284
  44.0 0.0 collective-permute-done.7.ci_ref
  44.0 1.3 %collective-permute-start.17 = (bf16[512,256]{1,0:T(8,128)(2,1)S(1)}, bf16[512,256]{1,0:T(8,128)(2,1)S(1)}, u32[]{:S(2)}, u32[]{:S(2)}) collective-permute-start(bf16[512,256]{1,0:T(8,128)(2,1)S(1)} %collective-permute-done.5.x_ref), channel_id=1, source_target_pairs={{0,16},{1,17},{2,18},{3,19},{4,20},{5,21},{6,22},{7,23}} | collective-permute-start | bytes 786440 | tf_op jit(solution)/shard_map/ppermute | solution.py:284
  45.3 9.0 %collective-permute-done.8.co_ref = bf16[256,256]{1,0:T(8,128)(2,1)S(1)} collective-permute-done((bf16[256,256]{1,0:T(8,128)(2,1)S(1)}, bf16[256,256]{1,0:T(8,128)(2,1)S(1)}, u32[]{:S(2)}, u32[]{:S(2)}) %collective-permute-start.8) | collective-permute-done | bytes 131104 | tf_op jit(solution)/shard_map/ppermute | solution.py:66
  54.3 4.4 %collective-permute-start.18 = (bf16[512,256]{1,0:T(8,128)(2,1)S(1)}, bf16[512,256]{1,0:T(8,128)(2,1)S(1)}, u32[]{:S(2)}, u32[]{:S(2)}) collective-permute-start(bf16[512,256]{1,0:T(8,128)(2,1)S(1)} %collective-permute-done.5.x_ref), channel_id=1, source_target_pairs={{0,24},{1,25},{2,26},{3,27},{4,28},{5,29},{6,30},{7,31}} | collective-permute-start | bytes 786440 | tf_op jit(solution)/shard_map/ppermute | solution.py:284
  58.7 0.0 collective-permute-done.3.in_ref
  58.7 0.0 collective-permute-done.6.out_ref
  58.7 0.0 copy-done.6
  58.7 0.9 %shard_map.118 = (bf16[256,256]{1,0:T(8,128)(2,1)S(1)}, f32[256,256]{1,0:T(8,128)S(1)}) custom-call(s32[12]{0:T(128)S(1)} %copy-done.6, bf16[256,1024]{1,0:T(8,128)(2,1)S(1)} %get-tuple-element.34.own_ref.first_ref, bf16[1024,256]{1,0:T(8,128)(2,1)S(1)} %get-tuple-element.35.own_ref, bf16[1024,256]{1,0:T(8,128)(2,1)S(1)} %collective-permute-done.3.in_ref, ...), custom_call_target="tpu_custom_call" | custom-call | flops 134217728 | bytes 3407920 | tf_op jit(solution)/shard_map/pallas_call | solution.py:30
  59.6 0.1 collective-permute-start.9
  59.7 0.1 collective-permute-start.10
  59.8 0.0 collective-permute-done.16.refs_0_
  59.8 3.4 %collective-permute-start.11 = (bf16[256,256]{1,0:T(8,128)(2,1)S(1)}, bf16[256,256]{1,0:T(8,128)(2,1)S(1)}, u32[]{:S(2)}, u32[]{:S(2)}) collective-permute-start(bf16[256,256]{1,0:T(8,128)(2,1)S(1)} %get-tuple-element.44.amp_ref.refs_0_), channel_id=1, source_target_pairs={{0,24},{8,16},{16,8},{24,0},{1,25},{9,17},{17,9},{25,1},{2,26},{10... | collective-permute-start | bytes 393224 | tf_op jit(solution)/shard_map/ppermute | solution.py:71
  63.2 0.4 shard_map.119
  63.6 0.0 collective-permute-done.17.refs_1_
  63.6 1.6 %collective-permute-done.18.refs_2_ = bf16[512,256]{1,0:T(8,128)(2,1)S(1)} collective-permute-done((bf16[512,256]{1,0:T(8,128)(2,1)S(1)}, bf16[512,256]{1,0:T(8,128)(2,1)S(1)}, u32[]{:S(2)}, u32[]{:S(2)}) %collective-permute-start.18) | collective-permute-done | bytes 262176 | tf_op jit(solution)/shard_map/ppermute | solution.py:284
  65.3 0.0 copy-start.8
  65.3 1.3 %collective-permute-done.9.refs_1_ = bf16[256,256]{1,0:T(8,128)(2,1)S(1)} collective-permute-done((bf16[256,256]{1,0:T(8,128)(2,1)S(1)}, bf16[256,256]{1,0:T(8,128)(2,1)S(1)}, u32[]{:S(2)}, u32[]{:S(2)}) %collective-permute-start.9) | collective-permute-done | bytes 131104 | tf_op jit(solution)/shard_map/ppermute | solution.py:71
  66.6 0.0 collective-permute-done.10.refs_2_
  66.6 1.4 %collective-permute-done.11.refs_3_ = bf16[256,256]{1,0:T(8,128)(2,1)S(1)} collective-permute-done((bf16[256,256]{1,0:T(8,128)(2,1)S(1)}, bf16[256,256]{1,0:T(8,128)(2,1)S(1)}, u32[]{:S(2)}, u32[]{:S(2)}) %collective-permute-start.11) | collective-permute-done | bytes 131104 | tf_op jit(solution)/shard_map/ppermute | solution.py:71
  68.0 1.4 %shard_map.121 = bf16[2,256,256]{2,1,0:T(8,128)(2,1)S(1)} custom-call(s32[12]{0:T(128)S(1)} %copy-done.6, f32[9]{0:T(128)S(1)} %collective-permute-done.of, bf16[4,256,256]{2,1,0:T(8,128)(2,1)S(1)} %get-tuple-element.50.s_ref, bf16[4,256,256]{2,1,0:T(8,128)(2,1)S(1)} %get-tuple-element.51.se_ref, bf16[256,256]{1,0:T(8,128)(2,1)S(1)} %get-tuple-element.44.amp_ref.refs_0_, ...), custom_call_target="tpu_custom_call" | custom-call | flops 536870912 | bytes 1572948 | tf_op jit(solution)/shard_map/pallas_call | solution.py:30
  69.4 0.1 collective-permute-start.15
  69.5 1.4 %shard_map.123 = bf16[2,256,256]{2,1,0:T(8,128)(2,1)S(1)} custom-call(s32[12]{0:T(128)S(1)} %copy-done.6, f32[9]{0:T(128)S(1)} %collective-permute-done.4.of, bf16[4,256,256]{2,1,0:T(8,128)(2,1)S(1)} %get-tuple-element.52.s_near_ref.s_ref, bf16[4,256,256]{2,1,0:T(8,128)(2,1)S(1)} %shard_map.122.se_ref, ...), custom_call_target="tpu_custom_call" | custom-call | flops 536870912 | bytes 1572948 | tf_op jit(solution)/shard_map/pallas_call | solution.py:30
  70.8 2.4 %collective-permute-start.19 = (bf16[2,256,256]{2,1,0:T(8,128)(2,1)S(1)}, bf16[2,256,256]{2,1,0:T(8,128)(2,1)S(1)}, u32[]{:S(2)}, u32[]{:S(2)}) collective-permute-start(bf16[2,256,256]{2,1,0:T(8,128)(2,1)S(1)} %shard_map.123), channel_id=1, source_target_pairs={{0,7},{1,2},{2,1},{3,4},{4,3},{5,6},{6,5},{7,0},{8,15},{9,10},{10,... | collective-permute-start | bytes 786440 | tf_op jit(solution)/shard_map/ppermute | solution.py:66
  73.2 2.1 %collective-permute-start.12 = (bf16[256,256]{1,0:T(8,128)(2,1)S(1)}, bf16[256,256]{1,0:T(8,128)(2,1)S(1)}, u32[]{:S(2)}, u32[]{:S(2)}) collective-permute-start(bf16[256,256]{1,0:T(8,128)(2,1)S(1)} %get-tuple-element.47), channel_id=1, source_target_pairs={{0,8},{1,9},{2,10},{3,11},{4,12},{5,13},{6,14},{7,15}} | collective-permute-start | bytes 393224 | tf_op jit(solution)/shard_map/ppermute | solution.py:329
  75.4 1.3 %collective-permute-start.13 = (bf16[256,256]{1,0:T(8,128)(2,1)S(1)}, bf16[256,256]{1,0:T(8,128)(2,1)S(1)}, u32[]{:S(2)}, u32[]{:S(2)}) collective-permute-start(bf16[256,256]{1,0:T(8,128)(2,1)S(1)} %get-tuple-element.47), channel_id=1, source_target_pairs={{0,16},{1,17},{2,18},{3,19},{4,20},{5,21},{6,22},{7,23}} | collective-permute-start | bytes 393224 | tf_op jit(solution)/shard_map/ppermute | solution.py:329
  76.7 2.9 %collective-permute-start.14 = (bf16[256,256]{1,0:T(8,128)(2,1)S(1)}, bf16[256,256]{1,0:T(8,128)(2,1)S(1)}, u32[]{:S(2)}, u32[]{:S(2)}) collective-permute-start(bf16[256,256]{1,0:T(8,128)(2,1)S(1)} %get-tuple-element.47), channel_id=1, source_target_pairs={{0,24},{1,25},{2,26},{3,27},{4,28},{5,29},{6,30},{7,31}} | collective-permute-start | bytes 393224 | tf_op jit(solution)/shard_map/ppermute | solution.py:329
  79.6 0.0 collective-permute-done.12.refs_4_
  79.6 0.0 collective-permute-done.13.refs_5_
  79.6 2.5 %collective-permute-done.14.refs_6_ = bf16[256,256]{1,0:T(8,128)(2,1)S(1)} collective-permute-done((bf16[256,256]{1,0:T(8,128)(2,1)S(1)}, bf16[256,256]{1,0:T(8,128)(2,1)S(1)}, u32[]{:S(2)}, u32[]{:S(2)}) %collective-permute-start.14) | collective-permute-done | bytes 131104 | tf_op jit(solution)/shard_map/ppermute | solution.py:329
  82.1 1.4 %shard_map.120 = (f32[256,256]{1,0:T(8,128)S(1)}, f32[256,256]{1,0:T(8,128)S(1)}) custom-call(s32[12]{0:T(128)S(1)} %copy-done.6, f32[10]{0:T(128)S(1)} %copy-done.8, bf16[4,256,256]{2,1,0:T(8,128)(2,1)S(1)} %get-tuple-element.32.s_ref, bf16[4,256,256]{2,1,0:T(8,128)(2,1)S(1)} %get-tuple-element.33.se_ref, ...), custom_call_target="tpu_custom_call" | custom-call | flops 536870912 | bytes 2228312 | tf_op jit(solution)/shard_map/pallas_call | solution.py:30
  83.5 0.0 collective-permute-done.15.ci_ref
  83.5 0.0 collective-permute-done.19.co_ref
  83.5 1.5 %shard_map.124 = (bf16[2,256,256]{2,1,0:T(8,128)(2,1)}, bf16[2,512,256]{2,1,0:T(8,128)(2,1)}) custom-call(s32[12]{0:T(128)S(1)} %copy-done.6, bf16[4,512,256]{2,1,0:T(8,128)(2,1)S(1)} %copy-done.1, f32[256,256]{1,0:T(8,128)S(1)} %get-tuple-element.30.gain_ref, f32[256,256]{1,0:T(8,128)S(1)} %get-tuple-element.31.gain_extra_ref, ...), custom_call_target="tpu_custom_call" | custom-call | flops 134217728 | bytes 2621488 | tf_op jit(solution)/shard_map/pallas_call | solution.py:30
  (8 shorter events, 0.1 us)
Async XLA Ops:
  18.9 13.5 %collective-permute-start.1 = (bf16[512,256]{1,0:T(8,128)(2,1)}, bf16[512,256]{1,0:T(8,128)(2,1)S(1)}, u32[]{:S(2)}, u32[]{:S(2)}) collective-permute-start(bf16[512,256]{1,0:T(8,128)(2,1)} %get-tuple-element.37), channel_id=1, source_target_pairs={{0,1},{1,0},{2,3},{3,2},{4,5},{5,4},{6,7},{7,6},{8,9},{9,8},{10,11... | collective-permute-start | bytes 786440 | tf_op jit(solution)/shard_map/ppermute | solution.py:63
  19.4 13.0 %collective-permute-start.2 = (bf16[512,256]{1,0:T(8,128)(2,1)}, bf16[512,256]{1,0:T(8,128)(2,1)S(1)}, u32[]{:S(2)}, u32[]{:S(2)}) collective-permute-start(bf16[512,256]{1,0:T(8,128)(2,1)} %get-tuple-element.38), channel_id=1, source_target_pairs={{0,1},{1,0},{2,3},{3,2},{4,5},{5,4},{6,7},{7,6},{8,9},{9,8},{10,11... | collective-permute-start | bytes 786440 | tf_op jit(solution)/shard_map/ppermute | solution.py:63
  19.5 15.0 %collective-permute-start.5 = (bf16[512,256]{1,0:T(8,128)(2,1)}, bf16[512,256]{1,0:T(8,128)(2,1)S(1)}, u32[]{:S(2)}, u32[]{:S(2)}) collective-permute-start(bf16[512,256]{1,0:T(8,128)(2,1)} %get-tuple-element.37), channel_id=1, source_target_pairs={{0,7},{1,2},{2,1},{3,4},{4,3},{5,6},{6,5},{7,0},{8,15},{9,10},{10,... | collective-permute-start | bytes 786440 | tf_op jit(solution)/shard_map/ppermute | solution.py:66
  24.2 8.2 %collective-permute-start = (f32[9]{0:T(128)}, f32[9]{0:T(128)S(1)}, u32[]{:S(2)}, u32[]{:S(2)}) collective-permute-start(f32[9]{0:T(128)} %get-tuple-element.36), channel_id=1, source_target_pairs={{0,1},{1,0},{2,3},{3,2},{4,5},{5,4},{6,7},{7,6},{8,9},{9,8},{10,11... | collective-permute-start | bytes 116 | tf_op jit(solution)/shard_map/ppermute | solution.py:63
  24.2 10.3 %collective-permute-start.4 = (f32[9]{0:T(128)}, f32[9]{0:T(128)S(1)}, u32[]{:S(2)}, u32[]{:S(2)}) collective-permute-start(f32[9]{0:T(128)} %get-tuple-element.40), channel_id=1, source_target_pairs={{0,7},{1,2},{2,1},{3,4},{4,3},{5,6},{6,5},{7,0},{8,15},{9,10},{10,... | collective-permute-start | bytes 116 | tf_op jit(solution)/shard_map/ppermute | solution.py:66
  24.8 1.2 %copy-start = (bf16[4,512,256]{2,1,0:T(8,128)(2,1)S(1)}, bf16[4,512,256]{2,1,0:T(8,128)(2,1)}, u32[]{:S(2)}) copy-start(bf16[4,512,256]{2,1,0:T(8,128)(2,1)} %coeff_ref.9) | copy-start | bytes 3145732
  26.0 1.0 %copy-start.3 = (bf16[4,256,256]{2,1,0:T(8,128)(2,1)S(1)}, bf16[4,256,256]{2,1,0:T(8,128)(2,1)}, u32[]{:S(2)}) copy-start(bf16[4,256,256]{2,1,0:T(8,128)(2,1)} %amps_ref.7) | copy-start | bytes 1572868
  27.1 0.6 copy-start.5
  27.7 0.6 copy-start.7
  28.3 0.7 copy-start.9
  29.0 3.5 %copy-start.2 = (bf16[2,1024,512]{2,1,0:T(8,128)(2,1)S(1)}, bf16[2,1024,512]{2,1,0:T(8,128)(2,1)}, u32[]{:S(2)}) copy-start(bf16[2,1024,512]{2,1,0:T(8,128)(2,1)} %three_ref.5) | copy-start | bytes 6291460
  34.4 4.2 %copy-start.1 = (bf16[4,512,256]{2,1,0:T(8,128)(2,1)S(1)}, bf16[4,512,256]{2,1,0:T(8,128)(2,1)}, u32[]{:S(2)}) copy-start(bf16[4,512,256]{2,1,0:T(8,128)(2,1)} %coeff_ref.9) | copy-start | bytes 3145732
  34.4 4.2 %copy-start.4 = (bf16[4,256,256]{2,1,0:T(8,128)(2,1)S(1)}, bf16[4,256,256]{2,1,0:T(8,128)(2,1)}, u32[]{:S(2)}) copy-start(bf16[4,256,256]{2,1,0:T(8,128)(2,1)} %amps_ref.7) | copy-start | bytes 1572868
  34.4 24.3 %collective-permute-start.3 = (bf16[1024,256]{1,0:T(8,128)(2,1)S(1)}, bf16[1024,256]{1,0:T(8,128)(2,1)S(1)}, u32[]{:S(2)}, u32[]{:S(2)}) collective-permute-start(bf16[1024,256]{1,0:T(8,128)(2,1)S(1)} %get-tuple-element.39.in_ref), channel_id=1, source_target_pairs={{0,1},{1,0},{2,3},{3,2},{4,5},{5,4},{6,7},{7,6},{8,9},{9,8},{10,11... | collective-permute-start | bytes 1572872 | tf_op jit(solution)/shard_map/ppermute | solution.py:63
  34.5 24.2 %copy-start.6 = (s32[12]{0:T(128)S(1)}, s32[12]{0:T(128)}, u32[]{:S(2)}) copy-start(s32[12]{0:T(128)} %get-tuple-element.28.ints) | copy-start | bytes 148
  35.5 23.2 %collective-permute-start.6 = (bf16[1024,256]{1,0:T(8,128)(2,1)S(1)}, bf16[1024,256]{1,0:T(8,128)(2,1)S(1)}, u32[]{:S(2)}, u32[]{:S(2)}) collective-permute-start(bf16[1024,256]{1,0:T(8,128)(2,1)S(1)} %shard_map.116), channel_id=1, source_target_pairs={{0,7},{1,2},{2,1},{3,4},{4,3},{5,6},{6,5},{7,0},{8,15},{9,10},{10,... | collective-permute-start | bytes 1572872 | tf_op jit(solution)/shard_map/ppermute | solution.py:66
  38.6 5.4 %collective-permute-start.7 = (bf16[256,256]{1,0:T(8,128)(2,1)S(1)}, bf16[256,256]{1,0:T(8,128)(2,1)S(1)}, u32[]{:S(2)}, u32[]{:S(2)}) collective-permute-start(bf16[256,256]{1,0:T(8,128)(2,1)S(1)} %get-tuple-element.42), channel_id=1, source_target_pairs={{0,1},{1,0},{2,3},{3,2},{4,5},{5,4},{6,7},{7,6},{8,9},{9,8},{10,11... | collective-permute-start | bytes 393224 | tf_op jit(solution)/shard_map/ppermute | solution.py:63
  40.0 14.3 %collective-permute-start.8 = (bf16[256,256]{1,0:T(8,128)(2,1)S(1)}, bf16[256,256]{1,0:T(8,128)(2,1)S(1)}, u32[]{:S(2)}, u32[]{:S(2)}) collective-permute-start(bf16[256,256]{1,0:T(8,128)(2,1)S(1)} %get-tuple-element.43), channel_id=1, source_target_pairs={{0,7},{1,2},{2,1},{3,4},{4,3},{5,6},{6,5},{7,0},{8,15},{9,10},{10,... | collective-permute-start | bytes 393224 | tf_op jit(solution)/shard_map/ppermute | solution.py:66
  40.6 19.2 %collective-permute-start.16 = (bf16[512,256]{1,0:T(8,128)(2,1)S(1)}, bf16[512,256]{1,0:T(8,128)(2,1)S(1)}, u32[]{:S(2)}, u32[]{:S(2)}) collective-permute-start(bf16[512,256]{1,0:T(8,128)(2,1)S(1)} %collective-permute-done.5.x_ref), channel_id=1, source_target_pairs={{0,8},{1,9},{2,10},{3,11},{4,12},{5,13},{6,14},{7,15}} | collective-permute-start | bytes 786440 | tf_op jit(solution)/shard_map/ppermute | solution.py:284
  44.0 19.6 %collective-permute-start.17 = (bf16[512,256]{1,0:T(8,128)(2,1)S(1)}, bf16[512,256]{1,0:T(8,128)(2,1)S(1)}, u32[]{:S(2)}, u32[]{:S(2)}) collective-permute-start(bf16[512,256]{1,0:T(8,128)(2,1)S(1)} %collective-permute-done.5.x_ref), channel_id=1, source_target_pairs={{0,16},{1,17},{2,18},{3,19},{4,20},{5,21},{6,22},{7,23}} | collective-permute-start | bytes 786440 | tf_op jit(solution)/shard_map/ppermute | solution.py:284
  54.3 10.9 %collective-permute-start.18 = (bf16[512,256]{1,0:T(8,128)(2,1)S(1)}, bf16[512,256]{1,0:T(8,128)(2,1)S(1)}, u32[]{:S(2)}, u32[]{:S(2)}) collective-permute-start(bf16[512,256]{1,0:T(8,128)(2,1)S(1)} %collective-permute-done.5.x_ref), channel_id=1, source_target_pairs={{0,24},{1,25},{2,26},{3,27},{4,28},{5,29},{6,30},{7,31}} | collective-permute-start | bytes 786440 | tf_op jit(solution)/shard_map/ppermute | solution.py:284
  59.6 7.0 %collective-permute-start.9 = (bf16[256,256]{1,0:T(8,128)(2,1)S(1)}, bf16[256,256]{1,0:T(8,128)(2,1)S(1)}, u32[]{:S(2)}, u32[]{:S(2)}) collective-permute-start(bf16[256,256]{1,0:T(8,128)(2,1)S(1)} %get-tuple-element.44.amp_ref.refs_0_), channel_id=1, source_target_pairs={{0,8},{8,0},{16,24},{24,16},{1,9},{9,1},{17,25},{25,17},{2,10},{10... | collective-permute-start | bytes 393224 | tf_op jit(solution)/shard_map/ppermute | solution.py:71
  59.7 6.9 %collective-permute-start.10 = (bf16[256,256]{1,0:T(8,128)(2,1)S(1)}, bf16[256,256]{1,0:T(8,128)(2,1)S(1)}, u32[]{:S(2)}, u32[]{:S(2)}) collective-permute-start(bf16[256,256]{1,0:T(8,128)(2,1)S(1)} %get-tuple-element.44.amp_ref.refs_0_), channel_id=1, source_target_pairs={{0,16},{8,24},{16,0},{24,8},{1,17},{9,25},{17,1},{25,9},{2,18},{10... | collective-permute-start | bytes 393224 | tf_op jit(solution)/shard_map/ppermute | solution.py:71
  59.8 8.2 %collective-permute-start.11 = (bf16[256,256]{1,0:T(8,128)(2,1)S(1)}, bf16[256,256]{1,0:T(8,128)(2,1)S(1)}, u32[]{:S(2)}, u32[]{:S(2)}) collective-permute-start(bf16[256,256]{1,0:T(8,128)(2,1)S(1)} %get-tuple-element.44.amp_ref.refs_0_), channel_id=1, source_target_pairs={{0,24},{8,16},{16,8},{24,0},{1,25},{9,17},{17,9},{25,1},{2,26},{10... | collective-permute-start | bytes 393224 | tf_op jit(solution)/shard_map/ppermute | solution.py:71
  65.3 16.8 %copy-start.8 = (f32[10]{0:T(128)S(1)}, f32[10]{0:T(128)}, u32[]{:S(2)}) copy-start(f32[10]{0:T(128)} %get-tuple-element.29.floats) | copy-start | bytes 124
  69.4 14.1 %collective-permute-start.15 = (bf16[2,256,256]{2,1,0:T(8,128)(2,1)S(1)}, bf16[2,256,256]{2,1,0:T(8,128)(2,1)S(1)}, u32[]{:S(2)}, u32[]{:S(2)}) collective-permute-start(bf16[2,256,256]{2,1,0:T(8,128)(2,1)S(1)} %shard_map.121), channel_id=1, source_target_pairs={{0,1},{1,0},{2,3},{3,2},{4,5},{5,4},{6,7},{7,6},{8,9},{9,8},{10,11... | collective-permute-start | bytes 786440 | tf_op jit(solution)/shard_map/ppermute | solution.py:63
  70.8 12.7 %collective-permute-start.19 = (bf16[2,256,256]{2,1,0:T(8,128)(2,1)S(1)}, bf16[2,256,256]{2,1,0:T(8,128)(2,1)S(1)}, u32[]{:S(2)}, u32[]{:S(2)}) collective-permute-start(bf16[2,256,256]{2,1,0:T(8,128)(2,1)S(1)} %shard_map.123), channel_id=1, source_target_pairs={{0,7},{1,2},{2,1},{3,4},{4,3},{5,6},{6,5},{7,0},{8,15},{9,10},{10,... | collective-permute-start | bytes 786440 | tf_op jit(solution)/shard_map/ppermute | solution.py:66
  73.2 6.3 %collective-permute-start.12 = (bf16[256,256]{1,0:T(8,128)(2,1)S(1)}, bf16[256,256]{1,0:T(8,128)(2,1)S(1)}, u32[]{:S(2)}, u32[]{:S(2)}) collective-permute-start(bf16[256,256]{1,0:T(8,128)(2,1)S(1)} %get-tuple-element.47), channel_id=1, source_target_pairs={{0,8},{1,9},{2,10},{3,11},{4,12},{5,13},{6,14},{7,15}} | collective-permute-start | bytes 393224 | tf_op jit(solution)/shard_map/ppermute | solution.py:329
  75.4 4.2 %collective-permute-start.13 = (bf16[256,256]{1,0:T(8,128)(2,1)S(1)}, bf16[256,256]{1,0:T(8,128)(2,1)S(1)}, u32[]{:S(2)}, u32[]{:S(2)}) collective-permute-start(bf16[256,256]{1,0:T(8,128)(2,1)S(1)} %get-tuple-element.47), channel_id=1, source_target_pairs={{0,16},{1,17},{2,18},{3,19},{4,20},{5,21},{6,22},{7,23}} | collective-permute-start | bytes 393224 | tf_op jit(solution)/shard_map/ppermute | solution.py:329
  76.7 5.4 %collective-permute-start.14 = (bf16[256,256]{1,0:T(8,128)(2,1)S(1)}, bf16[256,256]{1,0:T(8,128)(2,1)S(1)}, u32[]{:S(2)}, u32[]{:S(2)}) collective-permute-start(bf16[256,256]{1,0:T(8,128)(2,1)S(1)} %get-tuple-element.47), channel_id=1, source_target_pairs={{0,24},{1,25},{2,26},{3,27},{4,28},{5,29},{6,30},{7,31}} | collective-permute-start | bytes 393224 | tf_op jit(solution)/shard_map/ppermute | solution.py:329

commit v3 on v2

v3 whole, which is shorter than its diff:
```python
import math

import jax
import jax.numpy as jnp
from jax import lax
from jax.experimental import pallas as pl
from jax.experimental.pallas import tpu as pltpu
from jax.sharding import PartitionSpec as P

F32 = jnp.float32
BF16 = jnp.bfloat16
I32 = jnp.int32
NN = ((1,), (0,))
NT = ((1,), (1,))

VMEM = pl.BlockSpec(memory_space=pltpu.VMEM)
SMEM = pl.BlockSpec(memory_space=pltpu.SMEM)
ANY = pl.BlockSpec(memory_space=pl.ANY)
HBM = pl.BlockSpec(memory_space=pltpu.HBM)

MINE, EXTRA, OWNER, FIRST, SECOND, WHOSE, NV_MINE, NV_EXTRA, OCC_MINE, OCC_EXTRA, ROLE_PAIR = range(11)


def whole(number):
    return number.astype(jnp.int32)


def mxu(a, b, dims):
    return lax.dot_general(a, b, (dims, ((), ())), preferred_element_type=F32)


def call(body, ins, outs, args, scratch=(), flops=0, vmem=48):
    moved = sum(a.size * a.dtype.itemsize for a in args)
    return pl.pallas_call(
        body,
        in_specs=ins,
        out_specs=[spec for spec, _, _ in outs],
        out_shape=[jax.ShapeDtypeStruct(shape, dtype) for _, shape, dtype in outs],
        scratch_shapes=list(scratch),
        cost_estimate=pl.CostEstimate(flops=flops, bytes_accessed=moved, transcendentals=0),
        compiler_params=pltpu.CompilerParams(vmem_limit_bytes=vmem * 1024 * 1024),
    )(*args)


def local(
    three_index, coeff, amps, eps_virt, eps_occ, nvirt, pair_occ, partners, coupling, pair_owner
):
    columns = lax.axis_size("pairs")
    roles = lax.axis_size("role")
    occ_block, aux, pao = three_index.shape
    pairs, _, virt = coeff.shape
    partner_count = partners.shape[1]
    slots = 2
    assert roles == pairs and columns % 2 == 0
    tile = min(256, aux)
    pao_scale = 1.0 / math.sqrt(pao)
    aux_scale = 1.0 / math.sqrt(aux)
    virt_scale = 1.0 / math.sqrt(virt)
    square = (virt, virt)
    wide = (virt, pairs * virt)
    sq_b = (VMEM, square, BF16)
    sq_f = (VMEM, square, F32)
    two_b = (VMEM, (2, virt, virt), BF16)
    all_s = (VMEM, wide, BF16)
    half = (VMEM, (aux, virt), BF16)
    orb = (VMEM, (pao, virt), BF16)
    middle = pltpu.VMEM(wide, BF16)

    def inner(x):
        return lax.ppermute(x, "pairs", [(i, i ^ 1) for i in range(columns)])

    def outer(x):
        return lax.ppermute(
            x, "pairs", [(i, (i + (1 if i % 2 else -1)) % columns) for i in range(columns)]
        )

    def swap(x, by):
        return lax.ppermute(x, "role", [(i, i ^ by) for i in range(roles)])

    weights = 2 * pairs
    own_weights = ROLE_PAIR + roles

    def plan_body(
        owner_hbm, occ_hbm, partner_hbm, coupling_hbm, eps_hbm, nvirt_hbm, coeff_hbm,
        mine_ref, extra_ref, to_inner, to_outer, nums,
        owner_ref, occ_ref, partner_ref, coupling_ref, eps_ref, nvirt_ref, near_w, sems,
    ):
        small = [
            pltpu.make_async_copy(source, target, sems.at[at])
            for at, (source, target) in enumerate(
                (
                    (owner_hbm, owner_ref),
                    (occ_hbm, occ_ref),
                    (partner_hbm, partner_ref),
                    (coupling_hbm, coupling_ref),
                    (eps_hbm, eps_ref),
                    (nvirt_hbm, nvirt_ref),
                )
            )
        ]
        for copy in small:
            copy.start()
        role = lax.axis_index("role")
        column = lax.axis_index("pairs")
        small[0].wait()
        of_role = [jnp.int32(0)] * roles
        for p in range(pairs):
            earlier = jnp.int32(0)
            for o in range(p):
                earlier += (owner_ref[o] == owner_ref[p]).astype(I32)
            for s in range(roles):
                hit = (earlier == 0) & (owner_ref[p] == s) if s else earlier == 1
                of_role[s] = jnp.where(hit, p, of_role[s])
        extra = of_role[0]
        mine = extra
        for s in range(1, roles):
            mine = jnp.where(role == s, of_role[s], mine)
        large = [
            pltpu.make_async_copy(coeff_hbm.at[mine], mine_ref, sems.at[6]),
            pltpu.make_async_copy(coeff_hbm.at[extra], extra_ref, sems.at[7]),
        ]
        for copy in large:
            copy.start()
        for copy in small[1:]:
            copy.wait()
        nums[MINE] = mine.astype(F32)
        nums[EXTRA] = extra.astype(F32)
        nums[OWNER] = owner_ref[extra].astype(F32)
        for s in range(roles):
            nums[ROLE_PAIR + s] = of_role[s].astype(F32)
        nums[NV_MINE] = nvirt_ref[mine].astype(F32)
        nums[NV_EXTRA] = nvirt_ref[extra].astype(F32)
        nums[FIRST] = (occ_ref[0, mine] - column * occ_block).astype(F32)
        odd = lax.rem(column, 2) == 1
        inner_at = jnp.where(odd, 0, 2)
        outer_at = 2 - inner_at
        occ_all = occ_block * columns
        second = lax.rem(occ_ref[1, mine] - (column - 1) * occ_block + occ_all, occ_all)
        block = (second >= occ_block).astype(I32) + (second >= 2 * occ_block).astype(I32)
        place = (second - block * occ_block).astype(F32)
        nums[SECOND] = place
        to_inner[weights] = place
        to_outer[weights] = place
        nums[WHOSE] = jnp.where(block == 1, 0, jnp.where(block == inner_at, 1, 2)).astype(F32)
        nums[OCC_MINE] = eps_ref[occ_ref[0, mine]] + eps_ref[occ_ref[1, mine]]
        nums[OCC_EXTRA] = eps_ref[occ_ref[0, extra]] + eps_ref[occ_ref[1, extra]]
        pair_all = pairs * columns
        for which, pair in enumerate((mine, extra)):
            for q in range(3 * pairs):
                near_w[q] = jnp.float32(0)
            for k in range(partner_count):
                at = lax.rem(partner_ref[pair, k] - (column - 1) * pairs + pair_all, pair_all)
                near_w[at] += coupling_ref[pair, k]
            for q in range(pairs):
                to = which * pairs + q
                to_inner[to] = near_w[inner_at * pairs + q]
                nums[own_weights + to] = near_w[pairs + q]
                to_outer[to] = near_w[outer_at * pairs + q]
        for copy in large:
            copy.wait()

    meta = (SMEM, (weights + 1,), F32)
    x_mine, x_extra, to_inner, to_outer, nums = call(
        plan_body,
        [HBM] * 7,
        [orb, orb, meta, meta, (SMEM, (own_weights + weights,), F32)],
        (pair_owner, pair_occ.T, partners, coupling, eps_occ, nvirt, coeff),
        scratch=[
            pltpu.SMEM(pair_owner.shape, I32),
            pltpu.SMEM(pair_occ.shape[::-1], I32),
            pltpu.SMEM(partners.shape, I32),
            pltpu.SMEM(coupling.shape, F32),
            pltpu.SMEM(eps_occ.shape, F32),
            pltpu.SMEM(nvirt.shape, I32),
            pltpu.SMEM((3 * pairs,), F32),
            pltpu.SemaphoreType.DMA((8,)),
        ],
        vmem=60,
    )
    x_out = outer(x_mine)
    of_out = outer(to_outer)

    def place_of(at):
        return pl.ds(at * virt if isinstance(at, int) else pl.multiple_of(at * virt, virt), virt)

    def overlaps(x, coeff_ref, out_ref):
        turned = x.T
        for q in range(pairs):
            s = mxu(turned, coeff_ref[q], NN) * (1.0 / pao)
            out_ref[:, place_of(q)] = s.astype(BF16)

    def coupled(s_ref, middle_ref, parts):
        for at, weight, amp in parts:
            u = weight * mxu(s_ref[:, place_of(at)], amp, NN)
            middle_ref[:, place_of(at)] = u.astype(BF16)
        return mxu(middle_ref[...], s_ref[...], NT)

    def half_into(y_ref, three_ref, at_occ, x):
        for at in range(0, aux, tile):
            rows = pl.ds(at, tile)
            y_ref[rows, :] = (mxu(three_ref[at_occ, rows, :], x, NN) * pao_scale).astype(BF16)

    def own_half_body(
        nums, to_inner, three_ref, mine_ref, extra_ref, first_ref, second_ref, both_ref, inner_ref
    ):
        x = mine_ref[...]
        both_ref[0] = x
        both_ref[1] = extra_ref[...]
        for at in range(weights + 1):
            inner_ref[at] = to_inner[at]
        turned = x.T
        first = whole(nums[FIRST])
        for at in range(0, aux, tile):
            rows = pl.ds(at, tile)
            first_ref[:, rows] = (mxu(turned, three_ref[first, rows, :], NT) * pao_scale).astype(BF16)
        half_into(second_ref, three_ref, whole(nums[SECOND]), x)

    first_t, second_own, x_both, to_inner = call(
        own_half_body,
        [SMEM, SMEM, VMEM, VMEM, VMEM],
        [(VMEM, (virt, aux), BF16), half, (VMEM, (2, pao, virt), BF16), meta],
        (nums, to_inner, three_index, x_mine, x_extra),
        flops=4 * virt * aux * pao,
    )
    def outer_half_body(of, three_ref, x_ref, own_ref, y_ref):
        half_into(y_ref, three_ref, whole(of[weights]), x_ref[...])

    (y_out,) = call(
        outer_half_body,
        [SMEM, VMEM, VMEM, ANY],
        [half],
        (of_out, three_index, x_out, first_t),
        flops=2 * aux * pao * virt,
    )
    y_from_out = outer(y_out)
    def outer_body(of, coeff_ref, amps_ref, x_ref, after_ref, s_ref, c_ref, middle_ref):
        overlaps(x_ref[...], coeff_ref, s_ref)
        c = coupled(s_ref, middle_ref, [(q, of[q], amps_ref[q]) for q in range(pairs)])
        c_ref[...] = c.astype(BF16)

    s_out, c_out = call(
        outer_body,
        [SMEM, VMEM, VMEM, VMEM, ANY],
        [all_s, sq_b],
        (of_out, coeff, amps, x_out, y_out),
        scratch=[middle],
        flops=2 * pairs * virt * virt * (pao + 2 * virt),
    )
    c_from_out = outer(c_out)
    x_later, x_both, to_inner, _ = lax.optimization_barrier((x_extra, x_both, to_inner, c_out))
    x_extra_out = outer(x_later)
    x_in = inner(x_both)
    of_in = inner(to_inner)

    def inner_body(
        of, three_ref, coeff_ref, amps_ref, x_ref, after_ref, y_ref, s_ref, se_ref, c_ref, middle_ref
    ):
        half_into(y_ref, three_ref, whole(of[weights]), x_ref[0])
        overlaps(x_ref[0], coeff_ref, s_ref)
        c = coupled(s_ref, middle_ref, [(q, of[q], amps_ref[q]) for q in range(pairs)])
        c_ref[...] = c.astype(BF16)
        overlaps(x_ref[1], coeff_ref, se_ref)

    y_in, s_in, se_in, c_in = call(
        inner_body,
        [SMEM] + [VMEM] * 4 + [ANY],
        [half, all_s, all_s, sq_b],
        (of_in, three_index, coeff, amps, x_in, c_out),
        scratch=[middle],
        flops=2 * virt * (aux * pao + pairs * virt * (2 * pao + 2 * virt)),
    )
    y_from_in = inner(y_in)
    c_from_in = inner(c_in)

    def own_body(
        nums, coeff_ref, amps_ref, eps_ref, after_ref,
        s_ref, se_ref, c_ref, gain_ref, gain_extra_ref, middle_ref,
    ):
        mine, extra = whole(nums[MINE]), whole(nums[EXTRA])
        overlaps(coeff_ref[mine], coeff_ref, s_ref)
        c_ref[...] = coupled(
            s_ref, middle_ref, [(q, nums[own_weights + q], amps_ref[q]) for q in range(pairs)]
        )
        overlaps(coeff_ref[extra], coeff_ref, se_ref)

        def gain(pair, count, occupied):
            row = jnp.broadcast_to(eps_ref[pl.ds(pair, 1), :], square)
            energy = row + row.T - occupied
            inside = (lax.broadcasted_iota(I32, square, 0) < count) & (
                lax.broadcasted_iota(I32, square, 1) < count
            )
            return jnp.where(inside, 1.0 / (energy + 1.0), 0.0)

        gain_ref[...] = gain(mine, whole(nums[NV_MINE]), nums[OCC_MINE])
        gain_extra_ref[...] = gain(extra, whole(nums[NV_EXTRA]), nums[OCC_EXTRA])

    s_own, se_own, c_own, gain, gain_extra = call(
        own_body,
        [SMEM, VMEM, VMEM, VMEM, ANY],
        [all_s, all_s, sq_f, sq_f, sq_f],
        (nums, coeff, amps, eps_virt, c_out),
        scratch=[middle],
        flops=2 * pairs * virt * virt * (2 * pao + 2 * virt),
    )

    def first_body(
        nums, first_ref, own_ref, in_ref, out_ref, amps_ref, c_ref, ci_ref, co_ref, gain_ref,
        amp_ref, k_ref, held, sem,
    ):
        for whose, source in enumerate((own_ref, in_ref, out_ref)):

            @pl.when(whole(nums[WHOSE]) == whose)
            def _():
                copy = pltpu.make_async_copy(source, held, sem)
                copy.start()
                copy.wait()

        k = mxu(first_ref[...], held[...], NN) * aux_scale
        k_ref[...] = k
        c = c_ref[...] + ci_ref[...].astype(F32) + co_ref[...].astype(F32)
        old = amps_ref[whole(nums[MINE])].astype(F32)
        amp_ref[...] = (gain_ref[...] * (old - k - c)).astype(BF16)

    amp, k_first = call(
        first_body,
        [SMEM, VMEM, ANY, ANY, ANY, VMEM, VMEM, VMEM, VMEM, VMEM],
        [sq_b, sq_f],
        (
            nums, first_t, second_own, y_from_in, y_from_out,
            amps, c_own, c_from_in, c_from_out, gain,
        ),
        scratch=[pltpu.VMEM((aux, virt), BF16), pltpu.SemaphoreType.DMA],
        flops=2 * aux * virt * virt,
    )
    amp_roles = [amp] + [swap(amp, m) for m in range(1, roles)]

    def second_body(amp_ref, k_ref, out_ref, out_b_ref):
        amp = amp_ref[...]
        k = k_ref[...]
        right = k + mxu(k.astype(BF16), amp, NN) * virt_scale
        both = right + mxu(amp.T, right.astype(BF16), NN) * virt_scale
        rest = amp.astype(F32) - both
        out_ref[...] = rest
        out_b_ref[...] = rest.astype(BF16)

    rest, rest_b = call(
        second_body, [VMEM, VMEM], [sq_f, sq_b], (amp, k_first), flops=4 * virt * virt * virt
    )
    rests = [lax.ppermute(rest_b, "role", [(0, s)]) for s in range(1, roles)]

    def outer_extra_body(coeff_ref, x_ref, after_ref, s_ref):
        overlaps(x_ref[...], coeff_ref, s_ref)

    (se_out,) = call(
        outer_extra_body,
        [VMEM, VMEM, ANY],
        [all_s],
        (coeff, x_extra_out, rest),
        flops=2 * pairs * virt * virt * pao,
    )

    def parts_of(nums, weight_ref, first_weight, amp_refs):
        role = lax.axis_index("role")
        parts = []
        for m in range(roles):
            at = whole(nums[ROLE_PAIR + (role ^ m)])
            parts.append((at, weight_ref[first_weight + at], amp_refs[m][...]))
        return parts

    def near_again_body(nums, of, s_ref, se_ref, *refs):
        amp_refs, (c_ref, middle_ref, middle_e_ref) = refs[:roles], refs[-3:]
        c = coupled(s_ref, middle_ref, parts_of(nums, of, 0, amp_refs))
        c_ref[0] = c.astype(BF16)
        c = coupled(se_ref, middle_e_ref, parts_of(nums, of, pairs, amp_refs))
        c_ref[1] = c.astype(BF16)

    def near_again(of, s, se, after=()):
        (c,) = call(
            near_again_body,
            [SMEM, SMEM] + [VMEM] * (2 + roles) + [ANY] * len(after),
            [two_b],
            (nums, of, s, se, *amp_roles, *after),
            scratch=[middle, middle],
            flops=8 * pairs * virt * virt * virt,
        )
        return c

    cc_from_out = outer(near_again(of_out, s_out, se_out))
    cc_from_in = inner(near_again(of_in, s_in, se_in, rests))

    def own_again_body(nums, s_ref, se_ref, rest_ref, *refs):
        amp_refs, rest_refs = refs[:roles], refs[roles : 2 * roles - 1]
        out_ref, out_extra_ref, middle_ref, middle_e_ref = refs[2 * roles - 1 :]
        parts = parts_of(nums, nums, own_weights, amp_refs)
        out_ref[...] = rest_ref[...] - coupled(s_ref, middle_ref, parts)
        role = lax.axis_index("role")
        parts = parts_of(nums, nums, own_weights + pairs, amp_refs)
        total = -coupled(se_ref, middle_e_ref, parts)
        for s in range(1, roles):
            total += jnp.where(role == s, rest_refs[s - 1][...].astype(F32), 0.0)
        out_extra_ref[...] = total

    rest, rest_extra = call(
        own_again_body,
        [SMEM] + [VMEM] * (3 + 2 * roles - 1),
        [sq_f, sq_f],
        (nums, s_own, se_own, rest, *amp_roles, *rests),
        scratch=[middle, middle],
        flops=8 * pairs * virt * virt * virt,
    )

    def last_body(
        nums, coeff_ref, gain_ref, gain_extra_ref, rest_ref, rest_extra_ref, ci_ref, co_ref, amp_ref, orb_ref
    ):
        role = lax.axis_index("role")

        def store(slot, here, gain, rest, pair):
            @pl.when(here)
            def _():
                c = ci_ref[slot].astype(F32) + co_ref[slot].astype(F32)
                amp = (gain[...] * (rest[...] - c)).astype(BF16)
                amp_ref[slot] = amp
                x = coeff_ref[pair]
                orb_ref[slot] = (x.astype(F32) + mxu(x, amp, NN) * virt_scale).astype(BF16)

            @pl.when(jnp.logical_not(here))
            def _():
                amp_ref[slot] = jnp.zeros(square, BF16)
                orb_ref[slot] = jnp.zeros((pao, virt), BF16)

        store(0, role > 0, gain_ref, rest_ref, whole(nums[MINE]))
        store(1, role == whole(nums[OWNER]), gain_extra_ref, rest_extra_ref, whole(nums[EXTRA]))

    amps_out, dressed_out = call(
        last_body,
        [SMEM] + [VMEM] * 7,
        [(VMEM, (slots, virt, virt), BF16), (VMEM, (slots, pao, virt), BF16)],
        (nums, coeff, gain, gain_extra, rest, rest_extra, cc_from_in, cc_from_out),
        flops=4 * pao * virt * virt,
    )
    return amps_out, dressed_out


def solution(mesh):
    in_specs = (
        P("pairs", None, None),
        P("pairs", None, None),
        P("pairs", None, None),
        P("pairs", None),
        P(),
        P("pairs"),
        P("pairs", None),
        P("pairs", None),
        P("pairs", None),
        P("pairs"),
    )
    out_specs = (P(("role", "pairs"), None, None), P(("role", "pairs"), None, None))
    return jax.shard_map(local, mesh=mesh, in_specs=in_specs, out_specs=out_specs, check_vma=False)
```

time: 85.4 us -> 60.4 us (0.71)
  Pallas kernels: 33 us -> 18.5 us
  waiting for transfers between devices: 15.8 us -> 10.1 us
  starting transfers between devices: 31 us -> 25.4 us
  local copies, waits for them, and re-layouts: 4.18 us -> 5.14 us
    pallas_call x12 -> x13, Pallas kernels: 33 us -> 18.5 us  [call(): pl.pallas_call(body, in_specs=ins, out_specs=[spec for spec, _, _ in outs...]
    ppermute x3 -> x0, starting transfers between devices: 9.06 us -> none  [local(): x_extras = [lax.ppermute(x_sent, 'role', [(0, s)]) for s in range(1, roles)]]
    ppermute x3, waiting for transfers between devices: 2.74 us -> 0.01 us  [swap(): return lax.ppermute(x, 'role', [(i, i ^ by) for i in range(roles)])]
    ppermute x3, waiting for transfers between devices: 2.48 us -> 0.01 us  [local(): rests = [lax.ppermute(rest_b, 'role', [(0, s)]) for s in range(1, roles)]]
    ppermute x5 -> x6, starting transfers between devices: 11.4 us -> 13.3 us  [outer(): lax.ppermute(x, 'pairs', [(i, (i + (1 if i % 2 else -1)) % columns) for i...]
    ppermute x3 -> x0, waiting for transfers between devices: 1.58 us -> none  [local(): x_extras = [lax.ppermute(x_sent, 'role', [(0, s)]) for s in range(1, roles)]]
    ppermute x6 -> x5, waiting for transfers between devices: 0.02 us -> 1.13 us  [inner(): return lax.ppermute(x, 'pairs', [(i, i ^ 1) for i in range(columns)])]
    ppermute x3, starting transfers between devices: 6.32 us -> 7.35 us  [local(): rests = [lax.ppermute(rest_b, 'role', [(0, s)]) for s in range(1, roles)]]
  transfers between devices with their start and end apart: 20 -> 17, of which waited for: 5 -> 3; matrix products, arithmetic and copies ran while one was open for 0% -> 0% of each run, Pallas kernels for 14% -> 20%
where the time goes in v3:
time: 60.4 us; the launch traced here: 60 us
  starting transfers between devices  25.4 us (42%)
  Pallas kernels  18.5 us (31%)
  waiting for transfers between devices  10.1 us (17%)
  local copies, waits for them, and re-layouts  5.14 us (9%)
  between operations  0.87 us (1%)
    pallas_call x13, Pallas kernels, call(): pl.pallas_call(body, in_specs=ins, out_specs=[spec for spec, _, _ in outs...  18.5 us
    ppermute x6, starting transfers between devices, outer(): lax.ppermute(x, 'pairs', [(i, (i + (1 if i % 2 else -1)) % columns) for i...  13.3 us
    ppermute x6, waiting for transfers between devices, outer(): lax.ppermute(x, 'pairs', [(i, (i + (1 if i % 2 else -1)) % columns) for i...  8.92 us
    ppermute x3, starting transfers between devices, local(): rests = [lax.ppermute(rest_b, 'role', [(0, s)]) for s in range(1, roles)]  7.35 us
    unnamed x22, local copies, waits for them, and re-layouts  5.14 us
    ppermute x3, starting transfers between devices, swap(): return lax.ppermute(x, 'role', [(i, i ^ by) for i in range(roles)])  4.34 us
  transfers between devices with their start and end apart: 17, of which 3 were waited for; matrix products, arithmetic and copies ran while one was open for 0% of the time, Pallas kernels for 20%

profile of v3, /device:TPU:0, one launch (start us, length us, event | category | flops | bytes accessed | tf_op | source)
XLA Modules:
  0.0 60.0 jit_solution(15216382678833476861)
XLA Ops:
  0.6 2.6 %shard_map.113 = (bf16[512,256]{1,0:T(8,128)(2,1)}, bf16[512,256]{1,0:T(8,128)(2,1)}, f32[9]{0:T(128)}, f32[9]{0:T(128)}, f32[22]{0:T(128)}) custom-call(s32[4]{0:T(128)} %owner_hbm.1, s32[2,4]{1,0:T(2,128)} %bitcast.1, s32[4,8]{1,0:T(4,128)} %partner_hbm.1, f32[4,8]{1,0:T(4,128)} %coupling_hbm.1, f32[16]{0:T(128)} %eps_hbm.1, s32[4]{0:T(128)} %nvirt_hbm.1, ...), custom_call_target="tpu_custom_call" | custom-call | bytes 1048960 | tf_op jit(solution)/shard_map/pallas_call | solution.py:34
  3.2 4.6 %collective-permute-start.1 = (bf16[512,256]{1,0:T(8,128)(2,1)}, bf16[512,256]{1,0:T(8,128)(2,1)S(1)}, u32[]{:S(2)}, u32[]{:S(2)}) collective-permute-start(bf16[512,256]{1,0:T(8,128)(2,1)} %get-tuple-element.33.mine_ref), channel_id=1, source_target_pairs={{0,7},{1,2},{2,1},{3,4},{4,3},{5,6},{6,5},{7,0},{8,15},{9,10},{10,... | collective-permute-start | bytes 786440 | tf_op jit(solution)/shard_map/ppermute | solution.py:73
  7.8 0.1 collective-permute-start
  7.9 0.0 copy-start.1
  7.9 1.6 %copy-done.1 = bf16[2,1024,512]{2,1,0:T(8,128)(2,1)S(1)} copy-done((bf16[2,1024,512]{2,1,0:T(8,128)(2,1)S(1)}, bf16[2,1024,512]{2,1,0:T(8,128)(2,1)}, u32[]{:S(2)}) %copy-start.1) | copy-done | bytes 2097176
  9.5 0.9 %copy-done.4 = bf16[512,256]{1,0:T(8,128)(2,1)S(1)} copy-done((bf16[512,256]{1,0:T(8,128)(2,1)S(1)}, bf16[512,256]{1,0:T(8,128)(2,1)}, u32[]{:S(2)}) %copy-start.4) | copy-done | bytes 262168
  10.4 0.9 %copy-done.6 = bf16[512,256]{1,0:T(8,128)(2,1)S(1)} copy-done((bf16[512,256]{1,0:T(8,128)(2,1)S(1)}, bf16[512,256]{1,0:T(8,128)(2,1)}, u32[]{:S(2)}) %copy-start.6) | copy-done | bytes 262168
  11.4 0.7 %copy-done.7 = f32[22]{0:T(128)S(1)} copy-done((f32[22]{0:T(128)S(1)}, f32[22]{0:T(128)}, u32[]{:S(2)}) %copy-start.7) | copy-done | bytes 112
  12.0 0.6 copy-done.9
  12.6 1.4 %shard_map.114 = (bf16[256,1024]{1,0:T(8,128)(2,1)S(1)}, bf16[1024,256]{1,0:T(8,128)(2,1)S(1)}, bf16[2,512,256]{2,1,0:T(8,128)(2,1)S(1)}, f32[9]{0:T(128)S(1)}) custom-call(f32[22]{0:T(128)S(1)} %copy-done.7, f32[9]{0:T(128)S(1)} %copy-done.9, bf16[2,1024,512]{2,1,0:T(8,128)(2,1)S(1)} %copy-done.1, bf16[512,256]{1,0:T(8,128)(2,1)S(1)} %copy-done.6, ...), custom_call_target="tpu_custom_call" | custom-call | flops 536870912 | bytes 2621564 | tf_op jit(solution)/shard_map/pallas_call | solution.py:34
  14.1 0.0 copy-start
  14.1 0.0 copy-start.3
  14.1 0.0 collective-permute-done.of
  14.1 0.0 collective-permute-done.1.x_ref
  14.1 0.1 copy-done.2
  14.2 1.0 %shard_map.115.after_ref = bf16[1024,256]{1,0:T(8,128)(2,1)S(1)} custom-call(f32[9]{0:T(128)S(1)} %collective-permute-done.of, bf16[2,1024,512]{2,1,0:T(8,128)(2,1)S(1)} %copy-done.2, bf16[512,256]{1,0:T(8,128)(2,1)S(1)} %collective-permute-done.1.x_ref, bf16[256,1024]{1,0:T(8,128)(2,1)S(1)} %get-tuple-element.36.own_ref.first_ref), custom_call_target="tpu_custom_call" | custom-call | flops 268435456 | bytes 2883620 | tf_op jit(solution)/shard_map/pallas_call | solution.py:34
  15.2 0.1 copy-done
  15.3 0.1 copy-done.3
  15.4 1.5 %shard_map.116 = (bf16[256,1024]{1,0:T(8,128)(2,1)S(1)}, bf16[256,256]{1,0:T(8,128)(2,1)S(1)}) custom-call(f32[9]{0:T(128)S(1)} %collective-permute-done.of, bf16[4,512,256]{2,1,0:T(8,128)(2,1)S(1)} %copy-done, bf16[4,256,256]{2,1,0:T(8,128)(2,1)S(1)} %copy-done.3, bf16[512,256]{1,0:T(8,128)(2,1)S(1)} %collective-permute-done.1.x_ref, ...), custom_call_target="tpu_custom_call" | custom-call | flops 536870912 | bytes 2359332 | tf_op jit(solution)/shard_map/pallas_call | solution.py:34
  16.9 0.0 copy-start.5
  16.9 0.0 copy-start.8
  16.9 0.0 copy-start.10
  17.0 0.1 collective-permute-start.3
  17.0 3.5 %collective-permute-start.5 = (bf16[1024,256]{1,0:T(8,128)(2,1)S(1)}, bf16[1024,256]{1,0:T(8,128)(2,1)S(1)}, u32[]{:S(2)}, u32[]{:S(2)}) collective-permute-start(bf16[1024,256]{1,0:T(8,128)(2,1)S(1)} %shard_map.115.after_ref), channel_id=1, source_target_pairs={{0,7},{1,2},{2,1},{3,4},{4,3},{5,6},{6,5},{7,0},{8,15},{9,10},{10,... | collective-permute-start | bytes 1572872 | tf_op jit(solution)/shard_map/ppermute | solution.py:73
  20.6 0.0 collective-permute-start.2
  20.6 1.1 %collective-permute-done.2.of = f32[9]{0:T(128)S(1)} collective-permute-done((f32[9]{0:T(128)S(1)}, f32[9]{0:T(128)S(1)}, u32[]{:S(2)}, u32[]{:S(2)}) %collective-permute-start.2) | collective-permute-done | bytes 68 | tf_op jit(solution)/shard_map/ppermute | solution.py:70
  21.7 0.0 collective-permute-done.3.x_ref
  21.7 1.8 %shard_map.118 = (bf16[1024,256]{1,0:T(8,128)(2,1)S(1)}, bf16[256,1024]{1,0:T(8,128)(2,1)S(1)}, bf16[256,1024]{1,0:T(8,128)(2,1)S(1)}, bf16[256,256]{1,0:T(8,128)(2,1)S(1)}) custom-call(f32[9]{0:T(128)S(1)} %collective-permute-done.2.of, bf16[2,1024,512]{2,1,0:T(8,128)(2,1)S(1)} %copy-done.2, bf16[4,512,256]{2,1,0:T(8,128)(2,1)S(1)} %copy-done, ...), custom_call_target="tpu_custom_call" | custom-call | flops 1073741824 | bytes 4325412 | tf_op jit(solution)/shard_map/pallas_call | solution.py:34
  23.5 0.3 collective-permute-start.4
  23.8 0.6 %collective-permute-start.7 = (bf16[256,256]{1,0:T(8,128)(2,1)S(1)}, bf16[256,256]{1,0:T(8,128)(2,1)S(1)}, u32[]{:S(2)}, u32[]{:S(2)}) collective-permute-start(bf16[256,256]{1,0:T(8,128)(2,1)S(1)} %get-tuple-element.37.after_ref), channel_id=1, source_target_pairs={{0,7},{1,2},{2,1},{3,4},{4,3},{5,6},{6,5},{7,0},{8,15},{9,10},{10,... | collective-permute-start | bytes 393224 | tf_op jit(solution)/shard_map/ppermute | solution.py:73
  24.4 0.0 collective-permute-start.6
  24.4 0.0 copy-done.5
  24.4 2.9 %collective-permute-start.15 = (bf16[512,256]{1,0:T(8,128)(2,1)S(1)}, bf16[512,256]{1,0:T(8,128)(2,1)S(1)}, u32[]{:S(2)}, u32[]{:S(2)}) collective-permute-start(bf16[512,256]{1,0:T(8,128)(2,1)S(1)} %copy-done.5), channel_id=1, source_target_pairs={{0,7},{1,2},{2,1},{3,4},{4,3},{5,6},{6,5},{7,0},{8,15},{9,10},{10,... | collective-permute-start | bytes 786440 | tf_op jit(solution)/shard_map/ppermute | solution.py:73
  27.3 0.0 copy-done.8
  27.3 0.0 copy-done.10
  27.3 1.6 %shard_map.117 = (bf16[256,1024]{1,0:T(8,128)(2,1)S(1)}, bf16[256,1024]{1,0:T(8,128)(2,1)S(1)}, f32[256,256]{1,0:T(8,128)S(1)}, f32[256,256]{1,0:T(8,128)S(1)}, f32[256,256]{1,0:T(8,128)S(1)}) custom-call(f32[22]{0:T(128)S(1)} %copy-done.8, bf16[4,512,256]{2,1,0:T(8,128)(2,1)S(1)} %copy-done, bf16[4,256,256]{2,1,0:T(8,128)(2,1)S(1)} %copy-done.3, ...), custom_call_target="tpu_custom_call" | custom-call | flops 805306368 | bytes 1708120 | tf_op jit(solution)/shard_map/pallas_call | solution.py:34
  28.9 6.6 %collective-permute-done.7.co_ref = bf16[256,256]{1,0:T(8,128)(2,1)S(1)} collective-permute-done((bf16[256,256]{1,0:T(8,128)(2,1)S(1)}, bf16[256,256]{1,0:T(8,128)(2,1)S(1)}, u32[]{:S(2)}, u32[]{:S(2)}) %collective-permute-start.7) | collective-permute-done | bytes 131104 | tf_op jit(solution)/shard_map/ppermute | solution.py:73
  35.5 0.0 collective-permute-done.5.out_ref
  35.5 0.0 collective-permute-done.6.ci_ref
  35.5 0.0 collective-permute-done.4.in_ref
  35.5 0.9 %shard_map.119 = (bf16[256,256]{1,0:T(8,128)(2,1)S(1)}, f32[256,256]{1,0:T(8,128)S(1)}) custom-call(f32[22]{0:T(128)S(1)} %copy-done.8, bf16[256,1024]{1,0:T(8,128)(2,1)S(1)} %get-tuple-element.36.own_ref.first_ref, bf16[1024,256]{1,0:T(8,128)(2,1)S(1)} %get-tuple-element.42.own_ref, bf16[1024,256]{1,0:T(8,128)(2,1)S(1)} %collective-permute-done.4.in_ref, ...), custom_call_target="tpu_custom_call" | custom-call | flops 134217728 | bytes 3407960 | tf_op jit(solution)/shard_map/pallas_call | solution.py:34
  36.4 3.7 %collective-permute-start.10 = (bf16[256,256]{1,0:T(8,128)(2,1)S(1)}, bf16[256,256]{1,0:T(8,128)(2,1)S(1)}, u32[]{:S(2)}, u32[]{:S(2)}) collective-permute-start(bf16[256,256]{1,0:T(8,128)(2,1)S(1)} %get-tuple-element.50.amp_ref.refs_0_), channel_id=1, source_target_pairs={{0,24},{8,16},{16,8},{24,0},{1,25},{9,17},{17,9},{25,1},{2,26},{10... | collective-permute-start | bytes 393224 | tf_op jit(solution)/shard_map/ppermute | solution.py:78
  40.1 0.5 collective-permute-start.9
  40.6 0.1 collective-permute-start.8
  40.8 0.4 shard_map.120
  41.2 4.8 %collective-permute-start.13 = (bf16[256,256]{1,0:T(8,128)(2,1)S(1)}, bf16[256,256]{1,0:T(8,128)(2,1)S(1)}, u32[]{:S(2)}, u32[]{:S(2)}) collective-permute-start(bf16[256,256]{1,0:T(8,128)(2,1)S(1)} %get-tuple-element.53), channel_id=1, source_target_pairs={{0,24},{1,25},{2,26},{3,27},{4,28},{5,29},{6,30},{7,31}} | collective-permute-start | bytes 393224 | tf_op jit(solution)/shard_map/ppermute | solution.py:349
  45.9 0.0 collective-permute-done.15.x_ref
  46.0 1.3 %collective-permute-start.12 = (bf16[256,256]{1,0:T(8,128)(2,1)S(1)}, bf16[256,256]{1,0:T(8,128)(2,1)S(1)}, u32[]{:S(2)}, u32[]{:S(2)}) collective-permute-start(bf16[256,256]{1,0:T(8,128)(2,1)S(1)} %get-tuple-element.53), channel_id=1, source_target_pairs={{0,16},{1,17},{2,18},{3,19},{4,20},{5,21},{6,22},{7,23}} | collective-permute-start | bytes 393224 | tf_op jit(solution)/shard_map/ppermute | solution.py:349
  47.3 0.0 collective-permute-done.10.refs_3_
  47.3 1.3 %collective-permute-start.11 = (bf16[256,256]{1,0:T(8,128)(2,1)S(1)}, bf16[256,256]{1,0:T(8,128)(2,1)S(1)}, u32[]{:S(2)}, u32[]{:S(2)}) collective-permute-start(bf16[256,256]{1,0:T(8,128)(2,1)S(1)} %get-tuple-element.53), channel_id=1, source_target_pairs={{0,8},{1,9},{2,10},{3,11},{4,12},{5,13},{6,14},{7,15}} | collective-permute-start | bytes 393224 | tf_op jit(solution)/shard_map/ppermute | solution.py:349
  48.6 0.5 shard_map.123.se_ref
  49.0 0.0 collective-permute-done.9.refs_2_
  49.0 0.0 collective-permute-done.8.refs_1_
  49.1 1.8 %shard_map.124 = bf16[2,256,256]{2,1,0:T(8,128)(2,1)S(1)} custom-call(f32[22]{0:T(128)S(1)} %copy-done.8, f32[9]{0:T(128)S(1)} %collective-permute-done.of, bf16[256,1024]{1,0:T(8,128)(2,1)S(1)} %get-tuple-element.58.s_ref, bf16[256,1024]{1,0:T(8,128)(2,1)S(1)} %shard_map.123.se_ref, bf16[256,256]{1,0:T(8,128)(2,1)S(1)} %get-tuple-element.50.amp_ref.refs_0_, ...), custom_call_target="tpu_custom_call" | custom-call | flops 536870912 | bytes 1572988 | tf_op jit(solution)/shard_map/pallas_call | solution.py:34
  50.9 1.6 %collective-permute-start.16 = (bf16[2,256,256]{2,1,0:T(8,128)(2,1)S(1)}, bf16[2,256,256]{2,1,0:T(8,128)(2,1)S(1)}, u32[]{:S(2)}, u32[]{:S(2)}) collective-permute-start(bf16[2,256,256]{2,1,0:T(8,128)(2,1)S(1)} %shard_map.124), channel_id=1, source_target_pairs={{0,7},{1,2},{2,1},{3,4},{4,3},{5,6},{6,5},{7,0},{8,15},{9,10},{10,... | collective-permute-start | bytes 786440 | tf_op jit(solution)/shard_map/ppermute | solution.py:73
  52.5 0.0 collective-permute-done.13.refs_6_
  52.5 0.0 collective-permute-done.12.refs_5_
  52.5 0.0 collective-permute-done.11.refs_4_
  52.5 1.8 %shard_map.122 = bf16[2,256,256]{2,1,0:T(8,128)(2,1)S(1)} custom-call(f32[22]{0:T(128)S(1)} %copy-done.8, f32[9]{0:T(128)S(1)} %collective-permute-done.2.of, bf16[256,1024]{1,0:T(8,128)(2,1)S(1)} %get-tuple-element.56.s_ref, bf16[256,1024]{1,0:T(8,128)(2,1)S(1)} %get-tuple-element.57.se_ref, bf16[256,256]{1,0:T(8,128)(2,1)S(1)} %get-tuple-element.50.amp_ref.refs_0_, ...), custom_call_target="tpu_custom_call" | custom-call | flops 536870912 | bytes 1966204 | tf_op jit(solution)/shard_map/pallas_call | solution.py:34
  54.3 0.1 collective-permute-start.14
  54.4 1.8 %shard_map.121 = (f32[256,256]{1,0:T(8,128)S(1)}, f32[256,256]{1,0:T(8,128)S(1)}) custom-call(f32[22]{0:T(128)S(1)} %copy-done.8, bf16[256,1024]{1,0:T(8,128)(2,1)S(1)} %get-tuple-element.40.s_ref, bf16[256,1024]{1,0:T(8,128)(2,1)S(1)} %get-tuple-element.41.se_ref, f32[256,256]{1,0:T(8,128)S(1)} %get-tuple-element.52.rest_ref.after_ref, ...), custom_call_target="tpu_custom_call" | custom-call | flops 536870912 | bytes 2228312 | tf_op jit(solution)/shard_map/pallas_call | solution.py:34
  56.2 2.3 %collective-permute-done.16.co_ref = bf16[2,256,256]{2,1,0:T(8,128)(2,1)S(1)} collective-permute-done((bf16[2,256,256]{2,1,0:T(8,128)(2,1)S(1)}, bf16[2,256,256]{2,1,0:T(8,128)(2,1)S(1)}, u32[]{:S(2)}, u32[]{:S(2)}) %collective-permute-start.16) | collective-permute-done | bytes 262176 | tf_op jit(solution)/shard_map/ppermute | solution.py:73
  58.5 0.0 collective-permute-done.14.ci_ref
  58.5 1.5 %shard_map.125 = (bf16[2,256,256]{2,1,0:T(8,128)(2,1)}, bf16[2,512,256]{2,1,0:T(8,128)(2,1)}) custom-call(f32[22]{0:T(128)S(1)} %copy-done.8, bf16[4,512,256]{2,1,0:T(8,128)(2,1)S(1)} %copy-done, f32[256,256]{1,0:T(8,128)S(1)} %get-tuple-element.38.gain_ref, f32[256,256]{1,0:T(8,128)S(1)} %get-tuple-element.39.gain_extra_ref, ...), custom_call_target="tpu_custom_call" | custom-call | flops 134217728 | bytes 2621528 | tf_op jit(solution)/shard_map/pallas_call | solution.py:34
  (5 shorter events, 0.0 us)
Async XLA Ops:
  3.2 10.9 %collective-permute-start.1 = (bf16[512,256]{1,0:T(8,128)(2,1)}, bf16[512,256]{1,0:T(8,128)(2,1)S(1)}, u32[]{:S(2)}, u32[]{:S(2)}) collective-permute-start(bf16[512,256]{1,0:T(8,128)(2,1)} %get-tuple-element.33.mine_ref), channel_id=1, source_target_pairs={{0,7},{1,2},{2,1},{3,4},{4,3},{5,6},{6,5},{7,0},{8,15},{9,10},{10,... | collective-permute-start | bytes 786440 | tf_op jit(solution)/shard_map/ppermute | solution.py:73
  7.8 6.3 %collective-permute-start = (f32[9]{0:T(128)}, f32[9]{0:T(128)S(1)}, u32[]{:S(2)}, u32[]{:S(2)}) collective-permute-start(f32[9]{0:T(128)} %get-tuple-element.32), channel_id=1, source_target_pairs={{0,7},{1,2},{2,1},{3,4},{4,3},{5,6},{6,5},{7,0},{8,15},{9,10},{10,... | collective-permute-start | bytes 116 | tf_op jit(solution)/shard_map/ppermute | solution.py:73
  7.9 1.6 %copy-start.1 = (bf16[2,1024,512]{2,1,0:T(8,128)(2,1)S(1)}, bf16[2,1024,512]{2,1,0:T(8,128)(2,1)}, u32[]{:S(2)}) copy-start(bf16[2,1024,512]{2,1,0:T(8,128)(2,1)} %three_ref.5) | copy-start | bytes 6291460
  9.4 0.9 %copy-start.4 = (bf16[512,256]{1,0:T(8,128)(2,1)S(1)}, bf16[512,256]{1,0:T(8,128)(2,1)}, u32[]{:S(2)}) copy-start(bf16[512,256]{1,0:T(8,128)(2,1)} %get-tuple-element.59.extra_ref) | copy-start | bytes 786436
  10.4 0.9 %copy-start.6 = (bf16[512,256]{1,0:T(8,128)(2,1)S(1)}, bf16[512,256]{1,0:T(8,128)(2,1)}, u32[]{:S(2)}) copy-start(bf16[512,256]{1,0:T(8,128)(2,1)} %get-tuple-element.33.mine_ref) | copy-start | bytes 786436
  11.4 0.7 %copy-start.7 = (f32[22]{0:T(128)S(1)}, f32[22]{0:T(128)}, u32[]{:S(2)}) copy-start(f32[22]{0:T(128)} %get-tuple-element.31.nums) | copy-start | bytes 268
  12.0 0.6 copy-start.9
  12.6 1.6 %copy-start.2 = (bf16[2,1024,512]{2,1,0:T(8,128)(2,1)S(1)}, bf16[2,1024,512]{2,1,0:T(8,128)(2,1)}, u32[]{:S(2)}) copy-start(bf16[2,1024,512]{2,1,0:T(8,128)(2,1)} %three_ref.5) | copy-start | bytes 6291460
  14.1 1.3 %copy-start = (bf16[4,512,256]{2,1,0:T(8,128)(2,1)S(1)}, bf16[4,512,256]{2,1,0:T(8,128)(2,1)}, u32[]{:S(2)}) copy-start(bf16[4,512,256]{2,1,0:T(8,128)(2,1)} %coeff_ref.9) | copy-start | bytes 3145732
  14.1 1.4 %copy-start.3 = (bf16[4,256,256]{2,1,0:T(8,128)(2,1)S(1)}, bf16[4,256,256]{2,1,0:T(8,128)(2,1)}, u32[]{:S(2)}) copy-start(bf16[4,256,256]{2,1,0:T(8,128)(2,1)} %amps_ref.7) | copy-start | bytes 1572868
  16.9 7.5 %copy-start.5 = (bf16[512,256]{1,0:T(8,128)(2,1)S(1)}, bf16[512,256]{1,0:T(8,128)(2,1)}, u32[]{:S(2)}) copy-start(bf16[512,256]{1,0:T(8,128)(2,1)} %get-tuple-element.59.extra_ref) | copy-start | bytes 786436
  16.9 10.4 %copy-start.8 = (f32[22]{0:T(128)S(1)}, f32[22]{0:T(128)}, u32[]{:S(2)}) copy-start(f32[22]{0:T(128)} %get-tuple-element.31.nums) | copy-start | bytes 268
  16.9 10.4 %copy-start.10 = (f32[4,256]{1,0:T(4,128)S(1)}, f32[4,256]{1,0:T(4,128)}, u32[]{:S(2)}) copy-start(f32[4,256]{1,0:T(4,128)} %eps_ref.1) | copy-start | bytes 12292
  17.0 4.7 %collective-permute-start.3 = (bf16[2,512,256]{2,1,0:T(8,128)(2,1)S(1)}, bf16[2,512,256]{2,1,0:T(8,128)(2,1)S(1)}, u32[]{:S(2)}, u32[]{:S(2)}) collective-permute-start(bf16[2,512,256]{2,1,0:T(8,128)(2,1)S(1)} %get-tuple-element.46), channel_id=1, source_target_pairs={{0,1},{1,0},{2,3},{3,2},{4,5},{5,4},{6,7},{7,6},{8,9},{9,8},{10,11... | collective-permute-start | bytes 1572872 | tf_op jit(solution)/shard_map/ppermute | solution.py:70
  17.0 18.4 %collective-permute-start.5 = (bf16[1024,256]{1,0:T(8,128)(2,1)S(1)}, bf16[1024,256]{1,0:T(8,128)(2,1)S(1)}, u32[]{:S(2)}, u32[]{:S(2)}) collective-permute-start(bf16[1024,256]{1,0:T(8,128)(2,1)S(1)} %shard_map.115.after_ref), channel_id=1, source_target_pairs={{0,7},{1,2},{2,1},{3,4},{4,3},{5,6},{6,5},{7,0},{8,15},{9,10},{10,... | collective-permute-start | bytes 1572872 | tf_op jit(solution)/shard_map/ppermute | solution.py:73
  20.6 1.1 %collective-permute-start.2 = (f32[9]{0:T(128)S(1)}, f32[9]{0:T(128)S(1)}, u32[]{:S(2)}, u32[]{:S(2)}) collective-permute-start(f32[9]{0:T(128)S(1)} %get-tuple-element.45), channel_id=1, source_target_pairs={{0,1},{1,0},{2,3},{3,2},{4,5},{5,4},{6,7},{7,6},{8,9},{9,8},{10,11... | collective-permute-start | bytes 116 | tf_op jit(solution)/shard_map/ppermute | solution.py:70
  23.5 12.0 %collective-permute-start.4 = (bf16[1024,256]{1,0:T(8,128)(2,1)S(1)}, bf16[1024,256]{1,0:T(8,128)(2,1)S(1)}, u32[]{:S(2)}, u32[]{:S(2)}) collective-permute-start(bf16[1024,256]{1,0:T(8,128)(2,1)S(1)} %get-tuple-element.47), channel_id=1, source_target_pairs={{0,1},{1,0},{2,3},{3,2},{4,5},{5,4},{6,7},{7,6},{8,9},{9,8},{10,11... | collective-permute-start | bytes 1572872 | tf_op jit(solution)/shard_map/ppermute | solution.py:70
  23.8 11.7 %collective-permute-start.7 = (bf16[256,256]{1,0:T(8,128)(2,1)S(1)}, bf16[256,256]{1,0:T(8,128)(2,1)S(1)}, u32[]{:S(2)}, u32[]{:S(2)}) collective-permute-start(bf16[256,256]{1,0:T(8,128)(2,1)S(1)} %get-tuple-element.37.after_ref), channel_id=1, source_target_pairs={{0,7},{1,2},{2,1},{3,4},{4,3},{5,6},{6,5},{7,0},{8,15},{9,10},{10,... | collective-permute-start | bytes 393224 | tf_op jit(solution)/shard_map/ppermute | solution.py:73
  24.4 11.0 %collective-permute-start.6 = (bf16[256,256]{1,0:T(8,128)(2,1)S(1)}, bf16[256,256]{1,0:T(8,128)(2,1)S(1)}, u32[]{:S(2)}, u32[]{:S(2)}) collective-permute-start(bf16[256,256]{1,0:T(8,128)(2,1)S(1)} %get-tuple-element.49), channel_id=1, source_target_pairs={{0,1},{1,0},{2,3},{3,2},{4,5},{5,4},{6,7},{7,6},{8,9},{9,8},{10,11... | collective-permute-start | bytes 393224 | tf_op jit(solution)/shard_map/ppermute | solution.py:70
  24.4 21.5 %collective-permute-start.15 = (bf16[512,256]{1,0:T(8,128)(2,1)S(1)}, bf16[512,256]{1,0:T(8,128)(2,1)S(1)}, u32[]{:S(2)}, u32[]{:S(2)}) collective-permute-start(bf16[512,256]{1,0:T(8,128)(2,1)S(1)} %copy-done.5), channel_id=1, source_target_pairs={{0,7},{1,2},{2,1},{3,4},{4,3},{5,6},{6,5},{7,0},{8,15},{9,10},{10,... | collective-permute-start | bytes 786440 | tf_op jit(solution)/shard_map/ppermute | solution.py:73
  36.4 10.8 %collective-permute-start.10 = (bf16[256,256]{1,0:T(8,128)(2,1)S(1)}, bf16[256,256]{1,0:T(8,128)(2,1)S(1)}, u32[]{:S(2)}, u32[]{:S(2)}) collective-permute-start(bf16[256,256]{1,0:T(8,128)(2,1)S(1)} %get-tuple-element.50.amp_ref.refs_0_), channel_id=1, source_target_pairs={{0,24},{8,16},{16,8},{24,0},{1,25},{9,17},{17,9},{25,1},{2,26},{10... | collective-permute-start | bytes 393224 | tf_op jit(solution)/shard_map/ppermute | solution.py:78
  40.1 8.9 %collective-permute-start.9 = (bf16[256,256]{1,0:T(8,128)(2,1)S(1)}, bf16[256,256]{1,0:T(8,128)(2,1)S(1)}, u32[]{:S(2)}, u32[]{:S(2)}) collective-permute-start(bf16[256,256]{1,0:T(8,128)(2,1)S(1)} %get-tuple-element.50.amp_ref.refs_0_), channel_id=1, source_target_pairs={{0,16},{8,24},{16,0},{24,8},{1,17},{9,25},{17,1},{25,9},{2,18},{10... | collective-permute-start | bytes 393224 | tf_op jit(solution)/shard_map/ppermute | solution.py:78
  40.6 8.4 %collective-permute-start.8 = (bf16[256,256]{1,0:T(8,128)(2,1)S(1)}, bf16[256,256]{1,0:T(8,128)(2,1)S(1)}, u32[]{:S(2)}, u32[]{:S(2)}) collective-permute-start(bf16[256,256]{1,0:T(8,128)(2,1)S(1)} %get-tuple-element.50.amp_ref.refs_0_), channel_id=1, source_target_pairs={{0,8},{8,0},{16,24},{24,16},{1,9},{9,1},{17,25},{25,17},{2,10},{10... | collective-permute-start | bytes 393224 | tf_op jit(solution)/shard_map/ppermute | solution.py:78
  41.2 11.3 %collective-permute-start.13 = (bf16[256,256]{1,0:T(8,128)(2,1)S(1)}, bf16[256,256]{1,0:T(8,128)(2,1)S(1)}, u32[]{:S(2)}, u32[]{:S(2)}) collective-permute-start(bf16[256,256]{1,0:T(8,128)(2,1)S(1)} %get-tuple-element.53), channel_id=1, source_target_pairs={{0,24},{1,25},{2,26},{3,27},{4,28},{5,29},{6,30},{7,31}} | collective-permute-start | bytes 393224 | tf_op jit(solution)/shard_map/ppermute | solution.py:349
  46.0 6.5 %collective-permute-start.12 = (bf16[256,256]{1,0:T(8,128)(2,1)S(1)}, bf16[256,256]{1,0:T(8,128)(2,1)S(1)}, u32[]{:S(2)}, u32[]{:S(2)}) collective-permute-start(bf16[256,256]{1,0:T(8,128)(2,1)S(1)} %get-tuple-element.53), channel_id=1, source_target_pairs={{0,16},{1,17},{2,18},{3,19},{4,20},{5,21},{6,22},{7,23}} | collective-permute-start | bytes 393224 | tf_op jit(solution)/shard_map/ppermute | solution.py:349
  47.3 5.2 %collective-permute-start.11 = (bf16[256,256]{1,0:T(8,128)(2,1)S(1)}, bf16[256,256]{1,0:T(8,128)(2,1)S(1)}, u32[]{:S(2)}, u32[]{:S(2)}) collective-permute-start(bf16[256,256]{1,0:T(8,128)(2,1)S(1)} %get-tuple-element.53), channel_id=1, source_target_pairs={{0,8},{1,9},{2,10},{3,11},{4,12},{5,13},{6,14},{7,15}} | collective-permute-start | bytes 393224 | tf_op jit(solution)/shard_map/ppermute | solution.py:349
  50.9 7.7 %collective-permute-start.16 = (bf16[2,256,256]{2,1,0:T(8,128)(2,1)S(1)}, bf16[2,256,256]{2,1,0:T(8,128)(2,1)S(1)}, u32[]{:S(2)}, u32[]{:S(2)}) collective-permute-start(bf16[2,256,256]{2,1,0:T(8,128)(2,1)S(1)} %shard_map.124), channel_id=1, source_target_pairs={{0,7},{1,2},{2,1},{3,4},{4,3},{5,6},{6,5},{7,0},{8,15},{9,10},{10,... | collective-permute-start | bytes 786440 | tf_op jit(solution)/shard_map/ppermute | solution.py:73
  54.3 4.2 %collective-permute-start.14 = (bf16[2,256,256]{2,1,0:T(8,128)(2,1)S(1)}, bf16[2,256,256]{2,1,0:T(8,128)(2,1)S(1)}, u32[]{:S(2)}, u32[]{:S(2)}) collective-permute-start(bf16[2,256,256]{2,1,0:T(8,128)(2,1)S(1)} %shard_map.122), channel_id=1, source_target_pairs={{0,1},{1,0},{2,3},{3,2},{4,5},{5,4},{6,7},{7,6},{8,9},{9,8},{10,11... | collective-permute-start | bytes 786440 | tf_op jit(solution)/shard_map/ppermute | solution.py:70

commit v4 on v3

v4 whole, which is shorter than its diff:
```python
import math

import jax
import jax.numpy as jnp
from jax import lax
from jax.experimental import pallas as pl
from jax.experimental.pallas import tpu as pltpu
from jax.sharding import PartitionSpec as P

F32 = jnp.float32
BF16 = jnp.bfloat16
I32 = jnp.int32
NN = ((1,), (0,))
NT = ((1,), (1,))

VMEM = pl.BlockSpec(memory_space=pltpu.VMEM)
SMEM = pl.BlockSpec(memory_space=pltpu.SMEM)
ANY = pl.BlockSpec(memory_space=pl.ANY)
HBM = pl.BlockSpec(memory_space=pltpu.HBM)

MINE, EXTRA, OWNER, FIRST, SECOND, WHOSE, NV_MINE, NV_EXTRA, OCC_MINE, OCC_EXTRA, ROLE_PAIR = range(11)


def whole(number):
    return number.astype(jnp.int32)


def mxu(a, b, dims):
    return lax.dot_general(a, b, (dims, ((), ())), preferred_element_type=F32)


def call(body, ins, outs, args, scratch=(), vmem=48):
    return pl.pallas_call(
        body,
        in_specs=ins,
        out_specs=[spec for spec, _, _ in outs],
        out_shape=[jax.ShapeDtypeStruct(shape, dtype) for _, shape, dtype in outs],
        scratch_shapes=list(scratch),
        cost_estimate=pl.CostEstimate(flops=1, bytes_accessed=1, transcendentals=0),
        compiler_params=pltpu.CompilerParams(vmem_limit_bytes=vmem * 1024 * 1024),
    )(*args)


def local(
    three_index, coeff, amps, eps_virt, eps_occ, nvirt, pair_occ, partners, coupling, pair_owner
):
    columns = lax.axis_size("pairs")
    roles = lax.axis_size("role")
    occ_block, aux, pao = three_index.shape
    pairs, _, virt = coeff.shape
    partner_count = partners.shape[1]
    slots = 2
    assert roles == pairs and columns % 2 == 0 and virt % 2 == 0
    tile = min(256, aux)
    pao_scale = 1.0 / math.sqrt(pao)
    aux_scale = 1.0 / math.sqrt(aux)
    virt_scale = 1.0 / math.sqrt(virt)
    square = (virt, virt)
    part = virt // 2
    sq_b = (VMEM, square, BF16)
    sq_f = (VMEM, square, F32)
    two_b = (VMEM, (2, virt, virt), BF16)
    all_s = (VMEM, (pairs, virt, virt), BF16)
    half = (VMEM, (aux, virt), BF16)

    inner_of = [i ^ 1 for i in range(columns)]
    outer_of = [(i + (1 if i % 2 else -1)) % columns for i in range(columns)]

    def inner(x):
        return lax.ppermute(x, "pairs", list(enumerate(inner_of)))

    def outer(x):
        return lax.ppermute(x, "pairs", list(enumerate(outer_of)))

    def owners(x, other):
        pairings = [
            (s * columns + i, s * columns + j) for s in range(1, roles) for i, j in enumerate(other)
        ]
        return lax.ppermute(x, ("role", "pairs"), pairings)

    def swap(x, by):
        return lax.ppermute(x, "role", [(i, i ^ by) for i in range(roles) if i ^ by])

    def pairs_of_roles(owner_ref):
        of_role = [jnp.int32(0)] * roles
        for p in range(pairs):
            earlier = jnp.int32(0)
            for o in range(p):
                earlier += (owner_ref[o] == owner_ref[p]).astype(I32)
            for s in range(roles):
                hit = (earlier == 0) & (owner_ref[p] == s) if s else earlier == 1
                of_role[s] = jnp.where(hit, p, of_role[s])
        return of_role

    def pick(numbers, at):
        chosen = numbers[0]
        for s in range(1, len(numbers)):
            chosen = jnp.where(at == s, numbers[s], chosen)
        return chosen

    weights = 2 * pairs
    riders = 16
    own_weights = ROLE_PAIR + roles

    def plan_body(
        owner_hbm, occ_hbm, partner_hbm, coupling_hbm, eps_hbm, nvirt_hbm, coeff_hbm,
        low_ref, high_ref, nums,
        owner_ref, occ_ref, partner_ref, coupling_ref, eps_ref, nvirt_ref, near_w, sems,
    ):
        small = [
            pltpu.make_async_copy(source, target, sems.at[at])
            for at, (source, target) in enumerate(
                (
                    (owner_hbm, owner_ref),
                    (occ_hbm, occ_ref),
                    (partner_hbm, partner_ref),
                    (coupling_hbm, coupling_ref),
                    (eps_hbm, eps_ref),
                    (nvirt_hbm, nvirt_ref),
                )
            )
        ]
        for copy in small:
            copy.start()
        role = lax.axis_index("role")
        column = lax.axis_index("pairs")
        small[0].wait()
        of_role = pairs_of_roles(owner_ref)
        extra = of_role[0]
        mine = pick(of_role, role)
        large = [
            pltpu.make_async_copy(coeff_hbm.at[mine, :, pl.ds(0, part)], low_ref.at[pl.ds(0, pao)], sems.at[6]),
            pltpu.make_async_copy(coeff_hbm.at[mine, :, pl.ds(part, part)], high_ref, sems.at[7]),
        ]
        for copy in large:
            copy.start()
        for copy in small[1:]:
            copy.wait()
        nums[MINE] = mine.astype(F32)
        nums[EXTRA] = extra.astype(F32)
        nums[OWNER] = owner_ref[extra].astype(F32)
        for s in range(roles):
            nums[ROLE_PAIR + s] = of_role[s].astype(F32)
        nums[NV_MINE] = nvirt_ref[mine].astype(F32)
        nums[NV_EXTRA] = nvirt_ref[extra].astype(F32)
        nums[FIRST] = (occ_ref[0, mine] - column * occ_block).astype(F32)
        odd = lax.rem(column, 2) == 1
        inner_at = jnp.where(odd, 0, 2)
        outer_at = 2 - inner_at
        occ_all = occ_block * columns
        second = lax.rem(occ_ref[1, mine] - (column - 1) * occ_block + occ_all, occ_all)
        block = (second >= occ_block).astype(I32) + (second >= 2 * occ_block).astype(I32)
        place = (second - block * occ_block).astype(F32)
        nums[SECOND] = place
        lane = lax.broadcasted_iota(I32, (riders, part), 1)
        row = lax.broadcasted_iota(I32, (riders, part), 0)
        told = jnp.where(lane == weights, place, 0.0)
        nums[WHOSE] = jnp.where(block == 1, 0, jnp.where(block == inner_at, 1, 2)).astype(F32)
        nums[OCC_MINE] = eps_ref[occ_ref[0, mine]] + eps_ref[occ_ref[1, mine]]
        nums[OCC_EXTRA] = eps_ref[occ_ref[0, extra]] + eps_ref[occ_ref[1, extra]]
        pair_all = pairs * columns
        for which, pair in enumerate((mine, extra)):
            for q in range(3 * pairs):
                near_w[q] = jnp.float32(0)
            for k in range(partner_count):
                at = lax.rem(partner_ref[pair, k] - (column - 1) * pairs + pair_all, pair_all)
                near_w[at] += coupling_ref[pair, k]
            for q in range(pairs):
                to = which * pairs + q
                nums[own_weights + 2 * which * pairs + q] = near_w[pairs + q]
                nums[own_weights + (2 * which + 1) * pairs + q] = near_w[inner_at * pairs + q]
                told = jnp.where(lane == to, near_w[outer_at * pairs + q], told)
        coarse = told.astype(BF16).astype(F32)
        middle = (told - coarse).astype(BF16).astype(F32)
        fine = told - coarse - middle
        told = jnp.where(row == 0, coarse, jnp.where(row == 1, middle, jnp.where(row == 2, fine, 0.0)))
        low_ref[pao:, :] = told.astype(BF16)
        for copy in large:
            copy.wait()

    rode = (VMEM, (pao + riders, part), BF16)
    x_low, x_high, nums = call(
        plan_body,
        [HBM] * 7,
        [rode, (VMEM, (pao, part), BF16), (SMEM, (own_weights + 2 * weights,), F32)],
        (pair_owner, pair_occ.T, partners, coupling, eps_occ, nvirt, coeff),
        scratch=[
            pltpu.SMEM(pair_owner.shape, I32),
            pltpu.SMEM(pair_occ.shape[::-1], I32),
            pltpu.SMEM(partners.shape, I32),
            pltpu.SMEM(coupling.shape, F32),
            pltpu.SMEM(eps_occ.shape, F32),
            pltpu.SMEM(nvirt.shape, I32),
            pltpu.SMEM((3 * pairs,), F32),
            pltpu.SemaphoreType.DMA((8,)),
        ],
        vmem=60,
    )
    low_out, high_out = outer(x_low), outer(x_high)

    def told_of(low_ref):
        rows = low_ref[pao:, :].astype(F32)
        return rows[0:1] + rows[1:2] + rows[2:3]

    def overlaps(x, coeff_ref, out_ref):
        turned = x.T
        for q in range(pairs):
            s = mxu(turned, coeff_ref[q], NN) * (1.0 / pao)
            out_ref[q] = s.astype(BF16)

    def coupled(s_ref, parts):
        total = None
        for at, weight, amp in parts:
            s = s_ref[at]
            u = mxu(s, amp, NN).astype(BF16)
            term = weight * mxu(u, s, NT)
            total = term if total is None else total + term
        return total

    def half_into(y_ref, three_ref, at_occ, x):
        for at in range(0, aux, tile):
            rows = pl.ds(at, tile)
            y_ref[rows, :] = (mxu(three_ref[at_occ, rows, :], x, NN) * pao_scale).astype(BF16)

    def outer_low_body(three_ref, x_ref, y_ref):
        half_into(y_ref, three_ref, whole(told_of(x_ref)[0, weights]), x_ref[:pao, :])
        y_ref[aux:, :] = jnp.zeros((2 * riders, part), BF16)

    (y_low,) = call(
        outer_low_body,
        [VMEM, VMEM],
        [(VMEM, (aux + 2 * riders, part), BF16)],
        (three_index, low_out),
    )
    y_low_from_out = outer(y_low)

    def outer_high_body(three_ref, low_ref, x_ref, after_ref, y_ref):
        half_into(y_ref, three_ref, whole(told_of(low_ref)[0, weights]), x_ref[...])
        y_ref[aux:, :] = jnp.zeros((riders, part), BF16)

    (y_high,) = call(
        outer_high_body,
        [VMEM, VMEM, VMEM, ANY],
        [(VMEM, (aux + riders, part), BF16)],
        (three_index, low_out, high_out, y_low),
    )
    y_high_from_out = outer(y_high)

    *sent, _ = lax.optimization_barrier((three_index, coeff, amps, pair_owner, y_high))
    three_in, coeff_in, amps_in, owner_in = [inner(x) for x in sent]

    def outer_body(coeff_ref, amps_ref, low_ref, high_ref, after_ref, s_ref, c_ref, x_ref):
        x_ref[:, :part] = low_ref[:pao, :]
        x_ref[:, part:] = high_ref[...]
        overlaps(x_ref[...], coeff_ref, s_ref)
        told = told_of(low_ref)
        c = coupled(s_ref, [(q, told[0, q], amps_ref[q]) for q in range(pairs)])
        c_ref[...] = c.astype(BF16)

    s_out, c_out = call(
        outer_body,
        [VMEM, VMEM, VMEM, VMEM, ANY],
        [all_s, sq_b],
        (coeff, amps, low_out, high_out, y_high),
        scratch=[pltpu.VMEM((pao, virt), BF16)],
    )
    c_from_out = outer(c_out)

    def own_half_body(
        nums, three_ref, three_in_ref, coeff_ref, after_ref, first_ref, second_ref, extra_ref
    ):
        x = coeff_ref[whole(nums[MINE])]
        extra_ref[...] = coeff_ref[whole(nums[EXTRA])]
        turned = x.T
        first = whole(nums[FIRST])
        for at in range(0, aux, tile):
            rows = pl.ds(at, tile)
            first_ref[:, rows] = (mxu(turned, three_ref[first, rows, :], NT) * pao_scale).astype(BF16)
        for whose, source in enumerate((three_ref, three_in_ref)):

            @pl.when(whole(nums[WHOSE]) == whose)
            def _():
                half_into(second_ref, source, whole(nums[SECOND]), x)

    first_t, second, x_extra = call(
        own_half_body,
        [SMEM, VMEM, VMEM, VMEM, ANY],
        [(VMEM, (virt, aux), BF16), (VMEM, (aux, virt), BF16), (VMEM, (pao, virt), BF16)],
        (nums, three_index, three_in, coeff, c_out),
    )
    x_extra_out = outer(x_extra)

    def own_body(
        nums, coeff_ref, coeff_in_ref, amps_ref, amps_in_ref, eps_ref, after_ref,
        s_ref, s_in_ref, c_ref, gain_ref, gain_extra_ref,
    ):
        mine, extra = whole(nums[MINE]), whole(nums[EXTRA])
        x = coeff_ref[mine]
        total = None
        for at, of_s, of_coeff, of_amps in (
            (own_weights, s_ref, coeff_ref, amps_ref),
            (own_weights + pairs, s_in_ref, coeff_in_ref, amps_in_ref),
        ):
            overlaps(x, of_coeff, of_s)
            c = coupled(of_s, [(q, nums[at + q], of_amps[q]) for q in range(pairs)])
            total = c if total is None else total + c
        c_ref[...] = total

        def gain(pair, count, occupied):
            row = jnp.broadcast_to(eps_ref[pl.ds(pair, 1), :], square)
            energy = row + row.T - occupied
            inside = (lax.broadcasted_iota(I32, square, 0) < count) & (
                lax.broadcasted_iota(I32, square, 1) < count
            )
            return jnp.where(inside, 1.0 / (energy + 1.0), 0.0)

        gain_ref[...] = gain(mine, whole(nums[NV_MINE]), nums[OCC_MINE])
        gain_extra_ref[...] = gain(extra, whole(nums[NV_EXTRA]), nums[OCC_EXTRA])

    s_own, s_in, c_own, gain, gain_extra = call(
        own_body,
        [SMEM] + [VMEM] * 5 + [ANY],
        [all_s, all_s, sq_f, sq_f, sq_f],
        (nums, coeff, coeff_in, amps, amps_in, eps_virt, first_t),
    )

    def first_body(
        nums, first_ref, second_ref, low_ref, high_ref, amps_ref, c_ref, co_ref, gain_ref, amp_ref, k_ref
    ):
        first = first_ref[...]
        outside = whole(nums[WHOSE]) == 2

        @pl.when(outside)
        def _():
            k_ref[:, :part] = mxu(first, low_ref[:aux, :], NN) * aux_scale
            k_ref[:, part:] = mxu(first, high_ref[:aux, :], NN) * aux_scale

        @pl.when(jnp.logical_not(outside))
        def _():
            k_ref[...] = mxu(first, second_ref[...], NN) * aux_scale

        old = amps_ref[whole(nums[MINE])].astype(F32)
        c = c_ref[...] + co_ref[...].astype(F32)
        amp_ref[...] = (gain_ref[...] * (old - k_ref[...] - c)).astype(BF16)

    amp, k_first = call(
        first_body,
        [SMEM] + [VMEM] * 8,
        [sq_b, sq_f],
        (nums, first_t, second, y_low_from_out, y_high_from_out, amps, c_own, c_from_out, gain),
    )
    amp_roles = [amp] + [swap(amp, m) for m in range(1, roles)]

    def second_body(amp_ref, k_ref, out_ref, out_b_ref):
        amp = amp_ref[...]
        k = k_ref[...]
        right = k + mxu(k.astype(BF16), amp, NN) * virt_scale
        both = right + mxu(amp.T, right.astype(BF16), NN) * virt_scale
        rest = amp.astype(F32) - both
        out_ref[...] = rest
        out_b_ref[...] = rest.astype(BF16)

    rest, rest_b = call(
        second_body, [VMEM, VMEM], [sq_f, sq_b], (amp, k_first)
    )
    rests = [lax.ppermute(rest_b, "role", [(0, s)]) for s in range(1, roles)]

    def extra_body(nums, coeff_ref, in_ref, out_ref, after_ref, own_s_ref, in_s_ref, out_s_ref):
        overlaps(out_ref[...], coeff_ref, out_s_ref)
        x = coeff_ref[whole(nums[EXTRA])]
        overlaps(x, coeff_ref, own_s_ref)
        overlaps(x, in_ref, in_s_ref)

    se_own, se_in, se_out = call(
        extra_body,
        [SMEM, VMEM, VMEM, VMEM, ANY],
        [all_s, all_s, all_s],
        (nums, coeff, coeff_in, x_extra_out, rest),
    )

    def outer_again_body(nums, low_ref, s_ref, se_ref, *refs):
        amp_refs, c_ref = refs[:roles], refs[-1]
        role = lax.axis_index("role")

        @pl.when(role > 0)
        def _():
            told = told_of(low_ref)
            for slot, of_s in enumerate((s_ref, se_ref)):
                parts = []
                for m in range(roles):
                    at = whole(nums[ROLE_PAIR + (role ^ m)])
                    weight = pick([told[:, slot * pairs + q : slot * pairs + q + 1] for q in range(pairs)], at)
                    parts.append((at, weight, amp_refs[m][...]))
                c_ref[slot] = coupled(of_s, parts).astype(BF16)

    (cc_out,) = call(
        outer_again_body,
        [SMEM] + [VMEM] * (3 + roles),
        [two_b],
        (nums, low_out, s_out, se_out, *amp_roles),
    )
    cc_from_out = owners(cc_out, outer_of)

    later = lax.optimization_barrier((*amp_roles, cc_out))[:roles]
    amp_roles_in = [owners(x, inner_of) for x in later]

    def own_again_body(nums, owner_in, rest_ref, s_ref, s_in_ref, se_ref, se_in_ref, *refs):
        amp_refs, amp_in_refs, rest_refs = refs[:roles], refs[roles : 2 * roles], refs[2 * roles : -2]
        out_ref, out_extra_ref = refs[-2:]
        role = lax.axis_index("role")

        @pl.when(role > 0)
        def _():
            of_role = [whole(nums[ROLE_PAIR + s]) for s in range(roles)]
            of_role_in = pairs_of_roles(owner_in)
            totals = []
            for slot, of_s, of_s_in in ((0, s_ref, s_in_ref), (1, se_ref, se_in_ref)):
                total = None
                for at_w, of, pair_of, amp_of in (
                    (own_weights + 2 * slot * pairs, of_s, of_role, amp_refs),
                    (own_weights + (2 * slot + 1) * pairs, of_s_in, of_role_in, amp_in_refs),
                ):
                    parts = []
                    for m in range(roles):
                        at = pick(pair_of, role ^ m)
                        parts.append((at, nums[at_w + at], amp_of[m][...]))
                    c = coupled(of, parts)
                    total = c if total is None else total + c
                totals.append(total)
            out_ref[...] = rest_ref[...] - totals[0]
            total = -totals[1]
            for s in range(1, roles):
                total += jnp.where(role == s, rest_refs[s - 1][...].astype(F32), 0.0)
            out_extra_ref[...] = total

    rest, rest_extra = call(
        own_again_body,
        [SMEM] * 2 + [VMEM] * (5 + 3 * roles - 1),
        [sq_f, sq_f],
        (nums, owner_in, rest, s_own, s_in, se_own, se_in, *amp_roles, *amp_roles_in, *rests),
    )

    def last_body(
        nums, coeff_ref, gain_ref, gain_extra_ref, rest_ref, rest_extra_ref, c_ref, amp_ref, orb_ref
    ):
        role = lax.axis_index("role")

        def store(slot, here, gain, rest, pair):
            @pl.when(here)
            def _():
                amp = (gain[...] * (rest[...] - c_ref[slot].astype(F32))).astype(BF16)
                amp_ref[slot] = amp
                x = coeff_ref[pair]
                orb_ref[slot] = (x.astype(F32) + mxu(x, amp, NN) * virt_scale).astype(BF16)

            @pl.when(jnp.logical_not(here))
            def _():
                amp_ref[slot] = jnp.zeros(square, BF16)
                orb_ref[slot] = jnp.zeros((pao, virt), BF16)

        store(0, role > 0, gain_ref, rest_ref, whole(nums[MINE]))
        store(1, role == whole(nums[OWNER]), gain_extra_ref, rest_extra_ref, whole(nums[EXTRA]))

    amps_out, dressed_out = call(
        last_body,
        [SMEM] + [VMEM] * 6,
        [(VMEM, (slots, virt, virt), BF16), (VMEM, (slots, pao, virt), BF16)],
        (nums, coeff, gain, gain_extra, rest, rest_extra, cc_from_out),
    )
    return amps_out, dressed_out


def solution(mesh):
    in_specs = (
        P("pairs", None, None),
        P("pairs", None, None),
        P("pairs", None, None),
        P("pairs", None),
        P(),
        P("pairs"),
        P("pairs", None),
        P("pairs", None),
        P("pairs", None),
        P("pairs"),
    )
    out_specs = (P(("role", "pairs"), None, None), P(("role", "pairs"), None, None))
    return jax.shard_map(local, mesh=mesh, in_specs=in_specs, out_specs=out_specs, check_vma=False)
```

time: 60.4 us -> 70.8 us (1.17)
  the two profiles are of different devices: /device:TPU:0 before, /device:TPU:5 now
where the time goes in v4:
time: 70.8 us; the launch traced here: 70.3 us
  starting transfers between devices  34.6 us (49%)
  Pallas kernels  20.9 us (30%)
  waiting for transfers between devices  12.5 us (18%)
  local copies, waits for them, and re-layouts  1.37 us (2%)
  between operations  0.92 us (1%)
    pallas_call x12, Pallas kernels, call(): pl.pallas_call(body, in_specs=ins, out_specs=[spec for spec, _, _ in outs...  20.9 us
    ppermute x5, starting transfers between devices, owners(): return lax.ppermute(x, ('role', 'pairs'), pairings)  10.8 us
    ppermute x4, starting transfers between devices, inner(): return lax.ppermute(x, 'pairs', list(enumerate(inner_of)))  8.6 us
    ppermute x3, starting transfers between devices, swap(): lax.ppermute(x, 'role', [(i, i ^ by) for i in range(roles) if i ^ by])  8.37 us
    ppermute x6, waiting for transfers between devices, outer(): return lax.ppermute(x, 'pairs', list(enumerate(outer_of)))  7.63 us
    ppermute x6, starting transfers between devices, outer(): return lax.ppermute(x, 'pairs', list(enumerate(outer_of)))  4.23 us
    ppermute x4, waiting for transfers between devices, inner(): return lax.ppermute(x, 'pairs', list(enumerate(inner_of)))  3.74 us
    ppermute x3, starting transfers between devices, local(): rests = [lax.ppermute(rest_b, 'role', [(0, s)]) for s in range(1, roles)]  2.63 us
  transfers between devices with their start and end apart: 21, of which 6 were waited for; matrix products, arithmetic and copies ran while one was open for 0% of the time, Pallas kernels for 21%

profile of v4, /device:TPU:5, one launch (start us, length us, event | category | flops | bytes accessed | tf_op | source)
XLA Modules:
  0.0 70.3 jit_solution(14579437917713197719)
XLA Ops:
  0.6 2.4 %shard_map.113 = (bf16[528,128]{1,0:T(8,128)(2,1)}, bf16[512,128]{1,0:T(8,128)(2,1)}, f32[30]{0:T(128)}) custom-call(s32[4]{0:T(128)} %owner_hbm.1, s32[2,4]{1,0:T(2,128)} %bitcast.1, s32[4,8]{1,0:T(4,128)} %partner_hbm.1, f32[4,8]{1,0:T(4,128)} %coupling_hbm.1, f32[16]{0:T(128)} %eps_hbm.1, s32[4]{0:T(128)} %nvirt_hbm.1, bf16[4,512,256]{2,1,0:T(8,128)(2,1)} %coeff_ref.9), custom_call_target="tpu_custom_call" | custom-call | flops 1 | bytes 1 | tf_op jit(solution)/shard_map/pallas_call | solution.py:33
  3.1 1.9 %collective-permute-start = (bf16[528,128]{1,0:T(8,128)(2,1)}, bf16[528,128]{1,0:T(8,128)(2,1)S(1)}, u32[]{:S(2)}, u32[]{:S(2)}) collective-permute-start(bf16[528,128]{1,0:T(8,128)(2,1)} %get-tuple-element.33), channel_id=1, source_target_pairs={{0,7},{1,2},{2,1},{3,4},{4,3},{5,6},{6,5},{7,0},{8,15},{9,10},{10,... | collective-permute-start | bytes 405512 | tf_op jit(solution)/shard_map/ppermute | solution.py:73
  5.0 0.0 copy-start
  5.0 0.0 copy-start.1
  5.0 0.1 collective-permute-start.1
  5.1 2.8 %collective-permute-done.x_ref.low_ref = bf16[528,128]{1,0:T(8,128)(2,1)S(1)} collective-permute-done((bf16[528,128]{1,0:T(8,128)(2,1)}, bf16[528,128]{1,0:T(8,128)(2,1)S(1)}, u32[]{:S(2)}, u32[]{:S(2)}) %collective-permute-start) | collective-permute-done | bytes 135200 | tf_op jit(solution)/shard_map/ppermute | solution.py:73
  7.9 2.1 %shard_map.114.after_ref = bf16[1056,128]{1,0:T(8,128)(2,1)S(1)} custom-call(bf16[2,1024,512]{2,1,0:T(8,128)(2,1)} %three_ref.5, bf16[528,128]{1,0:T(8,128)(2,1)S(1)} %collective-permute-done.x_ref.low_ref), custom_call_target="tpu_custom_call" | custom-call | flops 1 | bytes 1 | tf_op jit(solution)/shard_map/pallas_call | solution.py:33
  10.0 0.0 copy-start.2
  10.0 1.0 %collective-permute-done.1.x_ref.high_ref = bf16[512,128]{1,0:T(8,128)(2,1)S(1)} collective-permute-done((bf16[512,128]{1,0:T(8,128)(2,1)}, bf16[512,128]{1,0:T(8,128)(2,1)S(1)}, u32[]{:S(2)}, u32[]{:S(2)}) %collective-permute-start.1) | collective-permute-done | bytes 131104 | tf_op jit(solution)/shard_map/ppermute | solution.py:73
  11.0 2.1 %shard_map.115.after_ref = bf16[1040,128]{1,0:T(8,128)(2,1)S(1)} custom-call(bf16[2,1024,512]{2,1,0:T(8,128)(2,1)} %three_ref.5, bf16[528,128]{1,0:T(8,128)(2,1)S(1)} %collective-permute-done.x_ref.low_ref, bf16[512,128]{1,0:T(8,128)(2,1)S(1)} %collective-permute-done.1.x_ref.high_ref, bf16[1056,128]{1,0:T(8,128)(2,1)S(1)} %shard_map.114.after_ref), custom_call_target="tpu_custom_call" | custom-call | flops 1 | bytes 1 | tf_op jit(solution)/shard_map/pallas_call | solution.py:33
  13.2 3.5 %collective-permute-start.4 = (bf16[2,1024,512]{2,1,0:T(8,128)(2,1)}, bf16[2,1024,512]{2,1,0:T(8,128)(2,1)S(1)}, u32[]{:S(2)}, u32[]{:S(2)}) collective-permute-start(bf16[2,1024,512]{2,1,0:T(8,128)(2,1)} %three_ref.5), channel_id=1, source_target_pairs={{0,1},{1,0},{2,3},{3,2},{4,5},{5,4},{6,7},{7,6},{8,9},{9,8},{10,11... | collective-permute-start | bytes 6291464 | tf_op jit(solution)/shard_map/ppermute | solution.py:70
  16.7 0.0 copy-done
  16.7 0.1 collective-permute-start.2
  16.8 0.0 copy-done.1
  16.8 0.4 collective-permute-start.3
  17.2 0.0 collective-permute-start.6
  17.2 1.7 %collective-permute-start.7 = (bf16[1040,128]{1,0:T(8,128)(2,1)S(1)}, bf16[1040,128]{1,0:T(8,128)(2,1)S(1)}, u32[]{:S(2)}, u32[]{:S(2)}) collective-permute-start(bf16[1040,128]{1,0:T(8,128)(2,1)S(1)} %shard_map.115.after_ref), channel_id=1, source_target_pairs={{0,7},{1,2},{2,1},{3,4},{4,3},{5,6},{6,5},{7,0},{8,15},{9,10},{10,... | collective-permute-start | bytes 798728 | tf_op jit(solution)/shard_map/ppermute | solution.py:73
  19.0 0.9 %shard_map.116 = (bf16[4,256,256]{2,1,0:T(8,128)(2,1)S(1)}, bf16[256,256]{1,0:T(8,128)(2,1)S(1)}) custom-call(bf16[4,512,256]{2,1,0:T(8,128)(2,1)S(1)} %copy-done, bf16[4,256,256]{2,1,0:T(8,128)(2,1)S(1)} %copy-done.1, bf16[528,128]{1,0:T(8,128)(2,1)S(1)} %collective-permute-done.x_ref.low_ref, bf16[512,128]{1,0:T(8,128)(2,1)S(1)} %collective-permute-done.1.x_ref.high_ref, ...), custom_call_target="tpu_custom_call" | custom-call | flops 1 | bytes 1 | tf_op jit(solution)/shard_map/pallas_call | solution.py:33
  19.9 2.9 %collective-permute-done.4.three_in_ref = bf16[2,1024,512]{2,1,0:T(8,128)(2,1)S(1)} collective-permute-done((bf16[2,1024,512]{2,1,0:T(8,128)(2,1)}, bf16[2,1024,512]{2,1,0:T(8,128)(2,1)S(1)}, u32[]{:S(2)}, u32[]{:S(2)}) %collective-permute-start.4) | collective-permute-done | bytes 2097184 | tf_op jit(solution)/shard_map/ppermute | solution.py:70
  22.8 0.0 collective-permute-start.8
  22.8 1.3 %copy-done.4 = bf16[2,1024,512]{2,1,0:T(8,128)(2,1)} copy-done((bf16[2,1024,512]{2,1,0:T(8,128)(2,1)}, bf16[2,1024,512]{2,1,0:T(8,128)(2,1)S(1)}, u32[]{:S(2)}) %copy-start.4) | copy-done | bytes 2097176
  24.1 0.0 copy-done.2
  24.1 3.2 %shard_map.117 = (bf16[256,1024]{1,0:T(8,128)(2,1)S(1)}, bf16[1024,256]{1,0:T(8,128)(2,1)S(1)}, bf16[512,256]{1,0:T(8,128)(2,1)S(1)}) custom-call(f32[30]{0:T(128)S(1)} %copy-done.2, bf16[2,1024,512]{2,1,0:T(8,128)(2,1)} %three_ref.5, bf16[2,1024,512]{2,1,0:T(8,128)(2,1)} %copy-done.4, bf16[4,512,256]{2,1,0:T(8,128)(2,1)S(1)} %copy-done, ...), custom_call_target="tpu_custom_call" | custom-call | flops 1 | bytes 1 | tf_op jit(solution)/shard_map/pallas_call | solution.py:33
  27.3 0.0 collective-permute-done.3.amps_in_ref
  27.3 0.5 collective-permute-start.9
  27.8 0.0 collective-permute-done.2.coeff_in_ref.in_ref
  27.8 0.0 copy-done.3
  27.8 2.0 %shard_map.118 = (bf16[4,256,256]{2,1,0:T(8,128)(2,1)S(1)}, bf16[4,256,256]{2,1,0:T(8,128)(2,1)S(1)}, f32[256,256]{1,0:T(8,128)S(1)}, f32[256,256]{1,0:T(8,128)S(1)}, f32[256,256]{1,0:T(8,128)S(1)}) custom-call(f32[30]{0:T(128)S(1)} %copy-done.2, bf16[4,512,256]{2,1,0:T(8,128)(2,1)S(1)} %copy-done, ...), custom_call_target="tpu_custom_call" | custom-call | flops 1 | bytes 1 | tf_op jit(solution)/shard_map/pallas_call | solution.py:33
  29.8 3.8 %collective-permute-done.8.co_ref = bf16[256,256]{1,0:T(8,128)(2,1)S(1)} collective-permute-done((bf16[256,256]{1,0:T(8,128)(2,1)S(1)}, bf16[256,256]{1,0:T(8,128)(2,1)S(1)}, u32[]{:S(2)}, u32[]{:S(2)}) %collective-permute-start.8) | collective-permute-done | bytes 131104 | tf_op jit(solution)/shard_map/ppermute | solution.py:73
  33.6 0.0 collective-permute-done.7.high_ref
  33.6 0.0 collective-permute-done.6.low_ref
  33.6 1.0 %shard_map.119 = (bf16[256,256]{1,0:T(8,128)(2,1)S(1)}, f32[256,256]{1,0:T(8,128)S(1)}) custom-call(f32[30]{0:T(128)S(1)} %copy-done.2, bf16[256,1024]{1,0:T(8,128)(2,1)S(1)} %get-tuple-element.39.after_ref.first_ref, bf16[1024,256]{1,0:T(8,128)(2,1)S(1)} %get-tuple-element.43.second_ref, bf16[1056,128]{1,0:T(8,128)(2,1)S(1)} %collective-permute-done.6.low_ref, ...), custom_call_target="tpu_custom_call" | custom-call | flops 1 | bytes 1 | tf_op jit(solution)/shard_map/pallas_call | solution.py:33
  34.6 3.2 %collective-permute-start.10 = (bf16[256,256]{1,0:T(8,128)(2,1)S(1)}, bf16[256,256]{1,0:T(8,128)(2,1)S(1)}, u32[]{:S(2)}, u32[]{:S(2)}) collective-permute-start(bf16[256,256]{1,0:T(8,128)(2,1)S(1)} %get-tuple-element.55.amp_ref.refs_0_), channel_id=1, source_target_pairs={{0,8},{16,24},{24,16},{1,9},{17,25},{25,17},{2,10},{18,26},{26,18}... | collective-permute-start | bytes 393224 | tf_op jit(solution)/shard_map/ppermute | solution.py:82
  37.8 1.3 %collective-permute-start.11 = (bf16[256,256]{1,0:T(8,128)(2,1)S(1)}, bf16[256,256]{1,0:T(8,128)(2,1)S(1)}, u32[]{:S(2)}, u32[]{:S(2)}) collective-permute-start(bf16[256,256]{1,0:T(8,128)(2,1)S(1)} %get-tuple-element.55.amp_ref.refs_0_), channel_id=1, source_target_pairs={{0,16},{8,24},{24,8},{1,17},{9,25},{25,9},{2,18},{10,26},{26,10},{... | collective-permute-start | bytes 393224 | tf_op jit(solution)/shard_map/ppermute | solution.py:82
  39.1 3.9 %collective-permute-start.12 = (bf16[256,256]{1,0:T(8,128)(2,1)S(1)}, bf16[256,256]{1,0:T(8,128)(2,1)S(1)}, u32[]{:S(2)}, u32[]{:S(2)}) collective-permute-start(bf16[256,256]{1,0:T(8,128)(2,1)S(1)} %get-tuple-element.55.amp_ref.refs_0_), channel_id=1, source_target_pairs={{0,24},{8,16},{16,8},{1,25},{9,17},{17,9},{2,26},{10,18},{18,10},{... | collective-permute-start | bytes 393224 | tf_op jit(solution)/shard_map/ppermute | solution.py:82
  43.0 0.4 shard_map.120
  43.4 0.7 collective-permute-start.17
  44.1 0.0 collective-permute-done.10.refs_1_
  44.1 1.3 %collective-permute-start.18 = (bf16[256,256]{1,0:T(8,128)(2,1)S(1)}, bf16[256,256]{1,0:T(8,128)(2,1)S(1)}, u32[]{:S(2)}, u32[]{:S(2)}) collective-permute-start(bf16[256,256]{1,0:T(8,128)(2,1)S(1)} %get-tuple-element.59), channel_id=1, source_target_pairs={{0,16},{1,17},{2,18},{3,19},{4,20},{5,21},{6,22},{7,23}} | collective-permute-start | bytes 393224 | tf_op jit(solution)/shard_map/ppermute | solution.py:366
  45.4 0.0 collective-permute-done.9.out_ref
  45.4 0.7 collective-permute-start.19
  46.1 0.0 copy-start.5
  46.1 1.6 %shard_map.121 = (bf16[4,256,256]{2,1,0:T(8,128)(2,1)S(1)}, bf16[4,256,256]{2,1,0:T(8,128)(2,1)S(1)}, bf16[4,256,256]{2,1,0:T(8,128)(2,1)S(1)}) custom-call(f32[30]{0:T(128)S(1)} %copy-done.2, bf16[4,512,256]{2,1,0:T(8,128)(2,1)S(1)} %copy-done, bf16[4,512,256]{2,1,0:T(8,128)(2,1)S(1)} %collective-permute-done.2.coeff_in_ref.in_ref, ...), custom_call_target="tpu_custom_call" | custom-call | flops 1 | bytes 1 | tf_op jit(solution)/shard_map/pallas_call | solution.py:33
  47.6 0.0 collective-permute-done.11.refs_2_
  47.6 0.0 collective-permute-done.12.refs_3_
  47.7 1.4 %shard_map.122 = bf16[2,256,256]{2,1,0:T(8,128)(2,1)S(1)} custom-call(f32[30]{0:T(128)S(1)} %copy-done.2, bf16[528,128]{1,0:T(8,128)(2,1)S(1)} %collective-permute-done.x_ref.low_ref, bf16[4,256,256]{2,1,0:T(8,128)(2,1)S(1)} %get-tuple-element.53.s_ref, bf16[4,256,256]{2,1,0:T(8,128)(2,1)S(1)} %get-tuple-element.54.se_ref, ...), custom_call_target="tpu_custom_call" | custom-call | flops 1 | bytes 1 | tf_op jit(solution)/shard_map/pallas_call | solution.py:33
  49.1 2.1 %collective-permute-start.20 = (bf16[2,256,256]{2,1,0:T(8,128)(2,1)S(1)}, bf16[2,256,256]{2,1,0:T(8,128)(2,1)S(1)}, u32[]{:S(2)}, u32[]{:S(2)}) collective-permute-start(bf16[2,256,256]{2,1,0:T(8,128)(2,1)S(1)} %shard_map.122), channel_id=1, source_target_pairs={{8,15},{9,10},{10,9},{11,12},{12,11},{13,14},{14,13},{15,8},{16,23... | collective-permute-start | bytes 786440 | tf_op jit(solution)/shard_map/ppermute | solution.py:79
  51.2 0.0 copy-done.5
  51.2 4.6 %collective-permute-start.5 = (s32[4]{0:T(128)S(1)}, s32[4]{0:T(128)S(1)}, u32[]{:S(2)}, u32[]{:S(2)}) collective-permute-start(s32[4]{0:T(128)S(1)} %copy-done.5), channel_id=1, source_target_pairs={{0,1},{1,0},{2,3},{3,2},{4,5},{5,4},{6,7},{7,6},{8,9},{9,8},{10,11... | collective-permute-start | bytes 56 | tf_op jit(solution)/shard_map/ppermute | solution.py:70
  55.8 0.8 %collective-permute-done.5.owner_in = s32[4]{0:T(128)S(1)} collective-permute-done((s32[4]{0:T(128)S(1)}, s32[4]{0:T(128)S(1)}, u32[]{:S(2)}, u32[]{:S(2)}) %collective-permute-start.5) | collective-permute-done | bytes 48 | tf_op jit(solution)/shard_map/ppermute | solution.py:70
  56.6 2.2 %collective-permute-start.13 = (bf16[256,256]{1,0:T(8,128)(2,1)S(1)}, bf16[256,256]{1,0:T(8,128)(2,1)S(1)}, u32[]{:S(2)}, u32[]{:S(2)}) collective-permute-start(bf16[256,256]{1,0:T(8,128)(2,1)S(1)} %get-tuple-element.55.amp_ref.refs_0_), channel_id=1, source_target_pairs={{8,9},{9,8},{10,11},{11,10},{12,13},{13,12},{14,15},{15,14},{16,17... | collective-permute-start | bytes 393224 | tf_op jit(solution)/shard_map/ppermute | solution.py:79
  58.8 0.0 collective-permute-done.17.refs_8_
  58.8 2.1 %collective-permute-start.14 = (bf16[256,256]{1,0:T(8,128)(2,1)S(1)}, bf16[256,256]{1,0:T(8,128)(2,1)S(1)}, u32[]{:S(2)}, u32[]{:S(2)}) collective-permute-start(bf16[256,256]{1,0:T(8,128)(2,1)S(1)} %collective-permute-done.10.refs_1_), channel_id=1, source_target_pairs={{8,9},{9,8},{10,11},{11,10},{12,13},{13,12},{14,15},{15,14},{16,17... | collective-permute-start | bytes 393224 | tf_op jit(solution)/shard_map/ppermute | solution.py:79
  61.0 0.0 collective-permute-done.18.refs_9_
  61.0 2.2 %collective-permute-start.15 = (bf16[256,256]{1,0:T(8,128)(2,1)S(1)}, bf16[256,256]{1,0:T(8,128)(2,1)S(1)}, u32[]{:S(2)}, u32[]{:S(2)}) collective-permute-start(bf16[256,256]{1,0:T(8,128)(2,1)S(1)} %collective-permute-done.11.refs_2_), channel_id=1, source_target_pairs={{8,9},{9,8},{10,11},{11,10},{12,13},{13,12},{14,15},{15,14},{16,17... | collective-permute-start | bytes 393224 | tf_op jit(solution)/shard_map/ppermute | solution.py:79
  63.2 0.0 collective-permute-done.19.refs_10_
  63.2 2.1 %collective-permute-start.16 = (bf16[256,256]{1,0:T(8,128)(2,1)S(1)}, bf16[256,256]{1,0:T(8,128)(2,1)S(1)}, u32[]{:S(2)}, u32[]{:S(2)}) collective-permute-start(bf16[256,256]{1,0:T(8,128)(2,1)S(1)} %collective-permute-done.12.refs_3_), channel_id=1, source_target_pairs={{8,9},{9,8},{10,11},{11,10},{12,13},{13,12},{14,15},{15,14},{16,17... | collective-permute-start | bytes 393224 | tf_op jit(solution)/shard_map/ppermute | solution.py:79
  65.3 0.0 collective-permute-done.13.refs_4_
  65.3 0.0 collective-permute-done.14.refs_5_
  65.3 0.0 collective-permute-done.15.refs_6_
  65.3 1.1 %collective-permute-done.16.refs_7_ = bf16[256,256]{1,0:T(8,128)(2,1)S(1)} collective-permute-done((bf16[256,256]{1,0:T(8,128)(2,1)S(1)}, bf16[256,256]{1,0:T(8,128)(2,1)S(1)}, u32[]{:S(2)}, u32[]{:S(2)}) %collective-permute-start.16) | collective-permute-done | bytes 131104 | tf_op jit(solution)/shard_map/ppermute | solution.py:79
  66.4 2.0 %shard_map.123 = (f32[256,256]{1,0:T(8,128)S(1)}, f32[256,256]{1,0:T(8,128)S(1)}) custom-call(f32[30]{0:T(128)S(1)} %copy-done.2, s32[4]{0:T(128)S(1)} %collective-permute-done.5.owner_in, f32[256,256]{1,0:T(8,128)S(1)} %get-tuple-element.47.after_ref.rest_ref, bf16[4,256,256]{2,1,0:T(8,128)(2,1)S(1)} %get-tuple-element.48.s_ref, ...), custom_call_target="tpu_custom_call" | custom-call | flops 1 | bytes 1 | tf_op jit(solution)/shard_map/pallas_call | solution.py:33
  68.4 0.0 collective-permute-done.20.c_ref
  68.4 1.9 %shard_map.124 = (bf16[2,256,256]{2,1,0:T(8,128)(2,1)}, bf16[2,512,256]{2,1,0:T(8,128)(2,1)}) custom-call(f32[30]{0:T(128)S(1)} %copy-done.2, bf16[4,512,256]{2,1,0:T(8,128)(2,1)S(1)} %copy-done, f32[256,256]{1,0:T(8,128)S(1)} %get-tuple-element.40.gain_ref, f32[256,256]{1,0:T(8,128)S(1)} %get-tuple-element.41.gain_extra_ref, ...), custom_call_target="tpu_custom_call" | custom-call | flops 1 | bytes 1 | tf_op jit(solution)/shard_map/pallas_call | solution.py:33
  (2 shorter events, 0.0 us)
Async XLA Ops:
  3.1 4.8 %collective-permute-start = (bf16[528,128]{1,0:T(8,128)(2,1)}, bf16[528,128]{1,0:T(8,128)(2,1)S(1)}, u32[]{:S(2)}, u32[]{:S(2)}) collective-permute-start(bf16[528,128]{1,0:T(8,128)(2,1)} %get-tuple-element.33), channel_id=1, source_target_pairs={{0,7},{1,2},{2,1},{3,4},{4,3},{5,6},{6,5},{7,0},{8,15},{9,10},{10,... | collective-permute-start | bytes 405512 | tf_op jit(solution)/shard_map/ppermute | solution.py:73
  5.0 11.7 %copy-start = (bf16[4,512,256]{2,1,0:T(8,128)(2,1)S(1)}, bf16[4,512,256]{2,1,0:T(8,128)(2,1)}, u32[]{:S(2)}) copy-start(bf16[4,512,256]{2,1,0:T(8,128)(2,1)} %coeff_ref.9) | copy-start | bytes 3145732
  5.0 11.8 %copy-start.1 = (bf16[4,256,256]{2,1,0:T(8,128)(2,1)S(1)}, bf16[4,256,256]{2,1,0:T(8,128)(2,1)}, u32[]{:S(2)}) copy-start(bf16[4,256,256]{2,1,0:T(8,128)(2,1)} %amps_ref.5) | copy-start | bytes 1572868
  5.0 6.0 %collective-permute-start.1 = (bf16[512,128]{1,0:T(8,128)(2,1)}, bf16[512,128]{1,0:T(8,128)(2,1)S(1)}, u32[]{:S(2)}, u32[]{:S(2)}) collective-permute-start(bf16[512,128]{1,0:T(8,128)(2,1)} %get-tuple-element.34), channel_id=1, source_target_pairs={{0,7},{1,2},{2,1},{3,4},{4,3},{5,6},{6,5},{7,0},{8,15},{9,10},{10,... | collective-permute-start | bytes 393224 | tf_op jit(solution)/shard_map/ppermute | solution.py:73
  10.0 14.1 %copy-start.2 = (f32[30]{0:T(128)S(1)}, f32[30]{0:T(128)}, u32[]{:S(2)}) copy-start(f32[30]{0:T(128)} %get-tuple-element.32.nums) | copy-start | bytes 364
  13.2 9.6 %collective-permute-start.4 = (bf16[2,1024,512]{2,1,0:T(8,128)(2,1)}, bf16[2,1024,512]{2,1,0:T(8,128)(2,1)S(1)}, u32[]{:S(2)}, u32[]{:S(2)}) collective-permute-start(bf16[2,1024,512]{2,1,0:T(8,128)(2,1)} %three_ref.5), channel_id=1, source_target_pairs={{0,1},{1,0},{2,3},{3,2},{4,5},{5,4},{6,7},{7,6},{8,9},{9,8},{10,11... | collective-permute-start | bytes 6291464 | tf_op jit(solution)/shard_map/ppermute | solution.py:70
  16.7 11.1 %collective-permute-start.2 = (bf16[4,512,256]{2,1,0:T(8,128)(2,1)S(1)}, bf16[4,512,256]{2,1,0:T(8,128)(2,1)S(1)}, u32[]{:S(2)}, u32[]{:S(2)}) collective-permute-start(bf16[4,512,256]{2,1,0:T(8,128)(2,1)S(1)} %copy-done), channel_id=1, source_target_pairs={{0,1},{1,0},{2,3},{3,2},{4,5},{5,4},{6,7},{7,6},{8,9},{9,8},{10,11... | collective-permute-start | bytes 3145736 | tf_op jit(solution)/shard_map/ppermute | solution.py:70
  16.8 10.5 %collective-permute-start.3 = (bf16[4,256,256]{2,1,0:T(8,128)(2,1)S(1)}, bf16[4,256,256]{2,1,0:T(8,128)(2,1)S(1)}, u32[]{:S(2)}, u32[]{:S(2)}) collective-permute-start(bf16[4,256,256]{2,1,0:T(8,128)(2,1)S(1)} %copy-done.1), channel_id=1, source_target_pairs={{0,1},{1,0},{2,3},{3,2},{4,5},{5,4},{6,7},{7,6},{8,9},{9,8},{10,11... | collective-permute-start | bytes 1572872 | tf_op jit(solution)/shard_map/ppermute | solution.py:70
  17.2 16.4 %collective-permute-start.6 = (bf16[1056,128]{1,0:T(8,128)(2,1)S(1)}, bf16[1056,128]{1,0:T(8,128)(2,1)S(1)}, u32[]{:S(2)}, u32[]{:S(2)}) collective-permute-start(bf16[1056,128]{1,0:T(8,128)(2,1)S(1)} %shard_map.114.after_ref), channel_id=1, source_target_pairs={{0,7},{1,2},{2,1},{3,4},{4,3},{5,6},{6,5},{7,0},{8,15},{9,10},{10,... | collective-permute-start | bytes 811016 | tf_op jit(solution)/shard_map/ppermute | solution.py:73
  17.2 16.4 %collective-permute-start.7 = (bf16[1040,128]{1,0:T(8,128)(2,1)S(1)}, bf16[1040,128]{1,0:T(8,128)(2,1)S(1)}, u32[]{:S(2)}, u32[]{:S(2)}) collective-permute-start(bf16[1040,128]{1,0:T(8,128)(2,1)S(1)} %shard_map.115.after_ref), channel_id=1, source_target_pairs={{0,7},{1,2},{2,1},{3,4},{4,3},{5,6},{6,5},{7,0},{8,15},{9,10},{10,... | collective-permute-start | bytes 798728 | tf_op jit(solution)/shard_map/ppermute | solution.py:73
  22.8 1.4 %copy-start.4 = (bf16[2,1024,512]{2,1,0:T(8,128)(2,1)}, bf16[2,1024,512]{2,1,0:T(8,128)(2,1)S(1)}, u32[]{:S(2)}) copy-start(bf16[2,1024,512]{2,1,0:T(8,128)(2,1)S(1)} %collective-permute-done.4.three_in_ref) | copy-start | bytes 6291460
  22.8 10.8 %collective-permute-start.8 = (bf16[256,256]{1,0:T(8,128)(2,1)S(1)}, bf16[256,256]{1,0:T(8,128)(2,1)S(1)}, u32[]{:S(2)}, u32[]{:S(2)}) collective-permute-start(bf16[256,256]{1,0:T(8,128)(2,1)S(1)} %get-tuple-element.38.after_ref), channel_id=1, source_target_pairs={{0,7},{1,2},{2,1},{3,4},{4,3},{5,6},{6,5},{7,0},{8,15},{9,10},{10,... | collective-permute-start | bytes 393224 | tf_op jit(solution)/shard_map/ppermute | solution.py:73
  24.1 3.7 %copy-start.3 = (f32[4,256]{1,0:T(4,128)S(1)}, f32[4,256]{1,0:T(4,128)}, u32[]{:S(2)}) copy-start(f32[4,256]{1,0:T(4,128)} %eps_ref.1) | copy-start | bytes 12292
  27.3 18.0 %collective-permute-start.9 = (bf16[512,256]{1,0:T(8,128)(2,1)S(1)}, bf16[512,256]{1,0:T(8,128)(2,1)S(1)}, u32[]{:S(2)}, u32[]{:S(2)}) collective-permute-start(bf16[512,256]{1,0:T(8,128)(2,1)S(1)} %get-tuple-element.50), channel_id=1, source_target_pairs={{0,7},{1,2},{2,1},{3,4},{4,3},{5,6},{6,5},{7,0},{8,15},{9,10},{10,... | collective-permute-start | bytes 786440 | tf_op jit(solution)/shard_map/ppermute | solution.py:73
  34.6 9.5 %collective-permute-start.10 = (bf16[256,256]{1,0:T(8,128)(2,1)S(1)}, bf16[256,256]{1,0:T(8,128)(2,1)S(1)}, u32[]{:S(2)}, u32[]{:S(2)}) collective-permute-start(bf16[256,256]{1,0:T(8,128)(2,1)S(1)} %get-tuple-element.55.amp_ref.refs_0_), channel_id=1, source_target_pairs={{0,8},{16,24},{24,16},{1,9},{17,25},{25,17},{2,10},{18,26},{26,18}... | collective-permute-start | bytes 393224 | tf_op jit(solution)/shard_map/ppermute | solution.py:82
  37.8 9.8 %collective-permute-start.11 = (bf16[256,256]{1,0:T(8,128)(2,1)S(1)}, bf16[256,256]{1,0:T(8,128)(2,1)S(1)}, u32[]{:S(2)}, u32[]{:S(2)}) collective-permute-start(bf16[256,256]{1,0:T(8,128)(2,1)S(1)} %get-tuple-element.55.amp_ref.refs_0_), channel_id=1, source_target_pairs={{0,16},{8,24},{24,8},{1,17},{9,25},{25,9},{2,18},{10,26},{26,10},{... | collective-permute-start | bytes 393224 | tf_op jit(solution)/shard_map/ppermute | solution.py:82
  39.1 8.5 %collective-permute-start.12 = (bf16[256,256]{1,0:T(8,128)(2,1)S(1)}, bf16[256,256]{1,0:T(8,128)(2,1)S(1)}, u32[]{:S(2)}, u32[]{:S(2)}) collective-permute-start(bf16[256,256]{1,0:T(8,128)(2,1)S(1)} %get-tuple-element.55.amp_ref.refs_0_), channel_id=1, source_target_pairs={{0,24},{8,16},{16,8},{1,25},{9,17},{17,9},{2,26},{10,18},{18,10},{... | collective-permute-start | bytes 393224 | tf_op jit(solution)/shard_map/ppermute | solution.py:82
  43.4 15.4 %collective-permute-start.17 = (bf16[256,256]{1,0:T(8,128)(2,1)S(1)}, bf16[256,256]{1,0:T(8,128)(2,1)S(1)}, u32[]{:S(2)}, u32[]{:S(2)}) collective-permute-start(bf16[256,256]{1,0:T(8,128)(2,1)S(1)} %get-tuple-element.59), channel_id=1, source_target_pairs={{0,8},{1,9},{2,10},{3,11},{4,12},{5,13},{6,14},{7,15}} | collective-permute-start | bytes 393224 | tf_op jit(solution)/shard_map/ppermute | solution.py:366
  44.1 16.9 %collective-permute-start.18 = (bf16[256,256]{1,0:T(8,128)(2,1)S(1)}, bf16[256,256]{1,0:T(8,128)(2,1)S(1)}, u32[]{:S(2)}, u32[]{:S(2)}) collective-permute-start(bf16[256,256]{1,0:T(8,128)(2,1)S(1)} %get-tuple-element.59), channel_id=1, source_target_pairs={{0,16},{1,17},{2,18},{3,19},{4,20},{5,21},{6,22},{7,23}} | collective-permute-start | bytes 393224 | tf_op jit(solution)/shard_map/ppermute | solution.py:366
  45.4 17.8 %collective-permute-start.19 = (bf16[256,256]{1,0:T(8,128)(2,1)S(1)}, bf16[256,256]{1,0:T(8,128)(2,1)S(1)}, u32[]{:S(2)}, u32[]{:S(2)}) collective-permute-start(bf16[256,256]{1,0:T(8,128)(2,1)S(1)} %get-tuple-element.59), channel_id=1, source_target_pairs={{0,24},{1,25},{2,26},{3,27},{4,28},{5,29},{6,30},{7,31}} | collective-permute-start | bytes 393224 | tf_op jit(solution)/shard_map/ppermute | solution.py:366
  46.1 5.2 %copy-start.5 = (s32[4]{0:T(128)S(1)}, s32[4]{0:T(128)}, u32[]{:S(2)}) copy-start(s32[4]{0:T(128)} %owner_hbm.1) | copy-start | bytes 52
  49.1 19.3 %collective-permute-start.20 = (bf16[2,256,256]{2,1,0:T(8,128)(2,1)S(1)}, bf16[2,256,256]{2,1,0:T(8,128)(2,1)S(1)}, u32[]{:S(2)}, u32[]{:S(2)}) collective-permute-start(bf16[2,256,256]{2,1,0:T(8,128)(2,1)S(1)} %shard_map.122), channel_id=1, source_target_pairs={{8,15},{9,10},{10,9},{11,12},{12,11},{13,14},{14,13},{15,8},{16,23... | collective-permute-start | bytes 786440 | tf_op jit(solution)/shard_map/ppermute | solution.py:79
  51.2 5.4 %collective-permute-start.5 = (s32[4]{0:T(128)S(1)}, s32[4]{0:T(128)S(1)}, u32[]{:S(2)}, u32[]{:S(2)}) collective-permute-start(s32[4]{0:T(128)S(1)} %copy-done.5), channel_id=1, source_target_pairs={{0,1},{1,0},{2,3},{3,2},{4,5},{5,4},{6,7},{7,6},{8,9},{9,8},{10,11... | collective-permute-start | bytes 56 | tf_op jit(solution)/shard_map/ppermute | solution.py:70
  56.6 8.7 %collective-permute-start.13 = (bf16[256,256]{1,0:T(8,128)(2,1)S(1)}, bf16[256,256]{1,0:T(8,128)(2,1)S(1)}, u32[]{:S(2)}, u32[]{:S(2)}) collective-permute-start(bf16[256,256]{1,0:T(8,128)(2,1)S(1)} %get-tuple-element.55.amp_ref.refs_0_), channel_id=1, source_target_pairs={{8,9},{9,8},{10,11},{11,10},{12,13},{13,12},{14,15},{15,14},{16,17... | collective-permute-start | bytes 393224 | tf_op jit(solution)/shard_map/ppermute | solution.py:79
  58.8 6.5 %collective-permute-start.14 = (bf16[256,256]{1,0:T(8,128)(2,1)S(1)}, bf16[256,256]{1,0:T(8,128)(2,1)S(1)}, u32[]{:S(2)}, u32[]{:S(2)}) collective-permute-start(bf16[256,256]{1,0:T(8,128)(2,1)S(1)} %collective-permute-done.10.refs_1_), channel_id=1, source_target_pairs={{8,9},{9,8},{10,11},{11,10},{12,13},{13,12},{14,15},{15,14},{16,17... | collective-permute-start | bytes 393224 | tf_op jit(solution)/shard_map/ppermute | solution.py:79
  61.0 4.4 %collective-permute-start.15 = (bf16[256,256]{1,0:T(8,128)(2,1)S(1)}, bf16[256,256]{1,0:T(8,128)(2,1)S(1)}, u32[]{:S(2)}, u32[]{:S(2)}) collective-permute-start(bf16[256,256]{1,0:T(8,128)(2,1)S(1)} %collective-permute-done.11.refs_2_), channel_id=1, source_target_pairs={{8,9},{9,8},{10,11},{11,10},{12,13},{13,12},{14,15},{15,14},{16,17... | collective-permute-start | bytes 393224 | tf_op jit(solution)/shard_map/ppermute | solution.py:79
  63.2 3.2 %collective-permute-start.16 = (bf16[256,256]{1,0:T(8,128)(2,1)S(1)}, bf16[256,256]{1,0:T(8,128)(2,1)S(1)}, u32[]{:S(2)}, u32[]{:S(2)}) collective-permute-start(bf16[256,256]{1,0:T(8,128)(2,1)S(1)} %collective-permute-done.12.refs_3_), channel_id=1, source_target_pairs={{8,9},{9,8},{10,11},{11,10},{12,13},{13,12},{14,15},{15,14},{16,17... | collective-permute-start | bytes 393224 | tf_op jit(solution)/shard_map/ppermute | solution.py:79

commit v5 on v4

--- a/solution.py
+++ b/solution.py
@@ -72,14 +72,10 @@
     def outer(x):
         return lax.ppermute(x, "pairs", list(enumerate(outer_of)))
 
-    def owners(x, other):
-        pairings = [
-            (s * columns + i, s * columns + j) for s in range(1, roles) for i, j in enumerate(other)
-        ]
-        return lax.ppermute(x, ("role", "pairs"), pairings)
-
     def swap(x, by):
-        return lax.ppermute(x, "role", [(i, i ^ by) for i in range(roles) if i ^ by])
+        return lax.ppermute(x, "role", [(i, i ^ by) for i in range(roles)])
+
+    three_in, coeff_in, amps_in = inner(three_index), inner(coeff), inner(amps)
 
     def pairs_of_roles(owner_ref):
         of_role = [jnp.int32(0)] * roles
@@ -217,37 +213,78 @@
             total = term if total is None else total + term
         return total
 
-    def half_into(y_ref, three_ref, at_occ, x):
+    block_scratch = [pltpu.VMEM((aux, pao), BF16), pltpu.SemaphoreType.DMA((aux // tile,))]
+
+    def by_tiles(three_ref, at_occ, block_ref, sems, product):
+        tiles = [pl.ds(at, tile) for at in range(0, aux, tile)]
+        copies = [
+            pltpu.make_async_copy(three_ref.at[at_occ, rows], block_ref.at[rows], sems.at[at])
+            for at, rows in enumerate(tiles)
+        ]
+        for copy in copies:
+            copy.start()
+        for copy, rows in zip(copies, tiles):
+            copy.wait()
+            product(rows, block_ref[rows, :])
+
+    def half_into(y_ref, x):
+        def product(rows, block):
+            y_ref[rows, :] = (mxu(block, x, NN) * pao_scale).astype(BF16)
+
+        return product
+
+    def own_first_body(nums, three_ref, coeff_ref, first_ref, extra_ref, x_ref, block_ref, sems, x_sems):
+        copies = [
+            pltpu.make_async_copy(coeff_ref.at[whole(nums[MINE])], x_ref, x_sems.at[0]),
+            pltpu.make_async_copy(coeff_ref.at[whole(nums[EXTRA])], extra_ref, x_sems.at[1]),
+        ]
+        for copy in copies:
+            copy.start()
+        copies[0].wait()
+        turned = x_ref[...].T
+
+        def product(rows, block):
+            first_ref[:, rows] = (mxu(turned, block, NT) * pao_scale).astype(BF16)
+
+        by_tiles(three_ref, whole(nums[FIRST]), block_ref, sems, product)
+        copies[1].wait()
+
+    first_t, x_extra = call(
+        own_first_body,
+        [SMEM, ANY, ANY],
+        [(VMEM, (virt, aux), BF16), (VMEM, (pao, virt), BF16)],
+        (nums, three_index, coeff),
+        scratch=[pltpu.VMEM((pao, virt), BF16), *block_scratch, pltpu.SemaphoreType.DMA((2,))],
+    )
+
+    def outer_low_body(three_ref, x_ref, after_ref, y_ref, block_ref, sems):
+        at_occ = whole(told_of(x_ref)[0, weights])
+        by_tiles(three_ref, at_occ, block_ref, sems, half_into(y_ref, x_ref[:pao, :]))
+        y_ref[aux:, :] = jnp.zeros((2 * riders, part), BF16)
+
+    y_low, block_out = call(
+        outer_low_body,
+        [ANY, VMEM, ANY],
+        [(VMEM, (aux + 2 * riders, part), BF16), (VMEM, (aux, pao), BF16)],
+        (three_index, low_out, first_t),
+        scratch=block_scratch[1:],
+    )
+    y_low_from_out = outer(y_low)
+
+    def outer_high_body(block_ref, x_ref, after_ref, y_ref):
+        product = half_into(y_ref, x_ref[...])
         for at in range(0, aux, tile):
             rows = pl.ds(at, tile)
-            y_ref[rows, :] = (mxu(three_ref[at_occ, rows, :], x, NN) * pao_scale).astype(BF16)
-
-    def outer_low_body(three_ref, x_ref, y_ref):
-        half_into(y_ref, three_ref, whole(told_of(x_ref)[0, weights]), x_ref[:pao, :])
-        y_ref[aux:, :] = jnp.zeros((2 * riders, part), BF16)
-
-    (y_low,) = call(
-        outer_low_body,
-        [VMEM, VMEM],
-        [(VMEM, (aux + 2 * riders, part), BF16)],
-        (three_index, low_out),
-    )
-    y_low_from_out = outer(y_low)
-
-    def outer_high_body(three_ref, low_ref, x_ref, after_ref, y_ref):
-        half_into(y_ref, three_ref, whole(told_of(low_ref)[0, weights]), x_ref[...])
+            product(rows, block_ref[rows, :])
         y_ref[aux:, :] = jnp.zeros((riders, part), BF16)
 
     (y_high,) = call(
         outer_high_body,
-        [VMEM, VMEM, VMEM, ANY],
+        [VMEM, VMEM, ANY],
         [(VMEM, (aux + riders, part), BF16)],
-        (three_index, low_out, high_out, y_low),
+        (block_out, high_out, y_low),
     )
     y_high_from_out = outer(y_high)
-
-    *sent, _ = lax.optimization_barrier((three_index, coeff, amps, pair_owner, y_high))
-    three_in, coeff_in, amps_in, owner_in = [inner(x) for x in sent]
 
     def outer_body(coeff_ref, amps_ref, low_ref, high_ref, after_ref, s_ref, c_ref, x_ref):
         x_ref[:, :part] = low_ref[:pao, :]
@@ -266,28 +303,22 @@
     )
     c_from_out = outer(c_out)
 
-    def own_half_body(
-        nums, three_ref, three_in_ref, coeff_ref, after_ref, first_ref, second_ref, extra_ref
-    ):
+    def own_second_body(nums, three_ref, three_in_ref, coeff_ref, after_ref, second_ref, block_ref, sems):
         x = coeff_ref[whole(nums[MINE])]
-        extra_ref[...] = coeff_ref[whole(nums[EXTRA])]
-        turned = x.T
-        first = whole(nums[FIRST])
-        for at in range(0, aux, tile):
-            rows = pl.ds(at, tile)
-            first_ref[:, rows] = (mxu(turned, three_ref[first, rows, :], NT) * pao_scale).astype(BF16)
         for whose, source in enumerate((three_ref, three_in_ref)):
 
             @pl.when(whole(nums[WHOSE]) == whose)
             def _():
-                half_into(second_ref, source, whole(nums[SECOND]), x)
-
-    first_t, second, x_extra = call(
-        own_half_body,
-        [SMEM, VMEM, VMEM, VMEM, ANY],
-        [(VMEM, (virt, aux), BF16), (VMEM, (aux, virt), BF16), (VMEM, (pao, virt), BF16)],
+                by_tiles(source, whole(nums[SECOND]), block_ref, sems, half_into(second_ref, x))
+
+    (second,) = call(
+        own_second_body,
+        [SMEM, ANY, ANY, VMEM, ANY],
+        [(VMEM, (aux, virt), BF16)],
         (nums, three_index, three_in, coeff, c_out),
-    )
+        scratch=block_scratch,
+    )
+    x_extra, _ = lax.optimization_barrier((x_extra, c_out))
     x_extra_out = outer(x_extra)
 
     def own_body(
@@ -321,7 +352,7 @@
         own_body,
         [SMEM] + [VMEM] * 5 + [ANY],
         [all_s, all_s, sq_f, sq_f, sq_f],
-        (nums, coeff, coeff_in, amps, amps_in, eps_virt, first_t),
+        (nums, coeff, coeff_in, amps, amps_in, eps_virt, c_out),
     )
 
     def first_body(
@@ -379,52 +410,47 @@
     )
 
     def outer_again_body(nums, low_ref, s_ref, se_ref, *refs):
-        amp_refs, c_ref = refs[:roles], refs[-1]
+        amp_refs, (c_ref, stack_ref) = refs[:roles], refs[-2:]
         role = lax.axis_index("role")
 
         @pl.when(role > 0)
         def _():
             told = told_of(low_ref)
+            pair_at = [whole(nums[ROLE_PAIR + (role ^ m)]) for m in range(roles)]
             for slot, of_s in enumerate((s_ref, se_ref)):
                 parts = []
                 for m in range(roles):
-                    at = whole(nums[ROLE_PAIR + (role ^ m)])
-                    weight = pick([told[:, slot * pairs + q : slot * pairs + q + 1] for q in range(pairs)], at)
-                    parts.append((at, weight, amp_refs[m][...]))
+                    choices = [told[:, slot * pairs + q : slot * pairs + q + 1] for q in range(pairs)]
+                    parts.append((pair_at[m], pick(choices, pair_at[m]), amp_refs[m][...]))
                 c_ref[slot] = coupled(of_s, parts).astype(BF16)
-
-    (cc_out,) = call(
+            for m in range(roles):
+                stack_ref[pair_at[m]] = amp_refs[m][...]
+
+    cc_out, stack = call(
         outer_again_body,
         [SMEM] + [VMEM] * (3 + roles),
-        [two_b],
+        [two_b, all_s],
         (nums, low_out, s_out, se_out, *amp_roles),
     )
-    cc_from_out = owners(cc_out, outer_of)
-
-    later = lax.optimization_barrier((*amp_roles, cc_out))[:roles]
-    amp_roles_in = [owners(x, inner_of) for x in later]
-
-    def own_again_body(nums, owner_in, rest_ref, s_ref, s_in_ref, se_ref, se_in_ref, *refs):
-        amp_refs, amp_in_refs, rest_refs = refs[:roles], refs[roles : 2 * roles], refs[2 * roles : -2]
-        out_ref, out_extra_ref = refs[-2:]
+    cc_from_out = outer(cc_out)
+    stack_in = inner(stack)
+
+    def own_again_body(
+        nums, rest_ref, s_ref, s_in_ref, se_ref, se_in_ref, stack_ref, stack_in_ref, *refs
+    ):
+        rest_refs, (out_ref, out_extra_ref) = refs[:-2], refs[-2:]
         role = lax.axis_index("role")
 
         @pl.when(role > 0)
         def _():
-            of_role = [whole(nums[ROLE_PAIR + s]) for s in range(roles)]
-            of_role_in = pairs_of_roles(owner_in)
             totals = []
             for slot, of_s, of_s_in in ((0, s_ref, s_in_ref), (1, se_ref, se_in_ref)):
                 total = None
-                for at_w, of, pair_of, amp_of in (
-                    (own_weights + 2 * slot * pairs, of_s, of_role, amp_refs),
-                    (own_weights + (2 * slot + 1) * pairs, of_s_in, of_role_in, amp_in_refs),
+                for at, of, amp_ref in (
+                    (own_weights + 2 * slot * pairs, of_s, stack_ref),
+                    (own_weights + (2 * slot + 1) * pairs, of_s_in, stack_in_ref),
                 ):
-                    parts = []
-                    for m in range(roles):
-                        at = pick(pair_of, role ^ m)
-                        parts.append((at, nums[at_w + at], amp_of[m][...]))
-                    c = coupled(of, parts)
+                    c = coupled(of, [(q, nums[at + q], amp_ref[q]) for q in range(pairs)])
                     total = c if total is None else total + c
                 totals.append(total)
             out_ref[...] = rest_ref[...] - totals[0]
@@ -435,9 +461,9 @@
 
     rest, rest_extra = call(
         own_again_body,
-        [SMEM] * 2 + [VMEM] * (5 + 3 * roles - 1),
+        [SMEM] + [VMEM] * (7 + roles - 1),
         [sq_f, sq_f],
-        (nums, owner_in, rest, s_own, s_in, se_own, se_in, *amp_roles, *amp_roles_in, *rests),
+        (nums, rest, s_own, s_in, se_own, se_in, stack, stack_in, *rests),
     )
 
     def last_body(

time: 70.8 us -> 58.5 us (0.83)
  the two profiles are of different devices: /device:TPU:5 before, /device:TPU:6 now
where the time goes in v5:
time: 58.5 us; the launch traced here: 58.1 us
  starting transfers between devices  18.6 us (32%)
  Pallas kernels  17.6 us (30%)
  waiting for transfers between devices  17.5 us (30%)
  local copies, waits for them, and re-layouts  3.47 us (6%)
  between operations  0.87 us (1%)
    pallas_call x13, Pallas kernels, call(): pl.pallas_call(body, in_specs=ins, out_specs=[spec for spec, _, _ in outs...  17.6 us
    ppermute x7, starting transfers between devices, outer(): return lax.ppermute(x, 'pairs', list(enumerate(outer_of)))  11.7 us
    ppermute x7, waiting for transfers between devices, outer(): return lax.ppermute(x, 'pairs', list(enumerate(outer_of)))  7.9 us
    ppermute x3, waiting for transfers between devices, local(): rests = [lax.ppermute(rest_b, 'role', [(0, s)]) for s in range(1, roles)]  7.21 us
    ppermute x3, starting transfers between devices, swap(): return lax.ppermute(x, 'role', [(i, i ^ by) for i in range(roles)])  3.55 us
    unnamed x16, local copies, waits for them, and re-layouts  3.47 us
    ppermute x3, starting transfers between devices, local(): rests = [lax.ppermute(rest_b, 'role', [(0, s)]) for s in range(1, roles)]  2.62 us
    ppermute x3, waiting for transfers between devices, swap(): return lax.ppermute(x, 'role', [(i, i ^ by) for i in range(roles)])  2.36 us
  transfers between devices with their start and end apart: 17, of which 4 were waited for; matrix products, arithmetic and copies ran while one was open for 0% of the time, Pallas kernels for 25%

profile of v5, /device:TPU:6, one launch (start us, length us, event | category | flops | bytes accessed | tf_op | source)
XLA Modules:
  0.0 58.1 jit_solution(15584916005146364160)
XLA Ops:
  0.6 0.1 collective-permute-start.4
  0.7 0.5 collective-permute-start
  1.2 0.1 collective-permute-start.1
  1.3 2.4 %shard_map.113 = (bf16[528,128]{1,0:T(8,128)(2,1)}, bf16[512,128]{1,0:T(8,128)(2,1)}, f32[30]{0:T(128)}) custom-call(s32[4]{0:T(128)} %owner_hbm.1, s32[2,4]{1,0:T(2,128)} %bitcast.1, s32[4,8]{1,0:T(4,128)} %partner_hbm.1, f32[4,8]{1,0:T(4,128)} %coupling_hbm.1, f32[16]{0:T(128)} %eps_hbm.1, s32[4]{0:T(128)} %nvirt_hbm.1, bf16[4,512,256]{2,1,0:T(8,128)(2,1)} %coeff_ref.11), custom_call_target="tpu_custom_call" | custom-call | flops 1 | bytes 1 | tf_op jit(solution)/shard_map/pallas_call | solution.py:33
  3.7 3.7 %collective-permute-start.2 = (bf16[528,128]{1,0:T(8,128)(2,1)}, bf16[528,128]{1,0:T(8,128)(2,1)S(1)}, u32[]{:S(2)}, u32[]{:S(2)}) collective-permute-start(bf16[528,128]{1,0:T(8,128)(2,1)} %get-tuple-element.29), channel_id=1, source_target_pairs={{0,7},{1,2},{2,1},{3,4},{4,3},{5,6},{6,5},{7,0},{8,15},{9,10},{10,... | collective-permute-start | bytes 405512 | tf_op jit(solution)/shard_map/ppermute | solution.py:73
  7.4 0.1 collective-permute-start.3
  7.5 0.0 copy-start
  7.5 1.2 %copy-done = bf16[4,512,256]{2,1,0:T(8,128)(2,1)S(1)} copy-done((bf16[4,512,256]{2,1,0:T(8,128)(2,1)S(1)}, bf16[4,512,256]{2,1,0:T(8,128)(2,1)}, u32[]{:S(2)}) %copy-start) | copy-done | bytes 1048600
  8.7 0.0 copy-start.2
  8.7 1.6 %copy-done.2 = bf16[2,1024,512]{2,1,0:T(8,128)(2,1)S(1)} copy-done((bf16[2,1024,512]{2,1,0:T(8,128)(2,1)S(1)}, bf16[2,1024,512]{2,1,0:T(8,128)(2,1)}, u32[]{:S(2)}) %copy-start.2) | copy-done | bytes 2097176
  10.3 0.0 copy-start.5
  10.3 0.6 %copy-done.5 = f32[30]{0:T(128)S(1)} copy-done((f32[30]{0:T(128)S(1)}, f32[30]{0:T(128)}, u32[]{:S(2)}) %copy-start.5) | copy-done | bytes 144
  11.0 0.0 copy-start.3
  11.0 2.1 %shard_map.114 = (bf16[256,1024]{1,0:T(8,128)(2,1)S(1)}, bf16[512,256]{1,0:T(8,128)(2,1)S(1)}) custom-call(f32[30]{0:T(128)S(1)} %copy-done.5, bf16[2,1024,512]{2,1,0:T(8,128)(2,1)S(1)} %copy-done.2, bf16[4,512,256]{2,1,0:T(8,128)(2,1)S(1)} %copy-done), custom_call_target="tpu_custom_call" | custom-call | flops 1 | bytes 1 | tf_op jit(solution)/shard_map/pallas_call | solution.py:33
  13.1 0.0 collective-permute-done.2.x_ref.low_ref
  13.1 0.0 copy-done.3
  13.1 0.0 copy-start.1
  13.1 0.0 copy-start.4
  13.1 1.1 %shard_map.115 = (bf16[1056,128]{1,0:T(8,128)(2,1)S(1)}, bf16[1024,512]{1,0:T(8,128)(2,1)S(1)}) custom-call(bf16[2,1024,512]{2,1,0:T(8,128)(2,1)S(1)} %copy-done.3, bf16[528,128]{1,0:T(8,128)(2,1)S(1)} %collective-permute-done.2.x_ref.low_ref, bf16[256,1024]{1,0:T(8,128)(2,1)S(1)} %get-tuple-element.31.after_ref.first_ref), custom_call_target="tpu_custom_call" | custom-call | flops 1 | bytes 1 | tf_op jit(solution)/shard_map/pallas_call | solution.py:33
  14.2 0.0 copy-start.6
  14.2 0.0 copy-start.7
  14.2 3.6 %collective-permute-start.5 = (bf16[1056,128]{1,0:T(8,128)(2,1)S(1)}, bf16[1056,128]{1,0:T(8,128)(2,1)S(1)}, u32[]{:S(2)}, u32[]{:S(2)}) collective-permute-start(bf16[1056,128]{1,0:T(8,128)(2,1)S(1)} %get-tuple-element.33.after_ref), channel_id=1, source_target_pairs={{0,7},{1,2},{2,1},{3,4},{4,3},{5,6},{6,5},{7,0},{8,15},{9,10},{10,... | collective-permute-start | bytes 811016 | tf_op jit(solution)/shard_map/ppermute | solution.py:73
  17.8 0.0 collective-permute-done.3.x_ref.high_ref
  17.8 0.4 shard_map.116.after_ref
  18.2 0.1 collective-permute-start.6
  18.3 0.0 copy-done.1
  18.3 0.0 copy-done.4
  18.3 0.9 %shard_map.117 = (bf16[4,256,256]{2,1,0:T(8,128)(2,1)S(1)}, bf16[256,256]{1,0:T(8,128)(2,1)S(1)}) custom-call(bf16[4,512,256]{2,1,0:T(8,128)(2,1)S(1)} %copy-done.1, bf16[4,256,256]{2,1,0:T(8,128)(2,1)S(1)} %copy-done.4, bf16[528,128]{1,0:T(8,128)(2,1)S(1)} %collective-permute-done.2.x_ref.low_ref, ...), custom_call_target="tpu_custom_call" | custom-call | flops 1 | bytes 1 | tf_op jit(solution)/shard_map/pallas_call | solution.py:33
  19.2 0.0 collective-permute-done.1.amps_in_ref
  19.3 3.6 %collective-permute-start.7 = (bf16[256,256]{1,0:T(8,128)(2,1)S(1)}, bf16[256,256]{1,0:T(8,128)(2,1)S(1)}, u32[]{:S(2)}, u32[]{:S(2)}) collective-permute-start(bf16[256,256]{1,0:T(8,128)(2,1)S(1)} %get-tuple-element.34.after_ref), channel_id=1, source_target_pairs={{0,7},{1,2},{2,1},{3,4},{4,3},{5,6},{6,5},{7,0},{8,15},{9,10},{10,... | collective-permute-start | bytes 393224 | tf_op jit(solution)/shard_map/ppermute | solution.py:73
  22.8 0.0 collective-permute-done.coeff_in_ref.in_ref
  22.8 0.1 collective-permute-start.8
  22.9 0.0 copy-done.6
  22.9 0.0 copy-done.7
  22.9 2.0 %shard_map.118 = (bf16[4,256,256]{2,1,0:T(8,128)(2,1)S(1)}, bf16[4,256,256]{2,1,0:T(8,128)(2,1)S(1)}, f32[256,256]{1,0:T(8,128)S(1)}, f32[256,256]{1,0:T(8,128)S(1)}, f32[256,256]{1,0:T(8,128)S(1)}) custom-call(f32[30]{0:T(128)S(1)} %copy-done.6, bf16[4,512,256]{2,1,0:T(8,128)(2,1)S(1)} %copy-done.1, ...), custom_call_target="tpu_custom_call" | custom-call | flops 1 | bytes 1 | tf_op jit(solution)/shard_map/pallas_call | solution.py:33
  24.9 0.0 collective-permute-done.4.three_in_ref
  24.9 0.6 %shard_map.119.second_ref = bf16[1024,256]{1,0:T(8,128)(2,1)S(1)} custom-call(f32[30]{0:T(128)S(1)} %copy-done.6, bf16[2,1024,512]{2,1,0:T(8,128)(2,1)S(1)} %copy-done.3, bf16[2,1024,512]{2,1,0:T(8,128)(2,1)S(1)} %collective-permute-done.4.three_in_ref, bf16[4,512,256]{2,1,0:T(8,128)(2,1)S(1)} %copy-done.1, bf16[256,256]{1,0:T(8,128)(2,1)S(1)} %get-tuple-element.34.after_ref), custom_call_target="tpu_custom_call" | custom-call | flops 1 | bytes 1 | tf_op jit(solution)/shard_map/pallas_call | solution.py:33
  25.5 7.9 %collective-permute-done.7.co_ref = bf16[256,256]{1,0:T(8,128)(2,1)S(1)} collective-permute-done((bf16[256,256]{1,0:T(8,128)(2,1)S(1)}, bf16[256,256]{1,0:T(8,128)(2,1)S(1)}, u32[]{:S(2)}, u32[]{:S(2)}) %collective-permute-start.7) | collective-permute-done | bytes 131104 | tf_op jit(solution)/shard_map/ppermute | solution.py:73
  33.4 0.0 collective-permute-done.6.high_ref
  33.4 0.0 collective-permute-done.5.low_ref
  33.4 1.1 %shard_map.120 = (bf16[256,256]{1,0:T(8,128)(2,1)S(1)}, f32[256,256]{1,0:T(8,128)S(1)}) custom-call(f32[30]{0:T(128)S(1)} %copy-done.6, bf16[256,1024]{1,0:T(8,128)(2,1)S(1)} %get-tuple-element.31.after_ref.first_ref, bf16[1024,256]{1,0:T(8,128)(2,1)S(1)} %shard_map.119.second_ref, bf16[1056,128]{1,0:T(8,128)(2,1)S(1)} %collective-permute-done.5.low_ref, ...), custom_call_target="tpu_custom_call" | custom-call | flops 1 | bytes 1 | tf_op jit(solution)/shard_map/pallas_call | solution.py:33
  34.5 0.5 collective-permute-start.10
  35.0 1.5 %collective-permute-start.11 = (bf16[256,256]{1,0:T(8,128)(2,1)S(1)}, bf16[256,256]{1,0:T(8,128)(2,1)S(1)}, u32[]{:S(2)}, u32[]{:S(2)}) collective-permute-start(bf16[256,256]{1,0:T(8,128)(2,1)S(1)} %get-tuple-element.38.amp_ref.refs_0_), channel_id=1, source_target_pairs={{0,24},{8,16},{16,8},{24,0},{1,25},{9,17},{17,9},{25,1},{2,26},{10... | collective-permute-start | bytes 393224 | tf_op jit(solution)/shard_map/ppermute | solution.py:76
  36.5 1.6 %collective-permute-start.9 = (bf16[256,256]{1,0:T(8,128)(2,1)S(1)}, bf16[256,256]{1,0:T(8,128)(2,1)S(1)}, u32[]{:S(2)}, u32[]{:S(2)}) collective-permute-start(bf16[256,256]{1,0:T(8,128)(2,1)S(1)} %get-tuple-element.38.amp_ref.refs_0_), channel_id=1, source_target_pairs={{0,8},{8,0},{16,24},{24,16},{1,9},{9,1},{17,25},{25,17},{2,10},{10... | collective-permute-start | bytes 393224 | tf_op jit(solution)/shard_map/ppermute | solution.py:76
  38.0 0.4 shard_map.121
  38.5 0.0 collective-permute-done.8.out_ref
  38.5 1.6 %shard_map.122 = (bf16[4,256,256]{2,1,0:T(8,128)(2,1)S(1)}, bf16[4,256,256]{2,1,0:T(8,128)(2,1)S(1)}, bf16[4,256,256]{2,1,0:T(8,128)(2,1)S(1)}) custom-call(f32[30]{0:T(128)S(1)} %copy-done.6, bf16[4,512,256]{2,1,0:T(8,128)(2,1)S(1)} %copy-done.1, bf16[4,512,256]{2,1,0:T(8,128)(2,1)S(1)} %collective-permute-done.coeff_in_ref.in_ref, ...), custom_call_target="tpu_custom_call" | custom-call | flops 1 | bytes 1 | tf_op jit(solution)/shard_map/pallas_call | solution.py:33
  40.0 0.0 collective-permute-done.10.refs_2_
  40.0 0.9 %collective-permute-done.11.refs_3_ = bf16[256,256]{1,0:T(8,128)(2,1)S(1)} collective-permute-done((bf16[256,256]{1,0:T(8,128)(2,1)S(1)}, bf16[256,256]{1,0:T(8,128)(2,1)S(1)}, u32[]{:S(2)}, u32[]{:S(2)}) %collective-permute-start.11) | collective-permute-done | bytes 131104 | tf_op jit(solution)/shard_map/ppermute | solution.py:76
  40.9 1.5 %collective-permute-done.9.refs_1_ = bf16[256,256]{1,0:T(8,128)(2,1)S(1)} collective-permute-done((bf16[256,256]{1,0:T(8,128)(2,1)S(1)}, bf16[256,256]{1,0:T(8,128)(2,1)S(1)}, u32[]{:S(2)}, u32[]{:S(2)}) %collective-permute-start.9) | collective-permute-done | bytes 131104 | tf_op jit(solution)/shard_map/ppermute | solution.py:76
  42.4 1.4 %shard_map.123 = (bf16[2,256,256]{2,1,0:T(8,128)(2,1)S(1)}, bf16[4,256,256]{2,1,0:T(8,128)(2,1)S(1)}) custom-call(f32[30]{0:T(128)S(1)} %copy-done.6, bf16[528,128]{1,0:T(8,128)(2,1)S(1)} %collective-permute-done.2.x_ref.low_ref, bf16[4,256,256]{2,1,0:T(8,128)(2,1)S(1)} %get-tuple-element.47.s_ref, bf16[4,256,256]{2,1,0:T(8,128)(2,1)S(1)} %get-tuple-element.48.se_ref, ...), custom_call_target="tpu_custom_call" | custom-call | flops 1 | bytes 1 | tf_op jit(solution)/shard_map/pallas_call | solution.py:33
  43.8 0.1 collective-permute-start.12
  43.9 0.6 %collective-permute-start.16 = (bf16[2,256,256]{2,1,0:T(8,128)(2,1)S(1)}, bf16[2,256,256]{2,1,0:T(8,128)(2,1)S(1)}, u32[]{:S(2)}, u32[]{:S(2)}) collective-permute-start(bf16[2,256,256]{2,1,0:T(8,128)(2,1)S(1)} %get-tuple-element.53), channel_id=1, source_target_pairs={{0,7},{1,2},{2,1},{3,4},{4,3},{5,6},{6,5},{7,0},{8,15},{9,10},{10,... | collective-permute-start | bytes 786440 | tf_op jit(solution)/shard_map/ppermute | solution.py:73
  44.5 0.7 %collective-permute-start.13 = (bf16[256,256]{1,0:T(8,128)(2,1)S(1)}, bf16[256,256]{1,0:T(8,128)(2,1)S(1)}, u32[]{:S(2)}, u32[]{:S(2)}) collective-permute-start(bf16[256,256]{1,0:T(8,128)(2,1)S(1)} %get-tuple-element.50), channel_id=1, source_target_pairs={{0,8},{1,9},{2,10},{3,11},{4,12},{5,13},{6,14},{7,15}} | collective-permute-start | bytes 393224 | tf_op jit(solution)/shard_map/ppermute | solution.py:397
  45.1 0.7 %collective-permute-start.14 = (bf16[256,256]{1,0:T(8,128)(2,1)S(1)}, bf16[256,256]{1,0:T(8,128)(2,1)S(1)}, u32[]{:S(2)}, u32[]{:S(2)}) collective-permute-start(bf16[256,256]{1,0:T(8,128)(2,1)S(1)} %get-tuple-element.50), channel_id=1, source_target_pairs={{0,16},{1,17},{2,18},{3,19},{4,20},{5,21},{6,22},{7,23}} | collective-permute-start | bytes 393224 | tf_op jit(solution)/shard_map/ppermute | solution.py:397
  45.8 1.3 %collective-permute-start.15 = (bf16[256,256]{1,0:T(8,128)(2,1)S(1)}, bf16[256,256]{1,0:T(8,128)(2,1)S(1)}, u32[]{:S(2)}, u32[]{:S(2)}) collective-permute-start(bf16[256,256]{1,0:T(8,128)(2,1)S(1)} %get-tuple-element.50), channel_id=1, source_target_pairs={{0,24},{1,25},{2,26},{3,27},{4,28},{5,29},{6,30},{7,31}} | collective-permute-start | bytes 393224 | tf_op jit(solution)/shard_map/ppermute | solution.py:397
  47.1 0.0 collective-permute-done.13.refs_0_
  47.1 0.0 collective-permute-done.14.refs_1_
  47.1 7.2 %collective-permute-done.15.refs_2_ = bf16[256,256]{1,0:T(8,128)(2,1)S(1)} collective-permute-done((bf16[256,256]{1,0:T(8,128)(2,1)S(1)}, bf16[256,256]{1,0:T(8,128)(2,1)S(1)}, u32[]{:S(2)}, u32[]{:S(2)}) %collective-permute-start.15) | collective-permute-done | bytes 131104 | tf_op jit(solution)/shard_map/ppermute | solution.py:397
  54.4 0.0 collective-permute-done.12.stack_in_ref
  54.4 2.0 %shard_map.124 = (f32[256,256]{1,0:T(8,128)S(1)}, f32[256,256]{1,0:T(8,128)S(1)}) custom-call(f32[30]{0:T(128)S(1)} %copy-done.6, f32[256,256]{1,0:T(8,128)S(1)} %get-tuple-element.40.after_ref.rest_ref, bf16[4,256,256]{2,1,0:T(8,128)(2,1)S(1)} %get-tuple-element.41.s_ref, bf16[4,256,256]{2,1,0:T(8,128)(2,1)S(1)} %get-tuple-element.42.s_in_ref, ...), custom_call_target="tpu_custom_call" | custom-call | flops 1 | bytes 1 | tf_op jit(solution)/shard_map/pallas_call | solution.py:33
  56.3 0.0 collective-permute-done.16.c_ref
  56.3 1.7 %shard_map.125 = (bf16[2,256,256]{2,1,0:T(8,128)(2,1)}, bf16[2,512,256]{2,1,0:T(8,128)(2,1)}) custom-call(f32[30]{0:T(128)S(1)} %copy-done.6, bf16[4,512,256]{2,1,0:T(8,128)(2,1)S(1)} %copy-done.1, f32[256,256]{1,0:T(8,128)S(1)} %get-tuple-element.35.gain_ref, f32[256,256]{1,0:T(8,128)S(1)} %get-tuple-element.36.gain_extra_ref, ...), custom_call_target="tpu_custom_call" | custom-call | flops 1 | bytes 1 | tf_op jit(solution)/shard_map/pallas_call | solution.py:33
Async XLA Ops:
  0.6 24.3 %collective-permute-start.4 = (bf16[2,1024,512]{2,1,0:T(8,128)(2,1)}, bf16[2,1024,512]{2,1,0:T(8,128)(2,1)S(1)}, u32[]{:S(2)}, u32[]{:S(2)}) collective-permute-start(bf16[2,1024,512]{2,1,0:T(8,128)(2,1)} %three_ref.5), channel_id=1, source_target_pairs={{0,1},{1,0},{2,3},{3,2},{4,5},{5,4},{6,7},{7,6},{8,9},{9,8},{10,11... | collective-permute-start | bytes 6291464 | tf_op jit(solution)/shard_map/ppermute | solution.py:70
  0.7 22.1 %collective-permute-start = (bf16[4,512,256]{2,1,0:T(8,128)(2,1)}, bf16[4,512,256]{2,1,0:T(8,128)(2,1)S(1)}, u32[]{:S(2)}, u32[]{:S(2)}) collective-permute-start(bf16[4,512,256]{2,1,0:T(8,128)(2,1)} %coeff_ref.11), channel_id=1, source_target_pairs={{0,1},{1,0},{2,3},{3,2},{4,5},{5,4},{6,7},{7,6},{8,9},{9,8},{10,11... | collective-permute-start | bytes 3145736 | tf_op jit(solution)/shard_map/ppermute | solution.py:70
  1.2 18.0 %collective-permute-start.1 = (bf16[4,256,256]{2,1,0:T(8,128)(2,1)}, bf16[4,256,256]{2,1,0:T(8,128)(2,1)S(1)}, u32[]{:S(2)}, u32[]{:S(2)}) collective-permute-start(bf16[4,256,256]{2,1,0:T(8,128)(2,1)} %amps_ref.5), channel_id=1, source_target_pairs={{0,1},{1,0},{2,3},{3,2},{4,5},{5,4},{6,7},{7,6},{8,9},{9,8},{10,11... | collective-permute-start | bytes 1572872 | tf_op jit(solution)/shard_map/ppermute | solution.py:70
  3.7 9.4 %collective-permute-start.2 = (bf16[528,128]{1,0:T(8,128)(2,1)}, bf16[528,128]{1,0:T(8,128)(2,1)S(1)}, u32[]{:S(2)}, u32[]{:S(2)}) collective-permute-start(bf16[528,128]{1,0:T(8,128)(2,1)} %get-tuple-element.29), channel_id=1, source_target_pairs={{0,7},{1,2},{2,1},{3,4},{4,3},{5,6},{6,5},{7,0},{8,15},{9,10},{10,... | collective-permute-start | bytes 405512 | tf_op jit(solution)/shard_map/ppermute | solution.py:73
  7.4 10.4 %collective-permute-start.3 = (bf16[512,128]{1,0:T(8,128)(2,1)}, bf16[512,128]{1,0:T(8,128)(2,1)S(1)}, u32[]{:S(2)}, u32[]{:S(2)}) collective-permute-start(bf16[512,128]{1,0:T(8,128)(2,1)} %get-tuple-element.30), channel_id=1, source_target_pairs={{0,7},{1,2},{2,1},{3,4},{4,3},{5,6},{6,5},{7,0},{8,15},{9,10},{10,... | collective-permute-start | bytes 393224 | tf_op jit(solution)/shard_map/ppermute | solution.py:73
  7.5 1.2 %copy-start = (bf16[4,512,256]{2,1,0:T(8,128)(2,1)S(1)}, bf16[4,512,256]{2,1,0:T(8,128)(2,1)}, u32[]{:S(2)}) copy-start(bf16[4,512,256]{2,1,0:T(8,128)(2,1)} %coeff_ref.11) | copy-start | bytes 3145732
  8.7 1.6 %copy-start.2 = (bf16[2,1024,512]{2,1,0:T(8,128)(2,1)S(1)}, bf16[2,1024,512]{2,1,0:T(8,128)(2,1)}, u32[]{:S(2)}) copy-start(bf16[2,1024,512]{2,1,0:T(8,128)(2,1)} %three_ref.5) | copy-start | bytes 6291460
  10.3 0.6 %copy-start.5 = (f32[30]{0:T(128)S(1)}, f32[30]{0:T(128)}, u32[]{:S(2)}) copy-start(f32[30]{0:T(128)} %get-tuple-element.28.nums) | copy-start | bytes 364
  11.0 2.1 %copy-start.3 = (bf16[2,1024,512]{2,1,0:T(8,128)(2,1)S(1)}, bf16[2,1024,512]{2,1,0:T(8,128)(2,1)}, u32[]{:S(2)}) copy-start(bf16[2,1024,512]{2,1,0:T(8,128)(2,1)} %three_ref.5) | copy-start | bytes 6291460
  13.1 5.2 %copy-start.1 = (bf16[4,512,256]{2,1,0:T(8,128)(2,1)S(1)}, bf16[4,512,256]{2,1,0:T(8,128)(2,1)}, u32[]{:S(2)}) copy-start(bf16[4,512,256]{2,1,0:T(8,128)(2,1)} %coeff_ref.11) | copy-start | bytes 3145732
  13.1 5.2 %copy-start.4 = (bf16[4,256,256]{2,1,0:T(8,128)(2,1)S(1)}, bf16[4,256,256]{2,1,0:T(8,128)(2,1)}, u32[]{:S(2)}) copy-start(bf16[4,256,256]{2,1,0:T(8,128)(2,1)} %amps_ref.5) | copy-start | bytes 1572868
  14.2 8.7 %copy-start.6 = (f32[30]{0:T(128)S(1)}, f32[30]{0:T(128)}, u32[]{:S(2)}) copy-start(f32[30]{0:T(128)} %get-tuple-element.28.nums) | copy-start | bytes 364
  14.2 8.7 %copy-start.7 = (f32[4,256]{1,0:T(4,128)S(1)}, f32[4,256]{1,0:T(4,128)}, u32[]{:S(2)}) copy-start(f32[4,256]{1,0:T(4,128)} %eps_ref.1) | copy-start | bytes 12292
  14.2 19.2 %collective-permute-start.5 = (bf16[1056,128]{1,0:T(8,128)(2,1)S(1)}, bf16[1056,128]{1,0:T(8,128)(2,1)S(1)}, u32[]{:S(2)}, u32[]{:S(2)}) collective-permute-start(bf16[1056,128]{1,0:T(8,128)(2,1)S(1)} %get-tuple-element.33.after_ref), channel_id=1, source_target_pairs={{0,7},{1,2},{2,1},{3,4},{4,3},{5,6},{6,5},{7,0},{8,15},{9,10},{10,... | collective-permute-start | bytes 811016 | tf_op jit(solution)/shard_map/ppermute | solution.py:73
  18.2 15.2 %collective-permute-start.6 = (bf16[1040,128]{1,0:T(8,128)(2,1)S(1)}, bf16[1040,128]{1,0:T(8,128)(2,1)S(1)}, u32[]{:S(2)}, u32[]{:S(2)}) collective-permute-start(bf16[1040,128]{1,0:T(8,128)(2,1)S(1)} %shard_map.116.after_ref), channel_id=1, source_target_pairs={{0,7},{1,2},{2,1},{3,4},{4,3},{5,6},{6,5},{7,0},{8,15},{9,10},{10,... | collective-permute-start | bytes 798728 | tf_op jit(solution)/shard_map/ppermute | solution.py:73
  19.3 14.1 %collective-permute-start.7 = (bf16[256,256]{1,0:T(8,128)(2,1)S(1)}, bf16[256,256]{1,0:T(8,128)(2,1)S(1)}, u32[]{:S(2)}, u32[]{:S(2)}) collective-permute-start(bf16[256,256]{1,0:T(8,128)(2,1)S(1)} %get-tuple-element.34.after_ref), channel_id=1, source_target_pairs={{0,7},{1,2},{2,1},{3,4},{4,3},{5,6},{6,5},{7,0},{8,15},{9,10},{10,... | collective-permute-start | bytes 393224 | tf_op jit(solution)/shard_map/ppermute | solution.py:73
  22.8 15.6 %collective-permute-start.8 = (bf16[512,256]{1,0:T(8,128)(2,1)S(1)}, bf16[512,256]{1,0:T(8,128)(2,1)S(1)}, u32[]{:S(2)}, u32[]{:S(2)}) collective-permute-start(bf16[512,256]{1,0:T(8,128)(2,1)S(1)} %get-tuple-element.44), channel_id=1, source_target_pairs={{0,7},{1,2},{2,1},{3,4},{4,3},{5,6},{6,5},{7,0},{8,15},{9,10},{10,... | collective-permute-start | bytes 786440 | tf_op jit(solution)/shard_map/ppermute | solution.py:73
  34.5 5.5 %collective-permute-start.10 = (bf16[256,256]{1,0:T(8,128)(2,1)S(1)}, bf16[256,256]{1,0:T(8,128)(2,1)S(1)}, u32[]{:S(2)}, u32[]{:S(2)}) collective-permute-start(bf16[256,256]{1,0:T(8,128)(2,1)S(1)} %get-tuple-element.38.amp_ref.refs_0_), channel_id=1, source_target_pairs={{0,16},{8,24},{16,0},{24,8},{1,17},{9,25},{17,1},{25,9},{2,18},{10... | collective-permute-start | bytes 393224 | tf_op jit(solution)/shard_map/ppermute | solution.py:76
  35.0 5.9 %collective-permute-start.11 = (bf16[256,256]{1,0:T(8,128)(2,1)S(1)}, bf16[256,256]{1,0:T(8,128)(2,1)S(1)}, u32[]{:S(2)}, u32[]{:S(2)}) collective-permute-start(bf16[256,256]{1,0:T(8,128)(2,1)S(1)} %get-tuple-element.38.amp_ref.refs_0_), channel_id=1, source_target_pairs={{0,24},{8,16},{16,8},{24,0},{1,25},{9,17},{17,9},{25,1},{2,26},{10... | collective-permute-start | bytes 393224 | tf_op jit(solution)/shard_map/ppermute | solution.py:76
  36.5 5.9 %collective-permute-start.9 = (bf16[256,256]{1,0:T(8,128)(2,1)S(1)}, bf16[256,256]{1,0:T(8,128)(2,1)S(1)}, u32[]{:S(2)}, u32[]{:S(2)}) collective-permute-start(bf16[256,256]{1,0:T(8,128)(2,1)S(1)} %get-tuple-element.38.amp_ref.refs_0_), channel_id=1, source_target_pairs={{0,8},{8,0},{16,24},{24,16},{1,9},{9,1},{17,25},{25,17},{2,10},{10... | collective-permute-start | bytes 393224 | tf_op jit(solution)/shard_map/ppermute | solution.py:76
  43.8 10.6 %collective-permute-start.12 = (bf16[4,256,256]{2,1,0:T(8,128)(2,1)S(1)}, bf16[4,256,256]{2,1,0:T(8,128)(2,1)S(1)}, u32[]{:S(2)}, u32[]{:S(2)}) collective-permute-start(bf16[4,256,256]{2,1,0:T(8,128)(2,1)S(1)} %get-tuple-element.49.stack_ref), channel_id=1, source_target_pairs={{0,1},{1,0},{2,3},{3,2},{4,5},{5,4},{6,7},{7,6},{8,9},{9,8},{10,11... | collective-permute-start | bytes 1572872 | tf_op jit(solution)/shard_map/ppermute | solution.py:70
  43.9 12.5 %collective-permute-start.16 = (bf16[2,256,256]{2,1,0:T(8,128)(2,1)S(1)}, bf16[2,256,256]{2,1,0:T(8,128)(2,1)S(1)}, u32[]{:S(2)}, u32[]{:S(2)}) collective-permute-start(bf16[2,256,256]{2,1,0:T(8,128)(2,1)S(1)} %get-tuple-element.53), channel_id=1, source_target_pairs={{0,7},{1,2},{2,1},{3,4},{4,3},{5,6},{6,5},{7,0},{8,15},{9,10},{10,... | collective-permute-start | bytes 786440 | tf_op jit(solution)/shard_map/ppermute | solution.py:73
  44.5 2.6 %collective-permute-start.13 = (bf16[256,256]{1,0:T(8,128)(2,1)S(1)}, bf16[256,256]{1,0:T(8,128)(2,1)S(1)}, u32[]{:S(2)}, u32[]{:S(2)}) collective-permute-start(bf16[256,256]{1,0:T(8,128)(2,1)S(1)} %get-tuple-element.50), channel_id=1, source_target_pairs={{0,8},{1,9},{2,10},{3,11},{4,12},{5,13},{6,14},{7,15}} | collective-permute-start | bytes 393224 | tf_op jit(solution)/shard_map/ppermute | solution.py:397
  45.1 2.0 %collective-permute-start.14 = (bf16[256,256]{1,0:T(8,128)(2,1)S(1)}, bf16[256,256]{1,0:T(8,128)(2,1)S(1)}, u32[]{:S(2)}, u32[]{:S(2)}) collective-permute-start(bf16[256,256]{1,0:T(8,128)(2,1)S(1)} %get-tuple-element.50), channel_id=1, source_target_pairs={{0,16},{1,17},{2,18},{3,19},{4,20},{5,21},{6,22},{7,23}} | collective-permute-start | bytes 393224 | tf_op jit(solution)/shard_map/ppermute | solution.py:397
  45.8 8.5 %collective-permute-start.15 = (bf16[256,256]{1,0:T(8,128)(2,1)S(1)}, bf16[256,256]{1,0:T(8,128)(2,1)S(1)}, u32[]{:S(2)}, u32[]{:S(2)}) collective-permute-start(bf16[256,256]{1,0:T(8,128)(2,1)S(1)} %get-tuple-element.50), channel_id=1, source_target_pairs={{0,24},{1,25},{2,26},{3,27},{4,28},{5,29},{6,30},{7,31}} | collective-permute-start | bytes 393224 | tf_op jit(solution)/shard_map/ppermute | solution.py:397

commit v6 on v5

--- a/solution.py
+++ b/solution.py
@@ -50,7 +50,7 @@
     pairs, _, virt = coeff.shape
     partner_count = partners.shape[1]
     slots = 2
-    assert roles == pairs and columns % 2 == 0 and virt % 2 == 0
+    assert roles == pairs and pairs % 2 == 0 and columns % 2 == 0 and virt % 2 == 0
     tile = min(256, aux)
     pao_scale = 1.0 / math.sqrt(pao)
     aux_scale = 1.0 / math.sqrt(aux)
@@ -96,6 +96,7 @@
 
     weights = 2 * pairs
     riders = 16
+    longer = (VMEM, (virt + riders, virt), BF16)
     own_weights = ROLE_PAIR + roles
 
     def plan_body(
@@ -233,56 +234,33 @@
 
         return product
 
-    def own_first_body(nums, three_ref, coeff_ref, first_ref, extra_ref, x_ref, block_ref, sems, x_sems):
-        copies = [
-            pltpu.make_async_copy(coeff_ref.at[whole(nums[MINE])], x_ref, x_sems.at[0]),
-            pltpu.make_async_copy(coeff_ref.at[whole(nums[EXTRA])], extra_ref, x_sems.at[1]),
-        ]
-        for copy in copies:
-            copy.start()
-        copies[0].wait()
-        turned = x_ref[...].T
-
-        def product(rows, block):
-            first_ref[:, rows] = (mxu(turned, block, NT) * pao_scale).astype(BF16)
-
-        by_tiles(three_ref, whole(nums[FIRST]), block_ref, sems, product)
-        copies[1].wait()
-
-    first_t, x_extra = call(
-        own_first_body,
-        [SMEM, ANY, ANY],
-        [(VMEM, (virt, aux), BF16), (VMEM, (pao, virt), BF16)],
-        (nums, three_index, coeff),
-        scratch=[pltpu.VMEM((pao, virt), BF16), *block_scratch, pltpu.SemaphoreType.DMA((2,))],
-    )
-
-    def outer_low_body(three_ref, x_ref, after_ref, y_ref, block_ref, sems):
+    def outer_low_body(three_ref, x_ref, y_ref, block_ref, sems):
         at_occ = whole(told_of(x_ref)[0, weights])
         by_tiles(three_ref, at_occ, block_ref, sems, half_into(y_ref, x_ref[:pao, :]))
         y_ref[aux:, :] = jnp.zeros((2 * riders, part), BF16)
 
-    y_low, block_out = call(
+    (y_low,) = call(
         outer_low_body,
-        [ANY, VMEM, ANY],
-        [(VMEM, (aux + 2 * riders, part), BF16), (VMEM, (aux, pao), BF16)],
-        (three_index, low_out, first_t),
-        scratch=block_scratch[1:],
+        [ANY, VMEM],
+        [(VMEM, (aux + 2 * riders, part), BF16)],
+        (three_index, low_out),
+        scratch=block_scratch,
+        vmem=52,
     )
     y_low_from_out = outer(y_low)
 
-    def outer_high_body(block_ref, x_ref, after_ref, y_ref):
-        product = half_into(y_ref, x_ref[...])
-        for at in range(0, aux, tile):
-            rows = pl.ds(at, tile)
-            product(rows, block_ref[rows, :])
+    def outer_high_body(three_ref, low_ref, x_ref, after_ref, y_ref, block_ref, sems):
+        at_occ = whole(told_of(low_ref)[0, weights])
+        by_tiles(three_ref, at_occ, block_ref, sems, half_into(y_ref, x_ref[...]))
         y_ref[aux:, :] = jnp.zeros((riders, part), BF16)
 
     (y_high,) = call(
         outer_high_body,
-        [VMEM, VMEM, ANY],
+        [ANY, VMEM, VMEM, ANY],
         [(VMEM, (aux + riders, part), BF16)],
-        (block_out, high_out, y_low),
+        (three_index, low_out, high_out, y_low),
+        scratch=block_scratch,
+        vmem=52,
     )
     y_high_from_out = outer(y_high)
 
@@ -303,22 +281,30 @@
     )
     c_from_out = outer(c_out)
 
-    def own_second_body(nums, three_ref, three_in_ref, coeff_ref, after_ref, second_ref, block_ref, sems):
+    def own_half_body(
+        nums, three_ref, three_in_ref, coeff_ref, after_ref, first_ref, second_ref, extra_ref, block_ref, sems
+    ):
         x = coeff_ref[whole(nums[MINE])]
+        extra_ref[...] = coeff_ref[whole(nums[EXTRA])]
+        turned = x.T
+
+        def product(rows, block):
+            first_ref[:, rows] = (mxu(turned, block, NT) * pao_scale).astype(BF16)
+
+        by_tiles(three_ref, whole(nums[FIRST]), block_ref, sems, product)
         for whose, source in enumerate((three_ref, three_in_ref)):
 
             @pl.when(whole(nums[WHOSE]) == whose)
             def _():
                 by_tiles(source, whole(nums[SECOND]), block_ref, sems, half_into(second_ref, x))
 
-    (second,) = call(
-        own_second_body,
+    first_t, second, x_extra = call(
+        own_half_body,
         [SMEM, ANY, ANY, VMEM, ANY],
-        [(VMEM, (aux, virt), BF16)],
+        [(VMEM, (virt, aux), BF16), (VMEM, (aux, virt), BF16), (VMEM, (pao, virt), BF16)],
         (nums, three_index, three_in, coeff, c_out),
         scratch=block_scratch,
     )
-    x_extra, _ = lax.optimization_barrier((x_extra, c_out))
     x_extra_out = outer(x_extra)
 
     def own_body(
@@ -389,10 +375,11 @@
         both = right + mxu(amp.T, right.astype(BF16), NN) * virt_scale
         rest = amp.astype(F32) - both
         out_ref[...] = rest
-        out_b_ref[...] = rest.astype(BF16)
+        out_b_ref[:virt, :] = rest.astype(BF16)
+        out_b_ref[virt:, :] = jnp.zeros((riders, virt), BF16)
 
     rest, rest_b = call(
-        second_body, [VMEM, VMEM], [sq_f, sq_b], (amp, k_first)
+        second_body, [VMEM, VMEM], [sq_f, longer], (amp, k_first)
     )
     rests = [lax.ppermute(rest_b, "role", [(0, s)]) for s in range(1, roles)]
 
@@ -410,7 +397,7 @@
     )
 
     def outer_again_body(nums, low_ref, s_ref, se_ref, *refs):
-        amp_refs, (c_ref, stack_ref) = refs[:roles], refs[-2:]
+        amp_refs, c_ref = refs[:roles], refs[-1]
         role = lax.axis_index("role")
 
         @pl.when(role > 0)
@@ -423,22 +410,40 @@
                     choices = [told[:, slot * pairs + q : slot * pairs + q + 1] for q in range(pairs)]
                     parts.append((pair_at[m], pick(choices, pair_at[m]), amp_refs[m][...]))
                 c_ref[slot] = coupled(of_s, parts).astype(BF16)
-            for m in range(roles):
-                stack_ref[pair_at[m]] = amp_refs[m][...]
-
-    cc_out, stack = call(
+
+    (cc_out,) = call(
         outer_again_body,
         [SMEM] + [VMEM] * (3 + roles),
-        [two_b, all_s],
+        [two_b],
         (nums, low_out, s_out, se_out, *amp_roles),
     )
     cc_from_out = outer(cc_out)
-    stack_in = inner(stack)
-
-    def own_again_body(
-        nums, rest_ref, s_ref, s_in_ref, se_ref, se_in_ref, stack_ref, stack_in_ref, *refs
-    ):
-        rest_refs, (out_ref, out_extra_ref) = refs[:-2], refs[-2:]
+
+    def order_body(nums, *refs):
+        amp_refs, ordered_refs = refs[:roles], refs[-pairs:]
+        role = lax.axis_index("role")
+        for m in range(roles):
+            at = whole(nums[ROLE_PAIR + (role ^ m)])
+            for q, ordered_ref in enumerate(ordered_refs):
+
+                @pl.when(at == q)
+                def _():
+                    ordered_ref[:virt, :] = amp_refs[m][...]
+
+        for ordered_ref in ordered_refs:
+            ordered_ref[virt:, :] = jnp.zeros((riders, virt), BF16)
+
+    ordered = call(
+        order_body,
+        [SMEM] + [VMEM] * roles + [ANY] * (roles - 1),
+        [longer] * pairs,
+        (nums, *amp_roles, *rests),
+    )
+    ordered_in = [inner(x) for x in ordered]
+
+    def own_again_body(nums, rest_ref, s_ref, s_in_ref, se_ref, se_in_ref, *refs):
+        amp_refs, amp_in_refs, rest_refs = refs[:pairs], refs[pairs : 2 * pairs], refs[2 * pairs : -2]
+        out_ref, out_extra_ref = refs[-2:]
         role = lax.axis_index("role")
 
         @pl.when(role > 0)
@@ -446,24 +451,25 @@
             totals = []
             for slot, of_s, of_s_in in ((0, s_ref, s_in_ref), (1, se_ref, se_in_ref)):
                 total = None
-                for at, of, amp_ref in (
-                    (own_weights + 2 * slot * pairs, of_s, stack_ref),
-                    (own_weights + (2 * slot + 1) * pairs, of_s_in, stack_in_ref),
+                for at, of, of_amps in (
+                    (own_weights + 2 * slot * pairs, of_s, amp_refs),
+                    (own_weights + (2 * slot + 1) * pairs, of_s_in, amp_in_refs),
                 ):
-                    c = coupled(of, [(q, nums[at + q], amp_ref[q]) for q in range(pairs)])
+                    parts = [(q, nums[at + q], of_amps[q][:virt, :]) for q in range(pairs)]
+                    c = coupled(of, parts)
                     total = c if total is None else total + c
                 totals.append(total)
             out_ref[...] = rest_ref[...] - totals[0]
             total = -totals[1]
             for s in range(1, roles):
-                total += jnp.where(role == s, rest_refs[s - 1][...].astype(F32), 0.0)
+                total += jnp.where(role == s, rest_refs[s - 1][:virt, :].astype(F32), 0.0)
             out_extra_ref[...] = total
 
     rest, rest_extra = call(
         own_again_body,
-        [SMEM] + [VMEM] * (7 + roles - 1),
+        [SMEM] + [VMEM] * (5 + 2 * pairs + roles - 1),
         [sq_f, sq_f],
-        (nums, rest, s_own, s_in, se_own, se_in, stack, stack_in, *rests),
+        (nums, rest, s_own, s_in, se_own, se_in, *ordered, *ordered_in, *rests),
     )
 
     def last_body(

time: 58.5 us -> 57.8 us (0.988)
  the two profiles are of different devices: /device:TPU:6 before, /device:TPU:0 now
where the time goes in v6:
time: 57.8 us; the launch traced here: 57.6 us
  starting transfers between devices  25.6 us (44%)
  Pallas kernels  19.6 us (34%)
  waiting for transfers between devices  11.5 us (20%)
  between operations  0.87 us (2%)
    pallas_call x13, Pallas kernels, call(): pl.pallas_call(body, in_specs=ins, out_specs=[spec for spec, _, _ in outs...  19.6 us
    ppermute x7, starting transfers between devices, outer(): return lax.ppermute(x, 'pairs', list(enumerate(outer_of)))  12.3 us
    ppermute x7, waiting for transfers between devices, outer(): return lax.ppermute(x, 'pairs', list(enumerate(outer_of)))  10.4 us
    ppermute x3, starting transfers between devices, local(): rests = [lax.ppermute(rest_b, 'role', [(0, s)]) for s in range(1, roles)]  7.62 us
    ppermute x3, starting transfers between devices, swap(): return lax.ppermute(x, 'role', [(i, i ^ by) for i in range(roles)])  3.55 us
    ppermute x7, starting transfers between devices, inner(): return lax.ppermute(x, 'pairs', list(enumerate(inner_of)))  2.11 us
  transfers between devices with their start and end apart: 20, of which 7 were waited for; matrix products, arithmetic and copies ran while one was open for 0% of the time, Pallas kernels for 31%

profile of v6, /device:TPU:0, one launch (start us, length us, event | category | flops | bytes accessed | tf_op | source)
XLA Modules:
  0.0 57.6 jit_solution(12237135096910245388)
XLA Ops:
  0.6 0.5 collective-permute-start.4
  1.1 0.1 collective-permute-start
  1.2 0.4 collective-permute-start.1
  1.7 2.4 %shard_map.113 = (bf16[528,128]{1,0:T(8,128)(2,1)}, bf16[512,128]{1,0:T(8,128)(2,1)}, f32[30]{0:T(128)}) custom-call(s32[4]{0:T(128)} %owner_hbm.1, s32[2,4]{1,0:T(2,128)} %bitcast.1, s32[4,8]{1,0:T(4,128)} %partner_hbm.1, f32[4,8]{1,0:T(4,128)} %coupling_hbm.1, f32[16]{0:T(128)} %eps_hbm.1, s32[4]{0:T(128)} %nvirt_hbm.1, bf16[4,512,256]{2,1,0:T(8,128)(2,1)} %coeff_ref.9), custom_call_target="tpu_custom_call" | custom-call | flops 1 | bytes 1 | tf_op jit(solution)/shard_map/pallas_call | solution.py:33
  4.1 4.8 %collective-permute-start.2 = (bf16[528,128]{1,0:T(8,128)(2,1)}, bf16[528,128]{1,0:T(8,128)(2,1)S(1)}, u32[]{:S(2)}, u32[]{:S(2)}) collective-permute-start(bf16[528,128]{1,0:T(8,128)(2,1)} %get-tuple-element.29), channel_id=1, source_target_pairs={{0,7},{1,2},{2,1},{3,4},{4,3},{5,6},{6,5},{7,0},{8,15},{9,10},{10,... | collective-permute-start | bytes 405512 | tf_op jit(solution)/shard_map/ppermute | solution.py:73
  8.9 0.0 copy-start
  8.9 0.0 copy-start.2
  8.9 0.1 collective-permute-start.3
  9.0 3.6 %collective-permute-done.2.x_ref.low_ref = bf16[528,128]{1,0:T(8,128)(2,1)S(1)} collective-permute-done((bf16[528,128]{1,0:T(8,128)(2,1)}, bf16[528,128]{1,0:T(8,128)(2,1)S(1)}, u32[]{:S(2)}, u32[]{:S(2)}) %collective-permute-start.2) | collective-permute-done | bytes 135200 | tf_op jit(solution)/shard_map/ppermute | solution.py:73
  12.5 2.0 %shard_map.114.after_ref = bf16[1056,128]{1,0:T(8,128)(2,1)S(1)} custom-call(bf16[2,1024,512]{2,1,0:T(8,128)(2,1)} %three_ref.5, bf16[528,128]{1,0:T(8,128)(2,1)S(1)} %collective-permute-done.2.x_ref.low_ref), custom_call_target="tpu_custom_call" | custom-call | flops 1 | bytes 1 | tf_op jit(solution)/shard_map/pallas_call | solution.py:33
  14.5 0.0 copy-start.1
  14.5 0.0 copy-start.3
  14.5 3.2 %collective-permute-start.5 = (bf16[1056,128]{1,0:T(8,128)(2,1)S(1)}, bf16[1056,128]{1,0:T(8,128)(2,1)S(1)}, u32[]{:S(2)}, u32[]{:S(2)}) collective-permute-start(bf16[1056,128]{1,0:T(8,128)(2,1)S(1)} %shard_map.114.after_ref), channel_id=1, source_target_pairs={{0,7},{1,2},{2,1},{3,4},{4,3},{5,6},{6,5},{7,0},{8,15},{9,10},{10,... | collective-permute-start | bytes 811016 | tf_op jit(solution)/shard_map/ppermute | solution.py:73
  17.7 0.0 collective-permute-done.3.x_ref.high_ref
  17.7 1.9 %shard_map.115.after_ref = bf16[1040,128]{1,0:T(8,128)(2,1)S(1)} custom-call(bf16[2,1024,512]{2,1,0:T(8,128)(2,1)} %three_ref.5, bf16[528,128]{1,0:T(8,128)(2,1)S(1)} %collective-permute-done.2.x_ref.low_ref, bf16[512,128]{1,0:T(8,128)(2,1)S(1)} %collective-permute-done.3.x_ref.high_ref, bf16[1056,128]{1,0:T(8,128)(2,1)S(1)} %shard_map.114.after_ref), custom_call_target="tpu_custom_call" | custom-call | flops 1 | bytes 1 | tf_op jit(solution)/shard_map/pallas_call | solution.py:33
  19.7 0.5 collective-permute-start.6
  20.2 0.0 copy-done
  20.2 0.0 copy-done.2
  20.2 0.9 %shard_map.116 = (bf16[4,256,256]{2,1,0:T(8,128)(2,1)S(1)}, bf16[256,256]{1,0:T(8,128)(2,1)S(1)}) custom-call(bf16[4,512,256]{2,1,0:T(8,128)(2,1)S(1)} %copy-done, bf16[4,256,256]{2,1,0:T(8,128)(2,1)S(1)} %copy-done.2, bf16[528,128]{1,0:T(8,128)(2,1)S(1)} %collective-permute-done.2.x_ref.low_ref, bf16[512,128]{1,0:T(8,128)(2,1)S(1)} %collective-permute-done.3.x_ref.high_ref, ...), custom_call_target="tpu_custom_call" | custom-call | flops 1 | bytes 1 | tf_op jit(solution)/shard_map/pallas_call | solution.py:33
  21.1 0.0 collective-permute-done.4.three_in_ref
  21.1 0.0 copy-start.5
  21.1 3.1 %collective-permute-start.7 = (bf16[256,256]{1,0:T(8,128)(2,1)S(1)}, bf16[256,256]{1,0:T(8,128)(2,1)S(1)}, u32[]{:S(2)}, u32[]{:S(2)}) collective-permute-start(bf16[256,256]{1,0:T(8,128)(2,1)S(1)} %get-tuple-element.31.after_ref), channel_id=1, source_target_pairs={{0,7},{1,2},{2,1},{3,4},{4,3},{5,6},{6,5},{7,0},{8,15},{9,10},{10,... | collective-permute-start | bytes 393224 | tf_op jit(solution)/shard_map/ppermute | solution.py:73
  24.3 0.0 copy-done.5
  24.3 0.0 copy-done.1
  24.3 0.0 copy-done.3
  24.3 4.2 %shard_map.118 = (bf16[256,1024]{1,0:T(8,128)(2,1)S(1)}, bf16[1024,256]{1,0:T(8,128)(2,1)S(1)}, bf16[512,256]{1,0:T(8,128)(2,1)S(1)}) custom-call(f32[30]{0:T(128)S(1)} %copy-done.3, bf16[2,1024,512]{2,1,0:T(8,128)(2,1)S(1)} %copy-done.1, bf16[2,1024,512]{2,1,0:T(8,128)(2,1)} %copy-done.5, bf16[4,512,256]{2,1,0:T(8,128)(2,1)S(1)} %copy-done, ...), custom_call_target="tpu_custom_call" | custom-call | flops 1 | bytes 1 | tf_op jit(solution)/shard_map/pallas_call | solution.py:33
  28.5 0.0 collective-permute-done.1.amps_in_ref
  28.5 0.1 collective-permute-start.8
  28.6 0.0 collective-permute-done.coeff_in_ref.in_ref
  28.6 0.0 copy-done.4
  28.6 2.0 %shard_map.117 = (bf16[4,256,256]{2,1,0:T(8,128)(2,1)S(1)}, bf16[4,256,256]{2,1,0:T(8,128)(2,1)S(1)}, f32[256,256]{1,0:T(8,128)S(1)}, f32[256,256]{1,0:T(8,128)S(1)}, f32[256,256]{1,0:T(8,128)S(1)}) custom-call(f32[30]{0:T(128)S(1)} %copy-done.3, bf16[4,512,256]{2,1,0:T(8,128)(2,1)S(1)} %copy-done, ...), custom_call_target="tpu_custom_call" | custom-call | flops 1 | bytes 1 | tf_op jit(solution)/shard_map/pallas_call | solution.py:33
  30.6 3.1 %collective-permute-done.7.co_ref = bf16[256,256]{1,0:T(8,128)(2,1)S(1)} collective-permute-done((bf16[256,256]{1,0:T(8,128)(2,1)S(1)}, bf16[256,256]{1,0:T(8,128)(2,1)S(1)}, u32[]{:S(2)}, u32[]{:S(2)}) %collective-permute-start.7) | collective-permute-done | bytes 131104 | tf_op jit(solution)/shard_map/ppermute | solution.py:73
  33.7 0.0 collective-permute-done.6.high_ref
  33.7 0.0 collective-permute-done.5.low_ref
  33.7 1.0 %shard_map.119 = (bf16[256,256]{1,0:T(8,128)(2,1)S(1)}, f32[256,256]{1,0:T(8,128)S(1)}) custom-call(f32[30]{0:T(128)S(1)} %copy-done.3, bf16[256,1024]{1,0:T(8,128)(2,1)S(1)} %get-tuple-element.34.first_ref, bf16[1024,256]{1,0:T(8,128)(2,1)S(1)} %get-tuple-element.35.second_ref, bf16[1056,128]{1,0:T(8,128)(2,1)S(1)} %collective-permute-done.5.low_ref, ...), custom_call_target="tpu_custom_call" | custom-call | flops 1 | bytes 1 | tf_op jit(solution)/shard_map/pallas_call | solution.py:33
  34.6 1.6 %collective-permute-start.10 = (bf16[256,256]{1,0:T(8,128)(2,1)S(1)}, bf16[256,256]{1,0:T(8,128)(2,1)S(1)}, u32[]{:S(2)}, u32[]{:S(2)}) collective-permute-start(bf16[256,256]{1,0:T(8,128)(2,1)S(1)} %get-tuple-element.37.amp_ref.refs_0_), channel_id=1, source_target_pairs={{0,16},{8,24},{16,0},{24,8},{1,17},{9,25},{17,1},{25,9},{2,18},{10... | collective-permute-start | bytes 393224 | tf_op jit(solution)/shard_map/ppermute | solution.py:76
  36.2 1.4 %collective-permute-start.11 = (bf16[256,256]{1,0:T(8,128)(2,1)S(1)}, bf16[256,256]{1,0:T(8,128)(2,1)S(1)}, u32[]{:S(2)}, u32[]{:S(2)}) collective-permute-start(bf16[256,256]{1,0:T(8,128)(2,1)S(1)} %get-tuple-element.37.amp_ref.refs_0_), channel_id=1, source_target_pairs={{0,24},{8,16},{16,8},{24,0},{1,25},{9,17},{17,9},{25,1},{2,26},{10... | collective-permute-start | bytes 393224 | tf_op jit(solution)/shard_map/ppermute | solution.py:76
  37.6 0.6 collective-permute-start.9
  38.2 0.4 shard_map.120
  38.6 3.4 %collective-permute-start.12 = (bf16[272,256]{1,0:T(8,128)(2,1)S(1)}, bf16[272,256]{1,0:T(8,128)(2,1)S(1)}, u32[]{:S(2)}, u32[]{:S(2)}) collective-permute-start(bf16[272,256]{1,0:T(8,128)(2,1)S(1)} %get-tuple-element.45), channel_id=1, source_target_pairs={{0,8},{1,9},{2,10},{3,11},{4,12},{5,13},{6,14},{7,15}} | collective-permute-start | bytes 417800 | tf_op jit(solution)/shard_map/ppermute | solution.py:384
  42.0 0.0 collective-permute-done.10.refs_2_
  42.0 2.9 %collective-permute-start.13 = (bf16[272,256]{1,0:T(8,128)(2,1)S(1)}, bf16[272,256]{1,0:T(8,128)(2,1)S(1)}, u32[]{:S(2)}, u32[]{:S(2)}) collective-permute-start(bf16[272,256]{1,0:T(8,128)(2,1)S(1)} %get-tuple-element.45), channel_id=1, source_target_pairs={{0,16},{1,17},{2,18},{3,19},{4,20},{5,21},{6,22},{7,23}} | collective-permute-start | bytes 417800 | tf_op jit(solution)/shard_map/ppermute | solution.py:384
  44.9 0.0 collective-permute-done.8.out_ref
  44.9 1.3 %collective-permute-start.14 = (bf16[272,256]{1,0:T(8,128)(2,1)S(1)}, bf16[272,256]{1,0:T(8,128)(2,1)S(1)}, u32[]{:S(2)}, u32[]{:S(2)}) collective-permute-start(bf16[272,256]{1,0:T(8,128)(2,1)S(1)} %get-tuple-element.45), channel_id=1, source_target_pairs={{0,24},{1,25},{2,26},{3,27},{4,28},{5,29},{6,30},{7,31}} | collective-permute-start | bytes 417800 | tf_op jit(solution)/shard_map/ppermute | solution.py:384
  46.3 1.6 %shard_map.121 = (bf16[4,256,256]{2,1,0:T(8,128)(2,1)S(1)}, bf16[4,256,256]{2,1,0:T(8,128)(2,1)S(1)}, bf16[4,256,256]{2,1,0:T(8,128)(2,1)S(1)}) custom-call(f32[30]{0:T(128)S(1)} %copy-done.3, bf16[4,512,256]{2,1,0:T(8,128)(2,1)S(1)} %copy-done, bf16[4,512,256]{2,1,0:T(8,128)(2,1)S(1)} %collective-permute-done.coeff_in_ref.in_ref, ...), custom_call_target="tpu_custom_call" | custom-call | flops 1 | bytes 1 | tf_op jit(solution)/shard_map/pallas_call | solution.py:33
  47.8 0.0 collective-permute-done.11.refs_3_
  47.8 0.0 collective-permute-done.9.refs_1_
  47.8 0.6 shard_map.124
  48.4 0.5 collective-permute-start.19
  48.9 0.0 collective-permute-done.12.refs_4_.refs_8_
  48.9 0.0 collective-permute-done.13.refs_5_.refs_9_
  48.9 0.0 collective-permute-done.14.refs_6_.refs_10_
  48.9 0.7 %shard_map.122 = (bf16[272,256]{1,0:T(8,128)(2,1)S(1)}, bf16[272,256]{1,0:T(8,128)(2,1)S(1)}, bf16[272,256]{1,0:T(8,128)(2,1)S(1)}, bf16[272,256]{1,0:T(8,128)(2,1)S(1)}) custom-call(f32[30]{0:T(128)S(1)} %copy-done.3, bf16[256,256]{1,0:T(8,128)(2,1)S(1)} %get-tuple-element.37.amp_ref.refs_0_, bf16[256,256]{1,0:T(8,128)(2,1)S(1)} %collective-permute-done.9.refs_1_, ...), custom_call_target="tpu_custom_call" | custom-call | flops 1 | bytes 1 | tf_op jit(solution)/shard_map/pallas_call | solution.py:33
  49.6 0.1 collective-permute-start.15
  49.7 0.5 collective-permute-start.16
  50.2 0.1 collective-permute-start.17
  50.2 0.4 collective-permute-start.18
  50.7 0.3 collective-permute-done.15.refs_4_
  51.0 0.2 collective-permute-done.16.refs_5_
  51.2 0.3 collective-permute-done.17.refs_6_
  51.5 0.2 collective-permute-done.18.refs_7_
  51.7 0.6 shard_map.123
  52.3 3.8 %collective-permute-done.19.c_ref = bf16[2,256,256]{2,1,0:T(8,128)(2,1)S(1)} collective-permute-done((bf16[2,256,256]{2,1,0:T(8,128)(2,1)S(1)}, bf16[2,256,256]{2,1,0:T(8,128)(2,1)S(1)}, u32[]{:S(2)}, u32[]{:S(2)}) %collective-permute-start.19) | collective-permute-done | bytes 262176 | tf_op jit(solution)/shard_map/ppermute | solution.py:73
  56.1 1.5 %shard_map.125 = (bf16[2,256,256]{2,1,0:T(8,128)(2,1)}, bf16[2,512,256]{2,1,0:T(8,128)(2,1)}) custom-call(f32[30]{0:T(128)S(1)} %copy-done.3, bf16[4,512,256]{2,1,0:T(8,128)(2,1)S(1)} %copy-done, f32[256,256]{1,0:T(8,128)S(1)} %get-tuple-element.32.gain_ref, f32[256,256]{1,0:T(8,128)S(1)} %get-tuple-element.33.gain_extra_ref, ...), custom_call_target="tpu_custom_call" | custom-call | flops 1 | bytes 1 | tf_op jit(solution)/shard_map/pallas_call | solution.py:33
  (1 shorter events, 0.0 us)
Async XLA Ops:
  0.6 20.5 %collective-permute-start.4 = (bf16[2,1024,512]{2,1,0:T(8,128)(2,1)}, bf16[2,1024,512]{2,1,0:T(8,128)(2,1)S(1)}, u32[]{:S(2)}, u32[]{:S(2)}) collective-permute-start(bf16[2,1024,512]{2,1,0:T(8,128)(2,1)} %three_ref.5), channel_id=1, source_target_pairs={{0,1},{1,0},{2,3},{3,2},{4,5},{5,4},{6,7},{7,6},{8,9},{9,8},{10,11... | collective-permute-start | bytes 6291464 | tf_op jit(solution)/shard_map/ppermute | solution.py:70
  1.1 27.4 %collective-permute-start = (bf16[4,512,256]{2,1,0:T(8,128)(2,1)}, bf16[4,512,256]{2,1,0:T(8,128)(2,1)S(1)}, u32[]{:S(2)}, u32[]{:S(2)}) collective-permute-start(bf16[4,512,256]{2,1,0:T(8,128)(2,1)} %coeff_ref.9), channel_id=1, source_target_pairs={{0,1},{1,0},{2,3},{3,2},{4,5},{5,4},{6,7},{7,6},{8,9},{9,8},{10,11... | collective-permute-start | bytes 3145736 | tf_op jit(solution)/shard_map/ppermute | solution.py:70
  1.2 27.2 %collective-permute-start.1 = (bf16[4,256,256]{2,1,0:T(8,128)(2,1)}, bf16[4,256,256]{2,1,0:T(8,128)(2,1)S(1)}, u32[]{:S(2)}, u32[]{:S(2)}) collective-permute-start(bf16[4,256,256]{2,1,0:T(8,128)(2,1)} %amps_ref.5), channel_id=1, source_target_pairs={{0,1},{1,0},{2,3},{3,2},{4,5},{5,4},{6,7},{7,6},{8,9},{9,8},{10,11... | collective-permute-start | bytes 1572872 | tf_op jit(solution)/shard_map/ppermute | solution.py:70
  4.1 8.4 %collective-permute-start.2 = (bf16[528,128]{1,0:T(8,128)(2,1)}, bf16[528,128]{1,0:T(8,128)(2,1)S(1)}, u32[]{:S(2)}, u32[]{:S(2)}) collective-permute-start(bf16[528,128]{1,0:T(8,128)(2,1)} %get-tuple-element.29), channel_id=1, source_target_pairs={{0,7},{1,2},{2,1},{3,4},{4,3},{5,6},{6,5},{7,0},{8,15},{9,10},{10,... | collective-permute-start | bytes 405512 | tf_op jit(solution)/shard_map/ppermute | solution.py:73
  8.9 11.3 %copy-start = (bf16[4,512,256]{2,1,0:T(8,128)(2,1)S(1)}, bf16[4,512,256]{2,1,0:T(8,128)(2,1)}, u32[]{:S(2)}) copy-start(bf16[4,512,256]{2,1,0:T(8,128)(2,1)} %coeff_ref.9) | copy-start | bytes 3145732
  8.9 11.3 %copy-start.2 = (bf16[4,256,256]{2,1,0:T(8,128)(2,1)S(1)}, bf16[4,256,256]{2,1,0:T(8,128)(2,1)}, u32[]{:S(2)}) copy-start(bf16[4,256,256]{2,1,0:T(8,128)(2,1)} %amps_ref.5) | copy-start | bytes 1572868
  8.9 8.9 %collective-permute-start.3 = (bf16[512,128]{1,0:T(8,128)(2,1)}, bf16[512,128]{1,0:T(8,128)(2,1)S(1)}, u32[]{:S(2)}, u32[]{:S(2)}) collective-permute-start(bf16[512,128]{1,0:T(8,128)(2,1)} %get-tuple-element.30), channel_id=1, source_target_pairs={{0,7},{1,2},{2,1},{3,4},{4,3},{5,6},{6,5},{7,0},{8,15},{9,10},{10,... | collective-permute-start | bytes 393224 | tf_op jit(solution)/shard_map/ppermute | solution.py:73
  14.5 9.8 %copy-start.1 = (bf16[2,1024,512]{2,1,0:T(8,128)(2,1)S(1)}, bf16[2,1024,512]{2,1,0:T(8,128)(2,1)}, u32[]{:S(2)}) copy-start(bf16[2,1024,512]{2,1,0:T(8,128)(2,1)} %three_ref.5) | copy-start | bytes 6291460
  14.5 9.8 %copy-start.3 = (f32[30]{0:T(128)S(1)}, f32[30]{0:T(128)}, u32[]{:S(2)}) copy-start(f32[30]{0:T(128)} %get-tuple-element.28.nums) | copy-start | bytes 364
  14.5 19.1 %collective-permute-start.5 = (bf16[1056,128]{1,0:T(8,128)(2,1)S(1)}, bf16[1056,128]{1,0:T(8,128)(2,1)S(1)}, u32[]{:S(2)}, u32[]{:S(2)}) collective-permute-start(bf16[1056,128]{1,0:T(8,128)(2,1)S(1)} %shard_map.114.after_ref), channel_id=1, source_target_pairs={{0,7},{1,2},{2,1},{3,4},{4,3},{5,6},{6,5},{7,0},{8,15},{9,10},{10,... | collective-permute-start | bytes 811016 | tf_op jit(solution)/shard_map/ppermute | solution.py:73
  19.7 14.0 %collective-permute-start.6 = (bf16[1040,128]{1,0:T(8,128)(2,1)S(1)}, bf16[1040,128]{1,0:T(8,128)(2,1)S(1)}, u32[]{:S(2)}, u32[]{:S(2)}) collective-permute-start(bf16[1040,128]{1,0:T(8,128)(2,1)S(1)} %shard_map.115.after_ref), channel_id=1, source_target_pairs={{0,7},{1,2},{2,1},{3,4},{4,3},{5,6},{6,5},{7,0},{8,15},{9,10},{10,... | collective-permute-start | bytes 798728 | tf_op jit(solution)/shard_map/ppermute | solution.py:73
  21.1 3.2 %copy-start.5 = (bf16[2,1024,512]{2,1,0:T(8,128)(2,1)}, bf16[2,1024,512]{2,1,0:T(8,128)(2,1)S(1)}, u32[]{:S(2)}) copy-start(bf16[2,1024,512]{2,1,0:T(8,128)(2,1)S(1)} %collective-permute-done.4.three_in_ref) | copy-start | bytes 6291460
  21.1 12.5 %collective-permute-start.7 = (bf16[256,256]{1,0:T(8,128)(2,1)S(1)}, bf16[256,256]{1,0:T(8,128)(2,1)S(1)}, u32[]{:S(2)}, u32[]{:S(2)}) collective-permute-start(bf16[256,256]{1,0:T(8,128)(2,1)S(1)} %get-tuple-element.31.after_ref), channel_id=1, source_target_pairs={{0,7},{1,2},{2,1},{3,4},{4,3},{5,6},{6,5},{7,0},{8,15},{9,10},{10,... | collective-permute-start | bytes 393224 | tf_op jit(solution)/shard_map/ppermute | solution.py:73
  24.3 4.3 %copy-start.4 = (f32[4,256]{1,0:T(4,128)S(1)}, f32[4,256]{1,0:T(4,128)}, u32[]{:S(2)}) copy-start(f32[4,256]{1,0:T(4,128)} %eps_ref.1) | copy-start | bytes 12292
  28.5 16.4 %collective-permute-start.8 = (bf16[512,256]{1,0:T(8,128)(2,1)S(1)}, bf16[512,256]{1,0:T(8,128)(2,1)S(1)}, u32[]{:S(2)}, u32[]{:S(2)}) collective-permute-start(bf16[512,256]{1,0:T(8,128)(2,1)S(1)} %get-tuple-element.42), channel_id=1, source_target_pairs={{0,7},{1,2},{2,1},{3,4},{4,3},{5,6},{6,5},{7,0},{8,15},{9,10},{10,... | collective-permute-start | bytes 786440 | tf_op jit(solution)/shard_map/ppermute | solution.py:73
  34.6 7.3 %collective-permute-start.10 = (bf16[256,256]{1,0:T(8,128)(2,1)S(1)}, bf16[256,256]{1,0:T(8,128)(2,1)S(1)}, u32[]{:S(2)}, u32[]{:S(2)}) collective-permute-start(bf16[256,256]{1,0:T(8,128)(2,1)S(1)} %get-tuple-element.37.amp_ref.refs_0_), channel_id=1, source_target_pairs={{0,16},{8,24},{16,0},{24,8},{1,17},{9,25},{17,1},{25,9},{2,18},{10... | collective-permute-start | bytes 393224 | tf_op jit(solution)/shard_map/ppermute | solution.py:76
  36.2 11.6 %collective-permute-start.11 = (bf16[256,256]{1,0:T(8,128)(2,1)S(1)}, bf16[256,256]{1,0:T(8,128)(2,1)S(1)}, u32[]{:S(2)}, u32[]{:S(2)}) collective-permute-start(bf16[256,256]{1,0:T(8,128)(2,1)S(1)} %get-tuple-element.37.amp_ref.refs_0_), channel_id=1, source_target_pairs={{0,24},{8,16},{16,8},{24,0},{1,25},{9,17},{17,9},{25,1},{2,26},{10... | collective-permute-start | bytes 393224 | tf_op jit(solution)/shard_map/ppermute | solution.py:76
  37.6 10.2 %collective-permute-start.9 = (bf16[256,256]{1,0:T(8,128)(2,1)S(1)}, bf16[256,256]{1,0:T(8,128)(2,1)S(1)}, u32[]{:S(2)}, u32[]{:S(2)}) collective-permute-start(bf16[256,256]{1,0:T(8,128)(2,1)S(1)} %get-tuple-element.37.amp_ref.refs_0_), channel_id=1, source_target_pairs={{0,8},{8,0},{16,24},{24,16},{1,9},{9,1},{17,25},{25,17},{2,10},{10... | collective-permute-start | bytes 393224 | tf_op jit(solution)/shard_map/ppermute | solution.py:76
  38.6 10.3 %collective-permute-start.12 = (bf16[272,256]{1,0:T(8,128)(2,1)S(1)}, bf16[272,256]{1,0:T(8,128)(2,1)S(1)}, u32[]{:S(2)}, u32[]{:S(2)}) collective-permute-start(bf16[272,256]{1,0:T(8,128)(2,1)S(1)} %get-tuple-element.45), channel_id=1, source_target_pairs={{0,8},{1,9},{2,10},{3,11},{4,12},{5,13},{6,14},{7,15}} | collective-permute-start | bytes 417800 | tf_op jit(solution)/shard_map/ppermute | solution.py:384
  42.0 6.9 %collective-permute-start.13 = (bf16[272,256]{1,0:T(8,128)(2,1)S(1)}, bf16[272,256]{1,0:T(8,128)(2,1)S(1)}, u32[]{:S(2)}, u32[]{:S(2)}) collective-permute-start(bf16[272,256]{1,0:T(8,128)(2,1)S(1)} %get-tuple-element.45), channel_id=1, source_target_pairs={{0,16},{1,17},{2,18},{3,19},{4,20},{5,21},{6,22},{7,23}} | collective-permute-start | bytes 417800 | tf_op jit(solution)/shard_map/ppermute | solution.py:384
  44.9 4.0 %collective-permute-start.14 = (bf16[272,256]{1,0:T(8,128)(2,1)S(1)}, bf16[272,256]{1,0:T(8,128)(2,1)S(1)}, u32[]{:S(2)}, u32[]{:S(2)}) collective-permute-start(bf16[272,256]{1,0:T(8,128)(2,1)S(1)} %get-tuple-element.45), channel_id=1, source_target_pairs={{0,24},{1,25},{2,26},{3,27},{4,28},{5,29},{6,30},{7,31}} | collective-permute-start | bytes 417800 | tf_op jit(solution)/shard_map/ppermute | solution.py:384
  48.4 7.7 %collective-permute-start.19 = (bf16[2,256,256]{2,1,0:T(8,128)(2,1)S(1)}, bf16[2,256,256]{2,1,0:T(8,128)(2,1)S(1)}, u32[]{:S(2)}, u32[]{:S(2)}) collective-permute-start(bf16[2,256,256]{2,1,0:T(8,128)(2,1)S(1)} %shard_map.124), channel_id=1, source_target_pairs={{0,7},{1,2},{2,1},{3,4},{4,3},{5,6},{6,5},{7,0},{8,15},{9,10},{10,... | collective-permute-start | bytes 786440 | tf_op jit(solution)/shard_map/ppermute | solution.py:73
  49.6 1.4 %collective-permute-start.15 = (bf16[272,256]{1,0:T(8,128)(2,1)S(1)}, bf16[272,256]{1,0:T(8,128)(2,1)S(1)}, u32[]{:S(2)}, u32[]{:S(2)}) collective-permute-start(bf16[272,256]{1,0:T(8,128)(2,1)S(1)} %get-tuple-element.46.refs_0_), channel_id=1, source_target_pairs={{0,1},{1,0},{2,3},{3,2},{4,5},{5,4},{6,7},{7,6},{8,9},{9,8},{10,11... | collective-permute-start | bytes 417800 | tf_op jit(solution)/shard_map/ppermute | solution.py:70
  49.7 1.5 %collective-permute-start.16 = (bf16[272,256]{1,0:T(8,128)(2,1)S(1)}, bf16[272,256]{1,0:T(8,128)(2,1)S(1)}, u32[]{:S(2)}, u32[]{:S(2)}) collective-permute-start(bf16[272,256]{1,0:T(8,128)(2,1)S(1)} %get-tuple-element.47.refs_1_), channel_id=1, source_target_pairs={{0,1},{1,0},{2,3},{3,2},{4,5},{5,4},{6,7},{7,6},{8,9},{9,8},{10,11... | collective-permute-start | bytes 417800 | tf_op jit(solution)/shard_map/ppermute | solution.py:70
  50.2 1.4 %collective-permute-start.17 = (bf16[272,256]{1,0:T(8,128)(2,1)S(1)}, bf16[272,256]{1,0:T(8,128)(2,1)S(1)}, u32[]{:S(2)}, u32[]{:S(2)}) collective-permute-start(bf16[272,256]{1,0:T(8,128)(2,1)S(1)} %get-tuple-element.48.refs_2_), channel_id=1, source_target_pairs={{0,1},{1,0},{2,3},{3,2},{4,5},{5,4},{6,7},{7,6},{8,9},{9,8},{10,11... | collective-permute-start | bytes 417800 | tf_op jit(solution)/shard_map/ppermute | solution.py:70
  50.2 1.5 %collective-permute-start.18 = (bf16[272,256]{1,0:T(8,128)(2,1)S(1)}, bf16[272,256]{1,0:T(8,128)(2,1)S(1)}, u32[]{:S(2)}, u32[]{:S(2)}) collective-permute-start(bf16[272,256]{1,0:T(8,128)(2,1)S(1)} %get-tuple-element.49.refs_3_), channel_id=1, source_target_pairs={{0,1},{1,0},{2,3},{3,2},{4,5},{5,4},{6,7},{7,6},{8,9},{9,8},{10,11... | collective-permute-start | bytes 417800 | tf_op jit(solution)/shard_map/ppermute | solution.py:70

commit v7 on v6

--- a/solution.py
+++ b/solution.py
@@ -214,53 +214,47 @@
             total = term if total is None else total + term
         return total
 
-    block_scratch = [pltpu.VMEM((aux, pao), BF16), pltpu.SemaphoreType.DMA((aux // tile,))]
-
-    def by_tiles(three_ref, at_occ, block_ref, sems, product):
-        tiles = [pl.ds(at, tile) for at in range(0, aux, tile)]
-        copies = [
-            pltpu.make_async_copy(three_ref.at[at_occ, rows], block_ref.at[rows], sems.at[at])
-            for at, rows in enumerate(tiles)
-        ]
-        for copy in copies:
-            copy.start()
-        for copy, rows in zip(copies, tiles):
-            copy.wait()
-            product(rows, block_ref[rows, :])
-
-    def half_into(y_ref, x):
-        def product(rows, block):
-            y_ref[rows, :] = (mxu(block, x, NN) * pao_scale).astype(BF16)
-
-        return product
-
-    def outer_low_body(three_ref, x_ref, y_ref, block_ref, sems):
-        at_occ = whole(told_of(x_ref)[0, weights])
-        by_tiles(three_ref, at_occ, block_ref, sems, half_into(y_ref, x_ref[:pao, :]))
+    tiles = [pl.ds(at, tile) for at in range(0, aux, tile)]
+
+    def half_into(y_ref, three_ref, at_occ, x):
+        for rows in tiles:
+            y_ref[rows, :] = (mxu(three_ref[at_occ, rows, :], x, NN) * pao_scale).astype(BF16)
+
+    def fetch_body(three_ref, after_ref, held_ref, sem):
+        copy = pltpu.make_async_copy(three_ref, held_ref, sem)
+        copy.start()
+        copy.wait()
+
+    (blocks,) = call(
+        fetch_body,
+        [ANY, ANY],
+        [(VMEM, three_index.shape, BF16)],
+        (three_index, x_high),
+        scratch=[pltpu.SemaphoreType.DMA],
+        vmem=50,
+    )
+
+    def outer_low_body(three_ref, x_ref, y_ref):
+        half_into(y_ref, three_ref, whole(told_of(x_ref)[0, weights]), x_ref[:pao, :])
         y_ref[aux:, :] = jnp.zeros((2 * riders, part), BF16)
 
     (y_low,) = call(
         outer_low_body,
-        [ANY, VMEM],
+        [VMEM, VMEM],
         [(VMEM, (aux + 2 * riders, part), BF16)],
-        (three_index, low_out),
-        scratch=block_scratch,
-        vmem=52,
+        (blocks, low_out),
     )
     y_low_from_out = outer(y_low)
 
-    def outer_high_body(three_ref, low_ref, x_ref, after_ref, y_ref, block_ref, sems):
-        at_occ = whole(told_of(low_ref)[0, weights])
-        by_tiles(three_ref, at_occ, block_ref, sems, half_into(y_ref, x_ref[...]))
+    def outer_high_body(three_ref, low_ref, x_ref, after_ref, y_ref):
+        half_into(y_ref, three_ref, whole(told_of(low_ref)[0, weights]), x_ref[...])
         y_ref[aux:, :] = jnp.zeros((riders, part), BF16)
 
     (y_high,) = call(
         outer_high_body,
-        [ANY, VMEM, VMEM, ANY],
+        [VMEM, VMEM, VMEM, ANY],
         [(VMEM, (aux + riders, part), BF16)],
-        (three_index, low_out, high_out, y_low),
-        scratch=block_scratch,
-        vmem=52,
+        (blocks, low_out, high_out, y_low),
     )
     y_high_from_out = outer(y_high)
 
@@ -270,40 +264,55 @@
         overlaps(x_ref[...], coeff_ref, s_ref)
         told = told_of(low_ref)
         c = coupled(s_ref, [(q, told[0, q], amps_ref[q]) for q in range(pairs)])
-        c_ref[...] = c.astype(BF16)
+        c_ref[:virt, :] = c.astype(BF16)
+        c_ref[virt:, :] = jnp.zeros((3 * riders, virt), BF16)
 
     s_out, c_out = call(
         outer_body,
         [VMEM, VMEM, VMEM, VMEM, ANY],
-        [all_s, sq_b],
+        [all_s, (VMEM, (virt + 3 * riders, virt), BF16)],
         (coeff, amps, low_out, high_out, y_high),
         scratch=[pltpu.VMEM((pao, virt), BF16)],
     )
     c_from_out = outer(c_out)
 
     def own_half_body(
-        nums, three_ref, three_in_ref, coeff_ref, after_ref, first_ref, second_ref, extra_ref, block_ref, sems
+        nums, three_ref, three_in_ref, coeff_ref, after_ref, first_ref, second_ref, extra_ref, block_ref, sem
     ):
         x = coeff_ref[whole(nums[MINE])]
-        extra_ref[...] = coeff_ref[whole(nums[EXTRA])]
+        extra_ref[:pao, :] = coeff_ref[whole(nums[EXTRA])]
+        extra_ref[pao:, :] = jnp.zeros((2 * riders, virt), BF16)
+        whose, second = whole(nums[WHOSE]), whole(nums[SECOND])
+        copy = pltpu.make_async_copy(three_in_ref.at[second], block_ref.at[0], sem)
+
+        @pl.when(whose == 1)
+        def _():
+            copy.start()
+
         turned = x.T
-
-        def product(rows, block):
-            first_ref[:, rows] = (mxu(turned, block, NT) * pao_scale).astype(BF16)
-
-        by_tiles(three_ref, whole(nums[FIRST]), block_ref, sems, product)
-        for whose, source in enumerate((three_ref, three_in_ref)):
-
-            @pl.when(whole(nums[WHOSE]) == whose)
-            def _():
-                by_tiles(source, whole(nums[SECOND]), block_ref, sems, half_into(second_ref, x))
+        first = whole(nums[FIRST])
+        for rows in tiles:
+            first_ref[:, rows] = (mxu(turned, three_ref[first, rows, :], NT) * pao_scale).astype(BF16)
+
+        @pl.when(whose == 0)
+        def _():
+            half_into(second_ref, three_ref, second, x)
+
+        @pl.when(whose == 1)
+        def _():
+            copy.wait()
+            half_into(second_ref, block_ref, 0, x)
 
     first_t, second, x_extra = call(
         own_half_body,
-        [SMEM, ANY, ANY, VMEM, ANY],
-        [(VMEM, (virt, aux), BF16), (VMEM, (aux, virt), BF16), (VMEM, (pao, virt), BF16)],
-        (nums, three_index, three_in, coeff, c_out),
-        scratch=block_scratch,
+        [SMEM, VMEM, ANY, VMEM, ANY],
+        [
+            (VMEM, (virt, aux), BF16),
+            (VMEM, (aux, virt), BF16),
+            (VMEM, (pao + 2 * riders, virt), BF16),
+        ],
+        (nums, blocks, three_in, coeff, c_out),
+        scratch=[pltpu.VMEM((1, aux, pao), BF16), pltpu.SemaphoreType.DMA],
     )
     x_extra_out = outer(x_extra)
 
@@ -341,9 +350,7 @@
         (nums, coeff, coeff_in, amps, amps_in, eps_virt, c_out),
     )
 
-    def first_body(
-        nums, first_ref, second_ref, low_ref, high_ref, amps_ref, c_ref, co_ref, gain_ref, amp_ref, k_ref
-    ):
+    def k_body(nums, first_ref, second_ref, low_ref, high_ref, after_ref, k_ref, k_b_ref):
         first = first_ref[...]
         outside = whole(nums[WHOSE]) == 2
 
@@ -356,44 +363,40 @@
         def _():
             k_ref[...] = mxu(first, second_ref[...], NN) * aux_scale
 
+        k_b_ref[:virt, :] = k_ref[...].astype(BF16)
+        k_b_ref[virt:, :] = jnp.zeros((riders, virt), BF16)
+
+    k_first, k_b = call(
+        k_body,
+        [SMEM] + [VMEM] * 4 + [ANY],
+        [sq_f, longer],
+        (nums, first_t, second, y_low_from_out, y_high_from_out, c_own),
+    )
+    k_extras = [lax.ppermute(k_b, "role", [(0, s)]) for s in range(1, roles)]
+
+    def first_body(nums, k_ref, amps_ref, c_ref, co_ref, gain_ref, amp_ref):
         old = amps_ref[whole(nums[MINE])].astype(F32)
-        c = c_ref[...] + co_ref[...].astype(F32)
+        c = c_ref[...] + co_ref[:virt, :].astype(F32)
         amp_ref[...] = (gain_ref[...] * (old - k_ref[...] - c)).astype(BF16)
 
-    amp, k_first = call(
+    (amp,) = call(
         first_body,
-        [SMEM] + [VMEM] * 8,
-        [sq_b, sq_f],
-        (nums, first_t, second, y_low_from_out, y_high_from_out, amps, c_own, c_from_out, gain),
+        [SMEM] + [VMEM] * 5,
+        [sq_b],
+        (nums, k_first, amps, c_own, c_from_out, gain),
     )
     amp_roles = [amp] + [swap(amp, m) for m in range(1, roles)]
 
-    def second_body(amp_ref, k_ref, out_ref, out_b_ref):
-        amp = amp_ref[...]
-        k = k_ref[...]
-        right = k + mxu(k.astype(BF16), amp, NN) * virt_scale
-        both = right + mxu(amp.T, right.astype(BF16), NN) * virt_scale
-        rest = amp.astype(F32) - both
-        out_ref[...] = rest
-        out_b_ref[:virt, :] = rest.astype(BF16)
-        out_b_ref[virt:, :] = jnp.zeros((riders, virt), BF16)
-
-    rest, rest_b = call(
-        second_body, [VMEM, VMEM], [sq_f, longer], (amp, k_first)
-    )
-    rests = [lax.ppermute(rest_b, "role", [(0, s)]) for s in range(1, roles)]
-
-    def extra_body(nums, coeff_ref, in_ref, out_ref, after_ref, own_s_ref, in_s_ref, out_s_ref):
-        overlaps(out_ref[...], coeff_ref, out_s_ref)
-        x = coeff_ref[whole(nums[EXTRA])]
-        overlaps(x, coeff_ref, own_s_ref)
-        overlaps(x, in_ref, in_s_ref)
-
-    se_own, se_in, se_out = call(
-        extra_body,
-        [SMEM, VMEM, VMEM, VMEM, ANY],
-        [all_s, all_s, all_s],
-        (nums, coeff, coeff_in, x_extra_out, rest),
+    def extra_out_body(coeff_ref, x_ref, *refs):
+        @pl.when(lax.axis_index("role") > 0)
+        def _():
+            overlaps(x_ref[:pao, :], coeff_ref, refs[-1])
+
+    (se_out,) = call(
+        extra_out_body,
+        [VMEM, VMEM] + [ANY] * roles,
+        [all_s],
+        (coeff, x_extra_out, amp, *k_extras),
     )
 
     def outer_again_body(nums, low_ref, s_ref, se_ref, *refs):
@@ -435,41 +438,54 @@
 
     ordered = call(
         order_body,
-        [SMEM] + [VMEM] * roles + [ANY] * (roles - 1),
+        [SMEM] + [VMEM] * roles,
         [longer] * pairs,
-        (nums, *amp_roles, *rests),
+        (nums, *amp_roles),
     )
     ordered_in = [inner(x) for x in ordered]
 
-    def own_again_body(nums, rest_ref, s_ref, s_in_ref, se_ref, se_in_ref, *refs):
-        amp_refs, amp_in_refs, rest_refs = refs[:pairs], refs[pairs : 2 * pairs], refs[2 * pairs : -2]
-        out_ref, out_extra_ref = refs[-2:]
+    def extra_body(nums, coeff_ref, in_ref, after_ref, s_ref, s_in_ref):
+        @pl.when(lax.axis_index("role") > 0)
+        def _():
+            x = coeff_ref[whole(nums[EXTRA])]
+            overlaps(x, coeff_ref, s_ref)
+            overlaps(x, in_ref, s_in_ref)
+
+    se_own, se_in = call(
+        extra_body,
+        [SMEM, VMEM, VMEM, ANY],
+        [all_s, all_s],
+        (nums, coeff, coeff_in, cc_out),
+    )
+
+    def own_again_body(nums, k_ref, s_ref, s_in_ref, se_ref, se_in_ref, *refs):
+        amp_refs, amp_in_refs, k_refs = refs[:pairs], refs[pairs : 2 * pairs], refs[2 * pairs : -2]
         role = lax.axis_index("role")
 
+        def rest(pair, k, of_s, of_s_in, at):
+            amp = amp_refs[0][:virt, :]
+            for q in range(1, pairs):
+                amp = jnp.where(pair == q, amp_refs[q][:virt, :], amp)
+            right = k + mxu(k.astype(BF16), amp, NN) * virt_scale
+            total = right + mxu(amp.T, right.astype(BF16), NN) * virt_scale
+            for first, of, of_amps in ((at, of_s, amp_refs), (at + pairs, of_s_in, amp_in_refs)):
+                parts = [(q, nums[first + q], of_amps[q][:virt, :]) for q in range(pairs)]
+                total += coupled(of, parts)
+            return amp.astype(F32) - total
+
         @pl.when(role > 0)
         def _():
-            totals = []
-            for slot, of_s, of_s_in in ((0, s_ref, s_in_ref), (1, se_ref, se_in_ref)):
-                total = None
-                for at, of, of_amps in (
-                    (own_weights + 2 * slot * pairs, of_s, amp_refs),
-                    (own_weights + (2 * slot + 1) * pairs, of_s_in, amp_in_refs),
-                ):
-                    parts = [(q, nums[at + q], of_amps[q][:virt, :]) for q in range(pairs)]
-                    c = coupled(of, parts)
-                    total = c if total is None else total + c
-                totals.append(total)
-            out_ref[...] = rest_ref[...] - totals[0]
-            total = -totals[1]
-            for s in range(1, roles):
-                total += jnp.where(role == s, rest_refs[s - 1][:virt, :].astype(F32), 0.0)
-            out_extra_ref[...] = total
+            refs[-2][...] = rest(whole(nums[MINE]), k_ref[...], s_ref, s_in_ref, own_weights)
+            k = k_refs[0][:virt, :].astype(F32)
+            for s in range(2, roles):
+                k = jnp.where(role == s, k_refs[s - 1][:virt, :].astype(F32), k)
+            refs[-1][...] = rest(whole(nums[EXTRA]), k, se_ref, se_in_ref, own_weights + 2 * pairs)
 
     rest, rest_extra = call(
         own_again_body,
         [SMEM] + [VMEM] * (5 + 2 * pairs + roles - 1),
         [sq_f, sq_f],
-        (nums, rest, s_own, s_in, se_own, se_in, *ordered, *ordered_in, *rests),
+        (nums, k_first, s_own, s_in, se_own, se_in, *ordered, *ordered_in, *k_extras),
     )
 
     def last_body(

time: 57.8 us -> 56.9 us (0.984)
  Pallas kernels: 19.6 us -> 15.6 us
  waiting for transfers between devices: 11.5 us -> 13.5 us
  local copies, waits for them, and re-layouts: 0.03 us -> 0.96 us
    ppermute x3, waiting for transfers between devices: 0.01 us -> 4.35 us  [swap(): return lax.ppermute(x, 'role', [(i, i ^ by) for i in range(roles)])]
    pallas_call x13 -> x15, Pallas kernels: 19.6 us -> 15.6 us  [call(): pl.pallas_call(body, in_specs=ins, out_specs=[spec for spec, _, _ in outs...]
    ppermute x7, waiting for transfers between devices: 10.4 us -> 7.57 us  [outer(): return lax.ppermute(x, 'pairs', list(enumerate(outer_of)))]
    ppermute x3, starting transfers between devices: 7.62 us -> 6.43 us  [local(): k_extras = [lax.ppermute(k_b, 'role', [(0, s)]) for s in range(1, roles)]]
    ppermute x3, waiting for transfers between devices: 0.01 us -> 1.12 us  [local(): k_extras = [lax.ppermute(k_b, 'role', [(0, s)]) for s in range(1, roles)]]
    unnamed x12, local copies, waits for them, and re-layouts: 0.03 us -> 0.96 us
    ppermute x7, starting transfers between devices: 12.3 us -> 13.1 us  [outer(): return lax.ppermute(x, 'pairs', list(enumerate(outer_of)))]
  transfers between devices with their start and end apart: 20 -> 20, of which waited for: 7 -> 8; matrix products, arithmetic and copies ran while one was open for 0% -> 0% of each run, Pallas kernels for 31% -> 24%
where the time goes in v7:
time: 56.9 us; the launch traced here: 56.7 us
  starting transfers between devices  25.7 us (45%)
  Pallas kernels  15.6 us (27%)
  waiting for transfers between devices  13.5 us (24%)
  local copies, waits for them, and re-layouts  0.96 us (2%)
  between operations  0.85 us (1%)
    pallas_call x15, Pallas kernels, call(): pl.pallas_call(body, in_specs=ins, out_specs=[spec for spec, _, _ in outs...  15.6 us
    ppermute x7, starting transfers between devices, outer(): return lax.ppermute(x, 'pairs', list(enumerate(outer_of)))  13.1 us
    ppermute x7, waiting for transfers between devices, outer(): return lax.ppermute(x, 'pairs', list(enumerate(outer_of)))  7.57 us
    ppermute x3, starting transfers between devices, local(): k_extras = [lax.ppermute(k_b, 'role', [(0, s)]) for s in range(1, roles)]  6.43 us
    ppermute x3, waiting for transfers between devices, swap(): return lax.ppermute(x, 'role', [(i, i ^ by) for i in range(roles)])  4.35 us
    ppermute x3, starting transfers between devices, swap(): return lax.ppermute(x, 'role', [(i, i ^ by) for i in range(roles)])  4.06 us
    ppermute x7, starting transfers between devices, inner(): return lax.ppermute(x, 'pairs', list(enumerate(inner_of)))  2.11 us
  transfers between devices with their start and end apart: 20, of which 8 were waited for; matrix products, arithmetic and copies ran while one was open for 0% of the time, Pallas kernels for 24%

profile of v7, /device:TPU:0, one launch (start us, length us, event | category | flops | bytes accessed | tf_op | source)
XLA Modules:
  0.0 56.7 jit_solution(16025839505921314786)
XLA Ops:
  0.6 0.5 collective-permute-start.4
  1.1 0.1 collective-permute-start
  1.2 0.4 collective-permute-start.1
  1.7 2.4 %shard_map.113 = (bf16[528,128]{1,0:T(8,128)(2,1)}, bf16[512,128]{1,0:T(8,128)(2,1)}, f32[30]{0:T(128)}) custom-call(s32[4]{0:T(128)} %owner_hbm.1, s32[2,4]{1,0:T(2,128)} %bitcast.1, s32[4,8]{1,0:T(4,128)} %partner_hbm.1, f32[4,8]{1,0:T(4,128)} %coupling_hbm.1, f32[16]{0:T(128)} %eps_hbm.1, s32[4]{0:T(128)} %nvirt_hbm.1, bf16[4,512,256]{2,1,0:T(8,128)(2,1)} %coeff_ref.11), custom_call_target="tpu_custom_call" | custom-call | flops 1 | bytes 1 | tf_op jit(solution)/shard_map/pallas_call | solution.py:33
  4.1 4.8 %collective-permute-start.2 = (bf16[528,128]{1,0:T(8,128)(2,1)}, bf16[528,128]{1,0:T(8,128)(2,1)S(1)}, u32[]{:S(2)}, u32[]{:S(2)}) collective-permute-start(bf16[528,128]{1,0:T(8,128)(2,1)} %get-tuple-element.26), channel_id=1, source_target_pairs={{0,7},{1,2},{2,1},{3,4},{4,3},{5,6},{6,5},{7,0},{8,15},{9,10},{10,... | collective-permute-start | bytes 405512 | tf_op jit(solution)/shard_map/ppermute | solution.py:73
  8.9 0.1 collective-permute-start.3
  9.0 0.9 %copy-done.2 = bf16[512,128]{1,0:T(8,128)(2,1)S(1)} copy-done((bf16[512,128]{1,0:T(8,128)(2,1)S(1)}, bf16[512,128]{1,0:T(8,128)(2,1)}, u32[]{:S(2)}) %copy-start.2) | copy-done | bytes 131096
  9.9 1.6 %shard_map.114.three_ref = bf16[2,1024,512]{2,1,0:T(8,128)(2,1)S(1)} custom-call(bf16[2,1024,512]{2,1,0:T(8,128)(2,1)} %three_ref.1, bf16[512,128]{1,0:T(8,128)(2,1)S(1)} %copy-done.2), custom_call_target="tpu_custom_call" | custom-call | flops 1 | bytes 1 | tf_op jit(solution)/shard_map/pallas_call | solution.py:33
  11.5 0.0 copy-start
  11.5 0.0 copy-start.1
  11.5 1.0 %collective-permute-done.2.x_ref.low_ref = bf16[528,128]{1,0:T(8,128)(2,1)S(1)} collective-permute-done((bf16[528,128]{1,0:T(8,128)(2,1)}, bf16[528,128]{1,0:T(8,128)(2,1)S(1)}, u32[]{:S(2)}, u32[]{:S(2)}) %collective-permute-start.2) | collective-permute-done | bytes 135200 | tf_op jit(solution)/shard_map/ppermute | solution.py:73
  12.5 0.5 shard_map.115.after_ref
  13.0 0.0 copy-start.3
  13.1 3.2 %collective-permute-start.5 = (bf16[1056,128]{1,0:T(8,128)(2,1)S(1)}, bf16[1056,128]{1,0:T(8,128)(2,1)S(1)}, u32[]{:S(2)}, u32[]{:S(2)}) collective-permute-start(bf16[1056,128]{1,0:T(8,128)(2,1)S(1)} %shard_map.115.after_ref), channel_id=1, source_target_pairs={{0,7},{1,2},{2,1},{3,4},{4,3},{5,6},{6,5},{7,0},{8,15},{9,10},{10,... | collective-permute-start | bytes 811016 | tf_op jit(solution)/shard_map/ppermute | solution.py:73
  16.3 0.0 collective-permute-done.3.x_ref.high_ref
  16.3 0.5 shard_map.116.after_ref
  16.8 1.4 %collective-permute-start.6 = (bf16[1040,128]{1,0:T(8,128)(2,1)S(1)}, bf16[1040,128]{1,0:T(8,128)(2,1)S(1)}, u32[]{:S(2)}, u32[]{:S(2)}) collective-permute-start(bf16[1040,128]{1,0:T(8,128)(2,1)S(1)} %shard_map.116.after_ref), channel_id=1, source_target_pairs={{0,7},{1,2},{2,1},{3,4},{4,3},{5,6},{6,5},{7,0},{8,15},{9,10},{10,... | collective-permute-start | bytes 798728 | tf_op jit(solution)/shard_map/ppermute | solution.py:73
  18.2 0.0 copy-done
  18.2 0.0 copy-done.1
  18.2 0.9 %shard_map.117 = (bf16[4,256,256]{2,1,0:T(8,128)(2,1)S(1)}, bf16[304,256]{1,0:T(8,128)(2,1)S(1)}) custom-call(bf16[4,512,256]{2,1,0:T(8,128)(2,1)S(1)} %copy-done, bf16[4,256,256]{2,1,0:T(8,128)(2,1)S(1)} %copy-done.1, bf16[528,128]{1,0:T(8,128)(2,1)S(1)} %collective-permute-done.2.x_ref.low_ref, bf16[512,128]{1,0:T(8,128)(2,1)S(1)} %collective-permute-done.3.x_ref.high_ref, ...), custom_call_target="tpu_custom_call" | custom-call | flops 1 | bytes 1 | tf_op jit(solution)/shard_map/pallas_call | solution.py:33
  19.1 0.0 collective-permute-done.4.three_in_ref
  19.1 0.0 copy-start.5
  19.2 2.3 %collective-permute-start.8 = (bf16[304,256]{1,0:T(8,128)(2,1)S(1)}, bf16[304,256]{1,0:T(8,128)(2,1)S(1)}, u32[]{:S(2)}, u32[]{:S(2)}) collective-permute-start(bf16[304,256]{1,0:T(8,128)(2,1)S(1)} %get-tuple-element.28.after_ref), channel_id=1, source_target_pairs={{0,7},{1,2},{2,1},{3,4},{4,3},{5,6},{6,5},{7,0},{8,15},{9,10},{10,... | collective-permute-start | bytes 466952 | tf_op jit(solution)/shard_map/ppermute | solution.py:73
  21.4 0.0 copy-done.5
  21.4 0.0 copy-done.3
  21.4 2.3 %shard_map.119 = (bf16[256,1024]{1,0:T(8,128)(2,1)S(1)}, bf16[1024,256]{1,0:T(8,128)(2,1)S(1)}, bf16[544,256]{1,0:T(8,128)(2,1)S(1)}) custom-call(f32[30]{0:T(128)S(1)} %copy-done.3, bf16[2,1024,512]{2,1,0:T(8,128)(2,1)S(1)} %shard_map.114.three_ref, bf16[2,1024,512]{2,1,0:T(8,128)(2,1)} %copy-done.5, bf16[4,512,256]{2,1,0:T(8,128)(2,1)S(1)} %copy-done, ...), custom_call_target="tpu_custom_call" | custom-call | flops 1 | bytes 1 | tf_op jit(solution)/shard_map/pallas_call | solution.py:33
  23.7 0.0 collective-permute-done.1.amps_in_ref
  23.7 0.1 collective-permute-start.7
  23.9 0.0 collective-permute-done.coeff_in_ref.in_ref
  23.9 0.0 copy-done.4
  23.9 2.0 %shard_map.118 = (bf16[4,256,256]{2,1,0:T(8,128)(2,1)S(1)}, bf16[4,256,256]{2,1,0:T(8,128)(2,1)S(1)}, f32[256,256]{1,0:T(8,128)S(1)}, f32[256,256]{1,0:T(8,128)S(1)}, f32[256,256]{1,0:T(8,128)S(1)}) custom-call(f32[30]{0:T(128)S(1)} %copy-done.3, bf16[4,512,256]{2,1,0:T(8,128)(2,1)S(1)} %copy-done, ...), custom_call_target="tpu_custom_call" | custom-call | flops 1 | bytes 1 | tf_op jit(solution)/shard_map/pallas_call | solution.py:33
  25.9 3.5 %collective-permute-done.6.high_ref = bf16[1040,128]{1,0:T(8,128)(2,1)S(1)} collective-permute-done((bf16[1040,128]{1,0:T(8,128)(2,1)S(1)}, bf16[1040,128]{1,0:T(8,128)(2,1)S(1)}, u32[]{:S(2)}, u32[]{:S(2)}) %collective-permute-start.6) | collective-permute-done | bytes 266272 | tf_op jit(solution)/shard_map/ppermute | solution.py:73
  29.4 0.0 collective-permute-done.5.low_ref
  29.4 0.9 %shard_map.120 = (f32[256,256]{1,0:T(8,128)S(1)}, bf16[272,256]{1,0:T(8,128)(2,1)S(1)}) custom-call(f32[30]{0:T(128)S(1)} %copy-done.3, bf16[256,1024]{1,0:T(8,128)(2,1)S(1)} %get-tuple-element.31.first_ref, bf16[1024,256]{1,0:T(8,128)(2,1)S(1)} %get-tuple-element.32.second_ref, bf16[1056,128]{1,0:T(8,128)(2,1)S(1)} %collective-permute-done.5.low_ref, ...), custom_call_target="tpu_custom_call" | custom-call | flops 1 | bytes 1 | tf_op jit(solution)/shard_map/pallas_call | solution.py:33
  30.3 3.4 %collective-permute-start.10 = (bf16[272,256]{1,0:T(8,128)(2,1)S(1)}, bf16[272,256]{1,0:T(8,128)(2,1)S(1)}, u32[]{:S(2)}, u32[]{:S(2)}) collective-permute-start(bf16[272,256]{1,0:T(8,128)(2,1)S(1)} %get-tuple-element.39), channel_id=1, source_target_pairs={{0,16},{1,17},{2,18},{3,19},{4,20},{5,21},{6,22},{7,23}} | collective-permute-start | bytes 417800 | tf_op jit(solution)/shard_map/ppermute | solution.py:375
  33.7 1.7 %collective-permute-start.11 = (bf16[272,256]{1,0:T(8,128)(2,1)S(1)}, bf16[272,256]{1,0:T(8,128)(2,1)S(1)}, u32[]{:S(2)}, u32[]{:S(2)}) collective-permute-start(bf16[272,256]{1,0:T(8,128)(2,1)S(1)} %get-tuple-element.39), channel_id=1, source_target_pairs={{0,24},{1,25},{2,26},{3,27},{4,28},{5,29},{6,30},{7,31}} | collective-permute-start | bytes 417800 | tf_op jit(solution)/shard_map/ppermute | solution.py:375
  35.4 1.3 %collective-permute-start.9 = (bf16[272,256]{1,0:T(8,128)(2,1)S(1)}, bf16[272,256]{1,0:T(8,128)(2,1)S(1)}, u32[]{:S(2)}, u32[]{:S(2)}) collective-permute-start(bf16[272,256]{1,0:T(8,128)(2,1)S(1)} %get-tuple-element.39), channel_id=1, source_target_pairs={{0,8},{1,9},{2,10},{3,11},{4,12},{5,13},{6,14},{7,15}} | collective-permute-start | bytes 417800 | tf_op jit(solution)/shard_map/ppermute | solution.py:375
  36.7 0.0 collective-permute-done.8.co_ref
  36.8 0.6 %shard_map.121.refs_0_ = bf16[256,256]{1,0:T(8,128)(2,1)S(1)} custom-call(f32[30]{0:T(128)S(1)} %copy-done.3, f32[256,256]{1,0:T(8,128)S(1)} %get-tuple-element.34.k_ref, bf16[4,256,256]{2,1,0:T(8,128)(2,1)S(1)} %copy-done.1, f32[256,256]{1,0:T(8,128)S(1)} %get-tuple-element.33.after_ref.c_ref, bf16[304,256]{1,0:T(8,128)(2,1)S(1)} %collective-permute-done.8.co_ref, ...), custom_call_target="tpu_custom_call" | custom-call | flops 1 | bytes 1 | tf_op jit(solution)/shard_map/pallas_call | solution.py:33
  37.4 0.1 collective-permute-start.12
  37.5 1.1 %collective-permute-done.10.refs_2_.refs_9_ = bf16[272,256]{1,0:T(8,128)(2,1)S(1)} collective-permute-done((bf16[272,256]{1,0:T(8,128)(2,1)S(1)}, bf16[272,256]{1,0:T(8,128)(2,1)S(1)}, u32[]{:S(2)}, u32[]{:S(2)}) %collective-permute-start.10) | collective-permute-done | bytes 139296 | tf_op jit(solution)/shard_map/ppermute | solution.py:375
  38.6 2.5 %collective-permute-start.13 = (bf16[256,256]{1,0:T(8,128)(2,1)S(1)}, bf16[256,256]{1,0:T(8,128)(2,1)S(1)}, u32[]{:S(2)}, u32[]{:S(2)}) collective-permute-start(bf16[256,256]{1,0:T(8,128)(2,1)S(1)} %shard_map.121.refs_0_), channel_id=1, source_target_pairs={{0,16},{8,24},{16,0},{24,8},{1,17},{9,25},{17,1},{25,9},{2,18},{10... | collective-permute-start | bytes 393224 | tf_op jit(solution)/shard_map/ppermute | solution.py:76
  41.1 0.0 collective-permute-done.11.refs_3_.refs_10_
  41.1 1.5 %collective-permute-start.14 = (bf16[256,256]{1,0:T(8,128)(2,1)S(1)}, bf16[256,256]{1,0:T(8,128)(2,1)S(1)}, u32[]{:S(2)}, u32[]{:S(2)}) collective-permute-start(bf16[256,256]{1,0:T(8,128)(2,1)S(1)} %shard_map.121.refs_0_), channel_id=1, source_target_pairs={{0,24},{8,16},{16,8},{24,0},{1,25},{9,17},{17,9},{25,1},{2,26},{10... | collective-permute-start | bytes 393224 | tf_op jit(solution)/shard_map/ppermute | solution.py:76
  42.6 0.0 collective-permute-done.9.refs_1_.refs_8_
  42.6 0.0 collective-permute-done.7.x_ref
  42.6 0.0 collective-permute-done.12.refs_1_
  42.6 2.4 %collective-permute-done.13.refs_2_ = bf16[256,256]{1,0:T(8,128)(2,1)S(1)} collective-permute-done((bf16[256,256]{1,0:T(8,128)(2,1)S(1)}, bf16[256,256]{1,0:T(8,128)(2,1)S(1)}, u32[]{:S(2)}, u32[]{:S(2)}) %collective-permute-start.13) | collective-permute-done | bytes 131104 | tf_op jit(solution)/shard_map/ppermute | solution.py:76
  45.0 1.9 %collective-permute-done.14.refs_3_ = bf16[256,256]{1,0:T(8,128)(2,1)S(1)} collective-permute-done((bf16[256,256]{1,0:T(8,128)(2,1)S(1)}, bf16[256,256]{1,0:T(8,128)(2,1)S(1)}, u32[]{:S(2)}, u32[]{:S(2)}) %collective-permute-start.14) | collective-permute-done | bytes 131104 | tf_op jit(solution)/shard_map/ppermute | solution.py:76
  46.9 0.6 shard_map.123.after_ref
  47.5 1.2 %collective-permute-start.19 = (bf16[2,256,256]{2,1,0:T(8,128)(2,1)S(1)}, bf16[2,256,256]{2,1,0:T(8,128)(2,1)S(1)}, u32[]{:S(2)}, u32[]{:S(2)}) collective-permute-start(bf16[2,256,256]{2,1,0:T(8,128)(2,1)S(1)} %shard_map.123.after_ref), channel_id=1, source_target_pairs={{0,7},{1,2},{2,1},{3,4},{4,3},{5,6},{6,5},{7,0},{8,15},{9,10},{10,... | collective-permute-start | bytes 786440 | tf_op jit(solution)/shard_map/ppermute | solution.py:73
  48.7 0.7 %shard_map.125 = (bf16[272,256]{1,0:T(8,128)(2,1)S(1)}, bf16[272,256]{1,0:T(8,128)(2,1)S(1)}, bf16[272,256]{1,0:T(8,128)(2,1)S(1)}, bf16[272,256]{1,0:T(8,128)(2,1)S(1)}) custom-call(f32[30]{0:T(128)S(1)} %copy-done.3, bf16[256,256]{1,0:T(8,128)(2,1)S(1)} %shard_map.121.refs_0_, bf16[256,256]{1,0:T(8,128)(2,1)S(1)} %collective-permute-done.12.refs_1_, ...), custom_call_target="tpu_custom_call" | custom-call | flops 1 | bytes 1 | tf_op jit(solution)/shard_map/pallas_call | solution.py:33
  49.4 0.1 collective-permute-start.15
  49.5 0.5 collective-permute-start.16
  50.0 0.1 collective-permute-start.17
  50.1 0.4 collective-permute-start.18
  50.5 0.6 shard_map.124
  51.1 0.0 collective-permute-done.15.refs_4_
  51.1 0.0 collective-permute-done.16.refs_5_
  51.1 0.3 collective-permute-done.17.refs_6_
  51.4 0.2 collective-permute-done.18.refs_7_
  51.6 0.6 shard_map.126
  52.1 3.0 %collective-permute-done.19.c_ref = bf16[2,256,256]{2,1,0:T(8,128)(2,1)S(1)} collective-permute-done((bf16[2,256,256]{2,1,0:T(8,128)(2,1)S(1)}, bf16[2,256,256]{2,1,0:T(8,128)(2,1)S(1)}, u32[]{:S(2)}, u32[]{:S(2)}) %collective-permute-start.19) | collective-permute-done | bytes 262176 | tf_op jit(solution)/shard_map/ppermute | solution.py:73
  55.2 1.5 %shard_map.127 = (bf16[2,256,256]{2,1,0:T(8,128)(2,1)}, bf16[2,512,256]{2,1,0:T(8,128)(2,1)}) custom-call(f32[30]{0:T(128)S(1)} %copy-done.3, bf16[4,512,256]{2,1,0:T(8,128)(2,1)S(1)} %copy-done, f32[256,256]{1,0:T(8,128)S(1)} %get-tuple-element.29.gain_ref, f32[256,256]{1,0:T(8,128)S(1)} %get-tuple-element.30.gain_extra_ref, ...), custom_call_target="tpu_custom_call" | custom-call | flops 1 | bytes 1 | tf_op jit(solution)/shard_map/pallas_call | solution.py:33
  (3 shorter events, 0.0 us)
Async XLA Ops:
  0.6 18.5 %collective-permute-start.4 = (bf16[2,1024,512]{2,1,0:T(8,128)(2,1)}, bf16[2,1024,512]{2,1,0:T(8,128)(2,1)S(1)}, u32[]{:S(2)}, u32[]{:S(2)}) collective-permute-start(bf16[2,1024,512]{2,1,0:T(8,128)(2,1)} %three_ref.1), channel_id=1, source_target_pairs={{0,1},{1,0},{2,3},{3,2},{4,5},{5,4},{6,7},{7,6},{8,9},{9,8},{10,11... | collective-permute-start | bytes 6291464 | tf_op jit(solution)/shard_map/ppermute | solution.py:70
  1.1 22.7 %collective-permute-start = (bf16[4,512,256]{2,1,0:T(8,128)(2,1)}, bf16[4,512,256]{2,1,0:T(8,128)(2,1)S(1)}, u32[]{:S(2)}, u32[]{:S(2)}) collective-permute-start(bf16[4,512,256]{2,1,0:T(8,128)(2,1)} %coeff_ref.11), channel_id=1, source_target_pairs={{0,1},{1,0},{2,3},{3,2},{4,5},{5,4},{6,7},{7,6},{8,9},{9,8},{10,11... | collective-permute-start | bytes 3145736 | tf_op jit(solution)/shard_map/ppermute | solution.py:70
  1.2 22.5 %collective-permute-start.1 = (bf16[4,256,256]{2,1,0:T(8,128)(2,1)}, bf16[4,256,256]{2,1,0:T(8,128)(2,1)S(1)}, u32[]{:S(2)}, u32[]{:S(2)}) collective-permute-start(bf16[4,256,256]{2,1,0:T(8,128)(2,1)} %amps_ref.5), channel_id=1, source_target_pairs={{0,1},{1,0},{2,3},{3,2},{4,5},{5,4},{6,7},{7,6},{8,9},{9,8},{10,11... | collective-permute-start | bytes 1572872 | tf_op jit(solution)/shard_map/ppermute | solution.py:70
  4.1 8.4 %collective-permute-start.2 = (bf16[528,128]{1,0:T(8,128)(2,1)}, bf16[528,128]{1,0:T(8,128)(2,1)S(1)}, u32[]{:S(2)}, u32[]{:S(2)}) collective-permute-start(bf16[528,128]{1,0:T(8,128)(2,1)} %get-tuple-element.26), channel_id=1, source_target_pairs={{0,7},{1,2},{2,1},{3,4},{4,3},{5,6},{6,5},{7,0},{8,15},{9,10},{10,... | collective-permute-start | bytes 405512 | tf_op jit(solution)/shard_map/ppermute | solution.py:73
  8.9 7.4 %collective-permute-start.3 = (bf16[512,128]{1,0:T(8,128)(2,1)}, bf16[512,128]{1,0:T(8,128)(2,1)S(1)}, u32[]{:S(2)}, u32[]{:S(2)}) collective-permute-start(bf16[512,128]{1,0:T(8,128)(2,1)} %get-tuple-element.27.after_ref), channel_id=1, source_target_pairs={{0,7},{1,2},{2,1},{3,4},{4,3},{5,6},{6,5},{7,0},{8,15},{9,10},{10,... | collective-permute-start | bytes 393224 | tf_op jit(solution)/shard_map/ppermute | solution.py:73
  9.0 0.9 %copy-start.2 = (bf16[512,128]{1,0:T(8,128)(2,1)S(1)}, bf16[512,128]{1,0:T(8,128)(2,1)}, u32[]{:S(2)}) copy-start(bf16[512,128]{1,0:T(8,128)(2,1)} %get-tuple-element.27.after_ref) | copy-start | bytes 393220
  11.5 6.7 %copy-start = (bf16[4,512,256]{2,1,0:T(8,128)(2,1)S(1)}, bf16[4,512,256]{2,1,0:T(8,128)(2,1)}, u32[]{:S(2)}) copy-start(bf16[4,512,256]{2,1,0:T(8,128)(2,1)} %coeff_ref.11) | copy-start | bytes 3145732
  11.5 6.7 %copy-start.1 = (bf16[4,256,256]{2,1,0:T(8,128)(2,1)S(1)}, bf16[4,256,256]{2,1,0:T(8,128)(2,1)}, u32[]{:S(2)}) copy-start(bf16[4,256,256]{2,1,0:T(8,128)(2,1)} %amps_ref.5) | copy-start | bytes 1572868
  13.0 8.4 %copy-start.3 = (f32[30]{0:T(128)S(1)}, f32[30]{0:T(128)}, u32[]{:S(2)}) copy-start(f32[30]{0:T(128)} %get-tuple-element.25.nums) | copy-start | bytes 364
  13.1 16.3 %collective-permute-start.5 = (bf16[1056,128]{1,0:T(8,128)(2,1)S(1)}, bf16[1056,128]{1,0:T(8,128)(2,1)S(1)}, u32[]{:S(2)}, u32[]{:S(2)}) collective-permute-start(bf16[1056,128]{1,0:T(8,128)(2,1)S(1)} %shard_map.115.after_ref), channel_id=1, source_target_pairs={{0,7},{1,2},{2,1},{3,4},{4,3},{5,6},{6,5},{7,0},{8,15},{9,10},{10,... | collective-permute-start | bytes 811016 | tf_op jit(solution)/shard_map/ppermute | solution.py:73
  16.8 12.6 %collective-permute-start.6 = (bf16[1040,128]{1,0:T(8,128)(2,1)S(1)}, bf16[1040,128]{1,0:T(8,128)(2,1)S(1)}, u32[]{:S(2)}, u32[]{:S(2)}) collective-permute-start(bf16[1040,128]{1,0:T(8,128)(2,1)S(1)} %shard_map.116.after_ref), channel_id=1, source_target_pairs={{0,7},{1,2},{2,1},{3,4},{4,3},{5,6},{6,5},{7,0},{8,15},{9,10},{10,... | collective-permute-start | bytes 798728 | tf_op jit(solution)/shard_map/ppermute | solution.py:73
  19.1 2.3 %copy-start.5 = (bf16[2,1024,512]{2,1,0:T(8,128)(2,1)}, bf16[2,1024,512]{2,1,0:T(8,128)(2,1)S(1)}, u32[]{:S(2)}) copy-start(bf16[2,1024,512]{2,1,0:T(8,128)(2,1)S(1)} %collective-permute-done.4.three_in_ref) | copy-start | bytes 6291460
  19.2 17.6 %collective-permute-start.8 = (bf16[304,256]{1,0:T(8,128)(2,1)S(1)}, bf16[304,256]{1,0:T(8,128)(2,1)S(1)}, u32[]{:S(2)}, u32[]{:S(2)}) collective-permute-start(bf16[304,256]{1,0:T(8,128)(2,1)S(1)} %get-tuple-element.28.after_ref), channel_id=1, source_target_pairs={{0,7},{1,2},{2,1},{3,4},{4,3},{5,6},{6,5},{7,0},{8,15},{9,10},{10,... | collective-permute-start | bytes 466952 | tf_op jit(solution)/shard_map/ppermute | solution.py:73
  21.4 2.5 %copy-start.4 = (f32[4,256]{1,0:T(4,128)S(1)}, f32[4,256]{1,0:T(4,128)}, u32[]{:S(2)}) copy-start(f32[4,256]{1,0:T(4,128)} %eps_ref.1) | copy-start | bytes 12292
  23.7 18.8 %collective-permute-start.7 = (bf16[544,256]{1,0:T(8,128)(2,1)S(1)}, bf16[544,256]{1,0:T(8,128)(2,1)S(1)}, u32[]{:S(2)}, u32[]{:S(2)}) collective-permute-start(bf16[544,256]{1,0:T(8,128)(2,1)S(1)} %get-tuple-element.38), channel_id=1, source_target_pairs={{0,7},{1,2},{2,1},{3,4},{4,3},{5,6},{6,5},{7,0},{8,15},{9,10},{10,... | collective-permute-start | bytes 835592 | tf_op jit(solution)/shard_map/ppermute | solution.py:73
  30.3 8.3 %collective-permute-start.10 = (bf16[272,256]{1,0:T(8,128)(2,1)S(1)}, bf16[272,256]{1,0:T(8,128)(2,1)S(1)}, u32[]{:S(2)}, u32[]{:S(2)}) collective-permute-start(bf16[272,256]{1,0:T(8,128)(2,1)S(1)} %get-tuple-element.39), channel_id=1, source_target_pairs={{0,16},{1,17},{2,18},{3,19},{4,20},{5,21},{6,22},{7,23}} | collective-permute-start | bytes 417800 | tf_op jit(solution)/shard_map/ppermute | solution.py:375
  33.7 7.3 %collective-permute-start.11 = (bf16[272,256]{1,0:T(8,128)(2,1)S(1)}, bf16[272,256]{1,0:T(8,128)(2,1)S(1)}, u32[]{:S(2)}, u32[]{:S(2)}) collective-permute-start(bf16[272,256]{1,0:T(8,128)(2,1)S(1)} %get-tuple-element.39), channel_id=1, source_target_pairs={{0,24},{1,25},{2,26},{3,27},{4,28},{5,29},{6,30},{7,31}} | collective-permute-start | bytes 417800 | tf_op jit(solution)/shard_map/ppermute | solution.py:375
  35.4 7.1 %collective-permute-start.9 = (bf16[272,256]{1,0:T(8,128)(2,1)S(1)}, bf16[272,256]{1,0:T(8,128)(2,1)S(1)}, u32[]{:S(2)}, u32[]{:S(2)}) collective-permute-start(bf16[272,256]{1,0:T(8,128)(2,1)S(1)} %get-tuple-element.39), channel_id=1, source_target_pairs={{0,8},{1,9},{2,10},{3,11},{4,12},{5,13},{6,14},{7,15}} | collective-permute-start | bytes 417800 | tf_op jit(solution)/shard_map/ppermute | solution.py:375
  37.4 5.2 %collective-permute-start.12 = (bf16[256,256]{1,0:T(8,128)(2,1)S(1)}, bf16[256,256]{1,0:T(8,128)(2,1)S(1)}, u32[]{:S(2)}, u32[]{:S(2)}) collective-permute-start(bf16[256,256]{1,0:T(8,128)(2,1)S(1)} %shard_map.121.refs_0_), channel_id=1, source_target_pairs={{0,8},{8,0},{16,24},{24,16},{1,9},{9,1},{17,25},{25,17},{2,10},{10... | collective-permute-start | bytes 393224 | tf_op jit(solution)/shard_map/ppermute | solution.py:76
  38.6 6.4 %collective-permute-start.13 = (bf16[256,256]{1,0:T(8,128)(2,1)S(1)}, bf16[256,256]{1,0:T(8,128)(2,1)S(1)}, u32[]{:S(2)}, u32[]{:S(2)}) collective-permute-start(bf16[256,256]{1,0:T(8,128)(2,1)S(1)} %shard_map.121.refs_0_), channel_id=1, source_target_pairs={{0,16},{8,24},{16,0},{24,8},{1,17},{9,25},{17,1},{25,9},{2,18},{10... | collective-permute-start | bytes 393224 | tf_op jit(solution)/shard_map/ppermute | solution.py:76
  41.1 5.9 %collective-permute-start.14 = (bf16[256,256]{1,0:T(8,128)(2,1)S(1)}, bf16[256,256]{1,0:T(8,128)(2,1)S(1)}, u32[]{:S(2)}, u32[]{:S(2)}) collective-permute-start(bf16[256,256]{1,0:T(8,128)(2,1)S(1)} %shard_map.121.refs_0_), channel_id=1, source_target_pairs={{0,24},{8,16},{16,8},{24,0},{1,25},{9,17},{17,9},{25,1},{2,26},{10... | collective-permute-start | bytes 393224 | tf_op jit(solution)/shard_map/ppermute | solution.py:76
  47.5 7.7 %collective-permute-start.19 = (bf16[2,256,256]{2,1,0:T(8,128)(2,1)S(1)}, bf16[2,256,256]{2,1,0:T(8,128)(2,1)S(1)}, u32[]{:S(2)}, u32[]{:S(2)}) collective-permute-start(bf16[2,256,256]{2,1,0:T(8,128)(2,1)S(1)} %shard_map.123.after_ref), channel_id=1, source_target_pairs={{0,7},{1,2},{2,1},{3,4},{4,3},{5,6},{6,5},{7,0},{8,15},{9,10},{10,... | collective-permute-start | bytes 786440 | tf_op jit(solution)/shard_map/ppermute | solution.py:73
  49.4 1.7 %collective-permute-start.15 = (bf16[272,256]{1,0:T(8,128)(2,1)S(1)}, bf16[272,256]{1,0:T(8,128)(2,1)S(1)}, u32[]{:S(2)}, u32[]{:S(2)}) collective-permute-start(bf16[272,256]{1,0:T(8,128)(2,1)S(1)} %get-tuple-element.42.refs_0_), channel_id=1, source_target_pairs={{0,1},{1,0},{2,3},{3,2},{4,5},{5,4},{6,7},{7,6},{8,9},{9,8},{10,11... | collective-permute-start | bytes 417800 | tf_op jit(solution)/shard_map/ppermute | solution.py:70
  49.5 1.6 %collective-permute-start.16 = (bf16[272,256]{1,0:T(8,128)(2,1)S(1)}, bf16[272,256]{1,0:T(8,128)(2,1)S(1)}, u32[]{:S(2)}, u32[]{:S(2)}) collective-permute-start(bf16[272,256]{1,0:T(8,128)(2,1)S(1)} %get-tuple-element.43.refs_1_), channel_id=1, source_target_pairs={{0,1},{1,0},{2,3},{3,2},{4,5},{5,4},{6,7},{7,6},{8,9},{9,8},{10,11... | collective-permute-start | bytes 417800 | tf_op jit(solution)/shard_map/ppermute | solution.py:70
  50.0 1.4 %collective-permute-start.17 = (bf16[272,256]{1,0:T(8,128)(2,1)S(1)}, bf16[272,256]{1,0:T(8,128)(2,1)S(1)}, u32[]{:S(2)}, u32[]{:S(2)}) collective-permute-start(bf16[272,256]{1,0:T(8,128)(2,1)S(1)} %get-tuple-element.44.refs_2_), channel_id=1, source_target_pairs={{0,1},{1,0},{2,3},{3,2},{4,5},{5,4},{6,7},{7,6},{8,9},{9,8},{10,11... | collective-permute-start | bytes 417800 | tf_op jit(solution)/shard_map/ppermute | solution.py:70
  50.1 1.5 %collective-permute-start.18 = (bf16[272,256]{1,0:T(8,128)(2,1)S(1)}, bf16[272,256]{1,0:T(8,128)(2,1)S(1)}, u32[]{:S(2)}, u32[]{:S(2)}) collective-permute-start(bf16[272,256]{1,0:T(8,128)(2,1)S(1)} %get-tuple-element.45.refs_3_), channel_id=1, source_target_pairs={{0,1},{1,0},{2,3},{3,2},{4,5},{5,4},{6,7},{7,6},{8,9},{9,8},{10,11... | collective-permute-start | bytes 417800 | tf_op jit(solution)/shard_map/ppermute | solution.py:70

commit v8 on v7

--- a/solution.py
+++ b/solution.py
@@ -95,6 +95,7 @@
         return chosen
 
     weights = 2 * pairs
+    place_at, mine_at, extra_at = 2 * weights, 2 * weights + 1, 2 * weights + 2
     riders = 16
     longer = (VMEM, (virt + riders, virt), BF16)
     own_weights = ROLE_PAIR + roles
@@ -151,7 +152,9 @@
         nums[SECOND] = place
         lane = lax.broadcasted_iota(I32, (riders, part), 1)
         row = lax.broadcasted_iota(I32, (riders, part), 0)
-        told = jnp.where(lane == weights, place, 0.0)
+        told = jnp.where(lane == place_at, place, 0.0)
+        told = jnp.where(lane == mine_at, mine.astype(F32), told)
+        told = jnp.where(lane == extra_at, extra.astype(F32), told)
         nums[WHOSE] = jnp.where(block == 1, 0, jnp.where(block == inner_at, 1, 2)).astype(F32)
         nums[OCC_MINE] = eps_ref[occ_ref[0, mine]] + eps_ref[occ_ref[1, mine]]
         nums[OCC_EXTRA] = eps_ref[occ_ref[0, extra]] + eps_ref[occ_ref[1, extra]]
@@ -164,9 +167,10 @@
                 near_w[at] += coupling_ref[pair, k]
             for q in range(pairs):
                 to = which * pairs + q
-                nums[own_weights + 2 * which * pairs + q] = near_w[pairs + q]
-                nums[own_weights + (2 * which + 1) * pairs + q] = near_w[inner_at * pairs + q]
+                nums[own_weights + to] = near_w[pairs + q]
+                nums[own_weights + weights + to] = near_w[inner_at * pairs + q]
                 told = jnp.where(lane == to, near_w[outer_at * pairs + q], told)
+                told = jnp.where(lane == weights + to, near_w[inner_at * pairs + q], told)
         coarse = told.astype(BF16).astype(F32)
         middle = (told - coarse).astype(BF16).astype(F32)
         fine = told - coarse - middle
@@ -193,7 +197,7 @@
         ],
         vmem=60,
     )
-    low_out, high_out = outer(x_low), outer(x_high)
+    low_out, high_out, low_in = outer(x_low), outer(x_high), inner(x_low)
 
     def told_of(low_ref):
         rows = low_ref[pao:, :].astype(F32)
@@ -229,13 +233,13 @@
         fetch_body,
         [ANY, ANY],
         [(VMEM, three_index.shape, BF16)],
-        (three_index, x_high),
+        (three_index, nums),
         scratch=[pltpu.SemaphoreType.DMA],
         vmem=50,
     )
 
     def outer_low_body(three_ref, x_ref, y_ref):
-        half_into(y_ref, three_ref, whole(told_of(x_ref)[0, weights]), x_ref[:pao, :])
+        half_into(y_ref, three_ref, whole(told_of(x_ref)[0, place_at]), x_ref[:pao, :])
         y_ref[aux:, :] = jnp.zeros((2 * riders, part), BF16)
 
     (y_low,) = call(
@@ -247,7 +251,7 @@
     y_low_from_out = outer(y_low)
 
     def outer_high_body(three_ref, low_ref, x_ref, after_ref, y_ref):
-        half_into(y_ref, three_ref, whole(told_of(low_ref)[0, weights]), x_ref[...])
+        half_into(y_ref, three_ref, whole(told_of(low_ref)[0, place_at]), x_ref[...])
         y_ref[aux:, :] = jnp.zeros((riders, part), BF16)
 
     (y_high,) = call(
@@ -318,14 +322,14 @@
 
     def own_body(
         nums, coeff_ref, coeff_in_ref, amps_ref, amps_in_ref, eps_ref, after_ref,
-        s_ref, s_in_ref, c_ref, gain_ref, gain_extra_ref,
+        s_ref, c_ref, gain_ref, gain_extra_ref, s_in_ref,
     ):
         mine, extra = whole(nums[MINE]), whole(nums[EXTRA])
         x = coeff_ref[mine]
         total = None
         for at, of_s, of_coeff, of_amps in (
             (own_weights, s_ref, coeff_ref, amps_ref),
-            (own_weights + pairs, s_in_ref, coeff_in_ref, amps_in_ref),
+            (own_weights + weights, s_in_ref, coeff_in_ref, amps_in_ref),
         ):
             overlaps(x, of_coeff, of_s)
             c = coupled(of_s, [(q, nums[at + q], of_amps[q]) for q in range(pairs)])
@@ -343,14 +347,33 @@
         gain_ref[...] = gain(mine, whole(nums[NV_MINE]), nums[OCC_MINE])
         gain_extra_ref[...] = gain(extra, whole(nums[NV_EXTRA]), nums[OCC_EXTRA])
 
-    s_own, s_in, c_own, gain, gain_extra = call(
+    s_own, c_own, gain, gain_extra = call(
         own_body,
         [SMEM] + [VMEM] * 5 + [ANY],
-        [all_s, all_s, sq_f, sq_f, sq_f],
+        [all_s, sq_f, sq_f, sq_f],
         (nums, coeff, coeff_in, amps, amps_in, eps_virt, c_out),
-    )
-
-    def k_body(nums, first_ref, second_ref, low_ref, high_ref, after_ref, k_ref, k_b_ref):
+        scratch=[pltpu.VMEM((pairs, virt, virt), BF16)],
+    )
+
+    def more_body(nums, coeff_ref, in_ref, low_ref, after_ref, se_ref, s_in_ref, se_in_ref):
+        @pl.when(lax.axis_index("role") > 0)
+        def _():
+            told = told_of(low_ref)
+            overlaps(coeff_ref[whole(nums[EXTRA])], coeff_ref, se_ref)
+            overlaps(in_ref[whole(told[0, mine_at])], coeff_ref, s_in_ref)
+            overlaps(in_ref[whole(told[0, extra_at])], coeff_ref, se_in_ref)
+
+    se_own, s_in, se_in = call(
+        more_body,
+        [SMEM, VMEM, VMEM, VMEM, ANY],
+        [all_s, all_s, all_s],
+        (nums, coeff, coeff_in, low_in, c_own),
+    )
+
+    def first_body(
+        nums, first_ref, second_ref, low_ref, high_ref, amps_ref, c_ref, co_ref, gain_ref, after_ref,
+        amp_ref, k_ref,
+    ):
         first = first_ref[...]
         outside = whole(nums[WHOSE]) == 2
 
@@ -363,55 +386,65 @@
         def _():
             k_ref[...] = mxu(first, second_ref[...], NN) * aux_scale
 
-        k_b_ref[:virt, :] = k_ref[...].astype(BF16)
-        k_b_ref[virt:, :] = jnp.zeros((riders, virt), BF16)
-
-    k_first, k_b = call(
-        k_body,
-        [SMEM] + [VMEM] * 4 + [ANY],
-        [sq_f, longer],
-        (nums, first_t, second, y_low_from_out, y_high_from_out, c_own),
-    )
-    k_extras = [lax.ppermute(k_b, "role", [(0, s)]) for s in range(1, roles)]
-
-    def first_body(nums, k_ref, amps_ref, c_ref, co_ref, gain_ref, amp_ref):
         old = amps_ref[whole(nums[MINE])].astype(F32)
         c = c_ref[...] + co_ref[:virt, :].astype(F32)
         amp_ref[...] = (gain_ref[...] * (old - k_ref[...] - c)).astype(BF16)
 
-    (amp,) = call(
+    amp, k_first = call(
         first_body,
-        [SMEM] + [VMEM] * 5,
-        [sq_b],
-        (nums, k_first, amps, c_own, c_from_out, gain),
+        [SMEM] + [VMEM] * 8 + [ANY],
+        [sq_b, sq_f],
+        (
+            nums, first_t, second, y_low_from_out, y_high_from_out,
+            amps, c_own, c_from_out, gain, se_own,
+        ),
     )
     amp_roles = [amp] + [swap(amp, m) for m in range(1, roles)]
 
-    def extra_out_body(coeff_ref, x_ref, *refs):
+    def rest_body(amp_ref, k_ref, out_ref, out_b_ref):
+        amp = amp_ref[...]
+        k = k_ref[...]
+        right = k + mxu(k.astype(BF16), amp, NN) * virt_scale
+        both = right + mxu(amp.T, right.astype(BF16), NN) * virt_scale
+        rest = amp.astype(F32) - both
+        out_ref[...] = rest
+        out_b_ref[:virt, :] = rest.astype(BF16)
+        out_b_ref[virt:, :] = jnp.zeros((riders, virt), BF16)
+
+    rest, rest_b = call(rest_body, [VMEM, VMEM], [sq_f, longer], (amp, k_first))
+    rests = [lax.ppermute(rest_b, "role", [(0, s)]) for s in range(1, roles)]
+
+    def extra_out_body(coeff_ref, x_ref, after_ref, s_ref):
         @pl.when(lax.axis_index("role") > 0)
         def _():
-            overlaps(x_ref[:pao, :], coeff_ref, refs[-1])
+            overlaps(x_ref[:pao, :], coeff_ref, s_ref)
 
     (se_out,) = call(
         extra_out_body,
-        [VMEM, VMEM] + [ANY] * roles,
+        [VMEM, VMEM, ANY],
         [all_s],
-        (coeff, x_extra_out, amp, *k_extras),
-    )
+        (coeff, x_extra_out, amp),
+    )
+
+    def parts_of(nums, weight_of, amp_refs):
+        role = lax.axis_index("role")
+        parts = []
+        for m in range(roles):
+            at = whole(nums[ROLE_PAIR + (role ^ m)])
+            parts.append((at, weight_of(at), amp_refs[m][...]))
+        return parts
+
+    def told_weight(told, first):
+        return lambda at: pick([told[:, first + q : first + q + 1] for q in range(pairs)], at)
 
     def outer_again_body(nums, low_ref, s_ref, se_ref, *refs):
         amp_refs, c_ref = refs[:roles], refs[-1]
-        role = lax.axis_index("role")
-
-        @pl.when(role > 0)
+
+        @pl.when(lax.axis_index("role") > 0)
         def _():
             told = told_of(low_ref)
-            pair_at = [whole(nums[ROLE_PAIR + (role ^ m)]) for m in range(roles)]
             for slot, of_s in enumerate((s_ref, se_ref)):
-                parts = []
-                for m in range(roles):
-                    choices = [told[:, slot * pairs + q : slot * pairs + q + 1] for q in range(pairs)]
-                    parts.append((pair_at[m], pick(choices, pair_at[m]), amp_refs[m][...]))
+                parts = parts_of(nums, told_weight(told, slot * pairs), amp_refs)
                 c_ref[slot] = coupled(of_s, parts).astype(BF16)
 
     (cc_out,) = call(
@@ -422,98 +455,108 @@
     )
     cc_from_out = outer(cc_out)
 
-    def order_body(nums, *refs):
-        amp_refs, ordered_refs = refs[:roles], refs[-pairs:]
-        role = lax.axis_index("role")
-        for m in range(roles):
-            at = whole(nums[ROLE_PAIR + (role ^ m)])
-            for q, ordered_ref in enumerate(ordered_refs):
-
-                @pl.when(at == q)
-                def _():
-                    ordered_ref[:virt, :] = amp_refs[m][...]
-
-        for ordered_ref in ordered_refs:
-            ordered_ref[virt:, :] = jnp.zeros((riders, virt), BF16)
-
-    ordered = call(
-        order_body,
-        [SMEM] + [VMEM] * roles,
-        [longer] * pairs,
-        (nums, *amp_roles),
-    )
-    ordered_in = [inner(x) for x in ordered]
-
-    def extra_body(nums, coeff_ref, in_ref, after_ref, s_ref, s_in_ref):
+    def inner_again_body(nums, low_ref, s_ref, se_ref, *refs):
+        amp_refs, c_refs = refs[:roles], refs[-2:]
+
         @pl.when(lax.axis_index("role") > 0)
         def _():
-            x = coeff_ref[whole(nums[EXTRA])]
-            overlaps(x, coeff_ref, s_ref)
-            overlaps(x, in_ref, s_in_ref)
-
-    se_own, se_in = call(
-        extra_body,
-        [SMEM, VMEM, VMEM, ANY],
-        [all_s, all_s],
-        (nums, coeff, coeff_in, cc_out),
-    )
-
-    def own_again_body(nums, k_ref, s_ref, s_in_ref, se_ref, se_in_ref, *refs):
-        amp_refs, amp_in_refs, k_refs = refs[:pairs], refs[pairs : 2 * pairs], refs[2 * pairs : -2]
-        role = lax.axis_index("role")
-
-        def rest(pair, k, of_s, of_s_in, at):
-            amp = amp_refs[0][:virt, :]
-            for q in range(1, pairs):
-                amp = jnp.where(pair == q, amp_refs[q][:virt, :], amp)
-            right = k + mxu(k.astype(BF16), amp, NN) * virt_scale
-            total = right + mxu(amp.T, right.astype(BF16), NN) * virt_scale
-            for first, of, of_amps in ((at, of_s, amp_refs), (at + pairs, of_s_in, amp_in_refs)):
-                parts = [(q, nums[first + q], of_amps[q][:virt, :]) for q in range(pairs)]
-                total += coupled(of, parts)
-            return amp.astype(F32) - total
-
-        @pl.when(role > 0)
-        def _():
-            refs[-2][...] = rest(whole(nums[MINE]), k_ref[...], s_ref, s_in_ref, own_weights)
-            k = k_refs[0][:virt, :].astype(F32)
-            for s in range(2, roles):
-                k = jnp.where(role == s, k_refs[s - 1][:virt, :].astype(F32), k)
-            refs[-1][...] = rest(whole(nums[EXTRA]), k, se_ref, se_in_ref, own_weights + 2 * pairs)
+            told = told_of(low_ref)
+            for slot, of_s, c_ref in zip(range(2), (s_ref, se_ref), c_refs):
+                parts = parts_of(nums, told_weight(told, weights + slot * pairs), amp_refs)
+                c_ref[:virt, :] = coupled(of_s, parts).astype(BF16)
+                c_ref[virt:, :] = jnp.zeros((riders, virt), BF16)
+
+    c_in, ce_in = call(
+        inner_again_body,
+        [SMEM] + [VMEM] * (3 + roles) + [ANY],
+        [longer, longer],
+        (nums, low_in, s_in, se_in, *amp_roles, cc_out),
+    )
+    c_from_in = inner(c_in)
+
+    def own_again_body(nums, rest_ref, s_ref, se_ref, *refs):
+        amp_refs, (after_ref, out_ref, out_extra_ref) = refs[:roles], refs[-3:]
+
+        @pl.when(lax.axis_index("role") > 0)
+        def _():
+            parts = parts_of(nums, lambda at: nums[own_weights + at], amp_refs)
+            out_ref[...] = rest_ref[...] - coupled(s_ref, parts)
+            parts = parts_of(nums, lambda at: nums[own_weights + pairs + at], amp_refs)
+            out_extra_ref[...] = -coupled(se_ref, parts)
 
     rest, rest_extra = call(
         own_again_body,
-        [SMEM] + [VMEM] * (5 + 2 * pairs + roles - 1),
+        [SMEM] + [VMEM] * (3 + roles) + [ANY],
         [sq_f, sq_f],
-        (nums, k_first, s_own, s_in, se_own, se_in, *ordered, *ordered_in, *k_extras),
-    )
+        (nums, rest, s_own, se_own, *amp_roles, c_in),
+    )
+
+    def tell_body(last_ref, *refs):
+        refs[-1][...] = last_ref[...]
+
+    (ce_in,) = call(tell_body, [VMEM] + [ANY] * roles, [longer], (ce_in, rest, *rests))
+    ce_from_in = inner(ce_in)
 
     def last_body(
-        nums, coeff_ref, gain_ref, gain_extra_ref, rest_ref, rest_extra_ref, c_ref, amp_ref, orb_ref
+        nums, coeff_ref, gain_ref, gain_extra_ref, rest_ref, rest_extra_ref, co_ref, ci_ref, cei_ref, *refs
     ):
+        rest_refs, (amp_out, orb_out, amp_ref, orb_ref, sems) = refs[: roles - 1], refs[roles - 1 :]
         role = lax.axis_index("role")
-
-        def store(slot, here, gain, rest, pair):
+        copies = []
+
+        def send(source, target):
+            copies.append(pltpu.make_async_copy(source, target, sems.at[len(copies)]))
+            copies[-1].start()
+
+        def store(slot, here, gain, rest, c_in, pair):
             @pl.when(here)
             def _():
-                amp = (gain[...] * (rest[...] - c_ref[slot].astype(F32))).astype(BF16)
-                amp_ref[slot] = amp
-                x = coeff_ref[pair]
-                orb_ref[slot] = (x.astype(F32) + mxu(x, amp, NN) * virt_scale).astype(BF16)
+                total = rest[...] - co_ref[slot].astype(F32) - c_in[:virt, :].astype(F32)
+                for s in range(1, roles):
+                    if slot:
+                        come = rest_refs[s - 1][:virt, :].astype(F32)
+                        total += jnp.where(role == s, come, 0.0)
+                amp_ref[slot] = (gain[...] * total).astype(BF16)
 
             @pl.when(jnp.logical_not(here))
             def _():
                 amp_ref[slot] = jnp.zeros(square, BF16)
-                orb_ref[slot] = jnp.zeros((pao, virt), BF16)
-
-        store(0, role > 0, gain_ref, rest_ref, whole(nums[MINE]))
-        store(1, role == whole(nums[OWNER]), gain_extra_ref, rest_extra_ref, whole(nums[EXTRA]))
+
+            send(amp_ref.at[slot], amp_out.at[slot])
+            for at in range(0, pao, virt):
+                rows = pl.ds(at, virt)
+
+                @pl.when(here)
+                def _():
+                    x = coeff_ref[pair, rows, :]
+                    dressed = x.astype(F32) + mxu(x, amp_ref[slot], NN) * virt_scale
+                    orb_ref[slot, rows, :] = dressed.astype(BF16)
+
+                @pl.when(jnp.logical_not(here))
+                def _():
+                    orb_ref[slot, rows, :] = jnp.zeros((virt, virt), BF16)
+
+                send(orb_ref.at[slot, rows], orb_out.at[slot, rows])
+
+        store(0, role > 0, gain_ref, rest_ref, ci_ref, whole(nums[MINE]))
+        has_extra = role == whole(nums[OWNER])
+        store(1, has_extra, gain_extra_ref, rest_extra_ref, cei_ref, whole(nums[EXTRA]))
+        for copy in copies:
+            copy.wait()
 
     amps_out, dressed_out = call(
         last_body,
-        [SMEM] + [VMEM] * 6,
-        [(VMEM, (slots, virt, virt), BF16), (VMEM, (slots, pao, virt), BF16)],
-        (nums, coeff, gain, gain_extra, rest, rest_extra, cc_from_out),
+        [SMEM] + [VMEM] * (8 + roles - 1),
+        [(ANY, (slots, virt, virt), BF16), (ANY, (slots, pao, virt), BF16)],
+        (
+            nums, coeff, gain, gain_extra, rest, rest_extra,
+            cc_from_out, c_from_in, ce_from_in, *rests,
+        ),
+        scratch=[
+            pltpu.VMEM((slots, virt, virt), BF16),
+            pltpu.VMEM((slots, pao, virt), BF16),
+            pltpu.SemaphoreType.DMA((slots * (1 + pao // virt),)),
+        ],
     )
     return amps_out, dressed_out
 

time: 56.9 us -> 53.8 us (0.946)
  waiting for transfers between devices: 13.5 us -> 10.2 us
  starting transfers between devices: 25.7 us -> 27.6 us
  Pallas kernels: 15.6 us -> 14.2 us
    ppermute x3, waiting for transfers between devices: 4.35 us -> 0.01 us  [swap(): return lax.ppermute(x, 'role', [(i, i ^ by) for i in range(roles)])]
    ppermute x7, starting transfers between devices: 13.1 us -> 16.4 us  [outer(): return lax.ppermute(x, 'pairs', list(enumerate(outer_of)))]
    ppermute x7, waiting for transfers between devices: 7.57 us -> 9.14 us  [outer(): return lax.ppermute(x, 'pairs', list(enumerate(outer_of)))]
    pallas_call x15 -> x16, Pallas kernels: 15.6 us -> 14.2 us  [call(): pl.pallas_call(body, in_specs=ins, out_specs=[spec for spec, _, _ in outs...]
    ppermute x3, waiting for transfers between devices: 1.12 us -> 0.01 us  [local(): rests = [lax.ppermute(rest_b, 'role', [(0, s)]) for s in range(1, roles)]]
    ppermute x7 -> x6, starting transfers between devices: 2.11 us -> 1.66 us  [inner(): return lax.ppermute(x, 'pairs', list(enumerate(inner_of)))]
  transfers between devices with their start and end apart: 20 -> 19, of which waited for: 8 -> 5; matrix products, arithmetic and copies ran while one was open for 0% -> 0% of each run, Pallas kernels for 24% -> 24%
where the time goes in v8:
time: 53.8 us; the launch traced here: 53.6 us
  starting transfers between devices  27.6 us (51%)
  Pallas kernels  14.2 us (26%)
  waiting for transfers between devices  10.2 us (19%)
  between operations  0.91 us (2%)
  local copies, waits for them, and re-layouts  0.7 us (1%)
    ppermute x7, starting transfers between devices, outer(): return lax.ppermute(x, 'pairs', list(enumerate(outer_of)))  16.4 us
    pallas_call x16, Pallas kernels, call(): pl.pallas_call(body, in_specs=ins, out_specs=[spec for spec, _, _ in outs...  14.2 us
    ppermute x7, waiting for transfers between devices, outer(): return lax.ppermute(x, 'pairs', list(enumerate(outer_of)))  9.14 us
    ppermute x3, starting transfers between devices, local(): rests = [lax.ppermute(rest_b, 'role', [(0, s)]) for s in range(1, roles)]  6 us
    ppermute x3, starting transfers between devices, swap(): return lax.ppermute(x, 'role', [(i, i ^ by) for i in range(roles)])  3.55 us
    ppermute x6, starting transfers between devices, inner(): return lax.ppermute(x, 'pairs', list(enumerate(inner_of)))  1.66 us
  transfers between devices with their start and end apart: 19, of which 5 were waited for; matrix products, arithmetic and copies ran while one was open for 0% of the time, Pallas kernels for 24%

profile of v8, /device:TPU:0, one launch (start us, length us, event | category | flops | bytes accessed | tf_op | source)
XLA Modules:
  0.0 53.6 jit_solution(2198389342431202876)
XLA Ops:
  0.6 0.5 collective-permute-start.4
  1.1 0.1 collective-permute-start
  1.2 0.4 collective-permute-start.1
  1.7 2.4 %shard_map.113 = (bf16[528,128]{1,0:T(8,128)(2,1)}, bf16[512,128]{1,0:T(8,128)(2,1)}, f32[30]{0:T(128)}) custom-call(s32[4]{0:T(128)} %owner_hbm.1, s32[2,4]{1,0:T(2,128)} %bitcast.1, s32[4,8]{1,0:T(4,128)} %partner_hbm.1, f32[4,8]{1,0:T(4,128)} %coupling_hbm.1, f32[16]{0:T(128)} %eps_hbm.1, s32[4]{0:T(128)} %nvirt_hbm.1, bf16[4,512,256]{2,1,0:T(8,128)(2,1)} %coeff_ref.11), custom_call_target="tpu_custom_call" | custom-call | flops 1 | bytes 1 | tf_op jit(solution)/shard_map/pallas_call | solution.py:33
  4.1 4.8 %collective-permute-start.2 = (bf16[528,128]{1,0:T(8,128)(2,1)}, bf16[528,128]{1,0:T(8,128)(2,1)S(1)}, u32[]{:S(2)}, u32[]{:S(2)}) collective-permute-start(bf16[528,128]{1,0:T(8,128)(2,1)} %get-tuple-element.26), channel_id=1, source_target_pairs={{0,7},{1,2},{2,1},{3,4},{4,3},{5,6},{6,5},{7,0},{8,15},{9,10},{10,... | collective-permute-start | bytes 405512 | tf_op jit(solution)/shard_map/ppermute | solution.py:73
  8.9 0.1 collective-permute-start.3
  9.0 0.0 copy-start.2
  9.0 0.7 %copy-done.2 = f32[30]{0:T(128)S(1)} copy-done((f32[30]{0:T(128)S(1)}, f32[30]{0:T(128)}, u32[]{:S(2)}) %copy-start.2) | copy-done | bytes 144
  9.6 1.6 %shard_map.114.three_ref = bf16[2,1024,512]{2,1,0:T(8,128)(2,1)S(1)} custom-call(bf16[2,1024,512]{2,1,0:T(8,128)(2,1)} %three_ref.1, f32[30]{0:T(128)S(1)} %copy-done.2), custom_call_target="tpu_custom_call" | custom-call | flops 1 | bytes 1 | tf_op jit(solution)/shard_map/pallas_call | solution.py:33
  11.2 0.0 copy-start
  11.2 0.0 copy-start.1
  11.3 1.3 %collective-permute-done.2.x_ref.low_ref = bf16[528,128]{1,0:T(8,128)(2,1)S(1)} collective-permute-done((bf16[528,128]{1,0:T(8,128)(2,1)}, bf16[528,128]{1,0:T(8,128)(2,1)S(1)}, u32[]{:S(2)}, u32[]{:S(2)}) %collective-permute-start.2) | collective-permute-done | bytes 135200 | tf_op jit(solution)/shard_map/ppermute | solution.py:73
  12.5 0.5 shard_map.115.after_ref
  13.0 3.2 %collective-permute-start.5 = (bf16[1056,128]{1,0:T(8,128)(2,1)S(1)}, bf16[1056,128]{1,0:T(8,128)(2,1)S(1)}, u32[]{:S(2)}, u32[]{:S(2)}) collective-permute-start(bf16[1056,128]{1,0:T(8,128)(2,1)S(1)} %shard_map.115.after_ref), channel_id=1, source_target_pairs={{0,7},{1,2},{2,1},{3,4},{4,3},{5,6},{6,5},{7,0},{8,15},{9,10},{10,... | collective-permute-start | bytes 811016 | tf_op jit(solution)/shard_map/ppermute | solution.py:73
  16.3 0.0 collective-permute-done.3.x_ref.high_ref
  16.3 0.5 shard_map.116.after_ref
  16.8 1.4 %collective-permute-start.6 = (bf16[1040,128]{1,0:T(8,128)(2,1)S(1)}, bf16[1040,128]{1,0:T(8,128)(2,1)S(1)}, u32[]{:S(2)}, u32[]{:S(2)}) collective-permute-start(bf16[1040,128]{1,0:T(8,128)(2,1)S(1)} %shard_map.116.after_ref), channel_id=1, source_target_pairs={{0,7},{1,2},{2,1},{3,4},{4,3},{5,6},{6,5},{7,0},{8,15},{9,10},{10,... | collective-permute-start | bytes 798728 | tf_op jit(solution)/shard_map/ppermute | solution.py:73
  18.2 0.0 copy-done
  18.2 0.0 copy-done.1
  18.2 0.9 %shard_map.117 = (bf16[4,256,256]{2,1,0:T(8,128)(2,1)S(1)}, bf16[304,256]{1,0:T(8,128)(2,1)S(1)}) custom-call(bf16[4,512,256]{2,1,0:T(8,128)(2,1)S(1)} %copy-done, bf16[4,256,256]{2,1,0:T(8,128)(2,1)S(1)} %copy-done.1, bf16[528,128]{1,0:T(8,128)(2,1)S(1)} %collective-permute-done.2.x_ref.low_ref, bf16[512,128]{1,0:T(8,128)(2,1)S(1)} %collective-permute-done.3.x_ref.high_ref, ...), custom_call_target="tpu_custom_call" | custom-call | flops 1 | bytes 1 | tf_op jit(solution)/shard_map/pallas_call | solution.py:33
  19.2 0.0 collective-permute-done.4.three_in_ref
  19.2 0.0 copy-start.4
  19.2 0.0 copy-start.5
  19.2 0.0 copy-start.3
  19.2 2.2 %collective-permute-start.7 = (bf16[304,256]{1,0:T(8,128)(2,1)S(1)}, bf16[304,256]{1,0:T(8,128)(2,1)S(1)}, u32[]{:S(2)}, u32[]{:S(2)}) collective-permute-start(bf16[304,256]{1,0:T(8,128)(2,1)S(1)} %get-tuple-element.28.after_ref), channel_id=1, source_target_pairs={{0,7},{1,2},{2,1},{3,4},{4,3},{5,6},{6,5},{7,0},{8,15},{9,10},{10,... | collective-permute-start | bytes 466952 | tf_op jit(solution)/shard_map/ppermute | solution.py:73
  21.4 0.0 copy-done.4
  21.4 1.0 %shard_map.119 = (bf16[256,1024]{1,0:T(8,128)(2,1)S(1)}, bf16[1024,256]{1,0:T(8,128)(2,1)S(1)}, bf16[544,256]{1,0:T(8,128)(2,1)S(1)}) custom-call(f32[30]{0:T(128)S(1)} %copy-done.2, bf16[2,1024,512]{2,1,0:T(8,128)(2,1)S(1)} %shard_map.114.three_ref, bf16[2,1024,512]{2,1,0:T(8,128)(2,1)} %copy-done.4, bf16[4,512,256]{2,1,0:T(8,128)(2,1)S(1)} %copy-done, ...), custom_call_target="tpu_custom_call" | custom-call | flops 1 | bytes 1 | tf_op jit(solution)/shard_map/pallas_call | solution.py:33
  22.5 0.0 collective-permute-done.1.amps_in_ref
  22.5 2.7 %collective-permute-start.12 = (bf16[544,256]{1,0:T(8,128)(2,1)S(1)}, bf16[544,256]{1,0:T(8,128)(2,1)S(1)}, u32[]{:S(2)}, u32[]{:S(2)}) collective-permute-start(bf16[544,256]{1,0:T(8,128)(2,1)S(1)} %get-tuple-element.42), channel_id=1, source_target_pairs={{0,7},{1,2},{2,1},{3,4},{4,3},{5,6},{6,5},{7,0},{8,15},{9,10},{10,... | collective-permute-start | bytes 835592 | tf_op jit(solution)/shard_map/ppermute | solution.py:73
  25.2 0.0 collective-permute-done.coeff_in_ref.in_ref
  25.2 0.0 copy-done.5
  25.2 0.0 collective-permute-start.8
  25.2 0.0 copy-done.3
  25.2 2.0 %shard_map.118 = (bf16[4,256,256]{2,1,0:T(8,128)(2,1)S(1)}, f32[256,256]{1,0:T(8,128)S(1)}, f32[256,256]{1,0:T(8,128)S(1)}, f32[256,256]{1,0:T(8,128)S(1)}) custom-call(f32[30]{0:T(128)S(1)} %copy-done.2, bf16[4,512,256]{2,1,0:T(8,128)(2,1)S(1)} %copy-done, bf16[4,512,256]{2,1,0:T(8,128)(2,1)S(1)} %collective-permute-done.coeff_in_ref.in_ref, ...), custom_call_target="tpu_custom_call" | custom-call | flops 1 | bytes 1 | tf_op jit(solution)/shard_map/pallas_call | solution.py:33
  27.2 0.0 collective-permute-done.8.low_ref
  27.2 0.6 %shard_map.120 = (bf16[4,256,256]{2,1,0:T(8,128)(2,1)S(1)}, bf16[4,256,256]{2,1,0:T(8,128)(2,1)S(1)}, bf16[4,256,256]{2,1,0:T(8,128)(2,1)S(1)}) custom-call(f32[30]{0:T(128)S(1)} %copy-done.2, bf16[4,512,256]{2,1,0:T(8,128)(2,1)S(1)} %copy-done, bf16[4,512,256]{2,1,0:T(8,128)(2,1)S(1)} %collective-permute-done.coeff_in_ref.in_ref, ...), custom_call_target="tpu_custom_call" | custom-call | flops 1 | bytes 1 | tf_op jit(solution)/shard_map/pallas_call | solution.py:33
  27.8 4.9 %collective-permute-done.7.co_ref = bf16[304,256]{1,0:T(8,128)(2,1)S(1)} collective-permute-done((bf16[304,256]{1,0:T(8,128)(2,1)S(1)}, bf16[304,256]{1,0:T(8,128)(2,1)S(1)}, u32[]{:S(2)}, u32[]{:S(2)}) %collective-permute-start.7) | collective-permute-done | bytes 155680 | tf_op jit(solution)/shard_map/ppermute | solution.py:73
  32.7 0.0 collective-permute-done.6.high_ref
  32.7 0.0 collective-permute-done.5.low_ref
  32.7 1.1 %shard_map.121 = (bf16[256,256]{1,0:T(8,128)(2,1)S(1)}, f32[256,256]{1,0:T(8,128)S(1)}) custom-call(f32[30]{0:T(128)S(1)} %copy-done.2, bf16[256,1024]{1,0:T(8,128)(2,1)S(1)} %get-tuple-element.31.first_ref, bf16[1024,256]{1,0:T(8,128)(2,1)S(1)} %get-tuple-element.32.second_ref, bf16[1056,128]{1,0:T(8,128)(2,1)S(1)} %collective-permute-done.5.low_ref, ...), custom_call_target="tpu_custom_call" | custom-call | flops 1 | bytes 1 | tf_op jit(solution)/shard_map/pallas_call | solution.py:33
  33.8 1.6 %collective-permute-start.9 = (bf16[256,256]{1,0:T(8,128)(2,1)S(1)}, bf16[256,256]{1,0:T(8,128)(2,1)S(1)}, u32[]{:S(2)}, u32[]{:S(2)}) collective-permute-start(bf16[256,256]{1,0:T(8,128)(2,1)S(1)} %get-tuple-element.35.amp_ref.after_ref.refs_0_), channel_id=1, source_target_pairs={{0,8},{8,0},{16,24},{24,16},{1,9},{9,1},{17,25},{25,17},{2,10},{10... | collective-permute-start | bytes 393224 | tf_op jit(solution)/shard_map/ppermute | solution.py:76
  35.4 1.4 %collective-permute-start.10 = (bf16[256,256]{1,0:T(8,128)(2,1)S(1)}, bf16[256,256]{1,0:T(8,128)(2,1)S(1)}, u32[]{:S(2)}, u32[]{:S(2)}) collective-permute-start(bf16[256,256]{1,0:T(8,128)(2,1)S(1)} %get-tuple-element.35.amp_ref.after_ref.refs_0_), channel_id=1, source_target_pairs={{0,16},{8,24},{16,0},{24,8},{1,17},{9,25},{17,1},{25,9},{2,18},{10... | collective-permute-start | bytes 393224 | tf_op jit(solution)/shard_map/ppermute | solution.py:76
  36.7 0.6 %collective-permute-start.11 = (bf16[256,256]{1,0:T(8,128)(2,1)S(1)}, bf16[256,256]{1,0:T(8,128)(2,1)S(1)}, u32[]{:S(2)}, u32[]{:S(2)}) collective-permute-start(bf16[256,256]{1,0:T(8,128)(2,1)S(1)} %get-tuple-element.35.amp_ref.after_ref.refs_0_), channel_id=1, source_target_pairs={{0,24},{8,16},{16,8},{24,0},{1,25},{9,17},{17,9},{25,1},{2,26},{10... | collective-permute-start | bytes 393224 | tf_op jit(solution)/shard_map/ppermute | solution.py:76
  37.4 0.4 shard_map.122
  37.8 3.4 %collective-permute-start.15 = (bf16[272,256]{1,0:T(8,128)(2,1)S(1)}, bf16[272,256]{1,0:T(8,128)(2,1)S(1)}, u32[]{:S(2)}, u32[]{:S(2)}) collective-permute-start(bf16[272,256]{1,0:T(8,128)(2,1)S(1)} %get-tuple-element.47), channel_id=1, source_target_pairs={{0,8},{1,9},{2,10},{3,11},{4,12},{5,13},{6,14},{7,15}} | collective-permute-start | bytes 417800 | tf_op jit(solution)/shard_map/ppermute | solution.py:415
  41.2 0.0 collective-permute-done.9.refs_1_
  41.2 1.3 %collective-permute-start.16 = (bf16[272,256]{1,0:T(8,128)(2,1)S(1)}, bf16[272,256]{1,0:T(8,128)(2,1)S(1)}, u32[]{:S(2)}, u32[]{:S(2)}) collective-permute-start(bf16[272,256]{1,0:T(8,128)(2,1)S(1)} %get-tuple-element.47), channel_id=1, source_target_pairs={{0,16},{1,17},{2,18},{3,19},{4,20},{5,21},{6,22},{7,23}} | collective-permute-start | bytes 417800 | tf_op jit(solution)/shard_map/ppermute | solution.py:415
  42.5 0.0 collective-permute-done.12.x_ref
  42.5 1.3 %collective-permute-start.17 = (bf16[272,256]{1,0:T(8,128)(2,1)S(1)}, bf16[272,256]{1,0:T(8,128)(2,1)S(1)}, u32[]{:S(2)}, u32[]{:S(2)}) collective-permute-start(bf16[272,256]{1,0:T(8,128)(2,1)S(1)} %get-tuple-element.47), channel_id=1, source_target_pairs={{0,24},{1,25},{2,26},{3,27},{4,28},{5,29},{6,30},{7,31}} | collective-permute-start | bytes 417800 | tf_op jit(solution)/shard_map/ppermute | solution.py:415
  43.8 0.0 collective-permute-done.10.refs_2_
  43.8 0.0 collective-permute-done.11.refs_3_
  43.9 0.6 %shard_map.124.refs_4_ = bf16[2,256,256]{2,1,0:T(8,128)(2,1)S(1)} custom-call(f32[30]{0:T(128)S(1)} %copy-done.2, bf16[528,128]{1,0:T(8,128)(2,1)S(1)} %collective-permute-done.2.x_ref.low_ref, bf16[4,256,256]{2,1,0:T(8,128)(2,1)S(1)} %get-tuple-element.41.s_ref, bf16[4,256,256]{2,1,0:T(8,128)(2,1)S(1)} %shard_map.123.se_ref, ...), custom_call_target="tpu_custom_call" | custom-call | flops 1 | bytes 1 | tf_op jit(solution)/shard_map/pallas_call | solution.py:33
  44.4 1.9 %collective-permute-start.13 = (bf16[2,256,256]{2,1,0:T(8,128)(2,1)S(1)}, bf16[2,256,256]{2,1,0:T(8,128)(2,1)S(1)}, u32[]{:S(2)}, u32[]{:S(2)}) collective-permute-start(bf16[2,256,256]{2,1,0:T(8,128)(2,1)S(1)} %shard_map.124.refs_4_), channel_id=1, source_target_pairs={{0,7},{1,2},{2,1},{3,4},{4,3},{5,6},{6,5},{7,0},{8,15},{9,10},{10,... | collective-permute-start | bytes 786440 | tf_op jit(solution)/shard_map/ppermute | solution.py:73
  46.3 0.6 %shard_map.125 = (bf16[272,256]{1,0:T(8,128)(2,1)S(1)}, bf16[272,256]{1,0:T(8,128)(2,1)S(1)}) custom-call(f32[30]{0:T(128)S(1)} %copy-done.2, bf16[528,128]{1,0:T(8,128)(2,1)S(1)} %collective-permute-done.8.low_ref, bf16[4,256,256]{2,1,0:T(8,128)(2,1)S(1)} %get-tuple-element.39.s_ref, bf16[4,256,256]{2,1,0:T(8,128)(2,1)S(1)} %get-tuple-element.40.se_ref, ...), custom_call_target="tpu_custom_call" | custom-call | flops 1 | bytes 1 | tf_op jit(solution)/shard_map/pallas_call | solution.py:33
  46.9 0.1 collective-permute-start.14
  47.0 0.6 %shard_map.126 = (f32[256,256]{1,0:T(8,128)S(1)}, f32[256,256]{1,0:T(8,128)S(1)}) custom-call(f32[30]{0:T(128)S(1)} %copy-done.2, f32[256,256]{1,0:T(8,128)S(1)} %get-tuple-element.37.rest_ref, bf16[4,256,256]{2,1,0:T(8,128)(2,1)S(1)} %get-tuple-element.38.s_ref, bf16[4,256,256]{2,1,0:T(8,128)(2,1)S(1)} %get-tuple-element.34.after_ref.se_ref, ...), custom_call_target="tpu_custom_call" | custom-call | flops 1 | bytes 1 | tf_op jit(solution)/shard_map/pallas_call | solution.py:33
  47.5 0.0 collective-permute-done.15.refs_1_.refs_0_
  47.5 0.0 collective-permute-done.16.refs_2_.refs_1_
  47.6 0.0 collective-permute-done.17.refs_3_.refs_2_
  47.6 0.6 %collective-permute-start.18 = (bf16[272,256]{1,0:T(8,128)(2,1)S(1)}, bf16[272,256]{1,0:T(8,128)(2,1)S(1)}, u32[]{:S(2)}, u32[]{:S(2)}) collective-permute-start(bf16[272,256]{1,0:T(8,128)(2,1)S(1)} %shard_map.127), channel_id=1, source_target_pairs={{0,1},{1,0},{2,3},{3,2},{4,5},{5,4},{6,7},{7,6},{8,9},{9,8},{10,11... | collective-permute-start | bytes 417800 | tf_op jit(solution)/shard_map/ppermute | solution.py:70
  48.1 0.2 collective-permute-done.14.ci_ref
  48.3 0.8 %collective-permute-done.18.cei_ref = bf16[272,256]{1,0:T(8,128)(2,1)S(1)} collective-permute-done((bf16[272,256]{1,0:T(8,128)(2,1)S(1)}, bf16[272,256]{1,0:T(8,128)(2,1)S(1)}, u32[]{:S(2)}, u32[]{:S(2)}) %collective-permute-start.18) | collective-permute-done | bytes 139296 | tf_op jit(solution)/shard_map/ppermute | solution.py:70
  49.1 2.9 %collective-permute-done.13.co_ref = bf16[2,256,256]{2,1,0:T(8,128)(2,1)S(1)} collective-permute-done((bf16[2,256,256]{2,1,0:T(8,128)(2,1)S(1)}, bf16[2,256,256]{2,1,0:T(8,128)(2,1)S(1)}, u32[]{:S(2)}, u32[]{:S(2)}) %collective-permute-start.13) | collective-permute-done | bytes 262176 | tf_op jit(solution)/shard_map/ppermute | solution.py:73
  52.1 1.5 %shard_map.128 = (bf16[2,256,256]{2,1,0:T(8,128)(2,1)}, bf16[2,512,256]{2,1,0:T(8,128)(2,1)}) custom-call(f32[30]{0:T(128)S(1)} %copy-done.2, bf16[4,512,256]{2,1,0:T(8,128)(2,1)S(1)} %copy-done, f32[256,256]{1,0:T(8,128)S(1)} %get-tuple-element.29.gain_ref, f32[256,256]{1,0:T(8,128)S(1)} %get-tuple-element.30.gain_extra_ref, ...), custom_call_target="tpu_custom_call" | custom-call | flops 1 | bytes 1 | tf_op jit(solution)/shard_map/pallas_call | solution.py:33
  (2 shorter events, 0.0 us)
Async XLA Ops:
  0.6 18.5 %collective-permute-start.4 = (bf16[2,1024,512]{2,1,0:T(8,128)(2,1)}, bf16[2,1024,512]{2,1,0:T(8,128)(2,1)S(1)}, u32[]{:S(2)}, u32[]{:S(2)}) collective-permute-start(bf16[2,1024,512]{2,1,0:T(8,128)(2,1)} %three_ref.1), channel_id=1, source_target_pairs={{0,1},{1,0},{2,3},{3,2},{4,5},{5,4},{6,7},{7,6},{8,9},{9,8},{10,11... | collective-permute-start | bytes 6291464 | tf_op jit(solution)/shard_map/ppermute | solution.py:70
  1.1 24.1 %collective-permute-start = (bf16[4,512,256]{2,1,0:T(8,128)(2,1)}, bf16[4,512,256]{2,1,0:T(8,128)(2,1)S(1)}, u32[]{:S(2)}, u32[]{:S(2)}) collective-permute-start(bf16[4,512,256]{2,1,0:T(8,128)(2,1)} %coeff_ref.11), channel_id=1, source_target_pairs={{0,1},{1,0},{2,3},{3,2},{4,5},{5,4},{6,7},{7,6},{8,9},{9,8},{10,11... | collective-permute-start | bytes 3145736 | tf_op jit(solution)/shard_map/ppermute | solution.py:70
  1.2 21.2 %collective-permute-start.1 = (bf16[4,256,256]{2,1,0:T(8,128)(2,1)}, bf16[4,256,256]{2,1,0:T(8,128)(2,1)S(1)}, u32[]{:S(2)}, u32[]{:S(2)}) collective-permute-start(bf16[4,256,256]{2,1,0:T(8,128)(2,1)} %amps_ref.5), channel_id=1, source_target_pairs={{0,1},{1,0},{2,3},{3,2},{4,5},{5,4},{6,7},{7,6},{8,9},{9,8},{10,11... | collective-permute-start | bytes 1572872 | tf_op jit(solution)/shard_map/ppermute | solution.py:70
  4.1 8.4 %collective-permute-start.2 = (bf16[528,128]{1,0:T(8,128)(2,1)}, bf16[528,128]{1,0:T(8,128)(2,1)S(1)}, u32[]{:S(2)}, u32[]{:S(2)}) collective-permute-start(bf16[528,128]{1,0:T(8,128)(2,1)} %get-tuple-element.26), channel_id=1, source_target_pairs={{0,7},{1,2},{2,1},{3,4},{4,3},{5,6},{6,5},{7,0},{8,15},{9,10},{10,... | collective-permute-start | bytes 405512 | tf_op jit(solution)/shard_map/ppermute | solution.py:73
  8.9 7.4 %collective-permute-start.3 = (bf16[512,128]{1,0:T(8,128)(2,1)}, bf16[512,128]{1,0:T(8,128)(2,1)S(1)}, u32[]{:S(2)}, u32[]{:S(2)}) collective-permute-start(bf16[512,128]{1,0:T(8,128)(2,1)} %get-tuple-element.27), channel_id=1, source_target_pairs={{0,7},{1,2},{2,1},{3,4},{4,3},{5,6},{6,5},{7,0},{8,15},{9,10},{10,... | collective-permute-start | bytes 393224 | tf_op jit(solution)/shard_map/ppermute | solution.py:73
  9.0 0.7 %copy-start.2 = (f32[30]{0:T(128)S(1)}, f32[30]{0:T(128)}, u32[]{:S(2)}) copy-start(f32[30]{0:T(128)} %get-tuple-element.25.after_ref.nums) | copy-start | bytes 364
  11.2 7.0 %copy-start = (bf16[4,512,256]{2,1,0:T(8,128)(2,1)S(1)}, bf16[4,512,256]{2,1,0:T(8,128)(2,1)}, u32[]{:S(2)}) copy-start(bf16[4,512,256]{2,1,0:T(8,128)(2,1)} %coeff_ref.11) | copy-start | bytes 3145732
  11.2 7.0 %copy-start.1 = (bf16[4,256,256]{2,1,0:T(8,128)(2,1)S(1)}, bf16[4,256,256]{2,1,0:T(8,128)(2,1)}, u32[]{:S(2)}) copy-start(bf16[4,256,256]{2,1,0:T(8,128)(2,1)} %amps_ref.5) | copy-start | bytes 1572868
  13.0 19.7 %collective-permute-start.5 = (bf16[1056,128]{1,0:T(8,128)(2,1)S(1)}, bf16[1056,128]{1,0:T(8,128)(2,1)S(1)}, u32[]{:S(2)}, u32[]{:S(2)}) collective-permute-start(bf16[1056,128]{1,0:T(8,128)(2,1)S(1)} %shard_map.115.after_ref), channel_id=1, source_target_pairs={{0,7},{1,2},{2,1},{3,4},{4,3},{5,6},{6,5},{7,0},{8,15},{9,10},{10,... | collective-permute-start | bytes 811016 | tf_op jit(solution)/shard_map/ppermute | solution.py:73
  16.8 15.9 %collective-permute-start.6 = (bf16[1040,128]{1,0:T(8,128)(2,1)S(1)}, bf16[1040,128]{1,0:T(8,128)(2,1)S(1)}, u32[]{:S(2)}, u32[]{:S(2)}) collective-permute-start(bf16[1040,128]{1,0:T(8,128)(2,1)S(1)} %shard_map.116.after_ref), channel_id=1, source_target_pairs={{0,7},{1,2},{2,1},{3,4},{4,3},{5,6},{6,5},{7,0},{8,15},{9,10},{10,... | collective-permute-start | bytes 798728 | tf_op jit(solution)/shard_map/ppermute | solution.py:73
  19.2 2.3 %copy-start.4 = (bf16[2,1024,512]{2,1,0:T(8,128)(2,1)}, bf16[2,1024,512]{2,1,0:T(8,128)(2,1)S(1)}, u32[]{:S(2)}) copy-start(bf16[2,1024,512]{2,1,0:T(8,128)(2,1)S(1)} %collective-permute-done.4.three_in_ref) | copy-start | bytes 6291460
  19.2 6.0 %copy-start.5 = (bf16[528,128]{1,0:T(8,128)(2,1)S(1)}, bf16[528,128]{1,0:T(8,128)(2,1)}, u32[]{:S(2)}) copy-start(bf16[528,128]{1,0:T(8,128)(2,1)} %get-tuple-element.26) | copy-start | bytes 405508
  19.2 6.0 %copy-start.3 = (f32[4,256]{1,0:T(4,128)S(1)}, f32[4,256]{1,0:T(4,128)}, u32[]{:S(2)}) copy-start(f32[4,256]{1,0:T(4,128)} %eps_ref.1) | copy-start | bytes 12292
  19.2 13.5 %collective-permute-start.7 = (bf16[304,256]{1,0:T(8,128)(2,1)S(1)}, bf16[304,256]{1,0:T(8,128)(2,1)S(1)}, u32[]{:S(2)}, u32[]{:S(2)}) collective-permute-start(bf16[304,256]{1,0:T(8,128)(2,1)S(1)} %get-tuple-element.28.after_ref), channel_id=1, source_target_pairs={{0,7},{1,2},{2,1},{3,4},{4,3},{5,6},{6,5},{7,0},{8,15},{9,10},{10,... | collective-permute-start | bytes 466952 | tf_op jit(solution)/shard_map/ppermute | solution.py:73
  22.5 20.0 %collective-permute-start.12 = (bf16[544,256]{1,0:T(8,128)(2,1)S(1)}, bf16[544,256]{1,0:T(8,128)(2,1)S(1)}, u32[]{:S(2)}, u32[]{:S(2)}) collective-permute-start(bf16[544,256]{1,0:T(8,128)(2,1)S(1)} %get-tuple-element.42), channel_id=1, source_target_pairs={{0,7},{1,2},{2,1},{3,4},{4,3},{5,6},{6,5},{7,0},{8,15},{9,10},{10,... | collective-permute-start | bytes 835592 | tf_op jit(solution)/shard_map/ppermute | solution.py:73
  25.2 2.0 %collective-permute-start.8 = (bf16[528,128]{1,0:T(8,128)(2,1)S(1)}, bf16[528,128]{1,0:T(8,128)(2,1)S(1)}, u32[]{:S(2)}, u32[]{:S(2)}) collective-permute-start(bf16[528,128]{1,0:T(8,128)(2,1)S(1)} %copy-done.5), channel_id=1, source_target_pairs={{0,1},{1,0},{2,3},{3,2},{4,5},{5,4},{6,7},{7,6},{8,9},{9,8},{10,11... | collective-permute-start | bytes 405512 | tf_op jit(solution)/shard_map/ppermute | solution.py:70
  33.8 7.4 %collective-permute-start.9 = (bf16[256,256]{1,0:T(8,128)(2,1)S(1)}, bf16[256,256]{1,0:T(8,128)(2,1)S(1)}, u32[]{:S(2)}, u32[]{:S(2)}) collective-permute-start(bf16[256,256]{1,0:T(8,128)(2,1)S(1)} %get-tuple-element.35.amp_ref.after_ref.refs_0_), channel_id=1, source_target_pairs={{0,8},{8,0},{16,24},{24,16},{1,9},{9,1},{17,25},{25,17},{2,10},{10... | collective-permute-start | bytes 393224 | tf_op jit(solution)/shard_map/ppermute | solution.py:76
  35.4 8.5 %collective-permute-start.10 = (bf16[256,256]{1,0:T(8,128)(2,1)S(1)}, bf16[256,256]{1,0:T(8,128)(2,1)S(1)}, u32[]{:S(2)}, u32[]{:S(2)}) collective-permute-start(bf16[256,256]{1,0:T(8,128)(2,1)S(1)} %get-tuple-element.35.amp_ref.after_ref.refs_0_), channel_id=1, source_target_pairs={{0,16},{8,24},{16,0},{24,8},{1,17},{9,25},{17,1},{25,9},{2,18},{10... | collective-permute-start | bytes 393224 | tf_op jit(solution)/shard_map/ppermute | solution.py:76
  36.7 7.1 %collective-permute-start.11 = (bf16[256,256]{1,0:T(8,128)(2,1)S(1)}, bf16[256,256]{1,0:T(8,128)(2,1)S(1)}, u32[]{:S(2)}, u32[]{:S(2)}) collective-permute-start(bf16[256,256]{1,0:T(8,128)(2,1)S(1)} %get-tuple-element.35.amp_ref.after_ref.refs_0_), channel_id=1, source_target_pairs={{0,24},{8,16},{16,8},{24,0},{1,25},{9,17},{17,9},{25,1},{2,26},{10... | collective-permute-start | bytes 393224 | tf_op jit(solution)/shard_map/ppermute | solution.py:76
  37.8 9.8 %collective-permute-start.15 = (bf16[272,256]{1,0:T(8,128)(2,1)S(1)}, bf16[272,256]{1,0:T(8,128)(2,1)S(1)}, u32[]{:S(2)}, u32[]{:S(2)}) collective-permute-start(bf16[272,256]{1,0:T(8,128)(2,1)S(1)} %get-tuple-element.47), channel_id=1, source_target_pairs={{0,8},{1,9},{2,10},{3,11},{4,12},{5,13},{6,14},{7,15}} | collective-permute-start | bytes 417800 | tf_op jit(solution)/shard_map/ppermute | solution.py:415
  41.2 6.4 %collective-permute-start.16 = (bf16[272,256]{1,0:T(8,128)(2,1)S(1)}, bf16[272,256]{1,0:T(8,128)(2,1)S(1)}, u32[]{:S(2)}, u32[]{:S(2)}) collective-permute-start(bf16[272,256]{1,0:T(8,128)(2,1)S(1)} %get-tuple-element.47), channel_id=1, source_target_pairs={{0,16},{1,17},{2,18},{3,19},{4,20},{5,21},{6,22},{7,23}} | collective-permute-start | bytes 417800 | tf_op jit(solution)/shard_map/ppermute | solution.py:415
  42.5 5.1 %collective-permute-start.17 = (bf16[272,256]{1,0:T(8,128)(2,1)S(1)}, bf16[272,256]{1,0:T(8,128)(2,1)S(1)}, u32[]{:S(2)}, u32[]{:S(2)}) collective-permute-start(bf16[272,256]{1,0:T(8,128)(2,1)S(1)} %get-tuple-element.47), channel_id=1, source_target_pairs={{0,24},{1,25},{2,26},{3,27},{4,28},{5,29},{6,30},{7,31}} | collective-permute-start | bytes 417800 | tf_op jit(solution)/shard_map/ppermute | solution.py:415
  44.4 7.7 %collective-permute-start.13 = (bf16[2,256,256]{2,1,0:T(8,128)(2,1)S(1)}, bf16[2,256,256]{2,1,0:T(8,128)(2,1)S(1)}, u32[]{:S(2)}, u32[]{:S(2)}) collective-permute-start(bf16[2,256,256]{2,1,0:T(8,128)(2,1)S(1)} %shard_map.124.refs_4_), channel_id=1, source_target_pairs={{0,7},{1,2},{2,1},{3,4},{4,3},{5,6},{6,5},{7,0},{8,15},{9,10},{10,... | collective-permute-start | bytes 786440 | tf_op jit(solution)/shard_map/ppermute | solution.py:73
  46.9 1.4 %collective-permute-start.14 = (bf16[272,256]{1,0:T(8,128)(2,1)S(1)}, bf16[272,256]{1,0:T(8,128)(2,1)S(1)}, u32[]{:S(2)}, u32[]{:S(2)}) collective-permute-start(bf16[272,256]{1,0:T(8,128)(2,1)S(1)} %get-tuple-element.43.refs_4_), channel_id=1, source_target_pairs={{0,1},{1,0},{2,3},{3,2},{4,5},{5,4},{6,7},{7,6},{8,9},{9,8},{10,11... | collective-permute-start | bytes 417800 | tf_op jit(solution)/shard_map/ppermute | solution.py:70
  47.6 1.6 %collective-permute-start.18 = (bf16[272,256]{1,0:T(8,128)(2,1)S(1)}, bf16[272,256]{1,0:T(8,128)(2,1)S(1)}, u32[]{:S(2)}, u32[]{:S(2)}) collective-permute-start(bf16[272,256]{1,0:T(8,128)(2,1)S(1)} %shard_map.127), channel_id=1, source_target_pairs={{0,1},{1,0},{2,3},{3,2},{4,5},{5,4},{6,7},{7,6},{8,9},{9,8},{10,11... | collective-permute-start | bytes 417800 | tf_op jit(solution)/shard_map/ppermute | solution.py:70

commit v9 on v8

--- a/solution.py
+++ b/solution.py
@@ -50,13 +50,14 @@
     pairs, _, virt = coeff.shape
     partner_count = partners.shape[1]
     slots = 2
-    assert roles == pairs and pairs % 2 == 0 and columns % 2 == 0 and virt % 2 == 0
+    assert roles == pairs and pairs % 2 == 0 and columns % 2 == 0 and virt % 2 == 0 and pao % roles == 0 and roles == 4
     tile = min(256, aux)
     pao_scale = 1.0 / math.sqrt(pao)
     aux_scale = 1.0 / math.sqrt(aux)
     virt_scale = 1.0 / math.sqrt(virt)
     square = (virt, virt)
     part = virt // 2
+    quarter = pao // roles
     sq_b = (VMEM, square, BF16)
     sq_f = (VMEM, square, F32)
     two_b = (VMEM, (2, virt, virt), BF16)
@@ -102,8 +103,9 @@
 
     def plan_body(
         owner_hbm, occ_hbm, partner_hbm, coupling_hbm, eps_hbm, nvirt_hbm, coeff_hbm,
-        low_ref, high_ref, nums,
-        owner_ref, occ_ref, partner_ref, coupling_ref, eps_ref, nvirt_ref, near_w, sems,
+        low_out, high_out, nums,
+        owner_ref, occ_ref, partner_ref, coupling_ref, eps_ref, nvirt_ref, near_w,
+        lows_ref, high_ref, quarter_ref, told_ref, sems,
     ):
         small = [
             pltpu.make_async_copy(source, target, sems.at[at])
@@ -118,7 +120,8 @@
                 )
             )
         ]
-        for copy in small:
+        lows = pltpu.make_async_copy(coeff_hbm.at[:, :, pl.ds(0, part)], lows_ref, sems.at[6])
+        for copy in (*small, lows):
             copy.start()
         role = lax.axis_index("role")
         column = lax.axis_index("pairs")
@@ -126,12 +129,24 @@
         of_role = pairs_of_roles(owner_ref)
         extra = of_role[0]
         mine = pick(of_role, role)
+        rows = pl.ds(pl.multiple_of(role * quarter, quarter), quarter)
         large = [
-            pltpu.make_async_copy(coeff_hbm.at[mine, :, pl.ds(0, part)], low_ref.at[pl.ds(0, pao)], sems.at[6]),
-            pltpu.make_async_copy(coeff_hbm.at[mine, :, pl.ds(part, part)], high_ref, sems.at[7]),
+            pltpu.make_async_copy(coeff_hbm.at[mine, :, pl.ds(part, part)], high_ref, sems.at[7])
         ]
+        for half in range(2):
+            source = coeff_hbm.at[extra, rows, pl.ds(half * part, part)]
+            target = quarter_ref.at[pl.ds(half * quarter, quarter)]
+            large.append(pltpu.make_async_copy(source, target, sems.at[8 + half]))
         for copy in large:
             copy.start()
+        lows.wait()
+        leaving = [
+            pltpu.make_async_copy(lows_ref.at[mine], low_out.at[pl.ds(0, pao)], sems.at[10]),
+            pltpu.make_async_copy(told_ref, low_out.at[pl.ds(pao, riders)], sems.at[11]),
+            pltpu.make_async_copy(high_ref, high_out, sems.at[12]),
+            pltpu.make_async_copy(quarter_ref, low_out.at[pl.ds(pao + riders, 2 * quarter)], sems.at[13]),
+        ]
+        leaving[0].start()
         for copy in small[1:]:
             copy.wait()
         nums[MINE] = mine.astype(F32)
@@ -175,15 +190,23 @@
         middle = (told - coarse).astype(BF16).astype(F32)
         fine = told - coarse - middle
         told = jnp.where(row == 0, coarse, jnp.where(row == 1, middle, jnp.where(row == 2, fine, 0.0)))
-        low_ref[pao:, :] = told.astype(BF16)
+        told_ref[...] = told.astype(BF16)
+        leaving[1].start()
         for copy in large:
             copy.wait()
-
-    rode = (VMEM, (pao + riders, part), BF16)
+        for copy in leaving[2:]:
+            copy.start()
+        for copy in leaving:
+            copy.wait()
+
     x_low, x_high, nums = call(
         plan_body,
         [HBM] * 7,
-        [rode, (VMEM, (pao, part), BF16), (SMEM, (own_weights + 2 * weights,), F32)],
+        [
+            (ANY, (pao + riders + 2 * quarter, part), BF16),
+            (ANY, (pao, part), BF16),
+            (SMEM, (own_weights + 2 * weights,), F32),
+        ],
         (pair_owner, pair_occ.T, partners, coupling, eps_occ, nvirt, coeff),
         scratch=[
             pltpu.SMEM(pair_owner.shape, I32),
@@ -193,14 +216,18 @@
             pltpu.SMEM(eps_occ.shape, F32),
             pltpu.SMEM(nvirt.shape, I32),
             pltpu.SMEM((3 * pairs,), F32),
-            pltpu.SemaphoreType.DMA((8,)),
+            pltpu.VMEM((pairs, pao, part), BF16),
+            pltpu.VMEM((pao, part), BF16),
+            pltpu.VMEM((2 * quarter, part), BF16),
+            pltpu.VMEM((riders, part), BF16),
+            pltpu.SemaphoreType.DMA((14,)),
         ],
-        vmem=60,
+        vmem=61,
     )
     low_out, high_out, low_in = outer(x_low), outer(x_high), inner(x_low)
 
     def told_of(low_ref):
-        rows = low_ref[pao:, :].astype(F32)
+        rows = low_ref[pao : pao + riders, :].astype(F32)
         return rows[0:1] + rows[1:2] + rows[2:3]
 
     def overlaps(x, coeff_ref, out_ref):
@@ -224,40 +251,42 @@
         for rows in tiles:
             y_ref[rows, :] = (mxu(three_ref[at_occ, rows, :], x, NN) * pao_scale).astype(BF16)
 
-    def fetch_body(three_ref, after_ref, held_ref, sem):
+    def fetch_body(three_ref, *refs):
+        held_ref, sem = refs[-2:]
         copy = pltpu.make_async_copy(three_ref, held_ref, sem)
         copy.start()
         copy.wait()
 
     (blocks,) = call(
         fetch_body,
-        [ANY, ANY],
+        [ANY] * 4,
         [(VMEM, three_index.shape, BF16)],
-        (three_index, nums),
+        (three_index, nums, coeff_in, amps_in),
         scratch=[pltpu.SemaphoreType.DMA],
         vmem=50,
     )
 
-    def outer_low_body(three_ref, x_ref, y_ref):
+    def outer_low_body(three_ref, x_ref, after_ref, y_ref):
         half_into(y_ref, three_ref, whole(told_of(x_ref)[0, place_at]), x_ref[:pao, :])
         y_ref[aux:, :] = jnp.zeros((2 * riders, part), BF16)
 
     (y_low,) = call(
         outer_low_body,
-        [VMEM, VMEM],
+        [VMEM, VMEM, ANY],
         [(VMEM, (aux + 2 * riders, part), BF16)],
-        (blocks, low_out),
+        (blocks, low_out, three_in),
     )
     y_low_from_out = outer(y_low)
 
-    def outer_high_body(three_ref, low_ref, x_ref, after_ref, y_ref):
+    def outer_high_body(three_ref, low_ref, x_ref, after_ref, y_ref, quarter_ref):
         half_into(y_ref, three_ref, whole(told_of(low_ref)[0, place_at]), x_ref[...])
         y_ref[aux:, :] = jnp.zeros((riders, part), BF16)
-
-    (y_high,) = call(
+        quarter_ref[...] = low_ref[pao + riders :, :]
+
+    y_high, quarters = call(
         outer_high_body,
         [VMEM, VMEM, VMEM, ANY],
-        [(VMEM, (aux + riders, part), BF16)],
+        [(VMEM, (aux + riders, part), BF16), (VMEM, (2 * quarter, part), BF16)],
         (blocks, low_out, high_out, y_low),
     )
     y_high_from_out = outer(y_high)
@@ -280,12 +309,22 @@
     )
     c_from_out = outer(c_out)
 
+    def double_body(mine_ref, come_ref, out_ref):
+        out_ref[0] = mine_ref[...]
+        out_ref[1] = come_ref[...]
+
+    steps = [1 << at for at in range(roles.bit_length() - 1)]
+    for step in steps[:-1]:
+        shape = (2, *quarters.shape)
+        (quarters,) = call(
+            double_body, [VMEM, VMEM], [(VMEM, shape, BF16)], (quarters, swap(quarters, step))
+        )
+    quarters = [quarters, swap(quarters, steps[-1])]
+
     def own_half_body(
-        nums, three_ref, three_in_ref, coeff_ref, after_ref, first_ref, second_ref, extra_ref, block_ref, sem
+        nums, three_ref, three_in_ref, coeff_ref, after_ref, first_ref, second_ref, block_ref, sem
     ):
         x = coeff_ref[whole(nums[MINE])]
-        extra_ref[:pao, :] = coeff_ref[whole(nums[EXTRA])]
-        extra_ref[pao:, :] = jnp.zeros((2 * riders, virt), BF16)
         whose, second = whole(nums[WHOSE]), whole(nums[SECOND])
         copy = pltpu.make_async_copy(three_in_ref.at[second], block_ref.at[0], sem)
 
@@ -307,19 +346,13 @@
             copy.wait()
             half_into(second_ref, block_ref, 0, x)
 
-    first_t, second, x_extra = call(
+    first_t, second = call(
         own_half_body,
         [SMEM, VMEM, ANY, VMEM, ANY],
-        [
-            (VMEM, (virt, aux), BF16),
-            (VMEM, (aux, virt), BF16),
-            (VMEM, (pao + 2 * riders, virt), BF16),
-        ],
+        [(VMEM, (virt, aux), BF16), (VMEM, (aux, virt), BF16)],
         (nums, blocks, three_in, coeff, c_out),
         scratch=[pltpu.VMEM((1, aux, pao), BF16), pltpu.SemaphoreType.DMA],
     )
-    x_extra_out = outer(x_extra)
-
     def own_body(
         nums, coeff_ref, coeff_in_ref, amps_ref, amps_in_ref, eps_ref, after_ref,
         s_ref, c_ref, gain_ref, gain_extra_ref, s_in_ref,
@@ -370,6 +403,27 @@
         (nums, coeff, coeff_in, low_in, c_own),
     )
 
+    def extra_out_body(coeff_ref, after_ref, *refs):
+        mine_ref, come_ref, s_ref, x_ref = refs
+        role = lax.axis_index("role")
+
+        @pl.when(role > 0)
+        def _():
+            for m in range(roles):
+                part_ref = (mine_ref, come_ref)[m // steps[-1]].at[m % steps[-1]]
+                rows = pl.ds(pl.multiple_of((role ^ m) * quarter, quarter), quarter)
+                x_ref[rows, :part] = part_ref[:quarter, :]
+                x_ref[rows, part:] = part_ref[quarter:, :]
+            overlaps(x_ref[...], coeff_ref, s_ref)
+
+    (se_out,) = call(
+        extra_out_body,
+        [VMEM, ANY, VMEM, VMEM],
+        [all_s],
+        (coeff, se_own, *quarters),
+        scratch=[pltpu.VMEM((pao, virt), BF16)],
+    )
+
     def first_body(
         nums, first_ref, second_ref, low_ref, high_ref, amps_ref, c_ref, co_ref, gain_ref, after_ref,
         amp_ref, k_ref,
@@ -396,7 +450,7 @@
         [sq_b, sq_f],
         (
             nums, first_t, second, y_low_from_out, y_high_from_out,
-            amps, c_own, c_from_out, gain, se_own,
+            amps, c_own, c_from_out, gain, se_out,
         ),
     )
     amp_roles = [amp] + [swap(amp, m) for m in range(1, roles)]
@@ -413,18 +467,6 @@
 
     rest, rest_b = call(rest_body, [VMEM, VMEM], [sq_f, longer], (amp, k_first))
     rests = [lax.ppermute(rest_b, "role", [(0, s)]) for s in range(1, roles)]
-
-    def extra_out_body(coeff_ref, x_ref, after_ref, s_ref):
-        @pl.when(lax.axis_index("role") > 0)
-        def _():
-            overlaps(x_ref[:pao, :], coeff_ref, s_ref)
-
-    (se_out,) = call(
-        extra_out_body,
-        [VMEM, VMEM, ANY],
-        [all_s],
-        (coeff, x_extra_out, amp),
-    )
 
     def parts_of(nums, weight_of, amp_refs):
         role = lax.axis_index("role")

time: 53.8 us -> 56.6 us (1.052)
  waiting for transfers between devices: 10.2 us -> 13.1 us
  starting transfers between devices: 27.6 us -> 25.8 us
  Pallas kernels: 14.2 us -> 15.9 us
    ppermute x7 -> x6, starting transfers between devices: 16.4 us -> 12.1 us  [outer(): return lax.ppermute(x, 'pairs', list(enumerate(outer_of)))]
    ppermute x3 -> x5, starting transfers between devices: 3.55 us -> 5.43 us  [swap(): return lax.ppermute(x, 'role', [(i, i ^ by) for i in range(roles)])]
    pallas_call x16 -> x17, Pallas kernels: 14.2 us -> 15.9 us  [call(): pl.pallas_call(body, in_specs=ins, out_specs=[spec for spec, _, _ in outs...]
    ppermute x7 -> x6, waiting for transfers between devices: 9.14 us -> 10.3 us  [outer(): return lax.ppermute(x, 'pairs', list(enumerate(outer_of)))]
    ppermute x3, starting transfers between devices: 6 us -> 7.07 us  [local(): rests = [lax.ppermute(rest_b, 'role', [(0, s)]) for s in range(1, roles)]]
    ppermute x3 -> x5, waiting for transfers between devices: 0.01 us -> 0.77 us  [swap(): return lax.ppermute(x, 'role', [(i, i ^ by) for i in range(roles)])]
    ppermute x3, waiting for transfers between devices: 0.01 us -> 0.68 us  [local(): rests = [lax.ppermute(rest_b, 'role', [(0, s)]) for s in range(1, roles)]]
  transfers between devices with their start and end apart: 19 -> 20, of which waited for: 5 -> 6; matrix products, arithmetic and copies ran while one was open for 0% -> 0% of each run, Pallas kernels for 24% -> 24%
where the time goes in v9:
time: 56.6 us; the launch traced here: 56.4 us
  starting transfers between devices  25.8 us (46%)
  Pallas kernels  15.9 us (28%)
  waiting for transfers between devices  13.1 us (23%)
  between operations  0.91 us (2%)
  local copies, waits for them, and re-layouts  0.7 us (1%)
    pallas_call x17, Pallas kernels, call(): pl.pallas_call(body, in_specs=ins, out_specs=[spec for spec, _, _ in outs...  15.9 us
    ppermute x6, starting transfers between devices, outer(): return lax.ppermute(x, 'pairs', list(enumerate(outer_of)))  12.1 us
    ppermute x6, waiting for transfers between devices, outer(): return lax.ppermute(x, 'pairs', list(enumerate(outer_of)))  10.3 us
    ppermute x3, starting transfers between devices, local(): rests = [lax.ppermute(rest_b, 'role', [(0, s)]) for s in range(1, roles)]  7.07 us
    ppermute x5, starting transfers between devices, swap(): return lax.ppermute(x, 'role', [(i, i ^ by) for i in range(roles)])  5.43 us
    ppermute x6, waiting for transfers between devices, inner(): return lax.ppermute(x, 'pairs', list(enumerate(inner_of)))  1.35 us
    ppermute x6, starting transfers between devices, inner(): return lax.ppermute(x, 'pairs', list(enumerate(inner_of)))  1.17 us
  transfers between devices with their start and end apart: 20, of which 6 were waited for; matrix products, arithmetic and copies ran while one was open for 0% of the time, Pallas kernels for 24%

profile of v9, /device:TPU:0, one launch (start us, length us, event | category | flops | bytes accessed | tf_op | source)
XLA Modules:
  0.0 56.4 jit_solution(12010142559779243264)
XLA Ops:
  0.6 0.5 collective-permute-start.4
  1.1 0.1 collective-permute-start
  1.2 0.4 collective-permute-start.1
  1.7 2.9 %shard_map.113 = (bf16[784,128]{1,0:T(8,128)(2,1)}, bf16[512,128]{1,0:T(8,128)(2,1)}, f32[30]{0:T(128)}) custom-call(s32[4]{0:T(128)} %owner_hbm.1, s32[2,4]{1,0:T(2,128)} %bitcast.1, s32[4,8]{1,0:T(4,128)} %partner_hbm.1, f32[4,8]{1,0:T(4,128)} %coupling_hbm.1, f32[16]{0:T(128)} %eps_hbm.1, s32[4]{0:T(128)} %nvirt_hbm.1, bf16[4,512,256]{2,1,0:T(8,128)(2,1)} %coeff_ref.11), custom_call_target="tpu_custom_call" | custom-call | flops 1 | bytes 1 | tf_op jit(solution)/shard_map/pallas_call | solution.py:33
  4.6 4.8 %collective-permute-start.2 = (bf16[784,128]{1,0:T(8,128)(2,1)}, bf16[784,128]{1,0:T(8,128)(2,1)S(1)}, u32[]{:S(2)}, u32[]{:S(2)}) collective-permute-start(bf16[784,128]{1,0:T(8,128)(2,1)} %get-tuple-element.27), channel_id=1, source_target_pairs={{0,7},{1,2},{2,1},{3,4},{4,3},{5,6},{6,5},{7,0},{8,15},{9,10},{10,... | collective-permute-start | bytes 602120 | tf_op jit(solution)/shard_map/ppermute | solution.py:74
  9.4 0.1 collective-permute-start.3
  9.5 0.0 collective-permute-done.1.refs_2_.amps_in_ref
  9.5 0.0 collective-permute-done.refs_1_.coeff_in_ref.in_ref
  9.5 0.7 %copy-done.2 = f32[30]{0:T(128)S(1)} copy-done((f32[30]{0:T(128)S(1)}, f32[30]{0:T(128)}, u32[]{:S(2)}) %copy-start.2) | copy-done | bytes 144
  10.1 1.6 %shard_map.114.three_ref = bf16[2,1024,512]{2,1,0:T(8,128)(2,1)S(1)} custom-call(bf16[2,1024,512]{2,1,0:T(8,128)(2,1)} %three_ref.1, f32[30]{0:T(128)S(1)} %copy-done.2, bf16[4,512,256]{2,1,0:T(8,128)(2,1)S(1)} %collective-permute-done.refs_1_.coeff_in_ref.in_ref, bf16[4,256,256]{2,1,0:T(8,128)(2,1)S(1)} %collective-permute-done.1.refs_2_.amps_in_ref), custom_call_target="tpu_custom_call" | custom-call | flops 1 | bytes 1 | tf_op jit(solution)/shard_map/pallas_call | solution.py:33
  11.8 2.7 %collective-permute-done.2.x_ref.low_ref = bf16[784,128]{1,0:T(8,128)(2,1)S(1)} collective-permute-done((bf16[784,128]{1,0:T(8,128)(2,1)}, bf16[784,128]{1,0:T(8,128)(2,1)S(1)}, u32[]{:S(2)}, u32[]{:S(2)}) %collective-permute-start.2) | collective-permute-done | bytes 200736 | tf_op jit(solution)/shard_map/ppermute | solution.py:74
  14.4 0.0 collective-permute-done.4.after_ref.three_in_ref
  14.5 0.5 shard_map.115.after_ref
  15.0 0.0 copy-start.5
  15.0 0.0 copy-start
  15.0 0.0 copy-start.1
  15.0 0.0 copy-start.3
  15.0 3.2 %collective-permute-start.5 = (bf16[1056,128]{1,0:T(8,128)(2,1)S(1)}, bf16[1056,128]{1,0:T(8,128)(2,1)S(1)}, u32[]{:S(2)}, u32[]{:S(2)}) collective-permute-start(bf16[1056,128]{1,0:T(8,128)(2,1)S(1)} %shard_map.115.after_ref), channel_id=1, source_target_pairs={{0,7},{1,2},{2,1},{3,4},{4,3},{5,6},{6,5},{7,0},{8,15},{9,10},{10,... | collective-permute-start | bytes 811016 | tf_op jit(solution)/shard_map/ppermute | solution.py:74
  18.2 0.0 collective-permute-done.3.x_ref.high_ref
  18.2 0.5 shard_map.116
  18.8 2.0 %collective-permute-start.6 = (bf16[1040,128]{1,0:T(8,128)(2,1)S(1)}, bf16[1040,128]{1,0:T(8,128)(2,1)S(1)}, u32[]{:S(2)}, u32[]{:S(2)}) collective-permute-start(bf16[1040,128]{1,0:T(8,128)(2,1)S(1)} %get-tuple-element.29.after_ref), channel_id=1, source_target_pairs={{0,7},{1,2},{2,1},{3,4},{4,3},{5,6},{6,5},{7,0},{8,15},{9,10},{10,... | collective-permute-start | bytes 798728 | tf_op jit(solution)/shard_map/ppermute | solution.py:74
  20.8 0.0 copy-done.5
  20.8 0.0 collective-permute-start.8
  20.8 0.9 %collective-permute-start.9 = (bf16[256,128]{1,0:T(8,128)(2,1)S(1)}, bf16[256,128]{1,0:T(8,128)(2,1)S(1)}, u32[]{:S(2)}, u32[]{:S(2)}) collective-permute-start(bf16[256,128]{1,0:T(8,128)(2,1)S(1)} %get-tuple-element.37.mine_ref), channel_id=1, source_target_pairs={{0,8},{8,0},{16,24},{24,16},{1,9},{9,1},{17,25},{25,17},{2,10},{10... | collective-permute-start | bytes 196616 | tf_op jit(solution)/shard_map/ppermute | solution.py:77
  21.7 0.0 copy-done
  21.7 0.0 copy-done.1
  21.7 0.9 %shard_map.117 = (bf16[4,256,256]{2,1,0:T(8,128)(2,1)S(1)}, bf16[304,256]{1,0:T(8,128)(2,1)S(1)}) custom-call(bf16[4,512,256]{2,1,0:T(8,128)(2,1)S(1)} %copy-done, bf16[4,256,256]{2,1,0:T(8,128)(2,1)S(1)} %copy-done.1, bf16[784,128]{1,0:T(8,128)(2,1)S(1)} %collective-permute-done.2.x_ref.low_ref, bf16[512,128]{1,0:T(8,128)(2,1)S(1)} %collective-permute-done.3.x_ref.high_ref, ...), custom_call_target="tpu_custom_call" | custom-call | flops 1 | bytes 1 | tf_op jit(solution)/shard_map/pallas_call | solution.py:33
  22.6 1.9 %collective-permute-start.7 = (bf16[304,256]{1,0:T(8,128)(2,1)S(1)}, bf16[304,256]{1,0:T(8,128)(2,1)S(1)}, u32[]{:S(2)}, u32[]{:S(2)}) collective-permute-start(bf16[304,256]{1,0:T(8,128)(2,1)S(1)} %get-tuple-element.30.after_ref), channel_id=1, source_target_pairs={{0,7},{1,2},{2,1},{3,4},{4,3},{5,6},{6,5},{7,0},{8,15},{9,10},{10,... | collective-permute-start | bytes 466952 | tf_op jit(solution)/shard_map/ppermute | solution.py:74
  24.6 0.8 %collective-permute-done.9.come_ref = bf16[256,128]{1,0:T(8,128)(2,1)S(1)} collective-permute-done((bf16[256,128]{1,0:T(8,128)(2,1)S(1)}, bf16[256,128]{1,0:T(8,128)(2,1)S(1)}, u32[]{:S(2)}, u32[]{:S(2)}) %collective-permute-start.9) | collective-permute-done | bytes 65568 | tf_op jit(solution)/shard_map/ppermute | solution.py:77
  25.3 0.0 copy-start.4
  25.4 1.0 %collective-permute-start.10 = (bf16[2,256,128]{2,1,0:T(8,128)(2,1)S(1)}, bf16[2,256,128]{2,1,0:T(8,128)(2,1)S(1)}, u32[]{:S(2)}, u32[]{:S(2)}) collective-permute-start(bf16[2,256,128]{2,1,0:T(8,128)(2,1)S(1)} %shard_map.121.refs_0_), channel_id=1, source_target_pairs={{0,16},{8,24},{16,0},{24,8},{1,17},{9,25},{17,1},{25,9},{2,18},{10... | collective-permute-start | bytes 393224 | tf_op jit(solution)/shard_map/ppermute | solution.py:77
  26.3 0.0 copy-done.3
  26.3 2.3 %shard_map.119 = (bf16[256,1024]{1,0:T(8,128)(2,1)S(1)}, bf16[1024,256]{1,0:T(8,128)(2,1)S(1)}) custom-call(f32[30]{0:T(128)S(1)} %copy-done.3, bf16[2,1024,512]{2,1,0:T(8,128)(2,1)S(1)} %shard_map.114.three_ref, bf16[2,1024,512]{2,1,0:T(8,128)(2,1)} %collective-permute-done.4.after_ref.three_in_ref, bf16[4,512,256]{2,1,0:T(8,128)(2,1)S(1)} %copy-done, ...), custom_call_target="tpu_custom_call" | custom-call | flops 1 | bytes 1 | tf_op jit(solution)/shard_map/pallas_call | solution.py:33
  28.7 2.0 %shard_map.118 = (bf16[4,256,256]{2,1,0:T(8,128)(2,1)S(1)}, f32[256,256]{1,0:T(8,128)S(1)}, f32[256,256]{1,0:T(8,128)S(1)}, f32[256,256]{1,0:T(8,128)S(1)}) custom-call(f32[30]{0:T(128)S(1)} %copy-done.3, bf16[4,512,256]{2,1,0:T(8,128)(2,1)S(1)} %copy-done, bf16[4,512,256]{2,1,0:T(8,128)(2,1)S(1)} %collective-permute-done.refs_1_.coeff_in_ref.in_ref, ...), custom_call_target="tpu_custom_call" | custom-call | flops 1 | bytes 1 | tf_op jit(solution)/shard_map/pallas_call | solution.py:33
  30.7 0.0 collective-permute-done.8.low_ref
  30.7 0.6 shard_map.120
  31.2 0.0 collective-permute-done.10.refs_1_
  31.3 3.3 %collective-permute-done.7.co_ref = bf16[304,256]{1,0:T(8,128)(2,1)S(1)} collective-permute-done((bf16[304,256]{1,0:T(8,128)(2,1)S(1)}, bf16[304,256]{1,0:T(8,128)(2,1)S(1)}, u32[]{:S(2)}, u32[]{:S(2)}) %collective-permute-start.7) | collective-permute-done | bytes 155680 | tf_op jit(solution)/shard_map/ppermute | solution.py:74
  34.6 0.0 collective-permute-done.6.high_ref
  34.6 0.0 collective-permute-done.5.low_ref
  34.6 0.9 %shard_map.123 = (bf16[256,256]{1,0:T(8,128)(2,1)S(1)}, f32[256,256]{1,0:T(8,128)S(1)}) custom-call(f32[30]{0:T(128)S(1)} %copy-done.3, bf16[256,1024]{1,0:T(8,128)(2,1)S(1)} %get-tuple-element.33.first_ref, bf16[1024,256]{1,0:T(8,128)(2,1)S(1)} %get-tuple-element.34.second_ref, bf16[1056,128]{1,0:T(8,128)(2,1)S(1)} %collective-permute-done.5.low_ref, ...), custom_call_target="tpu_custom_call" | custom-call | flops 1 | bytes 1 | tf_op jit(solution)/shard_map/pallas_call | solution.py:33
  35.6 2.6 %collective-permute-start.13 = (bf16[256,256]{1,0:T(8,128)(2,1)S(1)}, bf16[256,256]{1,0:T(8,128)(2,1)S(1)}, u32[]{:S(2)}, u32[]{:S(2)}) collective-permute-start(bf16[256,256]{1,0:T(8,128)(2,1)S(1)} %get-tuple-element.38.amp_ref.refs_0_), channel_id=1, source_target_pairs={{0,24},{8,16},{16,8},{24,0},{1,25},{9,17},{17,9},{25,1},{2,26},{10... | collective-permute-start | bytes 393224 | tf_op jit(solution)/shard_map/ppermute | solution.py:77
  38.2 0.4 collective-permute-start.12
  38.6 0.5 collective-permute-start.11
  39.1 0.4 shard_map.124
  39.5 4.5 %collective-permute-start.18 = (bf16[272,256]{1,0:T(8,128)(2,1)S(1)}, bf16[272,256]{1,0:T(8,128)(2,1)S(1)}, u32[]{:S(2)}, u32[]{:S(2)}) collective-permute-start(bf16[272,256]{1,0:T(8,128)(2,1)S(1)} %get-tuple-element.49), channel_id=1, source_target_pairs={{0,24},{1,25},{2,26},{3,27},{4,28},{5,29},{6,30},{7,31}} | collective-permute-start | bytes 417800 | tf_op jit(solution)/shard_map/ppermute | solution.py:469
  44.0 1.3 %collective-permute-start.17 = (bf16[272,256]{1,0:T(8,128)(2,1)S(1)}, bf16[272,256]{1,0:T(8,128)(2,1)S(1)}, u32[]{:S(2)}, u32[]{:S(2)}) collective-permute-start(bf16[272,256]{1,0:T(8,128)(2,1)S(1)} %get-tuple-element.49), channel_id=1, source_target_pairs={{0,16},{1,17},{2,18},{3,19},{4,20},{5,21},{6,22},{7,23}} | collective-permute-start | bytes 417800 | tf_op jit(solution)/shard_map/ppermute | solution.py:469
  45.3 0.0 collective-permute-done.13.refs_3_
  45.3 1.3 %collective-permute-start.16 = (bf16[272,256]{1,0:T(8,128)(2,1)S(1)}, bf16[272,256]{1,0:T(8,128)(2,1)S(1)}, u32[]{:S(2)}, u32[]{:S(2)}) collective-permute-start(bf16[272,256]{1,0:T(8,128)(2,1)S(1)} %get-tuple-element.49), channel_id=1, source_target_pairs={{0,8},{1,9},{2,10},{3,11},{4,12},{5,13},{6,14},{7,15}} | collective-permute-start | bytes 417800 | tf_op jit(solution)/shard_map/ppermute | solution.py:469
  46.6 0.0 collective-permute-done.12.refs_2_
  46.6 0.0 collective-permute-done.11.refs_1_
  46.6 0.6 shard_map.125.refs_4_
  47.2 0.1 collective-permute-start.14
  47.3 0.6 shard_map.126
  47.9 0.1 collective-permute-start.15
  47.9 0.6 shard_map.127
  48.5 0.0 collective-permute-done.18.refs_3_.refs_2_
  48.5 0.0 collective-permute-done.17.refs_2_.refs_1_
  48.5 0.7 %collective-permute-done.16.refs_1_.refs_0_ = bf16[272,256]{1,0:T(8,128)(2,1)S(1)} collective-permute-done((bf16[272,256]{1,0:T(8,128)(2,1)S(1)}, bf16[272,256]{1,0:T(8,128)(2,1)S(1)}, u32[]{:S(2)}, u32[]{:S(2)}) %collective-permute-start.16) | collective-permute-done | bytes 139296 | tf_op jit(solution)/shard_map/ppermute | solution.py:469
  49.2 0.1 collective-permute-start.19
  49.3 0.0 collective-permute-done.15.ci_ref
  49.3 1.3 %collective-permute-done.19.cei_ref = bf16[272,256]{1,0:T(8,128)(2,1)S(1)} collective-permute-done((bf16[272,256]{1,0:T(8,128)(2,1)S(1)}, bf16[272,256]{1,0:T(8,128)(2,1)S(1)}, u32[]{:S(2)}, u32[]{:S(2)}) %collective-permute-start.19) | collective-permute-done | bytes 139296 | tf_op jit(solution)/shard_map/ppermute | solution.py:71
  50.6 4.2 %collective-permute-done.14.co_ref = bf16[2,256,256]{2,1,0:T(8,128)(2,1)S(1)} collective-permute-done((bf16[2,256,256]{2,1,0:T(8,128)(2,1)S(1)}, bf16[2,256,256]{2,1,0:T(8,128)(2,1)S(1)}, u32[]{:S(2)}, u32[]{:S(2)}) %collective-permute-start.14) | collective-permute-done | bytes 262176 | tf_op jit(solution)/shard_map/ppermute | solution.py:74
  54.9 1.5 %shard_map.129 = (bf16[2,256,256]{2,1,0:T(8,128)(2,1)}, bf16[2,512,256]{2,1,0:T(8,128)(2,1)}) custom-call(f32[30]{0:T(128)S(1)} %copy-done.3, bf16[4,512,256]{2,1,0:T(8,128)(2,1)S(1)} %copy-done, f32[256,256]{1,0:T(8,128)S(1)} %get-tuple-element.31.gain_ref, f32[256,256]{1,0:T(8,128)S(1)} %get-tuple-element.32.gain_extra_ref, ...), custom_call_target="tpu_custom_call" | custom-call | flops 1 | bytes 1 | tf_op jit(solution)/shard_map/pallas_call | solution.py:33
  (5 shorter events, 0.0 us)
Async XLA Ops:
  0.6 13.8 %collective-permute-start.4 = (bf16[2,1024,512]{2,1,0:T(8,128)(2,1)}, bf16[2,1024,512]{2,1,0:T(8,128)(2,1)}, u32[]{:S(2)}, u32[]{:S(2)}) collective-permute-start(bf16[2,1024,512]{2,1,0:T(8,128)(2,1)} %three_ref.1), channel_id=1, source_target_pairs={{0,1},{1,0},{2,3},{3,2},{4,5},{5,4},{6,7},{7,6},{8,9},{9,8},{10,11... | collective-permute-start | bytes 6291464 | tf_op jit(solution)/shard_map/ppermute | solution.py:71
  1.1 8.3 %collective-permute-start = (bf16[4,512,256]{2,1,0:T(8,128)(2,1)}, bf16[4,512,256]{2,1,0:T(8,128)(2,1)S(1)}, u32[]{:S(2)}, u32[]{:S(2)}) collective-permute-start(bf16[4,512,256]{2,1,0:T(8,128)(2,1)} %coeff_ref.11), channel_id=1, source_target_pairs={{0,1},{1,0},{2,3},{3,2},{4,5},{5,4},{6,7},{7,6},{8,9},{9,8},{10,11... | collective-permute-start | bytes 3145736 | tf_op jit(solution)/shard_map/ppermute | solution.py:71
  1.2 8.2 %collective-permute-start.1 = (bf16[4,256,256]{2,1,0:T(8,128)(2,1)}, bf16[4,256,256]{2,1,0:T(8,128)(2,1)S(1)}, u32[]{:S(2)}, u32[]{:S(2)}) collective-permute-start(bf16[4,256,256]{2,1,0:T(8,128)(2,1)} %amps_ref.5), channel_id=1, source_target_pairs={{0,1},{1,0},{2,3},{3,2},{4,5},{5,4},{6,7},{7,6},{8,9},{9,8},{10,11... | collective-permute-start | bytes 1572872 | tf_op jit(solution)/shard_map/ppermute | solution.py:71
  4.6 9.8 %collective-permute-start.2 = (bf16[784,128]{1,0:T(8,128)(2,1)}, bf16[784,128]{1,0:T(8,128)(2,1)S(1)}, u32[]{:S(2)}, u32[]{:S(2)}) collective-permute-start(bf16[784,128]{1,0:T(8,128)(2,1)} %get-tuple-element.27), channel_id=1, source_target_pairs={{0,7},{1,2},{2,1},{3,4},{4,3},{5,6},{6,5},{7,0},{8,15},{9,10},{10,... | collective-permute-start | bytes 602120 | tf_op jit(solution)/shard_map/ppermute | solution.py:74
  9.4 8.9 %collective-permute-start.3 = (bf16[512,128]{1,0:T(8,128)(2,1)}, bf16[512,128]{1,0:T(8,128)(2,1)S(1)}, u32[]{:S(2)}, u32[]{:S(2)}) collective-permute-start(bf16[512,128]{1,0:T(8,128)(2,1)} %get-tuple-element.28), channel_id=1, source_target_pairs={{0,7},{1,2},{2,1},{3,4},{4,3},{5,6},{6,5},{7,0},{8,15},{9,10},{10,... | collective-permute-start | bytes 393224 | tf_op jit(solution)/shard_map/ppermute | solution.py:74
  9.5 0.7 %copy-start.2 = (f32[30]{0:T(128)S(1)}, f32[30]{0:T(128)}, u32[]{:S(2)}) copy-start(f32[30]{0:T(128)} %get-tuple-element.26.refs_0_.nums) | copy-start | bytes 364
  15.0 5.8 %copy-start.5 = (bf16[784,128]{1,0:T(8,128)(2,1)S(1)}, bf16[784,128]{1,0:T(8,128)(2,1)}, u32[]{:S(2)}) copy-start(bf16[784,128]{1,0:T(8,128)(2,1)} %get-tuple-element.27) | copy-start | bytes 602116
  15.0 6.7 %copy-start = (bf16[4,512,256]{2,1,0:T(8,128)(2,1)S(1)}, bf16[4,512,256]{2,1,0:T(8,128)(2,1)}, u32[]{:S(2)}) copy-start(bf16[4,512,256]{2,1,0:T(8,128)(2,1)} %coeff_ref.11) | copy-start | bytes 3145732
  15.0 6.7 %copy-start.1 = (bf16[4,256,256]{2,1,0:T(8,128)(2,1)S(1)}, bf16[4,256,256]{2,1,0:T(8,128)(2,1)}, u32[]{:S(2)}) copy-start(bf16[4,256,256]{2,1,0:T(8,128)(2,1)} %amps_ref.5) | copy-start | bytes 1572868
  15.0 11.3 %copy-start.3 = (f32[30]{0:T(128)S(1)}, f32[30]{0:T(128)}, u32[]{:S(2)}) copy-start(f32[30]{0:T(128)} %get-tuple-element.26.refs_0_.nums) | copy-start | bytes 364
  15.0 19.6 %collective-permute-start.5 = (bf16[1056,128]{1,0:T(8,128)(2,1)S(1)}, bf16[1056,128]{1,0:T(8,128)(2,1)S(1)}, u32[]{:S(2)}, u32[]{:S(2)}) collective-permute-start(bf16[1056,128]{1,0:T(8,128)(2,1)S(1)} %shard_map.115.after_ref), channel_id=1, source_target_pairs={{0,7},{1,2},{2,1},{3,4},{4,3},{5,6},{6,5},{7,0},{8,15},{9,10},{10,... | collective-permute-start | bytes 811016 | tf_op jit(solution)/shard_map/ppermute | solution.py:74
  18.8 15.8 %collective-permute-start.6 = (bf16[1040,128]{1,0:T(8,128)(2,1)S(1)}, bf16[1040,128]{1,0:T(8,128)(2,1)S(1)}, u32[]{:S(2)}, u32[]{:S(2)}) collective-permute-start(bf16[1040,128]{1,0:T(8,128)(2,1)S(1)} %get-tuple-element.29.after_ref), channel_id=1, source_target_pairs={{0,7},{1,2},{2,1},{3,4},{4,3},{5,6},{6,5},{7,0},{8,15},{9,10},{10,... | collective-permute-start | bytes 798728 | tf_op jit(solution)/shard_map/ppermute | solution.py:74
  20.8 9.8 %collective-permute-start.8 = (bf16[784,128]{1,0:T(8,128)(2,1)S(1)}, bf16[784,128]{1,0:T(8,128)(2,1)S(1)}, u32[]{:S(2)}, u32[]{:S(2)}) collective-permute-start(bf16[784,128]{1,0:T(8,128)(2,1)S(1)} %copy-done.5), channel_id=1, source_target_pairs={{0,1},{1,0},{2,3},{3,2},{4,5},{5,4},{6,7},{7,6},{8,9},{9,8},{10,11... | collective-permute-start | bytes 602120 | tf_op jit(solution)/shard_map/ppermute | solution.py:71
  20.8 4.5 %collective-permute-start.9 = (bf16[256,128]{1,0:T(8,128)(2,1)S(1)}, bf16[256,128]{1,0:T(8,128)(2,1)S(1)}, u32[]{:S(2)}, u32[]{:S(2)}) collective-permute-start(bf16[256,128]{1,0:T(8,128)(2,1)S(1)} %get-tuple-element.37.mine_ref), channel_id=1, source_target_pairs={{0,8},{8,0},{16,24},{24,16},{1,9},{9,1},{17,25},{25,17},{2,10},{10... | collective-permute-start | bytes 196616 | tf_op jit(solution)/shard_map/ppermute | solution.py:77
  22.6 12.0 %collective-permute-start.7 = (bf16[304,256]{1,0:T(8,128)(2,1)S(1)}, bf16[304,256]{1,0:T(8,128)(2,1)S(1)}, u32[]{:S(2)}, u32[]{:S(2)}) collective-permute-start(bf16[304,256]{1,0:T(8,128)(2,1)S(1)} %get-tuple-element.30.after_ref), channel_id=1, source_target_pairs={{0,7},{1,2},{2,1},{3,4},{4,3},{5,6},{6,5},{7,0},{8,15},{9,10},{10,... | collective-permute-start | bytes 466952 | tf_op jit(solution)/shard_map/ppermute | solution.py:74
  25.3 3.3 %copy-start.4 = (f32[4,256]{1,0:T(4,128)S(1)}, f32[4,256]{1,0:T(4,128)}, u32[]{:S(2)}) copy-start(f32[4,256]{1,0:T(4,128)} %eps_ref.1) | copy-start | bytes 12292
  25.4 5.9 %collective-permute-start.10 = (bf16[2,256,128]{2,1,0:T(8,128)(2,1)S(1)}, bf16[2,256,128]{2,1,0:T(8,128)(2,1)S(1)}, u32[]{:S(2)}, u32[]{:S(2)}) collective-permute-start(bf16[2,256,128]{2,1,0:T(8,128)(2,1)S(1)} %shard_map.121.refs_0_), channel_id=1, source_target_pairs={{0,16},{8,24},{16,0},{24,8},{1,17},{9,25},{17,1},{25,9},{2,18},{10... | collective-permute-start | bytes 393224 | tf_op jit(solution)/shard_map/ppermute | solution.py:77
  35.6 9.8 %collective-permute-start.13 = (bf16[256,256]{1,0:T(8,128)(2,1)S(1)}, bf16[256,256]{1,0:T(8,128)(2,1)S(1)}, u32[]{:S(2)}, u32[]{:S(2)}) collective-permute-start(bf16[256,256]{1,0:T(8,128)(2,1)S(1)} %get-tuple-element.38.amp_ref.refs_0_), channel_id=1, source_target_pairs={{0,24},{8,16},{16,8},{24,0},{1,25},{9,17},{17,9},{25,1},{2,26},{10... | collective-permute-start | bytes 393224 | tf_op jit(solution)/shard_map/ppermute | solution.py:77
  38.2 8.4 %collective-permute-start.12 = (bf16[256,256]{1,0:T(8,128)(2,1)S(1)}, bf16[256,256]{1,0:T(8,128)(2,1)S(1)}, u32[]{:S(2)}, u32[]{:S(2)}) collective-permute-start(bf16[256,256]{1,0:T(8,128)(2,1)S(1)} %get-tuple-element.38.amp_ref.refs_0_), channel_id=1, source_target_pairs={{0,16},{8,24},{16,0},{24,8},{1,17},{9,25},{17,1},{25,9},{2,18},{10... | collective-permute-start | bytes 393224 | tf_op jit(solution)/shard_map/ppermute | solution.py:77
  38.6 8.1 %collective-permute-start.11 = (bf16[256,256]{1,0:T(8,128)(2,1)S(1)}, bf16[256,256]{1,0:T(8,128)(2,1)S(1)}, u32[]{:S(2)}, u32[]{:S(2)}) collective-permute-start(bf16[256,256]{1,0:T(8,128)(2,1)S(1)} %get-tuple-element.38.amp_ref.refs_0_), channel_id=1, source_target_pairs={{0,8},{8,0},{16,24},{24,16},{1,9},{9,1},{17,25},{25,17},{2,10},{10... | collective-permute-start | bytes 393224 | tf_op jit(solution)/shard_map/ppermute | solution.py:77
  39.5 9.0 %collective-permute-start.18 = (bf16[272,256]{1,0:T(8,128)(2,1)S(1)}, bf16[272,256]{1,0:T(8,128)(2,1)S(1)}, u32[]{:S(2)}, u32[]{:S(2)}) collective-permute-start(bf16[272,256]{1,0:T(8,128)(2,1)S(1)} %get-tuple-element.49), channel_id=1, source_target_pairs={{0,24},{1,25},{2,26},{3,27},{4,28},{5,29},{6,30},{7,31}} | collective-permute-start | bytes 417800 | tf_op jit(solution)/shard_map/ppermute | solution.py:469
  44.0 4.5 %collective-permute-start.17 = (bf16[272,256]{1,0:T(8,128)(2,1)S(1)}, bf16[272,256]{1,0:T(8,128)(2,1)S(1)}, u32[]{:S(2)}, u32[]{:S(2)}) collective-permute-start(bf16[272,256]{1,0:T(8,128)(2,1)S(1)} %get-tuple-element.49), channel_id=1, source_target_pairs={{0,16},{1,17},{2,18},{3,19},{4,20},{5,21},{6,22},{7,23}} | collective-permute-start | bytes 417800 | tf_op jit(solution)/shard_map/ppermute | solution.py:469
  45.3 3.9 %collective-permute-start.16 = (bf16[272,256]{1,0:T(8,128)(2,1)S(1)}, bf16[272,256]{1,0:T(8,128)(2,1)S(1)}, u32[]{:S(2)}, u32[]{:S(2)}) collective-permute-start(bf16[272,256]{1,0:T(8,128)(2,1)S(1)} %get-tuple-element.49), channel_id=1, source_target_pairs={{0,8},{1,9},{2,10},{3,11},{4,12},{5,13},{6,14},{7,15}} | collective-permute-start | bytes 417800 | tf_op jit(solution)/shard_map/ppermute | solution.py:469
  47.2 7.7 %collective-permute-start.14 = (bf16[2,256,256]{2,1,0:T(8,128)(2,1)S(1)}, bf16[2,256,256]{2,1,0:T(8,128)(2,1)S(1)}, u32[]{:S(2)}, u32[]{:S(2)}) collective-permute-start(bf16[2,256,256]{2,1,0:T(8,128)(2,1)S(1)} %shard_map.125.refs_4_), channel_id=1, source_target_pairs={{0,7},{1,2},{2,1},{3,4},{4,3},{5,6},{6,5},{7,0},{8,15},{9,10},{10,... | collective-permute-start | bytes 786440 | tf_op jit(solution)/shard_map/ppermute | solution.py:74
  47.9 1.4 %collective-permute-start.15 = (bf16[272,256]{1,0:T(8,128)(2,1)S(1)}, bf16[272,256]{1,0:T(8,128)(2,1)S(1)}, u32[]{:S(2)}, u32[]{:S(2)}) collective-permute-start(bf16[272,256]{1,0:T(8,128)(2,1)S(1)} %get-tuple-element.45.refs_4_), channel_id=1, source_target_pairs={{0,1},{1,0},{2,3},{3,2},{4,5},{5,4},{6,7},{7,6},{8,9},{9,8},{10,11... | collective-permute-start | bytes 417800 | tf_op jit(solution)/shard_map/ppermute | solution.py:71
  49.2 1.4 %collective-permute-start.19 = (bf16[272,256]{1,0:T(8,128)(2,1)S(1)}, bf16[272,256]{1,0:T(8,128)(2,1)S(1)}, u32[]{:S(2)}, u32[]{:S(2)}) collective-permute-start(bf16[272,256]{1,0:T(8,128)(2,1)S(1)} %shard_map.128), channel_id=1, source_target_pairs={{0,1},{1,0},{2,3},{3,2},{4,5},{5,4},{6,7},{7,6},{8,9},{9,8},{10,11... | collective-permute-start | bytes 417800 | tf_op jit(solution)/shard_map/ppermute | solution.py:71

commit v10 on v8

--- a/solution.py
+++ b/solution.py
@@ -240,24 +240,23 @@
 
     def outer_low_body(three_ref, x_ref, y_ref):
         half_into(y_ref, three_ref, whole(told_of(x_ref)[0, place_at]), x_ref[:pao, :])
-        y_ref[aux:, :] = jnp.zeros((2 * riders, part), BF16)
+        y_ref[aux:, :] = jnp.zeros((riders, part), BF16)
 
     (y_low,) = call(
         outer_low_body,
         [VMEM, VMEM],
-        [(VMEM, (aux + 2 * riders, part), BF16)],
+        [(VMEM, (aux + riders, part), BF16)],
         (blocks, low_out),
     )
     y_low_from_out = outer(y_low)
 
     def outer_high_body(three_ref, low_ref, x_ref, after_ref, y_ref):
         half_into(y_ref, three_ref, whole(told_of(low_ref)[0, place_at]), x_ref[...])
-        y_ref[aux:, :] = jnp.zeros((riders, part), BF16)
 
     (y_high,) = call(
         outer_high_body,
         [VMEM, VMEM, VMEM, ANY],
-        [(VMEM, (aux + riders, part), BF16)],
+        [(VMEM, (aux, part), BF16)],
         (blocks, low_out, high_out, y_low),
     )
     y_high_from_out = outer(y_high)
@@ -269,12 +268,12 @@
         told = told_of(low_ref)
         c = coupled(s_ref, [(q, told[0, q], amps_ref[q]) for q in range(pairs)])
         c_ref[:virt, :] = c.astype(BF16)
-        c_ref[virt:, :] = jnp.zeros((3 * riders, virt), BF16)
+        c_ref[virt:, :] = jnp.zeros((riders, virt), BF16)
 
     s_out, c_out = call(
         outer_body,
         [VMEM, VMEM, VMEM, VMEM, ANY],
-        [all_s, (VMEM, (virt + 3 * riders, virt), BF16)],
+        [all_s, longer],
         (coeff, amps, low_out, high_out, y_high),
         scratch=[pltpu.VMEM((pao, virt), BF16)],
     )
@@ -284,8 +283,7 @@
         nums, three_ref, three_in_ref, coeff_ref, after_ref, first_ref, second_ref, extra_ref, block_ref, sem
     ):
         x = coeff_ref[whole(nums[MINE])]
-        extra_ref[:pao, :] = coeff_ref[whole(nums[EXTRA])]
-        extra_ref[pao:, :] = jnp.zeros((2 * riders, virt), BF16)
+        extra_ref[...] = coeff_ref[whole(nums[EXTRA])]
         whose, second = whole(nums[WHOSE]), whole(nums[SECOND])
         copy = pltpu.make_async_copy(three_in_ref.at[second], block_ref.at[0], sem)
 
@@ -313,7 +311,7 @@
         [
             (VMEM, (virt, aux), BF16),
             (VMEM, (aux, virt), BF16),
-            (VMEM, (pao + 2 * riders, virt), BF16),
+            (VMEM, (pao, virt), BF16),
         ],
         (nums, blocks, three_in, coeff, c_out),
         scratch=[pltpu.VMEM((1, aux, pao), BF16), pltpu.SemaphoreType.DMA],
@@ -380,7 +378,7 @@
         @pl.when(outside)
         def _():
             k_ref[:, :part] = mxu(first, low_ref[:aux, :], NN) * aux_scale
-            k_ref[:, part:] = mxu(first, high_ref[:aux, :], NN) * aux_scale
+            k_ref[:, part:] = mxu(first, high_ref[...], NN) * aux_scale
 
         @pl.when(jnp.logical_not(outside))
         def _():
@@ -417,7 +415,7 @@
     def extra_out_body(coeff_ref, x_ref, after_ref, s_ref):
         @pl.when(lax.axis_index("role") > 0)
         def _():
-            overlaps(x_ref[:pao, :], coeff_ref, s_ref)
+            overlaps(x_ref[...], coeff_ref, s_ref)
 
     (se_out,) = call(
         extra_out_body,

time: 53.8 us -> 53.3 us (level)
  starting transfers between devices: 27.6 us -> 24.6 us
  Pallas kernels: 14.2 us -> 15.5 us
  local copies, waits for them, and re-layouts: 0.7 us -> 1.97 us
    ppermute x7, starting transfers between devices: 16.4 us -> 13.2 us  [outer(): return lax.ppermute(x, 'pairs', list(enumerate(outer_of)))]
    pallas_call x16, Pallas kernels: 14.2 us -> 15.5 us  [call(): pl.pallas_call(body, in_specs=ins, out_specs=[spec for spec, _, _ in outs...]
    unnamed x12 -> x14, local copies, waits for them, and re-layouts: 0.7 us -> 1.97 us
  transfers between devices with their start and end apart: 19 -> 19, of which waited for: 5 -> 5; matrix products, arithmetic and copies ran while one was open for 0% -> 0% of each run, Pallas kernels for 24% -> 26%
where the time goes in v10:
time: 53.3 us; the launch traced here: 53.1 us
  starting transfers between devices  24.6 us (46%)
  Pallas kernels  15.5 us (29%)
  waiting for transfers between devices  10.1 us (19%)
  local copies, waits for them, and re-layouts  1.97 us (4%)
  between operations  0.92 us (2%)
    pallas_call x16, Pallas kernels, call(): pl.pallas_call(body, in_specs=ins, out_specs=[spec for spec, _, _ in outs...  15.5 us
    ppermute x7, starting transfers between devices, outer(): return lax.ppermute(x, 'pairs', list(enumerate(outer_of)))  13.2 us
    ppermute x7, waiting for transfers between devices, outer(): return lax.ppermute(x, 'pairs', list(enumerate(outer_of)))  9.04 us
    ppermute x3, starting transfers between devices, local(): rests = [lax.ppermute(rest_b, 'role', [(0, s)]) for s in range(1, roles)]  6.13 us
    ppermute x3, starting transfers between devices, swap(): return lax.ppermute(x, 'role', [(i, i ^ by) for i in range(roles)])  3.55 us
    unnamed x14, local copies, waits for them, and re-layouts  1.97 us
    ppermute x6, starting transfers between devices, inner(): return lax.ppermute(x, 'pairs', list(enumerate(inner_of)))  1.72 us
  transfers between devices with their start and end apart: 19, of which 5 were waited for; matrix products, arithmetic and copies ran while one was open for 0% of the time, Pallas kernels for 26%

profile of v10, /device:TPU:0, one launch (start us, length us, event | category | flops | bytes accessed | tf_op | source)
XLA Modules:
  0.0 53.1 jit_solution(11136470591720128919)
XLA Ops:
  0.6 0.5 collective-permute-start.4
  1.1 0.1 collective-permute-start
  1.2 0.4 collective-permute-start.1
  1.7 2.4 %shard_map.113 = (bf16[528,128]{1,0:T(8,128)(2,1)}, bf16[512,128]{1,0:T(8,128)(2,1)}, f32[30]{0:T(128)}) custom-call(s32[4]{0:T(128)} %owner_hbm.1, s32[2,4]{1,0:T(2,128)} %bitcast.1, s32[4,8]{1,0:T(4,128)} %partner_hbm.1, f32[4,8]{1,0:T(4,128)} %coupling_hbm.1, f32[16]{0:T(128)} %eps_hbm.1, s32[4]{0:T(128)} %nvirt_hbm.1, bf16[4,512,256]{2,1,0:T(8,128)(2,1)} %coeff_ref.11), custom_call_target="tpu_custom_call" | custom-call | flops 1 | bytes 1 | tf_op jit(solution)/shard_map/pallas_call | solution.py:33
  4.1 4.8 %collective-permute-start.2 = (bf16[528,128]{1,0:T(8,128)(2,1)}, bf16[528,128]{1,0:T(8,128)(2,1)S(1)}, u32[]{:S(2)}, u32[]{:S(2)}) collective-permute-start(bf16[528,128]{1,0:T(8,128)(2,1)} %get-tuple-element.26), channel_id=1, source_target_pairs={{0,7},{1,2},{2,1},{3,4},{4,3},{5,6},{6,5},{7,0},{8,15},{9,10},{10,... | collective-permute-start | bytes 405512 | tf_op jit(solution)/shard_map/ppermute | solution.py:73
  8.9 0.1 collective-permute-start.3
  9.0 0.7 %copy-done.2 = f32[30]{0:T(128)S(1)} copy-done((f32[30]{0:T(128)S(1)}, f32[30]{0:T(128)}, u32[]{:S(2)}) %copy-start.2) | copy-done | bytes 144
  9.6 1.6 %shard_map.114.three_ref = bf16[2,1024,512]{2,1,0:T(8,128)(2,1)S(1)} custom-call(bf16[2,1024,512]{2,1,0:T(8,128)(2,1)} %three_ref.1, f32[30]{0:T(128)S(1)} %copy-done.2), custom_call_target="tpu_custom_call" | custom-call | flops 1 | bytes 1 | tf_op jit(solution)/shard_map/pallas_call | solution.py:33
  11.2 0.0 copy-start
  11.2 0.0 copy-start.1
  11.2 1.3 %collective-permute-done.2.x_ref.low_ref = bf16[528,128]{1,0:T(8,128)(2,1)S(1)} collective-permute-done((bf16[528,128]{1,0:T(8,128)(2,1)}, bf16[528,128]{1,0:T(8,128)(2,1)S(1)}, u32[]{:S(2)}, u32[]{:S(2)}) %collective-permute-start.2) | collective-permute-done | bytes 135200 | tf_op jit(solution)/shard_map/ppermute | solution.py:73
  12.5 0.5 shard_map.115.after_ref
  13.0 0.0 copy-start.6
  13.1 0.0 copy-start.3
  13.1 3.2 %collective-permute-start.5 = (bf16[1040,128]{1,0:T(8,128)(2,1)S(1)}, bf16[1040,128]{1,0:T(8,128)(2,1)S(1)}, u32[]{:S(2)}, u32[]{:S(2)}) collective-permute-start(bf16[1040,128]{1,0:T(8,128)(2,1)S(1)} %shard_map.115.after_ref), channel_id=1, source_target_pairs={{0,7},{1,2},{2,1},{3,4},{4,3},{5,6},{6,5},{7,0},{8,15},{9,10},{10,... | collective-permute-start | bytes 798728 | tf_op jit(solution)/shard_map/ppermute | solution.py:73
  16.3 0.0 collective-permute-done.3.x_ref.high_ref
  16.3 0.5 shard_map.116.after_ref
  16.8 1.4 %collective-permute-start.6 = (bf16[1024,128]{1,0:T(8,128)(2,1)S(1)}, bf16[1024,128]{1,0:T(8,128)(2,1)S(1)}, u32[]{:S(2)}, u32[]{:S(2)}) collective-permute-start(bf16[1024,128]{1,0:T(8,128)(2,1)S(1)} %shard_map.116.after_ref), channel_id=1, source_target_pairs={{0,7},{1,2},{2,1},{3,4},{4,3},{5,6},{6,5},{7,0},{8,15},{9,10},{10,... | collective-permute-start | bytes 786440 | tf_op jit(solution)/shard_map/ppermute | solution.py:73
  18.2 0.0 copy-done
  18.2 0.0 copy-done.1
  18.2 0.9 %shard_map.117 = (bf16[4,256,256]{2,1,0:T(8,128)(2,1)S(1)}, bf16[272,256]{1,0:T(8,128)(2,1)S(1)}) custom-call(bf16[4,512,256]{2,1,0:T(8,128)(2,1)S(1)} %copy-done, bf16[4,256,256]{2,1,0:T(8,128)(2,1)S(1)} %copy-done.1, bf16[528,128]{1,0:T(8,128)(2,1)S(1)} %collective-permute-done.2.x_ref.low_ref, bf16[512,128]{1,0:T(8,128)(2,1)S(1)} %collective-permute-done.3.x_ref.high_ref, ...), custom_call_target="tpu_custom_call" | custom-call | flops 1 | bytes 1 | tf_op jit(solution)/shard_map/pallas_call | solution.py:33
  19.1 0.0 collective-permute-done.1.amps_in_ref
  19.1 0.0 copy-start.4
  19.2 2.3 %collective-permute-start.7 = (bf16[272,256]{1,0:T(8,128)(2,1)S(1)}, bf16[272,256]{1,0:T(8,128)(2,1)S(1)}, u32[]{:S(2)}, u32[]{:S(2)}) collective-permute-start(bf16[272,256]{1,0:T(8,128)(2,1)S(1)} %get-tuple-element.28.after_ref), channel_id=1, source_target_pairs={{0,7},{1,2},{2,1},{3,4},{4,3},{5,6},{6,5},{7,0},{8,15},{9,10},{10,... | collective-permute-start | bytes 417800 | tf_op jit(solution)/shard_map/ppermute | solution.py:73
  21.4 0.0 collective-permute-done.4.three_in_ref
  21.4 0.0 copy-done.6
  21.4 0.1 collective-permute-start.8
  21.5 1.3 %copy-done.5 = bf16[2,1024,512]{2,1,0:T(8,128)(2,1)} copy-done((bf16[2,1024,512]{2,1,0:T(8,128)(2,1)}, bf16[2,1024,512]{2,1,0:T(8,128)(2,1)S(1)}, u32[]{:S(2)}) %copy-start.5) | copy-done | bytes 2097176
  22.8 0.0 copy-done.3
  22.8 2.5 %shard_map.119 = (bf16[256,1024]{1,0:T(8,128)(2,1)S(1)}, bf16[1024,256]{1,0:T(8,128)(2,1)S(1)}, bf16[512,256]{1,0:T(8,128)(2,1)S(1)}) custom-call(f32[30]{0:T(128)S(1)} %copy-done.3, bf16[2,1024,512]{2,1,0:T(8,128)(2,1)S(1)} %shard_map.114.three_ref, bf16[2,1024,512]{2,1,0:T(8,128)(2,1)} %copy-done.5, bf16[4,512,256]{2,1,0:T(8,128)(2,1)S(1)} %copy-done, ...), custom_call_target="tpu_custom_call" | custom-call | flops 1 | bytes 1 | tf_op jit(solution)/shard_map/pallas_call | solution.py:33
  25.3 0.0 collective-permute-done.coeff_in_ref.in_ref
  25.3 0.1 collective-permute-start.12
  25.4 0.0 copy-done.4
  25.4 2.0 %shard_map.118 = (bf16[4,256,256]{2,1,0:T(8,128)(2,1)S(1)}, f32[256,256]{1,0:T(8,128)S(1)}, f32[256,256]{1,0:T(8,128)S(1)}, f32[256,256]{1,0:T(8,128)S(1)}) custom-call(f32[30]{0:T(128)S(1)} %copy-done.3, bf16[4,512,256]{2,1,0:T(8,128)(2,1)S(1)} %copy-done, bf16[4,512,256]{2,1,0:T(8,128)(2,1)S(1)} %collective-permute-done.coeff_in_ref.in_ref, ...), custom_call_target="tpu_custom_call" | custom-call | flops 1 | bytes 1 | tf_op jit(solution)/shard_map/pallas_call | solution.py:33
  27.4 0.0 collective-permute-done.8.low_ref
  27.4 0.6 %shard_map.120 = (bf16[4,256,256]{2,1,0:T(8,128)(2,1)S(1)}, bf16[4,256,256]{2,1,0:T(8,128)(2,1)S(1)}, bf16[4,256,256]{2,1,0:T(8,128)(2,1)S(1)}) custom-call(f32[30]{0:T(128)S(1)} %copy-done.3, bf16[4,512,256]{2,1,0:T(8,128)(2,1)S(1)} %copy-done, bf16[4,512,256]{2,1,0:T(8,128)(2,1)S(1)} %collective-permute-done.coeff_in_ref.in_ref, ...), custom_call_target="tpu_custom_call" | custom-call | flops 1 | bytes 1 | tf_op jit(solution)/shard_map/pallas_call | solution.py:33
  28.0 4.2 %collective-permute-done.7.co_ref = bf16[272,256]{1,0:T(8,128)(2,1)S(1)} collective-permute-done((bf16[272,256]{1,0:T(8,128)(2,1)S(1)}, bf16[272,256]{1,0:T(8,128)(2,1)S(1)}, u32[]{:S(2)}, u32[]{:S(2)}) %collective-permute-start.7) | collective-permute-done | bytes 139296 | tf_op jit(solution)/shard_map/ppermute | solution.py:73
  32.2 0.0 collective-permute-done.6.high_ref
  32.2 0.0 collective-permute-done.5.low_ref
  32.2 1.0 %shard_map.121 = (bf16[256,256]{1,0:T(8,128)(2,1)S(1)}, f32[256,256]{1,0:T(8,128)S(1)}) custom-call(f32[30]{0:T(128)S(1)} %copy-done.3, bf16[256,1024]{1,0:T(8,128)(2,1)S(1)} %get-tuple-element.31.first_ref, bf16[1024,256]{1,0:T(8,128)(2,1)S(1)} %get-tuple-element.32.second_ref, bf16[1040,128]{1,0:T(8,128)(2,1)S(1)} %collective-permute-done.5.low_ref, ...), custom_call_target="tpu_custom_call" | custom-call | flops 1 | bytes 1 | tf_op jit(solution)/shard_map/pallas_call | solution.py:33
  33.2 1.7 %collective-permute-start.9 = (bf16[256,256]{1,0:T(8,128)(2,1)S(1)}, bf16[256,256]{1,0:T(8,128)(2,1)S(1)}, u32[]{:S(2)}, u32[]{:S(2)}) collective-permute-start(bf16[256,256]{1,0:T(8,128)(2,1)S(1)} %get-tuple-element.35.amp_ref.after_ref.refs_0_), channel_id=1, source_target_pairs={{0,8},{8,0},{16,24},{24,16},{1,9},{9,1},{17,25},{25,17},{2,10},{10... | collective-permute-start | bytes 393224 | tf_op jit(solution)/shard_map/ppermute | solution.py:76
  34.9 1.4 %collective-permute-start.10 = (bf16[256,256]{1,0:T(8,128)(2,1)S(1)}, bf16[256,256]{1,0:T(8,128)(2,1)S(1)}, u32[]{:S(2)}, u32[]{:S(2)}) collective-permute-start(bf16[256,256]{1,0:T(8,128)(2,1)S(1)} %get-tuple-element.35.amp_ref.after_ref.refs_0_), channel_id=1, source_target_pairs={{0,16},{8,24},{16,0},{24,8},{1,17},{9,25},{17,1},{25,9},{2,18},{10... | collective-permute-start | bytes 393224 | tf_op jit(solution)/shard_map/ppermute | solution.py:76
  36.2 0.5 collective-permute-start.11
  36.7 0.4 shard_map.122
  37.1 3.5 %collective-permute-start.15 = (bf16[272,256]{1,0:T(8,128)(2,1)S(1)}, bf16[272,256]{1,0:T(8,128)(2,1)S(1)}, u32[]{:S(2)}, u32[]{:S(2)}) collective-permute-start(bf16[272,256]{1,0:T(8,128)(2,1)S(1)} %get-tuple-element.47), channel_id=1, source_target_pairs={{0,8},{1,9},{2,10},{3,11},{4,12},{5,13},{6,14},{7,15}} | collective-permute-start | bytes 417800 | tf_op jit(solution)/shard_map/ppermute | solution.py:413
  40.7 0.0 collective-permute-done.9.refs_1_
  40.7 1.3 %collective-permute-start.16 = (bf16[272,256]{1,0:T(8,128)(2,1)S(1)}, bf16[272,256]{1,0:T(8,128)(2,1)S(1)}, u32[]{:S(2)}, u32[]{:S(2)}) collective-permute-start(bf16[272,256]{1,0:T(8,128)(2,1)S(1)} %get-tuple-element.47), channel_id=1, source_target_pairs={{0,16},{1,17},{2,18},{3,19},{4,20},{5,21},{6,22},{7,23}} | collective-permute-start | bytes 417800 | tf_op jit(solution)/shard_map/ppermute | solution.py:413
  42.0 0.0 collective-permute-done.12.x_ref
  42.0 1.3 %collective-permute-start.17 = (bf16[272,256]{1,0:T(8,128)(2,1)S(1)}, bf16[272,256]{1,0:T(8,128)(2,1)S(1)}, u32[]{:S(2)}, u32[]{:S(2)}) collective-permute-start(bf16[272,256]{1,0:T(8,128)(2,1)S(1)} %get-tuple-element.47), channel_id=1, source_target_pairs={{0,24},{1,25},{2,26},{3,27},{4,28},{5,29},{6,30},{7,31}} | collective-permute-start | bytes 417800 | tf_op jit(solution)/shard_map/ppermute | solution.py:413
  43.3 0.0 collective-permute-done.10.refs_2_
  43.3 0.0 collective-permute-done.11.refs_3_
  43.4 0.6 %shard_map.124.refs_4_ = bf16[2,256,256]{2,1,0:T(8,128)(2,1)S(1)} custom-call(f32[30]{0:T(128)S(1)} %copy-done.3, bf16[528,128]{1,0:T(8,128)(2,1)S(1)} %collective-permute-done.2.x_ref.low_ref, bf16[4,256,256]{2,1,0:T(8,128)(2,1)S(1)} %get-tuple-element.41.s_ref, bf16[4,256,256]{2,1,0:T(8,128)(2,1)S(1)} %shard_map.123.se_ref, ...), custom_call_target="tpu_custom_call" | custom-call | flops 1 | bytes 1 | tf_op jit(solution)/shard_map/pallas_call | solution.py:33
  43.9 1.3 %collective-permute-start.13 = (bf16[2,256,256]{2,1,0:T(8,128)(2,1)S(1)}, bf16[2,256,256]{2,1,0:T(8,128)(2,1)S(1)}, u32[]{:S(2)}, u32[]{:S(2)}) collective-permute-start(bf16[2,256,256]{2,1,0:T(8,128)(2,1)S(1)} %shard_map.124.refs_4_), channel_id=1, source_target_pairs={{0,7},{1,2},{2,1},{3,4},{4,3},{5,6},{6,5},{7,0},{8,15},{9,10},{10,... | collective-permute-start | bytes 786440 | tf_op jit(solution)/shard_map/ppermute | solution.py:73
  45.3 0.6 %shard_map.125 = (bf16[272,256]{1,0:T(8,128)(2,1)S(1)}, bf16[272,256]{1,0:T(8,128)(2,1)S(1)}) custom-call(f32[30]{0:T(128)S(1)} %copy-done.3, bf16[528,128]{1,0:T(8,128)(2,1)S(1)} %collective-permute-done.8.low_ref, bf16[4,256,256]{2,1,0:T(8,128)(2,1)S(1)} %get-tuple-element.39.s_ref, bf16[4,256,256]{2,1,0:T(8,128)(2,1)S(1)} %get-tuple-element.40.se_ref, ...), custom_call_target="tpu_custom_call" | custom-call | flops 1 | bytes 1 | tf_op jit(solution)/shard_map/pallas_call | solution.py:33
  45.8 0.1 collective-permute-start.14
  45.9 0.6 %shard_map.126 = (f32[256,256]{1,0:T(8,128)S(1)}, f32[256,256]{1,0:T(8,128)S(1)}) custom-call(f32[30]{0:T(128)S(1)} %copy-done.3, f32[256,256]{1,0:T(8,128)S(1)} %get-tuple-element.37.rest_ref, bf16[4,256,256]{2,1,0:T(8,128)(2,1)S(1)} %get-tuple-element.38.s_ref, bf16[4,256,256]{2,1,0:T(8,128)(2,1)S(1)} %get-tuple-element.34.after_ref.se_ref, ...), custom_call_target="tpu_custom_call" | custom-call | flops 1 | bytes 1 | tf_op jit(solution)/shard_map/pallas_call | solution.py:33
  46.5 0.0 collective-permute-done.15.refs_1_.refs_0_
  46.5 0.0 collective-permute-done.16.refs_2_.refs_1_
  46.5 0.0 collective-permute-done.17.refs_3_.refs_2_
  46.5 0.6 %collective-permute-start.18 = (bf16[272,256]{1,0:T(8,128)(2,1)S(1)}, bf16[272,256]{1,0:T(8,128)(2,1)S(1)}, u32[]{:S(2)}, u32[]{:S(2)}) collective-permute-start(bf16[272,256]{1,0:T(8,128)(2,1)S(1)} %shard_map.127), channel_id=1, source_target_pairs={{0,1},{1,0},{2,3},{3,2},{4,5},{5,4},{6,7},{7,6},{8,9},{9,8},{10,11... | collective-permute-start | bytes 417800 | tf_op jit(solution)/shard_map/ppermute | solution.py:70
  47.1 0.2 collective-permute-done.14.ci_ref
  47.2 0.8 %collective-permute-done.18.cei_ref = bf16[272,256]{1,0:T(8,128)(2,1)S(1)} collective-permute-done((bf16[272,256]{1,0:T(8,128)(2,1)S(1)}, bf16[272,256]{1,0:T(8,128)(2,1)S(1)}, u32[]{:S(2)}, u32[]{:S(2)}) %collective-permute-start.18) | collective-permute-done | bytes 139296 | tf_op jit(solution)/shard_map/ppermute | solution.py:70
  48.1 3.5 %collective-permute-done.13.co_ref = bf16[2,256,256]{2,1,0:T(8,128)(2,1)S(1)} collective-permute-done((bf16[2,256,256]{2,1,0:T(8,128)(2,1)S(1)}, bf16[2,256,256]{2,1,0:T(8,128)(2,1)S(1)}, u32[]{:S(2)}, u32[]{:S(2)}) %collective-permute-start.13) | collective-permute-done | bytes 262176 | tf_op jit(solution)/shard_map/ppermute | solution.py:73
  51.6 1.5 %shard_map.128 = (bf16[2,256,256]{2,1,0:T(8,128)(2,1)}, bf16[2,512,256]{2,1,0:T(8,128)(2,1)}) custom-call(f32[30]{0:T(128)S(1)} %copy-done.3, bf16[4,512,256]{2,1,0:T(8,128)(2,1)S(1)} %copy-done, f32[256,256]{1,0:T(8,128)S(1)} %get-tuple-element.29.gain_ref, f32[256,256]{1,0:T(8,128)S(1)} %get-tuple-element.30.gain_extra_ref, ...), custom_call_target="tpu_custom_call" | custom-call | flops 1 | bytes 1 | tf_op jit(solution)/shard_map/pallas_call | solution.py:33
  (4 shorter events, 0.0 us)
Async XLA Ops:
  0.6 20.8 %collective-permute-start.4 = (bf16[2,1024,512]{2,1,0:T(8,128)(2,1)}, bf16[2,1024,512]{2,1,0:T(8,128)(2,1)S(1)}, u32[]{:S(2)}, u32[]{:S(2)}) collective-permute-start(bf16[2,1024,512]{2,1,0:T(8,128)(2,1)} %three_ref.1), channel_id=1, source_target_pairs={{0,1},{1,0},{2,3},{3,2},{4,5},{5,4},{6,7},{7,6},{8,9},{9,8},{10,11... | collective-permute-start | bytes 6291464 | tf_op jit(solution)/shard_map/ppermute | solution.py:70
  1.1 24.1 %collective-permute-start = (bf16[4,512,256]{2,1,0:T(8,128)(2,1)}, bf16[4,512,256]{2,1,0:T(8,128)(2,1)S(1)}, u32[]{:S(2)}, u32[]{:S(2)}) collective-permute-start(bf16[4,512,256]{2,1,0:T(8,128)(2,1)} %coeff_ref.11), channel_id=1, source_target_pairs={{0,1},{1,0},{2,3},{3,2},{4,5},{5,4},{6,7},{7,6},{8,9},{9,8},{10,11... | collective-permute-start | bytes 3145736 | tf_op jit(solution)/shard_map/ppermute | solution.py:70
  1.2 17.9 %collective-permute-start.1 = (bf16[4,256,256]{2,1,0:T(8,128)(2,1)}, bf16[4,256,256]{2,1,0:T(8,128)(2,1)S(1)}, u32[]{:S(2)}, u32[]{:S(2)}) collective-permute-start(bf16[4,256,256]{2,1,0:T(8,128)(2,1)} %amps_ref.5), channel_id=1, source_target_pairs={{0,1},{1,0},{2,3},{3,2},{4,5},{5,4},{6,7},{7,6},{8,9},{9,8},{10,11... | collective-permute-start | bytes 1572872 | tf_op jit(solution)/shard_map/ppermute | solution.py:70
  4.1 8.4 %collective-permute-start.2 = (bf16[528,128]{1,0:T(8,128)(2,1)}, bf16[528,128]{1,0:T(8,128)(2,1)S(1)}, u32[]{:S(2)}, u32[]{:S(2)}) collective-permute-start(bf16[528,128]{1,0:T(8,128)(2,1)} %get-tuple-element.26), channel_id=1, source_target_pairs={{0,7},{1,2},{2,1},{3,4},{4,3},{5,6},{6,5},{7,0},{8,15},{9,10},{10,... | collective-permute-start | bytes 405512 | tf_op jit(solution)/shard_map/ppermute | solution.py:73
  8.9 7.4 %collective-permute-start.3 = (bf16[512,128]{1,0:T(8,128)(2,1)}, bf16[512,128]{1,0:T(8,128)(2,1)S(1)}, u32[]{:S(2)}, u32[]{:S(2)}) collective-permute-start(bf16[512,128]{1,0:T(8,128)(2,1)} %get-tuple-element.27), channel_id=1, source_target_pairs={{0,7},{1,2},{2,1},{3,4},{4,3},{5,6},{6,5},{7,0},{8,15},{9,10},{10,... | collective-permute-start | bytes 393224 | tf_op jit(solution)/shard_map/ppermute | solution.py:73
  9.0 0.7 %copy-start.2 = (f32[30]{0:T(128)S(1)}, f32[30]{0:T(128)}, u32[]{:S(2)}) copy-start(f32[30]{0:T(128)} %get-tuple-element.25.after_ref.nums) | copy-start | bytes 364
  11.2 7.0 %copy-start = (bf16[4,512,256]{2,1,0:T(8,128)(2,1)S(1)}, bf16[4,512,256]{2,1,0:T(8,128)(2,1)}, u32[]{:S(2)}) copy-start(bf16[4,512,256]{2,1,0:T(8,128)(2,1)} %coeff_ref.11) | copy-start | bytes 3145732
  11.2 7.0 %copy-start.1 = (bf16[4,256,256]{2,1,0:T(8,128)(2,1)S(1)}, bf16[4,256,256]{2,1,0:T(8,128)(2,1)}, u32[]{:S(2)}) copy-start(bf16[4,256,256]{2,1,0:T(8,128)(2,1)} %amps_ref.5) | copy-start | bytes 1572868
  13.0 8.4 %copy-start.6 = (bf16[528,128]{1,0:T(8,128)(2,1)S(1)}, bf16[528,128]{1,0:T(8,128)(2,1)}, u32[]{:S(2)}) copy-start(bf16[528,128]{1,0:T(8,128)(2,1)} %get-tuple-element.26) | copy-start | bytes 405508
  13.1 9.7 %copy-start.3 = (f32[30]{0:T(128)S(1)}, f32[30]{0:T(128)}, u32[]{:S(2)}) copy-start(f32[30]{0:T(128)} %get-tuple-element.25.after_ref.nums) | copy-start | bytes 364
  13.1 19.1 %collective-permute-start.5 = (bf16[1040,128]{1,0:T(8,128)(2,1)S(1)}, bf16[1040,128]{1,0:T(8,128)(2,1)S(1)}, u32[]{:S(2)}, u32[]{:S(2)}) collective-permute-start(bf16[1040,128]{1,0:T(8,128)(2,1)S(1)} %shard_map.115.after_ref), channel_id=1, source_target_pairs={{0,7},{1,2},{2,1},{3,4},{4,3},{5,6},{6,5},{7,0},{8,15},{9,10},{10,... | collective-permute-start | bytes 798728 | tf_op jit(solution)/shard_map/ppermute | solution.py:73
  16.8 15.4 %collective-permute-start.6 = (bf16[1024,128]{1,0:T(8,128)(2,1)S(1)}, bf16[1024,128]{1,0:T(8,128)(2,1)S(1)}, u32[]{:S(2)}, u32[]{:S(2)}) collective-permute-start(bf16[1024,128]{1,0:T(8,128)(2,1)S(1)} %shard_map.116.after_ref), channel_id=1, source_target_pairs={{0,7},{1,2},{2,1},{3,4},{4,3},{5,6},{6,5},{7,0},{8,15},{9,10},{10,... | collective-permute-start | bytes 786440 | tf_op jit(solution)/shard_map/ppermute | solution.py:73
  19.1 6.3 %copy-start.4 = (f32[4,256]{1,0:T(4,128)S(1)}, f32[4,256]{1,0:T(4,128)}, u32[]{:S(2)}) copy-start(f32[4,256]{1,0:T(4,128)} %eps_ref.1) | copy-start | bytes 12292
  19.2 13.1 %collective-permute-start.7 = (bf16[272,256]{1,0:T(8,128)(2,1)S(1)}, bf16[272,256]{1,0:T(8,128)(2,1)S(1)}, u32[]{:S(2)}, u32[]{:S(2)}) collective-permute-start(bf16[272,256]{1,0:T(8,128)(2,1)S(1)} %get-tuple-element.28.after_ref), channel_id=1, source_target_pairs={{0,7},{1,2},{2,1},{3,4},{4,3},{5,6},{6,5},{7,0},{8,15},{9,10},{10,... | collective-permute-start | bytes 417800 | tf_op jit(solution)/shard_map/ppermute | solution.py:73
  21.4 1.4 %copy-start.5 = (bf16[2,1024,512]{2,1,0:T(8,128)(2,1)}, bf16[2,1024,512]{2,1,0:T(8,128)(2,1)S(1)}, u32[]{:S(2)}) copy-start(bf16[2,1024,512]{2,1,0:T(8,128)(2,1)S(1)} %collective-permute-done.4.three_in_ref) | copy-start | bytes 6291460
  21.4 6.0 %collective-permute-start.8 = (bf16[528,128]{1,0:T(8,128)(2,1)S(1)}, bf16[528,128]{1,0:T(8,128)(2,1)S(1)}, u32[]{:S(2)}, u32[]{:S(2)}) collective-permute-start(bf16[528,128]{1,0:T(8,128)(2,1)S(1)} %copy-done.6), channel_id=1, source_target_pairs={{0,1},{1,0},{2,3},{3,2},{4,5},{5,4},{6,7},{7,6},{8,9},{9,8},{10,11... | collective-permute-start | bytes 405512 | tf_op jit(solution)/shard_map/ppermute | solution.py:70
  25.3 16.7 %collective-permute-start.12 = (bf16[512,256]{1,0:T(8,128)(2,1)S(1)}, bf16[512,256]{1,0:T(8,128)(2,1)S(1)}, u32[]{:S(2)}, u32[]{:S(2)}) collective-permute-start(bf16[512,256]{1,0:T(8,128)(2,1)S(1)} %get-tuple-element.42), channel_id=1, source_target_pairs={{0,7},{1,2},{2,1},{3,4},{4,3},{5,6},{6,5},{7,0},{8,15},{9,10},{10,... | collective-permute-start | bytes 786440 | tf_op jit(solution)/shard_map/ppermute | solution.py:73
  33.2 7.5 %collective-permute-start.9 = (bf16[256,256]{1,0:T(8,128)(2,1)S(1)}, bf16[256,256]{1,0:T(8,128)(2,1)S(1)}, u32[]{:S(2)}, u32[]{:S(2)}) collective-permute-start(bf16[256,256]{1,0:T(8,128)(2,1)S(1)} %get-tuple-element.35.amp_ref.after_ref.refs_0_), channel_id=1, source_target_pairs={{0,8},{8,0},{16,24},{24,16},{1,9},{9,1},{17,25},{25,17},{2,10},{10... | collective-permute-start | bytes 393224 | tf_op jit(solution)/shard_map/ppermute | solution.py:76
  34.9 8.5 %collective-permute-start.10 = (bf16[256,256]{1,0:T(8,128)(2,1)S(1)}, bf16[256,256]{1,0:T(8,128)(2,1)S(1)}, u32[]{:S(2)}, u32[]{:S(2)}) collective-permute-start(bf16[256,256]{1,0:T(8,128)(2,1)S(1)} %get-tuple-element.35.amp_ref.after_ref.refs_0_), channel_id=1, source_target_pairs={{0,16},{8,24},{16,0},{24,8},{1,17},{9,25},{17,1},{25,9},{2,18},{10... | collective-permute-start | bytes 393224 | tf_op jit(solution)/shard_map/ppermute | solution.py:76
  36.2 7.1 %collective-permute-start.11 = (bf16[256,256]{1,0:T(8,128)(2,1)S(1)}, bf16[256,256]{1,0:T(8,128)(2,1)S(1)}, u32[]{:S(2)}, u32[]{:S(2)}) collective-permute-start(bf16[256,256]{1,0:T(8,128)(2,1)S(1)} %get-tuple-element.35.amp_ref.after_ref.refs_0_), channel_id=1, source_target_pairs={{0,24},{8,16},{16,8},{24,0},{1,25},{9,17},{17,9},{25,1},{2,26},{10... | collective-permute-start | bytes 393224 | tf_op jit(solution)/shard_map/ppermute | solution.py:76
  37.1 9.3 %collective-permute-start.15 = (bf16[272,256]{1,0:T(8,128)(2,1)S(1)}, bf16[272,256]{1,0:T(8,128)(2,1)S(1)}, u32[]{:S(2)}, u32[]{:S(2)}) collective-permute-start(bf16[272,256]{1,0:T(8,128)(2,1)S(1)} %get-tuple-element.47), channel_id=1, source_target_pairs={{0,8},{1,9},{2,10},{3,11},{4,12},{5,13},{6,14},{7,15}} | collective-permute-start | bytes 417800 | tf_op jit(solution)/shard_map/ppermute | solution.py:413
  40.7 5.8 %collective-permute-start.16 = (bf16[272,256]{1,0:T(8,128)(2,1)S(1)}, bf16[272,256]{1,0:T(8,128)(2,1)S(1)}, u32[]{:S(2)}, u32[]{:S(2)}) collective-permute-start(bf16[272,256]{1,0:T(8,128)(2,1)S(1)} %get-tuple-element.47), channel_id=1, source_target_pairs={{0,16},{1,17},{2,18},{3,19},{4,20},{5,21},{6,22},{7,23}} | collective-permute-start | bytes 417800 | tf_op jit(solution)/shard_map/ppermute | solution.py:413
  42.0 4.5 %collective-permute-start.17 = (bf16[272,256]{1,0:T(8,128)(2,1)S(1)}, bf16[272,256]{1,0:T(8,128)(2,1)S(1)}, u32[]{:S(2)}, u32[]{:S(2)}) collective-permute-start(bf16[272,256]{1,0:T(8,128)(2,1)S(1)} %get-tuple-element.47), channel_id=1, source_target_pairs={{0,24},{1,25},{2,26},{3,27},{4,28},{5,29},{6,30},{7,31}} | collective-permute-start | bytes 417800 | tf_op jit(solution)/shard_map/ppermute | solution.py:413
  43.9 7.7 %collective-permute-start.13 = (bf16[2,256,256]{2,1,0:T(8,128)(2,1)S(1)}, bf16[2,256,256]{2,1,0:T(8,128)(2,1)S(1)}, u32[]{:S(2)}, u32[]{:S(2)}) collective-permute-start(bf16[2,256,256]{2,1,0:T(8,128)(2,1)S(1)} %shard_map.124.refs_4_), channel_id=1, source_target_pairs={{0,7},{1,2},{2,1},{3,4},{4,3},{5,6},{6,5},{7,0},{8,15},{9,10},{10,... | collective-permute-start | bytes 786440 | tf_op jit(solution)/shard_map/ppermute | solution.py:73
  45.8 1.4 %collective-permute-start.14 = (bf16[272,256]{1,0:T(8,128)(2,1)S(1)}, bf16[272,256]{1,0:T(8,128)(2,1)S(1)}, u32[]{:S(2)}, u32[]{:S(2)}) collective-permute-start(bf16[272,256]{1,0:T(8,128)(2,1)S(1)} %get-tuple-element.43.refs_4_), channel_id=1, source_target_pairs={{0,1},{1,0},{2,3},{3,2},{4,5},{5,4},{6,7},{7,6},{8,9},{9,8},{10,11... | collective-permute-start | bytes 417800 | tf_op jit(solution)/shard_map/ppermute | solution.py:70
  46.5 1.6 %collective-permute-start.18 = (bf16[272,256]{1,0:T(8,128)(2,1)S(1)}, bf16[272,256]{1,0:T(8,128)(2,1)S(1)}, u32[]{:S(2)}, u32[]{:S(2)}) collective-permute-start(bf16[272,256]{1,0:T(8,128)(2,1)S(1)} %shard_map.127), channel_id=1, source_target_pairs={{0,1},{1,0},{2,3},{3,2},{4,5},{5,4},{6,7},{7,6},{8,9},{9,8},{10,11... | collective-permute-start | bytes 417800 | tf_op jit(solution)/shard_map/ppermute | solution.py:70

commit v11 on v10

--- a/solution.py
+++ b/solution.py
@@ -407,9 +407,10 @@
         rest = amp.astype(F32) - both
         out_ref[...] = rest
         out_b_ref[:virt, :] = rest.astype(BF16)
-        out_b_ref[virt:, :] = jnp.zeros((riders, virt), BF16)
-
-    rest, rest_b = call(rest_body, [VMEM, VMEM], [sq_f, longer], (amp, k_first))
+        out_b_ref[virt:, :] = jnp.zeros((2 * riders, virt), BF16)
+
+    longest = (VMEM, (virt + 2 * riders, virt), BF16)
+    rest, rest_b = call(rest_body, [VMEM, VMEM], [sq_f, longest], (amp, k_first))
     rests = [lax.ppermute(rest_b, "role", [(0, s)]) for s in range(1, roles)]
 
     def extra_out_body(coeff_ref, x_ref, after_ref, s_ref):
@@ -470,7 +471,7 @@
         [longer, longer],
         (nums, low_in, s_in, se_in, *amp_roles, cc_out),
     )
-    c_from_in = inner(c_in)
+    c_from_in, ce_from_in = inner(c_in), inner(ce_in)
 
     def own_again_body(nums, rest_ref, s_ref, se_ref, *refs):
         amp_refs, (after_ref, out_ref, out_extra_ref) = refs[:roles], refs[-3:]
@@ -488,12 +489,6 @@
         [sq_f, sq_f],
         (nums, rest, s_own, se_own, *amp_roles, c_in),
     )
-
-    def tell_body(last_ref, *refs):
-        refs[-1][...] = last_ref[...]
-
-    (ce_in,) = call(tell_body, [VMEM] + [ANY] * roles, [longer], (ce_in, rest, *rests))
-    ce_from_in = inner(ce_in)
 
     def last_body(
         nums, coeff_ref, gain_ref, gain_extra_ref, rest_ref, rest_extra_ref, co_ref, ci_ref, cei_ref, *refs

time: 53.3 us -> 52.6 us (0.987)
  waiting for transfers between devices: 10.1 us -> 8 us
  starting transfers between devices: 24.6 us -> 25.9 us
    ppermute x7, waiting for transfers between devices: 9.04 us -> 5.54 us  [outer(): return lax.ppermute(x, 'pairs', list(enumerate(outer_of)))]
    ppermute x3, starting transfers between devices: 6.13 us -> 8.54 us  [local(): rests = [lax.ppermute(rest_b, 'role', [(0, s)]) for s in range(1, roles)]]
    ppermute x3, waiting for transfers between devices: 0.01 us -> 1.51 us  [swap(): return lax.ppermute(x, 'role', [(i, i ^ by) for i in range(roles)])]
    ppermute x7, starting transfers between devices: 13.2 us -> 12.1 us  [outer(): return lax.ppermute(x, 'pairs', list(enumerate(outer_of)))]
    ppermute x6, waiting for transfers between devices: 1.01 us -> 0.02 us  [inner(): return lax.ppermute(x, 'pairs', list(enumerate(inner_of)))]
    ppermute x3, waiting for transfers between devices: 0.01 us -> 0.94 us  [local(): rests = [lax.ppermute(rest_b, 'role', [(0, s)]) for s in range(1, roles)]]
    pallas_call x16 -> x15, Pallas kernels: 15.5 us -> 15.5 us  [call(): pl.pallas_call(body, in_specs=ins, out_specs=[spec for spec, _, _ in outs...]
  transfers between devices with their start and end apart: 19 -> 19, of which waited for: 5 -> 4; matrix products, arithmetic and copies ran while one was open for 0% -> 0% of each run, Pallas kernels for 26% -> 27%
where the time goes in v11:
time: 52.6 us; the launch traced here: 52.3 us
  starting transfers between devices  25.9 us (49%)
  Pallas kernels  15.5 us (29%)
  waiting for transfers between devices  8 us (15%)
  local copies, waits for them, and re-layouts  1.97 us (4%)
  between operations  0.9 us (2%)
    pallas_call x15, Pallas kernels, call(): pl.pallas_call(body, in_specs=ins, out_specs=[spec for spec, _, _ in outs...  15.5 us
    ppermute x7, starting transfers between devices, outer(): return lax.ppermute(x, 'pairs', list(enumerate(outer_of)))  12.1 us
    ppermute x3, starting transfers between devices, local(): rests = [lax.ppermute(rest_b, 'role', [(0, s)]) for s in range(1, roles)]  8.54 us
    ppermute x7, waiting for transfers between devices, outer(): return lax.ppermute(x, 'pairs', list(enumerate(outer_of)))  5.54 us
    ppermute x3, starting transfers between devices, swap(): return lax.ppermute(x, 'role', [(i, i ^ by) for i in range(roles)])  3.55 us
    unnamed x14, local copies, waits for them, and re-layouts  1.97 us
    ppermute x6, starting transfers between devices, inner(): return lax.ppermute(x, 'pairs', list(enumerate(inner_of)))  1.66 us
    ppermute x3, waiting for transfers between devices, swap(): return lax.ppermute(x, 'role', [(i, i ^ by) for i in range(roles)])  1.51 us
  transfers between devices with their start and end apart: 19, of which 4 were waited for; matrix products, arithmetic and copies ran while one was open for 0% of the time, Pallas kernels for 27%

profile of v11, /device:TPU:0, one launch (start us, length us, event | category | flops | bytes accessed | tf_op | source)
XLA Modules:
  0.0 52.3 jit_solution(773904100386636901)
XLA Ops:
  0.6 0.5 collective-permute-start.4
  1.1 0.1 collective-permute-start
  1.2 0.4 collective-permute-start.1
  1.7 2.4 %shard_map.113 = (bf16[528,128]{1,0:T(8,128)(2,1)}, bf16[512,128]{1,0:T(8,128)(2,1)}, f32[30]{0:T(128)}) custom-call(s32[4]{0:T(128)} %owner_hbm.1, s32[2,4]{1,0:T(2,128)} %bitcast.1, s32[4,8]{1,0:T(4,128)} %partner_hbm.1, f32[4,8]{1,0:T(4,128)} %coupling_hbm.1, f32[16]{0:T(128)} %eps_hbm.1, s32[4]{0:T(128)} %nvirt_hbm.1, bf16[4,512,256]{2,1,0:T(8,128)(2,1)} %coeff_ref.11), custom_call_target="tpu_custom_call" | custom-call | flops 1 | bytes 1 | tf_op jit(solution)/shard_map/pallas_call | solution.py:33
  4.1 4.8 %collective-permute-start.2 = (bf16[528,128]{1,0:T(8,128)(2,1)}, bf16[528,128]{1,0:T(8,128)(2,1)S(1)}, u32[]{:S(2)}, u32[]{:S(2)}) collective-permute-start(bf16[528,128]{1,0:T(8,128)(2,1)} %get-tuple-element.26), channel_id=1, source_target_pairs={{0,7},{1,2},{2,1},{3,4},{4,3},{5,6},{6,5},{7,0},{8,15},{9,10},{10,... | collective-permute-start | bytes 405512 | tf_op jit(solution)/shard_map/ppermute | solution.py:73
  8.9 0.1 collective-permute-start.3
  9.0 0.7 %copy-done.2 = f32[30]{0:T(128)S(1)} copy-done((f32[30]{0:T(128)S(1)}, f32[30]{0:T(128)}, u32[]{:S(2)}) %copy-start.2) | copy-done | bytes 144
  9.6 1.6 %shard_map.114.three_ref = bf16[2,1024,512]{2,1,0:T(8,128)(2,1)S(1)} custom-call(bf16[2,1024,512]{2,1,0:T(8,128)(2,1)} %three_ref.1, f32[30]{0:T(128)S(1)} %copy-done.2), custom_call_target="tpu_custom_call" | custom-call | flops 1 | bytes 1 | tf_op jit(solution)/shard_map/pallas_call | solution.py:33
  11.2 0.0 copy-start
  11.2 0.0 copy-start.1
  11.2 1.3 %collective-permute-done.2.x_ref.low_ref = bf16[528,128]{1,0:T(8,128)(2,1)S(1)} collective-permute-done((bf16[528,128]{1,0:T(8,128)(2,1)}, bf16[528,128]{1,0:T(8,128)(2,1)S(1)}, u32[]{:S(2)}, u32[]{:S(2)}) %collective-permute-start.2) | collective-permute-done | bytes 135200 | tf_op jit(solution)/shard_map/ppermute | solution.py:73
  12.5 0.5 shard_map.115.after_ref
  13.0 0.0 copy-start.6
  13.1 0.0 copy-start.3
  13.1 3.2 %collective-permute-start.5 = (bf16[1040,128]{1,0:T(8,128)(2,1)S(1)}, bf16[1040,128]{1,0:T(8,128)(2,1)S(1)}, u32[]{:S(2)}, u32[]{:S(2)}) collective-permute-start(bf16[1040,128]{1,0:T(8,128)(2,1)S(1)} %shard_map.115.after_ref), channel_id=1, source_target_pairs={{0,7},{1,2},{2,1},{3,4},{4,3},{5,6},{6,5},{7,0},{8,15},{9,10},{10,... | collective-permute-start | bytes 798728 | tf_op jit(solution)/shard_map/ppermute | solution.py:73
  16.3 0.0 collective-permute-done.3.x_ref.high_ref
  16.3 0.5 shard_map.116.after_ref
  16.8 1.4 %collective-permute-start.6 = (bf16[1024,128]{1,0:T(8,128)(2,1)S(1)}, bf16[1024,128]{1,0:T(8,128)(2,1)S(1)}, u32[]{:S(2)}, u32[]{:S(2)}) collective-permute-start(bf16[1024,128]{1,0:T(8,128)(2,1)S(1)} %shard_map.116.after_ref), channel_id=1, source_target_pairs={{0,7},{1,2},{2,1},{3,4},{4,3},{5,6},{6,5},{7,0},{8,15},{9,10},{10,... | collective-permute-start | bytes 786440 | tf_op jit(solution)/shard_map/ppermute | solution.py:73
  18.2 0.0 copy-done
  18.2 0.0 copy-done.1
  18.2 0.9 %shard_map.117 = (bf16[4,256,256]{2,1,0:T(8,128)(2,1)S(1)}, bf16[272,256]{1,0:T(8,128)(2,1)S(1)}) custom-call(bf16[4,512,256]{2,1,0:T(8,128)(2,1)S(1)} %copy-done, bf16[4,256,256]{2,1,0:T(8,128)(2,1)S(1)} %copy-done.1, bf16[528,128]{1,0:T(8,128)(2,1)S(1)} %collective-permute-done.2.x_ref.low_ref, bf16[512,128]{1,0:T(8,128)(2,1)S(1)} %collective-permute-done.3.x_ref.high_ref, ...), custom_call_target="tpu_custom_call" | custom-call | flops 1 | bytes 1 | tf_op jit(solution)/shard_map/pallas_call | solution.py:33
  19.1 0.0 collective-permute-done.1.amps_in_ref
  19.1 0.0 copy-start.4
  19.2 2.3 %collective-permute-start.7 = (bf16[272,256]{1,0:T(8,128)(2,1)S(1)}, bf16[272,256]{1,0:T(8,128)(2,1)S(1)}, u32[]{:S(2)}, u32[]{:S(2)}) collective-permute-start(bf16[272,256]{1,0:T(8,128)(2,1)S(1)} %get-tuple-element.28.after_ref), channel_id=1, source_target_pairs={{0,7},{1,2},{2,1},{3,4},{4,3},{5,6},{6,5},{7,0},{8,15},{9,10},{10,... | collective-permute-start | bytes 417800 | tf_op jit(solution)/shard_map/ppermute | solution.py:73
  21.4 0.0 collective-permute-done.4.three_in_ref
  21.4 0.0 copy-done.6
  21.4 0.1 collective-permute-start.8
  21.5 1.3 %copy-done.5 = bf16[2,1024,512]{2,1,0:T(8,128)(2,1)} copy-done((bf16[2,1024,512]{2,1,0:T(8,128)(2,1)}, bf16[2,1024,512]{2,1,0:T(8,128)(2,1)S(1)}, u32[]{:S(2)}) %copy-start.5) | copy-done | bytes 2097176
  22.8 0.0 copy-done.3
  22.8 2.5 %shard_map.119 = (bf16[256,1024]{1,0:T(8,128)(2,1)S(1)}, bf16[1024,256]{1,0:T(8,128)(2,1)S(1)}, bf16[512,256]{1,0:T(8,128)(2,1)S(1)}) custom-call(f32[30]{0:T(128)S(1)} %copy-done.3, bf16[2,1024,512]{2,1,0:T(8,128)(2,1)S(1)} %shard_map.114.three_ref, bf16[2,1024,512]{2,1,0:T(8,128)(2,1)} %copy-done.5, bf16[4,512,256]{2,1,0:T(8,128)(2,1)S(1)} %copy-done, ...), custom_call_target="tpu_custom_call" | custom-call | flops 1 | bytes 1 | tf_op jit(solution)/shard_map/pallas_call | solution.py:33
  25.3 0.0 collective-permute-done.coeff_in_ref.in_ref
  25.3 0.1 collective-permute-start.12
  25.4 0.0 copy-done.4
  25.4 2.0 %shard_map.118 = (bf16[4,256,256]{2,1,0:T(8,128)(2,1)S(1)}, f32[256,256]{1,0:T(8,128)S(1)}, f32[256,256]{1,0:T(8,128)S(1)}, f32[256,256]{1,0:T(8,128)S(1)}) custom-call(f32[30]{0:T(128)S(1)} %copy-done.3, bf16[4,512,256]{2,1,0:T(8,128)(2,1)S(1)} %copy-done, bf16[4,512,256]{2,1,0:T(8,128)(2,1)S(1)} %collective-permute-done.coeff_in_ref.in_ref, ...), custom_call_target="tpu_custom_call" | custom-call | flops 1 | bytes 1 | tf_op jit(solution)/shard_map/pallas_call | solution.py:33
  27.4 0.0 collective-permute-done.8.low_ref
  27.4 0.6 %shard_map.120 = (bf16[4,256,256]{2,1,0:T(8,128)(2,1)S(1)}, bf16[4,256,256]{2,1,0:T(8,128)(2,1)S(1)}, bf16[4,256,256]{2,1,0:T(8,128)(2,1)S(1)}) custom-call(f32[30]{0:T(128)S(1)} %copy-done.3, bf16[4,512,256]{2,1,0:T(8,128)(2,1)S(1)} %copy-done, bf16[4,512,256]{2,1,0:T(8,128)(2,1)S(1)} %collective-permute-done.coeff_in_ref.in_ref, ...), custom_call_target="tpu_custom_call" | custom-call | flops 1 | bytes 1 | tf_op jit(solution)/shard_map/pallas_call | solution.py:33
  28.0 4.2 %collective-permute-done.7.co_ref = bf16[272,256]{1,0:T(8,128)(2,1)S(1)} collective-permute-done((bf16[272,256]{1,0:T(8,128)(2,1)S(1)}, bf16[272,256]{1,0:T(8,128)(2,1)S(1)}, u32[]{:S(2)}, u32[]{:S(2)}) %collective-permute-start.7) | collective-permute-done | bytes 139296 | tf_op jit(solution)/shard_map/ppermute | solution.py:73
  32.2 0.0 collective-permute-done.6.high_ref
  32.2 0.0 collective-permute-done.5.low_ref
  32.2 1.0 %shard_map.121 = (bf16[256,256]{1,0:T(8,128)(2,1)S(1)}, f32[256,256]{1,0:T(8,128)S(1)}) custom-call(f32[30]{0:T(128)S(1)} %copy-done.3, bf16[256,1024]{1,0:T(8,128)(2,1)S(1)} %get-tuple-element.31.first_ref, bf16[1024,256]{1,0:T(8,128)(2,1)S(1)} %get-tuple-element.32.second_ref, bf16[1040,128]{1,0:T(8,128)(2,1)S(1)} %collective-permute-done.5.low_ref, ...), custom_call_target="tpu_custom_call" | custom-call | flops 1 | bytes 1 | tf_op jit(solution)/shard_map/pallas_call | solution.py:33
  33.2 1.6 %collective-permute-start.9 = (bf16[256,256]{1,0:T(8,128)(2,1)S(1)}, bf16[256,256]{1,0:T(8,128)(2,1)S(1)}, u32[]{:S(2)}, u32[]{:S(2)}) collective-permute-start(bf16[256,256]{1,0:T(8,128)(2,1)S(1)} %get-tuple-element.35.amp_ref.after_ref.refs_0_), channel_id=1, source_target_pairs={{0,8},{8,0},{16,24},{24,16},{1,9},{9,1},{17,25},{25,17},{2,10},{10... | collective-permute-start | bytes 393224 | tf_op jit(solution)/shard_map/ppermute | solution.py:76
  34.7 1.5 %collective-permute-start.10 = (bf16[256,256]{1,0:T(8,128)(2,1)S(1)}, bf16[256,256]{1,0:T(8,128)(2,1)S(1)}, u32[]{:S(2)}, u32[]{:S(2)}) collective-permute-start(bf16[256,256]{1,0:T(8,128)(2,1)S(1)} %get-tuple-element.35.amp_ref.after_ref.refs_0_), channel_id=1, source_target_pairs={{0,16},{8,24},{16,0},{24,8},{1,17},{9,25},{17,1},{25,9},{2,18},{10... | collective-permute-start | bytes 393224 | tf_op jit(solution)/shard_map/ppermute | solution.py:76
  36.2 0.5 collective-permute-start.11
  36.7 0.4 shard_map.122
  37.1 3.4 %collective-permute-start.16 = (bf16[288,256]{1,0:T(8,128)(2,1)S(1)}, bf16[288,256]{1,0:T(8,128)(2,1)S(1)}, u32[]{:S(2)}, u32[]{:S(2)}) collective-permute-start(bf16[288,256]{1,0:T(8,128)(2,1)S(1)} %get-tuple-element.47), channel_id=1, source_target_pairs={{0,8},{1,9},{2,10},{3,11},{4,12},{5,13},{6,14},{7,15}} | collective-permute-start | bytes 442376 | tf_op jit(solution)/shard_map/ppermute | solution.py:414
  40.6 0.0 collective-permute-done.12.x_ref
  40.6 0.0 collective-permute-done.9.refs_1_
  40.6 0.0 collective-permute-done.10.refs_2_
  40.6 1.5 %collective-permute-done.11.refs_3_ = bf16[256,256]{1,0:T(8,128)(2,1)S(1)} collective-permute-done((bf16[256,256]{1,0:T(8,128)(2,1)S(1)}, bf16[256,256]{1,0:T(8,128)(2,1)S(1)}, u32[]{:S(2)}, u32[]{:S(2)}) %collective-permute-start.11) | collective-permute-done | bytes 131104 | tf_op jit(solution)/shard_map/ppermute | solution.py:76
  42.1 0.6 %shard_map.124.refs_4_ = bf16[2,256,256]{2,1,0:T(8,128)(2,1)S(1)} custom-call(f32[30]{0:T(128)S(1)} %copy-done.3, bf16[528,128]{1,0:T(8,128)(2,1)S(1)} %collective-permute-done.2.x_ref.low_ref, bf16[4,256,256]{2,1,0:T(8,128)(2,1)S(1)} %get-tuple-element.41.s_ref, bf16[4,256,256]{2,1,0:T(8,128)(2,1)S(1)} %shard_map.123.se_ref, ...), custom_call_target="tpu_custom_call" | custom-call | flops 1 | bytes 1 | tf_op jit(solution)/shard_map/pallas_call | solution.py:33
  42.7 0.3 collective-permute-start.13
  43.0 3.8 %collective-permute-start.17 = (bf16[288,256]{1,0:T(8,128)(2,1)S(1)}, bf16[288,256]{1,0:T(8,128)(2,1)S(1)}, u32[]{:S(2)}, u32[]{:S(2)}) collective-permute-start(bf16[288,256]{1,0:T(8,128)(2,1)S(1)} %get-tuple-element.47), channel_id=1, source_target_pairs={{0,16},{1,17},{2,18},{3,19},{4,20},{5,21},{6,22},{7,23}} | collective-permute-start | bytes 442376 | tf_op jit(solution)/shard_map/ppermute | solution.py:414
  46.8 1.3 %collective-permute-start.18 = (bf16[288,256]{1,0:T(8,128)(2,1)S(1)}, bf16[288,256]{1,0:T(8,128)(2,1)S(1)}, u32[]{:S(2)}, u32[]{:S(2)}) collective-permute-start(bf16[288,256]{1,0:T(8,128)(2,1)S(1)} %get-tuple-element.47), channel_id=1, source_target_pairs={{0,24},{1,25},{2,26},{3,27},{4,28},{5,29},{6,30},{7,31}} | collective-permute-start | bytes 442376 | tf_op jit(solution)/shard_map/ppermute | solution.py:414
  48.1 0.6 %shard_map.125 = (bf16[272,256]{1,0:T(8,128)(2,1)S(1)}, bf16[272,256]{1,0:T(8,128)(2,1)S(1)}) custom-call(f32[30]{0:T(128)S(1)} %copy-done.3, bf16[528,128]{1,0:T(8,128)(2,1)S(1)} %collective-permute-done.8.low_ref, bf16[4,256,256]{2,1,0:T(8,128)(2,1)S(1)} %get-tuple-element.39.s_ref, bf16[4,256,256]{2,1,0:T(8,128)(2,1)S(1)} %get-tuple-element.40.se_ref, ...), custom_call_target="tpu_custom_call" | custom-call | flops 1 | bytes 1 | tf_op jit(solution)/shard_map/pallas_call | solution.py:33
  48.7 0.1 collective-permute-start.14
  48.8 0.0 collective-permute-done.16.refs_0_
  48.8 0.5 collective-permute-start.15
  49.3 0.6 %shard_map.126 = (f32[256,256]{1,0:T(8,128)S(1)}, f32[256,256]{1,0:T(8,128)S(1)}) custom-call(f32[30]{0:T(128)S(1)} %copy-done.3, f32[256,256]{1,0:T(8,128)S(1)} %get-tuple-element.37.rest_ref, bf16[4,256,256]{2,1,0:T(8,128)(2,1)S(1)} %get-tuple-element.38.s_ref, bf16[4,256,256]{2,1,0:T(8,128)(2,1)S(1)} %get-tuple-element.34.after_ref.se_ref, ...), custom_call_target="tpu_custom_call" | custom-call | flops 1 | bytes 1 | tf_op jit(solution)/shard_map/pallas_call | solution.py:33
  49.8 0.0 collective-permute-done.17.refs_1_
  49.8 0.9 %collective-permute-done.18.refs_2_ = bf16[288,256]{1,0:T(8,128)(2,1)S(1)} collective-permute-done((bf16[288,256]{1,0:T(8,128)(2,1)S(1)}, bf16[288,256]{1,0:T(8,128)(2,1)S(1)}, u32[]{:S(2)}, u32[]{:S(2)}) %collective-permute-start.18) | collective-permute-done | bytes 147488 | tf_op jit(solution)/shard_map/ppermute | solution.py:414
  50.8 0.0 collective-permute-done.14.ci_ref
  50.8 0.0 collective-permute-done.15.cei_ref
  50.8 0.0 collective-permute-done.13.co_ref
  50.8 1.5 %shard_map.127 = (bf16[2,256,256]{2,1,0:T(8,128)(2,1)}, bf16[2,512,256]{2,1,0:T(8,128)(2,1)}) custom-call(f32[30]{0:T(128)S(1)} %copy-done.3, bf16[4,512,256]{2,1,0:T(8,128)(2,1)S(1)} %copy-done, f32[256,256]{1,0:T(8,128)S(1)} %get-tuple-element.29.gain_ref, f32[256,256]{1,0:T(8,128)S(1)} %get-tuple-element.30.gain_extra_ref, ...), custom_call_target="tpu_custom_call" | custom-call | flops 1 | bytes 1 | tf_op jit(solution)/shard_map/pallas_call | solution.py:33
  (3 shorter events, 0.0 us)
Async XLA Ops:
  0.6 20.8 %collective-permute-start.4 = (bf16[2,1024,512]{2,1,0:T(8,128)(2,1)}, bf16[2,1024,512]{2,1,0:T(8,128)(2,1)S(1)}, u32[]{:S(2)}, u32[]{:S(2)}) collective-permute-start(bf16[2,1024,512]{2,1,0:T(8,128)(2,1)} %three_ref.1), channel_id=1, source_target_pairs={{0,1},{1,0},{2,3},{3,2},{4,5},{5,4},{6,7},{7,6},{8,9},{9,8},{10,11... | collective-permute-start | bytes 6291464 | tf_op jit(solution)/shard_map/ppermute | solution.py:70
  1.1 24.1 %collective-permute-start = (bf16[4,512,256]{2,1,0:T(8,128)(2,1)}, bf16[4,512,256]{2,1,0:T(8,128)(2,1)S(1)}, u32[]{:S(2)}, u32[]{:S(2)}) collective-permute-start(bf16[4,512,256]{2,1,0:T(8,128)(2,1)} %coeff_ref.11), channel_id=1, source_target_pairs={{0,1},{1,0},{2,3},{3,2},{4,5},{5,4},{6,7},{7,6},{8,9},{9,8},{10,11... | collective-permute-start | bytes 3145736 | tf_op jit(solution)/shard_map/ppermute | solution.py:70
  1.2 17.9 %collective-permute-start.1 = (bf16[4,256,256]{2,1,0:T(8,128)(2,1)}, bf16[4,256,256]{2,1,0:T(8,128)(2,1)S(1)}, u32[]{:S(2)}, u32[]{:S(2)}) collective-permute-start(bf16[4,256,256]{2,1,0:T(8,128)(2,1)} %amps_ref.5), channel_id=1, source_target_pairs={{0,1},{1,0},{2,3},{3,2},{4,5},{5,4},{6,7},{7,6},{8,9},{9,8},{10,11... | collective-permute-start | bytes 1572872 | tf_op jit(solution)/shard_map/ppermute | solution.py:70
  4.1 8.4 %collective-permute-start.2 = (bf16[528,128]{1,0:T(8,128)(2,1)}, bf16[528,128]{1,0:T(8,128)(2,1)S(1)}, u32[]{:S(2)}, u32[]{:S(2)}) collective-permute-start(bf16[528,128]{1,0:T(8,128)(2,1)} %get-tuple-element.26), channel_id=1, source_target_pairs={{0,7},{1,2},{2,1},{3,4},{4,3},{5,6},{6,5},{7,0},{8,15},{9,10},{10,... | collective-permute-start | bytes 405512 | tf_op jit(solution)/shard_map/ppermute | solution.py:73
  8.9 7.4 %collective-permute-start.3 = (bf16[512,128]{1,0:T(8,128)(2,1)}, bf16[512,128]{1,0:T(8,128)(2,1)S(1)}, u32[]{:S(2)}, u32[]{:S(2)}) collective-permute-start(bf16[512,128]{1,0:T(8,128)(2,1)} %get-tuple-element.27), channel_id=1, source_target_pairs={{0,7},{1,2},{2,1},{3,4},{4,3},{5,6},{6,5},{7,0},{8,15},{9,10},{10,... | collective-permute-start | bytes 393224 | tf_op jit(solution)/shard_map/ppermute | solution.py:73
  9.0 0.7 %copy-start.2 = (f32[30]{0:T(128)S(1)}, f32[30]{0:T(128)}, u32[]{:S(2)}) copy-start(f32[30]{0:T(128)} %get-tuple-element.25.after_ref.nums) | copy-start | bytes 364
  11.2 7.0 %copy-start = (bf16[4,512,256]{2,1,0:T(8,128)(2,1)S(1)}, bf16[4,512,256]{2,1,0:T(8,128)(2,1)}, u32[]{:S(2)}) copy-start(bf16[4,512,256]{2,1,0:T(8,128)(2,1)} %coeff_ref.11) | copy-start | bytes 3145732
  11.2 7.0 %copy-start.1 = (bf16[4,256,256]{2,1,0:T(8,128)(2,1)S(1)}, bf16[4,256,256]{2,1,0:T(8,128)(2,1)}, u32[]{:S(2)}) copy-start(bf16[4,256,256]{2,1,0:T(8,128)(2,1)} %amps_ref.5) | copy-start | bytes 1572868
  13.0 8.4 %copy-start.6 = (bf16[528,128]{1,0:T(8,128)(2,1)S(1)}, bf16[528,128]{1,0:T(8,128)(2,1)}, u32[]{:S(2)}) copy-start(bf16[528,128]{1,0:T(8,128)(2,1)} %get-tuple-element.26) | copy-start | bytes 405508
  13.1 9.7 %copy-start.3 = (f32[30]{0:T(128)S(1)}, f32[30]{0:T(128)}, u32[]{:S(2)}) copy-start(f32[30]{0:T(128)} %get-tuple-element.25.after_ref.nums) | copy-start | bytes 364
  13.1 19.1 %collective-permute-start.5 = (bf16[1040,128]{1,0:T(8,128)(2,1)S(1)}, bf16[1040,128]{1,0:T(8,128)(2,1)S(1)}, u32[]{:S(2)}, u32[]{:S(2)}) collective-permute-start(bf16[1040,128]{1,0:T(8,128)(2,1)S(1)} %shard_map.115.after_ref), channel_id=1, source_target_pairs={{0,7},{1,2},{2,1},{3,4},{4,3},{5,6},{6,5},{7,0},{8,15},{9,10},{10,... | collective-permute-start | bytes 798728 | tf_op jit(solution)/shard_map/ppermute | solution.py:73
  16.8 15.4 %collective-permute-start.6 = (bf16[1024,128]{1,0:T(8,128)(2,1)S(1)}, bf16[1024,128]{1,0:T(8,128)(2,1)S(1)}, u32[]{:S(2)}, u32[]{:S(2)}) collective-permute-start(bf16[1024,128]{1,0:T(8,128)(2,1)S(1)} %shard_map.116.after_ref), channel_id=1, source_target_pairs={{0,7},{1,2},{2,1},{3,4},{4,3},{5,6},{6,5},{7,0},{8,15},{9,10},{10,... | collective-permute-start | bytes 786440 | tf_op jit(solution)/shard_map/ppermute | solution.py:73
  19.1 6.3 %copy-start.4 = (f32[4,256]{1,0:T(4,128)S(1)}, f32[4,256]{1,0:T(4,128)}, u32[]{:S(2)}) copy-start(f32[4,256]{1,0:T(4,128)} %eps_ref.1) | copy-start | bytes 12292
  19.2 13.1 %collective-permute-start.7 = (bf16[272,256]{1,0:T(8,128)(2,1)S(1)}, bf16[272,256]{1,0:T(8,128)(2,1)S(1)}, u32[]{:S(2)}, u32[]{:S(2)}) collective-permute-start(bf16[272,256]{1,0:T(8,128)(2,1)S(1)} %get-tuple-element.28.after_ref), channel_id=1, source_target_pairs={{0,7},{1,2},{2,1},{3,4},{4,3},{5,6},{6,5},{7,0},{8,15},{9,10},{10,... | collective-permute-start | bytes 417800 | tf_op jit(solution)/shard_map/ppermute | solution.py:73
  21.4 1.4 %copy-start.5 = (bf16[2,1024,512]{2,1,0:T(8,128)(2,1)}, bf16[2,1024,512]{2,1,0:T(8,128)(2,1)S(1)}, u32[]{:S(2)}) copy-start(bf16[2,1024,512]{2,1,0:T(8,128)(2,1)S(1)} %collective-permute-done.4.three_in_ref) | copy-start | bytes 6291460
  21.4 6.0 %collective-permute-start.8 = (bf16[528,128]{1,0:T(8,128)(2,1)S(1)}, bf16[528,128]{1,0:T(8,128)(2,1)S(1)}, u32[]{:S(2)}, u32[]{:S(2)}) collective-permute-start(bf16[528,128]{1,0:T(8,128)(2,1)S(1)} %copy-done.6), channel_id=1, source_target_pairs={{0,1},{1,0},{2,3},{3,2},{4,5},{5,4},{6,7},{7,6},{8,9},{9,8},{10,11... | collective-permute-start | bytes 405512 | tf_op jit(solution)/shard_map/ppermute | solution.py:70
  25.3 15.2 %collective-permute-start.12 = (bf16[512,256]{1,0:T(8,128)(2,1)S(1)}, bf16[512,256]{1,0:T(8,128)(2,1)S(1)}, u32[]{:S(2)}, u32[]{:S(2)}) collective-permute-start(bf16[512,256]{1,0:T(8,128)(2,1)S(1)} %get-tuple-element.42), channel_id=1, source_target_pairs={{0,7},{1,2},{2,1},{3,4},{4,3},{5,6},{6,5},{7,0},{8,15},{9,10},{10,... | collective-permute-start | bytes 786440 | tf_op jit(solution)/shard_map/ppermute | solution.py:73
  33.2 7.4 %collective-permute-start.9 = (bf16[256,256]{1,0:T(8,128)(2,1)S(1)}, bf16[256,256]{1,0:T(8,128)(2,1)S(1)}, u32[]{:S(2)}, u32[]{:S(2)}) collective-permute-start(bf16[256,256]{1,0:T(8,128)(2,1)S(1)} %get-tuple-element.35.amp_ref.after_ref.refs_0_), channel_id=1, source_target_pairs={{0,8},{8,0},{16,24},{24,16},{1,9},{9,1},{17,25},{25,17},{2,10},{10... | collective-permute-start | bytes 393224 | tf_op jit(solution)/shard_map/ppermute | solution.py:76
  34.7 5.9 %collective-permute-start.10 = (bf16[256,256]{1,0:T(8,128)(2,1)S(1)}, bf16[256,256]{1,0:T(8,128)(2,1)S(1)}, u32[]{:S(2)}, u32[]{:S(2)}) collective-permute-start(bf16[256,256]{1,0:T(8,128)(2,1)S(1)} %get-tuple-element.35.amp_ref.after_ref.refs_0_), channel_id=1, source_target_pairs={{0,16},{8,24},{16,0},{24,8},{1,17},{9,25},{17,1},{25,9},{2,18},{10... | collective-permute-start | bytes 393224 | tf_op jit(solution)/shard_map/ppermute | solution.py:76
  36.2 5.9 %collective-permute-start.11 = (bf16[256,256]{1,0:T(8,128)(2,1)S(1)}, bf16[256,256]{1,0:T(8,128)(2,1)S(1)}, u32[]{:S(2)}, u32[]{:S(2)}) collective-permute-start(bf16[256,256]{1,0:T(8,128)(2,1)S(1)} %get-tuple-element.35.amp_ref.after_ref.refs_0_), channel_id=1, source_target_pairs={{0,24},{8,16},{16,8},{24,0},{1,25},{9,17},{17,9},{25,1},{2,26},{10... | collective-permute-start | bytes 393224 | tf_op jit(solution)/shard_map/ppermute | solution.py:76
  37.1 11.6 %collective-permute-start.16 = (bf16[288,256]{1,0:T(8,128)(2,1)S(1)}, bf16[288,256]{1,0:T(8,128)(2,1)S(1)}, u32[]{:S(2)}, u32[]{:S(2)}) collective-permute-start(bf16[288,256]{1,0:T(8,128)(2,1)S(1)} %get-tuple-element.47), channel_id=1, source_target_pairs={{0,8},{1,9},{2,10},{3,11},{4,12},{5,13},{6,14},{7,15}} | collective-permute-start | bytes 442376 | tf_op jit(solution)/shard_map/ppermute | solution.py:414
  42.7 8.1 %collective-permute-start.13 = (bf16[2,256,256]{2,1,0:T(8,128)(2,1)S(1)}, bf16[2,256,256]{2,1,0:T(8,128)(2,1)S(1)}, u32[]{:S(2)}, u32[]{:S(2)}) collective-permute-start(bf16[2,256,256]{2,1,0:T(8,128)(2,1)S(1)} %shard_map.124.refs_4_), channel_id=1, source_target_pairs={{0,7},{1,2},{2,1},{3,4},{4,3},{5,6},{6,5},{7,0},{8,15},{9,10},{10,... | collective-permute-start | bytes 786440 | tf_op jit(solution)/shard_map/ppermute | solution.py:73
  43.0 6.9 %collective-permute-start.17 = (bf16[288,256]{1,0:T(8,128)(2,1)S(1)}, bf16[288,256]{1,0:T(8,128)(2,1)S(1)}, u32[]{:S(2)}, u32[]{:S(2)}) collective-permute-start(bf16[288,256]{1,0:T(8,128)(2,1)S(1)} %get-tuple-element.47), channel_id=1, source_target_pairs={{0,16},{1,17},{2,18},{3,19},{4,20},{5,21},{6,22},{7,23}} | collective-permute-start | bytes 442376 | tf_op jit(solution)/shard_map/ppermute | solution.py:414
  46.8 4.0 %collective-permute-start.18 = (bf16[288,256]{1,0:T(8,128)(2,1)S(1)}, bf16[288,256]{1,0:T(8,128)(2,1)S(1)}, u32[]{:S(2)}, u32[]{:S(2)}) collective-permute-start(bf16[288,256]{1,0:T(8,128)(2,1)S(1)} %get-tuple-element.47), channel_id=1, source_target_pairs={{0,24},{1,25},{2,26},{3,27},{4,28},{5,29},{6,30},{7,31}} | collective-permute-start | bytes 442376 | tf_op jit(solution)/shard_map/ppermute | solution.py:414
  48.7 2.1 %collective-permute-start.14 = (bf16[272,256]{1,0:T(8,128)(2,1)S(1)}, bf16[272,256]{1,0:T(8,128)(2,1)S(1)}, u32[]{:S(2)}, u32[]{:S(2)}) collective-permute-start(bf16[272,256]{1,0:T(8,128)(2,1)S(1)} %get-tuple-element.43.refs_4_), channel_id=1, source_target_pairs={{0,1},{1,0},{2,3},{3,2},{4,5},{5,4},{6,7},{7,6},{8,9},{9,8},{10,11... | collective-permute-start | bytes 417800 | tf_op jit(solution)/shard_map/ppermute | solution.py:70
  48.8 2.0 %collective-permute-start.15 = (bf16[272,256]{1,0:T(8,128)(2,1)S(1)}, bf16[272,256]{1,0:T(8,128)(2,1)S(1)}, u32[]{:S(2)}, u32[]{:S(2)}) collective-permute-start(bf16[272,256]{1,0:T(8,128)(2,1)S(1)} %get-tuple-element.46), channel_id=1, source_target_pairs={{0,1},{1,0},{2,3},{3,2},{4,5},{5,4},{6,7},{7,6},{8,9},{9,8},{10,11... | collective-permute-start | bytes 417800 | tf_op jit(solution)/shard_map/ppermute | solution.py:70

commit v12 on v11

--- a/solution.py
+++ b/solution.py
@@ -370,7 +370,7 @@
 
     def first_body(
         nums, first_ref, second_ref, low_ref, high_ref, amps_ref, c_ref, co_ref, gain_ref, after_ref,
-        amp_ref, k_ref,
+        amp_ref, amp_long_ref, k_ref,
     ):
         first = first_ref[...]
         outside = whole(nums[WHOSE]) == 2
@@ -386,18 +386,21 @@
 
         old = amps_ref[whole(nums[MINE])].astype(F32)
         c = c_ref[...] + co_ref[:virt, :].astype(F32)
-        amp_ref[...] = (gain_ref[...] * (old - k_ref[...] - c)).astype(BF16)
-
-    amp, k_first = call(
+        amp = (gain_ref[...] * (old - k_ref[...] - c)).astype(BF16)
+        amp_ref[...] = amp
+        amp_long_ref[:virt, :] = amp
+        amp_long_ref[virt:, :] = jnp.zeros((riders, virt), BF16)
+
+    amp, amp_long, k_first = call(
         first_body,
         [SMEM] + [VMEM] * 8 + [ANY],
-        [sq_b, sq_f],
+        [sq_b, longer, sq_f],
         (
             nums, first_t, second, y_low_from_out, y_high_from_out,
             amps, c_own, c_from_out, gain, se_own,
         ),
     )
-    amp_roles = [amp] + [swap(amp, m) for m in range(1, roles)]
+    amp_roles = [amp] + [swap(amp, m) for m in range(1, roles - 1)] + [swap(amp_long, roles - 1)]
 
     def rest_body(amp_ref, k_ref, out_ref, out_b_ref):
         amp = amp_ref[...]
@@ -411,7 +414,7 @@
 
     longest = (VMEM, (virt + 2 * riders, virt), BF16)
     rest, rest_b = call(rest_body, [VMEM, VMEM], [sq_f, longest], (amp, k_first))
-    rests = [lax.ppermute(rest_b, "role", [(0, s)]) for s in range(1, roles)]
+    rests = [lax.ppermute(rest_b, "role", [(0, s)]) for s in range(roles - 1, 0, -1)]
 
     def extra_out_body(coeff_ref, x_ref, after_ref, s_ref):
         @pl.when(lax.axis_index("role") > 0)
@@ -430,7 +433,7 @@
         parts = []
         for m in range(roles):
             at = whole(nums[ROLE_PAIR + (role ^ m)])
-            parts.append((at, weight_of(at), amp_refs[m][...]))
+            parts.append((at, weight_of(at), amp_refs[m][:virt, :]))
         return parts
 
     def told_weight(told, first):
@@ -507,7 +510,7 @@
                 total = rest[...] - co_ref[slot].astype(F32) - c_in[:virt, :].astype(F32)
                 for s in range(1, roles):
                     if slot:
-                        come = rest_refs[s - 1][:virt, :].astype(F32)
+                        come = rest_refs[roles - 1 - s][:virt, :].astype(F32)
                         total += jnp.where(role == s, come, 0.0)
                 amp_ref[slot] = (gain[...] * total).astype(BF16)
 

time: 52.6 us -> 52.4 us (level)
  waiting for transfers between devices: 8 us -> 6.5 us
  starting transfers between devices: 25.9 us -> 27.1 us
    ppermute x3, waiting for transfers between devices: 1.51 us -> 0.01 us  [swap(): return lax.ppermute(x, 'role', [(i, i ^ by) for i in range(roles)])]
    ppermute x7, starting transfers between devices: 12.1 us -> 12.8 us  [outer(): return lax.ppermute(x, 'pairs', list(enumerate(outer_of)))]
    ppermute x3, starting transfers between devices: 8.54 us -> 9.1 us  [local(): lax.ppermute(rest_b, 'role', [(0, s)])]
  transfers between devices with their start and end apart: 19 -> 19, of which waited for: 4 -> 3; matrix products, arithmetic and copies ran while one was open for 0% -> 0% of each run, Pallas kernels for 27% -> 27%
where the time goes in v12:
time: 52.4 us; the launch traced here: 52 us
  starting transfers between devices  27.1 us (52%)
  Pallas kernels  15.5 us (30%)
  waiting for transfers between devices  6.5 us (12%)
  local copies, waits for them, and re-layouts  1.97 us (4%)
  between operations  0.91 us (2%)
    pallas_call x15, Pallas kernels, call(): pl.pallas_call(body, in_specs=ins, out_specs=[spec for spec, _, _ in outs...  15.5 us
    ppermute x7, starting transfers between devices, outer(): return lax.ppermute(x, 'pairs', list(enumerate(outer_of)))  12.8 us
    ppermute x3, starting transfers between devices, local(): lax.ppermute(rest_b, 'role', [(0, s)])  9.1 us
    ppermute x7, waiting for transfers between devices, outer(): return lax.ppermute(x, 'pairs', list(enumerate(outer_of)))  5.54 us
    ppermute x3, starting transfers between devices, swap(): return lax.ppermute(x, 'role', [(i, i ^ by) for i in range(roles)])  3.55 us
    unnamed x14, local copies, waits for them, and re-layouts  1.97 us
    ppermute x6, starting transfers between devices, inner(): return lax.ppermute(x, 'pairs', list(enumerate(inner_of)))  1.66 us
  transfers between devices with their start and end apart: 19, of which 3 were waited for; matrix products, arithmetic and copies ran while one was open for 0% of the time, Pallas kernels for 27%

profile of v12, /device:TPU:0, one launch (start us, length us, event | category | flops | bytes accessed | tf_op | source)
XLA Modules:
  0.0 52.0 jit_solution(17188225309963897834)
XLA Ops:
  0.6 0.5 collective-permute-start.4
  1.1 0.1 collective-permute-start
  1.2 0.4 collective-permute-start.1
  1.7 2.4 %shard_map.113 = (bf16[528,128]{1,0:T(8,128)(2,1)}, bf16[512,128]{1,0:T(8,128)(2,1)}, f32[30]{0:T(128)}) custom-call(s32[4]{0:T(128)} %owner_hbm.1, s32[2,4]{1,0:T(2,128)} %bitcast.1, s32[4,8]{1,0:T(4,128)} %partner_hbm.1, f32[4,8]{1,0:T(4,128)} %coupling_hbm.1, f32[16]{0:T(128)} %eps_hbm.1, s32[4]{0:T(128)} %nvirt_hbm.1, bf16[4,512,256]{2,1,0:T(8,128)(2,1)} %coeff_ref.11), custom_call_target="tpu_custom_call" | custom-call | flops 1 | bytes 1 | tf_op jit(solution)/shard_map/pallas_call | solution.py:33
  4.1 4.8 %collective-permute-start.2 = (bf16[528,128]{1,0:T(8,128)(2,1)}, bf16[528,128]{1,0:T(8,128)(2,1)S(1)}, u32[]{:S(2)}, u32[]{:S(2)}) collective-permute-start(bf16[528,128]{1,0:T(8,128)(2,1)} %get-tuple-element.27), channel_id=1, source_target_pairs={{0,7},{1,2},{2,1},{3,4},{4,3},{5,6},{6,5},{7,0},{8,15},{9,10},{10,... | collective-permute-start | bytes 405512 | tf_op jit(solution)/shard_map/ppermute | solution.py:73
  8.9 0.1 collective-permute-start.3
  9.0 0.7 %copy-done.2 = f32[30]{0:T(128)S(1)} copy-done((f32[30]{0:T(128)S(1)}, f32[30]{0:T(128)}, u32[]{:S(2)}) %copy-start.2) | copy-done | bytes 144
  9.6 1.6 %shard_map.114.three_ref = bf16[2,1024,512]{2,1,0:T(8,128)(2,1)S(1)} custom-call(bf16[2,1024,512]{2,1,0:T(8,128)(2,1)} %three_ref.1, f32[30]{0:T(128)S(1)} %copy-done.2), custom_call_target="tpu_custom_call" | custom-call | flops 1 | bytes 1 | tf_op jit(solution)/shard_map/pallas_call | solution.py:33
  11.2 0.0 copy-start
  11.2 0.0 copy-start.1
  11.2 1.3 %collective-permute-done.2.x_ref.low_ref = bf16[528,128]{1,0:T(8,128)(2,1)S(1)} collective-permute-done((bf16[528,128]{1,0:T(8,128)(2,1)}, bf16[528,128]{1,0:T(8,128)(2,1)S(1)}, u32[]{:S(2)}, u32[]{:S(2)}) %collective-permute-start.2) | collective-permute-done | bytes 135200 | tf_op jit(solution)/shard_map/ppermute | solution.py:73
  12.5 0.5 shard_map.115.after_ref
  13.0 0.0 copy-start.6
  13.1 0.0 copy-start.3
  13.1 3.2 %collective-permute-start.5 = (bf16[1040,128]{1,0:T(8,128)(2,1)S(1)}, bf16[1040,128]{1,0:T(8,128)(2,1)S(1)}, u32[]{:S(2)}, u32[]{:S(2)}) collective-permute-start(bf16[1040,128]{1,0:T(8,128)(2,1)S(1)} %shard_map.115.after_ref), channel_id=1, source_target_pairs={{0,7},{1,2},{2,1},{3,4},{4,3},{5,6},{6,5},{7,0},{8,15},{9,10},{10,... | collective-permute-start | bytes 798728 | tf_op jit(solution)/shard_map/ppermute | solution.py:73
  16.3 0.0 collective-permute-done.3.x_ref.high_ref
  16.3 0.5 shard_map.116.after_ref
  16.8 1.4 %collective-permute-start.6 = (bf16[1024,128]{1,0:T(8,128)(2,1)S(1)}, bf16[1024,128]{1,0:T(8,128)(2,1)S(1)}, u32[]{:S(2)}, u32[]{:S(2)}) collective-permute-start(bf16[1024,128]{1,0:T(8,128)(2,1)S(1)} %shard_map.116.after_ref), channel_id=1, source_target_pairs={{0,7},{1,2},{2,1},{3,4},{4,3},{5,6},{6,5},{7,0},{8,15},{9,10},{10,... | collective-permute-start | bytes 786440 | tf_op jit(solution)/shard_map/ppermute | solution.py:73
  18.2 0.0 copy-done
  18.2 0.0 copy-done.1
  18.2 0.9 %shard_map.117 = (bf16[4,256,256]{2,1,0:T(8,128)(2,1)S(1)}, bf16[272,256]{1,0:T(8,128)(2,1)S(1)}) custom-call(bf16[4,512,256]{2,1,0:T(8,128)(2,1)S(1)} %copy-done, bf16[4,256,256]{2,1,0:T(8,128)(2,1)S(1)} %copy-done.1, bf16[528,128]{1,0:T(8,128)(2,1)S(1)} %collective-permute-done.2.x_ref.low_ref, bf16[512,128]{1,0:T(8,128)(2,1)S(1)} %collective-permute-done.3.x_ref.high_ref, ...), custom_call_target="tpu_custom_call" | custom-call | flops 1 | bytes 1 | tf_op jit(solution)/shard_map/pallas_call | solution.py:33
  19.1 0.0 collective-permute-done.1.amps_in_ref
  19.1 0.0 copy-start.4
  19.2 2.3 %collective-permute-start.7 = (bf16[272,256]{1,0:T(8,128)(2,1)S(1)}, bf16[272,256]{1,0:T(8,128)(2,1)S(1)}, u32[]{:S(2)}, u32[]{:S(2)}) collective-permute-start(bf16[272,256]{1,0:T(8,128)(2,1)S(1)} %get-tuple-element.29.after_ref), channel_id=1, source_target_pairs={{0,7},{1,2},{2,1},{3,4},{4,3},{5,6},{6,5},{7,0},{8,15},{9,10},{10,... | collective-permute-start | bytes 417800 | tf_op jit(solution)/shard_map/ppermute | solution.py:73
  21.4 0.0 collective-permute-done.4.three_in_ref
  21.4 0.0 copy-done.6
  21.4 0.1 collective-permute-start.8
  21.5 1.3 %copy-done.5 = bf16[2,1024,512]{2,1,0:T(8,128)(2,1)} copy-done((bf16[2,1024,512]{2,1,0:T(8,128)(2,1)}, bf16[2,1024,512]{2,1,0:T(8,128)(2,1)S(1)}, u32[]{:S(2)}) %copy-start.5) | copy-done | bytes 2097176
  22.8 0.0 copy-done.3
  22.8 2.5 %shard_map.119 = (bf16[256,1024]{1,0:T(8,128)(2,1)S(1)}, bf16[1024,256]{1,0:T(8,128)(2,1)S(1)}, bf16[512,256]{1,0:T(8,128)(2,1)S(1)}) custom-call(f32[30]{0:T(128)S(1)} %copy-done.3, bf16[2,1024,512]{2,1,0:T(8,128)(2,1)S(1)} %shard_map.114.three_ref, bf16[2,1024,512]{2,1,0:T(8,128)(2,1)} %copy-done.5, bf16[4,512,256]{2,1,0:T(8,128)(2,1)S(1)} %copy-done, ...), custom_call_target="tpu_custom_call" | custom-call | flops 1 | bytes 1 | tf_op jit(solution)/shard_map/pallas_call | solution.py:33
  25.3 0.0 collective-permute-done.coeff_in_ref.in_ref
  25.3 0.1 collective-permute-start.12
  25.4 0.0 copy-done.4
  25.4 2.0 %shard_map.118 = (bf16[4,256,256]{2,1,0:T(8,128)(2,1)S(1)}, f32[256,256]{1,0:T(8,128)S(1)}, f32[256,256]{1,0:T(8,128)S(1)}, f32[256,256]{1,0:T(8,128)S(1)}) custom-call(f32[30]{0:T(128)S(1)} %copy-done.3, bf16[4,512,256]{2,1,0:T(8,128)(2,1)S(1)} %copy-done, bf16[4,512,256]{2,1,0:T(8,128)(2,1)S(1)} %collective-permute-done.coeff_in_ref.in_ref, ...), custom_call_target="tpu_custom_call" | custom-call | flops 1 | bytes 1 | tf_op jit(solution)/shard_map/pallas_call | solution.py:33
  27.4 0.0 collective-permute-done.8.low_ref
  27.4 0.6 %shard_map.120 = (bf16[4,256,256]{2,1,0:T(8,128)(2,1)S(1)}, bf16[4,256,256]{2,1,0:T(8,128)(2,1)S(1)}, bf16[4,256,256]{2,1,0:T(8,128)(2,1)S(1)}) custom-call(f32[30]{0:T(128)S(1)} %copy-done.3, bf16[4,512,256]{2,1,0:T(8,128)(2,1)S(1)} %copy-done, bf16[4,512,256]{2,1,0:T(8,128)(2,1)S(1)} %collective-permute-done.coeff_in_ref.in_ref, ...), custom_call_target="tpu_custom_call" | custom-call | flops 1 | bytes 1 | tf_op jit(solution)/shard_map/pallas_call | solution.py:33
  28.0 4.2 %collective-permute-done.7.co_ref = bf16[272,256]{1,0:T(8,128)(2,1)S(1)} collective-permute-done((bf16[272,256]{1,0:T(8,128)(2,1)S(1)}, bf16[272,256]{1,0:T(8,128)(2,1)S(1)}, u32[]{:S(2)}, u32[]{:S(2)}) %collective-permute-start.7) | collective-permute-done | bytes 139296 | tf_op jit(solution)/shard_map/ppermute | solution.py:73
  32.2 0.0 collective-permute-done.6.high_ref
  32.2 0.0 collective-permute-done.5.low_ref
  32.2 1.0 %shard_map.121 = (bf16[256,256]{1,0:T(8,128)(2,1)S(1)}, bf16[272,256]{1,0:T(8,128)(2,1)S(1)}, f32[256,256]{1,0:T(8,128)S(1)}) custom-call(f32[30]{0:T(128)S(1)} %copy-done.3, bf16[256,1024]{1,0:T(8,128)(2,1)S(1)} %get-tuple-element.32.first_ref, bf16[1024,256]{1,0:T(8,128)(2,1)S(1)} %get-tuple-element.33.second_ref, ...), custom_call_target="tpu_custom_call" | custom-call | flops 1 | bytes 1 | tf_op jit(solution)/shard_map/pallas_call | solution.py:33
  33.2 2.5 %collective-permute-start.11 = (bf16[272,256]{1,0:T(8,128)(2,1)S(1)}, bf16[272,256]{1,0:T(8,128)(2,1)S(1)}, u32[]{:S(2)}, u32[]{:S(2)}) collective-permute-start(bf16[272,256]{1,0:T(8,128)(2,1)S(1)} %get-tuple-element.40), channel_id=1, source_target_pairs={{0,24},{8,16},{16,8},{24,0},{1,25},{9,17},{17,9},{25,1},{2,26},{10... | collective-permute-start | bytes 417800 | tf_op jit(solution)/shard_map/ppermute | solution.py:76
  35.7 0.7 %collective-permute-start.9 = (bf16[256,256]{1,0:T(8,128)(2,1)S(1)}, bf16[256,256]{1,0:T(8,128)(2,1)S(1)}, u32[]{:S(2)}, u32[]{:S(2)}) collective-permute-start(bf16[256,256]{1,0:T(8,128)(2,1)S(1)} %get-tuple-element.36.amp_ref.after_ref.refs_0_), channel_id=1, source_target_pairs={{0,8},{8,0},{16,24},{24,16},{1,9},{9,1},{17,25},{25,17},{2,10},{10... | collective-permute-start | bytes 393224 | tf_op jit(solution)/shard_map/ppermute | solution.py:76
  36.3 0.4 collective-permute-start.10
  36.7 0.4 shard_map.122
  37.1 4.4 %collective-permute-start.16 = (bf16[288,256]{1,0:T(8,128)(2,1)S(1)}, bf16[288,256]{1,0:T(8,128)(2,1)S(1)}, u32[]{:S(2)}, u32[]{:S(2)}) collective-permute-start(bf16[288,256]{1,0:T(8,128)(2,1)S(1)} %get-tuple-element.49), channel_id=1, source_target_pairs={{0,24},{1,25},{2,26},{3,27},{4,28},{5,29},{6,30},{7,31}} | collective-permute-start | bytes 442376 | tf_op jit(solution)/shard_map/ppermute | solution.py:417
  41.5 0.0 collective-permute-done.12.x_ref
  41.5 0.0 collective-permute-done.9.refs_1_
  41.5 0.0 collective-permute-done.10.refs_2_
  41.6 0.0 collective-permute-done.11.refs_3_
  41.6 0.6 %shard_map.124.refs_4_ = bf16[2,256,256]{2,1,0:T(8,128)(2,1)S(1)} custom-call(f32[30]{0:T(128)S(1)} %copy-done.3, bf16[528,128]{1,0:T(8,128)(2,1)S(1)} %collective-permute-done.2.x_ref.low_ref, bf16[4,256,256]{2,1,0:T(8,128)(2,1)S(1)} %get-tuple-element.43.s_ref, bf16[4,256,256]{2,1,0:T(8,128)(2,1)S(1)} %shard_map.123.se_ref, ...), custom_call_target="tpu_custom_call" | custom-call | flops 1 | bytes 1 | tf_op jit(solution)/shard_map/pallas_call | solution.py:33
  42.1 0.9 %collective-permute-start.13 = (bf16[2,256,256]{2,1,0:T(8,128)(2,1)S(1)}, bf16[2,256,256]{2,1,0:T(8,128)(2,1)S(1)}, u32[]{:S(2)}, u32[]{:S(2)}) collective-permute-start(bf16[2,256,256]{2,1,0:T(8,128)(2,1)S(1)} %shard_map.124.refs_4_), channel_id=1, source_target_pairs={{0,7},{1,2},{2,1},{3,4},{4,3},{5,6},{6,5},{7,0},{8,15},{9,10},{10,... | collective-permute-start | bytes 786440 | tf_op jit(solution)/shard_map/ppermute | solution.py:73
  43.1 3.0 %collective-permute-start.17 = (bf16[288,256]{1,0:T(8,128)(2,1)S(1)}, bf16[288,256]{1,0:T(8,128)(2,1)S(1)}, u32[]{:S(2)}, u32[]{:S(2)}) collective-permute-start(bf16[288,256]{1,0:T(8,128)(2,1)S(1)} %get-tuple-element.49), channel_id=1, source_target_pairs={{0,16},{1,17},{2,18},{3,19},{4,20},{5,21},{6,22},{7,23}} | collective-permute-start | bytes 442376 | tf_op jit(solution)/shard_map/ppermute | solution.py:417
  46.1 1.8 %collective-permute-start.18 = (bf16[288,256]{1,0:T(8,128)(2,1)S(1)}, bf16[288,256]{1,0:T(8,128)(2,1)S(1)}, u32[]{:S(2)}, u32[]{:S(2)}) collective-permute-start(bf16[288,256]{1,0:T(8,128)(2,1)S(1)} %get-tuple-element.49), channel_id=1, source_target_pairs={{0,8},{1,9},{2,10},{3,11},{4,12},{5,13},{6,14},{7,15}} | collective-permute-start | bytes 442376 | tf_op jit(solution)/shard_map/ppermute | solution.py:417
  47.8 0.6 %shard_map.125 = (bf16[272,256]{1,0:T(8,128)(2,1)S(1)}, bf16[272,256]{1,0:T(8,128)(2,1)S(1)}) custom-call(f32[30]{0:T(128)S(1)} %copy-done.3, bf16[528,128]{1,0:T(8,128)(2,1)S(1)} %collective-permute-done.8.low_ref, bf16[4,256,256]{2,1,0:T(8,128)(2,1)S(1)} %get-tuple-element.41.s_ref, bf16[4,256,256]{2,1,0:T(8,128)(2,1)S(1)} %get-tuple-element.42.se_ref, ...), custom_call_target="tpu_custom_call" | custom-call | flops 1 | bytes 1 | tf_op jit(solution)/shard_map/pallas_call | solution.py:33
  48.4 0.1 collective-permute-start.14
  48.5 0.0 collective-permute-done.16.refs_0_
  48.5 0.5 collective-permute-start.15
  49.0 0.6 %shard_map.126 = (f32[256,256]{1,0:T(8,128)S(1)}, f32[256,256]{1,0:T(8,128)S(1)}) custom-call(f32[30]{0:T(128)S(1)} %copy-done.3, f32[256,256]{1,0:T(8,128)S(1)} %get-tuple-element.38.rest_ref, bf16[4,256,256]{2,1,0:T(8,128)(2,1)S(1)} %get-tuple-element.39.s_ref, bf16[4,256,256]{2,1,0:T(8,128)(2,1)S(1)} %get-tuple-element.35.after_ref.se_ref, ...), custom_call_target="tpu_custom_call" | custom-call | flops 1 | bytes 1 | tf_op jit(solution)/shard_map/pallas_call | solution.py:33
  49.5 0.0 collective-permute-done.17.refs_1_
  49.6 0.9 %collective-permute-done.18.refs_2_ = bf16[288,256]{1,0:T(8,128)(2,1)S(1)} collective-permute-done((bf16[288,256]{1,0:T(8,128)(2,1)S(1)}, bf16[288,256]{1,0:T(8,128)(2,1)S(1)}, u32[]{:S(2)}, u32[]{:S(2)}) %collective-permute-start.18) | collective-permute-done | bytes 147488 | tf_op jit(solution)/shard_map/ppermute | solution.py:417
  50.5 0.0 collective-permute-done.14.ci_ref
  50.5 0.0 collective-permute-done.15.cei_ref
  50.5 0.0 collective-permute-done.13.co_ref
  50.5 1.5 %shard_map.127 = (bf16[2,256,256]{2,1,0:T(8,128)(2,1)}, bf16[2,512,256]{2,1,0:T(8,128)(2,1)}) custom-call(f32[30]{0:T(128)S(1)} %copy-done.3, bf16[4,512,256]{2,1,0:T(8,128)(2,1)S(1)} %copy-done, f32[256,256]{1,0:T(8,128)S(1)} %get-tuple-element.30.gain_ref, f32[256,256]{1,0:T(8,128)S(1)} %get-tuple-element.31.gain_extra_ref, ...), custom_call_target="tpu_custom_call" | custom-call | flops 1 | bytes 1 | tf_op jit(solution)/shard_map/pallas_call | solution.py:33
  (3 shorter events, 0.0 us)
Async XLA Ops:
  0.6 20.8 %collective-permute-start.4 = (bf16[2,1024,512]{2,1,0:T(8,128)(2,1)}, bf16[2,1024,512]{2,1,0:T(8,128)(2,1)S(1)}, u32[]{:S(2)}, u32[]{:S(2)}) collective-permute-start(bf16[2,1024,512]{2,1,0:T(8,128)(2,1)} %three_ref.1), channel_id=1, source_target_pairs={{0,1},{1,0},{2,3},{3,2},{4,5},{5,4},{6,7},{7,6},{8,9},{9,8},{10,11... | collective-permute-start | bytes 6291464 | tf_op jit(solution)/shard_map/ppermute | solution.py:70
  1.1 24.1 %collective-permute-start = (bf16[4,512,256]{2,1,0:T(8,128)(2,1)}, bf16[4,512,256]{2,1,0:T(8,128)(2,1)S(1)}, u32[]{:S(2)}, u32[]{:S(2)}) collective-permute-start(bf16[4,512,256]{2,1,0:T(8,128)(2,1)} %coeff_ref.11), channel_id=1, source_target_pairs={{0,1},{1,0},{2,3},{3,2},{4,5},{5,4},{6,7},{7,6},{8,9},{9,8},{10,11... | collective-permute-start | bytes 3145736 | tf_op jit(solution)/shard_map/ppermute | solution.py:70
  1.2 17.9 %collective-permute-start.1 = (bf16[4,256,256]{2,1,0:T(8,128)(2,1)}, bf16[4,256,256]{2,1,0:T(8,128)(2,1)S(1)}, u32[]{:S(2)}, u32[]{:S(2)}) collective-permute-start(bf16[4,256,256]{2,1,0:T(8,128)(2,1)} %amps_ref.5), channel_id=1, source_target_pairs={{0,1},{1,0},{2,3},{3,2},{4,5},{5,4},{6,7},{7,6},{8,9},{9,8},{10,11... | collective-permute-start | bytes 1572872 | tf_op jit(solution)/shard_map/ppermute | solution.py:70
  4.1 8.4 %collective-permute-start.2 = (bf16[528,128]{1,0:T(8,128)(2,1)}, bf16[528,128]{1,0:T(8,128)(2,1)S(1)}, u32[]{:S(2)}, u32[]{:S(2)}) collective-permute-start(bf16[528,128]{1,0:T(8,128)(2,1)} %get-tuple-element.27), channel_id=1, source_target_pairs={{0,7},{1,2},{2,1},{3,4},{4,3},{5,6},{6,5},{7,0},{8,15},{9,10},{10,... | collective-permute-start | bytes 405512 | tf_op jit(solution)/shard_map/ppermute | solution.py:73
  8.9 7.4 %collective-permute-start.3 = (bf16[512,128]{1,0:T(8,128)(2,1)}, bf16[512,128]{1,0:T(8,128)(2,1)S(1)}, u32[]{:S(2)}, u32[]{:S(2)}) collective-permute-start(bf16[512,128]{1,0:T(8,128)(2,1)} %get-tuple-element.28), channel_id=1, source_target_pairs={{0,7},{1,2},{2,1},{3,4},{4,3},{5,6},{6,5},{7,0},{8,15},{9,10},{10,... | collective-permute-start | bytes 393224 | tf_op jit(solution)/shard_map/ppermute | solution.py:73
  9.0 0.7 %copy-start.2 = (f32[30]{0:T(128)S(1)}, f32[30]{0:T(128)}, u32[]{:S(2)}) copy-start(f32[30]{0:T(128)} %get-tuple-element.26.after_ref.nums) | copy-start | bytes 364
  11.2 7.0 %copy-start = (bf16[4,512,256]{2,1,0:T(8,128)(2,1)S(1)}, bf16[4,512,256]{2,1,0:T(8,128)(2,1)}, u32[]{:S(2)}) copy-start(bf16[4,512,256]{2,1,0:T(8,128)(2,1)} %coeff_ref.11) | copy-start | bytes 3145732
  11.2 7.0 %copy-start.1 = (bf16[4,256,256]{2,1,0:T(8,128)(2,1)S(1)}, bf16[4,256,256]{2,1,0:T(8,128)(2,1)}, u32[]{:S(2)}) copy-start(bf16[4,256,256]{2,1,0:T(8,128)(2,1)} %amps_ref.5) | copy-start | bytes 1572868
  13.0 8.4 %copy-start.6 = (bf16[528,128]{1,0:T(8,128)(2,1)S(1)}, bf16[528,128]{1,0:T(8,128)(2,1)}, u32[]{:S(2)}) copy-start(bf16[528,128]{1,0:T(8,128)(2,1)} %get-tuple-element.27) | copy-start | bytes 405508
  13.1 9.7 %copy-start.3 = (f32[30]{0:T(128)S(1)}, f32[30]{0:T(128)}, u32[]{:S(2)}) copy-start(f32[30]{0:T(128)} %get-tuple-element.26.after_ref.nums) | copy-start | bytes 364
  13.1 19.1 %collective-permute-start.5 = (bf16[1040,128]{1,0:T(8,128)(2,1)S(1)}, bf16[1040,128]{1,0:T(8,128)(2,1)S(1)}, u32[]{:S(2)}, u32[]{:S(2)}) collective-permute-start(bf16[1040,128]{1,0:T(8,128)(2,1)S(1)} %shard_map.115.after_ref), channel_id=1, source_target_pairs={{0,7},{1,2},{2,1},{3,4},{4,3},{5,6},{6,5},{7,0},{8,15},{9,10},{10,... | collective-permute-start | bytes 798728 | tf_op jit(solution)/shard_map/ppermute | solution.py:73
  16.8 15.4 %collective-permute-start.6 = (bf16[1024,128]{1,0:T(8,128)(2,1)S(1)}, bf16[1024,128]{1,0:T(8,128)(2,1)S(1)}, u32[]{:S(2)}, u32[]{:S(2)}) collective-permute-start(bf16[1024,128]{1,0:T(8,128)(2,1)S(1)} %shard_map.116.after_ref), channel_id=1, source_target_pairs={{0,7},{1,2},{2,1},{3,4},{4,3},{5,6},{6,5},{7,0},{8,15},{9,10},{10,... | collective-permute-start | bytes 786440 | tf_op jit(solution)/shard_map/ppermute | solution.py:73
  19.1 6.3 %copy-start.4 = (f32[4,256]{1,0:T(4,128)S(1)}, f32[4,256]{1,0:T(4,128)}, u32[]{:S(2)}) copy-start(f32[4,256]{1,0:T(4,128)} %eps_ref.1) | copy-start | bytes 12292
  19.2 13.1 %collective-permute-start.7 = (bf16[272,256]{1,0:T(8,128)(2,1)S(1)}, bf16[272,256]{1,0:T(8,128)(2,1)S(1)}, u32[]{:S(2)}, u32[]{:S(2)}) collective-permute-start(bf16[272,256]{1,0:T(8,128)(2,1)S(1)} %get-tuple-element.29.after_ref), channel_id=1, source_target_pairs={{0,7},{1,2},{2,1},{3,4},{4,3},{5,6},{6,5},{7,0},{8,15},{9,10},{10,... | collective-permute-start | bytes 417800 | tf_op jit(solution)/shard_map/ppermute | solution.py:73
  21.4 1.4 %copy-start.5 = (bf16[2,1024,512]{2,1,0:T(8,128)(2,1)}, bf16[2,1024,512]{2,1,0:T(8,128)(2,1)S(1)}, u32[]{:S(2)}) copy-start(bf16[2,1024,512]{2,1,0:T(8,128)(2,1)S(1)} %collective-permute-done.4.three_in_ref) | copy-start | bytes 6291460
  21.4 6.0 %collective-permute-start.8 = (bf16[528,128]{1,0:T(8,128)(2,1)S(1)}, bf16[528,128]{1,0:T(8,128)(2,1)S(1)}, u32[]{:S(2)}, u32[]{:S(2)}) collective-permute-start(bf16[528,128]{1,0:T(8,128)(2,1)S(1)} %copy-done.6), channel_id=1, source_target_pairs={{0,1},{1,0},{2,3},{3,2},{4,5},{5,4},{6,7},{7,6},{8,9},{9,8},{10,11... | collective-permute-start | bytes 405512 | tf_op jit(solution)/shard_map/ppermute | solution.py:70
  25.3 16.2 %collective-permute-start.12 = (bf16[512,256]{1,0:T(8,128)(2,1)S(1)}, bf16[512,256]{1,0:T(8,128)(2,1)S(1)}, u32[]{:S(2)}, u32[]{:S(2)}) collective-permute-start(bf16[512,256]{1,0:T(8,128)(2,1)S(1)} %get-tuple-element.44), channel_id=1, source_target_pairs={{0,7},{1,2},{2,1},{3,4},{4,3},{5,6},{6,5},{7,0},{8,15},{9,10},{10,... | collective-permute-start | bytes 786440 | tf_op jit(solution)/shard_map/ppermute | solution.py:73
  33.2 8.4 %collective-permute-start.11 = (bf16[272,256]{1,0:T(8,128)(2,1)S(1)}, bf16[272,256]{1,0:T(8,128)(2,1)S(1)}, u32[]{:S(2)}, u32[]{:S(2)}) collective-permute-start(bf16[272,256]{1,0:T(8,128)(2,1)S(1)} %get-tuple-element.40), channel_id=1, source_target_pairs={{0,24},{8,16},{16,8},{24,0},{1,25},{9,17},{17,9},{25,1},{2,26},{10... | collective-permute-start | bytes 417800 | tf_op jit(solution)/shard_map/ppermute | solution.py:76
  35.7 5.9 %collective-permute-start.9 = (bf16[256,256]{1,0:T(8,128)(2,1)S(1)}, bf16[256,256]{1,0:T(8,128)(2,1)S(1)}, u32[]{:S(2)}, u32[]{:S(2)}) collective-permute-start(bf16[256,256]{1,0:T(8,128)(2,1)S(1)} %get-tuple-element.36.amp_ref.after_ref.refs_0_), channel_id=1, source_target_pairs={{0,8},{8,0},{16,24},{24,16},{1,9},{9,1},{17,25},{25,17},{2,10},{10... | collective-permute-start | bytes 393224 | tf_op jit(solution)/shard_map/ppermute | solution.py:76
  36.3 5.2 %collective-permute-start.10 = (bf16[256,256]{1,0:T(8,128)(2,1)S(1)}, bf16[256,256]{1,0:T(8,128)(2,1)S(1)}, u32[]{:S(2)}, u32[]{:S(2)}) collective-permute-start(bf16[256,256]{1,0:T(8,128)(2,1)S(1)} %get-tuple-element.36.amp_ref.after_ref.refs_0_), channel_id=1, source_target_pairs={{0,16},{8,24},{16,0},{24,8},{1,17},{9,25},{17,1},{25,9},{2,18},{10... | collective-permute-start | bytes 393224 | tf_op jit(solution)/shard_map/ppermute | solution.py:76
  37.1 11.3 %collective-permute-start.16 = (bf16[288,256]{1,0:T(8,128)(2,1)S(1)}, bf16[288,256]{1,0:T(8,128)(2,1)S(1)}, u32[]{:S(2)}, u32[]{:S(2)}) collective-permute-start(bf16[288,256]{1,0:T(8,128)(2,1)S(1)} %get-tuple-element.49), channel_id=1, source_target_pairs={{0,24},{1,25},{2,26},{3,27},{4,28},{5,29},{6,30},{7,31}} | collective-permute-start | bytes 442376 | tf_op jit(solution)/shard_map/ppermute | solution.py:417
  42.1 8.4 %collective-permute-start.13 = (bf16[2,256,256]{2,1,0:T(8,128)(2,1)S(1)}, bf16[2,256,256]{2,1,0:T(8,128)(2,1)S(1)}, u32[]{:S(2)}, u32[]{:S(2)}) collective-permute-start(bf16[2,256,256]{2,1,0:T(8,128)(2,1)S(1)} %shard_map.124.refs_4_), channel_id=1, source_target_pairs={{0,7},{1,2},{2,1},{3,4},{4,3},{5,6},{6,5},{7,0},{8,15},{9,10},{10,... | collective-permute-start | bytes 786440 | tf_op jit(solution)/shard_map/ppermute | solution.py:73
  43.1 6.5 %collective-permute-start.17 = (bf16[288,256]{1,0:T(8,128)(2,1)S(1)}, bf16[288,256]{1,0:T(8,128)(2,1)S(1)}, u32[]{:S(2)}, u32[]{:S(2)}) collective-permute-start(bf16[288,256]{1,0:T(8,128)(2,1)S(1)} %get-tuple-element.49), channel_id=1, source_target_pairs={{0,16},{1,17},{2,18},{3,19},{4,20},{5,21},{6,22},{7,23}} | collective-permute-start | bytes 442376 | tf_op jit(solution)/shard_map/ppermute | solution.py:417
  46.1 4.4 %collective-permute-start.18 = (bf16[288,256]{1,0:T(8,128)(2,1)S(1)}, bf16[288,256]{1,0:T(8,128)(2,1)S(1)}, u32[]{:S(2)}, u32[]{:S(2)}) collective-permute-start(bf16[288,256]{1,0:T(8,128)(2,1)S(1)} %get-tuple-element.49), channel_id=1, source_target_pairs={{0,8},{1,9},{2,10},{3,11},{4,12},{5,13},{6,14},{7,15}} | collective-permute-start | bytes 442376 | tf_op jit(solution)/shard_map/ppermute | solution.py:417
  48.4 2.1 %collective-permute-start.14 = (bf16[272,256]{1,0:T(8,128)(2,1)S(1)}, bf16[272,256]{1,0:T(8,128)(2,1)S(1)}, u32[]{:S(2)}, u32[]{:S(2)}) collective-permute-start(bf16[272,256]{1,0:T(8,128)(2,1)S(1)} %get-tuple-element.45.refs_4_), channel_id=1, source_target_pairs={{0,1},{1,0},{2,3},{3,2},{4,5},{5,4},{6,7},{7,6},{8,9},{9,8},{10,11... | collective-permute-start | bytes 417800 | tf_op jit(solution)/shard_map/ppermute | solution.py:70
  48.5 2.0 %collective-permute-start.15 = (bf16[272,256]{1,0:T(8,128)(2,1)S(1)}, bf16[272,256]{1,0:T(8,128)(2,1)S(1)}, u32[]{:S(2)}, u32[]{:S(2)}) collective-permute-start(bf16[272,256]{1,0:T(8,128)(2,1)S(1)} %get-tuple-element.48), channel_id=1, source_target_pairs={{0,1},{1,0},{2,3},{3,2},{4,5},{5,4},{6,7},{7,6},{8,9},{9,8},{10,11... | collective-permute-start | bytes 417800 | tf_op jit(solution)/shard_map/ppermute | solution.py:70

commit v13 on v12

--- a/solution.py
+++ b/solution.py
@@ -1,3 +1,4 @@
+import functools
 import math
 
 import jax
@@ -98,6 +99,7 @@
     place_at, mine_at, extra_at = 2 * weights, 2 * weights + 1, 2 * weights + 2
     riders = 16
     longer = (VMEM, (virt + riders, virt), BF16)
+    longest = (VMEM, (virt + 2 * riders, virt), BF16)
     own_weights = ROLE_PAIR + roles
 
     def plan_body(
@@ -280,10 +282,12 @@
     c_from_out = outer(c_out)
 
     def own_half_body(
-        nums, three_ref, three_in_ref, coeff_ref, after_ref, first_ref, second_ref, extra_ref, block_ref, sem
+        nums, three_ref, three_in_ref, coeff_ref, after_ref,
+        first_ref, second_ref, extra_0_ref, extra_1_ref, block_ref, sem,
     ):
         x = coeff_ref[whole(nums[MINE])]
-        extra_ref[...] = coeff_ref[whole(nums[EXTRA])]
+        extra_0_ref[...] = coeff_ref[whole(nums[EXTRA]), : pao // 2, :]
+        extra_1_ref[...] = coeff_ref[whole(nums[EXTRA]), pao // 2 :, :]
         whose, second = whole(nums[WHOSE]), whole(nums[SECOND])
         copy = pltpu.make_async_copy(three_in_ref.at[second], block_ref.at[0], sem)
 
@@ -305,18 +309,19 @@
             copy.wait()
             half_into(second_ref, block_ref, 0, x)
 
-    first_t, second, x_extra = call(
+    first_t, second, *x_extra = call(
         own_half_body,
         [SMEM, VMEM, ANY, VMEM, ANY],
         [
             (VMEM, (virt, aux), BF16),
             (VMEM, (aux, virt), BF16),
-            (VMEM, (pao, virt), BF16),
+            (VMEM, (pao // 2, virt), BF16),
+            (VMEM, (pao // 2, virt), BF16),
         ],
         (nums, blocks, three_in, coeff, c_out),
         scratch=[pltpu.VMEM((1, aux, pao), BF16), pltpu.SemaphoreType.DMA],
     )
-    x_extra_out = outer(x_extra)
+    x_extra_out = [outer(x) for x in x_extra]
 
     def own_body(
         nums, coeff_ref, coeff_in_ref, amps_ref, amps_in_ref, eps_ref, after_ref,
@@ -387,14 +392,14 @@
         old = amps_ref[whole(nums[MINE])].astype(F32)
         c = c_ref[...] + co_ref[:virt, :].astype(F32)
         amp = (gain_ref[...] * (old - k_ref[...] - c)).astype(BF16)
-        amp_ref[...] = amp
-        amp_long_ref[:virt, :] = amp
-        amp_long_ref[virt:, :] = jnp.zeros((riders, virt), BF16)
+        for ref in (amp_ref, amp_long_ref):
+            ref[:virt, :] = amp
+            ref[virt:, :] = jnp.zeros((ref.shape[0] - virt, virt), BF16)
 
     amp, amp_long, k_first = call(
         first_body,
         [SMEM] + [VMEM] * 8 + [ANY],
-        [sq_b, longer, sq_f],
+        [longer, longest, sq_f],
         (
             nums, first_t, second, y_low_from_out, y_high_from_out,
             amps, c_own, c_from_out, gain, se_own,
@@ -403,7 +408,7 @@
     amp_roles = [amp] + [swap(amp, m) for m in range(1, roles - 1)] + [swap(amp_long, roles - 1)]
 
     def rest_body(amp_ref, k_ref, out_ref, out_b_ref):
-        amp = amp_ref[...]
+        amp = amp_ref[:virt, :]
         k = k_ref[...]
         right = k + mxu(k.astype(BF16), amp, NN) * virt_scale
         both = right + mxu(amp.T, right.astype(BF16), NN) * virt_scale
@@ -412,21 +417,8 @@
         out_b_ref[:virt, :] = rest.astype(BF16)
         out_b_ref[virt:, :] = jnp.zeros((2 * riders, virt), BF16)
 
-    longest = (VMEM, (virt + 2 * riders, virt), BF16)
     rest, rest_b = call(rest_body, [VMEM, VMEM], [sq_f, longest], (amp, k_first))
     rests = [lax.ppermute(rest_b, "role", [(0, s)]) for s in range(roles - 1, 0, -1)]
-
-    def extra_out_body(coeff_ref, x_ref, after_ref, s_ref):
-        @pl.when(lax.axis_index("role") > 0)
-        def _():
-            overlaps(x_ref[...], coeff_ref, s_ref)
-
-    (se_out,) = call(
-        extra_out_body,
-        [VMEM, VMEM, ANY],
-        [all_s],
-        (coeff, x_extra_out, amp),
-    )
 
     def parts_of(nums, weight_of, amp_refs):
         role = lax.axis_index("role")
@@ -439,22 +431,46 @@
     def told_weight(told, first):
         return lambda at: pick([told[:, first + q : first + q + 1] for q in range(pairs)], at)
 
-    def outer_again_body(nums, low_ref, s_ref, se_ref, *refs):
+    def outer_again_body(slot, nums, low_ref, s_ref, *refs):
         amp_refs, c_ref = refs[:roles], refs[-1]
 
         @pl.when(lax.axis_index("role") > 0)
         def _():
-            told = told_of(low_ref)
-            for slot, of_s in enumerate((s_ref, se_ref)):
-                parts = parts_of(nums, told_weight(told, slot * pairs), amp_refs)
-                c_ref[slot] = coupled(of_s, parts).astype(BF16)
-
-    (cc_out,) = call(
-        outer_again_body,
-        [SMEM] + [VMEM] * (3 + roles),
-        [two_b],
-        (nums, low_out, s_out, se_out, *amp_roles),
-    )
+            parts = parts_of(nums, told_weight(told_of(low_ref), slot * pairs), amp_refs)
+            c = coupled(s_ref, parts).astype(BF16)
+            if slot:
+                c_ref[0] = refs[roles][...]
+                c_ref[1] = c
+            else:
+                c_ref[...] = c
+
+    def outer_again(slot, s, out, *before):
+        (c,) = call(
+            functools.partial(outer_again_body, slot),
+            [SMEM] + [VMEM] * (2 + roles + len(before)),
+            [out],
+            (nums, low_out, s, *amp_roles, *before),
+        )
+        return c
+
+    c_mine = outer_again(0, s_out, sq_b)
+
+    def extra_out_body(coeff_ref, x_0_ref, x_1_ref, after_ref, s_ref, x_ref):
+        @pl.when(lax.axis_index("role") > 0)
+        def _():
+            x_ref[: pao // 2, :] = x_0_ref[...]
+            x_ref[pao // 2 :, :] = x_1_ref[...]
+            overlaps(x_ref[...], coeff_ref, s_ref)
+
+    (se_out,) = call(
+        extra_out_body,
+        [VMEM, VMEM, VMEM, ANY],
+        [all_s],
+        (coeff, *x_extra_out, c_mine),
+        scratch=[pltpu.VMEM((pao, virt), BF16)],
+    )
+
+    cc_out = outer_again(1, se_out, two_b, c_mine)
     cc_from_out = outer(cc_out)
 
     def inner_again_body(nums, low_ref, s_ref, se_ref, *refs):

time: 52.4 us -> 56.6 us (1.080)
  starting transfers between devices: 27.1 us -> 31.3 us
  Pallas kernels: 15.5 us -> 14.7 us
  waiting for transfers between devices: 6.5 us -> 7.27 us
    ppermute x7 -> x8, starting transfers between devices: 12.8 us -> 16.2 us  [outer(): return lax.ppermute(x, 'pairs', list(enumerate(outer_of)))]
    pallas_call x15 -> x16, Pallas kernels: 15.5 us -> 14.7 us  [call(): pl.pallas_call(body, in_specs=ins, out_specs=[spec for spec, _, _ in outs...]
    ppermute x7 -> x8, waiting for transfers between devices: 5.54 us -> 6.31 us  [outer(): return lax.ppermute(x, 'pairs', list(enumerate(outer_of)))]
    ppermute x3, starting transfers between devices: 9.1 us -> 9.87 us  [local(): lax.ppermute(rest_b, 'role', [(0, s)])]
  transfers between devices with their start and end apart: 19 -> 20, of which waited for: 3 -> 3; matrix products, arithmetic and copies ran while one was open for 0% -> 0% of each run, Pallas kernels for 27% -> 22%
where the time goes in v13:
time: 56.6 us; the launch traced here: 56.2 us
  starting transfers between devices  31.3 us (55%)
  Pallas kernels  14.7 us (26%)
  waiting for transfers between devices  7.27 us (13%)
  local copies, waits for them, and re-layouts  2.04 us (4%)
  between operations  0.92 us (2%)
    ppermute x8, starting transfers between devices, outer(): return lax.ppermute(x, 'pairs', list(enumerate(outer_of)))  16.2 us
    pallas_call x16, Pallas kernels, call(): pl.pallas_call(body, in_specs=ins, out_specs=[spec for spec, _, _ in outs...  14.7 us
    ppermute x3, starting transfers between devices, local(): lax.ppermute(rest_b, 'role', [(0, s)])  9.87 us
    ppermute x8, waiting for transfers between devices, outer(): return lax.ppermute(x, 'pairs', list(enumerate(outer_of)))  6.31 us
    ppermute x3, starting transfers between devices, swap(): return lax.ppermute(x, 'role', [(i, i ^ by) for i in range(roles)])  3.55 us
    unnamed x14, local copies, waits for them, and re-layouts  2.04 us
    ppermute x6, starting transfers between devices, inner(): return lax.ppermute(x, 'pairs', list(enumerate(inner_of)))  1.59 us
  transfers between devices with their start and end apart: 20, of which 3 were waited for; matrix products, arithmetic and copies ran while one was open for 0% of the time, Pallas kernels for 22%

profile of v13, /device:TPU:0, one launch (start us, length us, event | category | flops | bytes accessed | tf_op | source)
XLA Modules:
  0.0 56.2 jit_solution(2629732097124099611)
XLA Ops:
  0.6 0.5 collective-permute-start.4
  1.1 0.1 collective-permute-start
  1.2 0.4 collective-permute-start.1
  1.7 2.4 %shard_map.113 = (bf16[528,128]{1,0:T(8,128)(2,1)}, bf16[512,128]{1,0:T(8,128)(2,1)}, f32[30]{0:T(128)}) custom-call(s32[4]{0:T(128)} %owner_hbm.1, s32[2,4]{1,0:T(2,128)} %bitcast.1, s32[4,8]{1,0:T(4,128)} %partner_hbm.1, f32[4,8]{1,0:T(4,128)} %coupling_hbm.1, f32[16]{0:T(128)} %eps_hbm.1, s32[4]{0:T(128)} %nvirt_hbm.1, bf16[4,512,256]{2,1,0:T(8,128)(2,1)} %coeff_ref.11), custom_call_target="tpu_custom_call" | custom-call | flops 1 | bytes 1 | tf_op jit(solution)/shard_map/pallas_call | solution.py:34
  4.1 4.8 %collective-permute-start.2 = (bf16[528,128]{1,0:T(8,128)(2,1)}, bf16[528,128]{1,0:T(8,128)(2,1)S(1)}, u32[]{:S(2)}, u32[]{:S(2)}) collective-permute-start(bf16[528,128]{1,0:T(8,128)(2,1)} %get-tuple-element.28), channel_id=1, source_target_pairs={{0,7},{1,2},{2,1},{3,4},{4,3},{5,6},{6,5},{7,0},{8,15},{9,10},{10,... | collective-permute-start | bytes 405512 | tf_op jit(solution)/shard_map/ppermute | solution.py:74
  8.9 0.1 collective-permute-start.3
  9.0 0.7 %copy-done.2 = f32[30]{0:T(128)S(1)} copy-done((f32[30]{0:T(128)S(1)}, f32[30]{0:T(128)}, u32[]{:S(2)}) %copy-start.2) | copy-done | bytes 144
  9.6 1.6 %shard_map.114.three_ref = bf16[2,1024,512]{2,1,0:T(8,128)(2,1)S(1)} custom-call(bf16[2,1024,512]{2,1,0:T(8,128)(2,1)} %three_ref.1, f32[30]{0:T(128)S(1)} %copy-done.2), custom_call_target="tpu_custom_call" | custom-call | flops 1 | bytes 1 | tf_op jit(solution)/shard_map/pallas_call | solution.py:34
  11.2 0.0 copy-start
  11.2 0.0 copy-start.1
  11.3 1.3 %collective-permute-done.2.x_ref.low_ref = bf16[528,128]{1,0:T(8,128)(2,1)S(1)} collective-permute-done((bf16[528,128]{1,0:T(8,128)(2,1)}, bf16[528,128]{1,0:T(8,128)(2,1)S(1)}, u32[]{:S(2)}, u32[]{:S(2)}) %collective-permute-start.2) | collective-permute-done | bytes 135200 | tf_op jit(solution)/shard_map/ppermute | solution.py:74
  12.5 0.5 shard_map.115.after_ref
  13.0 0.0 copy-start.6
  13.1 0.0 copy-start.4
  13.1 3.2 %collective-permute-start.5 = (bf16[1040,128]{1,0:T(8,128)(2,1)S(1)}, bf16[1040,128]{1,0:T(8,128)(2,1)S(1)}, u32[]{:S(2)}, u32[]{:S(2)}) collective-permute-start(bf16[1040,128]{1,0:T(8,128)(2,1)S(1)} %shard_map.115.after_ref), channel_id=1, source_target_pairs={{0,7},{1,2},{2,1},{3,4},{4,3},{5,6},{6,5},{7,0},{8,15},{9,10},{10,... | collective-permute-start | bytes 798728 | tf_op jit(solution)/shard_map/ppermute | solution.py:74
  16.3 0.0 collective-permute-done.3.x_ref.high_ref
  16.3 0.5 shard_map.116.after_ref
  16.8 1.4 %collective-permute-start.6 = (bf16[1024,128]{1,0:T(8,128)(2,1)S(1)}, bf16[1024,128]{1,0:T(8,128)(2,1)S(1)}, u32[]{:S(2)}, u32[]{:S(2)}) collective-permute-start(bf16[1024,128]{1,0:T(8,128)(2,1)S(1)} %shard_map.116.after_ref), channel_id=1, source_target_pairs={{0,7},{1,2},{2,1},{3,4},{4,3},{5,6},{6,5},{7,0},{8,15},{9,10},{10,... | collective-permute-start | bytes 786440 | tf_op jit(solution)/shard_map/ppermute | solution.py:74
  18.2 0.0 copy-done
  18.2 0.0 copy-done.1
  18.2 0.9 %shard_map.117 = (bf16[4,256,256]{2,1,0:T(8,128)(2,1)S(1)}, bf16[272,256]{1,0:T(8,128)(2,1)S(1)}) custom-call(bf16[4,512,256]{2,1,0:T(8,128)(2,1)S(1)} %copy-done, bf16[4,256,256]{2,1,0:T(8,128)(2,1)S(1)} %copy-done.1, bf16[528,128]{1,0:T(8,128)(2,1)S(1)} %collective-permute-done.2.x_ref.low_ref, bf16[512,128]{1,0:T(8,128)(2,1)S(1)} %collective-permute-done.3.x_ref.high_ref, ...), custom_call_target="tpu_custom_call" | custom-call | flops 1 | bytes 1 | tf_op jit(solution)/shard_map/pallas_call | solution.py:34
  19.1 0.0 collective-permute-done.1.amps_in_ref
  19.1 2.3 %collective-permute-start.7 = (bf16[272,256]{1,0:T(8,128)(2,1)S(1)}, bf16[272,256]{1,0:T(8,128)(2,1)S(1)}, u32[]{:S(2)}, u32[]{:S(2)}) collective-permute-start(bf16[272,256]{1,0:T(8,128)(2,1)S(1)} %get-tuple-element.30.after_ref), channel_id=1, source_target_pairs={{0,7},{1,2},{2,1},{3,4},{4,3},{5,6},{6,5},{7,0},{8,15},{9,10},{10,... | collective-permute-start | bytes 417800 | tf_op jit(solution)/shard_map/ppermute | solution.py:74
  21.4 0.0 collective-permute-done.coeff_in_ref.in_ref
  21.4 0.0 collective-permute-start.8
  21.4 2.0 %shard_map.118 = (bf16[4,256,256]{2,1,0:T(8,128)(2,1)S(1)}, f32[256,256]{1,0:T(8,128)S(1)}, f32[256,256]{1,0:T(8,128)S(1)}, f32[256,256]{1,0:T(8,128)S(1)}) custom-call(f32[30]{0:T(128)S(1)} %copy-done.2, bf16[4,512,256]{2,1,0:T(8,128)(2,1)S(1)} %copy-done, bf16[4,512,256]{2,1,0:T(8,128)(2,1)S(1)} %collective-permute-done.coeff_in_ref.in_ref, ...), custom_call_target="tpu_custom_call" | custom-call | flops 1 | bytes 1 | tf_op jit(solution)/shard_map/pallas_call | solution.py:34
  23.4 0.0 collective-permute-done.8.low_ref
  23.4 0.6 shard_map.120
  24.0 0.0 collective-permute-done.4.three_in_ref
  24.0 1.3 %copy-done.5 = bf16[2,1024,512]{2,1,0:T(8,128)(2,1)} copy-done((bf16[2,1024,512]{2,1,0:T(8,128)(2,1)}, bf16[2,1024,512]{2,1,0:T(8,128)(2,1)S(1)}, u32[]{:S(2)}) %copy-start.5) | copy-done | bytes 2097176
  25.4 1.0 %shard_map.119 = (bf16[256,1024]{1,0:T(8,128)(2,1)S(1)}, bf16[1024,256]{1,0:T(8,128)(2,1)S(1)}, bf16[256,256]{1,0:T(8,128)(2,1)S(1)}, bf16[256,256]{1,0:T(8,128)(2,1)S(1)}) custom-call(f32[30]{0:T(128)S(1)} %copy-done.2, bf16[2,1024,512]{2,1,0:T(8,128)(2,1)S(1)} %shard_map.114.three_ref, bf16[2,1024,512]{2,1,0:T(8,128)(2,1)} %copy-done.5, ...), custom_call_target="tpu_custom_call" | custom-call | flops 1 | bytes 1 | tf_op jit(solution)/shard_map/pallas_call | solution.py:34
  26.4 5.0 %collective-permute-done.7.co_ref = bf16[272,256]{1,0:T(8,128)(2,1)S(1)} collective-permute-done((bf16[272,256]{1,0:T(8,128)(2,1)S(1)}, bf16[272,256]{1,0:T(8,128)(2,1)S(1)}, u32[]{:S(2)}, u32[]{:S(2)}) %collective-permute-start.7) | collective-permute-done | bytes 139296 | tf_op jit(solution)/shard_map/ppermute | solution.py:74
  31.4 0.0 collective-permute-done.6.high_ref
  31.4 0.0 collective-permute-done.5.low_ref
  31.4 1.1 %shard_map.121 = (bf16[272,256]{1,0:T(8,128)(2,1)S(1)}, bf16[288,256]{1,0:T(8,128)(2,1)S(1)}, f32[256,256]{1,0:T(8,128)S(1)}) custom-call(f32[30]{0:T(128)S(1)} %copy-done.2, bf16[256,1024]{1,0:T(8,128)(2,1)S(1)} %get-tuple-element.33.first_ref, bf16[1024,256]{1,0:T(8,128)(2,1)S(1)} %get-tuple-element.34.second_ref, ...), custom_call_target="tpu_custom_call" | custom-call | flops 1 | bytes 1 | tf_op jit(solution)/shard_map/pallas_call | solution.py:34
  32.5 1.6 %collective-permute-start.9 = (bf16[272,256]{1,0:T(8,128)(2,1)S(1)}, bf16[272,256]{1,0:T(8,128)(2,1)S(1)}, u32[]{:S(2)}, u32[]{:S(2)}) collective-permute-start(bf16[272,256]{1,0:T(8,128)(2,1)S(1)} %get-tuple-element.37.amp_ref.refs_0_), channel_id=1, source_target_pairs={{0,8},{8,0},{16,24},{24,16},{1,9},{9,1},{17,25},{25,17},{2,10},{10... | collective-permute-start | bytes 417800 | tf_op jit(solution)/shard_map/ppermute | solution.py:77
  34.1 1.4 %collective-permute-start.11 = (bf16[288,256]{1,0:T(8,128)(2,1)S(1)}, bf16[288,256]{1,0:T(8,128)(2,1)S(1)}, u32[]{:S(2)}, u32[]{:S(2)}) collective-permute-start(bf16[288,256]{1,0:T(8,128)(2,1)S(1)} %get-tuple-element.41), channel_id=1, source_target_pairs={{0,24},{8,16},{16,8},{24,0},{1,25},{9,17},{17,9},{25,1},{2,26},{10... | collective-permute-start | bytes 442376 | tf_op jit(solution)/shard_map/ppermute | solution.py:77
  35.4 0.6 %collective-permute-start.10 = (bf16[272,256]{1,0:T(8,128)(2,1)S(1)}, bf16[272,256]{1,0:T(8,128)(2,1)S(1)}, u32[]{:S(2)}, u32[]{:S(2)}) collective-permute-start(bf16[272,256]{1,0:T(8,128)(2,1)S(1)} %get-tuple-element.37.amp_ref.refs_0_), channel_id=1, source_target_pairs={{0,16},{8,24},{16,0},{24,8},{1,17},{9,25},{17,1},{25,9},{2,18},{10... | collective-permute-start | bytes 417800 | tf_op jit(solution)/shard_map/ppermute | solution.py:77
  36.1 0.0 collective-permute-start.12
  36.1 3.5 %collective-permute-start.13 = (bf16[256,256]{1,0:T(8,128)(2,1)S(1)}, bf16[256,256]{1,0:T(8,128)(2,1)S(1)}, u32[]{:S(2)}, u32[]{:S(2)}) collective-permute-start(bf16[256,256]{1,0:T(8,128)(2,1)S(1)} %get-tuple-element.45), channel_id=1, source_target_pairs={{0,7},{1,2},{2,1},{3,4},{4,3},{5,6},{6,5},{7,0},{8,15},{9,10},{10,... | collective-permute-start | bytes 393224 | tf_op jit(solution)/shard_map/ppermute | solution.py:74
  39.6 0.4 shard_map.122
  40.0 0.0 collective-permute-done.9.refs_1_
  40.0 4.2 %collective-permute-start.17 = (bf16[288,256]{1,0:T(8,128)(2,1)S(1)}, bf16[288,256]{1,0:T(8,128)(2,1)S(1)}, u32[]{:S(2)}, u32[]{:S(2)}) collective-permute-start(bf16[288,256]{1,0:T(8,128)(2,1)S(1)} %get-tuple-element.51), channel_id=1, source_target_pairs={{0,24},{1,25},{2,26},{3,27},{4,28},{5,29},{6,30},{7,31}} | collective-permute-start | bytes 442376 | tf_op jit(solution)/shard_map/ppermute | solution.py:421
  44.3 0.0 collective-permute-done.10.refs_2_
  44.3 0.0 collective-permute-done.11.refs_3_
  44.3 0.6 shard_map.123.after_ref.refs_4_
  44.9 0.0 collective-permute-done.12.x_0_ref
  44.9 0.0 collective-permute-done.13.x_1_ref
  44.9 0.6 shard_map.125.refs_4_
  45.5 0.9 %collective-permute-start.14 = (bf16[2,256,256]{2,1,0:T(8,128)(2,1)S(1)}, bf16[2,256,256]{2,1,0:T(8,128)(2,1)S(1)}, u32[]{:S(2)}, u32[]{:S(2)}) collective-permute-start(bf16[2,256,256]{2,1,0:T(8,128)(2,1)S(1)} %shard_map.125.refs_4_), channel_id=1, source_target_pairs={{0,7},{1,2},{2,1},{3,4},{4,3},{5,6},{6,5},{7,0},{8,15},{9,10},{10,... | collective-permute-start | bytes 786440 | tf_op jit(solution)/shard_map/ppermute | solution.py:74
  46.4 4.3 %collective-permute-start.18 = (bf16[288,256]{1,0:T(8,128)(2,1)S(1)}, bf16[288,256]{1,0:T(8,128)(2,1)S(1)}, u32[]{:S(2)}, u32[]{:S(2)}) collective-permute-start(bf16[288,256]{1,0:T(8,128)(2,1)S(1)} %get-tuple-element.51), channel_id=1, source_target_pairs={{0,16},{1,17},{2,18},{3,19},{4,20},{5,21},{6,22},{7,23}} | collective-permute-start | bytes 442376 | tf_op jit(solution)/shard_map/ppermute | solution.py:421
  50.8 1.3 %collective-permute-start.19 = (bf16[288,256]{1,0:T(8,128)(2,1)S(1)}, bf16[288,256]{1,0:T(8,128)(2,1)S(1)}, u32[]{:S(2)}, u32[]{:S(2)}) collective-permute-start(bf16[288,256]{1,0:T(8,128)(2,1)S(1)} %get-tuple-element.51), channel_id=1, source_target_pairs={{0,8},{1,9},{2,10},{3,11},{4,12},{5,13},{6,14},{7,15}} | collective-permute-start | bytes 442376 | tf_op jit(solution)/shard_map/ppermute | solution.py:421
  52.1 0.6 shard_map.126
  52.6 0.1 collective-permute-start.15
  52.7 0.0 collective-permute-done.17.refs_0_
  52.7 0.5 collective-permute-start.16
  53.2 0.0 copy-done.3
  53.2 0.6 shard_map.127
  53.8 0.0 collective-permute-done.18.refs_1_
  53.8 0.9 %collective-permute-done.19.refs_2_ = bf16[288,256]{1,0:T(8,128)(2,1)S(1)} collective-permute-done((bf16[288,256]{1,0:T(8,128)(2,1)S(1)}, bf16[288,256]{1,0:T(8,128)(2,1)S(1)}, u32[]{:S(2)}, u32[]{:S(2)}) %collective-permute-start.19) | collective-permute-done | bytes 147488 | tf_op jit(solution)/shard_map/ppermute | solution.py:421
  54.7 0.0 collective-permute-done.15.ci_ref
  54.7 0.0 collective-permute-done.16.cei_ref
  54.7 0.0 collective-permute-done.14.co_ref
  54.7 1.5 %shard_map.128 = (bf16[2,256,256]{2,1,0:T(8,128)(2,1)}, bf16[2,512,256]{2,1,0:T(8,128)(2,1)}) custom-call(f32[30]{0:T(128)S(1)} %copy-done.3, bf16[4,512,256]{2,1,0:T(8,128)(2,1)S(1)} %copy-done, f32[256,256]{1,0:T(8,128)S(1)} %get-tuple-element.31.gain_ref, f32[256,256]{1,0:T(8,128)S(1)} %get-tuple-element.32.gain_extra_ref, ...), custom_call_target="tpu_custom_call" | custom-call | flops 1 | bytes 1 | tf_op jit(solution)/shard_map/pallas_call | solution.py:34
  (6 shorter events, 0.0 us)
Async XLA Ops:
  0.6 23.4 %collective-permute-start.4 = (bf16[2,1024,512]{2,1,0:T(8,128)(2,1)}, bf16[2,1024,512]{2,1,0:T(8,128)(2,1)S(1)}, u32[]{:S(2)}, u32[]{:S(2)}) collective-permute-start(bf16[2,1024,512]{2,1,0:T(8,128)(2,1)} %three_ref.1), channel_id=1, source_target_pairs={{0,1},{1,0},{2,3},{3,2},{4,5},{5,4},{6,7},{7,6},{8,9},{9,8},{10,11... | collective-permute-start | bytes 6291464 | tf_op jit(solution)/shard_map/ppermute | solution.py:71
  1.1 20.3 %collective-permute-start = (bf16[4,512,256]{2,1,0:T(8,128)(2,1)}, bf16[4,512,256]{2,1,0:T(8,128)(2,1)S(1)}, u32[]{:S(2)}, u32[]{:S(2)}) collective-permute-start(bf16[4,512,256]{2,1,0:T(8,128)(2,1)} %coeff_ref.11), channel_id=1, source_target_pairs={{0,1},{1,0},{2,3},{3,2},{4,5},{5,4},{6,7},{7,6},{8,9},{9,8},{10,11... | collective-permute-start | bytes 3145736 | tf_op jit(solution)/shard_map/ppermute | solution.py:71
  1.2 17.9 %collective-permute-start.1 = (bf16[4,256,256]{2,1,0:T(8,128)(2,1)}, bf16[4,256,256]{2,1,0:T(8,128)(2,1)S(1)}, u32[]{:S(2)}, u32[]{:S(2)}) collective-permute-start(bf16[4,256,256]{2,1,0:T(8,128)(2,1)} %amps_ref.5), channel_id=1, source_target_pairs={{0,1},{1,0},{2,3},{3,2},{4,5},{5,4},{6,7},{7,6},{8,9},{9,8},{10,11... | collective-permute-start | bytes 1572872 | tf_op jit(solution)/shard_map/ppermute | solution.py:71
  4.1 8.4 %collective-permute-start.2 = (bf16[528,128]{1,0:T(8,128)(2,1)}, bf16[528,128]{1,0:T(8,128)(2,1)S(1)}, u32[]{:S(2)}, u32[]{:S(2)}) collective-permute-start(bf16[528,128]{1,0:T(8,128)(2,1)} %get-tuple-element.28), channel_id=1, source_target_pairs={{0,7},{1,2},{2,1},{3,4},{4,3},{5,6},{6,5},{7,0},{8,15},{9,10},{10,... | collective-permute-start | bytes 405512 | tf_op jit(solution)/shard_map/ppermute | solution.py:74
  8.9 7.4 %collective-permute-start.3 = (bf16[512,128]{1,0:T(8,128)(2,1)}, bf16[512,128]{1,0:T(8,128)(2,1)S(1)}, u32[]{:S(2)}, u32[]{:S(2)}) collective-permute-start(bf16[512,128]{1,0:T(8,128)(2,1)} %get-tuple-element.29), channel_id=1, source_target_pairs={{0,7},{1,2},{2,1},{3,4},{4,3},{5,6},{6,5},{7,0},{8,15},{9,10},{10,... | collective-permute-start | bytes 393224 | tf_op jit(solution)/shard_map/ppermute | solution.py:74
  9.0 0.7 %copy-start.2 = (f32[30]{0:T(128)S(1)}, f32[30]{0:T(128)}, u32[]{:S(2)}) copy-start(f32[30]{0:T(128)} %get-tuple-element.27.after_ref.nums) | copy-start | bytes 364
  11.2 7.0 %copy-start = (bf16[4,512,256]{2,1,0:T(8,128)(2,1)S(1)}, bf16[4,512,256]{2,1,0:T(8,128)(2,1)}, u32[]{:S(2)}) copy-start(bf16[4,512,256]{2,1,0:T(8,128)(2,1)} %coeff_ref.11) | copy-start | bytes 3145732
  11.2 7.0 %copy-start.1 = (bf16[4,256,256]{2,1,0:T(8,128)(2,1)S(1)}, bf16[4,256,256]{2,1,0:T(8,128)(2,1)}, u32[]{:S(2)}) copy-start(bf16[4,256,256]{2,1,0:T(8,128)(2,1)} %amps_ref.5) | copy-start | bytes 1572868
  13.0 8.4 %copy-start.6 = (bf16[528,128]{1,0:T(8,128)(2,1)S(1)}, bf16[528,128]{1,0:T(8,128)(2,1)}, u32[]{:S(2)}) copy-start(bf16[528,128]{1,0:T(8,128)(2,1)} %get-tuple-element.28) | copy-start | bytes 405508
  13.1 8.4 %copy-start.4 = (f32[4,256]{1,0:T(4,128)S(1)}, f32[4,256]{1,0:T(4,128)}, u32[]{:S(2)}) copy-start(f32[4,256]{1,0:T(4,128)} %eps_ref.1) | copy-start | bytes 12292
  13.1 18.4 %collective-permute-start.5 = (bf16[1040,128]{1,0:T(8,128)(2,1)S(1)}, bf16[1040,128]{1,0:T(8,128)(2,1)S(1)}, u32[]{:S(2)}, u32[]{:S(2)}) collective-permute-start(bf16[1040,128]{1,0:T(8,128)(2,1)S(1)} %shard_map.115.after_ref), channel_id=1, source_target_pairs={{0,7},{1,2},{2,1},{3,4},{4,3},{5,6},{6,5},{7,0},{8,15},{9,10},{10,... | collective-permute-start | bytes 798728 | tf_op jit(solution)/shard_map/ppermute | solution.py:74
  16.8 14.6 %collective-permute-start.6 = (bf16[1024,128]{1,0:T(8,128)(2,1)S(1)}, bf16[1024,128]{1,0:T(8,128)(2,1)S(1)}, u32[]{:S(2)}, u32[]{:S(2)}) collective-permute-start(bf16[1024,128]{1,0:T(8,128)(2,1)S(1)} %shard_map.116.after_ref), channel_id=1, source_target_pairs={{0,7},{1,2},{2,1},{3,4},{4,3},{5,6},{6,5},{7,0},{8,15},{9,10},{10,... | collective-permute-start | bytes 786440 | tf_op jit(solution)/shard_map/ppermute | solution.py:74
  19.1 12.3 %collective-permute-start.7 = (bf16[272,256]{1,0:T(8,128)(2,1)S(1)}, bf16[272,256]{1,0:T(8,128)(2,1)S(1)}, u32[]{:S(2)}, u32[]{:S(2)}) collective-permute-start(bf16[272,256]{1,0:T(8,128)(2,1)S(1)} %get-tuple-element.30.after_ref), channel_id=1, source_target_pairs={{0,7},{1,2},{2,1},{3,4},{4,3},{5,6},{6,5},{7,0},{8,15},{9,10},{10,... | collective-permute-start | bytes 417800 | tf_op jit(solution)/shard_map/ppermute | solution.py:74
  21.4 2.0 %collective-permute-start.8 = (bf16[528,128]{1,0:T(8,128)(2,1)S(1)}, bf16[528,128]{1,0:T(8,128)(2,1)S(1)}, u32[]{:S(2)}, u32[]{:S(2)}) collective-permute-start(bf16[528,128]{1,0:T(8,128)(2,1)S(1)} %copy-done.6), channel_id=1, source_target_pairs={{0,1},{1,0},{2,3},{3,2},{4,5},{5,4},{6,7},{7,6},{8,9},{9,8},{10,11... | collective-permute-start | bytes 405512 | tf_op jit(solution)/shard_map/ppermute | solution.py:71
  24.0 1.3 %copy-start.5 = (bf16[2,1024,512]{2,1,0:T(8,128)(2,1)}, bf16[2,1024,512]{2,1,0:T(8,128)(2,1)S(1)}, u32[]{:S(2)}) copy-start(bf16[2,1024,512]{2,1,0:T(8,128)(2,1)S(1)} %collective-permute-done.4.three_in_ref) | copy-start | bytes 6291460
  32.5 7.5 %collective-permute-start.9 = (bf16[272,256]{1,0:T(8,128)(2,1)S(1)}, bf16[272,256]{1,0:T(8,128)(2,1)S(1)}, u32[]{:S(2)}, u32[]{:S(2)}) collective-permute-start(bf16[272,256]{1,0:T(8,128)(2,1)S(1)} %get-tuple-element.37.amp_ref.refs_0_), channel_id=1, source_target_pairs={{0,8},{8,0},{16,24},{24,16},{1,9},{9,1},{17,25},{25,17},{2,10},{10... | collective-permute-start | bytes 417800 | tf_op jit(solution)/shard_map/ppermute | solution.py:77
  34.1 10.2 %collective-permute-start.11 = (bf16[288,256]{1,0:T(8,128)(2,1)S(1)}, bf16[288,256]{1,0:T(8,128)(2,1)S(1)}, u32[]{:S(2)}, u32[]{:S(2)}) collective-permute-start(bf16[288,256]{1,0:T(8,128)(2,1)S(1)} %get-tuple-element.41), channel_id=1, source_target_pairs={{0,24},{8,16},{16,8},{24,0},{1,25},{9,17},{17,9},{25,1},{2,26},{10... | collective-permute-start | bytes 442376 | tf_op jit(solution)/shard_map/ppermute | solution.py:77
  35.4 8.8 %collective-permute-start.10 = (bf16[272,256]{1,0:T(8,128)(2,1)S(1)}, bf16[272,256]{1,0:T(8,128)(2,1)S(1)}, u32[]{:S(2)}, u32[]{:S(2)}) collective-permute-start(bf16[272,256]{1,0:T(8,128)(2,1)S(1)} %get-tuple-element.37.amp_ref.refs_0_), channel_id=1, source_target_pairs={{0,16},{8,24},{16,0},{24,8},{1,17},{9,25},{17,1},{25,9},{2,18},{10... | collective-permute-start | bytes 417800 | tf_op jit(solution)/shard_map/ppermute | solution.py:77
  36.1 8.8 %collective-permute-start.12 = (bf16[256,256]{1,0:T(8,128)(2,1)S(1)}, bf16[256,256]{1,0:T(8,128)(2,1)S(1)}, u32[]{:S(2)}, u32[]{:S(2)}) collective-permute-start(bf16[256,256]{1,0:T(8,128)(2,1)S(1)} %get-tuple-element.44), channel_id=1, source_target_pairs={{0,7},{1,2},{2,1},{3,4},{4,3},{5,6},{6,5},{7,0},{8,15},{9,10},{10,... | collective-permute-start | bytes 393224 | tf_op jit(solution)/shard_map/ppermute | solution.py:74
  36.1 8.8 %collective-permute-start.13 = (bf16[256,256]{1,0:T(8,128)(2,1)S(1)}, bf16[256,256]{1,0:T(8,128)(2,1)S(1)}, u32[]{:S(2)}, u32[]{:S(2)}) collective-permute-start(bf16[256,256]{1,0:T(8,128)(2,1)S(1)} %get-tuple-element.45), channel_id=1, source_target_pairs={{0,7},{1,2},{2,1},{3,4},{4,3},{5,6},{6,5},{7,0},{8,15},{9,10},{10,... | collective-permute-start | bytes 393224 | tf_op jit(solution)/shard_map/ppermute | solution.py:74
  40.0 12.7 %collective-permute-start.17 = (bf16[288,256]{1,0:T(8,128)(2,1)S(1)}, bf16[288,256]{1,0:T(8,128)(2,1)S(1)}, u32[]{:S(2)}, u32[]{:S(2)}) collective-permute-start(bf16[288,256]{1,0:T(8,128)(2,1)S(1)} %get-tuple-element.51), channel_id=1, source_target_pairs={{0,24},{1,25},{2,26},{3,27},{4,28},{5,29},{6,30},{7,31}} | collective-permute-start | bytes 442376 | tf_op jit(solution)/shard_map/ppermute | solution.py:421
  44.9 8.3 %copy-start.3 = (f32[30]{0:T(128)S(1)}, f32[30]{0:T(128)}, u32[]{:S(2)}) copy-start(f32[30]{0:T(128)} %get-tuple-element.27.after_ref.nums) | copy-start | bytes 364
  45.5 9.2 %collective-permute-start.14 = (bf16[2,256,256]{2,1,0:T(8,128)(2,1)S(1)}, bf16[2,256,256]{2,1,0:T(8,128)(2,1)S(1)}, u32[]{:S(2)}, u32[]{:S(2)}) collective-permute-start(bf16[2,256,256]{2,1,0:T(8,128)(2,1)S(1)} %shard_map.125.refs_4_), channel_id=1, source_target_pairs={{0,7},{1,2},{2,1},{3,4},{4,3},{5,6},{6,5},{7,0},{8,15},{9,10},{10,... | collective-permute-start | bytes 786440 | tf_op jit(solution)/shard_map/ppermute | solution.py:74
  46.4 7.4 %collective-permute-start.18 = (bf16[288,256]{1,0:T(8,128)(2,1)S(1)}, bf16[288,256]{1,0:T(8,128)(2,1)S(1)}, u32[]{:S(2)}, u32[]{:S(2)}) collective-permute-start(bf16[288,256]{1,0:T(8,128)(2,1)S(1)} %get-tuple-element.51), channel_id=1, source_target_pairs={{0,16},{1,17},{2,18},{3,19},{4,20},{5,21},{6,22},{7,23}} | collective-permute-start | bytes 442376 | tf_op jit(solution)/shard_map/ppermute | solution.py:421
  50.8 4.0 %collective-permute-start.19 = (bf16[288,256]{1,0:T(8,128)(2,1)S(1)}, bf16[288,256]{1,0:T(8,128)(2,1)S(1)}, u32[]{:S(2)}, u32[]{:S(2)}) collective-permute-start(bf16[288,256]{1,0:T(8,128)(2,1)S(1)} %get-tuple-element.51), channel_id=1, source_target_pairs={{0,8},{1,9},{2,10},{3,11},{4,12},{5,13},{6,14},{7,15}} | collective-permute-start | bytes 442376 | tf_op jit(solution)/shard_map/ppermute | solution.py:421
  52.6 2.1 %collective-permute-start.15 = (bf16[272,256]{1,0:T(8,128)(2,1)S(1)}, bf16[272,256]{1,0:T(8,128)(2,1)S(1)}, u32[]{:S(2)}, u32[]{:S(2)}) collective-permute-start(bf16[272,256]{1,0:T(8,128)(2,1)S(1)} %get-tuple-element.47.refs_4_), channel_id=1, source_target_pairs={{0,1},{1,0},{2,3},{3,2},{4,5},{5,4},{6,7},{7,6},{8,9},{9,8},{10,11... | collective-permute-start | bytes 417800 | tf_op jit(solution)/shard_map/ppermute | solution.py:71
  52.7 2.0 %collective-permute-start.16 = (bf16[272,256]{1,0:T(8,128)(2,1)S(1)}, bf16[272,256]{1,0:T(8,128)(2,1)S(1)}, u32[]{:S(2)}, u32[]{:S(2)}) collective-permute-start(bf16[272,256]{1,0:T(8,128)(2,1)S(1)} %get-tuple-element.50), channel_id=1, source_target_pairs={{0,1},{1,0},{2,3},{3,2},{4,5},{5,4},{6,7},{7,6},{8,9},{9,8},{10,11... | collective-permute-start | bytes 417800 | tf_op jit(solution)/shard_map/ppermute | solution.py:71

commit v14 on v12

--- a/solution.py
+++ b/solution.py
@@ -14,7 +14,6 @@
 NT = ((1,), (1,))
 
 VMEM = pl.BlockSpec(memory_space=pltpu.VMEM)
-SMEM = pl.BlockSpec(memory_space=pltpu.SMEM)
 ANY = pl.BlockSpec(memory_space=pl.ANY)
 HBM = pl.BlockSpec(memory_space=pltpu.HBM)
 
@@ -23,6 +22,11 @@
 
 def whole(number):
     return number.astype(jnp.int32)
+
+
+def read(nums_ref):
+    row = nums_ref[0:1, :]
+    return lambda at: row[0, at], lambda at: row[:, at : at + 1]
 
 
 def mxu(a, b, dims):
@@ -102,7 +106,7 @@
 
     def plan_body(
         owner_hbm, occ_hbm, partner_hbm, coupling_hbm, eps_hbm, nvirt_hbm, coeff_hbm,
-        low_ref, high_ref, nums,
+        low_ref, high_ref, nums_ref,
         owner_ref, occ_ref, partner_ref, coupling_ref, eps_ref, nvirt_ref, near_w, sems,
     ):
         small = [
@@ -134,11 +138,12 @@
             copy.start()
         for copy in small[1:]:
             copy.wait()
+        nums = {}
         nums[MINE] = mine.astype(F32)
         nums[EXTRA] = extra.astype(F32)
         nums[OWNER] = owner_ref[extra].astype(F32)
-        for s in range(roles):
-            nums[ROLE_PAIR + s] = of_role[s].astype(F32)
+        for m in range(roles):
+            nums[ROLE_PAIR + m] = pick(of_role, role ^ m).astype(F32)
         nums[NV_MINE] = nvirt_ref[mine].astype(F32)
         nums[NV_EXTRA] = nvirt_ref[extra].astype(F32)
         nums[FIRST] = (occ_ref[0, mine] - column * occ_block).astype(F32)
@@ -171,6 +176,11 @@
                 nums[own_weights + weights + to] = near_w[inner_at * pairs + q]
                 told = jnp.where(lane == to, near_w[outer_at * pairs + q], told)
                 told = jnp.where(lane == weights + to, near_w[inner_at * pairs + q], told)
+        row_of_nums = jnp.zeros(nums_ref.shape, F32)
+        lane_of_nums = lax.broadcasted_iota(I32, nums_ref.shape, 1)
+        for at, number in nums.items():
+            row_of_nums = jnp.where(lane_of_nums == at, number, row_of_nums)
+        nums_ref[...] = row_of_nums
         coarse = told.astype(BF16).astype(F32)
         middle = (told - coarse).astype(BF16).astype(F32)
         fine = told - coarse - middle
@@ -183,7 +193,7 @@
     x_low, x_high, nums = call(
         plan_body,
         [HBM] * 7,
-        [rode, (VMEM, (pao, part), BF16), (SMEM, (own_weights + 2 * weights,), F32)],
+        [rode, (VMEM, (pao, part), BF16), (VMEM, (8, part), F32)],
         (pair_owner, pair_occ.T, partners, coupling, eps_occ, nvirt, coeff),
         scratch=[
             pltpu.SMEM(pair_owner.shape, I32),
@@ -282,9 +292,10 @@
     def own_half_body(
         nums, three_ref, three_in_ref, coeff_ref, after_ref, first_ref, second_ref, extra_ref, block_ref, sem
     ):
-        x = coeff_ref[whole(nums[MINE])]
-        extra_ref[...] = coeff_ref[whole(nums[EXTRA])]
-        whose, second = whole(nums[WHOSE]), whole(nums[SECOND])
+        num, _ = read(nums)
+        x = coeff_ref[whole(num(MINE))]
+        extra_ref[...] = coeff_ref[whole(num(EXTRA))]
+        whose, second = whole(num(WHOSE)), whole(num(SECOND))
         copy = pltpu.make_async_copy(three_in_ref.at[second], block_ref.at[0], sem)
 
         @pl.when(whose == 1)
@@ -292,7 +303,7 @@
             copy.start()
 
         turned = x.T
-        first = whole(nums[FIRST])
+        first = whole(num(FIRST))
         for rows in tiles:
             first_ref[:, rows] = (mxu(turned, three_ref[first, rows, :], NT) * pao_scale).astype(BF16)
 
@@ -307,7 +318,7 @@
 
     first_t, second, x_extra = call(
         own_half_body,
-        [SMEM, VMEM, ANY, VMEM, ANY],
+        [VMEM, VMEM, ANY, VMEM, ANY],
         [
             (VMEM, (virt, aux), BF16),
             (VMEM, (aux, virt), BF16),
@@ -322,7 +333,8 @@
         nums, coeff_ref, coeff_in_ref, amps_ref, amps_in_ref, eps_ref, after_ref,
         s_ref, c_ref, gain_ref, gain_extra_ref, s_in_ref,
     ):
-        mine, extra = whole(nums[MINE]), whole(nums[EXTRA])
+        num, weight = read(nums)
+        mine, extra = whole(num(MINE)), whole(num(EXTRA))
         x = coeff_ref[mine]
         total = None
         for at, of_s, of_coeff, of_amps in (
@@ -330,7 +342,7 @@
             (own_weights + weights, s_in_ref, coeff_in_ref, amps_in_ref),
         ):
             overlaps(x, of_coeff, of_s)
-            c = coupled(of_s, [(q, nums[at + q], of_amps[q]) for q in range(pairs)])
+            c = coupled(of_s, [(q, weight(at + q), of_amps[q]) for q in range(pairs)])
             total = c if total is None else total + c
         c_ref[...] = total
 
@@ -342,12 +354,12 @@
             )
             return jnp.where(inside, 1.0 / (energy + 1.0), 0.0)
 
-        gain_ref[...] = gain(mine, whole(nums[NV_MINE]), nums[OCC_MINE])
-        gain_extra_ref[...] = gain(extra, whole(nums[NV_EXTRA]), nums[OCC_EXTRA])
+        gain_ref[...] = gain(mine, whole(num(NV_MINE)), num(OCC_MINE))
+        gain_extra_ref[...] = gain(extra, whole(num(NV_EXTRA)), num(OCC_EXTRA))
 
     s_own, c_own, gain, gain_extra = call(
         own_body,
-        [SMEM] + [VMEM] * 5 + [ANY],
+        [VMEM] + [VMEM] * 5 + [ANY],
         [all_s, sq_f, sq_f, sq_f],
         (nums, coeff, coeff_in, amps, amps_in, eps_virt, c_out),
         scratch=[pltpu.VMEM((pairs, virt, virt), BF16)],
@@ -357,13 +369,14 @@
         @pl.when(lax.axis_index("role") > 0)
         def _():
             told = told_of(low_ref)
-            overlaps(coeff_ref[whole(nums[EXTRA])], coeff_ref, se_ref)
+            num, _ = read(nums)
+            overlaps(coeff_ref[whole(num(EXTRA))], coeff_ref, se_ref)
             overlaps(in_ref[whole(told[0, mine_at])], coeff_ref, s_in_ref)
             overlaps(in_ref[whole(told[0, extra_at])], coeff_ref, se_in_ref)
 
     se_own, s_in, se_in = call(
         more_body,
-        [SMEM, VMEM, VMEM, VMEM, ANY],
+        [VMEM, VMEM, VMEM, VMEM, ANY],
         [all_s, all_s, all_s],
         (nums, coeff, coeff_in, low_in, c_own),
     )
@@ -373,7 +386,8 @@
         amp_ref, amp_long_ref, k_ref,
     ):
         first = first_ref[...]
-        outside = whole(nums[WHOSE]) == 2
+        num, _ = read(nums)
+        outside = whole(num(WHOSE)) == 2
 
         @pl.when(outside)
         def _():
@@ -384,7 +398,7 @@
         def _():
             k_ref[...] = mxu(first, second_ref[...], NN) * aux_scale
 
-        old = amps_ref[whole(nums[MINE])].astype(F32)
+        old = amps_ref[whole(num(MINE))].astype(F32)
         c = c_ref[...] + co_ref[:virt, :].astype(F32)
         amp = (gain_ref[...] * (old - k_ref[...] - c)).astype(BF16)
         amp_ref[...] = amp
@@ -393,7 +407,7 @@
 
     amp, amp_long, k_first = call(
         first_body,
-        [SMEM] + [VMEM] * 8 + [ANY],
+        [VMEM] + [VMEM] * 8 + [ANY],
         [sq_b, longer, sq_f],
         (
             nums, first_t, second, y_low_from_out, y_high_from_out,
@@ -429,10 +443,10 @@
     )
 
     def parts_of(nums, weight_of, amp_refs):
-        role = lax.axis_index("role")
+        num, _ = read(nums)
         parts = []
         for m in range(roles):
-            at = whole(nums[ROLE_PAIR + (role ^ m)])
+            at = whole(num(ROLE_PAIR + m))
             parts.append((at, weight_of(at), amp_refs[m][:virt, :]))
         return parts
 
@@ -451,7 +465,7 @@
 
     (cc_out,) = call(
         outer_again_body,
-        [SMEM] + [VMEM] * (3 + roles),
+        [VMEM] + [VMEM] * (3 + roles),
         [two_b],
         (nums, low_out, s_out, se_out, *amp_roles),
     )
@@ -470,7 +484,7 @@
 
     c_in, ce_in = call(
         inner_again_body,
-        [SMEM] + [VMEM] * (3 + roles) + [ANY],
+        [VMEM] + [VMEM] * (3 + roles) + [ANY],
         [longer, longer],
         (nums, low_in, s_in, se_in, *amp_roles, cc_out),
     )
@@ -481,14 +495,15 @@
 
         @pl.when(lax.axis_index("role") > 0)
         def _():
-            parts = parts_of(nums, lambda at: nums[own_weights + at], amp_refs)
+            row = nums[0:1, :]
+            parts = parts_of(nums, told_weight(row, own_weights), amp_refs)
             out_ref[...] = rest_ref[...] - coupled(s_ref, parts)
-            parts = parts_of(nums, lambda at: nums[own_weights + pairs + at], amp_refs)
+            parts = parts_of(nums, told_weight(row, own_weights + pairs), amp_refs)
             out_extra_ref[...] = -coupled(se_ref, parts)
 
     rest, rest_extra = call(
         own_again_body,
-        [SMEM] + [VMEM] * (3 + roles) + [ANY],
+        [VMEM] + [VMEM] * (3 + roles) + [ANY],
         [sq_f, sq_f],
         (nums, rest, s_own, se_own, *amp_roles, c_in),
     )
@@ -497,6 +512,7 @@
         nums, coeff_ref, gain_ref, gain_extra_ref, rest_ref, rest_extra_ref, co_ref, ci_ref, cei_ref, *refs
     ):
         rest_refs, (amp_out, orb_out, amp_ref, orb_ref, sems) = refs[: roles - 1], refs[roles - 1 :]
+        num, _ = read(nums)
         role = lax.axis_index("role")
         copies = []
 
@@ -534,15 +550,15 @@
 
                 send(orb_ref.at[slot, rows], orb_out.at[slot, rows])
 
-        store(0, role > 0, gain_ref, rest_ref, ci_ref, whole(nums[MINE]))
-        has_extra = role == whole(nums[OWNER])
-        store(1, has_extra, gain_extra_ref, rest_extra_ref, cei_ref, whole(nums[EXTRA]))
+        store(0, role > 0, gain_ref, rest_ref, ci_ref, whole(num(MINE)))
+        has_extra = role == whole(num(OWNER))
+        store(1, has_extra, gain_extra_ref, rest_extra_ref, cei_ref, whole(num(EXTRA)))
         for copy in copies:
             copy.wait()
 
     amps_out, dressed_out = call(
         last_body,
-        [SMEM] + [VMEM] * (8 + roles - 1),
+        [VMEM] + [VMEM] * (8 + roles - 1),
         [(ANY, (slots, virt, virt), BF16), (ANY, (slots, pao, virt), BF16)],
         (
             nums, coeff, gain, gain_extra, rest, rest_extra,

time: 52.4 us -> 51.1 us (0.975)
  Pallas kernels: 15.5 us -> 10.1 us
  waiting for transfers between devices: 6.5 us -> 9.23 us
  starting transfers between devices: 27.1 us -> 28.3 us
    pallas_call x15, Pallas kernels: 15.5 us -> 10.1 us  [call(): pl.pallas_call(body, in_specs=ins, out_specs=[spec for spec, _, _ in outs...]
    ppermute x7, waiting for transfers between devices: 5.54 us -> 7.17 us  [outer(): return lax.ppermute(x, 'pairs', list(enumerate(outer_of)))]
    ppermute x7, starting transfers between devices: 12.8 us -> 14.2 us  [outer(): return lax.ppermute(x, 'pairs', list(enumerate(outer_of)))]
    ppermute x3, waiting for transfers between devices: 0.94 us -> 2.04 us  [local(): lax.ppermute(rest_b, 'role', [(0, s)])]
  transfers between devices with their start and end apart: 19 -> 19, of which waited for: 3 -> 4; matrix products, arithmetic and copies ran while one was open for 0% -> 0% of each run, Pallas kernels for 27% -> 18%
where the time goes in v14:
time: 51.1 us; the launch traced here: 50.6 us
  starting transfers between devices  28.3 us (55%)
  Pallas kernels  10.1 us (20%)
  waiting for transfers between devices  9.23 us (18%)
  local copies, waits for them, and re-layouts  1.98 us (4%)
  between operations  0.88 us (2%)
    ppermute x7, starting transfers between devices, outer(): return lax.ppermute(x, 'pairs', list(enumerate(outer_of)))  14.2 us
    pallas_call x15, Pallas kernels, call(): pl.pallas_call(body, in_specs=ins, out_specs=[spec for spec, _, _ in outs...  10.1 us
    ppermute x3, starting transfers between devices, local(): lax.ppermute(rest_b, 'role', [(0, s)])  8.97 us
    ppermute x7, waiting for transfers between devices, outer(): return lax.ppermute(x, 'pairs', list(enumerate(outer_of)))  7.17 us
    ppermute x3, starting transfers between devices, swap(): return lax.ppermute(x, 'role', [(i, i ^ by) for i in range(roles)])  3.55 us
    ppermute x3, waiting for transfers between devices, local(): lax.ppermute(rest_b, 'role', [(0, s)])  2.04 us
    unnamed x14, local copies, waits for them, and re-layouts  1.98 us
    ppermute x6, starting transfers between devices, inner(): return lax.ppermute(x, 'pairs', list(enumerate(inner_of)))  1.66 us
  transfers between devices with their start and end apart: 19, of which 4 were waited for; matrix products, arithmetic and copies ran while one was open for 0% of the time, Pallas kernels for 18%

profile of v14, /device:TPU:0, one launch (start us, length us, event | category | flops | bytes accessed | tf_op | source)
XLA Modules:
  0.0 50.6 jit_solution(2974442845660106524)
XLA Ops:
  0.6 0.5 %collective-permute-start.4 = (bf16[2,1024,512]{2,1,0:T(8,128)(2,1)}, bf16[2,1024,512]{2,1,0:T(8,128)(2,1)S(1)}, u32[]{:S(2)}, u32[]{:S(2)}) collective-permute-start(bf16[2,1024,512]{2,1,0:T(8,128)(2,1)} %three_ref.1), channel_id=1, source_target_pairs={{0,1},{1,0},{2,3},{3,2},{4,5},{5,4},{6,7},{7,6},{8,9},{9,8},{10,11... | collective-permute-start | bytes 6291464 | tf_op jit(solution)/shard_map/ppermute | solution.py:74
  1.1 0.1 collective-permute-start
  1.2 0.4 collective-permute-start.1
  1.7 2.4 %shard_map.113 = (bf16[528,128]{1,0:T(8,128)(2,1)}, bf16[512,128]{1,0:T(8,128)(2,1)}, f32[8,128]{1,0:T(8,128)}) custom-call(s32[4]{0:T(128)} %owner_hbm.1, s32[2,4]{1,0:T(2,128)} %bitcast.1, s32[4,8]{1,0:T(4,128)} %partner_hbm.1, f32[4,8]{1,0:T(4,128)} %coupling_hbm.1, f32[16]{0:T(128)} %eps_hbm.1, s32[4]{0:T(128)} %nvirt_hbm.1, bf16[4,512,256]{2,1,0:T(8,128)(2,1)} %coeff_ref.11), custom_call_target="tpu_custom_call" | custom-call | flops 1 | bytes 1 | tf_op jit(solution)/shard_map/pallas_call | solution.py:37
  4.1 4.8 %collective-permute-start.2 = (bf16[528,128]{1,0:T(8,128)(2,1)}, bf16[528,128]{1,0:T(8,128)(2,1)S(1)}, u32[]{:S(2)}, u32[]{:S(2)}) collective-permute-start(bf16[528,128]{1,0:T(8,128)(2,1)} %get-tuple-element.27), channel_id=1, source_target_pairs={{0,7},{1,2},{2,1},{3,4},{4,3},{5,6},{6,5},{7,0},{8,15},{9,10},{10,... | collective-permute-start | bytes 405512 | tf_op jit(solution)/shard_map/ppermute | solution.py:77
  8.9 0.1 collective-permute-start.3
  8.9 0.0 copy-start.2
  8.9 0.7 %copy-done.2 = f32[8,128]{1,0:T(8,128)S(1)} copy-done((f32[8,128]{1,0:T(8,128)S(1)}, f32[8,128]{1,0:T(8,128)}, u32[]{:S(2)}) %copy-start.2) | copy-done | bytes 4120
  9.6 1.6 %shard_map.114.three_ref = bf16[2,1024,512]{2,1,0:T(8,128)(2,1)S(1)} custom-call(bf16[2,1024,512]{2,1,0:T(8,128)(2,1)} %three_ref.1, f32[8,128]{1,0:T(8,128)S(1)} %copy-done.2), custom_call_target="tpu_custom_call" | custom-call | flops 1 | bytes 1 | tf_op jit(solution)/shard_map/pallas_call | solution.py:37
  11.2 0.0 copy-start
  11.2 0.0 copy-start.1
  11.2 1.3 %collective-permute-done.2.x_ref.low_ref = bf16[528,128]{1,0:T(8,128)(2,1)S(1)} collective-permute-done((bf16[528,128]{1,0:T(8,128)(2,1)}, bf16[528,128]{1,0:T(8,128)(2,1)S(1)}, u32[]{:S(2)}, u32[]{:S(2)}) %collective-permute-start.2) | collective-permute-done | bytes 135200 | tf_op jit(solution)/shard_map/ppermute | solution.py:77
  12.5 0.5 %shard_map.115.after_ref = bf16[1040,128]{1,0:T(8,128)(2,1)S(1)} custom-call(bf16[2,1024,512]{2,1,0:T(8,128)(2,1)S(1)} %shard_map.114.three_ref, bf16[528,128]{1,0:T(8,128)(2,1)S(1)} %collective-permute-done.2.x_ref.low_ref), custom_call_target="tpu_custom_call" | custom-call | flops 1 | bytes 1 | tf_op jit(solution)/shard_map/pallas_call | solution.py:37
  13.0 0.0 copy-start.6
  13.1 0.0 copy-start.3
  13.1 3.2 %collective-permute-start.5 = (bf16[1040,128]{1,0:T(8,128)(2,1)S(1)}, bf16[1040,128]{1,0:T(8,128)(2,1)S(1)}, u32[]{:S(2)}, u32[]{:S(2)}) collective-permute-start(bf16[1040,128]{1,0:T(8,128)(2,1)S(1)} %shard_map.115.after_ref), channel_id=1, source_target_pairs={{0,7},{1,2},{2,1},{3,4},{4,3},{5,6},{6,5},{7,0},{8,15},{9,10},{10,... | collective-permute-start | bytes 798728 | tf_op jit(solution)/shard_map/ppermute | solution.py:77
  16.3 0.0 collective-permute-done.3.x_ref.high_ref
  16.3 0.5 %shard_map.116.after_ref = bf16[1024,128]{1,0:T(8,128)(2,1)S(1)} custom-call(bf16[2,1024,512]{2,1,0:T(8,128)(2,1)S(1)} %shard_map.114.three_ref, bf16[528,128]{1,0:T(8,128)(2,1)S(1)} %collective-permute-done.2.x_ref.low_ref, bf16[512,128]{1,0:T(8,128)(2,1)S(1)} %collective-permute-done.3.x_ref.high_ref, bf16[1040,128]{1,0:T(8,128)(2,1)S(1)} %shard_map.115.after_ref), custom_call_target="tpu_custom_call" | custom-call | flops 1 | bytes 1 | tf_op jit(solution)/shard_map/pallas_call | solution.py:37
  16.8 1.4 %collective-permute-start.6 = (bf16[1024,128]{1,0:T(8,128)(2,1)S(1)}, bf16[1024,128]{1,0:T(8,128)(2,1)S(1)}, u32[]{:S(2)}, u32[]{:S(2)}) collective-permute-start(bf16[1024,128]{1,0:T(8,128)(2,1)S(1)} %shard_map.116.after_ref), channel_id=1, source_target_pairs={{0,7},{1,2},{2,1},{3,4},{4,3},{5,6},{6,5},{7,0},{8,15},{9,10},{10,... | collective-permute-start | bytes 786440 | tf_op jit(solution)/shard_map/ppermute | solution.py:77
  18.2 0.0 copy-done
  18.2 0.0 copy-done.1
  18.2 0.9 %shard_map.117 = (bf16[4,256,256]{2,1,0:T(8,128)(2,1)S(1)}, bf16[272,256]{1,0:T(8,128)(2,1)S(1)}) custom-call(bf16[4,512,256]{2,1,0:T(8,128)(2,1)S(1)} %copy-done, bf16[4,256,256]{2,1,0:T(8,128)(2,1)S(1)} %copy-done.1, bf16[528,128]{1,0:T(8,128)(2,1)S(1)} %collective-permute-done.2.x_ref.low_ref, bf16[512,128]{1,0:T(8,128)(2,1)S(1)} %collective-permute-done.3.x_ref.high_ref, ...), custom_call_target="tpu_custom_call" | custom-call | flops 1 | bytes 1 | tf_op jit(solution)/shard_map/pallas_call | solution.py:37
  19.1 0.0 collective-permute-done.1.amps_in_ref
  19.1 0.0 copy-start.4
  19.1 2.3 %collective-permute-start.7 = (bf16[272,256]{1,0:T(8,128)(2,1)S(1)}, bf16[272,256]{1,0:T(8,128)(2,1)S(1)}, u32[]{:S(2)}, u32[]{:S(2)}) collective-permute-start(bf16[272,256]{1,0:T(8,128)(2,1)S(1)} %get-tuple-element.29.after_ref), channel_id=1, source_target_pairs={{0,7},{1,2},{2,1},{3,4},{4,3},{5,6},{6,5},{7,0},{8,15},{9,10},{10,... | collective-permute-start | bytes 417800 | tf_op jit(solution)/shard_map/ppermute | solution.py:77
  21.4 0.0 collective-permute-done.4.three_in_ref
  21.4 0.0 copy-done.6
  21.4 0.0 copy-start.5
  21.4 0.1 collective-permute-start.8
  21.5 1.3 %copy-done.5 = bf16[2,1024,512]{2,1,0:T(8,128)(2,1)} copy-done((bf16[2,1024,512]{2,1,0:T(8,128)(2,1)}, bf16[2,1024,512]{2,1,0:T(8,128)(2,1)S(1)}, u32[]{:S(2)}) %copy-start.5) | copy-done | bytes 2097176
  22.8 0.0 copy-done.3
  22.8 0.6 %shard_map.119 = (bf16[256,1024]{1,0:T(8,128)(2,1)S(1)}, bf16[1024,256]{1,0:T(8,128)(2,1)S(1)}, bf16[512,256]{1,0:T(8,128)(2,1)S(1)}) custom-call(f32[8,128]{1,0:T(8,128)S(1)} %copy-done.3, bf16[2,1024,512]{2,1,0:T(8,128)(2,1)S(1)} %shard_map.114.three_ref, bf16[2,1024,512]{2,1,0:T(8,128)(2,1)} %copy-done.5, bf16[4,512,256]{2,1,0:T(8,128)(2,1)S(1)} %copy-done, ...), custom_call_target="tpu_custom_call" | custom-call | flops 1 | bytes 1 | tf_op jit(solution)/shard_map/pallas_call | solution.py:37
  23.4 0.0 collective-permute-done.coeff_in_ref.in_ref
  23.4 1.4 %collective-permute-start.12 = (bf16[512,256]{1,0:T(8,128)(2,1)S(1)}, bf16[512,256]{1,0:T(8,128)(2,1)S(1)}, u32[]{:S(2)}, u32[]{:S(2)}) collective-permute-start(bf16[512,256]{1,0:T(8,128)(2,1)S(1)} %get-tuple-element.44), channel_id=1, source_target_pairs={{0,7},{1,2},{2,1},{3,4},{4,3},{5,6},{6,5},{7,0},{8,15},{9,10},{10,... | collective-permute-start | bytes 786440 | tf_op jit(solution)/shard_map/ppermute | solution.py:77
  24.8 0.0 copy-done.4
  24.8 1.5 %shard_map.118 = (bf16[4,256,256]{2,1,0:T(8,128)(2,1)S(1)}, f32[256,256]{1,0:T(8,128)S(1)}, f32[256,256]{1,0:T(8,128)S(1)}, f32[256,256]{1,0:T(8,128)S(1)}) custom-call(f32[8,128]{1,0:T(8,128)S(1)} %copy-done.3, bf16[4,512,256]{2,1,0:T(8,128)(2,1)S(1)} %copy-done, bf16[4,512,256]{2,1,0:T(8,128)(2,1)S(1)} %collective-permute-done.coeff_in_ref.in_ref, ...), custom_call_target="tpu_custom_call" | custom-call | flops 1 | bytes 1 | tf_op jit(solution)/shard_map/pallas_call | solution.py:37
  26.3 0.0 collective-permute-done.8.low_ref
  26.3 5.9 %collective-permute-done.7.co_ref = bf16[272,256]{1,0:T(8,128)(2,1)S(1)} collective-permute-done((bf16[272,256]{1,0:T(8,128)(2,1)S(1)}, bf16[272,256]{1,0:T(8,128)(2,1)S(1)}, u32[]{:S(2)}, u32[]{:S(2)}) %collective-permute-start.7) | collective-permute-done | bytes 139296 | tf_op jit(solution)/shard_map/ppermute | solution.py:77
  32.2 0.0 collective-permute-done.6.high_ref
  32.2 0.0 collective-permute-done.5.low_ref
  32.2 0.7 %shard_map.121 = (bf16[256,256]{1,0:T(8,128)(2,1)S(1)}, bf16[272,256]{1,0:T(8,128)(2,1)S(1)}, f32[256,256]{1,0:T(8,128)S(1)}) custom-call(f32[8,128]{1,0:T(8,128)S(1)} %copy-done.3, bf16[256,1024]{1,0:T(8,128)(2,1)S(1)} %get-tuple-element.32.first_ref, bf16[1024,256]{1,0:T(8,128)(2,1)S(1)} %get-tuple-element.33.second_ref, ...), custom_call_target="tpu_custom_call" | custom-call | flops 1 | bytes 1 | tf_op jit(solution)/shard_map/pallas_call | solution.py:37
  32.9 2.4 %collective-permute-start.11 = (bf16[272,256]{1,0:T(8,128)(2,1)S(1)}, bf16[272,256]{1,0:T(8,128)(2,1)S(1)}, u32[]{:S(2)}, u32[]{:S(2)}) collective-permute-start(bf16[272,256]{1,0:T(8,128)(2,1)S(1)} %get-tuple-element.40), channel_id=1, source_target_pairs={{0,24},{8,16},{16,8},{24,0},{1,25},{9,17},{17,9},{25,1},{2,26},{10... | collective-permute-start | bytes 417800 | tf_op jit(solution)/shard_map/ppermute | solution.py:80
  35.3 0.5 %collective-permute-start.9 = (bf16[256,256]{1,0:T(8,128)(2,1)S(1)}, bf16[256,256]{1,0:T(8,128)(2,1)S(1)}, u32[]{:S(2)}, u32[]{:S(2)}) collective-permute-start(bf16[256,256]{1,0:T(8,128)(2,1)S(1)} %get-tuple-element.36.amp_ref.after_ref.refs_0_), channel_id=1, source_target_pairs={{0,8},{8,0},{16,24},{24,16},{1,9},{9,1},{17,25},{25,17},{2,10},{10... | collective-permute-start | bytes 393224 | tf_op jit(solution)/shard_map/ppermute | solution.py:80
  35.8 0.6 %collective-permute-start.10 = (bf16[256,256]{1,0:T(8,128)(2,1)S(1)}, bf16[256,256]{1,0:T(8,128)(2,1)S(1)}, u32[]{:S(2)}, u32[]{:S(2)}) collective-permute-start(bf16[256,256]{1,0:T(8,128)(2,1)S(1)} %get-tuple-element.36.amp_ref.after_ref.refs_0_), channel_id=1, source_target_pairs={{0,16},{8,24},{16,0},{24,8},{1,17},{9,25},{17,1},{25,9},{2,18},{10... | collective-permute-start | bytes 393224 | tf_op jit(solution)/shard_map/ppermute | solution.py:80
  36.4 0.4 shard_map.122
  36.8 4.2 %collective-permute-start.16 = (bf16[288,256]{1,0:T(8,128)(2,1)S(1)}, bf16[288,256]{1,0:T(8,128)(2,1)S(1)}, u32[]{:S(2)}, u32[]{:S(2)}) collective-permute-start(bf16[288,256]{1,0:T(8,128)(2,1)S(1)} %get-tuple-element.49), channel_id=1, source_target_pairs={{0,24},{1,25},{2,26},{3,27},{4,28},{5,29},{6,30},{7,31}} | collective-permute-start | bytes 442376 | tf_op jit(solution)/shard_map/ppermute | solution.py:431
  41.1 0.0 collective-permute-done.12.x_ref
  41.1 0.0 collective-permute-done.9.refs_1_
  41.1 0.0 collective-permute-done.10.refs_2_
  41.2 0.0 collective-permute-done.11.refs_3_
  41.2 1.0 %collective-permute-start.13 = (bf16[2,256,256]{2,1,0:T(8,128)(2,1)S(1)}, bf16[2,256,256]{2,1,0:T(8,128)(2,1)S(1)}, u32[]{:S(2)}, u32[]{:S(2)}) collective-permute-start(bf16[2,256,256]{2,1,0:T(8,128)(2,1)S(1)} %shard_map.124.refs_4_), channel_id=1, source_target_pairs={{0,7},{1,2},{2,1},{3,4},{4,3},{5,6},{6,5},{7,0},{8,15},{9,10},{10,... | collective-permute-start | bytes 786440 | tf_op jit(solution)/shard_map/ppermute | solution.py:77
  42.2 3.2 %collective-permute-start.17 = (bf16[288,256]{1,0:T(8,128)(2,1)S(1)}, bf16[288,256]{1,0:T(8,128)(2,1)S(1)}, u32[]{:S(2)}, u32[]{:S(2)}) collective-permute-start(bf16[288,256]{1,0:T(8,128)(2,1)S(1)} %get-tuple-element.49), channel_id=1, source_target_pairs={{0,16},{1,17},{2,18},{3,19},{4,20},{5,21},{6,22},{7,23}} | collective-permute-start | bytes 442376 | tf_op jit(solution)/shard_map/ppermute | solution.py:431
  45.4 1.5 %collective-permute-start.18 = (bf16[288,256]{1,0:T(8,128)(2,1)S(1)}, bf16[288,256]{1,0:T(8,128)(2,1)S(1)}, u32[]{:S(2)}, u32[]{:S(2)}) collective-permute-start(bf16[288,256]{1,0:T(8,128)(2,1)S(1)} %get-tuple-element.49), channel_id=1, source_target_pairs={{0,8},{1,9},{2,10},{3,11},{4,12},{5,13},{6,14},{7,15}} | collective-permute-start | bytes 442376 | tf_op jit(solution)/shard_map/ppermute | solution.py:431
  47.0 0.1 collective-permute-start.14
  47.0 0.0 collective-permute-done.16.refs_0_
  47.0 0.5 collective-permute-start.15
  47.5 0.5 %collective-permute-done.17.refs_1_ = bf16[288,256]{1,0:T(8,128)(2,1)S(1)} collective-permute-done((bf16[288,256]{1,0:T(8,128)(2,1)S(1)}, bf16[288,256]{1,0:T(8,128)(2,1)S(1)}, u32[]{:S(2)}, u32[]{:S(2)}) %collective-permute-start.17) | collective-permute-done | bytes 147488 | tf_op jit(solution)/shard_map/ppermute | solution.py:431
  48.0 1.5 %collective-permute-done.18.refs_2_ = bf16[288,256]{1,0:T(8,128)(2,1)S(1)} collective-permute-done((bf16[288,256]{1,0:T(8,128)(2,1)S(1)}, bf16[288,256]{1,0:T(8,128)(2,1)S(1)}, u32[]{:S(2)}, u32[]{:S(2)}) %collective-permute-start.18) | collective-permute-done | bytes 147488 | tf_op jit(solution)/shard_map/ppermute | solution.py:431
  49.6 0.0 collective-permute-done.14.ci_ref
  49.6 0.0 collective-permute-done.15.cei_ref
  49.6 0.0 collective-permute-done.13.co_ref
  49.6 1.0 %shard_map.127 = (bf16[2,256,256]{2,1,0:T(8,128)(2,1)}, bf16[2,512,256]{2,1,0:T(8,128)(2,1)}) custom-call(f32[8,128]{1,0:T(8,128)S(1)} %copy-done.3, bf16[4,512,256]{2,1,0:T(8,128)(2,1)S(1)} %copy-done, f32[256,256]{1,0:T(8,128)S(1)} %get-tuple-element.30.gain_ref, f32[256,256]{1,0:T(8,128)S(1)} %get-tuple-element.31.gain_extra_ref, ...), custom_call_target="tpu_custom_call" | custom-call | flops 1 | bytes 1 | tf_op jit(solution)/shard_map/pallas_call | solution.py:37
  (5 shorter events, 0.1 us)
Async XLA Ops:
  0.6 20.8 %collective-permute-start.4 = (bf16[2,1024,512]{2,1,0:T(8,128)(2,1)}, bf16[2,1024,512]{2,1,0:T(8,128)(2,1)S(1)}, u32[]{:S(2)}, u32[]{:S(2)}) collective-permute-start(bf16[2,1024,512]{2,1,0:T(8,128)(2,1)} %three_ref.1), channel_id=1, source_target_pairs={{0,1},{1,0},{2,3},{3,2},{4,5},{5,4},{6,7},{7,6},{8,9},{9,8},{10,11... | collective-permute-start | bytes 6291464 | tf_op jit(solution)/shard_map/ppermute | solution.py:74
  1.1 22.3 %collective-permute-start = (bf16[4,512,256]{2,1,0:T(8,128)(2,1)}, bf16[4,512,256]{2,1,0:T(8,128)(2,1)S(1)}, u32[]{:S(2)}, u32[]{:S(2)}) collective-permute-start(bf16[4,512,256]{2,1,0:T(8,128)(2,1)} %coeff_ref.11), channel_id=1, source_target_pairs={{0,1},{1,0},{2,3},{3,2},{4,5},{5,4},{6,7},{7,6},{8,9},{9,8},{10,11... | collective-permute-start | bytes 3145736 | tf_op jit(solution)/shard_map/ppermute | solution.py:74
  1.2 17.9 %collective-permute-start.1 = (bf16[4,256,256]{2,1,0:T(8,128)(2,1)}, bf16[4,256,256]{2,1,0:T(8,128)(2,1)S(1)}, u32[]{:S(2)}, u32[]{:S(2)}) collective-permute-start(bf16[4,256,256]{2,1,0:T(8,128)(2,1)} %amps_ref.5), channel_id=1, source_target_pairs={{0,1},{1,0},{2,3},{3,2},{4,5},{5,4},{6,7},{7,6},{8,9},{9,8},{10,11... | collective-permute-start | bytes 1572872 | tf_op jit(solution)/shard_map/ppermute | solution.py:74
  4.1 8.4 %collective-permute-start.2 = (bf16[528,128]{1,0:T(8,128)(2,1)}, bf16[528,128]{1,0:T(8,128)(2,1)S(1)}, u32[]{:S(2)}, u32[]{:S(2)}) collective-permute-start(bf16[528,128]{1,0:T(8,128)(2,1)} %get-tuple-element.27), channel_id=1, source_target_pairs={{0,7},{1,2},{2,1},{3,4},{4,3},{5,6},{6,5},{7,0},{8,15},{9,10},{10,... | collective-permute-start | bytes 405512 | tf_op jit(solution)/shard_map/ppermute | solution.py:77
  8.9 7.4 %collective-permute-start.3 = (bf16[512,128]{1,0:T(8,128)(2,1)}, bf16[512,128]{1,0:T(8,128)(2,1)S(1)}, u32[]{:S(2)}, u32[]{:S(2)}) collective-permute-start(bf16[512,128]{1,0:T(8,128)(2,1)} %get-tuple-element.28), channel_id=1, source_target_pairs={{0,7},{1,2},{2,1},{3,4},{4,3},{5,6},{6,5},{7,0},{8,15},{9,10},{10,... | collective-permute-start | bytes 393224 | tf_op jit(solution)/shard_map/ppermute | solution.py:77
  8.9 0.7 %copy-start.2 = (f32[8,128]{1,0:T(8,128)S(1)}, f32[8,128]{1,0:T(8,128)}, u32[]{:S(2)}) copy-start(f32[8,128]{1,0:T(8,128)} %get-tuple-element.26.after_ref.nums) | copy-start | bytes 12292
  11.2 7.0 %copy-start = (bf16[4,512,256]{2,1,0:T(8,128)(2,1)S(1)}, bf16[4,512,256]{2,1,0:T(8,128)(2,1)}, u32[]{:S(2)}) copy-start(bf16[4,512,256]{2,1,0:T(8,128)(2,1)} %coeff_ref.11) | copy-start | bytes 3145732
  11.2 7.0 %copy-start.1 = (bf16[4,256,256]{2,1,0:T(8,128)(2,1)S(1)}, bf16[4,256,256]{2,1,0:T(8,128)(2,1)}, u32[]{:S(2)}) copy-start(bf16[4,256,256]{2,1,0:T(8,128)(2,1)} %amps_ref.5) | copy-start | bytes 1572868
  13.0 8.4 %copy-start.6 = (bf16[528,128]{1,0:T(8,128)(2,1)S(1)}, bf16[528,128]{1,0:T(8,128)(2,1)}, u32[]{:S(2)}) copy-start(bf16[528,128]{1,0:T(8,128)(2,1)} %get-tuple-element.27) | copy-start | bytes 405508
  13.1 9.7 %copy-start.3 = (f32[8,128]{1,0:T(8,128)S(1)}, f32[8,128]{1,0:T(8,128)}, u32[]{:S(2)}) copy-start(f32[8,128]{1,0:T(8,128)} %get-tuple-element.26.after_ref.nums) | copy-start | bytes 12292
  13.1 19.1 %collective-permute-start.5 = (bf16[1040,128]{1,0:T(8,128)(2,1)S(1)}, bf16[1040,128]{1,0:T(8,128)(2,1)S(1)}, u32[]{:S(2)}, u32[]{:S(2)}) collective-permute-start(bf16[1040,128]{1,0:T(8,128)(2,1)S(1)} %shard_map.115.after_ref), channel_id=1, source_target_pairs={{0,7},{1,2},{2,1},{3,4},{4,3},{5,6},{6,5},{7,0},{8,15},{9,10},{10,... | collective-permute-start | bytes 798728 | tf_op jit(solution)/shard_map/ppermute | solution.py:77
  16.8 15.4 %collective-permute-start.6 = (bf16[1024,128]{1,0:T(8,128)(2,1)S(1)}, bf16[1024,128]{1,0:T(8,128)(2,1)S(1)}, u32[]{:S(2)}, u32[]{:S(2)}) collective-permute-start(bf16[1024,128]{1,0:T(8,128)(2,1)S(1)} %shard_map.116.after_ref), channel_id=1, source_target_pairs={{0,7},{1,2},{2,1},{3,4},{4,3},{5,6},{6,5},{7,0},{8,15},{9,10},{10,... | collective-permute-start | bytes 786440 | tf_op jit(solution)/shard_map/ppermute | solution.py:77
  19.1 5.7 %copy-start.4 = (f32[4,256]{1,0:T(4,128)S(1)}, f32[4,256]{1,0:T(4,128)}, u32[]{:S(2)}) copy-start(f32[4,256]{1,0:T(4,128)} %eps_ref.1) | copy-start | bytes 12292
  19.1 13.0 %collective-permute-start.7 = (bf16[272,256]{1,0:T(8,128)(2,1)S(1)}, bf16[272,256]{1,0:T(8,128)(2,1)S(1)}, u32[]{:S(2)}, u32[]{:S(2)}) collective-permute-start(bf16[272,256]{1,0:T(8,128)(2,1)S(1)} %get-tuple-element.29.after_ref), channel_id=1, source_target_pairs={{0,7},{1,2},{2,1},{3,4},{4,3},{5,6},{6,5},{7,0},{8,15},{9,10},{10,... | collective-permute-start | bytes 417800 | tf_op jit(solution)/shard_map/ppermute | solution.py:77
  21.4 1.4 %copy-start.5 = (bf16[2,1024,512]{2,1,0:T(8,128)(2,1)}, bf16[2,1024,512]{2,1,0:T(8,128)(2,1)S(1)}, u32[]{:S(2)}) copy-start(bf16[2,1024,512]{2,1,0:T(8,128)(2,1)S(1)} %collective-permute-done.4.three_in_ref) | copy-start | bytes 6291460
  21.4 4.9 %collective-permute-start.8 = (bf16[528,128]{1,0:T(8,128)(2,1)S(1)}, bf16[528,128]{1,0:T(8,128)(2,1)S(1)}, u32[]{:S(2)}, u32[]{:S(2)}) collective-permute-start(bf16[528,128]{1,0:T(8,128)(2,1)S(1)} %copy-done.6), channel_id=1, source_target_pairs={{0,1},{1,0},{2,3},{3,2},{4,5},{5,4},{6,7},{7,6},{8,9},{9,8},{10,11... | collective-permute-start | bytes 405512 | tf_op jit(solution)/shard_map/ppermute | solution.py:74
  23.4 17.7 %collective-permute-start.12 = (bf16[512,256]{1,0:T(8,128)(2,1)S(1)}, bf16[512,256]{1,0:T(8,128)(2,1)S(1)}, u32[]{:S(2)}, u32[]{:S(2)}) collective-permute-start(bf16[512,256]{1,0:T(8,128)(2,1)S(1)} %get-tuple-element.44), channel_id=1, source_target_pairs={{0,7},{1,2},{2,1},{3,4},{4,3},{5,6},{6,5},{7,0},{8,15},{9,10},{10,... | collective-permute-start | bytes 786440 | tf_op jit(solution)/shard_map/ppermute | solution.py:77
  32.9 8.3 %collective-permute-start.11 = (bf16[272,256]{1,0:T(8,128)(2,1)S(1)}, bf16[272,256]{1,0:T(8,128)(2,1)S(1)}, u32[]{:S(2)}, u32[]{:S(2)}) collective-permute-start(bf16[272,256]{1,0:T(8,128)(2,1)S(1)} %get-tuple-element.40), channel_id=1, source_target_pairs={{0,24},{8,16},{16,8},{24,0},{1,25},{9,17},{17,9},{25,1},{2,26},{10... | collective-permute-start | bytes 417800 | tf_op jit(solution)/shard_map/ppermute | solution.py:80
  35.3 5.9 %collective-permute-start.9 = (bf16[256,256]{1,0:T(8,128)(2,1)S(1)}, bf16[256,256]{1,0:T(8,128)(2,1)S(1)}, u32[]{:S(2)}, u32[]{:S(2)}) collective-permute-start(bf16[256,256]{1,0:T(8,128)(2,1)S(1)} %get-tuple-element.36.amp_ref.after_ref.refs_0_), channel_id=1, source_target_pairs={{0,8},{8,0},{16,24},{24,16},{1,9},{9,1},{17,25},{25,17},{2,10},{10... | collective-permute-start | bytes 393224 | tf_op jit(solution)/shard_map/ppermute | solution.py:80
  35.8 5.3 %collective-permute-start.10 = (bf16[256,256]{1,0:T(8,128)(2,1)S(1)}, bf16[256,256]{1,0:T(8,128)(2,1)S(1)}, u32[]{:S(2)}, u32[]{:S(2)}) collective-permute-start(bf16[256,256]{1,0:T(8,128)(2,1)S(1)} %get-tuple-element.36.amp_ref.after_ref.refs_0_), channel_id=1, source_target_pairs={{0,16},{8,24},{16,0},{24,8},{1,17},{9,25},{17,1},{25,9},{2,18},{10... | collective-permute-start | bytes 393224 | tf_op jit(solution)/shard_map/ppermute | solution.py:80
  36.8 10.2 %collective-permute-start.16 = (bf16[288,256]{1,0:T(8,128)(2,1)S(1)}, bf16[288,256]{1,0:T(8,128)(2,1)S(1)}, u32[]{:S(2)}, u32[]{:S(2)}) collective-permute-start(bf16[288,256]{1,0:T(8,128)(2,1)S(1)} %get-tuple-element.49), channel_id=1, source_target_pairs={{0,24},{1,25},{2,26},{3,27},{4,28},{5,29},{6,30},{7,31}} | collective-permute-start | bytes 442376 | tf_op jit(solution)/shard_map/ppermute | solution.py:431
  41.2 8.4 %collective-permute-start.13 = (bf16[2,256,256]{2,1,0:T(8,128)(2,1)S(1)}, bf16[2,256,256]{2,1,0:T(8,128)(2,1)S(1)}, u32[]{:S(2)}, u32[]{:S(2)}) collective-permute-start(bf16[2,256,256]{2,1,0:T(8,128)(2,1)S(1)} %shard_map.124.refs_4_), channel_id=1, source_target_pairs={{0,7},{1,2},{2,1},{3,4},{4,3},{5,6},{6,5},{7,0},{8,15},{9,10},{10,... | collective-permute-start | bytes 786440 | tf_op jit(solution)/shard_map/ppermute | solution.py:77
  42.2 5.9 %collective-permute-start.17 = (bf16[288,256]{1,0:T(8,128)(2,1)S(1)}, bf16[288,256]{1,0:T(8,128)(2,1)S(1)}, u32[]{:S(2)}, u32[]{:S(2)}) collective-permute-start(bf16[288,256]{1,0:T(8,128)(2,1)S(1)} %get-tuple-element.49), channel_id=1, source_target_pairs={{0,16},{1,17},{2,18},{3,19},{4,20},{5,21},{6,22},{7,23}} | collective-permute-start | bytes 442376 | tf_op jit(solution)/shard_map/ppermute | solution.py:431
  45.4 4.2 %collective-permute-start.18 = (bf16[288,256]{1,0:T(8,128)(2,1)S(1)}, bf16[288,256]{1,0:T(8,128)(2,1)S(1)}, u32[]{:S(2)}, u32[]{:S(2)}) collective-permute-start(bf16[288,256]{1,0:T(8,128)(2,1)S(1)} %get-tuple-element.49), channel_id=1, source_target_pairs={{0,8},{1,9},{2,10},{3,11},{4,12},{5,13},{6,14},{7,15}} | collective-permute-start | bytes 442376 | tf_op jit(solution)/shard_map/ppermute | solution.py:431
  47.0 2.6 %collective-permute-start.14 = (bf16[272,256]{1,0:T(8,128)(2,1)S(1)}, bf16[272,256]{1,0:T(8,128)(2,1)S(1)}, u32[]{:S(2)}, u32[]{:S(2)}) collective-permute-start(bf16[272,256]{1,0:T(8,128)(2,1)S(1)} %get-tuple-element.45.refs_4_), channel_id=1, source_target_pairs={{0,1},{1,0},{2,3},{3,2},{4,5},{5,4},{6,7},{7,6},{8,9},{9,8},{10,11... | collective-permute-start | bytes 417800 | tf_op jit(solution)/shard_map/ppermute | solution.py:74
  47.0 2.5 %collective-permute-start.15 = (bf16[272,256]{1,0:T(8,128)(2,1)S(1)}, bf16[272,256]{1,0:T(8,128)(2,1)S(1)}, u32[]{:S(2)}, u32[]{:S(2)}) collective-permute-start(bf16[272,256]{1,0:T(8,128)(2,1)S(1)} %get-tuple-element.48), channel_id=1, source_target_pairs={{0,1},{1,0},{2,3},{3,2},{4,5},{5,4},{6,7},{7,6},{8,9},{9,8},{10,11... | collective-permute-start | bytes 417800 | tf_op jit(solution)/shard_map/ppermute | solution.py:74

commit v15 on v14

--- a/solution.py
+++ b/solution.py
@@ -383,7 +383,7 @@
 
     def first_body(
         nums, first_ref, second_ref, low_ref, high_ref, amps_ref, c_ref, co_ref, gain_ref, after_ref,
-        amp_ref, amp_long_ref, k_ref,
+        amp_ref, k_ref,
     ):
         first = first_ref[...]
         num, _ = read(nums)
@@ -400,21 +400,18 @@
 
         old = amps_ref[whole(num(MINE))].astype(F32)
         c = c_ref[...] + co_ref[:virt, :].astype(F32)
-        amp = (gain_ref[...] * (old - k_ref[...] - c)).astype(BF16)
-        amp_ref[...] = amp
-        amp_long_ref[:virt, :] = amp
-        amp_long_ref[virt:, :] = jnp.zeros((riders, virt), BF16)
-
-    amp, amp_long, k_first = call(
+        amp_ref[...] = (gain_ref[...] * (old - k_ref[...] - c)).astype(BF16)
+
+    amp, k_first = call(
         first_body,
         [VMEM] + [VMEM] * 8 + [ANY],
-        [sq_b, longer, sq_f],
+        [sq_b, sq_f],
         (
             nums, first_t, second, y_low_from_out, y_high_from_out,
             amps, c_own, c_from_out, gain, se_own,
         ),
     )
-    amp_roles = [amp] + [swap(amp, m) for m in range(1, roles - 1)] + [swap(amp_long, roles - 1)]
+    amp_roles = [amp] + [swap(amp, m) for m in range(1, roles)]
 
     def rest_body(amp_ref, k_ref, out_ref, out_b_ref):
         amp = amp_ref[...]
@@ -428,7 +425,8 @@
 
     longest = (VMEM, (virt + 2 * riders, virt), BF16)
     rest, rest_b = call(rest_body, [VMEM, VMEM], [sq_f, longest], (amp, k_first))
-    rests = [lax.ppermute(rest_b, "role", [(0, s)]) for s in range(roles - 1, 0, -1)]
+    sends = [1, *range(roles - 1, 1, -1)]
+    rests = [lax.ppermute(rest_b, "role", [(0, s)]) for s in sends]
 
     def extra_out_body(coeff_ref, x_ref, after_ref, s_ref):
         @pl.when(lax.axis_index("role") > 0)
@@ -447,7 +445,7 @@
         parts = []
         for m in range(roles):
             at = whole(num(ROLE_PAIR + m))
-            parts.append((at, weight_of(at), amp_refs[m][:virt, :]))
+            parts.append((at, weight_of(at), amp_refs[m][...]))
         return parts
 
     def told_weight(told, first):
@@ -526,7 +524,7 @@
                 total = rest[...] - co_ref[slot].astype(F32) - c_in[:virt, :].astype(F32)
                 for s in range(1, roles):
                     if slot:
-                        come = rest_refs[roles - 1 - s][:virt, :].astype(F32)
+                        come = rest_refs[sends.index(s)][:virt, :].astype(F32)
                         total += jnp.where(role == s, come, 0.0)
                 amp_ref[slot] = (gain[...] * total).astype(BF16)
 

time: 51.1 us -> 51.4 us (level)
    ppermute x3, waiting for transfers between devices: 0.01 us -> 1.41 us  [swap(): return lax.ppermute(x, 'role', [(i, i ^ by) for i in range(roles)])]
    ppermute x7, waiting for transfers between devices: 7.17 us -> 5.98 us  [outer(): return lax.ppermute(x, 'pairs', list(enumerate(outer_of)))]
    ppermute x7, starting transfers between devices: 14.2 us -> 14.7 us  [outer(): return lax.ppermute(x, 'pairs', list(enumerate(outer_of)))]
  transfers between devices with their start and end apart: 19 -> 19, of which waited for: 4 -> 5; matrix products, arithmetic and copies ran while one was open for 0% -> 0% of each run, Pallas kernels for 18% -> 18%
where the time goes in v15:
time: 51.4 us; the launch traced here: 51.1 us
  starting transfers between devices  28.7 us (56%)
  Pallas kernels  10.1 us (20%)
  waiting for transfers between devices  9.45 us (18%)
  local copies, waits for them, and re-layouts  1.98 us (4%)
  between operations  0.87 us (2%)
    ppermute x7, starting transfers between devices, outer(): return lax.ppermute(x, 'pairs', list(enumerate(outer_of)))  14.7 us
    pallas_call x15, Pallas kernels, call(): pl.pallas_call(body, in_specs=ins, out_specs=[spec for spec, _, _ in outs...  10.1 us
    ppermute x3, starting transfers between devices, local(): rests = [lax.ppermute(rest_b, 'role', [(0, s)]) for s in sends]  8.84 us
    ppermute x7, waiting for transfers between devices, outer(): return lax.ppermute(x, 'pairs', list(enumerate(outer_of)))  5.98 us
    ppermute x3, starting transfers between devices, swap(): return lax.ppermute(x, 'role', [(i, i ^ by) for i in range(roles)])  3.55 us
    ppermute x3, waiting for transfers between devices, local(): rests = [lax.ppermute(rest_b, 'role', [(0, s)]) for s in sends]  2.04 us
    unnamed x14, local copies, waits for them, and re-layouts  1.98 us
    ppermute x6, starting transfers between devices, inner(): return lax.ppermute(x, 'pairs', list(enumerate(inner_of)))  1.66 us
  transfers between devices with their start and end apart: 19, of which 5 were waited for; matrix products, arithmetic and copies ran while one was open for 0% of the time, Pallas kernels for 18%

profile of v15, /device:TPU:0, one launch (start us, length us, event | category | flops | bytes accessed | tf_op | source)
XLA Modules:
  0.0 51.1 jit_solution(6316430718557014681)
XLA Ops:
  0.6 0.5 %collective-permute-start.4 = (bf16[2,1024,512]{2,1,0:T(8,128)(2,1)}, bf16[2,1024,512]{2,1,0:T(8,128)(2,1)S(1)}, u32[]{:S(2)}, u32[]{:S(2)}) collective-permute-start(bf16[2,1024,512]{2,1,0:T(8,128)(2,1)} %three_ref.1), channel_id=1, source_target_pairs={{0,1},{1,0},{2,3},{3,2},{4,5},{5,4},{6,7},{7,6},{8,9},{9,8},{10,11... | collective-permute-start | bytes 6291464 | tf_op jit(solution)/shard_map/ppermute | solution.py:74
  1.1 0.1 collective-permute-start
  1.2 0.4 collective-permute-start.1
  1.7 2.4 %shard_map.113 = (bf16[528,128]{1,0:T(8,128)(2,1)}, bf16[512,128]{1,0:T(8,128)(2,1)}, f32[8,128]{1,0:T(8,128)}) custom-call(s32[4]{0:T(128)} %owner_hbm.1, s32[2,4]{1,0:T(2,128)} %bitcast.1, s32[4,8]{1,0:T(4,128)} %partner_hbm.1, f32[4,8]{1,0:T(4,128)} %coupling_hbm.1, f32[16]{0:T(128)} %eps_hbm.1, s32[4]{0:T(128)} %nvirt_hbm.1, bf16[4,512,256]{2,1,0:T(8,128)(2,1)} %coeff_ref.11), custom_call_target="tpu_custom_call" | custom-call | flops 1 | bytes 1 | tf_op jit(solution)/shard_map/pallas_call | solution.py:37
  4.1 4.8 %collective-permute-start.2 = (bf16[528,128]{1,0:T(8,128)(2,1)}, bf16[528,128]{1,0:T(8,128)(2,1)S(1)}, u32[]{:S(2)}, u32[]{:S(2)}) collective-permute-start(bf16[528,128]{1,0:T(8,128)(2,1)} %get-tuple-element.26), channel_id=1, source_target_pairs={{0,7},{1,2},{2,1},{3,4},{4,3},{5,6},{6,5},{7,0},{8,15},{9,10},{10,... | collective-permute-start | bytes 405512 | tf_op jit(solution)/shard_map/ppermute | solution.py:77
  8.9 0.1 collective-permute-start.3
  8.9 0.0 copy-start.2
  8.9 0.7 %copy-done.2 = f32[8,128]{1,0:T(8,128)S(1)} copy-done((f32[8,128]{1,0:T(8,128)S(1)}, f32[8,128]{1,0:T(8,128)}, u32[]{:S(2)}) %copy-start.2) | copy-done | bytes 4120
  9.6 1.6 %shard_map.114.three_ref = bf16[2,1024,512]{2,1,0:T(8,128)(2,1)S(1)} custom-call(bf16[2,1024,512]{2,1,0:T(8,128)(2,1)} %three_ref.1, f32[8,128]{1,0:T(8,128)S(1)} %copy-done.2), custom_call_target="tpu_custom_call" | custom-call | flops 1 | bytes 1 | tf_op jit(solution)/shard_map/pallas_call | solution.py:37
  11.2 0.0 copy-start
  11.2 0.0 copy-start.1
  11.2 1.3 %collective-permute-done.2.x_ref.low_ref = bf16[528,128]{1,0:T(8,128)(2,1)S(1)} collective-permute-done((bf16[528,128]{1,0:T(8,128)(2,1)}, bf16[528,128]{1,0:T(8,128)(2,1)S(1)}, u32[]{:S(2)}, u32[]{:S(2)}) %collective-permute-start.2) | collective-permute-done | bytes 135200 | tf_op jit(solution)/shard_map/ppermute | solution.py:77
  12.5 0.5 %shard_map.115.after_ref = bf16[1040,128]{1,0:T(8,128)(2,1)S(1)} custom-call(bf16[2,1024,512]{2,1,0:T(8,128)(2,1)S(1)} %shard_map.114.three_ref, bf16[528,128]{1,0:T(8,128)(2,1)S(1)} %collective-permute-done.2.x_ref.low_ref), custom_call_target="tpu_custom_call" | custom-call | flops 1 | bytes 1 | tf_op jit(solution)/shard_map/pallas_call | solution.py:37
  13.0 0.0 copy-start.6
  13.1 0.0 copy-start.3
  13.1 3.2 %collective-permute-start.5 = (bf16[1040,128]{1,0:T(8,128)(2,1)S(1)}, bf16[1040,128]{1,0:T(8,128)(2,1)S(1)}, u32[]{:S(2)}, u32[]{:S(2)}) collective-permute-start(bf16[1040,128]{1,0:T(8,128)(2,1)S(1)} %shard_map.115.after_ref), channel_id=1, source_target_pairs={{0,7},{1,2},{2,1},{3,4},{4,3},{5,6},{6,5},{7,0},{8,15},{9,10},{10,... | collective-permute-start | bytes 798728 | tf_op jit(solution)/shard_map/ppermute | solution.py:77
  16.3 0.0 collective-permute-done.3.x_ref.high_ref
  16.3 0.5 %shard_map.116.after_ref = bf16[1024,128]{1,0:T(8,128)(2,1)S(1)} custom-call(bf16[2,1024,512]{2,1,0:T(8,128)(2,1)S(1)} %shard_map.114.three_ref, bf16[528,128]{1,0:T(8,128)(2,1)S(1)} %collective-permute-done.2.x_ref.low_ref, bf16[512,128]{1,0:T(8,128)(2,1)S(1)} %collective-permute-done.3.x_ref.high_ref, bf16[1040,128]{1,0:T(8,128)(2,1)S(1)} %shard_map.115.after_ref), custom_call_target="tpu_custom_call" | custom-call | flops 1 | bytes 1 | tf_op jit(solution)/shard_map/pallas_call | solution.py:37
  16.8 1.4 %collective-permute-start.6 = (bf16[1024,128]{1,0:T(8,128)(2,1)S(1)}, bf16[1024,128]{1,0:T(8,128)(2,1)S(1)}, u32[]{:S(2)}, u32[]{:S(2)}) collective-permute-start(bf16[1024,128]{1,0:T(8,128)(2,1)S(1)} %shard_map.116.after_ref), channel_id=1, source_target_pairs={{0,7},{1,2},{2,1},{3,4},{4,3},{5,6},{6,5},{7,0},{8,15},{9,10},{10,... | collective-permute-start | bytes 786440 | tf_op jit(solution)/shard_map/ppermute | solution.py:77
  18.2 0.0 copy-done
  18.2 0.0 copy-done.1
  18.2 0.9 %shard_map.117 = (bf16[4,256,256]{2,1,0:T(8,128)(2,1)S(1)}, bf16[272,256]{1,0:T(8,128)(2,1)S(1)}) custom-call(bf16[4,512,256]{2,1,0:T(8,128)(2,1)S(1)} %copy-done, bf16[4,256,256]{2,1,0:T(8,128)(2,1)S(1)} %copy-done.1, bf16[528,128]{1,0:T(8,128)(2,1)S(1)} %collective-permute-done.2.x_ref.low_ref, bf16[512,128]{1,0:T(8,128)(2,1)S(1)} %collective-permute-done.3.x_ref.high_ref, ...), custom_call_target="tpu_custom_call" | custom-call | flops 1 | bytes 1 | tf_op jit(solution)/shard_map/pallas_call | solution.py:37
  19.1 0.0 collective-permute-done.1.amps_in_ref
  19.1 0.0 copy-start.4
  19.1 2.3 %collective-permute-start.7 = (bf16[272,256]{1,0:T(8,128)(2,1)S(1)}, bf16[272,256]{1,0:T(8,128)(2,1)S(1)}, u32[]{:S(2)}, u32[]{:S(2)}) collective-permute-start(bf16[272,256]{1,0:T(8,128)(2,1)S(1)} %get-tuple-element.28.after_ref), channel_id=1, source_target_pairs={{0,7},{1,2},{2,1},{3,4},{4,3},{5,6},{6,5},{7,0},{8,15},{9,10},{10,... | collective-permute-start | bytes 417800 | tf_op jit(solution)/shard_map/ppermute | solution.py:77
  21.4 0.0 collective-permute-done.4.three_in_ref
  21.4 0.0 copy-done.6
  21.4 0.0 copy-start.5
  21.4 0.1 collective-permute-start.8
  21.5 1.3 %copy-done.5 = bf16[2,1024,512]{2,1,0:T(8,128)(2,1)} copy-done((bf16[2,1024,512]{2,1,0:T(8,128)(2,1)}, bf16[2,1024,512]{2,1,0:T(8,128)(2,1)S(1)}, u32[]{:S(2)}) %copy-start.5) | copy-done | bytes 2097176
  22.8 0.0 copy-done.3
  22.8 0.6 %shard_map.119 = (bf16[256,1024]{1,0:T(8,128)(2,1)S(1)}, bf16[1024,256]{1,0:T(8,128)(2,1)S(1)}, bf16[512,256]{1,0:T(8,128)(2,1)S(1)}) custom-call(f32[8,128]{1,0:T(8,128)S(1)} %copy-done.3, bf16[2,1024,512]{2,1,0:T(8,128)(2,1)S(1)} %shard_map.114.three_ref, bf16[2,1024,512]{2,1,0:T(8,128)(2,1)} %copy-done.5, bf16[4,512,256]{2,1,0:T(8,128)(2,1)S(1)} %copy-done, ...), custom_call_target="tpu_custom_call" | custom-call | flops 1 | bytes 1 | tf_op jit(solution)/shard_map/pallas_call | solution.py:37
  23.4 0.0 collective-permute-done.coeff_in_ref.in_ref
  23.4 2.6 %collective-permute-start.12 = (bf16[512,256]{1,0:T(8,128)(2,1)S(1)}, bf16[512,256]{1,0:T(8,128)(2,1)S(1)}, u32[]{:S(2)}, u32[]{:S(2)}) collective-permute-start(bf16[512,256]{1,0:T(8,128)(2,1)S(1)} %get-tuple-element.42), channel_id=1, source_target_pairs={{0,7},{1,2},{2,1},{3,4},{4,3},{5,6},{6,5},{7,0},{8,15},{9,10},{10,... | collective-permute-start | bytes 786440 | tf_op jit(solution)/shard_map/ppermute | solution.py:77
  26.0 0.0 copy-done.4
  26.0 1.5 %shard_map.118 = (bf16[4,256,256]{2,1,0:T(8,128)(2,1)S(1)}, f32[256,256]{1,0:T(8,128)S(1)}, f32[256,256]{1,0:T(8,128)S(1)}, f32[256,256]{1,0:T(8,128)S(1)}) custom-call(f32[8,128]{1,0:T(8,128)S(1)} %copy-done.3, bf16[4,512,256]{2,1,0:T(8,128)(2,1)S(1)} %copy-done, bf16[4,512,256]{2,1,0:T(8,128)(2,1)S(1)} %collective-permute-done.coeff_in_ref.in_ref, ...), custom_call_target="tpu_custom_call" | custom-call | flops 1 | bytes 1 | tf_op jit(solution)/shard_map/pallas_call | solution.py:37
  27.5 0.0 collective-permute-done.8.low_ref
  27.5 4.7 %collective-permute-done.7.co_ref = bf16[272,256]{1,0:T(8,128)(2,1)S(1)} collective-permute-done((bf16[272,256]{1,0:T(8,128)(2,1)S(1)}, bf16[272,256]{1,0:T(8,128)(2,1)S(1)}, u32[]{:S(2)}, u32[]{:S(2)}) %collective-permute-start.7) | collective-permute-done | bytes 139296 | tf_op jit(solution)/shard_map/ppermute | solution.py:77
  32.2 0.0 collective-permute-done.6.high_ref
  32.2 0.0 collective-permute-done.5.low_ref
  32.2 0.7 %shard_map.121 = (bf16[256,256]{1,0:T(8,128)(2,1)S(1)}, f32[256,256]{1,0:T(8,128)S(1)}) custom-call(f32[8,128]{1,0:T(8,128)S(1)} %copy-done.3, bf16[256,1024]{1,0:T(8,128)(2,1)S(1)} %get-tuple-element.31.first_ref, bf16[1024,256]{1,0:T(8,128)(2,1)S(1)} %get-tuple-element.32.second_ref, bf16[1040,128]{1,0:T(8,128)(2,1)S(1)} %collective-permute-done.5.low_ref, ...), custom_call_target="tpu_custom_call" | custom-call | flops 1 | bytes 1 | tf_op jit(solution)/shard_map/pallas_call | solution.py:37
  32.9 1.6 %collective-permute-start.9 = (bf16[256,256]{1,0:T(8,128)(2,1)S(1)}, bf16[256,256]{1,0:T(8,128)(2,1)S(1)}, u32[]{:S(2)}, u32[]{:S(2)}) collective-permute-start(bf16[256,256]{1,0:T(8,128)(2,1)S(1)} %get-tuple-element.35.amp_ref.after_ref.refs_0_), channel_id=1, source_target_pairs={{0,8},{8,0},{16,24},{24,16},{1,9},{9,1},{17,25},{25,17},{2,10},{10... | collective-permute-start | bytes 393224 | tf_op jit(solution)/shard_map/ppermute | solution.py:80
  34.4 1.4 %collective-permute-start.10 = (bf16[256,256]{1,0:T(8,128)(2,1)S(1)}, bf16[256,256]{1,0:T(8,128)(2,1)S(1)}, u32[]{:S(2)}, u32[]{:S(2)}) collective-permute-start(bf16[256,256]{1,0:T(8,128)(2,1)S(1)} %get-tuple-element.35.amp_ref.after_ref.refs_0_), channel_id=1, source_target_pairs={{0,16},{8,24},{16,0},{24,8},{1,17},{9,25},{17,1},{25,9},{2,18},{10... | collective-permute-start | bytes 393224 | tf_op jit(solution)/shard_map/ppermute | solution.py:80
  35.8 0.6 %collective-permute-start.11 = (bf16[256,256]{1,0:T(8,128)(2,1)S(1)}, bf16[256,256]{1,0:T(8,128)(2,1)S(1)}, u32[]{:S(2)}, u32[]{:S(2)}) collective-permute-start(bf16[256,256]{1,0:T(8,128)(2,1)S(1)} %get-tuple-element.35.amp_ref.after_ref.refs_0_), channel_id=1, source_target_pairs={{0,24},{8,16},{16,8},{24,0},{1,25},{9,17},{17,9},{25,1},{2,26},{10... | collective-permute-start | bytes 393224 | tf_op jit(solution)/shard_map/ppermute | solution.py:80
  36.4 0.4 shard_map.122
  36.8 3.4 %collective-permute-start.16 = (bf16[288,256]{1,0:T(8,128)(2,1)S(1)}, bf16[288,256]{1,0:T(8,128)(2,1)S(1)}, u32[]{:S(2)}, u32[]{:S(2)}) collective-permute-start(bf16[288,256]{1,0:T(8,128)(2,1)S(1)} %get-tuple-element.47), channel_id=1, source_target_pairs={{0,8},{1,9},{2,10},{3,11},{4,12},{5,13},{6,14},{7,15}} | collective-permute-start | bytes 442376 | tf_op jit(solution)/shard_map/ppermute | solution.py:429
  40.2 0.0 collective-permute-done.12.x_ref
  40.3 0.0 collective-permute-done.9.refs_1_
  40.3 0.0 collective-permute-done.10.refs_2_
  40.3 1.4 %collective-permute-done.11.refs_3_ = bf16[256,256]{1,0:T(8,128)(2,1)S(1)} collective-permute-done((bf16[256,256]{1,0:T(8,128)(2,1)S(1)}, bf16[256,256]{1,0:T(8,128)(2,1)S(1)}, u32[]{:S(2)}, u32[]{:S(2)}) %collective-permute-start.11) | collective-permute-done | bytes 131104 | tf_op jit(solution)/shard_map/ppermute | solution.py:80
  41.7 0.3 collective-permute-start.13
  42.1 4.1 %collective-permute-start.17 = (bf16[288,256]{1,0:T(8,128)(2,1)S(1)}, bf16[288,256]{1,0:T(8,128)(2,1)S(1)}, u32[]{:S(2)}, u32[]{:S(2)}) collective-permute-start(bf16[288,256]{1,0:T(8,128)(2,1)S(1)} %get-tuple-element.47), channel_id=1, source_target_pairs={{0,24},{1,25},{2,26},{3,27},{4,28},{5,29},{6,30},{7,31}} | collective-permute-start | bytes 442376 | tf_op jit(solution)/shard_map/ppermute | solution.py:429
  46.2 1.3 %collective-permute-start.18 = (bf16[288,256]{1,0:T(8,128)(2,1)S(1)}, bf16[288,256]{1,0:T(8,128)(2,1)S(1)}, u32[]{:S(2)}, u32[]{:S(2)}) collective-permute-start(bf16[288,256]{1,0:T(8,128)(2,1)S(1)} %get-tuple-element.47), channel_id=1, source_target_pairs={{0,16},{1,17},{2,18},{3,19},{4,20},{5,21},{6,22},{7,23}} | collective-permute-start | bytes 442376 | tf_op jit(solution)/shard_map/ppermute | solution.py:429
  47.5 0.1 collective-permute-start.14
  47.6 0.0 collective-permute-done.16.refs_0_
  47.6 0.5 collective-permute-start.15
  48.1 0.7 %collective-permute-done.17.refs_1_ = bf16[288,256]{1,0:T(8,128)(2,1)S(1)} collective-permute-done((bf16[288,256]{1,0:T(8,128)(2,1)S(1)}, bf16[288,256]{1,0:T(8,128)(2,1)S(1)}, u32[]{:S(2)}, u32[]{:S(2)}) %collective-permute-start.17) | collective-permute-done | bytes 147488 | tf_op jit(solution)/shard_map/ppermute | solution.py:429
  48.8 1.3 %collective-permute-done.18.refs_2_ = bf16[288,256]{1,0:T(8,128)(2,1)S(1)} collective-permute-done((bf16[288,256]{1,0:T(8,128)(2,1)S(1)}, bf16[288,256]{1,0:T(8,128)(2,1)S(1)}, u32[]{:S(2)}, u32[]{:S(2)}) %collective-permute-start.18) | collective-permute-done | bytes 147488 | tf_op jit(solution)/shard_map/ppermute | solution.py:429
  50.1 0.0 collective-permute-done.14.ci_ref
  50.1 0.0 collective-permute-done.15.cei_ref
  50.2 0.0 collective-permute-done.13.co_ref
  50.2 1.0 %shard_map.127 = (bf16[2,256,256]{2,1,0:T(8,128)(2,1)}, bf16[2,512,256]{2,1,0:T(8,128)(2,1)}) custom-call(f32[8,128]{1,0:T(8,128)S(1)} %copy-done.3, bf16[4,512,256]{2,1,0:T(8,128)(2,1)S(1)} %copy-done, f32[256,256]{1,0:T(8,128)S(1)} %get-tuple-element.29.gain_ref, f32[256,256]{1,0:T(8,128)S(1)} %get-tuple-element.30.gain_extra_ref, ...), custom_call_target="tpu_custom_call" | custom-call | flops 1 | bytes 1 | tf_op jit(solution)/shard_map/pallas_call | solution.py:37
  (5 shorter events, 0.1 us)
Async XLA Ops:
  0.6 20.8 %collective-permute-start.4 = (bf16[2,1024,512]{2,1,0:T(8,128)(2,1)}, bf16[2,1024,512]{2,1,0:T(8,128)(2,1)S(1)}, u32[]{:S(2)}, u32[]{:S(2)}) collective-permute-start(bf16[2,1024,512]{2,1,0:T(8,128)(2,1)} %three_ref.1), channel_id=1, source_target_pairs={{0,1},{1,0},{2,3},{3,2},{4,5},{5,4},{6,7},{7,6},{8,9},{9,8},{10,11... | collective-permute-start | bytes 6291464 | tf_op jit(solution)/shard_map/ppermute | solution.py:74
  1.1 22.3 %collective-permute-start = (bf16[4,512,256]{2,1,0:T(8,128)(2,1)}, bf16[4,512,256]{2,1,0:T(8,128)(2,1)S(1)}, u32[]{:S(2)}, u32[]{:S(2)}) collective-permute-start(bf16[4,512,256]{2,1,0:T(8,128)(2,1)} %coeff_ref.11), channel_id=1, source_target_pairs={{0,1},{1,0},{2,3},{3,2},{4,5},{5,4},{6,7},{7,6},{8,9},{9,8},{10,11... | collective-permute-start | bytes 3145736 | tf_op jit(solution)/shard_map/ppermute | solution.py:74
  1.2 17.9 %collective-permute-start.1 = (bf16[4,256,256]{2,1,0:T(8,128)(2,1)}, bf16[4,256,256]{2,1,0:T(8,128)(2,1)S(1)}, u32[]{:S(2)}, u32[]{:S(2)}) collective-permute-start(bf16[4,256,256]{2,1,0:T(8,128)(2,1)} %amps_ref.5), channel_id=1, source_target_pairs={{0,1},{1,0},{2,3},{3,2},{4,5},{5,4},{6,7},{7,6},{8,9},{9,8},{10,11... | collective-permute-start | bytes 1572872 | tf_op jit(solution)/shard_map/ppermute | solution.py:74
  4.1 8.4 %collective-permute-start.2 = (bf16[528,128]{1,0:T(8,128)(2,1)}, bf16[528,128]{1,0:T(8,128)(2,1)S(1)}, u32[]{:S(2)}, u32[]{:S(2)}) collective-permute-start(bf16[528,128]{1,0:T(8,128)(2,1)} %get-tuple-element.26), channel_id=1, source_target_pairs={{0,7},{1,2},{2,1},{3,4},{4,3},{5,6},{6,5},{7,0},{8,15},{9,10},{10,... | collective-permute-start | bytes 405512 | tf_op jit(solution)/shard_map/ppermute | solution.py:77
  8.9 7.4 %collective-permute-start.3 = (bf16[512,128]{1,0:T(8,128)(2,1)}, bf16[512,128]{1,0:T(8,128)(2,1)S(1)}, u32[]{:S(2)}, u32[]{:S(2)}) collective-permute-start(bf16[512,128]{1,0:T(8,128)(2,1)} %get-tuple-element.27), channel_id=1, source_target_pairs={{0,7},{1,2},{2,1},{3,4},{4,3},{5,6},{6,5},{7,0},{8,15},{9,10},{10,... | collective-permute-start | bytes 393224 | tf_op jit(solution)/shard_map/ppermute | solution.py:77
  8.9 0.7 %copy-start.2 = (f32[8,128]{1,0:T(8,128)S(1)}, f32[8,128]{1,0:T(8,128)}, u32[]{:S(2)}) copy-start(f32[8,128]{1,0:T(8,128)} %get-tuple-element.25.after_ref.nums) | copy-start | bytes 12292
  11.2 7.0 %copy-start = (bf16[4,512,256]{2,1,0:T(8,128)(2,1)S(1)}, bf16[4,512,256]{2,1,0:T(8,128)(2,1)}, u32[]{:S(2)}) copy-start(bf16[4,512,256]{2,1,0:T(8,128)(2,1)} %coeff_ref.11) | copy-start | bytes 3145732
  11.2 7.0 %copy-start.1 = (bf16[4,256,256]{2,1,0:T(8,128)(2,1)S(1)}, bf16[4,256,256]{2,1,0:T(8,128)(2,1)}, u32[]{:S(2)}) copy-start(bf16[4,256,256]{2,1,0:T(8,128)(2,1)} %amps_ref.5) | copy-start | bytes 1572868
  13.0 8.4 %copy-start.6 = (bf16[528,128]{1,0:T(8,128)(2,1)S(1)}, bf16[528,128]{1,0:T(8,128)(2,1)}, u32[]{:S(2)}) copy-start(bf16[528,128]{1,0:T(8,128)(2,1)} %get-tuple-element.26) | copy-start | bytes 405508
  13.1 9.7 %copy-start.3 = (f32[8,128]{1,0:T(8,128)S(1)}, f32[8,128]{1,0:T(8,128)}, u32[]{:S(2)}) copy-start(f32[8,128]{1,0:T(8,128)} %get-tuple-element.25.after_ref.nums) | copy-start | bytes 12292
  13.1 19.1 %collective-permute-start.5 = (bf16[1040,128]{1,0:T(8,128)(2,1)S(1)}, bf16[1040,128]{1,0:T(8,128)(2,1)S(1)}, u32[]{:S(2)}, u32[]{:S(2)}) collective-permute-start(bf16[1040,128]{1,0:T(8,128)(2,1)S(1)} %shard_map.115.after_ref), channel_id=1, source_target_pairs={{0,7},{1,2},{2,1},{3,4},{4,3},{5,6},{6,5},{7,0},{8,15},{9,10},{10,... | collective-permute-start | bytes 798728 | tf_op jit(solution)/shard_map/ppermute | solution.py:77
  16.8 15.4 %collective-permute-start.6 = (bf16[1024,128]{1,0:T(8,128)(2,1)S(1)}, bf16[1024,128]{1,0:T(8,128)(2,1)S(1)}, u32[]{:S(2)}, u32[]{:S(2)}) collective-permute-start(bf16[1024,128]{1,0:T(8,128)(2,1)S(1)} %shard_map.116.after_ref), channel_id=1, source_target_pairs={{0,7},{1,2},{2,1},{3,4},{4,3},{5,6},{6,5},{7,0},{8,15},{9,10},{10,... | collective-permute-start | bytes 786440 | tf_op jit(solution)/shard_map/ppermute | solution.py:77
  19.1 6.9 %copy-start.4 = (f32[4,256]{1,0:T(4,128)S(1)}, f32[4,256]{1,0:T(4,128)}, u32[]{:S(2)}) copy-start(f32[4,256]{1,0:T(4,128)} %eps_ref.1) | copy-start | bytes 12292
  19.1 13.0 %collective-permute-start.7 = (bf16[272,256]{1,0:T(8,128)(2,1)S(1)}, bf16[272,256]{1,0:T(8,128)(2,1)S(1)}, u32[]{:S(2)}, u32[]{:S(2)}) collective-permute-start(bf16[272,256]{1,0:T(8,128)(2,1)S(1)} %get-tuple-element.28.after_ref), channel_id=1, source_target_pairs={{0,7},{1,2},{2,1},{3,4},{4,3},{5,6},{6,5},{7,0},{8,15},{9,10},{10,... | collective-permute-start | bytes 417800 | tf_op jit(solution)/shard_map/ppermute | solution.py:77
  21.4 1.4 %copy-start.5 = (bf16[2,1024,512]{2,1,0:T(8,128)(2,1)}, bf16[2,1024,512]{2,1,0:T(8,128)(2,1)S(1)}, u32[]{:S(2)}) copy-start(bf16[2,1024,512]{2,1,0:T(8,128)(2,1)S(1)} %collective-permute-done.4.three_in_ref) | copy-start | bytes 6291460
  21.4 6.0 %collective-permute-start.8 = (bf16[528,128]{1,0:T(8,128)(2,1)S(1)}, bf16[528,128]{1,0:T(8,128)(2,1)S(1)}, u32[]{:S(2)}, u32[]{:S(2)}) collective-permute-start(bf16[528,128]{1,0:T(8,128)(2,1)S(1)} %copy-done.6), channel_id=1, source_target_pairs={{0,1},{1,0},{2,3},{3,2},{4,5},{5,4},{6,7},{7,6},{8,9},{9,8},{10,11... | collective-permute-start | bytes 405512 | tf_op jit(solution)/shard_map/ppermute | solution.py:74
  23.4 16.8 %collective-permute-start.12 = (bf16[512,256]{1,0:T(8,128)(2,1)S(1)}, bf16[512,256]{1,0:T(8,128)(2,1)S(1)}, u32[]{:S(2)}, u32[]{:S(2)}) collective-permute-start(bf16[512,256]{1,0:T(8,128)(2,1)S(1)} %get-tuple-element.42), channel_id=1, source_target_pairs={{0,7},{1,2},{2,1},{3,4},{4,3},{5,6},{6,5},{7,0},{8,15},{9,10},{10,... | collective-permute-start | bytes 786440 | tf_op jit(solution)/shard_map/ppermute | solution.py:77
  32.9 7.4 %collective-permute-start.9 = (bf16[256,256]{1,0:T(8,128)(2,1)S(1)}, bf16[256,256]{1,0:T(8,128)(2,1)S(1)}, u32[]{:S(2)}, u32[]{:S(2)}) collective-permute-start(bf16[256,256]{1,0:T(8,128)(2,1)S(1)} %get-tuple-element.35.amp_ref.after_ref.refs_0_), channel_id=1, source_target_pairs={{0,8},{8,0},{16,24},{24,16},{1,9},{9,1},{17,25},{25,17},{2,10},{10... | collective-permute-start | bytes 393224 | tf_op jit(solution)/shard_map/ppermute | solution.py:80
  34.4 5.9 %collective-permute-start.10 = (bf16[256,256]{1,0:T(8,128)(2,1)S(1)}, bf16[256,256]{1,0:T(8,128)(2,1)S(1)}, u32[]{:S(2)}, u32[]{:S(2)}) collective-permute-start(bf16[256,256]{1,0:T(8,128)(2,1)S(1)} %get-tuple-element.35.amp_ref.after_ref.refs_0_), channel_id=1, source_target_pairs={{0,16},{8,24},{16,0},{24,8},{1,17},{9,25},{17,1},{25,9},{2,18},{10... | collective-permute-start | bytes 393224 | tf_op jit(solution)/shard_map/ppermute | solution.py:80
  35.8 5.9 %collective-permute-start.11 = (bf16[256,256]{1,0:T(8,128)(2,1)S(1)}, bf16[256,256]{1,0:T(8,128)(2,1)S(1)}, u32[]{:S(2)}, u32[]{:S(2)}) collective-permute-start(bf16[256,256]{1,0:T(8,128)(2,1)S(1)} %get-tuple-element.35.amp_ref.after_ref.refs_0_), channel_id=1, source_target_pairs={{0,24},{8,16},{16,8},{24,0},{1,25},{9,17},{17,9},{25,1},{2,26},{10... | collective-permute-start | bytes 393224 | tf_op jit(solution)/shard_map/ppermute | solution.py:80
  36.8 10.8 %collective-permute-start.16 = (bf16[288,256]{1,0:T(8,128)(2,1)S(1)}, bf16[288,256]{1,0:T(8,128)(2,1)S(1)}, u32[]{:S(2)}, u32[]{:S(2)}) collective-permute-start(bf16[288,256]{1,0:T(8,128)(2,1)S(1)} %get-tuple-element.47), channel_id=1, source_target_pairs={{0,8},{1,9},{2,10},{3,11},{4,12},{5,13},{6,14},{7,15}} | collective-permute-start | bytes 442376 | tf_op jit(solution)/shard_map/ppermute | solution.py:429
  41.7 8.4 %collective-permute-start.13 = (bf16[2,256,256]{2,1,0:T(8,128)(2,1)S(1)}, bf16[2,256,256]{2,1,0:T(8,128)(2,1)S(1)}, u32[]{:S(2)}, u32[]{:S(2)}) collective-permute-start(bf16[2,256,256]{2,1,0:T(8,128)(2,1)S(1)} %shard_map.124.refs_4_), channel_id=1, source_target_pairs={{0,7},{1,2},{2,1},{3,4},{4,3},{5,6},{6,5},{7,0},{8,15},{9,10},{10,... | collective-permute-start | bytes 786440 | tf_op jit(solution)/shard_map/ppermute | solution.py:77
  42.1 6.8 %collective-permute-start.17 = (bf16[288,256]{1,0:T(8,128)(2,1)S(1)}, bf16[288,256]{1,0:T(8,128)(2,1)S(1)}, u32[]{:S(2)}, u32[]{:S(2)}) collective-permute-start(bf16[288,256]{1,0:T(8,128)(2,1)S(1)} %get-tuple-element.47), channel_id=1, source_target_pairs={{0,24},{1,25},{2,26},{3,27},{4,28},{5,29},{6,30},{7,31}} | collective-permute-start | bytes 442376 | tf_op jit(solution)/shard_map/ppermute | solution.py:429
  46.2 4.0 %collective-permute-start.18 = (bf16[288,256]{1,0:T(8,128)(2,1)S(1)}, bf16[288,256]{1,0:T(8,128)(2,1)S(1)}, u32[]{:S(2)}, u32[]{:S(2)}) collective-permute-start(bf16[288,256]{1,0:T(8,128)(2,1)S(1)} %get-tuple-element.47), channel_id=1, source_target_pairs={{0,16},{1,17},{2,18},{3,19},{4,20},{5,21},{6,22},{7,23}} | collective-permute-start | bytes 442376 | tf_op jit(solution)/shard_map/ppermute | solution.py:429
  47.5 2.6 %collective-permute-start.14 = (bf16[272,256]{1,0:T(8,128)(2,1)S(1)}, bf16[272,256]{1,0:T(8,128)(2,1)S(1)}, u32[]{:S(2)}, u32[]{:S(2)}) collective-permute-start(bf16[272,256]{1,0:T(8,128)(2,1)S(1)} %get-tuple-element.43.refs_4_), channel_id=1, source_target_pairs={{0,1},{1,0},{2,3},{3,2},{4,5},{5,4},{6,7},{7,6},{8,9},{9,8},{10,11... | collective-permute-start | bytes 417800 | tf_op jit(solution)/shard_map/ppermute | solution.py:74
  47.6 2.5 %collective-permute-start.15 = (bf16[272,256]{1,0:T(8,128)(2,1)S(1)}, bf16[272,256]{1,0:T(8,128)(2,1)S(1)}, u32[]{:S(2)}, u32[]{:S(2)}) collective-permute-start(bf16[272,256]{1,0:T(8,128)(2,1)S(1)} %get-tuple-element.46), channel_id=1, source_target_pairs={{0,1},{1,0},{2,3},{3,2},{4,5},{5,4},{6,7},{7,6},{8,9},{9,8},{10,11... | collective-permute-start | bytes 417800 | tf_op jit(solution)/shard_map/ppermute | solution.py:74

commit v16 on v15

--- a/solution.py
+++ b/solution.py
@@ -55,6 +55,7 @@
     partner_count = partners.shape[1]
     slots = 2
     assert roles == pairs and pairs % 2 == 0 and columns % 2 == 0 and virt % 2 == 0
+    assert roles & (roles - 1) == 0
     tile = min(256, aux)
     pao_scale = 1.0 / math.sqrt(pao)
     aux_scale = 1.0 / math.sqrt(aux)
@@ -425,8 +426,24 @@
 
     longest = (VMEM, (virt + 2 * riders, virt), BF16)
     rest, rest_b = call(rest_body, [VMEM, VMEM], [sq_f, longest], (amp, k_first))
-    sends = [1, *range(roles - 1, 1, -1)]
-    rests = [lax.ppermute(rest_b, "role", [(0, s)]) for s in sends]
+
+    def relay_body(held_ref, come_ref, out_ref):
+        role = lax.axis_index("role")
+
+        @pl.when(role == 0)
+        def _():
+            out_ref[...] = held_ref[...]
+
+        @pl.when(role > 0)
+        def _():
+            out_ref[...] = come_ref[...]
+
+    rests, held, step = [], rest_b, 1
+    while step < roles:
+        rests.append(lax.ppermute(held, "role", [(i, i + step) for i in range(step)]))
+        step *= 2
+        if step < roles:
+            (held,) = call(relay_body, [VMEM, VMEM], [longest], (held, rests[-1]))
 
     def extra_out_body(coeff_ref, x_ref, after_ref, s_ref):
         @pl.when(lax.axis_index("role") > 0)
@@ -509,7 +526,7 @@
     def last_body(
         nums, coeff_ref, gain_ref, gain_extra_ref, rest_ref, rest_extra_ref, co_ref, ci_ref, cei_ref, *refs
     ):
-        rest_refs, (amp_out, orb_out, amp_ref, orb_ref, sems) = refs[: roles - 1], refs[roles - 1 :]
+        rest_refs, (amp_out, orb_out, amp_ref, orb_ref, sems) = refs[:-5], refs[-5:]
         num, _ = read(nums)
         role = lax.axis_index("role")
         copies = []
@@ -522,10 +539,11 @@
             @pl.when(here)
             def _():
                 total = rest[...] - co_ref[slot].astype(F32) - c_in[:virt, :].astype(F32)
-                for s in range(1, roles):
-                    if slot:
-                        come = rest_refs[sends.index(s)][:virt, :].astype(F32)
-                        total += jnp.where(role == s, come, 0.0)
+                if slot:
+                    come = rest_refs[0][:virt, :]
+                    for at, ref in enumerate(rest_refs[1:], 1):
+                        come = jnp.where(role >= 1 << at, ref[:virt, :], come)
+                    total += come.astype(F32)
                 amp_ref[slot] = (gain[...] * total).astype(BF16)
 
             @pl.when(jnp.logical_not(here))
@@ -556,7 +574,7 @@
 
     amps_out, dressed_out = call(
         last_body,
-        [VMEM] + [VMEM] * (8 + roles - 1),
+        [VMEM] * (9 + len(rests)),
         [(ANY, (slots, virt, virt), BF16), (ANY, (slots, pao, virt), BF16)],
         (
             nums, coeff, gain, gain_extra, rest, rest_extra,

time: 51.4 us -> 50.6 us (0.984)
  starting transfers between devices: 28.7 us -> 24.1 us
  waiting for transfers between devices: 9.45 us -> 12.3 us
  Pallas kernels: 10.1 us -> 11.2 us
    ppermute x7, starting transfers between devices: 14.7 us -> 12.2 us  [outer(): return lax.ppermute(x, 'pairs', list(enumerate(outer_of)))]
    ppermute x3 -> x2, starting transfers between devices: 8.84 us -> 6.65 us  [local(): lax.ppermute(held, 'role', [(i, i + step) for i in range(step)])]
    ppermute x7, waiting for transfers between devices: 5.98 us -> 7.87 us  [outer(): return lax.ppermute(x, 'pairs', list(enumerate(outer_of)))]
    pallas_call x15 -> x16, Pallas kernels: 10.1 us -> 11.2 us  [call(): pl.pallas_call(body, in_specs=ins, out_specs=[spec for spec, _, _ in outs...]
    ppermute x3 -> x2, waiting for transfers between devices: 2.04 us -> 2.79 us  [local(): lax.ppermute(held, 'role', [(i, i + step) for i in range(step)])]
  transfers between devices with their start and end apart: 19 -> 18, of which waited for: 5 -> 6; matrix products, arithmetic and copies ran while one was open for 0% -> 0% of each run, Pallas kernels for 18% -> 20%
where the time goes in v16:
time: 50.6 us; the launch traced here: 50.4 us
  starting transfers between devices  24.1 us (48%)
  waiting for transfers between devices  12.3 us (24%)
  Pallas kernels  11.2 us (22%)
  local copies, waits for them, and re-layouts  1.99 us (4%)
  between operations  0.86 us (2%)
    ppermute x7, starting transfers between devices, outer(): return lax.ppermute(x, 'pairs', list(enumerate(outer_of)))  12.2 us
    pallas_call x16, Pallas kernels, call(): pl.pallas_call(body, in_specs=ins, out_specs=[spec for spec, _, _ in outs...  11.2 us
    ppermute x7, waiting for transfers between devices, outer(): return lax.ppermute(x, 'pairs', list(enumerate(outer_of)))  7.87 us
    ppermute x2, starting transfers between devices, local(): lax.ppermute(held, 'role', [(i, i + step) for i in range(step)])  6.65 us
    ppermute x3, starting transfers between devices, swap(): return lax.ppermute(x, 'role', [(i, i ^ by) for i in range(roles)])  3.55 us
    ppermute x2, waiting for transfers between devices, local(): lax.ppermute(held, 'role', [(i, i + step) for i in range(step)])  2.79 us
    unnamed x14, local copies, waits for them, and re-layouts  1.99 us
    ppermute x6, starting transfers between devices, inner(): return lax.ppermute(x, 'pairs', list(enumerate(inner_of)))  1.66 us
  transfers between devices with their start and end apart: 18, of which 6 were waited for; matrix products, arithmetic and copies ran while one was open for 0% of the time, Pallas kernels for 20%

profile of v16, /device:TPU:0, one launch (start us, length us, event | category | flops | bytes accessed | tf_op | source)
XLA Modules:
  0.0 50.4 jit_solution(17668478041105911880)
XLA Ops:
  0.6 0.5 %collective-permute-start.4 = (bf16[2,1024,512]{2,1,0:T(8,128)(2,1)}, bf16[2,1024,512]{2,1,0:T(8,128)(2,1)S(1)}, u32[]{:S(2)}, u32[]{:S(2)}) collective-permute-start(bf16[2,1024,512]{2,1,0:T(8,128)(2,1)} %three_ref.1), channel_id=1, source_target_pairs={{0,1},{1,0},{2,3},{3,2},{4,5},{5,4},{6,7},{7,6},{8,9},{9,8},{10,11... | collective-permute-start | bytes 6291464 | tf_op jit(solution)/shard_map/ppermute | solution.py:75
  1.1 0.1 collective-permute-start
  1.2 0.4 collective-permute-start.1
  1.7 2.4 %shard_map.113 = (bf16[528,128]{1,0:T(8,128)(2,1)}, bf16[512,128]{1,0:T(8,128)(2,1)}, f32[8,128]{1,0:T(8,128)}) custom-call(s32[4]{0:T(128)} %owner_hbm.1, s32[2,4]{1,0:T(2,128)} %bitcast.1, s32[4,8]{1,0:T(4,128)} %partner_hbm.1, f32[4,8]{1,0:T(4,128)} %coupling_hbm.1, f32[16]{0:T(128)} %eps_hbm.1, s32[4]{0:T(128)} %nvirt_hbm.1, bf16[4,512,256]{2,1,0:T(8,128)(2,1)} %coeff_ref.11), custom_call_target="tpu_custom_call" | custom-call | flops 1 | bytes 1 | tf_op jit(solution)/shard_map/pallas_call | solution.py:37
  4.1 4.8 %collective-permute-start.2 = (bf16[528,128]{1,0:T(8,128)(2,1)}, bf16[528,128]{1,0:T(8,128)(2,1)S(1)}, u32[]{:S(2)}, u32[]{:S(2)}) collective-permute-start(bf16[528,128]{1,0:T(8,128)(2,1)} %get-tuple-element.26), channel_id=1, source_target_pairs={{0,7},{1,2},{2,1},{3,4},{4,3},{5,6},{6,5},{7,0},{8,15},{9,10},{10,... | collective-permute-start | bytes 405512 | tf_op jit(solution)/shard_map/ppermute | solution.py:78
  8.9 0.1 collective-permute-start.3
  8.9 0.0 copy-start.2
  8.9 0.7 %copy-done.2 = f32[8,128]{1,0:T(8,128)S(1)} copy-done((f32[8,128]{1,0:T(8,128)S(1)}, f32[8,128]{1,0:T(8,128)}, u32[]{:S(2)}) %copy-start.2) | copy-done | bytes 4120
  9.6 1.6 %shard_map.114.three_ref = bf16[2,1024,512]{2,1,0:T(8,128)(2,1)S(1)} custom-call(bf16[2,1024,512]{2,1,0:T(8,128)(2,1)} %three_ref.1, f32[8,128]{1,0:T(8,128)S(1)} %copy-done.2), custom_call_target="tpu_custom_call" | custom-call | flops 1 | bytes 1 | tf_op jit(solution)/shard_map/pallas_call | solution.py:37
  11.2 0.0 copy-start
  11.2 0.0 copy-start.1
  11.3 1.3 %collective-permute-done.2.x_ref.low_ref = bf16[528,128]{1,0:T(8,128)(2,1)S(1)} collective-permute-done((bf16[528,128]{1,0:T(8,128)(2,1)}, bf16[528,128]{1,0:T(8,128)(2,1)S(1)}, u32[]{:S(2)}, u32[]{:S(2)}) %collective-permute-start.2) | collective-permute-done | bytes 135200 | tf_op jit(solution)/shard_map/ppermute | solution.py:78
  12.5 0.5 %shard_map.115.after_ref = bf16[1040,128]{1,0:T(8,128)(2,1)S(1)} custom-call(bf16[2,1024,512]{2,1,0:T(8,128)(2,1)S(1)} %shard_map.114.three_ref, bf16[528,128]{1,0:T(8,128)(2,1)S(1)} %collective-permute-done.2.x_ref.low_ref), custom_call_target="tpu_custom_call" | custom-call | flops 1 | bytes 1 | tf_op jit(solution)/shard_map/pallas_call | solution.py:37
  13.0 0.0 copy-start.6
  13.1 0.0 copy-start.3
  13.1 3.2 %collective-permute-start.5 = (bf16[1040,128]{1,0:T(8,128)(2,1)S(1)}, bf16[1040,128]{1,0:T(8,128)(2,1)S(1)}, u32[]{:S(2)}, u32[]{:S(2)}) collective-permute-start(bf16[1040,128]{1,0:T(8,128)(2,1)S(1)} %shard_map.115.after_ref), channel_id=1, source_target_pairs={{0,7},{1,2},{2,1},{3,4},{4,3},{5,6},{6,5},{7,0},{8,15},{9,10},{10,... | collective-permute-start | bytes 798728 | tf_op jit(solution)/shard_map/ppermute | solution.py:78
  16.3 0.0 collective-permute-done.3.x_ref.high_ref
  16.3 0.5 %shard_map.116.after_ref = bf16[1024,128]{1,0:T(8,128)(2,1)S(1)} custom-call(bf16[2,1024,512]{2,1,0:T(8,128)(2,1)S(1)} %shard_map.114.three_ref, bf16[528,128]{1,0:T(8,128)(2,1)S(1)} %collective-permute-done.2.x_ref.low_ref, bf16[512,128]{1,0:T(8,128)(2,1)S(1)} %collective-permute-done.3.x_ref.high_ref, bf16[1040,128]{1,0:T(8,128)(2,1)S(1)} %shard_map.115.after_ref), custom_call_target="tpu_custom_call" | custom-call | flops 1 | bytes 1 | tf_op jit(solution)/shard_map/pallas_call | solution.py:37
  16.8 1.4 %collective-permute-start.6 = (bf16[1024,128]{1,0:T(8,128)(2,1)S(1)}, bf16[1024,128]{1,0:T(8,128)(2,1)S(1)}, u32[]{:S(2)}, u32[]{:S(2)}) collective-permute-start(bf16[1024,128]{1,0:T(8,128)(2,1)S(1)} %shard_map.116.after_ref), channel_id=1, source_target_pairs={{0,7},{1,2},{2,1},{3,4},{4,3},{5,6},{6,5},{7,0},{8,15},{9,10},{10,... | collective-permute-start | bytes 786440 | tf_op jit(solution)/shard_map/ppermute | solution.py:78
  18.2 0.0 copy-done
  18.2 0.0 copy-done.1
  18.2 0.9 %shard_map.117 = (bf16[4,256,256]{2,1,0:T(8,128)(2,1)S(1)}, bf16[272,256]{1,0:T(8,128)(2,1)S(1)}) custom-call(bf16[4,512,256]{2,1,0:T(8,128)(2,1)S(1)} %copy-done, bf16[4,256,256]{2,1,0:T(8,128)(2,1)S(1)} %copy-done.1, bf16[528,128]{1,0:T(8,128)(2,1)S(1)} %collective-permute-done.2.x_ref.low_ref, bf16[512,128]{1,0:T(8,128)(2,1)S(1)} %collective-permute-done.3.x_ref.high_ref, ...), custom_call_target="tpu_custom_call" | custom-call | flops 1 | bytes 1 | tf_op jit(solution)/shard_map/pallas_call | solution.py:37
  19.1 0.0 collective-permute-done.1.amps_in_ref
  19.1 0.0 copy-start.4
  19.1 2.3 %collective-permute-start.7 = (bf16[272,256]{1,0:T(8,128)(2,1)S(1)}, bf16[272,256]{1,0:T(8,128)(2,1)S(1)}, u32[]{:S(2)}, u32[]{:S(2)}) collective-permute-start(bf16[272,256]{1,0:T(8,128)(2,1)S(1)} %get-tuple-element.28.after_ref), channel_id=1, source_target_pairs={{0,7},{1,2},{2,1},{3,4},{4,3},{5,6},{6,5},{7,0},{8,15},{9,10},{10,... | collective-permute-start | bytes 417800 | tf_op jit(solution)/shard_map/ppermute | solution.py:78
  21.4 0.0 collective-permute-done.4.three_in_ref
  21.4 0.0 copy-done.6
  21.4 0.0 copy-start.5
  21.4 0.1 collective-permute-start.8
  21.5 1.3 %copy-done.5 = bf16[2,1024,512]{2,1,0:T(8,128)(2,1)} copy-done((bf16[2,1024,512]{2,1,0:T(8,128)(2,1)}, bf16[2,1024,512]{2,1,0:T(8,128)(2,1)S(1)}, u32[]{:S(2)}) %copy-start.5) | copy-done | bytes 2097176
  22.8 0.0 copy-done.3
  22.8 1.8 %shard_map.119 = (bf16[256,1024]{1,0:T(8,128)(2,1)S(1)}, bf16[1024,256]{1,0:T(8,128)(2,1)S(1)}, bf16[512,256]{1,0:T(8,128)(2,1)S(1)}) custom-call(f32[8,128]{1,0:T(8,128)S(1)} %copy-done.3, bf16[2,1024,512]{2,1,0:T(8,128)(2,1)S(1)} %shard_map.114.three_ref, bf16[2,1024,512]{2,1,0:T(8,128)(2,1)} %copy-done.5, bf16[4,512,256]{2,1,0:T(8,128)(2,1)S(1)} %copy-done, ...), custom_call_target="tpu_custom_call" | custom-call | flops 1 | bytes 1 | tf_op jit(solution)/shard_map/pallas_call | solution.py:37
  24.6 0.0 collective-permute-done.coeff_in_ref.in_ref
  24.6 0.2 collective-permute-start.12
  24.8 0.0 copy-done.4
  24.8 1.5 %shard_map.118 = (bf16[4,256,256]{2,1,0:T(8,128)(2,1)S(1)}, f32[256,256]{1,0:T(8,128)S(1)}, f32[256,256]{1,0:T(8,128)S(1)}, f32[256,256]{1,0:T(8,128)S(1)}) custom-call(f32[8,128]{1,0:T(8,128)S(1)} %copy-done.3, bf16[4,512,256]{2,1,0:T(8,128)(2,1)S(1)} %copy-done, bf16[4,512,256]{2,1,0:T(8,128)(2,1)S(1)} %collective-permute-done.coeff_in_ref.in_ref, ...), custom_call_target="tpu_custom_call" | custom-call | flops 1 | bytes 1 | tf_op jit(solution)/shard_map/pallas_call | solution.py:37
  26.3 0.0 collective-permute-done.8.low_ref
  26.3 5.9 %collective-permute-done.7.co_ref = bf16[272,256]{1,0:T(8,128)(2,1)S(1)} collective-permute-done((bf16[272,256]{1,0:T(8,128)(2,1)S(1)}, bf16[272,256]{1,0:T(8,128)(2,1)S(1)}, u32[]{:S(2)}, u32[]{:S(2)}) %collective-permute-start.7) | collective-permute-done | bytes 139296 | tf_op jit(solution)/shard_map/ppermute | solution.py:78
  32.2 0.0 collective-permute-done.6.high_ref
  32.2 0.0 collective-permute-done.5.low_ref
  32.2 0.5 %shard_map.121 = (bf16[256,256]{1,0:T(8,128)(2,1)S(1)}, f32[256,256]{1,0:T(8,128)S(1)}) custom-call(f32[8,128]{1,0:T(8,128)S(1)} %copy-done.3, bf16[256,1024]{1,0:T(8,128)(2,1)S(1)} %get-tuple-element.31.first_ref, bf16[1024,256]{1,0:T(8,128)(2,1)S(1)} %get-tuple-element.32.second_ref, bf16[1040,128]{1,0:T(8,128)(2,1)S(1)} %collective-permute-done.5.low_ref, ...), custom_call_target="tpu_custom_call" | custom-call | flops 1 | bytes 1 | tf_op jit(solution)/shard_map/pallas_call | solution.py:37
  32.8 1.6 %collective-permute-start.9 = (bf16[256,256]{1,0:T(8,128)(2,1)S(1)}, bf16[256,256]{1,0:T(8,128)(2,1)S(1)}, u32[]{:S(2)}, u32[]{:S(2)}) collective-permute-start(bf16[256,256]{1,0:T(8,128)(2,1)S(1)} %get-tuple-element.35.amp_ref.after_ref.refs_0_), channel_id=1, source_target_pairs={{0,8},{8,0},{16,24},{24,16},{1,9},{9,1},{17,25},{25,17},{2,10},{10... | collective-permute-start | bytes 393224 | tf_op jit(solution)/shard_map/ppermute | solution.py:81
  34.3 1.6 %collective-permute-start.10 = (bf16[256,256]{1,0:T(8,128)(2,1)S(1)}, bf16[256,256]{1,0:T(8,128)(2,1)S(1)}, u32[]{:S(2)}, u32[]{:S(2)}) collective-permute-start(bf16[256,256]{1,0:T(8,128)(2,1)S(1)} %get-tuple-element.35.amp_ref.after_ref.refs_0_), channel_id=1, source_target_pairs={{0,16},{8,24},{16,0},{24,8},{1,17},{9,25},{17,1},{25,9},{2,18},{10... | collective-permute-start | bytes 393224 | tf_op jit(solution)/shard_map/ppermute | solution.py:81
  36.0 0.3 collective-permute-start.11
  36.3 0.4 shard_map.122
  36.7 3.4 %collective-permute-start.16 = (bf16[288,256]{1,0:T(8,128)(2,1)S(1)}, bf16[288,256]{1,0:T(8,128)(2,1)S(1)}, u32[]{:S(2)}, u32[]{:S(2)}) collective-permute-start(bf16[288,256]{1,0:T(8,128)(2,1)S(1)} %get-tuple-element.47.held_ref), channel_id=1, source_target_pairs={{0,8},{1,9},{2,10},{3,11},{4,12},{5,13},{6,14},{7,15}} | collective-permute-start | bytes 442376 | tf_op jit(solution)/shard_map/ppermute | solution.py:443
  40.1 0.0 collective-permute-done.12.x_ref
  40.2 0.0 collective-permute-done.9.refs_1_
  40.2 0.0 collective-permute-done.10.refs_2_
  40.2 1.6 %collective-permute-done.11.refs_3_ = bf16[256,256]{1,0:T(8,128)(2,1)S(1)} collective-permute-done((bf16[256,256]{1,0:T(8,128)(2,1)S(1)}, bf16[256,256]{1,0:T(8,128)(2,1)S(1)}, u32[]{:S(2)}, u32[]{:S(2)}) %collective-permute-start.11) | collective-permute-done | bytes 131104 | tf_op jit(solution)/shard_map/ppermute | solution.py:81
  41.8 0.2 collective-permute-start.13
  42.0 0.7 %collective-permute-done.16.come_ref.refs_0_ = bf16[288,256]{1,0:T(8,128)(2,1)S(1)} collective-permute-done((bf16[288,256]{1,0:T(8,128)(2,1)S(1)}, bf16[288,256]{1,0:T(8,128)(2,1)S(1)}, u32[]{:S(2)}, u32[]{:S(2)}) %collective-permute-start.16) | collective-permute-done | bytes 147488 | tf_op jit(solution)/shard_map/ppermute | solution.py:443
  42.8 3.2 %collective-permute-start.17 = (bf16[288,256]{1,0:T(8,128)(2,1)S(1)}, bf16[288,256]{1,0:T(8,128)(2,1)S(1)}, u32[]{:S(2)}, u32[]{:S(2)}) collective-permute-start(bf16[288,256]{1,0:T(8,128)(2,1)S(1)} %shard_map.127), channel_id=1, source_target_pairs={{0,16},{8,24},{1,17},{9,25},{2,18},{10,26},{3,19},{11,27},{4,20},{... | collective-permute-start | bytes 442376 | tf_op jit(solution)/shard_map/ppermute | solution.py:443
  46.1 0.1 collective-permute-start.14
  46.1 0.5 collective-permute-start.15
  46.6 2.0 %collective-permute-done.17.refs_1_ = bf16[288,256]{1,0:T(8,128)(2,1)S(1)} collective-permute-done((bf16[288,256]{1,0:T(8,128)(2,1)S(1)}, bf16[288,256]{1,0:T(8,128)(2,1)S(1)}, u32[]{:S(2)}, u32[]{:S(2)}) %collective-permute-start.17) | collective-permute-done | bytes 147488 | tf_op jit(solution)/shard_map/ppermute | solution.py:443
  48.7 0.0 collective-permute-done.14.ci_ref
  48.7 0.0 collective-permute-done.15.cei_ref
  48.7 0.7 %collective-permute-done.13.co_ref = bf16[2,256,256]{2,1,0:T(8,128)(2,1)S(1)} collective-permute-done((bf16[2,256,256]{2,1,0:T(8,128)(2,1)S(1)}, bf16[2,256,256]{2,1,0:T(8,128)(2,1)S(1)}, u32[]{:S(2)}, u32[]{:S(2)}) %collective-permute-start.13) | collective-permute-done | bytes 262176 | tf_op jit(solution)/shard_map/ppermute | solution.py:78
  49.4 1.0 %shard_map.128 = (bf16[2,256,256]{2,1,0:T(8,128)(2,1)}, bf16[2,512,256]{2,1,0:T(8,128)(2,1)}) custom-call(f32[8,128]{1,0:T(8,128)S(1)} %copy-done.3, bf16[4,512,256]{2,1,0:T(8,128)(2,1)S(1)} %copy-done, f32[256,256]{1,0:T(8,128)S(1)} %get-tuple-element.29.gain_ref, f32[256,256]{1,0:T(8,128)S(1)} %get-tuple-element.30.gain_extra_ref, ...), custom_call_target="tpu_custom_call" | custom-call | flops 1 | bytes 1 | tf_op jit(solution)/shard_map/pallas_call | solution.py:37
  (6 shorter events, 0.1 us)
Async XLA Ops:
  0.6 20.8 %collective-permute-start.4 = (bf16[2,1024,512]{2,1,0:T(8,128)(2,1)}, bf16[2,1024,512]{2,1,0:T(8,128)(2,1)S(1)}, u32[]{:S(2)}, u32[]{:S(2)}) collective-permute-start(bf16[2,1024,512]{2,1,0:T(8,128)(2,1)} %three_ref.1), channel_id=1, source_target_pairs={{0,1},{1,0},{2,3},{3,2},{4,5},{5,4},{6,7},{7,6},{8,9},{9,8},{10,11... | collective-permute-start | bytes 6291464 | tf_op jit(solution)/shard_map/ppermute | solution.py:75
  1.1 23.4 %collective-permute-start = (bf16[4,512,256]{2,1,0:T(8,128)(2,1)}, bf16[4,512,256]{2,1,0:T(8,128)(2,1)S(1)}, u32[]{:S(2)}, u32[]{:S(2)}) collective-permute-start(bf16[4,512,256]{2,1,0:T(8,128)(2,1)} %coeff_ref.11), channel_id=1, source_target_pairs={{0,1},{1,0},{2,3},{3,2},{4,5},{5,4},{6,7},{7,6},{8,9},{9,8},{10,11... | collective-permute-start | bytes 3145736 | tf_op jit(solution)/shard_map/ppermute | solution.py:75
  1.2 17.9 %collective-permute-start.1 = (bf16[4,256,256]{2,1,0:T(8,128)(2,1)}, bf16[4,256,256]{2,1,0:T(8,128)(2,1)S(1)}, u32[]{:S(2)}, u32[]{:S(2)}) collective-permute-start(bf16[4,256,256]{2,1,0:T(8,128)(2,1)} %amps_ref.5), channel_id=1, source_target_pairs={{0,1},{1,0},{2,3},{3,2},{4,5},{5,4},{6,7},{7,6},{8,9},{9,8},{10,11... | collective-permute-start | bytes 1572872 | tf_op jit(solution)/shard_map/ppermute | solution.py:75
  4.1 8.4 %collective-permute-start.2 = (bf16[528,128]{1,0:T(8,128)(2,1)}, bf16[528,128]{1,0:T(8,128)(2,1)S(1)}, u32[]{:S(2)}, u32[]{:S(2)}) collective-permute-start(bf16[528,128]{1,0:T(8,128)(2,1)} %get-tuple-element.26), channel_id=1, source_target_pairs={{0,7},{1,2},{2,1},{3,4},{4,3},{5,6},{6,5},{7,0},{8,15},{9,10},{10,... | collective-permute-start | bytes 405512 | tf_op jit(solution)/shard_map/ppermute | solution.py:78
  8.9 7.4 %collective-permute-start.3 = (bf16[512,128]{1,0:T(8,128)(2,1)}, bf16[512,128]{1,0:T(8,128)(2,1)S(1)}, u32[]{:S(2)}, u32[]{:S(2)}) collective-permute-start(bf16[512,128]{1,0:T(8,128)(2,1)} %get-tuple-element.27), channel_id=1, source_target_pairs={{0,7},{1,2},{2,1},{3,4},{4,3},{5,6},{6,5},{7,0},{8,15},{9,10},{10,... | collective-permute-start | bytes 393224 | tf_op jit(solution)/shard_map/ppermute | solution.py:78
  8.9 0.7 %copy-start.2 = (f32[8,128]{1,0:T(8,128)S(1)}, f32[8,128]{1,0:T(8,128)}, u32[]{:S(2)}) copy-start(f32[8,128]{1,0:T(8,128)} %get-tuple-element.25.after_ref.nums) | copy-start | bytes 12292
  11.2 7.0 %copy-start = (bf16[4,512,256]{2,1,0:T(8,128)(2,1)S(1)}, bf16[4,512,256]{2,1,0:T(8,128)(2,1)}, u32[]{:S(2)}) copy-start(bf16[4,512,256]{2,1,0:T(8,128)(2,1)} %coeff_ref.11) | copy-start | bytes 3145732
  11.2 7.0 %copy-start.1 = (bf16[4,256,256]{2,1,0:T(8,128)(2,1)S(1)}, bf16[4,256,256]{2,1,0:T(8,128)(2,1)}, u32[]{:S(2)}) copy-start(bf16[4,256,256]{2,1,0:T(8,128)(2,1)} %amps_ref.5) | copy-start | bytes 1572868
  13.0 8.4 %copy-start.6 = (bf16[528,128]{1,0:T(8,128)(2,1)S(1)}, bf16[528,128]{1,0:T(8,128)(2,1)}, u32[]{:S(2)}) copy-start(bf16[528,128]{1,0:T(8,128)(2,1)} %get-tuple-element.26) | copy-start | bytes 405508
  13.1 9.7 %copy-start.3 = (f32[8,128]{1,0:T(8,128)S(1)}, f32[8,128]{1,0:T(8,128)}, u32[]{:S(2)}) copy-start(f32[8,128]{1,0:T(8,128)} %get-tuple-element.25.after_ref.nums) | copy-start | bytes 12292
  13.1 19.1 %collective-permute-start.5 = (bf16[1040,128]{1,0:T(8,128)(2,1)S(1)}, bf16[1040,128]{1,0:T(8,128)(2,1)S(1)}, u32[]{:S(2)}, u32[]{:S(2)}) collective-permute-start(bf16[1040,128]{1,0:T(8,128)(2,1)S(1)} %shard_map.115.after_ref), channel_id=1, source_target_pairs={{0,7},{1,2},{2,1},{3,4},{4,3},{5,6},{6,5},{7,0},{8,15},{9,10},{10,... | collective-permute-start | bytes 798728 | tf_op jit(solution)/shard_map/ppermute | solution.py:78
  16.8 15.4 %collective-permute-start.6 = (bf16[1024,128]{1,0:T(8,128)(2,1)S(1)}, bf16[1024,128]{1,0:T(8,128)(2,1)S(1)}, u32[]{:S(2)}, u32[]{:S(2)}) collective-permute-start(bf16[1024,128]{1,0:T(8,128)(2,1)S(1)} %shard_map.116.after_ref), channel_id=1, source_target_pairs={{0,7},{1,2},{2,1},{3,4},{4,3},{5,6},{6,5},{7,0},{8,15},{9,10},{10,... | collective-permute-start | bytes 786440 | tf_op jit(solution)/shard_map/ppermute | solution.py:78
  19.1 5.7 %copy-start.4 = (f32[4,256]{1,0:T(4,128)S(1)}, f32[4,256]{1,0:T(4,128)}, u32[]{:S(2)}) copy-start(f32[4,256]{1,0:T(4,128)} %eps_ref.1) | copy-start | bytes 12292
  19.1 13.0 %collective-permute-start.7 = (bf16[272,256]{1,0:T(8,128)(2,1)S(1)}, bf16[272,256]{1,0:T(8,128)(2,1)S(1)}, u32[]{:S(2)}, u32[]{:S(2)}) collective-permute-start(bf16[272,256]{1,0:T(8,128)(2,1)S(1)} %get-tuple-element.28.after_ref), channel_id=1, source_target_pairs={{0,7},{1,2},{2,1},{3,4},{4,3},{5,6},{6,5},{7,0},{8,15},{9,10},{10,... | collective-permute-start | bytes 417800 | tf_op jit(solution)/shard_map/ppermute | solution.py:78
  21.4 1.4 %copy-start.5 = (bf16[2,1024,512]{2,1,0:T(8,128)(2,1)}, bf16[2,1024,512]{2,1,0:T(8,128)(2,1)S(1)}, u32[]{:S(2)}) copy-start(bf16[2,1024,512]{2,1,0:T(8,128)(2,1)S(1)} %collective-permute-done.4.three_in_ref) | copy-start | bytes 6291460
  21.4 4.9 %collective-permute-start.8 = (bf16[528,128]{1,0:T(8,128)(2,1)S(1)}, bf16[528,128]{1,0:T(8,128)(2,1)S(1)}, u32[]{:S(2)}, u32[]{:S(2)}) collective-permute-start(bf16[528,128]{1,0:T(8,128)(2,1)S(1)} %copy-done.6), channel_id=1, source_target_pairs={{0,1},{1,0},{2,3},{3,2},{4,5},{5,4},{6,7},{7,6},{8,9},{9,8},{10,11... | collective-permute-start | bytes 405512 | tf_op jit(solution)/shard_map/ppermute | solution.py:75
  24.6 15.5 %collective-permute-start.12 = (bf16[512,256]{1,0:T(8,128)(2,1)S(1)}, bf16[512,256]{1,0:T(8,128)(2,1)S(1)}, u32[]{:S(2)}, u32[]{:S(2)}) collective-permute-start(bf16[512,256]{1,0:T(8,128)(2,1)S(1)} %get-tuple-element.42), channel_id=1, source_target_pairs={{0,7},{1,2},{2,1},{3,4},{4,3},{5,6},{6,5},{7,0},{8,15},{9,10},{10,... | collective-permute-start | bytes 786440 | tf_op jit(solution)/shard_map/ppermute | solution.py:78
  32.8 7.4 %collective-permute-start.9 = (bf16[256,256]{1,0:T(8,128)(2,1)S(1)}, bf16[256,256]{1,0:T(8,128)(2,1)S(1)}, u32[]{:S(2)}, u32[]{:S(2)}) collective-permute-start(bf16[256,256]{1,0:T(8,128)(2,1)S(1)} %get-tuple-element.35.amp_ref.after_ref.refs_0_), channel_id=1, source_target_pairs={{0,8},{8,0},{16,24},{24,16},{1,9},{9,1},{17,25},{25,17},{2,10},{10... | collective-permute-start | bytes 393224 | tf_op jit(solution)/shard_map/ppermute | solution.py:81
  34.3 5.9 %collective-permute-start.10 = (bf16[256,256]{1,0:T(8,128)(2,1)S(1)}, bf16[256,256]{1,0:T(8,128)(2,1)S(1)}, u32[]{:S(2)}, u32[]{:S(2)}) collective-permute-start(bf16[256,256]{1,0:T(8,128)(2,1)S(1)} %get-tuple-element.35.amp_ref.after_ref.refs_0_), channel_id=1, source_target_pairs={{0,16},{8,24},{16,0},{24,8},{1,17},{9,25},{17,1},{25,9},{2,18},{10... | collective-permute-start | bytes 393224 | tf_op jit(solution)/shard_map/ppermute | solution.py:81
  36.0 5.9 %collective-permute-start.11 = (bf16[256,256]{1,0:T(8,128)(2,1)S(1)}, bf16[256,256]{1,0:T(8,128)(2,1)S(1)}, u32[]{:S(2)}, u32[]{:S(2)}) collective-permute-start(bf16[256,256]{1,0:T(8,128)(2,1)S(1)} %get-tuple-element.35.amp_ref.after_ref.refs_0_), channel_id=1, source_target_pairs={{0,24},{8,16},{16,8},{24,0},{1,25},{9,17},{17,9},{25,1},{2,26},{10... | collective-permute-start | bytes 393224 | tf_op jit(solution)/shard_map/ppermute | solution.py:81
  36.7 6.1 %collective-permute-start.16 = (bf16[288,256]{1,0:T(8,128)(2,1)S(1)}, bf16[288,256]{1,0:T(8,128)(2,1)S(1)}, u32[]{:S(2)}, u32[]{:S(2)}) collective-permute-start(bf16[288,256]{1,0:T(8,128)(2,1)S(1)} %get-tuple-element.47.held_ref), channel_id=1, source_target_pairs={{0,8},{1,9},{2,10},{3,11},{4,12},{5,13},{6,14},{7,15}} | collective-permute-start | bytes 442376 | tf_op jit(solution)/shard_map/ppermute | solution.py:443
  41.8 7.6 %collective-permute-start.13 = (bf16[2,256,256]{2,1,0:T(8,128)(2,1)S(1)}, bf16[2,256,256]{2,1,0:T(8,128)(2,1)S(1)}, u32[]{:S(2)}, u32[]{:S(2)}) collective-permute-start(bf16[2,256,256]{2,1,0:T(8,128)(2,1)S(1)} %shard_map.124.refs_4_), channel_id=1, source_target_pairs={{0,7},{1,2},{2,1},{3,4},{4,3},{5,6},{6,5},{7,0},{8,15},{9,10},{10,... | collective-permute-start | bytes 786440 | tf_op jit(solution)/shard_map/ppermute | solution.py:78
  42.8 5.9 %collective-permute-start.17 = (bf16[288,256]{1,0:T(8,128)(2,1)S(1)}, bf16[288,256]{1,0:T(8,128)(2,1)S(1)}, u32[]{:S(2)}, u32[]{:S(2)}) collective-permute-start(bf16[288,256]{1,0:T(8,128)(2,1)S(1)} %shard_map.127), channel_id=1, source_target_pairs={{0,16},{8,24},{1,17},{9,25},{2,18},{10,26},{3,19},{11,27},{4,20},{... | collective-permute-start | bytes 442376 | tf_op jit(solution)/shard_map/ppermute | solution.py:443
  46.1 2.6 %collective-permute-start.14 = (bf16[272,256]{1,0:T(8,128)(2,1)S(1)}, bf16[272,256]{1,0:T(8,128)(2,1)S(1)}, u32[]{:S(2)}, u32[]{:S(2)}) collective-permute-start(bf16[272,256]{1,0:T(8,128)(2,1)S(1)} %get-tuple-element.43.refs_4_), channel_id=1, source_target_pairs={{0,1},{1,0},{2,3},{3,2},{4,5},{5,4},{6,7},{7,6},{8,9},{9,8},{10,11... | collective-permute-start | bytes 417800 | tf_op jit(solution)/shard_map/ppermute | solution.py:75
  46.1 2.6 %collective-permute-start.15 = (bf16[272,256]{1,0:T(8,128)(2,1)S(1)}, bf16[272,256]{1,0:T(8,128)(2,1)S(1)}, u32[]{:S(2)}, u32[]{:S(2)}) collective-permute-start(bf16[272,256]{1,0:T(8,128)(2,1)S(1)} %get-tuple-element.46), channel_id=1, source_target_pairs={{0,1},{1,0},{2,3},{3,2},{4,5},{5,4},{6,7},{7,6},{8,9},{9,8},{10,11... | collective-permute-start | bytes 417800 | tf_op jit(solution)/shard_map/ppermute | solution.py:75

commit v17 on v16

--- a/solution.py
+++ b/solution.py
@@ -33,13 +33,14 @@
     return lax.dot_general(a, b, (dims, ((), ())), preferred_element_type=F32)
 
 
-def call(body, ins, outs, args, scratch=(), vmem=48):
+def call(body, ins, outs, args, scratch=(), vmem=48, in_place=None):
     return pl.pallas_call(
         body,
         in_specs=ins,
         out_specs=[spec for spec, _, _ in outs],
         out_shape=[jax.ShapeDtypeStruct(shape, dtype) for _, shape, dtype in outs],
         scratch_shapes=list(scratch),
+        input_output_aliases=in_place or {},
         cost_estimate=pl.CostEstimate(flops=1, bytes_accessed=1, transcendentals=0),
         compiler_params=pltpu.CompilerParams(vmem_limit_bytes=vmem * 1024 * 1024),
     )(*args)
@@ -523,68 +524,95 @@
         (nums, rest, s_own, se_own, *amp_roles, c_in),
     )
 
+    def taken(num):
+        role = lax.axis_index("role")
+        return role > 0, role == whole(num(OWNER))
+
+    def clear_body(nums, after_ref, amp_out, orb_out, zero_ref, sems):
+        num, _ = read(nums)
+        zero_ref[...] = jnp.zeros((pao, virt), BF16)
+        for slot, here in enumerate(taken(num)):
+
+            @pl.when(jnp.logical_not(here))
+            def _():
+                copies = [
+                    pltpu.make_async_copy(zero_ref.at[pl.ds(0, virt)], amp_out.at[slot], sems.at[0]),
+                    pltpu.make_async_copy(zero_ref, orb_out.at[slot], sems.at[1]),
+                ]
+                for copy in copies:
+                    copy.start()
+                for copy in copies:
+                    copy.wait()
+
+    outs = [(ANY, (slots, virt, virt), BF16), (ANY, (slots, pao, virt), BF16)]
+    cleared = call(
+        clear_body,
+        [VMEM, ANY],
+        outs,
+        (nums, c_in),
+        scratch=[pltpu.VMEM((pao, virt), BF16), pltpu.SemaphoreType.DMA((2,))],
+    )
+
     def last_body(
         nums, coeff_ref, gain_ref, gain_extra_ref, rest_ref, rest_extra_ref, co_ref, ci_ref, cei_ref, *refs
     ):
-        rest_refs, (amp_out, orb_out, amp_ref, orb_ref, sems) = refs[:-5], refs[-5:]
+        rest_refs, (amp_out, orb_out, amp_ref, orb_ref, sems) = refs[: len(rests)], refs[-5:]
         num, _ = read(nums)
         role = lax.axis_index("role")
-        copies = []
-
-        def send(source, target):
-            copies.append(pltpu.make_async_copy(source, target, sems.at[len(copies)]))
-            copies[-1].start()
-
-        def store(slot, here, gain, rest, c_in, pair):
-            @pl.when(here)
+        halves = [pl.ds(at, virt) for at in range(0, pao, virt)]
+
+        def copies_of(slot):
+            copies = [(amp_ref.at[slot], amp_out.at[slot])]
+            copies += [(orb_ref.at[slot, rows], orb_out.at[slot, rows]) for rows in halves]
+            first = slot * len(copies)
+            return [
+                pltpu.make_async_copy(source, target, sems.at[first + at])
+                for at, (source, target) in enumerate(copies)
+            ]
+
+        here = taken(num)
+        gains, kept = (gain_ref, gain_extra_ref), (rest_ref, rest_extra_ref)
+        for slot, pair in ((0, MINE), (1, EXTRA)):
+
+            @pl.when(here[slot])
             def _():
-                total = rest[...] - co_ref[slot].astype(F32) - c_in[:virt, :].astype(F32)
+                copies = copies_of(slot)
+                c_in = (ci_ref, cei_ref)[slot][:virt, :]
+                total = kept[slot][...] - co_ref[slot].astype(F32) - c_in.astype(F32)
                 if slot:
                     come = rest_refs[0][:virt, :]
                     for at, ref in enumerate(rest_refs[1:], 1):
                         come = jnp.where(role >= 1 << at, ref[:virt, :], come)
                     total += come.astype(F32)
-                amp_ref[slot] = (gain[...] * total).astype(BF16)
-
-            @pl.when(jnp.logical_not(here))
-            def _():
-                amp_ref[slot] = jnp.zeros(square, BF16)
-
-            send(amp_ref.at[slot], amp_out.at[slot])
-            for at in range(0, pao, virt):
-                rows = pl.ds(at, virt)
-
-                @pl.when(here)
-                def _():
-                    x = coeff_ref[pair, rows, :]
+                amp_ref[slot] = (gains[slot][...] * total).astype(BF16)
+                copies[0].start()
+                for rows, copy in zip(halves, copies[1:]):
+                    x = coeff_ref[whole(num(pair)), rows, :]
                     dressed = x.astype(F32) + mxu(x, amp_ref[slot], NN) * virt_scale
                     orb_ref[slot, rows, :] = dressed.astype(BF16)
-
-                @pl.when(jnp.logical_not(here))
-                def _():
-                    orb_ref[slot, rows, :] = jnp.zeros((virt, virt), BF16)
-
-                send(orb_ref.at[slot, rows], orb_out.at[slot, rows])
-
-        store(0, role > 0, gain_ref, rest_ref, ci_ref, whole(num(MINE)))
-        has_extra = role == whole(num(OWNER))
-        store(1, has_extra, gain_extra_ref, rest_extra_ref, cei_ref, whole(num(EXTRA)))
-        for copy in copies:
-            copy.wait()
-
+                    copy.start()
+
+        for slot in range(slots):
+
+            @pl.when(here[slot])
+            def _():
+                for copy in copies_of(slot):
+                    copy.wait()
+
+    ins = (
+        nums, coeff, gain, gain_extra, rest, rest_extra, cc_from_out, c_from_in, ce_from_in, *rests, *cleared
+    )
     amps_out, dressed_out = call(
         last_body,
-        [VMEM] * (9 + len(rests)),
-        [(ANY, (slots, virt, virt), BF16), (ANY, (slots, pao, virt), BF16)],
-        (
-            nums, coeff, gain, gain_extra, rest, rest_extra,
-            cc_from_out, c_from_in, ce_from_in, *rests,
-        ),
+        [VMEM] * (len(ins) - 2) + [ANY] * 2,
+        outs,
+        ins,
         scratch=[
             pltpu.VMEM((slots, virt, virt), BF16),
             pltpu.VMEM((slots, pao, virt), BF16),
             pltpu.SemaphoreType.DMA((slots * (1 + pao // virt),)),
         ],
+        in_place={len(ins) - 2: 0, len(ins) - 1: 1},
     )
     return amps_out, dressed_out
 

time: 50.6 us -> 49.9 us (0.986)
  waiting for transfers between devices: 12.3 us -> 9.41 us
  starting transfers between devices: 24.1 us -> 25.4 us
  Pallas kernels: 11.2 us -> 11.9 us
    ppermute x2, waiting for transfers between devices: 2.79 us -> 0.98 us  [local(): lax.ppermute(held, 'role', [(i, i + step) for i in range(step)])]
    ppermute x7, starting transfers between devices: 12.2 us -> 13.6 us  [outer(): return lax.ppermute(x, 'pairs', list(enumerate(outer_of)))]
    ppermute x7, waiting for transfers between devices: 7.87 us -> 6.77 us  [outer(): return lax.ppermute(x, 'pairs', list(enumerate(outer_of)))]
    pallas_call x16 -> x17, Pallas kernels: 11.2 us -> 11.9 us  [call(): pl.pallas_call(body, in_specs=ins, out_specs=[spec for spec, _, _ in outs...]
  transfers between devices with their start and end apart: 18 -> 18, of which waited for: 6 -> 6; matrix products, arithmetic and copies ran while one was open for 0% -> 0% of each run, Pallas kernels for 20% -> 24%
where the time goes in v17:
time: 49.9 us; the launch traced here: 49.6 us
  starting transfers between devices  25.4 us (51%)
  Pallas kernels  11.9 us (24%)
  waiting for transfers between devices  9.41 us (19%)
  local copies, waits for them, and re-layouts  1.98 us (4%)
  between operations  0.87 us (2%)
    ppermute x7, starting transfers between devices, outer(): return lax.ppermute(x, 'pairs', list(enumerate(outer_of)))  13.6 us
    pallas_call x17, Pallas kernels, call(): pl.pallas_call(body, in_specs=ins, out_specs=[spec for spec, _, _ in outs...  11.9 us
    ppermute x7, waiting for transfers between devices, outer(): return lax.ppermute(x, 'pairs', list(enumerate(outer_of)))  6.77 us
    ppermute x2, starting transfers between devices, local(): lax.ppermute(held, 'role', [(i, i + step) for i in range(step)])  6.58 us
    ppermute x3, starting transfers between devices, swap(): return lax.ppermute(x, 'role', [(i, i ^ by) for i in range(roles)])  3.55 us
    unnamed x14, local copies, waits for them, and re-layouts  1.98 us
    ppermute x6, starting transfers between devices, inner(): return lax.ppermute(x, 'pairs', list(enumerate(inner_of)))  1.66 us
    ppermute x3, waiting for transfers between devices, swap(): return lax.ppermute(x, 'role', [(i, i ^ by) for i in range(roles)])  1.64 us
  transfers between devices with their start and end apart: 18, of which 6 were waited for; matrix products, arithmetic and copies ran while one was open for 0% of the time, Pallas kernels for 24%

profile of v17, /device:TPU:0, one launch (start us, length us, event | category | flops | bytes accessed | tf_op | source)
XLA Modules:
  0.0 49.6 jit_solution(8864882149937084304)
XLA Ops:
  0.6 0.5 %collective-permute-start.4 = (bf16[2,1024,512]{2,1,0:T(8,128)(2,1)}, bf16[2,1024,512]{2,1,0:T(8,128)(2,1)S(1)}, u32[]{:S(2)}, u32[]{:S(2)}) collective-permute-start(bf16[2,1024,512]{2,1,0:T(8,128)(2,1)} %three_ref.1), channel_id=1, source_target_pairs={{0,1},{1,0},{2,3},{3,2},{4,5},{5,4},{6,7},{7,6},{8,9},{9,8},{10,11... | collective-permute-start | bytes 6291464 | tf_op jit(solution)/shard_map/ppermute | solution.py:76
  1.1 0.1 collective-permute-start
  1.2 0.4 collective-permute-start.1
  1.7 2.4 %shard_map.113 = (bf16[528,128]{1,0:T(8,128)(2,1)}, bf16[512,128]{1,0:T(8,128)(2,1)}, f32[8,128]{1,0:T(8,128)}) custom-call(s32[4]{0:T(128)} %owner_hbm.1, s32[2,4]{1,0:T(2,128)} %bitcast.1, s32[4,8]{1,0:T(4,128)} %partner_hbm.1, f32[4,8]{1,0:T(4,128)} %coupling_hbm.1, f32[16]{0:T(128)} %eps_hbm.1, s32[4]{0:T(128)} %nvirt_hbm.1, bf16[4,512,256]{2,1,0:T(8,128)(2,1)} %coeff_ref.11), custom_call_target="tpu_custom_call" | custom-call | flops 1 | bytes 1 | tf_op jit(solution)/shard_map/pallas_call | solution.py:37
  4.1 4.8 %collective-permute-start.2 = (bf16[528,128]{1,0:T(8,128)(2,1)}, bf16[528,128]{1,0:T(8,128)(2,1)S(1)}, u32[]{:S(2)}, u32[]{:S(2)}) collective-permute-start(bf16[528,128]{1,0:T(8,128)(2,1)} %get-tuple-element.28), channel_id=1, source_target_pairs={{0,7},{1,2},{2,1},{3,4},{4,3},{5,6},{6,5},{7,0},{8,15},{9,10},{10,... | collective-permute-start | bytes 405512 | tf_op jit(solution)/shard_map/ppermute | solution.py:79
  8.9 0.1 collective-permute-start.3
  8.9 0.0 copy-start.2
  8.9 0.7 %copy-done.2 = f32[8,128]{1,0:T(8,128)S(1)} copy-done((f32[8,128]{1,0:T(8,128)S(1)}, f32[8,128]{1,0:T(8,128)}, u32[]{:S(2)}) %copy-start.2) | copy-done | bytes 4120
  9.6 1.6 %shard_map.114.three_ref = bf16[2,1024,512]{2,1,0:T(8,128)(2,1)S(1)} custom-call(bf16[2,1024,512]{2,1,0:T(8,128)(2,1)} %three_ref.1, f32[8,128]{1,0:T(8,128)S(1)} %copy-done.2), custom_call_target="tpu_custom_call" | custom-call | flops 1 | bytes 1 | tf_op jit(solution)/shard_map/pallas_call | solution.py:37
  11.2 0.0 copy-start
  11.2 0.0 copy-start.1
  11.2 1.3 %collective-permute-done.2.x_ref.low_ref = bf16[528,128]{1,0:T(8,128)(2,1)S(1)} collective-permute-done((bf16[528,128]{1,0:T(8,128)(2,1)}, bf16[528,128]{1,0:T(8,128)(2,1)S(1)}, u32[]{:S(2)}, u32[]{:S(2)}) %collective-permute-start.2) | collective-permute-done | bytes 135200 | tf_op jit(solution)/shard_map/ppermute | solution.py:79
  12.5 0.5 %shard_map.115.after_ref = bf16[1040,128]{1,0:T(8,128)(2,1)S(1)} custom-call(bf16[2,1024,512]{2,1,0:T(8,128)(2,1)S(1)} %shard_map.114.three_ref, bf16[528,128]{1,0:T(8,128)(2,1)S(1)} %collective-permute-done.2.x_ref.low_ref), custom_call_target="tpu_custom_call" | custom-call | flops 1 | bytes 1 | tf_op jit(solution)/shard_map/pallas_call | solution.py:37
  13.0 0.0 copy-start.6
  13.1 0.0 copy-start.3
  13.1 3.2 %collective-permute-start.5 = (bf16[1040,128]{1,0:T(8,128)(2,1)S(1)}, bf16[1040,128]{1,0:T(8,128)(2,1)S(1)}, u32[]{:S(2)}, u32[]{:S(2)}) collective-permute-start(bf16[1040,128]{1,0:T(8,128)(2,1)S(1)} %shard_map.115.after_ref), channel_id=1, source_target_pairs={{0,7},{1,2},{2,1},{3,4},{4,3},{5,6},{6,5},{7,0},{8,15},{9,10},{10,... | collective-permute-start | bytes 798728 | tf_op jit(solution)/shard_map/ppermute | solution.py:79
  16.3 0.0 collective-permute-done.3.x_ref.high_ref
  16.3 0.5 %shard_map.116.after_ref = bf16[1024,128]{1,0:T(8,128)(2,1)S(1)} custom-call(bf16[2,1024,512]{2,1,0:T(8,128)(2,1)S(1)} %shard_map.114.three_ref, bf16[528,128]{1,0:T(8,128)(2,1)S(1)} %collective-permute-done.2.x_ref.low_ref, bf16[512,128]{1,0:T(8,128)(2,1)S(1)} %collective-permute-done.3.x_ref.high_ref, bf16[1040,128]{1,0:T(8,128)(2,1)S(1)} %shard_map.115.after_ref), custom_call_target="tpu_custom_call" | custom-call | flops 1 | bytes 1 | tf_op jit(solution)/shard_map/pallas_call | solution.py:37
  16.8 1.4 %collective-permute-start.6 = (bf16[1024,128]{1,0:T(8,128)(2,1)S(1)}, bf16[1024,128]{1,0:T(8,128)(2,1)S(1)}, u32[]{:S(2)}, u32[]{:S(2)}) collective-permute-start(bf16[1024,128]{1,0:T(8,128)(2,1)S(1)} %shard_map.116.after_ref), channel_id=1, source_target_pairs={{0,7},{1,2},{2,1},{3,4},{4,3},{5,6},{6,5},{7,0},{8,15},{9,10},{10,... | collective-permute-start | bytes 786440 | tf_op jit(solution)/shard_map/ppermute | solution.py:79
  18.2 0.0 copy-done
  18.2 0.0 copy-done.1
  18.2 0.9 %shard_map.117 = (bf16[4,256,256]{2,1,0:T(8,128)(2,1)S(1)}, bf16[272,256]{1,0:T(8,128)(2,1)S(1)}) custom-call(bf16[4,512,256]{2,1,0:T(8,128)(2,1)S(1)} %copy-done, bf16[4,256,256]{2,1,0:T(8,128)(2,1)S(1)} %copy-done.1, bf16[528,128]{1,0:T(8,128)(2,1)S(1)} %collective-permute-done.2.x_ref.low_ref, bf16[512,128]{1,0:T(8,128)(2,1)S(1)} %collective-permute-done.3.x_ref.high_ref, ...), custom_call_target="tpu_custom_call" | custom-call | flops 1 | bytes 1 | tf_op jit(solution)/shard_map/pallas_call | solution.py:37
  19.1 0.0 collective-permute-done.1.amps_in_ref
  19.1 0.0 copy-start.4
  19.1 2.3 %collective-permute-start.7 = (bf16[272,256]{1,0:T(8,128)(2,1)S(1)}, bf16[272,256]{1,0:T(8,128)(2,1)S(1)}, u32[]{:S(2)}, u32[]{:S(2)}) collective-permute-start(bf16[272,256]{1,0:T(8,128)(2,1)S(1)} %get-tuple-element.30.after_ref), channel_id=1, source_target_pairs={{0,7},{1,2},{2,1},{3,4},{4,3},{5,6},{6,5},{7,0},{8,15},{9,10},{10,... | collective-permute-start | bytes 417800 | tf_op jit(solution)/shard_map/ppermute | solution.py:79
  21.4 0.0 collective-permute-done.4.three_in_ref
  21.4 0.0 copy-done.6
  21.4 0.0 copy-start.5
  21.4 0.1 collective-permute-start.8
  21.5 1.3 %copy-done.5 = bf16[2,1024,512]{2,1,0:T(8,128)(2,1)} copy-done((bf16[2,1024,512]{2,1,0:T(8,128)(2,1)}, bf16[2,1024,512]{2,1,0:T(8,128)(2,1)S(1)}, u32[]{:S(2)}) %copy-start.5) | copy-done | bytes 2097176
  22.8 0.0 copy-done.3
  22.8 1.8 %shard_map.119 = (bf16[256,1024]{1,0:T(8,128)(2,1)S(1)}, bf16[1024,256]{1,0:T(8,128)(2,1)S(1)}, bf16[512,256]{1,0:T(8,128)(2,1)S(1)}) custom-call(f32[8,128]{1,0:T(8,128)S(1)} %copy-done.3, bf16[2,1024,512]{2,1,0:T(8,128)(2,1)S(1)} %shard_map.114.three_ref, bf16[2,1024,512]{2,1,0:T(8,128)(2,1)} %copy-done.5, bf16[4,512,256]{2,1,0:T(8,128)(2,1)S(1)} %copy-done, ...), custom_call_target="tpu_custom_call" | custom-call | flops 1 | bytes 1 | tf_op jit(solution)/shard_map/pallas_call | solution.py:37
  24.6 0.0 collective-permute-done.coeff_in_ref.in_ref
  24.6 1.4 %collective-permute-start.12 = (bf16[512,256]{1,0:T(8,128)(2,1)S(1)}, bf16[512,256]{1,0:T(8,128)(2,1)S(1)}, u32[]{:S(2)}, u32[]{:S(2)}) collective-permute-start(bf16[512,256]{1,0:T(8,128)(2,1)S(1)} %get-tuple-element.44), channel_id=1, source_target_pairs={{0,7},{1,2},{2,1},{3,4},{4,3},{5,6},{6,5},{7,0},{8,15},{9,10},{10,... | collective-permute-start | bytes 786440 | tf_op jit(solution)/shard_map/ppermute | solution.py:79
  26.0 0.0 copy-done.4
  26.0 1.5 %shard_map.118 = (bf16[4,256,256]{2,1,0:T(8,128)(2,1)S(1)}, f32[256,256]{1,0:T(8,128)S(1)}, f32[256,256]{1,0:T(8,128)S(1)}, f32[256,256]{1,0:T(8,128)S(1)}) custom-call(f32[8,128]{1,0:T(8,128)S(1)} %copy-done.3, bf16[4,512,256]{2,1,0:T(8,128)(2,1)S(1)} %copy-done, bf16[4,512,256]{2,1,0:T(8,128)(2,1)S(1)} %collective-permute-done.coeff_in_ref.in_ref, ...), custom_call_target="tpu_custom_call" | custom-call | flops 1 | bytes 1 | tf_op jit(solution)/shard_map/pallas_call | solution.py:37
  27.5 0.0 collective-permute-done.8.low_ref
  27.5 4.7 %collective-permute-done.7.co_ref = bf16[272,256]{1,0:T(8,128)(2,1)S(1)} collective-permute-done((bf16[272,256]{1,0:T(8,128)(2,1)S(1)}, bf16[272,256]{1,0:T(8,128)(2,1)S(1)}, u32[]{:S(2)}, u32[]{:S(2)}) %collective-permute-start.7) | collective-permute-done | bytes 139296 | tf_op jit(solution)/shard_map/ppermute | solution.py:79
  32.2 0.0 collective-permute-done.6.high_ref
  32.2 0.0 collective-permute-done.5.low_ref
  32.2 0.5 %shard_map.121 = (bf16[256,256]{1,0:T(8,128)(2,1)S(1)}, f32[256,256]{1,0:T(8,128)S(1)}) custom-call(f32[8,128]{1,0:T(8,128)S(1)} %copy-done.3, bf16[256,1024]{1,0:T(8,128)(2,1)S(1)} %get-tuple-element.33.first_ref, bf16[1024,256]{1,0:T(8,128)(2,1)S(1)} %get-tuple-element.34.second_ref, bf16[1040,128]{1,0:T(8,128)(2,1)S(1)} %collective-permute-done.5.low_ref, ...), custom_call_target="tpu_custom_call" | custom-call | flops 1 | bytes 1 | tf_op jit(solution)/shard_map/pallas_call | solution.py:37
  32.8 1.6 %collective-permute-start.9 = (bf16[256,256]{1,0:T(8,128)(2,1)S(1)}, bf16[256,256]{1,0:T(8,128)(2,1)S(1)}, u32[]{:S(2)}, u32[]{:S(2)}) collective-permute-start(bf16[256,256]{1,0:T(8,128)(2,1)S(1)} %get-tuple-element.37.amp_ref.after_ref.refs_0_), channel_id=1, source_target_pairs={{0,8},{8,0},{16,24},{24,16},{1,9},{9,1},{17,25},{25,17},{2,10},{10... | collective-permute-start | bytes 393224 | tf_op jit(solution)/shard_map/ppermute | solution.py:82
  34.3 1.6 %collective-permute-start.10 = (bf16[256,256]{1,0:T(8,128)(2,1)S(1)}, bf16[256,256]{1,0:T(8,128)(2,1)S(1)}, u32[]{:S(2)}, u32[]{:S(2)}) collective-permute-start(bf16[256,256]{1,0:T(8,128)(2,1)S(1)} %get-tuple-element.37.amp_ref.after_ref.refs_0_), channel_id=1, source_target_pairs={{0,16},{8,24},{16,0},{24,8},{1,17},{9,25},{17,1},{25,9},{2,18},{10... | collective-permute-start | bytes 393224 | tf_op jit(solution)/shard_map/ppermute | solution.py:82
  36.0 0.3 collective-permute-start.11
  36.3 0.4 shard_map.122
  36.7 3.4 %collective-permute-start.16 = (bf16[288,256]{1,0:T(8,128)(2,1)S(1)}, bf16[288,256]{1,0:T(8,128)(2,1)S(1)}, u32[]{:S(2)}, u32[]{:S(2)}) collective-permute-start(bf16[288,256]{1,0:T(8,128)(2,1)S(1)} %get-tuple-element.49.held_ref), channel_id=1, source_target_pairs={{0,8},{1,9},{2,10},{3,11},{4,12},{5,13},{6,14},{7,15}} | collective-permute-start | bytes 442376 | tf_op jit(solution)/shard_map/ppermute | solution.py:444
  40.1 0.0 collective-permute-done.12.x_ref
  40.2 0.0 collective-permute-done.9.refs_1_
  40.2 0.0 collective-permute-done.10.refs_2_
  40.2 1.6 %collective-permute-done.11.refs_3_ = bf16[256,256]{1,0:T(8,128)(2,1)S(1)} collective-permute-done((bf16[256,256]{1,0:T(8,128)(2,1)S(1)}, bf16[256,256]{1,0:T(8,128)(2,1)S(1)}, u32[]{:S(2)}, u32[]{:S(2)}) %collective-permute-start.11) | collective-permute-done | bytes 131104 | tf_op jit(solution)/shard_map/ppermute | solution.py:82
  41.8 0.5 collective-permute-start.13
  42.3 0.5 collective-permute-done.16.come_ref.refs_0_
  42.8 3.2 %collective-permute-start.17 = (bf16[288,256]{1,0:T(8,128)(2,1)S(1)}, bf16[288,256]{1,0:T(8,128)(2,1)S(1)}, u32[]{:S(2)}, u32[]{:S(2)}) collective-permute-start(bf16[288,256]{1,0:T(8,128)(2,1)S(1)} %shard_map.127), channel_id=1, source_target_pairs={{0,16},{8,24},{1,17},{9,25},{2,18},{10,26},{3,19},{11,27},{4,20},{... | collective-permute-start | bytes 442376 | tf_op jit(solution)/shard_map/ppermute | solution.py:444
  46.0 0.1 collective-permute-start.14
  46.1 0.5 %collective-permute-start.15 = (bf16[272,256]{1,0:T(8,128)(2,1)S(1)}, bf16[272,256]{1,0:T(8,128)(2,1)S(1)}, u32[]{:S(2)}, u32[]{:S(2)}) collective-permute-start(bf16[272,256]{1,0:T(8,128)(2,1)S(1)} %get-tuple-element.48), channel_id=1, source_target_pairs={{0,1},{1,0},{2,3},{3,2},{4,5},{5,4},{6,7},{7,6},{8,9},{9,8},{10,11... | collective-permute-start | bytes 417800 | tf_op jit(solution)/shard_map/ppermute | solution.py:76
  46.6 1.5 %shard_map.128 = (bf16[2,256,256]{2,1,0:T(8,128)(2,1)}, bf16[2,512,256]{2,1,0:T(8,128)(2,1)}) custom-call(f32[8,128]{1,0:T(8,128)S(1)} %copy-done.3, bf16[272,256]{1,0:T(8,128)(2,1)S(1)} %get-tuple-element.45.refs_4_.after_ref), custom_call_target="tpu_custom_call" | custom-call | flops 1 | bytes 1 | tf_op jit(solution)/shard_map/pallas_call | solution.py:37
  48.1 0.5 collective-permute-done.17.refs_1_
  48.6 0.0 collective-permute-done.14.ci_ref
  48.6 0.0 collective-permute-done.15.cei_ref
  48.6 0.8 %collective-permute-done.13.co_ref = bf16[2,256,256]{2,1,0:T(8,128)(2,1)S(1)} collective-permute-done((bf16[2,256,256]{2,1,0:T(8,128)(2,1)S(1)}, bf16[2,256,256]{2,1,0:T(8,128)(2,1)S(1)}, u32[]{:S(2)}, u32[]{:S(2)}) %collective-permute-start.13) | collective-permute-done | bytes 262176 | tf_op jit(solution)/shard_map/ppermute | solution.py:79
  49.4 0.2 shard_map.129
  (6 shorter events, 0.1 us)
Async XLA Ops:
  0.6 20.8 %collective-permute-start.4 = (bf16[2,1024,512]{2,1,0:T(8,128)(2,1)}, bf16[2,1024,512]{2,1,0:T(8,128)(2,1)S(1)}, u32[]{:S(2)}, u32[]{:S(2)}) collective-permute-start(bf16[2,1024,512]{2,1,0:T(8,128)(2,1)} %three_ref.1), channel_id=1, source_target_pairs={{0,1},{1,0},{2,3},{3,2},{4,5},{5,4},{6,7},{7,6},{8,9},{9,8},{10,11... | collective-permute-start | bytes 6291464 | tf_op jit(solution)/shard_map/ppermute | solution.py:76
  1.1 23.4 %collective-permute-start = (bf16[4,512,256]{2,1,0:T(8,128)(2,1)}, bf16[4,512,256]{2,1,0:T(8,128)(2,1)S(1)}, u32[]{:S(2)}, u32[]{:S(2)}) collective-permute-start(bf16[4,512,256]{2,1,0:T(8,128)(2,1)} %coeff_ref.11), channel_id=1, source_target_pairs={{0,1},{1,0},{2,3},{3,2},{4,5},{5,4},{6,7},{7,6},{8,9},{9,8},{10,11... | collective-permute-start | bytes 3145736 | tf_op jit(solution)/shard_map/ppermute | solution.py:76
  1.2 17.9 %collective-permute-start.1 = (bf16[4,256,256]{2,1,0:T(8,128)(2,1)}, bf16[4,256,256]{2,1,0:T(8,128)(2,1)S(1)}, u32[]{:S(2)}, u32[]{:S(2)}) collective-permute-start(bf16[4,256,256]{2,1,0:T(8,128)(2,1)} %amps_ref.5), channel_id=1, source_target_pairs={{0,1},{1,0},{2,3},{3,2},{4,5},{5,4},{6,7},{7,6},{8,9},{9,8},{10,11... | collective-permute-start | bytes 1572872 | tf_op jit(solution)/shard_map/ppermute | solution.py:76
  4.1 8.4 %collective-permute-start.2 = (bf16[528,128]{1,0:T(8,128)(2,1)}, bf16[528,128]{1,0:T(8,128)(2,1)S(1)}, u32[]{:S(2)}, u32[]{:S(2)}) collective-permute-start(bf16[528,128]{1,0:T(8,128)(2,1)} %get-tuple-element.28), channel_id=1, source_target_pairs={{0,7},{1,2},{2,1},{3,4},{4,3},{5,6},{6,5},{7,0},{8,15},{9,10},{10,... | collective-permute-start | bytes 405512 | tf_op jit(solution)/shard_map/ppermute | solution.py:79
  8.9 7.4 %collective-permute-start.3 = (bf16[512,128]{1,0:T(8,128)(2,1)}, bf16[512,128]{1,0:T(8,128)(2,1)S(1)}, u32[]{:S(2)}, u32[]{:S(2)}) collective-permute-start(bf16[512,128]{1,0:T(8,128)(2,1)} %get-tuple-element.29), channel_id=1, source_target_pairs={{0,7},{1,2},{2,1},{3,4},{4,3},{5,6},{6,5},{7,0},{8,15},{9,10},{10,... | collective-permute-start | bytes 393224 | tf_op jit(solution)/shard_map/ppermute | solution.py:79
  8.9 0.7 %copy-start.2 = (f32[8,128]{1,0:T(8,128)S(1)}, f32[8,128]{1,0:T(8,128)}, u32[]{:S(2)}) copy-start(f32[8,128]{1,0:T(8,128)} %get-tuple-element.27.after_ref.nums) | copy-start | bytes 12292
  11.2 7.0 %copy-start = (bf16[4,512,256]{2,1,0:T(8,128)(2,1)S(1)}, bf16[4,512,256]{2,1,0:T(8,128)(2,1)}, u32[]{:S(2)}) copy-start(bf16[4,512,256]{2,1,0:T(8,128)(2,1)} %coeff_ref.11) | copy-start | bytes 3145732
  11.2 7.0 %copy-start.1 = (bf16[4,256,256]{2,1,0:T(8,128)(2,1)S(1)}, bf16[4,256,256]{2,1,0:T(8,128)(2,1)}, u32[]{:S(2)}) copy-start(bf16[4,256,256]{2,1,0:T(8,128)(2,1)} %amps_ref.5) | copy-start | bytes 1572868
  13.0 8.4 %copy-start.6 = (bf16[528,128]{1,0:T(8,128)(2,1)S(1)}, bf16[528,128]{1,0:T(8,128)(2,1)}, u32[]{:S(2)}) copy-start(bf16[528,128]{1,0:T(8,128)(2,1)} %get-tuple-element.28) | copy-start | bytes 405508
  13.1 9.7 %copy-start.3 = (f32[8,128]{1,0:T(8,128)S(1)}, f32[8,128]{1,0:T(8,128)}, u32[]{:S(2)}) copy-start(f32[8,128]{1,0:T(8,128)} %get-tuple-element.27.after_ref.nums) | copy-start | bytes 12292
  13.1 19.1 %collective-permute-start.5 = (bf16[1040,128]{1,0:T(8,128)(2,1)S(1)}, bf16[1040,128]{1,0:T(8,128)(2,1)S(1)}, u32[]{:S(2)}, u32[]{:S(2)}) collective-permute-start(bf16[1040,128]{1,0:T(8,128)(2,1)S(1)} %shard_map.115.after_ref), channel_id=1, source_target_pairs={{0,7},{1,2},{2,1},{3,4},{4,3},{5,6},{6,5},{7,0},{8,15},{9,10},{10,... | collective-permute-start | bytes 798728 | tf_op jit(solution)/shard_map/ppermute | solution.py:79
  16.8 15.4 %collective-permute-start.6 = (bf16[1024,128]{1,0:T(8,128)(2,1)S(1)}, bf16[1024,128]{1,0:T(8,128)(2,1)S(1)}, u32[]{:S(2)}, u32[]{:S(2)}) collective-permute-start(bf16[1024,128]{1,0:T(8,128)(2,1)S(1)} %shard_map.116.after_ref), channel_id=1, source_target_pairs={{0,7},{1,2},{2,1},{3,4},{4,3},{5,6},{6,5},{7,0},{8,15},{9,10},{10,... | collective-permute-start | bytes 786440 | tf_op jit(solution)/shard_map/ppermute | solution.py:79
  19.1 6.9 %copy-start.4 = (f32[4,256]{1,0:T(4,128)S(1)}, f32[4,256]{1,0:T(4,128)}, u32[]{:S(2)}) copy-start(f32[4,256]{1,0:T(4,128)} %eps_ref.1) | copy-start | bytes 12292
  19.1 13.0 %collective-permute-start.7 = (bf16[272,256]{1,0:T(8,128)(2,1)S(1)}, bf16[272,256]{1,0:T(8,128)(2,1)S(1)}, u32[]{:S(2)}, u32[]{:S(2)}) collective-permute-start(bf16[272,256]{1,0:T(8,128)(2,1)S(1)} %get-tuple-element.30.after_ref), channel_id=1, source_target_pairs={{0,7},{1,2},{2,1},{3,4},{4,3},{5,6},{6,5},{7,0},{8,15},{9,10},{10,... | collective-permute-start | bytes 417800 | tf_op jit(solution)/shard_map/ppermute | solution.py:79
  21.4 1.4 %copy-start.5 = (bf16[2,1024,512]{2,1,0:T(8,128)(2,1)}, bf16[2,1024,512]{2,1,0:T(8,128)(2,1)S(1)}, u32[]{:S(2)}) copy-start(bf16[2,1024,512]{2,1,0:T(8,128)(2,1)S(1)} %collective-permute-done.4.three_in_ref) | copy-start | bytes 6291460
  21.4 6.0 %collective-permute-start.8 = (bf16[528,128]{1,0:T(8,128)(2,1)S(1)}, bf16[528,128]{1,0:T(8,128)(2,1)S(1)}, u32[]{:S(2)}, u32[]{:S(2)}) collective-permute-start(bf16[528,128]{1,0:T(8,128)(2,1)S(1)} %copy-done.6), channel_id=1, source_target_pairs={{0,1},{1,0},{2,3},{3,2},{4,5},{5,4},{6,7},{7,6},{8,9},{9,8},{10,11... | collective-permute-start | bytes 405512 | tf_op jit(solution)/shard_map/ppermute | solution.py:76
  24.6 15.5 %collective-permute-start.12 = (bf16[512,256]{1,0:T(8,128)(2,1)S(1)}, bf16[512,256]{1,0:T(8,128)(2,1)S(1)}, u32[]{:S(2)}, u32[]{:S(2)}) collective-permute-start(bf16[512,256]{1,0:T(8,128)(2,1)S(1)} %get-tuple-element.44), channel_id=1, source_target_pairs={{0,7},{1,2},{2,1},{3,4},{4,3},{5,6},{6,5},{7,0},{8,15},{9,10},{10,... | collective-permute-start | bytes 786440 | tf_op jit(solution)/shard_map/ppermute | solution.py:79
  32.8 7.4 %collective-permute-start.9 = (bf16[256,256]{1,0:T(8,128)(2,1)S(1)}, bf16[256,256]{1,0:T(8,128)(2,1)S(1)}, u32[]{:S(2)}, u32[]{:S(2)}) collective-permute-start(bf16[256,256]{1,0:T(8,128)(2,1)S(1)} %get-tuple-element.37.amp_ref.after_ref.refs_0_), channel_id=1, source_target_pairs={{0,8},{8,0},{16,24},{24,16},{1,9},{9,1},{17,25},{25,17},{2,10},{10... | collective-permute-start | bytes 393224 | tf_op jit(solution)/shard_map/ppermute | solution.py:82
  34.3 5.9 %collective-permute-start.10 = (bf16[256,256]{1,0:T(8,128)(2,1)S(1)}, bf16[256,256]{1,0:T(8,128)(2,1)S(1)}, u32[]{:S(2)}, u32[]{:S(2)}) collective-permute-start(bf16[256,256]{1,0:T(8,128)(2,1)S(1)} %get-tuple-element.37.amp_ref.after_ref.refs_0_), channel_id=1, source_target_pairs={{0,16},{8,24},{16,0},{24,8},{1,17},{9,25},{17,1},{25,9},{2,18},{10... | collective-permute-start | bytes 393224 | tf_op jit(solution)/shard_map/ppermute | solution.py:82
  36.0 5.9 %collective-permute-start.11 = (bf16[256,256]{1,0:T(8,128)(2,1)S(1)}, bf16[256,256]{1,0:T(8,128)(2,1)S(1)}, u32[]{:S(2)}, u32[]{:S(2)}) collective-permute-start(bf16[256,256]{1,0:T(8,128)(2,1)S(1)} %get-tuple-element.37.amp_ref.after_ref.refs_0_), channel_id=1, source_target_pairs={{0,24},{8,16},{16,8},{24,0},{1,25},{9,17},{17,9},{25,1},{2,26},{10... | collective-permute-start | bytes 393224 | tf_op jit(solution)/shard_map/ppermute | solution.py:82
  36.7 6.1 %collective-permute-start.16 = (bf16[288,256]{1,0:T(8,128)(2,1)S(1)}, bf16[288,256]{1,0:T(8,128)(2,1)S(1)}, u32[]{:S(2)}, u32[]{:S(2)}) collective-permute-start(bf16[288,256]{1,0:T(8,128)(2,1)S(1)} %get-tuple-element.49.held_ref), channel_id=1, source_target_pairs={{0,8},{1,9},{2,10},{3,11},{4,12},{5,13},{6,14},{7,15}} | collective-permute-start | bytes 442376 | tf_op jit(solution)/shard_map/ppermute | solution.py:444
  41.8 7.6 %collective-permute-start.13 = (bf16[2,256,256]{2,1,0:T(8,128)(2,1)S(1)}, bf16[2,256,256]{2,1,0:T(8,128)(2,1)S(1)}, u32[]{:S(2)}, u32[]{:S(2)}) collective-permute-start(bf16[2,256,256]{2,1,0:T(8,128)(2,1)S(1)} %shard_map.124.refs_4_), channel_id=1, source_target_pairs={{0,7},{1,2},{2,1},{3,4},{4,3},{5,6},{6,5},{7,0},{8,15},{9,10},{10,... | collective-permute-start | bytes 786440 | tf_op jit(solution)/shard_map/ppermute | solution.py:79
  42.8 5.8 %collective-permute-start.17 = (bf16[288,256]{1,0:T(8,128)(2,1)S(1)}, bf16[288,256]{1,0:T(8,128)(2,1)S(1)}, u32[]{:S(2)}, u32[]{:S(2)}) collective-permute-start(bf16[288,256]{1,0:T(8,128)(2,1)S(1)} %shard_map.127), channel_id=1, source_target_pairs={{0,16},{8,24},{1,17},{9,25},{2,18},{10,26},{3,19},{11,27},{4,20},{... | collective-permute-start | bytes 442376 | tf_op jit(solution)/shard_map/ppermute | solution.py:444
  46.0 2.6 %collective-permute-start.14 = (bf16[272,256]{1,0:T(8,128)(2,1)S(1)}, bf16[272,256]{1,0:T(8,128)(2,1)S(1)}, u32[]{:S(2)}, u32[]{:S(2)}) collective-permute-start(bf16[272,256]{1,0:T(8,128)(2,1)S(1)} %get-tuple-element.45.refs_4_.after_ref), channel_id=1, source_target_pairs={{0,1},{1,0},{2,3},{3,2},{4,5},{5,4},{6,7},{7,6},{8,9},{9,8},{10,11... | collective-permute-start | bytes 417800 | tf_op jit(solution)/shard_map/ppermute | solution.py:76
  46.1 2.6 %collective-permute-start.15 = (bf16[272,256]{1,0:T(8,128)(2,1)S(1)}, bf16[272,256]{1,0:T(8,128)(2,1)S(1)}, u32[]{:S(2)}, u32[]{:S(2)}) collective-permute-start(bf16[272,256]{1,0:T(8,128)(2,1)S(1)} %get-tuple-element.48), channel_id=1, source_target_pairs={{0,1},{1,0},{2,3},{3,2},{4,5},{5,4},{6,7},{7,6},{8,9},{9,8},{10,11... | collective-permute-start | bytes 417800 | tf_op jit(solution)/shard_map/ppermute | solution.py:76

commit v18 on v17

--- a/solution.py
+++ b/solution.py
@@ -109,7 +109,7 @@
     def plan_body(
         owner_hbm, occ_hbm, partner_hbm, coupling_hbm, eps_hbm, nvirt_hbm, coeff_hbm,
         low_ref, high_ref, nums_ref,
-        owner_ref, occ_ref, partner_ref, coupling_ref, eps_ref, nvirt_ref, near_w, sems,
+        owner_ref, occ_ref, partner_ref, coupling_ref, eps_ref, nvirt_ref, near_w, coeff_ref, sems,
     ):
         small = [
             pltpu.make_async_copy(source, target, sems.at[at])
@@ -124,7 +124,8 @@
                 )
             )
         ]
-        for copy in small:
+        large = pltpu.make_async_copy(coeff_hbm, coeff_ref, sems.at[6])
+        for copy in (*small, large):
             copy.start()
         role = lax.axis_index("role")
         column = lax.axis_index("pairs")
@@ -132,12 +133,6 @@
         of_role = pairs_of_roles(owner_ref)
         extra = of_role[0]
         mine = pick(of_role, role)
-        large = [
-            pltpu.make_async_copy(coeff_hbm.at[mine, :, pl.ds(0, part)], low_ref.at[pl.ds(0, pao)], sems.at[6]),
-            pltpu.make_async_copy(coeff_hbm.at[mine, :, pl.ds(part, part)], high_ref, sems.at[7]),
-        ]
-        for copy in large:
-            copy.start()
         for copy in small[1:]:
             copy.wait()
         nums = {}
@@ -188,8 +183,9 @@
         fine = told - coarse - middle
         told = jnp.where(row == 0, coarse, jnp.where(row == 1, middle, jnp.where(row == 2, fine, 0.0)))
         low_ref[pao:, :] = told.astype(BF16)
-        for copy in large:
-            copy.wait()
+        large.wait()
+        low_ref[:pao, :] = coeff_ref[mine, :, :part]
+        high_ref[...] = coeff_ref[mine, :, part:]
 
     rode = (VMEM, (pao + riders, part), BF16)
     x_low, x_high, nums = call(
@@ -205,7 +201,8 @@
             pltpu.SMEM(eps_occ.shape, F32),
             pltpu.SMEM(nvirt.shape, I32),
             pltpu.SMEM((3 * pairs,), F32),
-            pltpu.SemaphoreType.DMA((8,)),
+            pltpu.VMEM(coeff.shape, BF16),
+            pltpu.SemaphoreType.DMA((7,)),
         ],
         vmem=60,
     )
@@ -423,10 +420,9 @@
         rest = amp.astype(F32) - both
         out_ref[...] = rest
         out_b_ref[:virt, :] = rest.astype(BF16)
-        out_b_ref[virt:, :] = jnp.zeros((2 * riders, virt), BF16)
-
-    longest = (VMEM, (virt + 2 * riders, virt), BF16)
-    rest, rest_b = call(rest_body, [VMEM, VMEM], [sq_f, longest], (amp, k_first))
+        out_b_ref[virt:, :] = jnp.zeros((riders, virt), BF16)
+
+    rest, rest_b = call(rest_body, [VMEM, VMEM], [sq_f, longer], (amp, k_first))
 
     def relay_body(held_ref, come_ref, out_ref):
         role = lax.axis_index("role")
@@ -444,7 +440,7 @@
         rests.append(lax.ppermute(held, "role", [(i, i + step) for i in range(step)]))
         step *= 2
         if step < roles:
-            (held,) = call(relay_body, [VMEM, VMEM], [longest], (held, rests[-1]))
+            (held,) = call(relay_body, [VMEM, VMEM], [longer], (held, rests[-1]))
 
     def extra_out_body(coeff_ref, x_ref, after_ref, s_ref):
         @pl.when(lax.axis_index("role") > 0)
@@ -495,13 +491,12 @@
             told = told_of(low_ref)
             for slot, of_s, c_ref in zip(range(2), (s_ref, se_ref), c_refs):
                 parts = parts_of(nums, told_weight(told, weights + slot * pairs), amp_refs)
-                c_ref[:virt, :] = coupled(of_s, parts).astype(BF16)
-                c_ref[virt:, :] = jnp.zeros((riders, virt), BF16)
+                c_ref[...] = coupled(of_s, parts).astype(BF16)
 
     c_in, ce_in = call(
         inner_again_body,
         [VMEM] + [VMEM] * (3 + roles) + [ANY],
-        [longer, longer],
+        [sq_b, sq_b],
         (nums, low_in, s_in, se_in, *amp_roles, cc_out),
     )
     c_from_in, ce_from_in = inner(c_in), inner(ce_in)
@@ -577,7 +572,7 @@
             @pl.when(here[slot])
             def _():
                 copies = copies_of(slot)
-                c_in = (ci_ref, cei_ref)[slot][:virt, :]
+                c_in = (ci_ref, cei_ref)[slot][...]
                 total = kept[slot][...] - co_ref[slot].astype(F32) - c_in.astype(F32)
                 if slot:
                     come = rest_refs[0][:virt, :]

time: 49.9 us -> 49.4 us (0.990)
  starting transfers between devices: 25.4 us -> 24.2 us
  waiting for transfers between devices: 9.41 us -> 10.5 us
    ppermute x7, starting transfers between devices: 13.6 us -> 12.4 us  [outer(): return lax.ppermute(x, 'pairs', list(enumerate(outer_of)))]
    ppermute x7, waiting for transfers between devices: 6.77 us -> 7.94 us  [outer(): return lax.ppermute(x, 'pairs', list(enumerate(outer_of)))]
  transfers between devices with their start and end apart: 18 -> 18, of which waited for: 6 -> 6; matrix products, arithmetic and copies ran while one was open for 0% -> 0% of each run, Pallas kernels for 24% -> 23%
where the time goes in v18:
time: 49.4 us; the launch traced here: 49.1 us
  starting transfers between devices  24.2 us (49%)
  Pallas kernels  11.5 us (23%)
  waiting for transfers between devices  10.5 us (21%)
  local copies, waits for them, and re-layouts  1.98 us (4%)
  between operations  0.87 us (2%)
    ppermute x7, starting transfers between devices, outer(): return lax.ppermute(x, 'pairs', list(enumerate(outer_of)))  12.4 us
    pallas_call x17, Pallas kernels, call(): pl.pallas_call(body, in_specs=ins, out_specs=[spec for spec, _, _ in outs...  11.5 us
    ppermute x7, waiting for transfers between devices, outer(): return lax.ppermute(x, 'pairs', list(enumerate(outer_of)))  7.94 us
    ppermute x2, starting transfers between devices, local(): lax.ppermute(held, 'role', [(i, i + step) for i in range(step)])  6.62 us
    ppermute x3, starting transfers between devices, swap(): return lax.ppermute(x, 'role', [(i, i ^ by) for i in range(roles)])  3.55 us
    unnamed x14, local copies, waits for them, and re-layouts  1.98 us
    ppermute x6, starting transfers between devices, inner(): return lax.ppermute(x, 'pairs', list(enumerate(inner_of)))  1.66 us
    ppermute x3, waiting for transfers between devices, swap(): return lax.ppermute(x, 'role', [(i, i ^ by) for i in range(roles)])  1.51 us
  transfers between devices with their start and end apart: 18, of which 6 were waited for; matrix products, arithmetic and copies ran while one was open for 0% of the time, Pallas kernels for 23%

profile of v18, /device:TPU:0, one launch (start us, length us, event | category | flops | bytes accessed | tf_op | source)
XLA Modules:
  0.0 49.1 jit_solution(14744704134087632484)
XLA Ops:
  0.6 0.5 %collective-permute-start.4 = (bf16[2,1024,512]{2,1,0:T(8,128)(2,1)}, bf16[2,1024,512]{2,1,0:T(8,128)(2,1)S(1)}, u32[]{:S(2)}, u32[]{:S(2)}) collective-permute-start(bf16[2,1024,512]{2,1,0:T(8,128)(2,1)} %three_ref.1), channel_id=1, source_target_pairs={{0,1},{1,0},{2,3},{3,2},{4,5},{5,4},{6,7},{7,6},{8,9},{9,8},{10,11... | collective-permute-start | bytes 6291464 | tf_op jit(solution)/shard_map/ppermute | solution.py:76
  1.1 0.1 collective-permute-start
  1.2 0.4 collective-permute-start.1
  1.7 2.0 %shard_map.113 = (bf16[528,128]{1,0:T(8,128)(2,1)}, bf16[512,128]{1,0:T(8,128)(2,1)}, f32[8,128]{1,0:T(8,128)}) custom-call(s32[4]{0:T(128)} %owner_hbm.1, s32[2,4]{1,0:T(2,128)} %bitcast.1, s32[4,8]{1,0:T(4,128)} %partner_hbm.1, f32[4,8]{1,0:T(4,128)} %coupling_hbm.1, f32[16]{0:T(128)} %eps_hbm.1, s32[4]{0:T(128)} %nvirt_hbm.1, bf16[4,512,256]{2,1,0:T(8,128)(2,1)} %coeff_ref.11), custom_call_target="tpu_custom_call" | custom-call | flops 1 | bytes 1 | tf_op jit(solution)/shard_map/pallas_call | solution.py:37
  3.7 4.8 %collective-permute-start.2 = (bf16[528,128]{1,0:T(8,128)(2,1)}, bf16[528,128]{1,0:T(8,128)(2,1)S(1)}, u32[]{:S(2)}, u32[]{:S(2)}) collective-permute-start(bf16[528,128]{1,0:T(8,128)(2,1)} %get-tuple-element.28), channel_id=1, source_target_pairs={{0,7},{1,2},{2,1},{3,4},{4,3},{5,6},{6,5},{7,0},{8,15},{9,10},{10,... | collective-permute-start | bytes 405512 | tf_op jit(solution)/shard_map/ppermute | solution.py:79
  8.5 0.1 collective-permute-start.3
  8.6 0.0 copy-start.2
  8.6 0.7 %copy-done.2 = f32[8,128]{1,0:T(8,128)S(1)} copy-done((f32[8,128]{1,0:T(8,128)S(1)}, f32[8,128]{1,0:T(8,128)}, u32[]{:S(2)}) %copy-start.2) | copy-done | bytes 4120
  9.2 1.6 %shard_map.114.three_ref = bf16[2,1024,512]{2,1,0:T(8,128)(2,1)S(1)} custom-call(bf16[2,1024,512]{2,1,0:T(8,128)(2,1)} %three_ref.1, f32[8,128]{1,0:T(8,128)S(1)} %copy-done.2), custom_call_target="tpu_custom_call" | custom-call | flops 1 | bytes 1 | tf_op jit(solution)/shard_map/pallas_call | solution.py:37
  10.8 0.0 copy-start
  10.8 0.0 copy-start.1
  10.9 1.3 %collective-permute-done.2.x_ref.low_ref = bf16[528,128]{1,0:T(8,128)(2,1)S(1)} collective-permute-done((bf16[528,128]{1,0:T(8,128)(2,1)}, bf16[528,128]{1,0:T(8,128)(2,1)S(1)}, u32[]{:S(2)}, u32[]{:S(2)}) %collective-permute-start.2) | collective-permute-done | bytes 135200 | tf_op jit(solution)/shard_map/ppermute | solution.py:79
  12.1 0.5 %shard_map.115.after_ref = bf16[1040,128]{1,0:T(8,128)(2,1)S(1)} custom-call(bf16[2,1024,512]{2,1,0:T(8,128)(2,1)S(1)} %shard_map.114.three_ref, bf16[528,128]{1,0:T(8,128)(2,1)S(1)} %collective-permute-done.2.x_ref.low_ref), custom_call_target="tpu_custom_call" | custom-call | flops 1 | bytes 1 | tf_op jit(solution)/shard_map/pallas_call | solution.py:37
  12.7 0.0 copy-start.6
  12.7 0.0 copy-start.3
  12.7 3.2 %collective-permute-start.5 = (bf16[1040,128]{1,0:T(8,128)(2,1)S(1)}, bf16[1040,128]{1,0:T(8,128)(2,1)S(1)}, u32[]{:S(2)}, u32[]{:S(2)}) collective-permute-start(bf16[1040,128]{1,0:T(8,128)(2,1)S(1)} %shard_map.115.after_ref), channel_id=1, source_target_pairs={{0,7},{1,2},{2,1},{3,4},{4,3},{5,6},{6,5},{7,0},{8,15},{9,10},{10,... | collective-permute-start | bytes 798728 | tf_op jit(solution)/shard_map/ppermute | solution.py:79
  15.9 0.0 collective-permute-done.3.x_ref.high_ref
  15.9 0.5 %shard_map.116.after_ref = bf16[1024,128]{1,0:T(8,128)(2,1)S(1)} custom-call(bf16[2,1024,512]{2,1,0:T(8,128)(2,1)S(1)} %shard_map.114.three_ref, bf16[528,128]{1,0:T(8,128)(2,1)S(1)} %collective-permute-done.2.x_ref.low_ref, bf16[512,128]{1,0:T(8,128)(2,1)S(1)} %collective-permute-done.3.x_ref.high_ref, bf16[1040,128]{1,0:T(8,128)(2,1)S(1)} %shard_map.115.after_ref), custom_call_target="tpu_custom_call" | custom-call | flops 1 | bytes 1 | tf_op jit(solution)/shard_map/pallas_call | solution.py:37
  16.4 1.4 %collective-permute-start.6 = (bf16[1024,128]{1,0:T(8,128)(2,1)S(1)}, bf16[1024,128]{1,0:T(8,128)(2,1)S(1)}, u32[]{:S(2)}, u32[]{:S(2)}) collective-permute-start(bf16[1024,128]{1,0:T(8,128)(2,1)S(1)} %shard_map.116.after_ref), channel_id=1, source_target_pairs={{0,7},{1,2},{2,1},{3,4},{4,3},{5,6},{6,5},{7,0},{8,15},{9,10},{10,... | collective-permute-start | bytes 786440 | tf_op jit(solution)/shard_map/ppermute | solution.py:79
  17.8 0.0 copy-done
  17.8 0.0 copy-done.1
  17.8 0.9 %shard_map.117 = (bf16[4,256,256]{2,1,0:T(8,128)(2,1)S(1)}, bf16[272,256]{1,0:T(8,128)(2,1)S(1)}) custom-call(bf16[4,512,256]{2,1,0:T(8,128)(2,1)S(1)} %copy-done, bf16[4,256,256]{2,1,0:T(8,128)(2,1)S(1)} %copy-done.1, bf16[528,128]{1,0:T(8,128)(2,1)S(1)} %collective-permute-done.2.x_ref.low_ref, bf16[512,128]{1,0:T(8,128)(2,1)S(1)} %collective-permute-done.3.x_ref.high_ref, ...), custom_call_target="tpu_custom_call" | custom-call | flops 1 | bytes 1 | tf_op jit(solution)/shard_map/pallas_call | solution.py:37
  18.7 0.0 collective-permute-done.1.amps_in_ref
  18.7 0.0 copy-start.4
  18.8 2.3 %collective-permute-start.7 = (bf16[272,256]{1,0:T(8,128)(2,1)S(1)}, bf16[272,256]{1,0:T(8,128)(2,1)S(1)}, u32[]{:S(2)}, u32[]{:S(2)}) collective-permute-start(bf16[272,256]{1,0:T(8,128)(2,1)S(1)} %get-tuple-element.30.after_ref), channel_id=1, source_target_pairs={{0,7},{1,2},{2,1},{3,4},{4,3},{5,6},{6,5},{7,0},{8,15},{9,10},{10,... | collective-permute-start | bytes 417800 | tf_op jit(solution)/shard_map/ppermute | solution.py:79
  21.0 0.0 collective-permute-done.4.three_in_ref
  21.0 0.0 copy-done.6
  21.0 0.0 copy-start.5
  21.0 0.1 collective-permute-start.8
  21.1 1.3 %copy-done.5 = bf16[2,1024,512]{2,1,0:T(8,128)(2,1)} copy-done((bf16[2,1024,512]{2,1,0:T(8,128)(2,1)}, bf16[2,1024,512]{2,1,0:T(8,128)(2,1)S(1)}, u32[]{:S(2)}) %copy-start.5) | copy-done | bytes 2097176
  22.4 0.0 copy-done.3
  22.4 1.8 %shard_map.119 = (bf16[256,1024]{1,0:T(8,128)(2,1)S(1)}, bf16[1024,256]{1,0:T(8,128)(2,1)S(1)}, bf16[512,256]{1,0:T(8,128)(2,1)S(1)}) custom-call(f32[8,128]{1,0:T(8,128)S(1)} %copy-done.3, bf16[2,1024,512]{2,1,0:T(8,128)(2,1)S(1)} %shard_map.114.three_ref, bf16[2,1024,512]{2,1,0:T(8,128)(2,1)} %copy-done.5, bf16[4,512,256]{2,1,0:T(8,128)(2,1)S(1)} %copy-done, ...), custom_call_target="tpu_custom_call" | custom-call | flops 1 | bytes 1 | tf_op jit(solution)/shard_map/pallas_call | solution.py:37
  24.2 0.0 collective-permute-done.coeff_in_ref.in_ref
  24.2 0.2 collective-permute-start.12
  24.4 0.0 copy-done.4
  24.4 1.5 %shard_map.118 = (bf16[4,256,256]{2,1,0:T(8,128)(2,1)S(1)}, f32[256,256]{1,0:T(8,128)S(1)}, f32[256,256]{1,0:T(8,128)S(1)}, f32[256,256]{1,0:T(8,128)S(1)}) custom-call(f32[8,128]{1,0:T(8,128)S(1)} %copy-done.3, bf16[4,512,256]{2,1,0:T(8,128)(2,1)S(1)} %copy-done, bf16[4,512,256]{2,1,0:T(8,128)(2,1)S(1)} %collective-permute-done.coeff_in_ref.in_ref, ...), custom_call_target="tpu_custom_call" | custom-call | flops 1 | bytes 1 | tf_op jit(solution)/shard_map/pallas_call | solution.py:37
  25.9 0.0 collective-permute-done.8.low_ref
  25.9 5.9 %collective-permute-done.7.co_ref = bf16[272,256]{1,0:T(8,128)(2,1)S(1)} collective-permute-done((bf16[272,256]{1,0:T(8,128)(2,1)S(1)}, bf16[272,256]{1,0:T(8,128)(2,1)S(1)}, u32[]{:S(2)}, u32[]{:S(2)}) %collective-permute-start.7) | collective-permute-done | bytes 139296 | tf_op jit(solution)/shard_map/ppermute | solution.py:79
  31.8 0.0 collective-permute-done.6.high_ref
  31.8 0.0 collective-permute-done.5.low_ref
  31.8 0.5 %shard_map.121 = (bf16[256,256]{1,0:T(8,128)(2,1)S(1)}, f32[256,256]{1,0:T(8,128)S(1)}) custom-call(f32[8,128]{1,0:T(8,128)S(1)} %copy-done.3, bf16[256,1024]{1,0:T(8,128)(2,1)S(1)} %get-tuple-element.33.first_ref, bf16[1024,256]{1,0:T(8,128)(2,1)S(1)} %get-tuple-element.34.second_ref, bf16[1040,128]{1,0:T(8,128)(2,1)S(1)} %collective-permute-done.5.low_ref, ...), custom_call_target="tpu_custom_call" | custom-call | flops 1 | bytes 1 | tf_op jit(solution)/shard_map/pallas_call | solution.py:37
  32.4 1.6 %collective-permute-start.9 = (bf16[256,256]{1,0:T(8,128)(2,1)S(1)}, bf16[256,256]{1,0:T(8,128)(2,1)S(1)}, u32[]{:S(2)}, u32[]{:S(2)}) collective-permute-start(bf16[256,256]{1,0:T(8,128)(2,1)S(1)} %get-tuple-element.37.amp_ref.after_ref.refs_0_), channel_id=1, source_target_pairs={{0,8},{8,0},{16,24},{24,16},{1,9},{9,1},{17,25},{25,17},{2,10},{10... | collective-permute-start | bytes 393224 | tf_op jit(solution)/shard_map/ppermute | solution.py:82
  33.9 1.5 %collective-permute-start.10 = (bf16[256,256]{1,0:T(8,128)(2,1)S(1)}, bf16[256,256]{1,0:T(8,128)(2,1)S(1)}, u32[]{:S(2)}, u32[]{:S(2)}) collective-permute-start(bf16[256,256]{1,0:T(8,128)(2,1)S(1)} %get-tuple-element.37.amp_ref.after_ref.refs_0_), channel_id=1, source_target_pairs={{0,16},{8,24},{16,0},{24,8},{1,17},{9,25},{17,1},{25,9},{2,18},{10... | collective-permute-start | bytes 393224 | tf_op jit(solution)/shard_map/ppermute | solution.py:82
  35.4 0.5 collective-permute-start.11
  35.9 0.4 shard_map.122
  36.3 3.4 %collective-permute-start.16 = (bf16[272,256]{1,0:T(8,128)(2,1)S(1)}, bf16[272,256]{1,0:T(8,128)(2,1)S(1)}, u32[]{:S(2)}, u32[]{:S(2)}) collective-permute-start(bf16[272,256]{1,0:T(8,128)(2,1)S(1)} %get-tuple-element.49.held_ref), channel_id=1, source_target_pairs={{0,8},{1,9},{2,10},{3,11},{4,12},{5,13},{6,14},{7,15}} | collective-permute-start | bytes 417800 | tf_op jit(solution)/shard_map/ppermute | solution.py:440
  39.8 0.0 collective-permute-done.12.x_ref
  39.8 0.0 collective-permute-done.9.refs_1_
  39.8 0.0 collective-permute-done.10.refs_2_
  39.8 1.5 %collective-permute-done.11.refs_3_ = bf16[256,256]{1,0:T(8,128)(2,1)S(1)} collective-permute-done((bf16[256,256]{1,0:T(8,128)(2,1)S(1)}, bf16[256,256]{1,0:T(8,128)(2,1)S(1)}, u32[]{:S(2)}, u32[]{:S(2)}) %collective-permute-start.11) | collective-permute-done | bytes 131104 | tf_op jit(solution)/shard_map/ppermute | solution.py:82
  41.3 0.4 collective-permute-start.13
  41.7 0.6 %collective-permute-done.16.come_ref.refs_0_ = bf16[272,256]{1,0:T(8,128)(2,1)S(1)} collective-permute-done((bf16[272,256]{1,0:T(8,128)(2,1)S(1)}, bf16[272,256]{1,0:T(8,128)(2,1)S(1)}, u32[]{:S(2)}, u32[]{:S(2)}) %collective-permute-start.16) | collective-permute-done | bytes 139296 | tf_op jit(solution)/shard_map/ppermute | solution.py:440
  42.3 3.2 %collective-permute-start.17 = (bf16[272,256]{1,0:T(8,128)(2,1)S(1)}, bf16[272,256]{1,0:T(8,128)(2,1)S(1)}, u32[]{:S(2)}, u32[]{:S(2)}) collective-permute-start(bf16[272,256]{1,0:T(8,128)(2,1)S(1)} %shard_map.127), channel_id=1, source_target_pairs={{0,16},{8,24},{1,17},{9,25},{2,18},{10,26},{3,19},{11,27},{4,20},{... | collective-permute-start | bytes 417800 | tf_op jit(solution)/shard_map/ppermute | solution.py:440
  45.6 0.1 collective-permute-start.14
  45.7 0.5 %collective-permute-start.15 = (bf16[256,256]{1,0:T(8,128)(2,1)S(1)}, bf16[256,256]{1,0:T(8,128)(2,1)S(1)}, u32[]{:S(2)}, u32[]{:S(2)}) collective-permute-start(bf16[256,256]{1,0:T(8,128)(2,1)S(1)} %get-tuple-element.48), channel_id=1, source_target_pairs={{0,1},{1,0},{2,3},{3,2},{4,5},{5,4},{6,7},{7,6},{8,9},{9,8},{10,11... | collective-permute-start | bytes 393224 | tf_op jit(solution)/shard_map/ppermute | solution.py:76
  46.2 1.5 %shard_map.128 = (bf16[2,256,256]{2,1,0:T(8,128)(2,1)}, bf16[2,512,256]{2,1,0:T(8,128)(2,1)}) custom-call(f32[8,128]{1,0:T(8,128)S(1)} %copy-done.3, bf16[256,256]{1,0:T(8,128)(2,1)S(1)} %get-tuple-element.45.refs_4_.after_ref), custom_call_target="tpu_custom_call" | custom-call | flops 1 | bytes 1 | tf_op jit(solution)/shard_map/pallas_call | solution.py:37
  47.7 0.4 collective-permute-done.17.refs_1_
  48.1 0.0 collective-permute-done.14.ci_ref
  48.1 0.0 collective-permute-done.15.cei_ref
  48.1 0.8 %collective-permute-done.13.co_ref = bf16[2,256,256]{2,1,0:T(8,128)(2,1)S(1)} collective-permute-done((bf16[2,256,256]{2,1,0:T(8,128)(2,1)S(1)}, bf16[2,256,256]{2,1,0:T(8,128)(2,1)S(1)}, u32[]{:S(2)}, u32[]{:S(2)}) %collective-permute-start.13) | collective-permute-done | bytes 262176 | tf_op jit(solution)/shard_map/ppermute | solution.py:79
  48.9 0.2 shard_map.129
  (6 shorter events, 0.1 us)
Async XLA Ops:
  0.6 20.4 %collective-permute-start.4 = (bf16[2,1024,512]{2,1,0:T(8,128)(2,1)}, bf16[2,1024,512]{2,1,0:T(8,128)(2,1)S(1)}, u32[]{:S(2)}, u32[]{:S(2)}) collective-permute-start(bf16[2,1024,512]{2,1,0:T(8,128)(2,1)} %three_ref.1), channel_id=1, source_target_pairs={{0,1},{1,0},{2,3},{3,2},{4,5},{5,4},{6,7},{7,6},{8,9},{9,8},{10,11... | collective-permute-start | bytes 6291464 | tf_op jit(solution)/shard_map/ppermute | solution.py:76
  1.1 23.0 %collective-permute-start = (bf16[4,512,256]{2,1,0:T(8,128)(2,1)}, bf16[4,512,256]{2,1,0:T(8,128)(2,1)S(1)}, u32[]{:S(2)}, u32[]{:S(2)}) collective-permute-start(bf16[4,512,256]{2,1,0:T(8,128)(2,1)} %coeff_ref.11), channel_id=1, source_target_pairs={{0,1},{1,0},{2,3},{3,2},{4,5},{5,4},{6,7},{7,6},{8,9},{9,8},{10,11... | collective-permute-start | bytes 3145736 | tf_op jit(solution)/shard_map/ppermute | solution.py:76
  1.2 17.5 %collective-permute-start.1 = (bf16[4,256,256]{2,1,0:T(8,128)(2,1)}, bf16[4,256,256]{2,1,0:T(8,128)(2,1)S(1)}, u32[]{:S(2)}, u32[]{:S(2)}) collective-permute-start(bf16[4,256,256]{2,1,0:T(8,128)(2,1)} %amps_ref.5), channel_id=1, source_target_pairs={{0,1},{1,0},{2,3},{3,2},{4,5},{5,4},{6,7},{7,6},{8,9},{9,8},{10,11... | collective-permute-start | bytes 1572872 | tf_op jit(solution)/shard_map/ppermute | solution.py:76
  3.7 8.4 %collective-permute-start.2 = (bf16[528,128]{1,0:T(8,128)(2,1)}, bf16[528,128]{1,0:T(8,128)(2,1)S(1)}, u32[]{:S(2)}, u32[]{:S(2)}) collective-permute-start(bf16[528,128]{1,0:T(8,128)(2,1)} %get-tuple-element.28), channel_id=1, source_target_pairs={{0,7},{1,2},{2,1},{3,4},{4,3},{5,6},{6,5},{7,0},{8,15},{9,10},{10,... | collective-permute-start | bytes 405512 | tf_op jit(solution)/shard_map/ppermute | solution.py:79
  8.5 7.4 %collective-permute-start.3 = (bf16[512,128]{1,0:T(8,128)(2,1)}, bf16[512,128]{1,0:T(8,128)(2,1)S(1)}, u32[]{:S(2)}, u32[]{:S(2)}) collective-permute-start(bf16[512,128]{1,0:T(8,128)(2,1)} %get-tuple-element.29), channel_id=1, source_target_pairs={{0,7},{1,2},{2,1},{3,4},{4,3},{5,6},{6,5},{7,0},{8,15},{9,10},{10,... | collective-permute-start | bytes 393224 | tf_op jit(solution)/shard_map/ppermute | solution.py:79
  8.6 0.7 %copy-start.2 = (f32[8,128]{1,0:T(8,128)S(1)}, f32[8,128]{1,0:T(8,128)}, u32[]{:S(2)}) copy-start(f32[8,128]{1,0:T(8,128)} %get-tuple-element.27.after_ref.nums) | copy-start | bytes 12292
  10.8 7.0 %copy-start = (bf16[4,512,256]{2,1,0:T(8,128)(2,1)S(1)}, bf16[4,512,256]{2,1,0:T(8,128)(2,1)}, u32[]{:S(2)}) copy-start(bf16[4,512,256]{2,1,0:T(8,128)(2,1)} %coeff_ref.11) | copy-start | bytes 3145732
  10.8 7.0 %copy-start.1 = (bf16[4,256,256]{2,1,0:T(8,128)(2,1)S(1)}, bf16[4,256,256]{2,1,0:T(8,128)(2,1)}, u32[]{:S(2)}) copy-start(bf16[4,256,256]{2,1,0:T(8,128)(2,1)} %amps_ref.5) | copy-start | bytes 1572868
  12.7 8.4 %copy-start.6 = (bf16[528,128]{1,0:T(8,128)(2,1)S(1)}, bf16[528,128]{1,0:T(8,128)(2,1)}, u32[]{:S(2)}) copy-start(bf16[528,128]{1,0:T(8,128)(2,1)} %get-tuple-element.28) | copy-start | bytes 405508
  12.7 9.7 %copy-start.3 = (f32[8,128]{1,0:T(8,128)S(1)}, f32[8,128]{1,0:T(8,128)}, u32[]{:S(2)}) copy-start(f32[8,128]{1,0:T(8,128)} %get-tuple-element.27.after_ref.nums) | copy-start | bytes 12292
  12.7 19.1 %collective-permute-start.5 = (bf16[1040,128]{1,0:T(8,128)(2,1)S(1)}, bf16[1040,128]{1,0:T(8,128)(2,1)S(1)}, u32[]{:S(2)}, u32[]{:S(2)}) collective-permute-start(bf16[1040,128]{1,0:T(8,128)(2,1)S(1)} %shard_map.115.after_ref), channel_id=1, source_target_pairs={{0,7},{1,2},{2,1},{3,4},{4,3},{5,6},{6,5},{7,0},{8,15},{9,10},{10,... | collective-permute-start | bytes 798728 | tf_op jit(solution)/shard_map/ppermute | solution.py:79
  16.4 15.4 %collective-permute-start.6 = (bf16[1024,128]{1,0:T(8,128)(2,1)S(1)}, bf16[1024,128]{1,0:T(8,128)(2,1)S(1)}, u32[]{:S(2)}, u32[]{:S(2)}) collective-permute-start(bf16[1024,128]{1,0:T(8,128)(2,1)S(1)} %shard_map.116.after_ref), channel_id=1, source_target_pairs={{0,7},{1,2},{2,1},{3,4},{4,3},{5,6},{6,5},{7,0},{8,15},{9,10},{10,... | collective-permute-start | bytes 786440 | tf_op jit(solution)/shard_map/ppermute | solution.py:79
  18.7 5.7 %copy-start.4 = (f32[4,256]{1,0:T(4,128)S(1)}, f32[4,256]{1,0:T(4,128)}, u32[]{:S(2)}) copy-start(f32[4,256]{1,0:T(4,128)} %eps_ref.1) | copy-start | bytes 12292
  18.8 13.1 %collective-permute-start.7 = (bf16[272,256]{1,0:T(8,128)(2,1)S(1)}, bf16[272,256]{1,0:T(8,128)(2,1)S(1)}, u32[]{:S(2)}, u32[]{:S(2)}) collective-permute-start(bf16[272,256]{1,0:T(8,128)(2,1)S(1)} %get-tuple-element.30.after_ref), channel_id=1, source_target_pairs={{0,7},{1,2},{2,1},{3,4},{4,3},{5,6},{6,5},{7,0},{8,15},{9,10},{10,... | collective-permute-start | bytes 417800 | tf_op jit(solution)/shard_map/ppermute | solution.py:79
  21.0 1.4 %copy-start.5 = (bf16[2,1024,512]{2,1,0:T(8,128)(2,1)}, bf16[2,1024,512]{2,1,0:T(8,128)(2,1)S(1)}, u32[]{:S(2)}) copy-start(bf16[2,1024,512]{2,1,0:T(8,128)(2,1)S(1)} %collective-permute-done.4.three_in_ref) | copy-start | bytes 6291460
  21.0 4.9 %collective-permute-start.8 = (bf16[528,128]{1,0:T(8,128)(2,1)S(1)}, bf16[528,128]{1,0:T(8,128)(2,1)S(1)}, u32[]{:S(2)}, u32[]{:S(2)}) collective-permute-start(bf16[528,128]{1,0:T(8,128)(2,1)S(1)} %copy-done.6), channel_id=1, source_target_pairs={{0,1},{1,0},{2,3},{3,2},{4,5},{5,4},{6,7},{7,6},{8,9},{9,8},{10,11... | collective-permute-start | bytes 405512 | tf_op jit(solution)/shard_map/ppermute | solution.py:76
  24.2 15.6 %collective-permute-start.12 = (bf16[512,256]{1,0:T(8,128)(2,1)S(1)}, bf16[512,256]{1,0:T(8,128)(2,1)S(1)}, u32[]{:S(2)}, u32[]{:S(2)}) collective-permute-start(bf16[512,256]{1,0:T(8,128)(2,1)S(1)} %get-tuple-element.44), channel_id=1, source_target_pairs={{0,7},{1,2},{2,1},{3,4},{4,3},{5,6},{6,5},{7,0},{8,15},{9,10},{10,... | collective-permute-start | bytes 786440 | tf_op jit(solution)/shard_map/ppermute | solution.py:79
  32.4 7.4 %collective-permute-start.9 = (bf16[256,256]{1,0:T(8,128)(2,1)S(1)}, bf16[256,256]{1,0:T(8,128)(2,1)S(1)}, u32[]{:S(2)}, u32[]{:S(2)}) collective-permute-start(bf16[256,256]{1,0:T(8,128)(2,1)S(1)} %get-tuple-element.37.amp_ref.after_ref.refs_0_), channel_id=1, source_target_pairs={{0,8},{8,0},{16,24},{24,16},{1,9},{9,1},{17,25},{25,17},{2,10},{10... | collective-permute-start | bytes 393224 | tf_op jit(solution)/shard_map/ppermute | solution.py:82
  33.9 5.9 %collective-permute-start.10 = (bf16[256,256]{1,0:T(8,128)(2,1)S(1)}, bf16[256,256]{1,0:T(8,128)(2,1)S(1)}, u32[]{:S(2)}, u32[]{:S(2)}) collective-permute-start(bf16[256,256]{1,0:T(8,128)(2,1)S(1)} %get-tuple-element.37.amp_ref.after_ref.refs_0_), channel_id=1, source_target_pairs={{0,16},{8,24},{16,0},{24,8},{1,17},{9,25},{17,1},{25,9},{2,18},{10... | collective-permute-start | bytes 393224 | tf_op jit(solution)/shard_map/ppermute | solution.py:82
  35.4 5.9 %collective-permute-start.11 = (bf16[256,256]{1,0:T(8,128)(2,1)S(1)}, bf16[256,256]{1,0:T(8,128)(2,1)S(1)}, u32[]{:S(2)}, u32[]{:S(2)}) collective-permute-start(bf16[256,256]{1,0:T(8,128)(2,1)S(1)} %get-tuple-element.37.amp_ref.after_ref.refs_0_), channel_id=1, source_target_pairs={{0,24},{8,16},{16,8},{24,0},{1,25},{9,17},{17,9},{25,1},{2,26},{10... | collective-permute-start | bytes 393224 | tf_op jit(solution)/shard_map/ppermute | solution.py:82
  36.3 6.0 %collective-permute-start.16 = (bf16[272,256]{1,0:T(8,128)(2,1)S(1)}, bf16[272,256]{1,0:T(8,128)(2,1)S(1)}, u32[]{:S(2)}, u32[]{:S(2)}) collective-permute-start(bf16[272,256]{1,0:T(8,128)(2,1)S(1)} %get-tuple-element.49.held_ref), channel_id=1, source_target_pairs={{0,8},{1,9},{2,10},{3,11},{4,12},{5,13},{6,14},{7,15}} | collective-permute-start | bytes 417800 | tf_op jit(solution)/shard_map/ppermute | solution.py:440
  41.3 7.6 %collective-permute-start.13 = (bf16[2,256,256]{2,1,0:T(8,128)(2,1)S(1)}, bf16[2,256,256]{2,1,0:T(8,128)(2,1)S(1)}, u32[]{:S(2)}, u32[]{:S(2)}) collective-permute-start(bf16[2,256,256]{2,1,0:T(8,128)(2,1)S(1)} %shard_map.124.refs_4_), channel_id=1, source_target_pairs={{0,7},{1,2},{2,1},{3,4},{4,3},{5,6},{6,5},{7,0},{8,15},{9,10},{10,... | collective-permute-start | bytes 786440 | tf_op jit(solution)/shard_map/ppermute | solution.py:79
  42.3 5.8 %collective-permute-start.17 = (bf16[272,256]{1,0:T(8,128)(2,1)S(1)}, bf16[272,256]{1,0:T(8,128)(2,1)S(1)}, u32[]{:S(2)}, u32[]{:S(2)}) collective-permute-start(bf16[272,256]{1,0:T(8,128)(2,1)S(1)} %shard_map.127), channel_id=1, source_target_pairs={{0,16},{8,24},{1,17},{9,25},{2,18},{10,26},{3,19},{11,27},{4,20},{... | collective-permute-start | bytes 417800 | tf_op jit(solution)/shard_map/ppermute | solution.py:440
  45.6 2.5 %collective-permute-start.14 = (bf16[256,256]{1,0:T(8,128)(2,1)S(1)}, bf16[256,256]{1,0:T(8,128)(2,1)S(1)}, u32[]{:S(2)}, u32[]{:S(2)}) collective-permute-start(bf16[256,256]{1,0:T(8,128)(2,1)S(1)} %get-tuple-element.45.refs_4_.after_ref), channel_id=1, source_target_pairs={{0,1},{1,0},{2,3},{3,2},{4,5},{5,4},{6,7},{7,6},{8,9},{9,8},{10,11... | collective-permute-start | bytes 393224 | tf_op jit(solution)/shard_map/ppermute | solution.py:76
  45.7 2.5 %collective-permute-start.15 = (bf16[256,256]{1,0:T(8,128)(2,1)S(1)}, bf16[256,256]{1,0:T(8,128)(2,1)S(1)}, u32[]{:S(2)}, u32[]{:S(2)}) collective-permute-start(bf16[256,256]{1,0:T(8,128)(2,1)S(1)} %get-tuple-element.48), channel_id=1, source_target_pairs={{0,1},{1,0},{2,3},{3,2},{4,5},{5,4},{6,7},{7,6},{8,9},{9,8},{10,11... | collective-permute-start | bytes 393224 | tf_op jit(solution)/shard_map/ppermute | solution.py:76

commit v19 on v18

--- a/solution.py
+++ b/solution.py
@@ -206,7 +206,7 @@
         ],
         vmem=60,
     )
-    low_out, high_out, low_in = outer(x_low), outer(x_high), inner(x_low)
+    low_out, low_in = outer(x_low), inner(x_low)
 
     def told_of(low_ref):
         rows = low_ref[pao:, :].astype(F32)
@@ -246,6 +246,9 @@
         scratch=[pltpu.SemaphoreType.DMA],
         vmem=50,
     )
+
+    x_high, _ = lax.optimization_barrier((x_high, blocks))
+    high_out = outer(x_high)
 
     def outer_low_body(three_ref, x_ref, y_ref):
         half_into(y_ref, three_ref, whole(told_of(x_ref)[0, place_at]), x_ref[:pao, :])

time: 49.4 us -> 50.6 us (1.024); the launches traced: 49.1 us -> 49.6 us
  starting transfers between devices: 24.2 us -> 27.5 us
  waiting for transfers between devices: 10.5 us -> 7.66 us
    ppermute x7, starting transfers between devices: 12.4 us -> 15.2 us  [outer(): return lax.ppermute(x, 'pairs', list(enumerate(outer_of)))]
    ppermute x7, waiting for transfers between devices: 7.94 us -> 6.23 us  [outer(): return lax.ppermute(x, 'pairs', list(enumerate(outer_of)))]
    ppermute x3, waiting for transfers between devices: 1.51 us -> 0.56 us  [swap(): return lax.ppermute(x, 'role', [(i, i ^ by) for i in range(roles)])]
    ppermute x2, starting transfers between devices: 6.62 us -> 7.17 us  [local(): lax.ppermute(held, 'role', [(i, i + step) for i in range(step)])]
    unnamed x14 -> x16, local copies, waits for them, and re-layouts: 1.98 us -> 1.98 us
  transfers between devices with their start and end apart: 18 -> 18, of which waited for: 6 -> 7; matrix products, arithmetic and copies ran while one was open for 0% -> 0% of each run, Pallas kernels for 23% -> 23%
where the time goes in v19:
time: 50.6 us; the launch traced here: 49.6 us
  starting transfers between devices  27.5 us (54%)
  Pallas kernels  11.6 us (23%)
  waiting for transfers between devices  7.66 us (15%)
  local copies, waits for them, and re-layouts  1.98 us (4%)
  between operations  0.88 us (2%)
    ppermute x7, starting transfers between devices, outer(): return lax.ppermute(x, 'pairs', list(enumerate(outer_of)))  15.2 us
    pallas_call x17, Pallas kernels, call(): pl.pallas_call(body, in_specs=ins, out_specs=[spec for spec, _, _ in outs...  11.6 us
    ppermute x2, starting transfers between devices, local(): lax.ppermute(held, 'role', [(i, i + step) for i in range(step)])  7.17 us
    ppermute x7, waiting for transfers between devices, outer(): return lax.ppermute(x, 'pairs', list(enumerate(outer_of)))  6.23 us
    ppermute x3, starting transfers between devices, swap(): return lax.ppermute(x, 'role', [(i, i ^ by) for i in range(roles)])  3.55 us
    unnamed x16, local copies, waits for them, and re-layouts  1.98 us
    ppermute x6, starting transfers between devices, inner(): return lax.ppermute(x, 'pairs', list(enumerate(inner_of)))  1.66 us
  transfers between devices with their start and end apart: 18, of which 7 were waited for; matrix products, arithmetic and copies ran while one was open for 0% of the time, Pallas kernels for 23%

profile of v19, /device:TPU:0, one launch (start us, length us, event | category | flops | bytes accessed | tf_op | source)
XLA Modules:
  0.0 49.6 jit_solution(2010346860166099954)
XLA Ops:
  0.6 0.5 %collective-permute-start.4 = (bf16[2,1024,512]{2,1,0:T(8,128)(2,1)}, bf16[2,1024,512]{2,1,0:T(8,128)(2,1)S(1)}, u32[]{:S(2)}, u32[]{:S(2)}) collective-permute-start(bf16[2,1024,512]{2,1,0:T(8,128)(2,1)} %three_ref.1), channel_id=1, source_target_pairs={{0,1},{1,0},{2,3},{3,2},{4,5},{5,4},{6,7},{7,6},{8,9},{9,8},{10,11... | collective-permute-start | bytes 6291464 | tf_op jit(solution)/shard_map/ppermute | solution.py:76
  1.1 0.1 collective-permute-start
  1.2 0.4 collective-permute-start.1
  1.7 2.0 %shard_map.113 = (bf16[528,128]{1,0:T(8,128)(2,1)}, bf16[512,128]{1,0:T(8,128)(2,1)}, f32[8,128]{1,0:T(8,128)}) custom-call(s32[4]{0:T(128)} %owner_hbm.1, s32[2,4]{1,0:T(2,128)} %bitcast.1, s32[4,8]{1,0:T(4,128)} %partner_hbm.1, f32[4,8]{1,0:T(4,128)} %coupling_hbm.1, f32[16]{0:T(128)} %eps_hbm.1, s32[4]{0:T(128)} %nvirt_hbm.1, bf16[4,512,256]{2,1,0:T(8,128)(2,1)} %coeff_ref.11), custom_call_target="tpu_custom_call" | custom-call | flops 1 | bytes 1 | tf_op jit(solution)/shard_map/pallas_call | solution.py:37
  3.7 4.8 %collective-permute-start.2 = (bf16[528,128]{1,0:T(8,128)(2,1)}, bf16[528,128]{1,0:T(8,128)(2,1)S(1)}, u32[]{:S(2)}, u32[]{:S(2)}) collective-permute-start(bf16[528,128]{1,0:T(8,128)(2,1)} %get-tuple-element.29), channel_id=1, source_target_pairs={{0,7},{1,2},{2,1},{3,4},{4,3},{5,6},{6,5},{7,0},{8,15},{9,10},{10,... | collective-permute-start | bytes 405512 | tf_op jit(solution)/shard_map/ppermute | solution.py:79
  8.5 0.0 copy-start.2
  8.5 0.7 %copy-done.2 = f32[8,128]{1,0:T(8,128)S(1)} copy-done((f32[8,128]{1,0:T(8,128)S(1)}, f32[8,128]{1,0:T(8,128)}, u32[]{:S(2)}) %copy-start.2) | copy-done | bytes 4120
  9.2 0.0 copy-start.7
  9.2 1.6 %shard_map.114.three_ref = bf16[2,1024,512]{2,1,0:T(8,128)(2,1)S(1)} custom-call(bf16[2,1024,512]{2,1,0:T(8,128)(2,1)} %three_ref.1, f32[8,128]{1,0:T(8,128)S(1)} %copy-done.2), custom_call_target="tpu_custom_call" | custom-call | flops 1 | bytes 1 | tf_op jit(solution)/shard_map/pallas_call | solution.py:37
  10.8 0.0 copy-done.7
  10.8 0.0 copy-start
  10.8 0.0 copy-start.1
  10.8 0.1 collective-permute-start.3
  10.9 1.4 %collective-permute-done.2.x_ref.low_ref = bf16[528,128]{1,0:T(8,128)(2,1)S(1)} collective-permute-done((bf16[528,128]{1,0:T(8,128)(2,1)}, bf16[528,128]{1,0:T(8,128)(2,1)S(1)}, u32[]{:S(2)}, u32[]{:S(2)}) %collective-permute-start.2) | collective-permute-done | bytes 135200 | tf_op jit(solution)/shard_map/ppermute | solution.py:79
  12.3 0.5 %shard_map.115.after_ref = bf16[1040,128]{1,0:T(8,128)(2,1)S(1)} custom-call(bf16[2,1024,512]{2,1,0:T(8,128)(2,1)S(1)} %shard_map.114.three_ref, bf16[528,128]{1,0:T(8,128)(2,1)S(1)} %collective-permute-done.2.x_ref.low_ref), custom_call_target="tpu_custom_call" | custom-call | flops 1 | bytes 1 | tf_op jit(solution)/shard_map/pallas_call | solution.py:37
  12.8 0.0 copy-start.6
  12.8 0.0 copy-start.3
  12.9 3.8 %collective-permute-start.5 = (bf16[1040,128]{1,0:T(8,128)(2,1)S(1)}, bf16[1040,128]{1,0:T(8,128)(2,1)S(1)}, u32[]{:S(2)}, u32[]{:S(2)}) collective-permute-start(bf16[1040,128]{1,0:T(8,128)(2,1)S(1)} %shard_map.115.after_ref), channel_id=1, source_target_pairs={{0,7},{1,2},{2,1},{3,4},{4,3},{5,6},{6,5},{7,0},{8,15},{9,10},{10,... | collective-permute-start | bytes 798728 | tf_op jit(solution)/shard_map/ppermute | solution.py:79
  16.7 0.8 %collective-permute-done.3.x_ref.high_ref = bf16[512,128]{1,0:T(8,128)(2,1)S(1)} collective-permute-done((bf16[512,128]{1,0:T(8,128)(2,1)S(1)}, bf16[512,128]{1,0:T(8,128)(2,1)S(1)}, u32[]{:S(2)}, u32[]{:S(2)}) %collective-permute-start.3) | collective-permute-done | bytes 131104 | tf_op jit(solution)/shard_map/ppermute | solution.py:79
  17.5 0.5 %shard_map.116.after_ref = bf16[1024,128]{1,0:T(8,128)(2,1)S(1)} custom-call(bf16[2,1024,512]{2,1,0:T(8,128)(2,1)S(1)} %shard_map.114.three_ref, bf16[528,128]{1,0:T(8,128)(2,1)S(1)} %collective-permute-done.2.x_ref.low_ref, bf16[512,128]{1,0:T(8,128)(2,1)S(1)} %collective-permute-done.3.x_ref.high_ref, bf16[1040,128]{1,0:T(8,128)(2,1)S(1)} %shard_map.115.after_ref), custom_call_target="tpu_custom_call" | custom-call | flops 1 | bytes 1 | tf_op jit(solution)/shard_map/pallas_call | solution.py:37
  18.0 1.3 %collective-permute-start.6 = (bf16[1024,128]{1,0:T(8,128)(2,1)S(1)}, bf16[1024,128]{1,0:T(8,128)(2,1)S(1)}, u32[]{:S(2)}, u32[]{:S(2)}) collective-permute-start(bf16[1024,128]{1,0:T(8,128)(2,1)S(1)} %shard_map.116.after_ref), channel_id=1, source_target_pairs={{0,7},{1,2},{2,1},{3,4},{4,3},{5,6},{6,5},{7,0},{8,15},{9,10},{10,... | collective-permute-start | bytes 786440 | tf_op jit(solution)/shard_map/ppermute | solution.py:79
  19.3 0.0 copy-done
  19.3 0.0 copy-done.1
  19.3 0.9 %shard_map.117 = (bf16[4,256,256]{2,1,0:T(8,128)(2,1)S(1)}, bf16[272,256]{1,0:T(8,128)(2,1)S(1)}) custom-call(bf16[4,512,256]{2,1,0:T(8,128)(2,1)S(1)} %copy-done, bf16[4,256,256]{2,1,0:T(8,128)(2,1)S(1)} %copy-done.1, bf16[528,128]{1,0:T(8,128)(2,1)S(1)} %collective-permute-done.2.x_ref.low_ref, bf16[512,128]{1,0:T(8,128)(2,1)S(1)} %collective-permute-done.3.x_ref.high_ref, ...), custom_call_target="tpu_custom_call" | custom-call | flops 1 | bytes 1 | tf_op jit(solution)/shard_map/pallas_call | solution.py:37
  20.2 0.0 collective-permute-done.1.amps_in_ref
  20.2 0.0 copy-start.4
  20.2 2.4 %collective-permute-start.7 = (bf16[272,256]{1,0:T(8,128)(2,1)S(1)}, bf16[272,256]{1,0:T(8,128)(2,1)S(1)}, u32[]{:S(2)}, u32[]{:S(2)}) collective-permute-start(bf16[272,256]{1,0:T(8,128)(2,1)S(1)} %get-tuple-element.32.after_ref), channel_id=1, source_target_pairs={{0,7},{1,2},{2,1},{3,4},{4,3},{5,6},{6,5},{7,0},{8,15},{9,10},{10,... | collective-permute-start | bytes 417800 | tf_op jit(solution)/shard_map/ppermute | solution.py:79
  22.6 0.0 collective-permute-done.4.three_in_ref
  22.6 0.0 copy-done.6
  22.6 0.0 copy-start.5
  22.6 0.1 collective-permute-start.8
  22.7 1.3 %copy-done.5 = bf16[2,1024,512]{2,1,0:T(8,128)(2,1)} copy-done((bf16[2,1024,512]{2,1,0:T(8,128)(2,1)}, bf16[2,1024,512]{2,1,0:T(8,128)(2,1)S(1)}, u32[]{:S(2)}) %copy-start.5) | copy-done | bytes 2097176
  23.9 0.0 copy-done.3
  23.9 1.8 %shard_map.119 = (bf16[256,1024]{1,0:T(8,128)(2,1)S(1)}, bf16[1024,256]{1,0:T(8,128)(2,1)S(1)}, bf16[512,256]{1,0:T(8,128)(2,1)S(1)}) custom-call(f32[8,128]{1,0:T(8,128)S(1)} %copy-done.3, bf16[2,1024,512]{2,1,0:T(8,128)(2,1)S(1)} %shard_map.114.three_ref, bf16[2,1024,512]{2,1,0:T(8,128)(2,1)} %copy-done.5, bf16[4,512,256]{2,1,0:T(8,128)(2,1)S(1)} %copy-done, ...), custom_call_target="tpu_custom_call" | custom-call | flops 1 | bytes 1 | tf_op jit(solution)/shard_map/pallas_call | solution.py:37
  25.7 0.0 collective-permute-done.coeff_in_ref.in_ref
  25.7 1.3 %collective-permute-start.12 = (bf16[512,256]{1,0:T(8,128)(2,1)S(1)}, bf16[512,256]{1,0:T(8,128)(2,1)S(1)}, u32[]{:S(2)}, u32[]{:S(2)}) collective-permute-start(bf16[512,256]{1,0:T(8,128)(2,1)S(1)} %get-tuple-element.46), channel_id=1, source_target_pairs={{0,7},{1,2},{2,1},{3,4},{4,3},{5,6},{6,5},{7,0},{8,15},{9,10},{10,... | collective-permute-start | bytes 786440 | tf_op jit(solution)/shard_map/ppermute | solution.py:79
  27.0 0.0 copy-done.4
  27.1 1.5 %shard_map.118 = (bf16[4,256,256]{2,1,0:T(8,128)(2,1)S(1)}, f32[256,256]{1,0:T(8,128)S(1)}, f32[256,256]{1,0:T(8,128)S(1)}, f32[256,256]{1,0:T(8,128)S(1)}) custom-call(f32[8,128]{1,0:T(8,128)S(1)} %copy-done.3, bf16[4,512,256]{2,1,0:T(8,128)(2,1)S(1)} %copy-done, bf16[4,512,256]{2,1,0:T(8,128)(2,1)S(1)} %collective-permute-done.coeff_in_ref.in_ref, ...), custom_call_target="tpu_custom_call" | custom-call | flops 1 | bytes 1 | tf_op jit(solution)/shard_map/pallas_call | solution.py:37
  28.5 0.0 collective-permute-done.8.low_ref
  28.6 3.7 %collective-permute-done.7.co_ref = bf16[272,256]{1,0:T(8,128)(2,1)S(1)} collective-permute-done((bf16[272,256]{1,0:T(8,128)(2,1)S(1)}, bf16[272,256]{1,0:T(8,128)(2,1)S(1)}, u32[]{:S(2)}, u32[]{:S(2)}) %collective-permute-start.7) | collective-permute-done | bytes 139296 | tf_op jit(solution)/shard_map/ppermute | solution.py:79
  32.2 0.0 collective-permute-done.6.high_ref
  32.2 0.0 collective-permute-done.5.low_ref
  32.2 0.5 %shard_map.121 = (bf16[256,256]{1,0:T(8,128)(2,1)S(1)}, f32[256,256]{1,0:T(8,128)S(1)}) custom-call(f32[8,128]{1,0:T(8,128)S(1)} %copy-done.3, bf16[256,1024]{1,0:T(8,128)(2,1)S(1)} %get-tuple-element.35.first_ref, bf16[1024,256]{1,0:T(8,128)(2,1)S(1)} %get-tuple-element.36.second_ref, bf16[1040,128]{1,0:T(8,128)(2,1)S(1)} %collective-permute-done.5.low_ref, ...), custom_call_target="tpu_custom_call" | custom-call | flops 1 | bytes 1 | tf_op jit(solution)/shard_map/pallas_call | solution.py:37
  32.8 1.9 %collective-permute-start.10 = (bf16[256,256]{1,0:T(8,128)(2,1)S(1)}, bf16[256,256]{1,0:T(8,128)(2,1)S(1)}, u32[]{:S(2)}, u32[]{:S(2)}) collective-permute-start(bf16[256,256]{1,0:T(8,128)(2,1)S(1)} %get-tuple-element.39.amp_ref.after_ref.refs_0_), channel_id=1, source_target_pairs={{0,16},{8,24},{16,0},{24,8},{1,17},{9,25},{17,1},{25,9},{2,18},{10... | collective-permute-start | bytes 393224 | tf_op jit(solution)/shard_map/ppermute | solution.py:82
  34.7 1.6 %collective-permute-start.11 = (bf16[256,256]{1,0:T(8,128)(2,1)S(1)}, bf16[256,256]{1,0:T(8,128)(2,1)S(1)}, u32[]{:S(2)}, u32[]{:S(2)}) collective-permute-start(bf16[256,256]{1,0:T(8,128)(2,1)S(1)} %get-tuple-element.39.amp_ref.after_ref.refs_0_), channel_id=1, source_target_pairs={{0,24},{8,16},{16,8},{24,0},{1,25},{9,17},{17,9},{25,1},{2,26},{10... | collective-permute-start | bytes 393224 | tf_op jit(solution)/shard_map/ppermute | solution.py:82
  36.2 0.1 collective-permute-start.9
  36.4 0.4 shard_map.122
  36.8 3.8 %collective-permute-start.16 = (bf16[272,256]{1,0:T(8,128)(2,1)S(1)}, bf16[272,256]{1,0:T(8,128)(2,1)S(1)}, u32[]{:S(2)}, u32[]{:S(2)}) collective-permute-start(bf16[272,256]{1,0:T(8,128)(2,1)S(1)} %get-tuple-element.51.held_ref), channel_id=1, source_target_pairs={{0,8},{1,9},{2,10},{3,11},{4,12},{5,13},{6,14},{7,15}} | collective-permute-start | bytes 417800 | tf_op jit(solution)/shard_map/ppermute | solution.py:443
  40.6 0.0 collective-permute-done.12.x_ref
  40.6 0.0 collective-permute-done.10.refs_2_
  40.6 0.0 collective-permute-done.11.refs_3_
  40.7 0.6 %collective-permute-done.9.refs_1_ = bf16[256,256]{1,0:T(8,128)(2,1)S(1)} collective-permute-done((bf16[256,256]{1,0:T(8,128)(2,1)S(1)}, bf16[256,256]{1,0:T(8,128)(2,1)S(1)}, u32[]{:S(2)}, u32[]{:S(2)}) %collective-permute-start.9) | collective-permute-done | bytes 131104 | tf_op jit(solution)/shard_map/ppermute | solution.py:82
  41.2 1.5 %collective-permute-start.13 = (bf16[2,256,256]{2,1,0:T(8,128)(2,1)S(1)}, bf16[2,256,256]{2,1,0:T(8,128)(2,1)S(1)}, u32[]{:S(2)}, u32[]{:S(2)}) collective-permute-start(bf16[2,256,256]{2,1,0:T(8,128)(2,1)S(1)} %shard_map.124.refs_4_), channel_id=1, source_target_pairs={{0,7},{1,2},{2,1},{3,4},{4,3},{5,6},{6,5},{7,0},{8,15},{9,10},{10,... | collective-permute-start | bytes 786440 | tf_op jit(solution)/shard_map/ppermute | solution.py:79
  42.7 0.4 collective-permute-done.16.come_ref.refs_0_
  43.2 3.3 %collective-permute-start.17 = (bf16[272,256]{1,0:T(8,128)(2,1)S(1)}, bf16[272,256]{1,0:T(8,128)(2,1)S(1)}, u32[]{:S(2)}, u32[]{:S(2)}) collective-permute-start(bf16[272,256]{1,0:T(8,128)(2,1)S(1)} %shard_map.127), channel_id=1, source_target_pairs={{0,16},{8,24},{1,17},{9,25},{2,18},{10,26},{3,19},{11,27},{4,20},{... | collective-permute-start | bytes 417800 | tf_op jit(solution)/shard_map/ppermute | solution.py:443
  46.6 0.1 collective-permute-start.14
  46.6 0.5 %collective-permute-start.15 = (bf16[256,256]{1,0:T(8,128)(2,1)S(1)}, bf16[256,256]{1,0:T(8,128)(2,1)S(1)}, u32[]{:S(2)}, u32[]{:S(2)}) collective-permute-start(bf16[256,256]{1,0:T(8,128)(2,1)S(1)} %get-tuple-element.50), channel_id=1, source_target_pairs={{0,1},{1,0},{2,3},{3,2},{4,5},{5,4},{6,7},{7,6},{8,9},{9,8},{10,11... | collective-permute-start | bytes 393224 | tf_op jit(solution)/shard_map/ppermute | solution.py:76
  47.1 1.5 %shard_map.128 = (bf16[2,256,256]{2,1,0:T(8,128)(2,1)}, bf16[2,512,256]{2,1,0:T(8,128)(2,1)}) custom-call(f32[8,128]{1,0:T(8,128)S(1)} %copy-done.3, bf16[256,256]{1,0:T(8,128)(2,1)S(1)} %get-tuple-element.47.refs_4_.after_ref), custom_call_target="tpu_custom_call" | custom-call | flops 1 | bytes 1 | tf_op jit(solution)/shard_map/pallas_call | solution.py:37
  48.7 0.4 collective-permute-done.17.refs_1_
  49.1 0.0 collective-permute-done.14.ci_ref
  49.1 0.0 collective-permute-done.15.cei_ref
  49.1 0.3 collective-permute-done.13.co_ref
  49.5 0.2 shard_map.129
  (6 shorter events, 0.1 us)
Async XLA Ops:
  0.6 22.0 %collective-permute-start.4 = (bf16[2,1024,512]{2,1,0:T(8,128)(2,1)}, bf16[2,1024,512]{2,1,0:T(8,128)(2,1)S(1)}, u32[]{:S(2)}, u32[]{:S(2)}) collective-permute-start(bf16[2,1024,512]{2,1,0:T(8,128)(2,1)} %three_ref.1), channel_id=1, source_target_pairs={{0,1},{1,0},{2,3},{3,2},{4,5},{5,4},{6,7},{7,6},{8,9},{9,8},{10,11... | collective-permute-start | bytes 6291464 | tf_op jit(solution)/shard_map/ppermute | solution.py:76
  1.1 24.6 %collective-permute-start = (bf16[4,512,256]{2,1,0:T(8,128)(2,1)}, bf16[4,512,256]{2,1,0:T(8,128)(2,1)S(1)}, u32[]{:S(2)}, u32[]{:S(2)}) collective-permute-start(bf16[4,512,256]{2,1,0:T(8,128)(2,1)} %coeff_ref.11), channel_id=1, source_target_pairs={{0,1},{1,0},{2,3},{3,2},{4,5},{5,4},{6,7},{7,6},{8,9},{9,8},{10,11... | collective-permute-start | bytes 3145736 | tf_op jit(solution)/shard_map/ppermute | solution.py:76
  1.2 19.0 %collective-permute-start.1 = (bf16[4,256,256]{2,1,0:T(8,128)(2,1)}, bf16[4,256,256]{2,1,0:T(8,128)(2,1)S(1)}, u32[]{:S(2)}, u32[]{:S(2)}) collective-permute-start(bf16[4,256,256]{2,1,0:T(8,128)(2,1)} %amps_ref.5), channel_id=1, source_target_pairs={{0,1},{1,0},{2,3},{3,2},{4,5},{5,4},{6,7},{7,6},{8,9},{9,8},{10,11... | collective-permute-start | bytes 1572872 | tf_op jit(solution)/shard_map/ppermute | solution.py:76
  3.7 8.6 %collective-permute-start.2 = (bf16[528,128]{1,0:T(8,128)(2,1)}, bf16[528,128]{1,0:T(8,128)(2,1)S(1)}, u32[]{:S(2)}, u32[]{:S(2)}) collective-permute-start(bf16[528,128]{1,0:T(8,128)(2,1)} %get-tuple-element.29), channel_id=1, source_target_pairs={{0,7},{1,2},{2,1},{3,4},{4,3},{5,6},{6,5},{7,0},{8,15},{9,10},{10,... | collective-permute-start | bytes 405512 | tf_op jit(solution)/shard_map/ppermute | solution.py:79
  8.5 0.7 %copy-start.2 = (f32[8,128]{1,0:T(8,128)S(1)}, f32[8,128]{1,0:T(8,128)}, u32[]{:S(2)}) copy-start(f32[8,128]{1,0:T(8,128)} %get-tuple-element.28.after_ref.nums) | copy-start | bytes 12292
  9.2 1.6 %copy-start.7 = (bf16[512,128]{1,0:T(8,128)(2,1)S(1)}, bf16[512,128]{1,0:T(8,128)(2,1)}, u32[]{:S(2)}) copy-start(bf16[512,128]{1,0:T(8,128)(2,1)} %get-tuple-element.31) | copy-start | bytes 393220
  10.8 8.5 %copy-start = (bf16[4,512,256]{2,1,0:T(8,128)(2,1)S(1)}, bf16[4,512,256]{2,1,0:T(8,128)(2,1)}, u32[]{:S(2)}) copy-start(bf16[4,512,256]{2,1,0:T(8,128)(2,1)} %coeff_ref.11) | copy-start | bytes 3145732
  10.8 8.5 %copy-start.1 = (bf16[4,256,256]{2,1,0:T(8,128)(2,1)S(1)}, bf16[4,256,256]{2,1,0:T(8,128)(2,1)}, u32[]{:S(2)}) copy-start(bf16[4,256,256]{2,1,0:T(8,128)(2,1)} %amps_ref.5) | copy-start | bytes 1572868
  10.8 6.6 %collective-permute-start.3 = (bf16[512,128]{1,0:T(8,128)(2,1)S(1)}, bf16[512,128]{1,0:T(8,128)(2,1)S(1)}, u32[]{:S(2)}, u32[]{:S(2)}) collective-permute-start(bf16[512,128]{1,0:T(8,128)(2,1)S(1)} %copy-done.7), channel_id=1, source_target_pairs={{0,7},{1,2},{2,1},{3,4},{4,3},{5,6},{6,5},{7,0},{8,15},{9,10},{10,... | collective-permute-start | bytes 393224 | tf_op jit(solution)/shard_map/ppermute | solution.py:79
  12.8 9.7 %copy-start.6 = (bf16[528,128]{1,0:T(8,128)(2,1)S(1)}, bf16[528,128]{1,0:T(8,128)(2,1)}, u32[]{:S(2)}) copy-start(bf16[528,128]{1,0:T(8,128)(2,1)} %get-tuple-element.29) | copy-start | bytes 405508
  12.8 11.1 %copy-start.3 = (f32[8,128]{1,0:T(8,128)S(1)}, f32[8,128]{1,0:T(8,128)}, u32[]{:S(2)}) copy-start(f32[8,128]{1,0:T(8,128)} %get-tuple-element.28.after_ref.nums) | copy-start | bytes 12292
  12.9 19.4 %collective-permute-start.5 = (bf16[1040,128]{1,0:T(8,128)(2,1)S(1)}, bf16[1040,128]{1,0:T(8,128)(2,1)S(1)}, u32[]{:S(2)}, u32[]{:S(2)}) collective-permute-start(bf16[1040,128]{1,0:T(8,128)(2,1)S(1)} %shard_map.115.after_ref), channel_id=1, source_target_pairs={{0,7},{1,2},{2,1},{3,4},{4,3},{5,6},{6,5},{7,0},{8,15},{9,10},{10,... | collective-permute-start | bytes 798728 | tf_op jit(solution)/shard_map/ppermute | solution.py:79
  18.0 14.3 %collective-permute-start.6 = (bf16[1024,128]{1,0:T(8,128)(2,1)S(1)}, bf16[1024,128]{1,0:T(8,128)(2,1)S(1)}, u32[]{:S(2)}, u32[]{:S(2)}) collective-permute-start(bf16[1024,128]{1,0:T(8,128)(2,1)S(1)} %shard_map.116.after_ref), channel_id=1, source_target_pairs={{0,7},{1,2},{2,1},{3,4},{4,3},{5,6},{6,5},{7,0},{8,15},{9,10},{10,... | collective-permute-start | bytes 786440 | tf_op jit(solution)/shard_map/ppermute | solution.py:79
  20.2 6.9 %copy-start.4 = (f32[4,256]{1,0:T(4,128)S(1)}, f32[4,256]{1,0:T(4,128)}, u32[]{:S(2)}) copy-start(f32[4,256]{1,0:T(4,128)} %eps_ref.1) | copy-start | bytes 12292
  20.2 12.0 %collective-permute-start.7 = (bf16[272,256]{1,0:T(8,128)(2,1)S(1)}, bf16[272,256]{1,0:T(8,128)(2,1)S(1)}, u32[]{:S(2)}, u32[]{:S(2)}) collective-permute-start(bf16[272,256]{1,0:T(8,128)(2,1)S(1)} %get-tuple-element.32.after_ref), channel_id=1, source_target_pairs={{0,7},{1,2},{2,1},{3,4},{4,3},{5,6},{6,5},{7,0},{8,15},{9,10},{10,... | collective-permute-start | bytes 417800 | tf_op jit(solution)/shard_map/ppermute | solution.py:79
  22.6 1.3 %copy-start.5 = (bf16[2,1024,512]{2,1,0:T(8,128)(2,1)}, bf16[2,1024,512]{2,1,0:T(8,128)(2,1)S(1)}, u32[]{:S(2)}) copy-start(bf16[2,1024,512]{2,1,0:T(8,128)(2,1)S(1)} %collective-permute-done.4.three_in_ref) | copy-start | bytes 6291460
  22.6 5.9 %collective-permute-start.8 = (bf16[528,128]{1,0:T(8,128)(2,1)S(1)}, bf16[528,128]{1,0:T(8,128)(2,1)S(1)}, u32[]{:S(2)}, u32[]{:S(2)}) collective-permute-start(bf16[528,128]{1,0:T(8,128)(2,1)S(1)} %copy-done.6), channel_id=1, source_target_pairs={{0,1},{1,0},{2,3},{3,2},{4,5},{5,4},{6,7},{7,6},{8,9},{9,8},{10,11... | collective-permute-start | bytes 405512 | tf_op jit(solution)/shard_map/ppermute | solution.py:76
  25.7 14.9 %collective-permute-start.12 = (bf16[512,256]{1,0:T(8,128)(2,1)S(1)}, bf16[512,256]{1,0:T(8,128)(2,1)S(1)}, u32[]{:S(2)}, u32[]{:S(2)}) collective-permute-start(bf16[512,256]{1,0:T(8,128)(2,1)S(1)} %get-tuple-element.46), channel_id=1, source_target_pairs={{0,7},{1,2},{2,1},{3,4},{4,3},{5,6},{6,5},{7,0},{8,15},{9,10},{10,... | collective-permute-start | bytes 786440 | tf_op jit(solution)/shard_map/ppermute | solution.py:79
  32.8 7.8 %collective-permute-start.10 = (bf16[256,256]{1,0:T(8,128)(2,1)S(1)}, bf16[256,256]{1,0:T(8,128)(2,1)S(1)}, u32[]{:S(2)}, u32[]{:S(2)}) collective-permute-start(bf16[256,256]{1,0:T(8,128)(2,1)S(1)} %get-tuple-element.39.amp_ref.after_ref.refs_0_), channel_id=1, source_target_pairs={{0,16},{8,24},{16,0},{24,8},{1,17},{9,25},{17,1},{25,9},{2,18},{10... | collective-permute-start | bytes 393224 | tf_op jit(solution)/shard_map/ppermute | solution.py:82
  34.7 6.0 %collective-permute-start.11 = (bf16[256,256]{1,0:T(8,128)(2,1)S(1)}, bf16[256,256]{1,0:T(8,128)(2,1)S(1)}, u32[]{:S(2)}, u32[]{:S(2)}) collective-permute-start(bf16[256,256]{1,0:T(8,128)(2,1)S(1)} %get-tuple-element.39.amp_ref.after_ref.refs_0_), channel_id=1, source_target_pairs={{0,24},{8,16},{16,8},{24,0},{1,25},{9,17},{17,9},{25,1},{2,26},{10... | collective-permute-start | bytes 393224 | tf_op jit(solution)/shard_map/ppermute | solution.py:82
  36.2 5.0 %collective-permute-start.9 = (bf16[256,256]{1,0:T(8,128)(2,1)S(1)}, bf16[256,256]{1,0:T(8,128)(2,1)S(1)}, u32[]{:S(2)}, u32[]{:S(2)}) collective-permute-start(bf16[256,256]{1,0:T(8,128)(2,1)S(1)} %get-tuple-element.39.amp_ref.after_ref.refs_0_), channel_id=1, source_target_pairs={{0,8},{8,0},{16,24},{24,16},{1,9},{9,1},{17,25},{25,17},{2,10},{10... | collective-permute-start | bytes 393224 | tf_op jit(solution)/shard_map/ppermute | solution.py:82
  36.8 6.4 %collective-permute-start.16 = (bf16[272,256]{1,0:T(8,128)(2,1)S(1)}, bf16[272,256]{1,0:T(8,128)(2,1)S(1)}, u32[]{:S(2)}, u32[]{:S(2)}) collective-permute-start(bf16[272,256]{1,0:T(8,128)(2,1)S(1)} %get-tuple-element.51.held_ref), channel_id=1, source_target_pairs={{0,8},{1,9},{2,10},{3,11},{4,12},{5,13},{6,14},{7,15}} | collective-permute-start | bytes 417800 | tf_op jit(solution)/shard_map/ppermute | solution.py:443
  41.2 8.3 %collective-permute-start.13 = (bf16[2,256,256]{2,1,0:T(8,128)(2,1)S(1)}, bf16[2,256,256]{2,1,0:T(8,128)(2,1)S(1)}, u32[]{:S(2)}, u32[]{:S(2)}) collective-permute-start(bf16[2,256,256]{2,1,0:T(8,128)(2,1)S(1)} %shard_map.124.refs_4_), channel_id=1, source_target_pairs={{0,7},{1,2},{2,1},{3,4},{4,3},{5,6},{6,5},{7,0},{8,15},{9,10},{10,... | collective-permute-start | bytes 786440 | tf_op jit(solution)/shard_map/ppermute | solution.py:79
  43.2 5.9 %collective-permute-start.17 = (bf16[272,256]{1,0:T(8,128)(2,1)S(1)}, bf16[272,256]{1,0:T(8,128)(2,1)S(1)}, u32[]{:S(2)}, u32[]{:S(2)}) collective-permute-start(bf16[272,256]{1,0:T(8,128)(2,1)S(1)} %shard_map.127), channel_id=1, source_target_pairs={{0,16},{8,24},{1,17},{9,25},{2,18},{10,26},{3,19},{11,27},{4,20},{... | collective-permute-start | bytes 417800 | tf_op jit(solution)/shard_map/ppermute | solution.py:443
  46.6 2.5 %collective-permute-start.14 = (bf16[256,256]{1,0:T(8,128)(2,1)S(1)}, bf16[256,256]{1,0:T(8,128)(2,1)S(1)}, u32[]{:S(2)}, u32[]{:S(2)}) collective-permute-start(bf16[256,256]{1,0:T(8,128)(2,1)S(1)} %get-tuple-element.47.refs_4_.after_ref), channel_id=1, source_target_pairs={{0,1},{1,0},{2,3},{3,2},{4,5},{5,4},{6,7},{7,6},{8,9},{9,8},{10,11... | collective-permute-start | bytes 393224 | tf_op jit(solution)/shard_map/ppermute | solution.py:76
  46.6 2.5 %collective-permute-start.15 = (bf16[256,256]{1,0:T(8,128)(2,1)S(1)}, bf16[256,256]{1,0:T(8,128)(2,1)S(1)}, u32[]{:S(2)}, u32[]{:S(2)}) collective-permute-start(bf16[256,256]{1,0:T(8,128)(2,1)S(1)} %get-tuple-element.50), channel_id=1, source_target_pairs={{0,1},{1,0},{2,3},{3,2},{4,5},{5,4},{6,7},{7,6},{8,9},{9,8},{10,11... | collective-permute-start | bytes 393224 | tf_op jit(solution)/shard_map/ppermute | solution.py:76

commit v20 on v18

--- a/solution.py
+++ b/solution.py
@@ -77,6 +77,14 @@
 
     def outer(x):
         return lax.ppermute(x, "pairs", list(enumerate(outer_of)))
+
+    def outer_for_owners(x):
+        pairings = [
+            (s * columns + i, s * columns + j)
+            for s in range(roles)
+            for i, j in enumerate(outer_of if s else inner_of)
+        ]
+        return lax.ppermute(x, ("role", "pairs"), pairings)
 
     def swap(x, by):
         return lax.ppermute(x, "role", [(i, i ^ by) for i in range(roles)])
@@ -326,7 +334,7 @@
         (nums, blocks, three_in, coeff, c_out),
         scratch=[pltpu.VMEM((1, aux, pao), BF16), pltpu.SemaphoreType.DMA],
     )
-    x_extra_out = outer(x_extra)
+    x_extra_out = outer_for_owners(x_extra)
 
     def own_body(
         nums, coeff_ref, coeff_in_ref, amps_ref, amps_in_ref, eps_ref, after_ref,
@@ -481,7 +489,7 @@
         [two_b],
         (nums, low_out, s_out, se_out, *amp_roles),
     )
-    cc_from_out = outer(cc_out)
+    cc_from_out = outer_for_owners(cc_out)
 
     def inner_again_body(nums, low_ref, s_ref, se_ref, *refs):
         amp_refs, c_refs = refs[:roles], refs[-2:]

time: 49.4 us -> 49.9 us (1.010)
  starting transfers between devices: 24.2 us -> 25.3 us
  waiting for transfers between devices: 10.5 us -> 9.47 us
    ppermute x7 -> x5, waiting for transfers between devices: 7.94 us -> 6.52 us  [outer(): return lax.ppermute(x, 'pairs', list(enumerate(outer_of)))]
    ppermute x2, starting transfers between devices: 6.62 us -> 7.81 us  [local(): lax.ppermute(held, 'role', [(i, i + step) for i in range(step)])]
    ppermute x7 -> x5, starting transfers between devices: 12.4 us -> 11.8 us  [outer(): return lax.ppermute(x, 'pairs', list(enumerate(outer_of)))]
    ppermute x2, waiting for transfers between devices: 1.01 us -> 1.54 us  [local(): lax.ppermute(held, 'role', [(i, i + step) for i in range(step)])]
  transfers between devices with their start and end apart: 18 -> 18, of which waited for: 6 -> 5; matrix products, arithmetic and copies ran while one was open for 0% -> 0% of each run, Pallas kernels for 23% -> 23%
where the time goes in v20:
time: 49.9 us; the launch traced here: 49.2 us
  starting transfers between devices  25.3 us (51%)
  Pallas kernels  11.5 us (23%)
  waiting for transfers between devices  9.47 us (19%)
  local copies, waits for them, and re-layouts  1.98 us (4%)
  between operations  0.89 us (2%)
    ppermute x5, starting transfers between devices, outer(): return lax.ppermute(x, 'pairs', list(enumerate(outer_of)))  11.8 us
    pallas_call x17, Pallas kernels, call(): pl.pallas_call(body, in_specs=ins, out_specs=[spec for spec, _, _ in outs...  11.5 us
    ppermute x2, starting transfers between devices, local(): lax.ppermute(held, 'role', [(i, i + step) for i in range(step)])  7.81 us
    ppermute x5, waiting for transfers between devices, outer(): return lax.ppermute(x, 'pairs', list(enumerate(outer_of)))  6.52 us
    ppermute x3, starting transfers between devices, swap(): return lax.ppermute(x, 'role', [(i, i ^ by) for i in range(roles)])  4 us
    unnamed x14, local copies, waits for them, and re-layouts  1.98 us
    ppermute x6, starting transfers between devices, inner(): return lax.ppermute(x, 'pairs', list(enumerate(inner_of)))  1.66 us
    ppermute x2, waiting for transfers between devices, local(): lax.ppermute(held, 'role', [(i, i + step) for i in range(step)])  1.54 us
  transfers between devices with their start and end apart: 18, of which 5 were waited for; matrix products, arithmetic and copies ran while one was open for 0% of the time, Pallas kernels for 23%

profile of v20, /device:TPU:0, one launch (start us, length us, event | category | flops | bytes accessed | tf_op | source)
XLA Modules:
  0.0 49.2 jit_solution(2514327854004167625)
XLA Ops:
  0.6 0.5 %collective-permute-start.4 = (bf16[2,1024,512]{2,1,0:T(8,128)(2,1)}, bf16[2,1024,512]{2,1,0:T(8,128)(2,1)S(1)}, u32[]{:S(2)}, u32[]{:S(2)}) collective-permute-start(bf16[2,1024,512]{2,1,0:T(8,128)(2,1)} %three_ref.1), channel_id=1, source_target_pairs={{0,1},{1,0},{2,3},{3,2},{4,5},{5,4},{6,7},{7,6},{8,9},{9,8},{10,11... | collective-permute-start | bytes 6291464 | tf_op jit(solution)/shard_map/ppermute | solution.py:76
  1.1 0.1 collective-permute-start
  1.2 0.4 collective-permute-start.1
  1.7 2.0 %shard_map.113 = (bf16[528,128]{1,0:T(8,128)(2,1)}, bf16[512,128]{1,0:T(8,128)(2,1)}, f32[8,128]{1,0:T(8,128)}) custom-call(s32[4]{0:T(128)} %owner_hbm.1, s32[2,4]{1,0:T(2,128)} %bitcast.1, s32[4,8]{1,0:T(4,128)} %partner_hbm.1, f32[4,8]{1,0:T(4,128)} %coupling_hbm.1, f32[16]{0:T(128)} %eps_hbm.1, s32[4]{0:T(128)} %nvirt_hbm.1, bf16[4,512,256]{2,1,0:T(8,128)(2,1)} %coeff_ref.11), custom_call_target="tpu_custom_call" | custom-call | flops 1 | bytes 1 | tf_op jit(solution)/shard_map/pallas_call | solution.py:37
  3.7 4.8 %collective-permute-start.2 = (bf16[528,128]{1,0:T(8,128)(2,1)}, bf16[528,128]{1,0:T(8,128)(2,1)S(1)}, u32[]{:S(2)}, u32[]{:S(2)}) collective-permute-start(bf16[528,128]{1,0:T(8,128)(2,1)} %get-tuple-element.28), channel_id=1, source_target_pairs={{0,7},{1,2},{2,1},{3,4},{4,3},{5,6},{6,5},{7,0},{8,15},{9,10},{10,... | collective-permute-start | bytes 405512 | tf_op jit(solution)/shard_map/ppermute | solution.py:79
  8.5 0.1 collective-permute-start.3
  8.6 0.0 copy-start.2
  8.6 0.7 %copy-done.2 = f32[8,128]{1,0:T(8,128)S(1)} copy-done((f32[8,128]{1,0:T(8,128)S(1)}, f32[8,128]{1,0:T(8,128)}, u32[]{:S(2)}) %copy-start.2) | copy-done | bytes 4120
  9.2 1.6 %shard_map.114.three_ref = bf16[2,1024,512]{2,1,0:T(8,128)(2,1)S(1)} custom-call(bf16[2,1024,512]{2,1,0:T(8,128)(2,1)} %three_ref.1, f32[8,128]{1,0:T(8,128)S(1)} %copy-done.2), custom_call_target="tpu_custom_call" | custom-call | flops 1 | bytes 1 | tf_op jit(solution)/shard_map/pallas_call | solution.py:37
  10.8 0.0 copy-start
  10.8 0.0 copy-start.1
  10.9 1.3 %collective-permute-done.2.x_ref.low_ref = bf16[528,128]{1,0:T(8,128)(2,1)S(1)} collective-permute-done((bf16[528,128]{1,0:T(8,128)(2,1)}, bf16[528,128]{1,0:T(8,128)(2,1)S(1)}, u32[]{:S(2)}, u32[]{:S(2)}) %collective-permute-start.2) | collective-permute-done | bytes 135200 | tf_op jit(solution)/shard_map/ppermute | solution.py:79
  12.1 0.5 %shard_map.115.after_ref = bf16[1040,128]{1,0:T(8,128)(2,1)S(1)} custom-call(bf16[2,1024,512]{2,1,0:T(8,128)(2,1)S(1)} %shard_map.114.three_ref, bf16[528,128]{1,0:T(8,128)(2,1)S(1)} %collective-permute-done.2.x_ref.low_ref), custom_call_target="tpu_custom_call" | custom-call | flops 1 | bytes 1 | tf_op jit(solution)/shard_map/pallas_call | solution.py:37
  12.7 0.0 copy-start.6
  12.7 0.0 copy-start.3
  12.7 3.2 %collective-permute-start.5 = (bf16[1040,128]{1,0:T(8,128)(2,1)S(1)}, bf16[1040,128]{1,0:T(8,128)(2,1)S(1)}, u32[]{:S(2)}, u32[]{:S(2)}) collective-permute-start(bf16[1040,128]{1,0:T(8,128)(2,1)S(1)} %shard_map.115.after_ref), channel_id=1, source_target_pairs={{0,7},{1,2},{2,1},{3,4},{4,3},{5,6},{6,5},{7,0},{8,15},{9,10},{10,... | collective-permute-start | bytes 798728 | tf_op jit(solution)/shard_map/ppermute | solution.py:79
  15.9 0.0 collective-permute-done.3.x_ref.high_ref
  15.9 0.5 %shard_map.116.after_ref = bf16[1024,128]{1,0:T(8,128)(2,1)S(1)} custom-call(bf16[2,1024,512]{2,1,0:T(8,128)(2,1)S(1)} %shard_map.114.three_ref, bf16[528,128]{1,0:T(8,128)(2,1)S(1)} %collective-permute-done.2.x_ref.low_ref, bf16[512,128]{1,0:T(8,128)(2,1)S(1)} %collective-permute-done.3.x_ref.high_ref, bf16[1040,128]{1,0:T(8,128)(2,1)S(1)} %shard_map.115.after_ref), custom_call_target="tpu_custom_call" | custom-call | flops 1 | bytes 1 | tf_op jit(solution)/shard_map/pallas_call | solution.py:37
  16.4 1.4 %collective-permute-start.6 = (bf16[1024,128]{1,0:T(8,128)(2,1)S(1)}, bf16[1024,128]{1,0:T(8,128)(2,1)S(1)}, u32[]{:S(2)}, u32[]{:S(2)}) collective-permute-start(bf16[1024,128]{1,0:T(8,128)(2,1)S(1)} %shard_map.116.after_ref), channel_id=1, source_target_pairs={{0,7},{1,2},{2,1},{3,4},{4,3},{5,6},{6,5},{7,0},{8,15},{9,10},{10,... | collective-permute-start | bytes 786440 | tf_op jit(solution)/shard_map/ppermute | solution.py:79
  17.8 0.0 copy-done
  17.8 0.0 copy-done.1
  17.8 0.9 %shard_map.117 = (bf16[4,256,256]{2,1,0:T(8,128)(2,1)S(1)}, bf16[272,256]{1,0:T(8,128)(2,1)S(1)}) custom-call(bf16[4,512,256]{2,1,0:T(8,128)(2,1)S(1)} %copy-done, bf16[4,256,256]{2,1,0:T(8,128)(2,1)S(1)} %copy-done.1, bf16[528,128]{1,0:T(8,128)(2,1)S(1)} %collective-permute-done.2.x_ref.low_ref, bf16[512,128]{1,0:T(8,128)(2,1)S(1)} %collective-permute-done.3.x_ref.high_ref, ...), custom_call_target="tpu_custom_call" | custom-call | flops 1 | bytes 1 | tf_op jit(solution)/shard_map/pallas_call | solution.py:37
  18.7 0.0 collective-permute-done.1.amps_in_ref
  18.7 0.0 copy-start.4
  18.8 2.3 %collective-permute-start.7 = (bf16[272,256]{1,0:T(8,128)(2,1)S(1)}, bf16[272,256]{1,0:T(8,128)(2,1)S(1)}, u32[]{:S(2)}, u32[]{:S(2)}) collective-permute-start(bf16[272,256]{1,0:T(8,128)(2,1)S(1)} %get-tuple-element.30.after_ref), channel_id=1, source_target_pairs={{0,7},{1,2},{2,1},{3,4},{4,3},{5,6},{6,5},{7,0},{8,15},{9,10},{10,... | collective-permute-start | bytes 417800 | tf_op jit(solution)/shard_map/ppermute | solution.py:79
  21.0 0.0 collective-permute-done.4.three_in_ref
  21.0 0.0 copy-done.6
  21.0 0.0 copy-start.5
  21.0 0.1 collective-permute-start.8
  21.1 1.3 %copy-done.5 = bf16[2,1024,512]{2,1,0:T(8,128)(2,1)} copy-done((bf16[2,1024,512]{2,1,0:T(8,128)(2,1)}, bf16[2,1024,512]{2,1,0:T(8,128)(2,1)S(1)}, u32[]{:S(2)}) %copy-start.5) | copy-done | bytes 2097176
  22.4 0.0 copy-done.3
  22.4 1.8 %shard_map.119 = (bf16[256,1024]{1,0:T(8,128)(2,1)S(1)}, bf16[1024,256]{1,0:T(8,128)(2,1)S(1)}, bf16[512,256]{1,0:T(8,128)(2,1)S(1)}) custom-call(f32[8,128]{1,0:T(8,128)S(1)} %copy-done.3, bf16[2,1024,512]{2,1,0:T(8,128)(2,1)S(1)} %shard_map.114.three_ref, bf16[2,1024,512]{2,1,0:T(8,128)(2,1)} %copy-done.5, bf16[4,512,256]{2,1,0:T(8,128)(2,1)S(1)} %copy-done, ...), custom_call_target="tpu_custom_call" | custom-call | flops 1 | bytes 1 | tf_op jit(solution)/shard_map/pallas_call | solution.py:37
  24.2 0.0 collective-permute-done.coeff_in_ref.in_ref
  24.2 0.1 collective-permute-start.12
  24.3 0.0 copy-done.4
  24.3 1.5 %shard_map.118 = (bf16[4,256,256]{2,1,0:T(8,128)(2,1)S(1)}, f32[256,256]{1,0:T(8,128)S(1)}, f32[256,256]{1,0:T(8,128)S(1)}, f32[256,256]{1,0:T(8,128)S(1)}) custom-call(f32[8,128]{1,0:T(8,128)S(1)} %copy-done.3, bf16[4,512,256]{2,1,0:T(8,128)(2,1)S(1)} %copy-done, bf16[4,512,256]{2,1,0:T(8,128)(2,1)S(1)} %collective-permute-done.coeff_in_ref.in_ref, ...), custom_call_target="tpu_custom_call" | custom-call | flops 1 | bytes 1 | tf_op jit(solution)/shard_map/pallas_call | solution.py:37
  25.8 0.0 collective-permute-done.8.low_ref
  25.8 5.2 %collective-permute-done.7.co_ref = bf16[272,256]{1,0:T(8,128)(2,1)S(1)} collective-permute-done((bf16[272,256]{1,0:T(8,128)(2,1)S(1)}, bf16[272,256]{1,0:T(8,128)(2,1)S(1)}, u32[]{:S(2)}, u32[]{:S(2)}) %collective-permute-start.7) | collective-permute-done | bytes 139296 | tf_op jit(solution)/shard_map/ppermute | solution.py:79
  31.0 0.0 collective-permute-done.6.high_ref
  31.0 0.0 collective-permute-done.5.low_ref
  31.0 0.5 %shard_map.121 = (bf16[256,256]{1,0:T(8,128)(2,1)S(1)}, f32[256,256]{1,0:T(8,128)S(1)}) custom-call(f32[8,128]{1,0:T(8,128)S(1)} %copy-done.3, bf16[256,1024]{1,0:T(8,128)(2,1)S(1)} %get-tuple-element.33.first_ref, bf16[1024,256]{1,0:T(8,128)(2,1)S(1)} %get-tuple-element.34.second_ref, bf16[1040,128]{1,0:T(8,128)(2,1)S(1)} %collective-permute-done.5.low_ref, ...), custom_call_target="tpu_custom_call" | custom-call | flops 1 | bytes 1 | tf_op jit(solution)/shard_map/pallas_call | solution.py:37
  31.6 2.5 %collective-permute-start.9 = (bf16[256,256]{1,0:T(8,128)(2,1)S(1)}, bf16[256,256]{1,0:T(8,128)(2,1)S(1)}, u32[]{:S(2)}, u32[]{:S(2)}) collective-permute-start(bf16[256,256]{1,0:T(8,128)(2,1)S(1)} %get-tuple-element.37.amp_ref.after_ref.refs_0_), channel_id=1, source_target_pairs={{0,8},{8,0},{16,24},{24,16},{1,9},{9,1},{17,25},{25,17},{2,10},{10... | collective-permute-start | bytes 393224 | tf_op jit(solution)/shard_map/ppermute | solution.py:90
  34.1 1.4 %collective-permute-start.10 = (bf16[256,256]{1,0:T(8,128)(2,1)S(1)}, bf16[256,256]{1,0:T(8,128)(2,1)S(1)}, u32[]{:S(2)}, u32[]{:S(2)}) collective-permute-start(bf16[256,256]{1,0:T(8,128)(2,1)S(1)} %get-tuple-element.37.amp_ref.after_ref.refs_0_), channel_id=1, source_target_pairs={{0,16},{8,24},{16,0},{24,8},{1,17},{9,25},{17,1},{25,9},{2,18},{10... | collective-permute-start | bytes 393224 | tf_op jit(solution)/shard_map/ppermute | solution.py:90
  35.4 0.1 collective-permute-start.11
  35.6 0.4 shard_map.122
  36.0 3.9 %collective-permute-start.16 = (bf16[272,256]{1,0:T(8,128)(2,1)S(1)}, bf16[272,256]{1,0:T(8,128)(2,1)S(1)}, u32[]{:S(2)}, u32[]{:S(2)}) collective-permute-start(bf16[272,256]{1,0:T(8,128)(2,1)S(1)} %get-tuple-element.49.held_ref), channel_id=1, source_target_pairs={{0,8},{1,9},{2,10},{3,11},{4,12},{5,13},{6,14},{7,15}} | collective-permute-start | bytes 417800 | tf_op jit(solution)/shard_map/ppermute | solution.py:448
  39.9 0.0 collective-permute-done.12.x_ref
  39.9 0.0 collective-permute-done.9.refs_1_
  39.9 0.0 collective-permute-done.10.refs_2_
  39.9 1.4 %collective-permute-done.11.refs_3_ = bf16[256,256]{1,0:T(8,128)(2,1)S(1)} collective-permute-done((bf16[256,256]{1,0:T(8,128)(2,1)S(1)}, bf16[256,256]{1,0:T(8,128)(2,1)S(1)}, u32[]{:S(2)}, u32[]{:S(2)}) %collective-permute-start.11) | collective-permute-done | bytes 131104 | tf_op jit(solution)/shard_map/ppermute | solution.py:90
  41.3 0.0 collective-permute-start.13
  41.3 1.1 %collective-permute-done.16.come_ref.refs_0_ = bf16[272,256]{1,0:T(8,128)(2,1)S(1)} collective-permute-done((bf16[272,256]{1,0:T(8,128)(2,1)S(1)}, bf16[272,256]{1,0:T(8,128)(2,1)S(1)}, u32[]{:S(2)}, u32[]{:S(2)}) %collective-permute-start.16) | collective-permute-done | bytes 139296 | tf_op jit(solution)/shard_map/ppermute | solution.py:448
  42.5 3.9 %collective-permute-start.17 = (bf16[272,256]{1,0:T(8,128)(2,1)S(1)}, bf16[272,256]{1,0:T(8,128)(2,1)S(1)}, u32[]{:S(2)}, u32[]{:S(2)}) collective-permute-start(bf16[272,256]{1,0:T(8,128)(2,1)S(1)} %shard_map.127), channel_id=1, source_target_pairs={{0,16},{8,24},{1,17},{9,25},{2,18},{10,26},{3,19},{11,27},{4,20},{... | collective-permute-start | bytes 417800 | tf_op jit(solution)/shard_map/ppermute | solution.py:448
  46.4 0.1 collective-permute-start.14
  46.5 0.5 %collective-permute-start.15 = (bf16[256,256]{1,0:T(8,128)(2,1)S(1)}, bf16[256,256]{1,0:T(8,128)(2,1)S(1)}, u32[]{:S(2)}, u32[]{:S(2)}) collective-permute-start(bf16[256,256]{1,0:T(8,128)(2,1)S(1)} %get-tuple-element.48), channel_id=1, source_target_pairs={{0,1},{1,0},{2,3},{3,2},{4,5},{5,4},{6,7},{7,6},{8,9},{9,8},{10,11... | collective-permute-start | bytes 393224 | tf_op jit(solution)/shard_map/ppermute | solution.py:76
  47.0 1.5 %shard_map.128 = (bf16[2,256,256]{2,1,0:T(8,128)(2,1)}, bf16[2,512,256]{2,1,0:T(8,128)(2,1)}) custom-call(f32[8,128]{1,0:T(8,128)S(1)} %copy-done.3, bf16[256,256]{1,0:T(8,128)(2,1)S(1)} %get-tuple-element.45.refs_4_.after_ref), custom_call_target="tpu_custom_call" | custom-call | flops 1 | bytes 1 | tf_op jit(solution)/shard_map/pallas_call | solution.py:37
  48.6 0.4 collective-permute-done.17.refs_1_
  49.0 0.0 collective-permute-done.14.ci_ref
  49.0 0.0 collective-permute-done.15.cei_ref
  49.0 0.0 collective-permute-done.13.co_ref
  49.0 0.2 shard_map.129
  (6 shorter events, 0.1 us)
Async XLA Ops:
  0.6 20.4 %collective-permute-start.4 = (bf16[2,1024,512]{2,1,0:T(8,128)(2,1)}, bf16[2,1024,512]{2,1,0:T(8,128)(2,1)S(1)}, u32[]{:S(2)}, u32[]{:S(2)}) collective-permute-start(bf16[2,1024,512]{2,1,0:T(8,128)(2,1)} %three_ref.1), channel_id=1, source_target_pairs={{0,1},{1,0},{2,3},{3,2},{4,5},{5,4},{6,7},{7,6},{8,9},{9,8},{10,11... | collective-permute-start | bytes 6291464 | tf_op jit(solution)/shard_map/ppermute | solution.py:76
  1.1 23.0 %collective-permute-start = (bf16[4,512,256]{2,1,0:T(8,128)(2,1)}, bf16[4,512,256]{2,1,0:T(8,128)(2,1)S(1)}, u32[]{:S(2)}, u32[]{:S(2)}) collective-permute-start(bf16[4,512,256]{2,1,0:T(8,128)(2,1)} %coeff_ref.11), channel_id=1, source_target_pairs={{0,1},{1,0},{2,3},{3,2},{4,5},{5,4},{6,7},{7,6},{8,9},{9,8},{10,11... | collective-permute-start | bytes 3145736 | tf_op jit(solution)/shard_map/ppermute | solution.py:76
  1.2 17.5 %collective-permute-start.1 = (bf16[4,256,256]{2,1,0:T(8,128)(2,1)}, bf16[4,256,256]{2,1,0:T(8,128)(2,1)S(1)}, u32[]{:S(2)}, u32[]{:S(2)}) collective-permute-start(bf16[4,256,256]{2,1,0:T(8,128)(2,1)} %amps_ref.5), channel_id=1, source_target_pairs={{0,1},{1,0},{2,3},{3,2},{4,5},{5,4},{6,7},{7,6},{8,9},{9,8},{10,11... | collective-permute-start | bytes 1572872 | tf_op jit(solution)/shard_map/ppermute | solution.py:76
  3.7 8.4 %collective-permute-start.2 = (bf16[528,128]{1,0:T(8,128)(2,1)}, bf16[528,128]{1,0:T(8,128)(2,1)S(1)}, u32[]{:S(2)}, u32[]{:S(2)}) collective-permute-start(bf16[528,128]{1,0:T(8,128)(2,1)} %get-tuple-element.28), channel_id=1, source_target_pairs={{0,7},{1,2},{2,1},{3,4},{4,3},{5,6},{6,5},{7,0},{8,15},{9,10},{10,... | collective-permute-start | bytes 405512 | tf_op jit(solution)/shard_map/ppermute | solution.py:79
  8.5 7.4 %collective-permute-start.3 = (bf16[512,128]{1,0:T(8,128)(2,1)}, bf16[512,128]{1,0:T(8,128)(2,1)S(1)}, u32[]{:S(2)}, u32[]{:S(2)}) collective-permute-start(bf16[512,128]{1,0:T(8,128)(2,1)} %get-tuple-element.29), channel_id=1, source_target_pairs={{0,7},{1,2},{2,1},{3,4},{4,3},{5,6},{6,5},{7,0},{8,15},{9,10},{10,... | collective-permute-start | bytes 393224 | tf_op jit(solution)/shard_map/ppermute | solution.py:79
  8.6 0.7 %copy-start.2 = (f32[8,128]{1,0:T(8,128)S(1)}, f32[8,128]{1,0:T(8,128)}, u32[]{:S(2)}) copy-start(f32[8,128]{1,0:T(8,128)} %get-tuple-element.27.after_ref.nums) | copy-start | bytes 12292
  10.8 7.0 %copy-start = (bf16[4,512,256]{2,1,0:T(8,128)(2,1)S(1)}, bf16[4,512,256]{2,1,0:T(8,128)(2,1)}, u32[]{:S(2)}) copy-start(bf16[4,512,256]{2,1,0:T(8,128)(2,1)} %coeff_ref.11) | copy-start | bytes 3145732
  10.8 7.0 %copy-start.1 = (bf16[4,256,256]{2,1,0:T(8,128)(2,1)S(1)}, bf16[4,256,256]{2,1,0:T(8,128)(2,1)}, u32[]{:S(2)}) copy-start(bf16[4,256,256]{2,1,0:T(8,128)(2,1)} %amps_ref.5) | copy-start | bytes 1572868
  12.7 8.4 %copy-start.6 = (bf16[528,128]{1,0:T(8,128)(2,1)S(1)}, bf16[528,128]{1,0:T(8,128)(2,1)}, u32[]{:S(2)}) copy-start(bf16[528,128]{1,0:T(8,128)(2,1)} %get-tuple-element.28) | copy-start | bytes 405508
  12.7 9.7 %copy-start.3 = (f32[8,128]{1,0:T(8,128)S(1)}, f32[8,128]{1,0:T(8,128)}, u32[]{:S(2)}) copy-start(f32[8,128]{1,0:T(8,128)} %get-tuple-element.27.after_ref.nums) | copy-start | bytes 12292
  12.7 18.4 %collective-permute-start.5 = (bf16[1040,128]{1,0:T(8,128)(2,1)S(1)}, bf16[1040,128]{1,0:T(8,128)(2,1)S(1)}, u32[]{:S(2)}, u32[]{:S(2)}) collective-permute-start(bf16[1040,128]{1,0:T(8,128)(2,1)S(1)} %shard_map.115.after_ref), channel_id=1, source_target_pairs={{0,7},{1,2},{2,1},{3,4},{4,3},{5,6},{6,5},{7,0},{8,15},{9,10},{10,... | collective-permute-start | bytes 798728 | tf_op jit(solution)/shard_map/ppermute | solution.py:79
  16.4 14.6 %collective-permute-start.6 = (bf16[1024,128]{1,0:T(8,128)(2,1)S(1)}, bf16[1024,128]{1,0:T(8,128)(2,1)S(1)}, u32[]{:S(2)}, u32[]{:S(2)}) collective-permute-start(bf16[1024,128]{1,0:T(8,128)(2,1)S(1)} %shard_map.116.after_ref), channel_id=1, source_target_pairs={{0,7},{1,2},{2,1},{3,4},{4,3},{5,6},{6,5},{7,0},{8,15},{9,10},{10,... | collective-permute-start | bytes 786440 | tf_op jit(solution)/shard_map/ppermute | solution.py:79
  18.7 5.5 %copy-start.4 = (f32[4,256]{1,0:T(4,128)S(1)}, f32[4,256]{1,0:T(4,128)}, u32[]{:S(2)}) copy-start(f32[4,256]{1,0:T(4,128)} %eps_ref.1) | copy-start | bytes 12292
  18.8 12.3 %collective-permute-start.7 = (bf16[272,256]{1,0:T(8,128)(2,1)S(1)}, bf16[272,256]{1,0:T(8,128)(2,1)S(1)}, u32[]{:S(2)}, u32[]{:S(2)}) collective-permute-start(bf16[272,256]{1,0:T(8,128)(2,1)S(1)} %get-tuple-element.30.after_ref), channel_id=1, source_target_pairs={{0,7},{1,2},{2,1},{3,4},{4,3},{5,6},{6,5},{7,0},{8,15},{9,10},{10,... | collective-permute-start | bytes 417800 | tf_op jit(solution)/shard_map/ppermute | solution.py:79
  21.0 1.4 %copy-start.5 = (bf16[2,1024,512]{2,1,0:T(8,128)(2,1)}, bf16[2,1024,512]{2,1,0:T(8,128)(2,1)S(1)}, u32[]{:S(2)}) copy-start(bf16[2,1024,512]{2,1,0:T(8,128)(2,1)S(1)} %collective-permute-done.4.three_in_ref) | copy-start | bytes 6291460
  21.0 4.7 %collective-permute-start.8 = (bf16[528,128]{1,0:T(8,128)(2,1)S(1)}, bf16[528,128]{1,0:T(8,128)(2,1)S(1)}, u32[]{:S(2)}, u32[]{:S(2)}) collective-permute-start(bf16[528,128]{1,0:T(8,128)(2,1)S(1)} %copy-done.6), channel_id=1, source_target_pairs={{0,1},{1,0},{2,3},{3,2},{4,5},{5,4},{6,7},{7,6},{8,9},{9,8},{10,11... | collective-permute-start | bytes 405512 | tf_op jit(solution)/shard_map/ppermute | solution.py:76
  24.2 15.7 %collective-permute-start.12 = (bf16[512,256]{1,0:T(8,128)(2,1)S(1)}, bf16[512,256]{1,0:T(8,128)(2,1)S(1)}, u32[]{:S(2)}, u32[]{:S(2)}) collective-permute-start(bf16[512,256]{1,0:T(8,128)(2,1)S(1)} %get-tuple-element.44), channel_id=1, source_target_pairs={{0,1},{1,0},{2,3},{3,2},{4,5},{5,4},{6,7},{7,6},{8,15},{9,10},{10,... | collective-permute-start | bytes 786440 | tf_op jit(solution)/shard_map/ppermute | solution.py:87
  31.6 8.3 %collective-permute-start.9 = (bf16[256,256]{1,0:T(8,128)(2,1)S(1)}, bf16[256,256]{1,0:T(8,128)(2,1)S(1)}, u32[]{:S(2)}, u32[]{:S(2)}) collective-permute-start(bf16[256,256]{1,0:T(8,128)(2,1)S(1)} %get-tuple-element.37.amp_ref.after_ref.refs_0_), channel_id=1, source_target_pairs={{0,8},{8,0},{16,24},{24,16},{1,9},{9,1},{17,25},{25,17},{2,10},{10... | collective-permute-start | bytes 393224 | tf_op jit(solution)/shard_map/ppermute | solution.py:90
  34.1 5.9 %collective-permute-start.10 = (bf16[256,256]{1,0:T(8,128)(2,1)S(1)}, bf16[256,256]{1,0:T(8,128)(2,1)S(1)}, u32[]{:S(2)}, u32[]{:S(2)}) collective-permute-start(bf16[256,256]{1,0:T(8,128)(2,1)S(1)} %get-tuple-element.37.amp_ref.after_ref.refs_0_), channel_id=1, source_target_pairs={{0,16},{8,24},{16,0},{24,8},{1,17},{9,25},{17,1},{25,9},{2,18},{10... | collective-permute-start | bytes 393224 | tf_op jit(solution)/shard_map/ppermute | solution.py:90
  35.4 5.9 %collective-permute-start.11 = (bf16[256,256]{1,0:T(8,128)(2,1)S(1)}, bf16[256,256]{1,0:T(8,128)(2,1)S(1)}, u32[]{:S(2)}, u32[]{:S(2)}) collective-permute-start(bf16[256,256]{1,0:T(8,128)(2,1)S(1)} %get-tuple-element.37.amp_ref.after_ref.refs_0_), channel_id=1, source_target_pairs={{0,24},{8,16},{16,8},{24,0},{1,25},{9,17},{17,9},{25,1},{2,26},{10... | collective-permute-start | bytes 393224 | tf_op jit(solution)/shard_map/ppermute | solution.py:90
  36.0 6.4 %collective-permute-start.16 = (bf16[272,256]{1,0:T(8,128)(2,1)S(1)}, bf16[272,256]{1,0:T(8,128)(2,1)S(1)}, u32[]{:S(2)}, u32[]{:S(2)}) collective-permute-start(bf16[272,256]{1,0:T(8,128)(2,1)S(1)} %get-tuple-element.49.held_ref), channel_id=1, source_target_pairs={{0,8},{1,9},{2,10},{3,11},{4,12},{5,13},{6,14},{7,15}} | collective-permute-start | bytes 417800 | tf_op jit(solution)/shard_map/ppermute | solution.py:448
  41.3 7.7 %collective-permute-start.13 = (bf16[2,256,256]{2,1,0:T(8,128)(2,1)S(1)}, bf16[2,256,256]{2,1,0:T(8,128)(2,1)S(1)}, u32[]{:S(2)}, u32[]{:S(2)}) collective-permute-start(bf16[2,256,256]{2,1,0:T(8,128)(2,1)S(1)} %shard_map.124.refs_4_), channel_id=1, source_target_pairs={{0,1},{1,0},{2,3},{3,2},{4,5},{5,4},{6,7},{7,6},{8,15},{9,10},{10,... | collective-permute-start | bytes 786440 | tf_op jit(solution)/shard_map/ppermute | solution.py:87
  42.5 6.5 %collective-permute-start.17 = (bf16[272,256]{1,0:T(8,128)(2,1)S(1)}, bf16[272,256]{1,0:T(8,128)(2,1)S(1)}, u32[]{:S(2)}, u32[]{:S(2)}) collective-permute-start(bf16[272,256]{1,0:T(8,128)(2,1)S(1)} %shard_map.127), channel_id=1, source_target_pairs={{0,16},{8,24},{1,17},{9,25},{2,18},{10,26},{3,19},{11,27},{4,20},{... | collective-permute-start | bytes 417800 | tf_op jit(solution)/shard_map/ppermute | solution.py:448
  46.4 2.5 %collective-permute-start.14 = (bf16[256,256]{1,0:T(8,128)(2,1)S(1)}, bf16[256,256]{1,0:T(8,128)(2,1)S(1)}, u32[]{:S(2)}, u32[]{:S(2)}) collective-permute-start(bf16[256,256]{1,0:T(8,128)(2,1)S(1)} %get-tuple-element.45.refs_4_.after_ref), channel_id=1, source_target_pairs={{0,1},{1,0},{2,3},{3,2},{4,5},{5,4},{6,7},{7,6},{8,9},{9,8},{10,11... | collective-permute-start | bytes 393224 | tf_op jit(solution)/shard_map/ppermute | solution.py:76
  46.5 2.5 %collective-permute-start.15 = (bf16[256,256]{1,0:T(8,128)(2,1)S(1)}, bf16[256,256]{1,0:T(8,128)(2,1)S(1)}, u32[]{:S(2)}, u32[]{:S(2)}) collective-permute-start(bf16[256,256]{1,0:T(8,128)(2,1)S(1)} %get-tuple-element.48), channel_id=1, source_target_pairs={{0,1},{1,0},{2,3},{3,2},{4,5},{5,4},{6,7},{7,6},{8,9},{9,8},{10,11... | collective-permute-start | bytes 393224 | tf_op jit(solution)/shard_map/ppermute | solution.py:76

commit v21 on v20

--- a/solution.py
+++ b/solution.py
@@ -489,7 +489,7 @@
         [two_b],
         (nums, low_out, s_out, se_out, *amp_roles),
     )
-    cc_from_out = outer_for_owners(cc_out)
+    cc_from_out = outer(cc_out)
 
     def inner_again_body(nums, low_ref, s_ref, se_ref, *refs):
         amp_refs, c_refs = refs[:roles], refs[-2:]

time: 49.9 us -> 50 us (level)
    ppermute x5 -> x6, starting transfers between devices: 11.8 us -> 12.3 us  [outer(): return lax.ppermute(x, 'pairs', list(enumerate(outer_of)))]
    ppermute x5 -> x6, waiting for transfers between devices: 6.52 us -> 6.56 us  [outer(): return lax.ppermute(x, 'pairs', list(enumerate(outer_of)))]
where the time goes in v21:
time: 50 us; the launch traced here: 49.1 us
  starting transfers between devices  25.7 us (51%)
  Pallas kernels  11.5 us (23%)
  waiting for transfers between devices  9.02 us (18%)
  local copies, waits for them, and re-layouts  1.98 us (4%)
  between operations  0.89 us (2%)
    ppermute x6, starting transfers between devices, outer(): return lax.ppermute(x, 'pairs', list(enumerate(outer_of)))  12.3 us
    pallas_call x17, Pallas kernels, call(): pl.pallas_call(body, in_specs=ins, out_specs=[spec for spec, _, _ in outs...  11.5 us
    ppermute x2, starting transfers between devices, local(): lax.ppermute(held, 'role', [(i, i + step) for i in range(step)])  7.68 us
    ppermute x6, waiting for transfers between devices, outer(): return lax.ppermute(x, 'pairs', list(enumerate(outer_of)))  6.56 us
    ppermute x3, starting transfers between devices, swap(): return lax.ppermute(x, 'role', [(i, i ^ by) for i in range(roles)])  4 us
    unnamed x14, local copies, waits for them, and re-layouts  1.98 us
    ppermute x6, starting transfers between devices, inner(): return lax.ppermute(x, 'pairs', list(enumerate(inner_of)))  1.66 us
    ppermute x3, waiting for transfers between devices, swap(): return lax.ppermute(x, 'role', [(i, i ^ by) for i in range(roles)])  1.39 us
  transfers between devices with their start and end apart: 18, of which 5 were waited for; matrix products, arithmetic and copies ran while one was open for 0% of the time, Pallas kernels for 23%

profile of v21, /device:TPU:0, one launch (start us, length us, event | category | flops | bytes accessed | tf_op | source)
XLA Modules:
  0.0 49.1 jit_solution(8443567820587838055)
XLA Ops:
  0.6 0.5 %collective-permute-start.4 = (bf16[2,1024,512]{2,1,0:T(8,128)(2,1)}, bf16[2,1024,512]{2,1,0:T(8,128)(2,1)S(1)}, u32[]{:S(2)}, u32[]{:S(2)}) collective-permute-start(bf16[2,1024,512]{2,1,0:T(8,128)(2,1)} %three_ref.1), channel_id=1, source_target_pairs={{0,1},{1,0},{2,3},{3,2},{4,5},{5,4},{6,7},{7,6},{8,9},{9,8},{10,11... | collective-permute-start | bytes 6291464 | tf_op jit(solution)/shard_map/ppermute | solution.py:76
  1.1 0.1 collective-permute-start
  1.2 0.4 collective-permute-start.1
  1.7 2.0 %shard_map.113 = (bf16[528,128]{1,0:T(8,128)(2,1)}, bf16[512,128]{1,0:T(8,128)(2,1)}, f32[8,128]{1,0:T(8,128)}) custom-call(s32[4]{0:T(128)} %owner_hbm.1, s32[2,4]{1,0:T(2,128)} %bitcast.1, s32[4,8]{1,0:T(4,128)} %partner_hbm.1, f32[4,8]{1,0:T(4,128)} %coupling_hbm.1, f32[16]{0:T(128)} %eps_hbm.1, s32[4]{0:T(128)} %nvirt_hbm.1, bf16[4,512,256]{2,1,0:T(8,128)(2,1)} %coeff_ref.11), custom_call_target="tpu_custom_call" | custom-call | flops 1 | bytes 1 | tf_op jit(solution)/shard_map/pallas_call | solution.py:37
  3.7 4.8 %collective-permute-start.2 = (bf16[528,128]{1,0:T(8,128)(2,1)}, bf16[528,128]{1,0:T(8,128)(2,1)S(1)}, u32[]{:S(2)}, u32[]{:S(2)}) collective-permute-start(bf16[528,128]{1,0:T(8,128)(2,1)} %get-tuple-element.28), channel_id=1, source_target_pairs={{0,7},{1,2},{2,1},{3,4},{4,3},{5,6},{6,5},{7,0},{8,15},{9,10},{10,... | collective-permute-start | bytes 405512 | tf_op jit(solution)/shard_map/ppermute | solution.py:79
  8.5 0.1 collective-permute-start.3
  8.6 0.0 copy-start.2
  8.6 0.7 %copy-done.2 = f32[8,128]{1,0:T(8,128)S(1)} copy-done((f32[8,128]{1,0:T(8,128)S(1)}, f32[8,128]{1,0:T(8,128)}, u32[]{:S(2)}) %copy-start.2) | copy-done | bytes 4120
  9.2 1.6 %shard_map.114.three_ref = bf16[2,1024,512]{2,1,0:T(8,128)(2,1)S(1)} custom-call(bf16[2,1024,512]{2,1,0:T(8,128)(2,1)} %three_ref.1, f32[8,128]{1,0:T(8,128)S(1)} %copy-done.2), custom_call_target="tpu_custom_call" | custom-call | flops 1 | bytes 1 | tf_op jit(solution)/shard_map/pallas_call | solution.py:37
  10.8 0.0 copy-start
  10.8 0.0 copy-start.1
  10.9 1.3 %collective-permute-done.2.x_ref.low_ref = bf16[528,128]{1,0:T(8,128)(2,1)S(1)} collective-permute-done((bf16[528,128]{1,0:T(8,128)(2,1)}, bf16[528,128]{1,0:T(8,128)(2,1)S(1)}, u32[]{:S(2)}, u32[]{:S(2)}) %collective-permute-start.2) | collective-permute-done | bytes 135200 | tf_op jit(solution)/shard_map/ppermute | solution.py:79
  12.1 0.5 %shard_map.115.after_ref = bf16[1040,128]{1,0:T(8,128)(2,1)S(1)} custom-call(bf16[2,1024,512]{2,1,0:T(8,128)(2,1)S(1)} %shard_map.114.three_ref, bf16[528,128]{1,0:T(8,128)(2,1)S(1)} %collective-permute-done.2.x_ref.low_ref), custom_call_target="tpu_custom_call" | custom-call | flops 1 | bytes 1 | tf_op jit(solution)/shard_map/pallas_call | solution.py:37
  12.7 0.0 copy-start.6
  12.7 0.0 copy-start.3
  12.7 3.2 %collective-permute-start.5 = (bf16[1040,128]{1,0:T(8,128)(2,1)S(1)}, bf16[1040,128]{1,0:T(8,128)(2,1)S(1)}, u32[]{:S(2)}, u32[]{:S(2)}) collective-permute-start(bf16[1040,128]{1,0:T(8,128)(2,1)S(1)} %shard_map.115.after_ref), channel_id=1, source_target_pairs={{0,7},{1,2},{2,1},{3,4},{4,3},{5,6},{6,5},{7,0},{8,15},{9,10},{10,... | collective-permute-start | bytes 798728 | tf_op jit(solution)/shard_map/ppermute | solution.py:79
  15.9 0.0 collective-permute-done.3.x_ref.high_ref
  15.9 0.5 %shard_map.116.after_ref = bf16[1024,128]{1,0:T(8,128)(2,1)S(1)} custom-call(bf16[2,1024,512]{2,1,0:T(8,128)(2,1)S(1)} %shard_map.114.three_ref, bf16[528,128]{1,0:T(8,128)(2,1)S(1)} %collective-permute-done.2.x_ref.low_ref, bf16[512,128]{1,0:T(8,128)(2,1)S(1)} %collective-permute-done.3.x_ref.high_ref, bf16[1040,128]{1,0:T(8,128)(2,1)S(1)} %shard_map.115.after_ref), custom_call_target="tpu_custom_call" | custom-call | flops 1 | bytes 1 | tf_op jit(solution)/shard_map/pallas_call | solution.py:37
  16.4 1.4 %collective-permute-start.6 = (bf16[1024,128]{1,0:T(8,128)(2,1)S(1)}, bf16[1024,128]{1,0:T(8,128)(2,1)S(1)}, u32[]{:S(2)}, u32[]{:S(2)}) collective-permute-start(bf16[1024,128]{1,0:T(8,128)(2,1)S(1)} %shard_map.116.after_ref), channel_id=1, source_target_pairs={{0,7},{1,2},{2,1},{3,4},{4,3},{5,6},{6,5},{7,0},{8,15},{9,10},{10,... | collective-permute-start | bytes 786440 | tf_op jit(solution)/shard_map/ppermute | solution.py:79
  17.8 0.0 copy-done
  17.8 0.0 copy-done.1
  17.8 0.9 %shard_map.117 = (bf16[4,256,256]{2,1,0:T(8,128)(2,1)S(1)}, bf16[272,256]{1,0:T(8,128)(2,1)S(1)}) custom-call(bf16[4,512,256]{2,1,0:T(8,128)(2,1)S(1)} %copy-done, bf16[4,256,256]{2,1,0:T(8,128)(2,1)S(1)} %copy-done.1, bf16[528,128]{1,0:T(8,128)(2,1)S(1)} %collective-permute-done.2.x_ref.low_ref, bf16[512,128]{1,0:T(8,128)(2,1)S(1)} %collective-permute-done.3.x_ref.high_ref, ...), custom_call_target="tpu_custom_call" | custom-call | flops 1 | bytes 1 | tf_op jit(solution)/shard_map/pallas_call | solution.py:37
  18.7 0.0 collective-permute-done.1.amps_in_ref
  18.7 0.0 copy-start.4
  18.8 2.3 %collective-permute-start.7 = (bf16[272,256]{1,0:T(8,128)(2,1)S(1)}, bf16[272,256]{1,0:T(8,128)(2,1)S(1)}, u32[]{:S(2)}, u32[]{:S(2)}) collective-permute-start(bf16[272,256]{1,0:T(8,128)(2,1)S(1)} %get-tuple-element.30.after_ref), channel_id=1, source_target_pairs={{0,7},{1,2},{2,1},{3,4},{4,3},{5,6},{6,5},{7,0},{8,15},{9,10},{10,... | collective-permute-start | bytes 417800 | tf_op jit(solution)/shard_map/ppermute | solution.py:79
  21.0 0.0 collective-permute-done.4.three_in_ref
  21.0 0.0 copy-done.6
  21.0 0.0 copy-start.5
  21.0 0.1 collective-permute-start.8
  21.1 1.3 %copy-done.5 = bf16[2,1024,512]{2,1,0:T(8,128)(2,1)} copy-done((bf16[2,1024,512]{2,1,0:T(8,128)(2,1)}, bf16[2,1024,512]{2,1,0:T(8,128)(2,1)S(1)}, u32[]{:S(2)}) %copy-start.5) | copy-done | bytes 2097176
  22.4 0.0 copy-done.3
  22.4 1.8 %shard_map.119 = (bf16[256,1024]{1,0:T(8,128)(2,1)S(1)}, bf16[1024,256]{1,0:T(8,128)(2,1)S(1)}, bf16[512,256]{1,0:T(8,128)(2,1)S(1)}) custom-call(f32[8,128]{1,0:T(8,128)S(1)} %copy-done.3, bf16[2,1024,512]{2,1,0:T(8,128)(2,1)S(1)} %shard_map.114.three_ref, bf16[2,1024,512]{2,1,0:T(8,128)(2,1)} %copy-done.5, bf16[4,512,256]{2,1,0:T(8,128)(2,1)S(1)} %copy-done, ...), custom_call_target="tpu_custom_call" | custom-call | flops 1 | bytes 1 | tf_op jit(solution)/shard_map/pallas_call | solution.py:37
  24.2 0.0 collective-permute-done.coeff_in_ref.in_ref
  24.2 0.1 collective-permute-start.12
  24.3 0.0 copy-done.4
  24.3 1.5 %shard_map.118 = (bf16[4,256,256]{2,1,0:T(8,128)(2,1)S(1)}, f32[256,256]{1,0:T(8,128)S(1)}, f32[256,256]{1,0:T(8,128)S(1)}, f32[256,256]{1,0:T(8,128)S(1)}) custom-call(f32[8,128]{1,0:T(8,128)S(1)} %copy-done.3, bf16[4,512,256]{2,1,0:T(8,128)(2,1)S(1)} %copy-done, bf16[4,512,256]{2,1,0:T(8,128)(2,1)S(1)} %collective-permute-done.coeff_in_ref.in_ref, ...), custom_call_target="tpu_custom_call" | custom-call | flops 1 | bytes 1 | tf_op jit(solution)/shard_map/pallas_call | solution.py:37
  25.8 0.0 collective-permute-done.8.low_ref
  25.8 5.2 %collective-permute-done.7.co_ref = bf16[272,256]{1,0:T(8,128)(2,1)S(1)} collective-permute-done((bf16[272,256]{1,0:T(8,128)(2,1)S(1)}, bf16[272,256]{1,0:T(8,128)(2,1)S(1)}, u32[]{:S(2)}, u32[]{:S(2)}) %collective-permute-start.7) | collective-permute-done | bytes 139296 | tf_op jit(solution)/shard_map/ppermute | solution.py:79
  31.0 0.0 collective-permute-done.6.high_ref
  31.0 0.0 collective-permute-done.5.low_ref
  31.0 0.5 %shard_map.121 = (bf16[256,256]{1,0:T(8,128)(2,1)S(1)}, f32[256,256]{1,0:T(8,128)S(1)}) custom-call(f32[8,128]{1,0:T(8,128)S(1)} %copy-done.3, bf16[256,1024]{1,0:T(8,128)(2,1)S(1)} %get-tuple-element.33.first_ref, bf16[1024,256]{1,0:T(8,128)(2,1)S(1)} %get-tuple-element.34.second_ref, bf16[1040,128]{1,0:T(8,128)(2,1)S(1)} %collective-permute-done.5.low_ref, ...), custom_call_target="tpu_custom_call" | custom-call | flops 1 | bytes 1 | tf_op jit(solution)/shard_map/pallas_call | solution.py:37
  31.6 2.5 %collective-permute-start.9 = (bf16[256,256]{1,0:T(8,128)(2,1)S(1)}, bf16[256,256]{1,0:T(8,128)(2,1)S(1)}, u32[]{:S(2)}, u32[]{:S(2)}) collective-permute-start(bf16[256,256]{1,0:T(8,128)(2,1)S(1)} %get-tuple-element.37.amp_ref.after_ref.refs_0_), channel_id=1, source_target_pairs={{0,8},{8,0},{16,24},{24,16},{1,9},{9,1},{17,25},{25,17},{2,10},{10... | collective-permute-start | bytes 393224 | tf_op jit(solution)/shard_map/ppermute | solution.py:90
  34.1 1.4 %collective-permute-start.10 = (bf16[256,256]{1,0:T(8,128)(2,1)S(1)}, bf16[256,256]{1,0:T(8,128)(2,1)S(1)}, u32[]{:S(2)}, u32[]{:S(2)}) collective-permute-start(bf16[256,256]{1,0:T(8,128)(2,1)S(1)} %get-tuple-element.37.amp_ref.after_ref.refs_0_), channel_id=1, source_target_pairs={{0,16},{8,24},{16,0},{24,8},{1,17},{9,25},{17,1},{25,9},{2,18},{10... | collective-permute-start | bytes 393224 | tf_op jit(solution)/shard_map/ppermute | solution.py:90
  35.4 0.1 collective-permute-start.11
  35.6 0.4 shard_map.122
  36.0 3.9 %collective-permute-start.16 = (bf16[272,256]{1,0:T(8,128)(2,1)S(1)}, bf16[272,256]{1,0:T(8,128)(2,1)S(1)}, u32[]{:S(2)}, u32[]{:S(2)}) collective-permute-start(bf16[272,256]{1,0:T(8,128)(2,1)S(1)} %get-tuple-element.49.held_ref), channel_id=1, source_target_pairs={{0,8},{1,9},{2,10},{3,11},{4,12},{5,13},{6,14},{7,15}} | collective-permute-start | bytes 417800 | tf_op jit(solution)/shard_map/ppermute | solution.py:448
  39.9 0.0 collective-permute-done.12.x_ref
  39.9 0.0 collective-permute-done.9.refs_1_
  39.9 0.0 collective-permute-done.10.refs_2_
  39.9 1.4 %collective-permute-done.11.refs_3_ = bf16[256,256]{1,0:T(8,128)(2,1)S(1)} collective-permute-done((bf16[256,256]{1,0:T(8,128)(2,1)S(1)}, bf16[256,256]{1,0:T(8,128)(2,1)S(1)}, u32[]{:S(2)}, u32[]{:S(2)}) %collective-permute-start.11) | collective-permute-done | bytes 131104 | tf_op jit(solution)/shard_map/ppermute | solution.py:90
  41.3 0.5 %collective-permute-start.13 = (bf16[2,256,256]{2,1,0:T(8,128)(2,1)S(1)}, bf16[2,256,256]{2,1,0:T(8,128)(2,1)S(1)}, u32[]{:S(2)}, u32[]{:S(2)}) collective-permute-start(bf16[2,256,256]{2,1,0:T(8,128)(2,1)S(1)} %shard_map.124.refs_4_), channel_id=1, source_target_pairs={{0,7},{1,2},{2,1},{3,4},{4,3},{5,6},{6,5},{7,0},{8,15},{9,10},{10,... | collective-permute-start | bytes 786440 | tf_op jit(solution)/shard_map/ppermute | solution.py:79
  41.8 0.6 %collective-permute-done.16.come_ref.refs_0_ = bf16[272,256]{1,0:T(8,128)(2,1)S(1)} collective-permute-done((bf16[272,256]{1,0:T(8,128)(2,1)S(1)}, bf16[272,256]{1,0:T(8,128)(2,1)S(1)}, u32[]{:S(2)}, u32[]{:S(2)}) %collective-permute-start.16) | collective-permute-done | bytes 139296 | tf_op jit(solution)/shard_map/ppermute | solution.py:448
  42.5 3.8 %collective-permute-start.17 = (bf16[272,256]{1,0:T(8,128)(2,1)S(1)}, bf16[272,256]{1,0:T(8,128)(2,1)S(1)}, u32[]{:S(2)}, u32[]{:S(2)}) collective-permute-start(bf16[272,256]{1,0:T(8,128)(2,1)S(1)} %shard_map.127), channel_id=1, source_target_pairs={{0,16},{8,24},{1,17},{9,25},{2,18},{10,26},{3,19},{11,27},{4,20},{... | collective-permute-start | bytes 417800 | tf_op jit(solution)/shard_map/ppermute | solution.py:448
  46.3 0.1 collective-permute-start.14
  46.4 0.5 %collective-permute-start.15 = (bf16[256,256]{1,0:T(8,128)(2,1)S(1)}, bf16[256,256]{1,0:T(8,128)(2,1)S(1)}, u32[]{:S(2)}, u32[]{:S(2)}) collective-permute-start(bf16[256,256]{1,0:T(8,128)(2,1)S(1)} %get-tuple-element.48), channel_id=1, source_target_pairs={{0,1},{1,0},{2,3},{3,2},{4,5},{5,4},{6,7},{7,6},{8,9},{9,8},{10,11... | collective-permute-start | bytes 393224 | tf_op jit(solution)/shard_map/ppermute | solution.py:76
  46.9 1.5 %shard_map.128 = (bf16[2,256,256]{2,1,0:T(8,128)(2,1)}, bf16[2,512,256]{2,1,0:T(8,128)(2,1)}) custom-call(f32[8,128]{1,0:T(8,128)S(1)} %copy-done.3, bf16[256,256]{1,0:T(8,128)(2,1)S(1)} %get-tuple-element.45.refs_4_.after_ref), custom_call_target="tpu_custom_call" | custom-call | flops 1 | bytes 1 | tf_op jit(solution)/shard_map/pallas_call | solution.py:37
  48.5 0.4 collective-permute-done.17.refs_1_
  48.9 0.0 collective-permute-done.14.ci_ref
  48.9 0.0 collective-permute-done.15.cei_ref
  48.9 0.0 collective-permute-done.13.co_ref
  48.9 0.2 shard_map.129
  (6 shorter events, 0.1 us)
Async XLA Ops:
  0.6 20.4 %collective-permute-start.4 = (bf16[2,1024,512]{2,1,0:T(8,128)(2,1)}, bf16[2,1024,512]{2,1,0:T(8,128)(2,1)S(1)}, u32[]{:S(2)}, u32[]{:S(2)}) collective-permute-start(bf16[2,1024,512]{2,1,0:T(8,128)(2,1)} %three_ref.1), channel_id=1, source_target_pairs={{0,1},{1,0},{2,3},{3,2},{4,5},{5,4},{6,7},{7,6},{8,9},{9,8},{10,11... | collective-permute-start | bytes 6291464 | tf_op jit(solution)/shard_map/ppermute | solution.py:76
  1.1 23.0 %collective-permute-start = (bf16[4,512,256]{2,1,0:T(8,128)(2,1)}, bf16[4,512,256]{2,1,0:T(8,128)(2,1)S(1)}, u32[]{:S(2)}, u32[]{:S(2)}) collective-permute-start(bf16[4,512,256]{2,1,0:T(8,128)(2,1)} %coeff_ref.11), channel_id=1, source_target_pairs={{0,1},{1,0},{2,3},{3,2},{4,5},{5,4},{6,7},{7,6},{8,9},{9,8},{10,11... | collective-permute-start | bytes 3145736 | tf_op jit(solution)/shard_map/ppermute | solution.py:76
  1.2 17.5 %collective-permute-start.1 = (bf16[4,256,256]{2,1,0:T(8,128)(2,1)}, bf16[4,256,256]{2,1,0:T(8,128)(2,1)S(1)}, u32[]{:S(2)}, u32[]{:S(2)}) collective-permute-start(bf16[4,256,256]{2,1,0:T(8,128)(2,1)} %amps_ref.5), channel_id=1, source_target_pairs={{0,1},{1,0},{2,3},{3,2},{4,5},{5,4},{6,7},{7,6},{8,9},{9,8},{10,11... | collective-permute-start | bytes 1572872 | tf_op jit(solution)/shard_map/ppermute | solution.py:76
  3.7 8.4 %collective-permute-start.2 = (bf16[528,128]{1,0:T(8,128)(2,1)}, bf16[528,128]{1,0:T(8,128)(2,1)S(1)}, u32[]{:S(2)}, u32[]{:S(2)}) collective-permute-start(bf16[528,128]{1,0:T(8,128)(2,1)} %get-tuple-element.28), channel_id=1, source_target_pairs={{0,7},{1,2},{2,1},{3,4},{4,3},{5,6},{6,5},{7,0},{8,15},{9,10},{10,... | collective-permute-start | bytes 405512 | tf_op jit(solution)/shard_map/ppermute | solution.py:79
  8.5 7.4 %collective-permute-start.3 = (bf16[512,128]{1,0:T(8,128)(2,1)}, bf16[512,128]{1,0:T(8,128)(2,1)S(1)}, u32[]{:S(2)}, u32[]{:S(2)}) collective-permute-start(bf16[512,128]{1,0:T(8,128)(2,1)} %get-tuple-element.29), channel_id=1, source_target_pairs={{0,7},{1,2},{2,1},{3,4},{4,3},{5,6},{6,5},{7,0},{8,15},{9,10},{10,... | collective-permute-start | bytes 393224 | tf_op jit(solution)/shard_map/ppermute | solution.py:79
  8.6 0.7 %copy-start.2 = (f32[8,128]{1,0:T(8,128)S(1)}, f32[8,128]{1,0:T(8,128)}, u32[]{:S(2)}) copy-start(f32[8,128]{1,0:T(8,128)} %get-tuple-element.27.after_ref.nums) | copy-start | bytes 12292
  10.8 7.0 %copy-start = (bf16[4,512,256]{2,1,0:T(8,128)(2,1)S(1)}, bf16[4,512,256]{2,1,0:T(8,128)(2,1)}, u32[]{:S(2)}) copy-start(bf16[4,512,256]{2,1,0:T(8,128)(2,1)} %coeff_ref.11) | copy-start | bytes 3145732
  10.8 7.0 %copy-start.1 = (bf16[4,256,256]{2,1,0:T(8,128)(2,1)S(1)}, bf16[4,256,256]{2,1,0:T(8,128)(2,1)}, u32[]{:S(2)}) copy-start(bf16[4,256,256]{2,1,0:T(8,128)(2,1)} %amps_ref.5) | copy-start | bytes 1572868
  12.7 8.4 %copy-start.6 = (bf16[528,128]{1,0:T(8,128)(2,1)S(1)}, bf16[528,128]{1,0:T(8,128)(2,1)}, u32[]{:S(2)}) copy-start(bf16[528,128]{1,0:T(8,128)(2,1)} %get-tuple-element.28) | copy-start | bytes 405508
  12.7 9.7 %copy-start.3 = (f32[8,128]{1,0:T(8,128)S(1)}, f32[8,128]{1,0:T(8,128)}, u32[]{:S(2)}) copy-start(f32[8,128]{1,0:T(8,128)} %get-tuple-element.27.after_ref.nums) | copy-start | bytes 12292
  12.7 18.4 %collective-permute-start.5 = (bf16[1040,128]{1,0:T(8,128)(2,1)S(1)}, bf16[1040,128]{1,0:T(8,128)(2,1)S(1)}, u32[]{:S(2)}, u32[]{:S(2)}) collective-permute-start(bf16[1040,128]{1,0:T(8,128)(2,1)S(1)} %shard_map.115.after_ref), channel_id=1, source_target_pairs={{0,7},{1,2},{2,1},{3,4},{4,3},{5,6},{6,5},{7,0},{8,15},{9,10},{10,... | collective-permute-start | bytes 798728 | tf_op jit(solution)/shard_map/ppermute | solution.py:79
  16.4 14.6 %collective-permute-start.6 = (bf16[1024,128]{1,0:T(8,128)(2,1)S(1)}, bf16[1024,128]{1,0:T(8,128)(2,1)S(1)}, u32[]{:S(2)}, u32[]{:S(2)}) collective-permute-start(bf16[1024,128]{1,0:T(8,128)(2,1)S(1)} %shard_map.116.after_ref), channel_id=1, source_target_pairs={{0,7},{1,2},{2,1},{3,4},{4,3},{5,6},{6,5},{7,0},{8,15},{9,10},{10,... | collective-permute-start | bytes 786440 | tf_op jit(solution)/shard_map/ppermute | solution.py:79
  18.7 5.5 %copy-start.4 = (f32[4,256]{1,0:T(4,128)S(1)}, f32[4,256]{1,0:T(4,128)}, u32[]{:S(2)}) copy-start(f32[4,256]{1,0:T(4,128)} %eps_ref.1) | copy-start | bytes 12292
  18.8 12.3 %collective-permute-start.7 = (bf16[272,256]{1,0:T(8,128)(2,1)S(1)}, bf16[272,256]{1,0:T(8,128)(2,1)S(1)}, u32[]{:S(2)}, u32[]{:S(2)}) collective-permute-start(bf16[272,256]{1,0:T(8,128)(2,1)S(1)} %get-tuple-element.30.after_ref), channel_id=1, source_target_pairs={{0,7},{1,2},{2,1},{3,4},{4,3},{5,6},{6,5},{7,0},{8,15},{9,10},{10,... | collective-permute-start | bytes 417800 | tf_op jit(solution)/shard_map/ppermute | solution.py:79
  21.0 1.4 %copy-start.5 = (bf16[2,1024,512]{2,1,0:T(8,128)(2,1)}, bf16[2,1024,512]{2,1,0:T(8,128)(2,1)S(1)}, u32[]{:S(2)}) copy-start(bf16[2,1024,512]{2,1,0:T(8,128)(2,1)S(1)} %collective-permute-done.4.three_in_ref) | copy-start | bytes 6291460
  21.0 4.7 %collective-permute-start.8 = (bf16[528,128]{1,0:T(8,128)(2,1)S(1)}, bf16[528,128]{1,0:T(8,128)(2,1)S(1)}, u32[]{:S(2)}, u32[]{:S(2)}) collective-permute-start(bf16[528,128]{1,0:T(8,128)(2,1)S(1)} %copy-done.6), channel_id=1, source_target_pairs={{0,1},{1,0},{2,3},{3,2},{4,5},{5,4},{6,7},{7,6},{8,9},{9,8},{10,11... | collective-permute-start | bytes 405512 | tf_op jit(solution)/shard_map/ppermute | solution.py:76
  24.2 15.7 %collective-permute-start.12 = (bf16[512,256]{1,0:T(8,128)(2,1)S(1)}, bf16[512,256]{1,0:T(8,128)(2,1)S(1)}, u32[]{:S(2)}, u32[]{:S(2)}) collective-permute-start(bf16[512,256]{1,0:T(8,128)(2,1)S(1)} %get-tuple-element.44), channel_id=1, source_target_pairs={{0,1},{1,0},{2,3},{3,2},{4,5},{5,4},{6,7},{7,6},{8,15},{9,10},{10,... | collective-permute-start | bytes 786440 | tf_op jit(solution)/shard_map/ppermute | solution.py:87
  31.6 8.3 %collective-permute-start.9 = (bf16[256,256]{1,0:T(8,128)(2,1)S(1)}, bf16[256,256]{1,0:T(8,128)(2,1)S(1)}, u32[]{:S(2)}, u32[]{:S(2)}) collective-permute-start(bf16[256,256]{1,0:T(8,128)(2,1)S(1)} %get-tuple-element.37.amp_ref.after_ref.refs_0_), channel_id=1, source_target_pairs={{0,8},{8,0},{16,24},{24,16},{1,9},{9,1},{17,25},{25,17},{2,10},{10... | collective-permute-start | bytes 393224 | tf_op jit(solution)/shard_map/ppermute | solution.py:90
  34.1 5.9 %collective-permute-start.10 = (bf16[256,256]{1,0:T(8,128)(2,1)S(1)}, bf16[256,256]{1,0:T(8,128)(2,1)S(1)}, u32[]{:S(2)}, u32[]{:S(2)}) collective-permute-start(bf16[256,256]{1,0:T(8,128)(2,1)S(1)} %get-tuple-element.37.amp_ref.after_ref.refs_0_), channel_id=1, source_target_pairs={{0,16},{8,24},{16,0},{24,8},{1,17},{9,25},{17,1},{25,9},{2,18},{10... | collective-permute-start | bytes 393224 | tf_op jit(solution)/shard_map/ppermute | solution.py:90
  35.4 5.9 %collective-permute-start.11 = (bf16[256,256]{1,0:T(8,128)(2,1)S(1)}, bf16[256,256]{1,0:T(8,128)(2,1)S(1)}, u32[]{:S(2)}, u32[]{:S(2)}) collective-permute-start(bf16[256,256]{1,0:T(8,128)(2,1)S(1)} %get-tuple-element.37.amp_ref.after_ref.refs_0_), channel_id=1, source_target_pairs={{0,24},{8,16},{16,8},{24,0},{1,25},{9,17},{17,9},{25,1},{2,26},{10... | collective-permute-start | bytes 393224 | tf_op jit(solution)/shard_map/ppermute | solution.py:90
  36.0 6.4 %collective-permute-start.16 = (bf16[272,256]{1,0:T(8,128)(2,1)S(1)}, bf16[272,256]{1,0:T(8,128)(2,1)S(1)}, u32[]{:S(2)}, u32[]{:S(2)}) collective-permute-start(bf16[272,256]{1,0:T(8,128)(2,1)S(1)} %get-tuple-element.49.held_ref), channel_id=1, source_target_pairs={{0,8},{1,9},{2,10},{3,11},{4,12},{5,13},{6,14},{7,15}} | collective-permute-start | bytes 417800 | tf_op jit(solution)/shard_map/ppermute | solution.py:448
  41.3 7.6 %collective-permute-start.13 = (bf16[2,256,256]{2,1,0:T(8,128)(2,1)S(1)}, bf16[2,256,256]{2,1,0:T(8,128)(2,1)S(1)}, u32[]{:S(2)}, u32[]{:S(2)}) collective-permute-start(bf16[2,256,256]{2,1,0:T(8,128)(2,1)S(1)} %shard_map.124.refs_4_), channel_id=1, source_target_pairs={{0,7},{1,2},{2,1},{3,4},{4,3},{5,6},{6,5},{7,0},{8,15},{9,10},{10,... | collective-permute-start | bytes 786440 | tf_op jit(solution)/shard_map/ppermute | solution.py:79
  42.5 6.4 %collective-permute-start.17 = (bf16[272,256]{1,0:T(8,128)(2,1)S(1)}, bf16[272,256]{1,0:T(8,128)(2,1)S(1)}, u32[]{:S(2)}, u32[]{:S(2)}) collective-permute-start(bf16[272,256]{1,0:T(8,128)(2,1)S(1)} %shard_map.127), channel_id=1, source_target_pairs={{0,16},{8,24},{1,17},{9,25},{2,18},{10,26},{3,19},{11,27},{4,20},{... | collective-permute-start | bytes 417800 | tf_op jit(solution)/shard_map/ppermute | solution.py:448
  46.3 2.5 %collective-permute-start.14 = (bf16[256,256]{1,0:T(8,128)(2,1)S(1)}, bf16[256,256]{1,0:T(8,128)(2,1)S(1)}, u32[]{:S(2)}, u32[]{:S(2)}) collective-permute-start(bf16[256,256]{1,0:T(8,128)(2,1)S(1)} %get-tuple-element.45.refs_4_.after_ref), channel_id=1, source_target_pairs={{0,1},{1,0},{2,3},{3,2},{4,5},{5,4},{6,7},{7,6},{8,9},{9,8},{10,11... | collective-permute-start | bytes 393224 | tf_op jit(solution)/shard_map/ppermute | solution.py:76
  46.4 2.5 %collective-permute-start.15 = (bf16[256,256]{1,0:T(8,128)(2,1)S(1)}, bf16[256,256]{1,0:T(8,128)(2,1)S(1)}, u32[]{:S(2)}, u32[]{:S(2)}) collective-permute-start(bf16[256,256]{1,0:T(8,128)(2,1)S(1)} %get-tuple-element.48), channel_id=1, source_target_pairs={{0,1},{1,0},{2,3},{3,2},{4,5},{5,4},{6,7},{7,6},{8,9},{9,8},{10,11... | collective-permute-start | bytes 393224 | tf_op jit(solution)/shard_map/ppermute | solution.py:76

commit v22 on v18

--- a/solution.py
+++ b/solution.py
@@ -1,3 +1,4 @@
+import functools
 import math
 
 import jax
@@ -65,7 +66,6 @@
     part = virt // 2
     sq_b = (VMEM, square, BF16)
     sq_f = (VMEM, square, F32)
-    two_b = (VMEM, (2, virt, virt), BF16)
     all_s = (VMEM, (pairs, virt, virt), BF16)
     half = (VMEM, (aux, virt), BF16)
 
@@ -454,33 +454,40 @@
         (coeff, x_extra_out, amp),
     )
 
-    def parts_of(nums, weight_of, amp_refs):
+    def parts_of(nums, weight_of, amp_refs, first=0):
         num, _ = read(nums)
         parts = []
-        for m in range(roles):
+        for m, amp_ref in enumerate(amp_refs, first):
             at = whole(num(ROLE_PAIR + m))
-            parts.append((at, weight_of(at), amp_refs[m][...]))
+            parts.append((at, weight_of(at), amp_ref[...]))
         return parts
 
     def told_weight(told, first):
         return lambda at: pick([told[:, first + q : first + q + 1] for q in range(pairs)], at)
 
-    def outer_again_body(nums, low_ref, s_ref, se_ref, *refs):
-        amp_refs, c_ref = refs[:roles], refs[-1]
+    def outer_again_body(first, last, nums, low_ref, s_ref, se_ref, *refs):
+        amp_refs, before, c_ref = refs[: last - first], refs[last - first : -1], refs[-1]
 
         @pl.when(lax.axis_index("role") > 0)
         def _():
             told = told_of(low_ref)
             for slot, of_s in enumerate((s_ref, se_ref)):
-                parts = parts_of(nums, told_weight(told, slot * pairs), amp_refs)
-                c_ref[slot] = coupled(of_s, parts).astype(BF16)
-
-    (cc_out,) = call(
-        outer_again_body,
-        [VMEM] + [VMEM] * (3 + roles),
-        [two_b],
-        (nums, low_out, s_out, se_out, *amp_roles),
-    )
+                parts = parts_of(nums, told_weight(told, slot * pairs), amp_refs, first)
+                total = coupled(of_s, parts)
+                for ref in before:
+                    total += ref[slot]
+                c_ref[slot] = total.astype(c_ref.dtype)
+
+    def outer_again(first, last, dtype, *before):
+        (c,) = call(
+            functools.partial(outer_again_body, first, last),
+            [VMEM] * (4 + last - first + len(before)),
+            [(VMEM, (2, virt, virt), dtype)],
+            (nums, low_out, s_out, se_out, *amp_roles[first:last], *before),
+        )
+        return c
+
+    cc_out = outer_again(roles // 2, roles, BF16, outer_again(0, roles // 2, F32))
     cc_from_out = outer(cc_out)
 
     def inner_again_body(nums, low_ref, s_ref, se_ref, *refs):

time: 49.4 us -> 49.4 us (level)
    pallas_call x17 -> x18, Pallas kernels: 11.5 us -> 11.6 us  [call(): pl.pallas_call(body, in_specs=ins, out_specs=[spec for spec, _, _ in outs...]
where the time goes in v22:
time: 49.4 us; the launch traced here: 49.2 us
  starting transfers between devices  24 us (49%)
  Pallas kernels  11.6 us (23%)
  waiting for transfers between devices  10.8 us (22%)
  local copies, waits for them, and re-layouts  1.98 us (4%)
  between operations  0.89 us (2%)
    ppermute x7, starting transfers between devices, outer(): return lax.ppermute(x, 'pairs', list(enumerate(outer_of)))  12.3 us
    pallas_call x18, Pallas kernels, call(): pl.pallas_call(body, in_specs=ins, out_specs=[spec for spec, _, _ in outs...  11.6 us
    ppermute x7, waiting for transfers between devices, outer(): return lax.ppermute(x, 'pairs', list(enumerate(outer_of)))  8.15 us
    ppermute x2, starting transfers between devices, local(): lax.ppermute(held, 'role', [(i, i + step) for i in range(step)])  6.48 us
    ppermute x3, starting transfers between devices, swap(): return lax.ppermute(x, 'role', [(i, i ^ by) for i in range(roles)])  3.55 us
    unnamed x14, local copies, waits for them, and re-layouts  1.98 us
    ppermute x6, starting transfers between devices, inner(): return lax.ppermute(x, 'pairs', list(enumerate(inner_of)))  1.66 us
    ppermute x3, waiting for transfers between devices, swap(): return lax.ppermute(x, 'role', [(i, i ^ by) for i in range(roles)])  1.47 us
  transfers between devices with their start and end apart: 18, of which 6 were waited for; matrix products, arithmetic and copies ran while one was open for 0% of the time, Pallas kernels for 23%

profile of v22, /device:TPU:0, one launch (start us, length us, event | category | flops | bytes accessed | tf_op | source)
XLA Modules:
  0.0 49.2 jit_solution(10094439622870382671)
XLA Ops:
  0.6 0.5 %collective-permute-start.4 = (bf16[2,1024,512]{2,1,0:T(8,128)(2,1)}, bf16[2,1024,512]{2,1,0:T(8,128)(2,1)S(1)}, u32[]{:S(2)}, u32[]{:S(2)}) collective-permute-start(bf16[2,1024,512]{2,1,0:T(8,128)(2,1)} %three_ref.1), channel_id=1, source_target_pairs={{0,1},{1,0},{2,3},{3,2},{4,5},{5,4},{6,7},{7,6},{8,9},{9,8},{10,11... | collective-permute-start | bytes 6291464 | tf_op jit(solution)/shard_map/ppermute | solution.py:76
  1.1 0.1 collective-permute-start
  1.2 0.4 collective-permute-start.1
  1.7 2.0 %shard_map.113 = (bf16[528,128]{1,0:T(8,128)(2,1)}, bf16[512,128]{1,0:T(8,128)(2,1)}, f32[8,128]{1,0:T(8,128)}) custom-call(s32[4]{0:T(128)} %owner_hbm.1, s32[2,4]{1,0:T(2,128)} %bitcast.1, s32[4,8]{1,0:T(4,128)} %partner_hbm.1, f32[4,8]{1,0:T(4,128)} %coupling_hbm.1, f32[16]{0:T(128)} %eps_hbm.1, s32[4]{0:T(128)} %nvirt_hbm.1, bf16[4,512,256]{2,1,0:T(8,128)(2,1)} %coeff_ref.11), custom_call_target="tpu_custom_call" | custom-call | flops 1 | bytes 1 | tf_op jit(solution)/shard_map/pallas_call | solution.py:38
  3.7 4.8 %collective-permute-start.2 = (bf16[528,128]{1,0:T(8,128)(2,1)}, bf16[528,128]{1,0:T(8,128)(2,1)S(1)}, u32[]{:S(2)}, u32[]{:S(2)}) collective-permute-start(bf16[528,128]{1,0:T(8,128)(2,1)} %get-tuple-element.28), channel_id=1, source_target_pairs={{0,7},{1,2},{2,1},{3,4},{4,3},{5,6},{6,5},{7,0},{8,15},{9,10},{10,... | collective-permute-start | bytes 405512 | tf_op jit(solution)/shard_map/ppermute | solution.py:79
  8.5 0.1 collective-permute-start.3
  8.6 0.0 copy-start.2
  8.6 0.7 %copy-done.2 = f32[8,128]{1,0:T(8,128)S(1)} copy-done((f32[8,128]{1,0:T(8,128)S(1)}, f32[8,128]{1,0:T(8,128)}, u32[]{:S(2)}) %copy-start.2) | copy-done | bytes 4120
  9.2 1.6 %shard_map.114.three_ref = bf16[2,1024,512]{2,1,0:T(8,128)(2,1)S(1)} custom-call(bf16[2,1024,512]{2,1,0:T(8,128)(2,1)} %three_ref.1, f32[8,128]{1,0:T(8,128)S(1)} %copy-done.2), custom_call_target="tpu_custom_call" | custom-call | flops 1 | bytes 1 | tf_op jit(solution)/shard_map/pallas_call | solution.py:38
  10.8 0.0 copy-start
  10.8 0.0 copy-start.1
  10.9 1.3 %collective-permute-done.2.x_ref.low_ref = bf16[528,128]{1,0:T(8,128)(2,1)S(1)} collective-permute-done((bf16[528,128]{1,0:T(8,128)(2,1)}, bf16[528,128]{1,0:T(8,128)(2,1)S(1)}, u32[]{:S(2)}, u32[]{:S(2)}) %collective-permute-start.2) | collective-permute-done | bytes 135200 | tf_op jit(solution)/shard_map/ppermute | solution.py:79
  12.1 0.5 %shard_map.115.after_ref = bf16[1040,128]{1,0:T(8,128)(2,1)S(1)} custom-call(bf16[2,1024,512]{2,1,0:T(8,128)(2,1)S(1)} %shard_map.114.three_ref, bf16[528,128]{1,0:T(8,128)(2,1)S(1)} %collective-permute-done.2.x_ref.low_ref), custom_call_target="tpu_custom_call" | custom-call | flops 1 | bytes 1 | tf_op jit(solution)/shard_map/pallas_call | solution.py:38
  12.7 0.0 copy-start.6
  12.7 3.2 %collective-permute-start.5 = (bf16[1040,128]{1,0:T(8,128)(2,1)S(1)}, bf16[1040,128]{1,0:T(8,128)(2,1)S(1)}, u32[]{:S(2)}, u32[]{:S(2)}) collective-permute-start(bf16[1040,128]{1,0:T(8,128)(2,1)S(1)} %shard_map.115.after_ref), channel_id=1, source_target_pairs={{0,7},{1,2},{2,1},{3,4},{4,3},{5,6},{6,5},{7,0},{8,15},{9,10},{10,... | collective-permute-start | bytes 798728 | tf_op jit(solution)/shard_map/ppermute | solution.py:79
  15.9 0.0 collective-permute-done.3.x_ref.high_ref
  15.9 0.5 %shard_map.116.after_ref = bf16[1024,128]{1,0:T(8,128)(2,1)S(1)} custom-call(bf16[2,1024,512]{2,1,0:T(8,128)(2,1)S(1)} %shard_map.114.three_ref, bf16[528,128]{1,0:T(8,128)(2,1)S(1)} %collective-permute-done.2.x_ref.low_ref, bf16[512,128]{1,0:T(8,128)(2,1)S(1)} %collective-permute-done.3.x_ref.high_ref, bf16[1040,128]{1,0:T(8,128)(2,1)S(1)} %shard_map.115.after_ref), custom_call_target="tpu_custom_call" | custom-call | flops 1 | bytes 1 | tf_op jit(solution)/shard_map/pallas_call | solution.py:38
  16.4 1.4 %collective-permute-start.6 = (bf16[1024,128]{1,0:T(8,128)(2,1)S(1)}, bf16[1024,128]{1,0:T(8,128)(2,1)S(1)}, u32[]{:S(2)}, u32[]{:S(2)}) collective-permute-start(bf16[1024,128]{1,0:T(8,128)(2,1)S(1)} %shard_map.116.after_ref), channel_id=1, source_target_pairs={{0,7},{1,2},{2,1},{3,4},{4,3},{5,6},{6,5},{7,0},{8,15},{9,10},{10,... | collective-permute-start | bytes 786440 | tf_op jit(solution)/shard_map/ppermute | solution.py:79
  17.8 0.0 copy-done
  17.8 0.0 copy-done.1
  17.8 0.9 %shard_map.117 = (bf16[4,256,256]{2,1,0:T(8,128)(2,1)S(1)}, bf16[272,256]{1,0:T(8,128)(2,1)S(1)}) custom-call(bf16[4,512,256]{2,1,0:T(8,128)(2,1)S(1)} %copy-done, bf16[4,256,256]{2,1,0:T(8,128)(2,1)S(1)} %copy-done.1, bf16[528,128]{1,0:T(8,128)(2,1)S(1)} %collective-permute-done.2.x_ref.low_ref, bf16[512,128]{1,0:T(8,128)(2,1)S(1)} %collective-permute-done.3.x_ref.high_ref, ...), custom_call_target="tpu_custom_call" | custom-call | flops 1 | bytes 1 | tf_op jit(solution)/shard_map/pallas_call | solution.py:38
  18.7 0.0 collective-permute-done.1.amps_in_ref
  18.8 0.0 copy-start.4
  18.8 2.3 %collective-permute-start.7 = (bf16[272,256]{1,0:T(8,128)(2,1)S(1)}, bf16[272,256]{1,0:T(8,128)(2,1)S(1)}, u32[]{:S(2)}, u32[]{:S(2)}) collective-permute-start(bf16[272,256]{1,0:T(8,128)(2,1)S(1)} %get-tuple-element.30.after_ref), channel_id=1, source_target_pairs={{0,7},{1,2},{2,1},{3,4},{4,3},{5,6},{6,5},{7,0},{8,15},{9,10},{10,... | collective-permute-start | bytes 417800 | tf_op jit(solution)/shard_map/ppermute | solution.py:79
  21.0 0.0 collective-permute-done.4.three_in_ref
  21.0 0.0 copy-done.6
  21.0 0.0 copy-start.5
  21.0 0.1 collective-permute-start.8
  21.1 1.3 %copy-done.5 = bf16[2,1024,512]{2,1,0:T(8,128)(2,1)} copy-done((bf16[2,1024,512]{2,1,0:T(8,128)(2,1)}, bf16[2,1024,512]{2,1,0:T(8,128)(2,1)S(1)}, u32[]{:S(2)}) %copy-start.5) | copy-done | bytes 2097176
  22.4 1.8 %shard_map.119 = (bf16[256,1024]{1,0:T(8,128)(2,1)S(1)}, bf16[1024,256]{1,0:T(8,128)(2,1)S(1)}, bf16[512,256]{1,0:T(8,128)(2,1)S(1)}) custom-call(f32[8,128]{1,0:T(8,128)S(1)} %copy-done.2, bf16[2,1024,512]{2,1,0:T(8,128)(2,1)S(1)} %shard_map.114.three_ref, bf16[2,1024,512]{2,1,0:T(8,128)(2,1)} %copy-done.5, bf16[4,512,256]{2,1,0:T(8,128)(2,1)S(1)} %copy-done, ...), custom_call_target="tpu_custom_call" | custom-call | flops 1 | bytes 1 | tf_op jit(solution)/shard_map/pallas_call | solution.py:38
  24.2 0.0 collective-permute-done.coeff_in_ref.in_ref
  24.2 0.2 collective-permute-start.12
  24.4 0.0 copy-done.4
  24.4 1.5 %shard_map.118 = (bf16[4,256,256]{2,1,0:T(8,128)(2,1)S(1)}, f32[256,256]{1,0:T(8,128)S(1)}, f32[256,256]{1,0:T(8,128)S(1)}, f32[256,256]{1,0:T(8,128)S(1)}) custom-call(f32[8,128]{1,0:T(8,128)S(1)} %copy-done.2, bf16[4,512,256]{2,1,0:T(8,128)(2,1)S(1)} %copy-done, bf16[4,512,256]{2,1,0:T(8,128)(2,1)S(1)} %collective-permute-done.coeff_in_ref.in_ref, ...), custom_call_target="tpu_custom_call" | custom-call | flops 1 | bytes 1 | tf_op jit(solution)/shard_map/pallas_call | solution.py:38
  25.9 0.0 collective-permute-done.8.low_ref
  25.9 5.8 %collective-permute-done.7.co_ref = bf16[272,256]{1,0:T(8,128)(2,1)S(1)} collective-permute-done((bf16[272,256]{1,0:T(8,128)(2,1)S(1)}, bf16[272,256]{1,0:T(8,128)(2,1)S(1)}, u32[]{:S(2)}, u32[]{:S(2)}) %collective-permute-start.7) | collective-permute-done | bytes 139296 | tf_op jit(solution)/shard_map/ppermute | solution.py:79
  31.8 0.0 collective-permute-done.6.high_ref
  31.8 0.0 collective-permute-done.5.low_ref
  31.8 0.6 %shard_map.121 = (bf16[256,256]{1,0:T(8,128)(2,1)S(1)}, f32[256,256]{1,0:T(8,128)S(1)}) custom-call(f32[8,128]{1,0:T(8,128)S(1)} %copy-done.2, bf16[256,1024]{1,0:T(8,128)(2,1)S(1)} %get-tuple-element.33.first_ref, bf16[1024,256]{1,0:T(8,128)(2,1)S(1)} %get-tuple-element.34.second_ref, bf16[1040,128]{1,0:T(8,128)(2,1)S(1)} %collective-permute-done.5.low_ref, ...), custom_call_target="tpu_custom_call" | custom-call | flops 1 | bytes 1 | tf_op jit(solution)/shard_map/pallas_call | solution.py:38
  32.4 1.7 %collective-permute-start.9 = (bf16[256,256]{1,0:T(8,128)(2,1)S(1)}, bf16[256,256]{1,0:T(8,128)(2,1)S(1)}, u32[]{:S(2)}, u32[]{:S(2)}) collective-permute-start(bf16[256,256]{1,0:T(8,128)(2,1)S(1)} %get-tuple-element.37.amp_ref.after_ref.refs_0_), channel_id=1, source_target_pairs={{0,8},{8,0},{16,24},{24,16},{1,9},{9,1},{17,25},{25,17},{2,10},{10... | collective-permute-start | bytes 393224 | tf_op jit(solution)/shard_map/ppermute | solution.py:82
  34.0 1.5 %collective-permute-start.10 = (bf16[256,256]{1,0:T(8,128)(2,1)S(1)}, bf16[256,256]{1,0:T(8,128)(2,1)S(1)}, u32[]{:S(2)}, u32[]{:S(2)}) collective-permute-start(bf16[256,256]{1,0:T(8,128)(2,1)S(1)} %get-tuple-element.37.amp_ref.after_ref.refs_0_), channel_id=1, source_target_pairs={{0,16},{8,24},{16,0},{24,8},{1,17},{9,25},{17,1},{25,9},{2,18},{10... | collective-permute-start | bytes 393224 | tf_op jit(solution)/shard_map/ppermute | solution.py:82
  35.6 0.4 collective-permute-start.11
  35.9 0.4 shard_map.122
  36.3 3.5 %collective-permute-start.16 = (bf16[272,256]{1,0:T(8,128)(2,1)S(1)}, bf16[272,256]{1,0:T(8,128)(2,1)S(1)}, u32[]{:S(2)}, u32[]{:S(2)}) collective-permute-start(bf16[272,256]{1,0:T(8,128)(2,1)S(1)} %get-tuple-element.49.held_ref), channel_id=1, source_target_pairs={{0,8},{1,9},{2,10},{3,11},{4,12},{5,13},{6,14},{7,15}} | collective-permute-start | bytes 417800 | tf_op jit(solution)/shard_map/ppermute | solution.py:440
  39.9 0.0 collective-permute-done.12.x_ref
  39.9 0.0 collective-permute-done.9.refs_1_
  39.9 0.0 copy-start.3
  39.9 0.0 collective-permute-done.10.refs_0_.refs_2_
  40.0 1.5 %collective-permute-done.11.refs_1_.refs_3_ = bf16[256,256]{1,0:T(8,128)(2,1)S(1)} collective-permute-done((bf16[256,256]{1,0:T(8,128)(2,1)S(1)}, bf16[256,256]{1,0:T(8,128)(2,1)S(1)}, u32[]{:S(2)}, u32[]{:S(2)}) %collective-permute-start.11) | collective-permute-done | bytes 131104 | tf_op jit(solution)/shard_map/ppermute | solution.py:82
  41.4 0.3 collective-permute-start.13
  41.7 0.8 %collective-permute-done.16.come_ref.refs_0_ = bf16[272,256]{1,0:T(8,128)(2,1)S(1)} collective-permute-done((bf16[272,256]{1,0:T(8,128)(2,1)S(1)}, bf16[272,256]{1,0:T(8,128)(2,1)S(1)}, u32[]{:S(2)}, u32[]{:S(2)}) %collective-permute-start.16) | collective-permute-done | bytes 139296 | tf_op jit(solution)/shard_map/ppermute | solution.py:440
  42.5 3.0 %collective-permute-start.17 = (bf16[272,256]{1,0:T(8,128)(2,1)S(1)}, bf16[272,256]{1,0:T(8,128)(2,1)S(1)}, u32[]{:S(2)}, u32[]{:S(2)}) collective-permute-start(bf16[272,256]{1,0:T(8,128)(2,1)S(1)} %shard_map.128), channel_id=1, source_target_pairs={{0,16},{8,24},{1,17},{9,25},{2,18},{10,26},{3,19},{11,27},{4,20},{... | collective-permute-start | bytes 417800 | tf_op jit(solution)/shard_map/ppermute | solution.py:440
  45.4 0.1 collective-permute-start.14
  45.5 0.5 %collective-permute-start.15 = (bf16[256,256]{1,0:T(8,128)(2,1)S(1)}, bf16[256,256]{1,0:T(8,128)(2,1)S(1)}, u32[]{:S(2)}, u32[]{:S(2)}) collective-permute-start(bf16[256,256]{1,0:T(8,128)(2,1)S(1)} %get-tuple-element.48), channel_id=1, source_target_pairs={{0,1},{1,0},{2,3},{3,2},{4,5},{5,4},{6,7},{7,6},{8,9},{9,8},{10,11... | collective-permute-start | bytes 393224 | tf_op jit(solution)/shard_map/ppermute | solution.py:76
  46.0 1.5 %shard_map.129 = (bf16[2,256,256]{2,1,0:T(8,128)(2,1)}, bf16[2,512,256]{2,1,0:T(8,128)(2,1)}) custom-call(f32[8,128]{1,0:T(8,128)S(1)} %copy-done.2, bf16[256,256]{1,0:T(8,128)(2,1)S(1)} %get-tuple-element.45.refs_4_.after_ref), custom_call_target="tpu_custom_call" | custom-call | flops 1 | bytes 1 | tf_op jit(solution)/shard_map/pallas_call | solution.py:38
  47.6 0.0 copy-done.3
  47.6 0.4 collective-permute-done.17.refs_1_
  48.0 0.0 collective-permute-done.14.ci_ref
  48.0 0.0 collective-permute-done.15.cei_ref
  48.0 1.0 %collective-permute-done.13.co_ref = bf16[2,256,256]{2,1,0:T(8,128)(2,1)S(1)} collective-permute-done((bf16[2,256,256]{2,1,0:T(8,128)(2,1)S(1)}, bf16[2,256,256]{2,1,0:T(8,128)(2,1)S(1)}, u32[]{:S(2)}, u32[]{:S(2)}) %collective-permute-start.13) | collective-permute-done | bytes 262176 | tf_op jit(solution)/shard_map/ppermute | solution.py:79
  49.0 0.2 shard_map.130
  (7 shorter events, 0.1 us)
Async XLA Ops:
  0.6 20.4 %collective-permute-start.4 = (bf16[2,1024,512]{2,1,0:T(8,128)(2,1)}, bf16[2,1024,512]{2,1,0:T(8,128)(2,1)S(1)}, u32[]{:S(2)}, u32[]{:S(2)}) collective-permute-start(bf16[2,1024,512]{2,1,0:T(8,128)(2,1)} %three_ref.1), channel_id=1, source_target_pairs={{0,1},{1,0},{2,3},{3,2},{4,5},{5,4},{6,7},{7,6},{8,9},{9,8},{10,11... | collective-permute-start | bytes 6291464 | tf_op jit(solution)/shard_map/ppermute | solution.py:76
  1.1 23.0 %collective-permute-start = (bf16[4,512,256]{2,1,0:T(8,128)(2,1)}, bf16[4,512,256]{2,1,0:T(8,128)(2,1)S(1)}, u32[]{:S(2)}, u32[]{:S(2)}) collective-permute-start(bf16[4,512,256]{2,1,0:T(8,128)(2,1)} %coeff_ref.11), channel_id=1, source_target_pairs={{0,1},{1,0},{2,3},{3,2},{4,5},{5,4},{6,7},{7,6},{8,9},{9,8},{10,11... | collective-permute-start | bytes 3145736 | tf_op jit(solution)/shard_map/ppermute | solution.py:76
  1.2 17.5 %collective-permute-start.1 = (bf16[4,256,256]{2,1,0:T(8,128)(2,1)}, bf16[4,256,256]{2,1,0:T(8,128)(2,1)S(1)}, u32[]{:S(2)}, u32[]{:S(2)}) collective-permute-start(bf16[4,256,256]{2,1,0:T(8,128)(2,1)} %amps_ref.5), channel_id=1, source_target_pairs={{0,1},{1,0},{2,3},{3,2},{4,5},{5,4},{6,7},{7,6},{8,9},{9,8},{10,11... | collective-permute-start | bytes 1572872 | tf_op jit(solution)/shard_map/ppermute | solution.py:76
  3.7 8.4 %collective-permute-start.2 = (bf16[528,128]{1,0:T(8,128)(2,1)}, bf16[528,128]{1,0:T(8,128)(2,1)S(1)}, u32[]{:S(2)}, u32[]{:S(2)}) collective-permute-start(bf16[528,128]{1,0:T(8,128)(2,1)} %get-tuple-element.28), channel_id=1, source_target_pairs={{0,7},{1,2},{2,1},{3,4},{4,3},{5,6},{6,5},{7,0},{8,15},{9,10},{10,... | collective-permute-start | bytes 405512 | tf_op jit(solution)/shard_map/ppermute | solution.py:79
  8.5 7.4 %collective-permute-start.3 = (bf16[512,128]{1,0:T(8,128)(2,1)}, bf16[512,128]{1,0:T(8,128)(2,1)S(1)}, u32[]{:S(2)}, u32[]{:S(2)}) collective-permute-start(bf16[512,128]{1,0:T(8,128)(2,1)} %get-tuple-element.29), channel_id=1, source_target_pairs={{0,7},{1,2},{2,1},{3,4},{4,3},{5,6},{6,5},{7,0},{8,15},{9,10},{10,... | collective-permute-start | bytes 393224 | tf_op jit(solution)/shard_map/ppermute | solution.py:79
  8.6 0.7 %copy-start.2 = (f32[8,128]{1,0:T(8,128)S(1)}, f32[8,128]{1,0:T(8,128)}, u32[]{:S(2)}) copy-start(f32[8,128]{1,0:T(8,128)} %get-tuple-element.27.after_ref.nums) | copy-start | bytes 12292
  10.8 7.0 %copy-start = (bf16[4,512,256]{2,1,0:T(8,128)(2,1)S(1)}, bf16[4,512,256]{2,1,0:T(8,128)(2,1)}, u32[]{:S(2)}) copy-start(bf16[4,512,256]{2,1,0:T(8,128)(2,1)} %coeff_ref.11) | copy-start | bytes 3145732
  10.8 7.0 %copy-start.1 = (bf16[4,256,256]{2,1,0:T(8,128)(2,1)S(1)}, bf16[4,256,256]{2,1,0:T(8,128)(2,1)}, u32[]{:S(2)}) copy-start(bf16[4,256,256]{2,1,0:T(8,128)(2,1)} %amps_ref.5) | copy-start | bytes 1572868
  12.7 8.4 %copy-start.6 = (bf16[528,128]{1,0:T(8,128)(2,1)S(1)}, bf16[528,128]{1,0:T(8,128)(2,1)}, u32[]{:S(2)}) copy-start(bf16[528,128]{1,0:T(8,128)(2,1)} %get-tuple-element.28) | copy-start | bytes 405508
  12.7 19.1 %collective-permute-start.5 = (bf16[1040,128]{1,0:T(8,128)(2,1)S(1)}, bf16[1040,128]{1,0:T(8,128)(2,1)S(1)}, u32[]{:S(2)}, u32[]{:S(2)}) collective-permute-start(bf16[1040,128]{1,0:T(8,128)(2,1)S(1)} %shard_map.115.after_ref), channel_id=1, source_target_pairs={{0,7},{1,2},{2,1},{3,4},{4,3},{5,6},{6,5},{7,0},{8,15},{9,10},{10,... | collective-permute-start | bytes 798728 | tf_op jit(solution)/shard_map/ppermute | solution.py:79
  16.4 15.4 %collective-permute-start.6 = (bf16[1024,128]{1,0:T(8,128)(2,1)S(1)}, bf16[1024,128]{1,0:T(8,128)(2,1)S(1)}, u32[]{:S(2)}, u32[]{:S(2)}) collective-permute-start(bf16[1024,128]{1,0:T(8,128)(2,1)S(1)} %shard_map.116.after_ref), channel_id=1, source_target_pairs={{0,7},{1,2},{2,1},{3,4},{4,3},{5,6},{6,5},{7,0},{8,15},{9,10},{10,... | collective-permute-start | bytes 786440 | tf_op jit(solution)/shard_map/ppermute | solution.py:79
  18.8 5.7 %copy-start.4 = (f32[4,256]{1,0:T(4,128)S(1)}, f32[4,256]{1,0:T(4,128)}, u32[]{:S(2)}) copy-start(f32[4,256]{1,0:T(4,128)} %eps_ref.1) | copy-start | bytes 12292
  18.8 13.0 %collective-permute-start.7 = (bf16[272,256]{1,0:T(8,128)(2,1)S(1)}, bf16[272,256]{1,0:T(8,128)(2,1)S(1)}, u32[]{:S(2)}, u32[]{:S(2)}) collective-permute-start(bf16[272,256]{1,0:T(8,128)(2,1)S(1)} %get-tuple-element.30.after_ref), channel_id=1, source_target_pairs={{0,7},{1,2},{2,1},{3,4},{4,3},{5,6},{6,5},{7,0},{8,15},{9,10},{10,... | collective-permute-start | bytes 417800 | tf_op jit(solution)/shard_map/ppermute | solution.py:79
  21.0 1.4 %copy-start.5 = (bf16[2,1024,512]{2,1,0:T(8,128)(2,1)}, bf16[2,1024,512]{2,1,0:T(8,128)(2,1)S(1)}, u32[]{:S(2)}) copy-start(bf16[2,1024,512]{2,1,0:T(8,128)(2,1)S(1)} %collective-permute-done.4.three_in_ref) | copy-start | bytes 6291460
  21.0 4.9 %collective-permute-start.8 = (bf16[528,128]{1,0:T(8,128)(2,1)S(1)}, bf16[528,128]{1,0:T(8,128)(2,1)S(1)}, u32[]{:S(2)}, u32[]{:S(2)}) collective-permute-start(bf16[528,128]{1,0:T(8,128)(2,1)S(1)} %copy-done.6), channel_id=1, source_target_pairs={{0,1},{1,0},{2,3},{3,2},{4,5},{5,4},{6,7},{7,6},{8,9},{9,8},{10,11... | collective-permute-start | bytes 405512 | tf_op jit(solution)/shard_map/ppermute | solution.py:76
  24.2 15.7 %collective-permute-start.12 = (bf16[512,256]{1,0:T(8,128)(2,1)S(1)}, bf16[512,256]{1,0:T(8,128)(2,1)S(1)}, u32[]{:S(2)}, u32[]{:S(2)}) collective-permute-start(bf16[512,256]{1,0:T(8,128)(2,1)S(1)} %get-tuple-element.44), channel_id=1, source_target_pairs={{0,7},{1,2},{2,1},{3,4},{4,3},{5,6},{6,5},{7,0},{8,15},{9,10},{10,... | collective-permute-start | bytes 786440 | tf_op jit(solution)/shard_map/ppermute | solution.py:79
  32.4 7.5 %collective-permute-start.9 = (bf16[256,256]{1,0:T(8,128)(2,1)S(1)}, bf16[256,256]{1,0:T(8,128)(2,1)S(1)}, u32[]{:S(2)}, u32[]{:S(2)}) collective-permute-start(bf16[256,256]{1,0:T(8,128)(2,1)S(1)} %get-tuple-element.37.amp_ref.after_ref.refs_0_), channel_id=1, source_target_pairs={{0,8},{8,0},{16,24},{24,16},{1,9},{9,1},{17,25},{25,17},{2,10},{10... | collective-permute-start | bytes 393224 | tf_op jit(solution)/shard_map/ppermute | solution.py:82
  34.0 5.9 %collective-permute-start.10 = (bf16[256,256]{1,0:T(8,128)(2,1)S(1)}, bf16[256,256]{1,0:T(8,128)(2,1)S(1)}, u32[]{:S(2)}, u32[]{:S(2)}) collective-permute-start(bf16[256,256]{1,0:T(8,128)(2,1)S(1)} %get-tuple-element.37.amp_ref.after_ref.refs_0_), channel_id=1, source_target_pairs={{0,16},{8,24},{16,0},{24,8},{1,17},{9,25},{17,1},{25,9},{2,18},{10... | collective-permute-start | bytes 393224 | tf_op jit(solution)/shard_map/ppermute | solution.py:82
  35.6 5.9 %collective-permute-start.11 = (bf16[256,256]{1,0:T(8,128)(2,1)S(1)}, bf16[256,256]{1,0:T(8,128)(2,1)S(1)}, u32[]{:S(2)}, u32[]{:S(2)}) collective-permute-start(bf16[256,256]{1,0:T(8,128)(2,1)S(1)} %get-tuple-element.37.amp_ref.after_ref.refs_0_), channel_id=1, source_target_pairs={{0,24},{8,16},{16,8},{24,0},{1,25},{9,17},{17,9},{25,1},{2,26},{10... | collective-permute-start | bytes 393224 | tf_op jit(solution)/shard_map/ppermute | solution.py:82
  36.3 6.1 %collective-permute-start.16 = (bf16[272,256]{1,0:T(8,128)(2,1)S(1)}, bf16[272,256]{1,0:T(8,128)(2,1)S(1)}, u32[]{:S(2)}, u32[]{:S(2)}) collective-permute-start(bf16[272,256]{1,0:T(8,128)(2,1)S(1)} %get-tuple-element.49.held_ref), channel_id=1, source_target_pairs={{0,8},{1,9},{2,10},{3,11},{4,12},{5,13},{6,14},{7,15}} | collective-permute-start | bytes 417800 | tf_op jit(solution)/shard_map/ppermute | solution.py:440
  39.9 7.6 %copy-start.3 = (f32[8,128]{1,0:T(8,128)S(1)}, f32[8,128]{1,0:T(8,128)}, u32[]{:S(2)}) copy-start(f32[8,128]{1,0:T(8,128)} %get-tuple-element.27.after_ref.nums) | copy-start | bytes 12292
  41.4 7.6 %collective-permute-start.13 = (bf16[2,256,256]{2,1,0:T(8,128)(2,1)S(1)}, bf16[2,256,256]{2,1,0:T(8,128)(2,1)S(1)}, u32[]{:S(2)}, u32[]{:S(2)}) collective-permute-start(bf16[2,256,256]{2,1,0:T(8,128)(2,1)S(1)} %shard_map.125.refs_4_), channel_id=1, source_target_pairs={{0,7},{1,2},{2,1},{3,4},{4,3},{5,6},{6,5},{7,0},{8,15},{9,10},{10,... | collective-permute-start | bytes 786440 | tf_op jit(solution)/shard_map/ppermute | solution.py:79
  42.5 5.5 %collective-permute-start.17 = (bf16[272,256]{1,0:T(8,128)(2,1)S(1)}, bf16[272,256]{1,0:T(8,128)(2,1)S(1)}, u32[]{:S(2)}, u32[]{:S(2)}) collective-permute-start(bf16[272,256]{1,0:T(8,128)(2,1)S(1)} %shard_map.128), channel_id=1, source_target_pairs={{0,16},{8,24},{1,17},{9,25},{2,18},{10,26},{3,19},{11,27},{4,20},{... | collective-permute-start | bytes 417800 | tf_op jit(solution)/shard_map/ppermute | solution.py:440
  45.4 2.5 %collective-permute-start.14 = (bf16[256,256]{1,0:T(8,128)(2,1)S(1)}, bf16[256,256]{1,0:T(8,128)(2,1)S(1)}, u32[]{:S(2)}, u32[]{:S(2)}) collective-permute-start(bf16[256,256]{1,0:T(8,128)(2,1)S(1)} %get-tuple-element.45.refs_4_.after_ref), channel_id=1, source_target_pairs={{0,1},{1,0},{2,3},{3,2},{4,5},{5,4},{6,7},{7,6},{8,9},{9,8},{10,11... | collective-permute-start | bytes 393224 | tf_op jit(solution)/shard_map/ppermute | solution.py:76
  45.5 2.5 %collective-permute-start.15 = (bf16[256,256]{1,0:T(8,128)(2,1)S(1)}, bf16[256,256]{1,0:T(8,128)(2,1)S(1)}, u32[]{:S(2)}, u32[]{:S(2)}) collective-permute-start(bf16[256,256]{1,0:T(8,128)(2,1)S(1)} %get-tuple-element.48), channel_id=1, source_target_pairs={{0,1},{1,0},{2,3},{3,2},{4,5},{5,4},{6,7},{7,6},{8,9},{9,8},{10,11... | collective-permute-start | bytes 393224 | tf_op jit(solution)/shard_map/ppermute | solution.py:76

commit v23 on v22

--- a/solution.py
+++ b/solution.py
@@ -77,6 +77,14 @@
 
     def outer(x):
         return lax.ppermute(x, "pairs", list(enumerate(outer_of)))
+
+    def outer_for_owners(x):
+        pairings = [
+            (s * columns + i, s * columns + j)
+            for s in range(roles)
+            for i, j in enumerate(outer_of if s else inner_of)
+        ]
+        return lax.ppermute(x, ("role", "pairs"), pairings)
 
     def swap(x, by):
         return lax.ppermute(x, "role", [(i, i ^ by) for i in range(roles)])
@@ -488,7 +496,7 @@
         return c
 
     cc_out = outer_again(roles // 2, roles, BF16, outer_again(0, roles // 2, F32))
-    cc_from_out = outer(cc_out)
+    cc_from_out = outer_for_owners(cc_out)
 
     def inner_again_body(nums, low_ref, s_ref, se_ref, *refs):
         amp_refs, c_refs = refs[:roles], refs[-2:]

time: 49.4 us -> 49.2 us (level); the launches traced: 49.2 us -> 48.3 us
  starting transfers between devices: 24 us -> 26.1 us
  waiting for transfers between devices: 10.8 us -> 8.87 us
  Pallas kernels: 11.6 us -> 10.5 us
    ppermute x7 -> x6, waiting for transfers between devices: 8.15 us -> 5.96 us  [outer(): return lax.ppermute(x, 'pairs', list(enumerate(outer_of)))]
    ppermute x7 -> x6, starting transfers between devices: 12.3 us -> 14.4 us  [outer(): return lax.ppermute(x, 'pairs', list(enumerate(outer_of)))]
    pallas_call x18, Pallas kernels: 11.6 us -> 10.5 us  [call(): pl.pallas_call(body, in_specs=ins, out_specs=[spec for spec, _, _ in outs...]
  transfers between devices with their start and end apart: 18 -> 18, of which waited for: 6 -> 5; matrix products, arithmetic and copies ran while one was open for 0% -> 0% of each run, Pallas kernels for 23% -> 21%
where the time goes in v23:
time: 49.2 us; the launch traced here: 48.3 us
  starting transfers between devices  26.1 us (53%)
  Pallas kernels  10.5 us (21%)
  waiting for transfers between devices  8.87 us (18%)
  local copies, waits for them, and re-layouts  1.98 us (4%)
  between operations  0.89 us (2%)
    ppermute x6, starting transfers between devices, outer(): return lax.ppermute(x, 'pairs', list(enumerate(outer_of)))  14.4 us
    pallas_call x18, Pallas kernels, call(): pl.pallas_call(body, in_specs=ins, out_specs=[spec for spec, _, _ in outs...  10.5 us
    ppermute x2, starting transfers between devices, local(): lax.ppermute(held, 'role', [(i, i + step) for i in range(step)])  6.51 us
    ppermute x6, waiting for transfers between devices, outer(): return lax.ppermute(x, 'pairs', list(enumerate(outer_of)))  5.96 us
    ppermute x3, starting transfers between devices, swap(): return lax.ppermute(x, 'role', [(i, i ^ by) for i in range(roles)])  3.55 us
    unnamed x14, local copies, waits for them, and re-layouts  1.98 us
    ppermute x6, starting transfers between devices, inner(): return lax.ppermute(x, 'pairs', list(enumerate(inner_of)))  1.66 us
    ppermute x3, waiting for transfers between devices, swap(): return lax.ppermute(x, 'role', [(i, i ^ by) for i in range(roles)])  1.48 us
  transfers between devices with their start and end apart: 18, of which 5 were waited for; matrix products, arithmetic and copies ran while one was open for 0% of the time, Pallas kernels for 21%

profile of v23, /device:TPU:0, one launch (start us, length us, event | category | flops | bytes accessed | tf_op | source)
XLA Modules:
  0.0 48.3 jit_solution(11166012845866203991)
XLA Ops:
  0.6 0.5 %collective-permute-start.4 = (bf16[2,1024,512]{2,1,0:T(8,128)(2,1)}, bf16[2,1024,512]{2,1,0:T(8,128)(2,1)S(1)}, u32[]{:S(2)}, u32[]{:S(2)}) collective-permute-start(bf16[2,1024,512]{2,1,0:T(8,128)(2,1)} %three_ref.1), channel_id=1, source_target_pairs={{0,1},{1,0},{2,3},{3,2},{4,5},{5,4},{6,7},{7,6},{8,9},{9,8},{10,11... | collective-permute-start | bytes 6291464 | tf_op jit(solution)/shard_map/ppermute | solution.py:76
  1.1 0.1 collective-permute-start
  1.2 0.4 collective-permute-start.1
  1.7 2.0 %shard_map.113 = (bf16[528,128]{1,0:T(8,128)(2,1)}, bf16[512,128]{1,0:T(8,128)(2,1)}, f32[8,128]{1,0:T(8,128)}) custom-call(s32[4]{0:T(128)} %owner_hbm.1, s32[2,4]{1,0:T(2,128)} %bitcast.1, s32[4,8]{1,0:T(4,128)} %partner_hbm.1, f32[4,8]{1,0:T(4,128)} %coupling_hbm.1, f32[16]{0:T(128)} %eps_hbm.1, s32[4]{0:T(128)} %nvirt_hbm.1, bf16[4,512,256]{2,1,0:T(8,128)(2,1)} %coeff_ref.11), custom_call_target="tpu_custom_call" | custom-call | flops 1 | bytes 1 | tf_op jit(solution)/shard_map/pallas_call | solution.py:38
  3.7 4.8 %collective-permute-start.2 = (bf16[528,128]{1,0:T(8,128)(2,1)}, bf16[528,128]{1,0:T(8,128)(2,1)S(1)}, u32[]{:S(2)}, u32[]{:S(2)}) collective-permute-start(bf16[528,128]{1,0:T(8,128)(2,1)} %get-tuple-element.28), channel_id=1, source_target_pairs={{0,7},{1,2},{2,1},{3,4},{4,3},{5,6},{6,5},{7,0},{8,15},{9,10},{10,... | collective-permute-start | bytes 405512 | tf_op jit(solution)/shard_map/ppermute | solution.py:79
  8.5 0.1 collective-permute-start.3
  8.6 0.0 copy-start.2
  8.6 0.7 %copy-done.2 = f32[8,128]{1,0:T(8,128)S(1)} copy-done((f32[8,128]{1,0:T(8,128)S(1)}, f32[8,128]{1,0:T(8,128)}, u32[]{:S(2)}) %copy-start.2) | copy-done | bytes 4120
  9.2 1.6 %shard_map.114.three_ref = bf16[2,1024,512]{2,1,0:T(8,128)(2,1)S(1)} custom-call(bf16[2,1024,512]{2,1,0:T(8,128)(2,1)} %three_ref.1, f32[8,128]{1,0:T(8,128)S(1)} %copy-done.2), custom_call_target="tpu_custom_call" | custom-call | flops 1 | bytes 1 | tf_op jit(solution)/shard_map/pallas_call | solution.py:38
  10.8 0.0 copy-start
  10.8 0.0 copy-start.1
  10.9 1.3 %collective-permute-done.2.x_ref.low_ref = bf16[528,128]{1,0:T(8,128)(2,1)S(1)} collective-permute-done((bf16[528,128]{1,0:T(8,128)(2,1)}, bf16[528,128]{1,0:T(8,128)(2,1)S(1)}, u32[]{:S(2)}, u32[]{:S(2)}) %collective-permute-start.2) | collective-permute-done | bytes 135200 | tf_op jit(solution)/shard_map/ppermute | solution.py:79
  12.1 0.5 %shard_map.115.after_ref = bf16[1040,128]{1,0:T(8,128)(2,1)S(1)} custom-call(bf16[2,1024,512]{2,1,0:T(8,128)(2,1)S(1)} %shard_map.114.three_ref, bf16[528,128]{1,0:T(8,128)(2,1)S(1)} %collective-permute-done.2.x_ref.low_ref), custom_call_target="tpu_custom_call" | custom-call | flops 1 | bytes 1 | tf_op jit(solution)/shard_map/pallas_call | solution.py:38
  12.7 0.0 copy-start.6
  12.7 3.2 %collective-permute-start.5 = (bf16[1040,128]{1,0:T(8,128)(2,1)S(1)}, bf16[1040,128]{1,0:T(8,128)(2,1)S(1)}, u32[]{:S(2)}, u32[]{:S(2)}) collective-permute-start(bf16[1040,128]{1,0:T(8,128)(2,1)S(1)} %shard_map.115.after_ref), channel_id=1, source_target_pairs={{0,7},{1,2},{2,1},{3,4},{4,3},{5,6},{6,5},{7,0},{8,15},{9,10},{10,... | collective-permute-start | bytes 798728 | tf_op jit(solution)/shard_map/ppermute | solution.py:79
  15.9 0.0 collective-permute-done.3.x_ref.high_ref
  15.9 0.5 %shard_map.116.after_ref = bf16[1024,128]{1,0:T(8,128)(2,1)S(1)} custom-call(bf16[2,1024,512]{2,1,0:T(8,128)(2,1)S(1)} %shard_map.114.three_ref, bf16[528,128]{1,0:T(8,128)(2,1)S(1)} %collective-permute-done.2.x_ref.low_ref, bf16[512,128]{1,0:T(8,128)(2,1)S(1)} %collective-permute-done.3.x_ref.high_ref, bf16[1040,128]{1,0:T(8,128)(2,1)S(1)} %shard_map.115.after_ref), custom_call_target="tpu_custom_call" | custom-call | flops 1 | bytes 1 | tf_op jit(solution)/shard_map/pallas_call | solution.py:38
  16.4 1.4 %collective-permute-start.6 = (bf16[1024,128]{1,0:T(8,128)(2,1)S(1)}, bf16[1024,128]{1,0:T(8,128)(2,1)S(1)}, u32[]{:S(2)}, u32[]{:S(2)}) collective-permute-start(bf16[1024,128]{1,0:T(8,128)(2,1)S(1)} %shard_map.116.after_ref), channel_id=1, source_target_pairs={{0,7},{1,2},{2,1},{3,4},{4,3},{5,6},{6,5},{7,0},{8,15},{9,10},{10,... | collective-permute-start | bytes 786440 | tf_op jit(solution)/shard_map/ppermute | solution.py:79
  17.8 0.0 copy-done
  17.8 0.0 copy-done.1
  17.8 0.9 %shard_map.117 = (bf16[4,256,256]{2,1,0:T(8,128)(2,1)S(1)}, bf16[272,256]{1,0:T(8,128)(2,1)S(1)}) custom-call(bf16[4,512,256]{2,1,0:T(8,128)(2,1)S(1)} %copy-done, bf16[4,256,256]{2,1,0:T(8,128)(2,1)S(1)} %copy-done.1, bf16[528,128]{1,0:T(8,128)(2,1)S(1)} %collective-permute-done.2.x_ref.low_ref, bf16[512,128]{1,0:T(8,128)(2,1)S(1)} %collective-permute-done.3.x_ref.high_ref, ...), custom_call_target="tpu_custom_call" | custom-call | flops 1 | bytes 1 | tf_op jit(solution)/shard_map/pallas_call | solution.py:38
  18.7 0.0 collective-permute-done.1.amps_in_ref
  18.8 0.0 copy-start.4
  18.8 2.3 %collective-permute-start.7 = (bf16[272,256]{1,0:T(8,128)(2,1)S(1)}, bf16[272,256]{1,0:T(8,128)(2,1)S(1)}, u32[]{:S(2)}, u32[]{:S(2)}) collective-permute-start(bf16[272,256]{1,0:T(8,128)(2,1)S(1)} %get-tuple-element.30.after_ref), channel_id=1, source_target_pairs={{0,7},{1,2},{2,1},{3,4},{4,3},{5,6},{6,5},{7,0},{8,15},{9,10},{10,... | collective-permute-start | bytes 417800 | tf_op jit(solution)/shard_map/ppermute | solution.py:79
  21.0 0.0 collective-permute-done.4.three_in_ref
  21.0 0.0 copy-done.6
  21.0 0.0 copy-start.5
  21.0 0.1 collective-permute-start.8
  21.1 1.3 %copy-done.5 = bf16[2,1024,512]{2,1,0:T(8,128)(2,1)} copy-done((bf16[2,1024,512]{2,1,0:T(8,128)(2,1)}, bf16[2,1024,512]{2,1,0:T(8,128)(2,1)S(1)}, u32[]{:S(2)}) %copy-start.5) | copy-done | bytes 2097176
  22.4 0.6 %shard_map.119 = (bf16[256,1024]{1,0:T(8,128)(2,1)S(1)}, bf16[1024,256]{1,0:T(8,128)(2,1)S(1)}, bf16[512,256]{1,0:T(8,128)(2,1)S(1)}) custom-call(f32[8,128]{1,0:T(8,128)S(1)} %copy-done.2, bf16[2,1024,512]{2,1,0:T(8,128)(2,1)S(1)} %shard_map.114.three_ref, bf16[2,1024,512]{2,1,0:T(8,128)(2,1)} %copy-done.5, bf16[4,512,256]{2,1,0:T(8,128)(2,1)S(1)} %copy-done, ...), custom_call_target="tpu_custom_call" | custom-call | flops 1 | bytes 1 | tf_op jit(solution)/shard_map/pallas_call | solution.py:38
  23.0 0.0 collective-permute-done.coeff_in_ref.in_ref
  23.0 2.6 %collective-permute-start.12 = (bf16[512,256]{1,0:T(8,128)(2,1)S(1)}, bf16[512,256]{1,0:T(8,128)(2,1)S(1)}, u32[]{:S(2)}, u32[]{:S(2)}) collective-permute-start(bf16[512,256]{1,0:T(8,128)(2,1)S(1)} %get-tuple-element.44), channel_id=1, source_target_pairs={{0,7},{1,2},{2,1},{3,4},{4,3},{5,6},{6,5},{7,0},{8,15},{9,10},{10,... | collective-permute-start | bytes 786440 | tf_op jit(solution)/shard_map/ppermute | solution.py:79
  25.6 0.0 copy-done.4
  25.6 1.5 %shard_map.118 = (bf16[4,256,256]{2,1,0:T(8,128)(2,1)S(1)}, f32[256,256]{1,0:T(8,128)S(1)}, f32[256,256]{1,0:T(8,128)S(1)}, f32[256,256]{1,0:T(8,128)S(1)}) custom-call(f32[8,128]{1,0:T(8,128)S(1)} %copy-done.2, bf16[4,512,256]{2,1,0:T(8,128)(2,1)S(1)} %copy-done, bf16[4,512,256]{2,1,0:T(8,128)(2,1)S(1)} %collective-permute-done.coeff_in_ref.in_ref, ...), custom_call_target="tpu_custom_call" | custom-call | flops 1 | bytes 1 | tf_op jit(solution)/shard_map/pallas_call | solution.py:38
  27.1 0.0 collective-permute-done.8.low_ref
  27.1 4.7 %collective-permute-done.7.co_ref = bf16[272,256]{1,0:T(8,128)(2,1)S(1)} collective-permute-done((bf16[272,256]{1,0:T(8,128)(2,1)S(1)}, bf16[272,256]{1,0:T(8,128)(2,1)S(1)}, u32[]{:S(2)}, u32[]{:S(2)}) %collective-permute-start.7) | collective-permute-done | bytes 139296 | tf_op jit(solution)/shard_map/ppermute | solution.py:79
  31.8 0.0 collective-permute-done.6.high_ref
  31.8 0.0 collective-permute-done.5.low_ref
  31.8 0.7 %shard_map.121 = (bf16[256,256]{1,0:T(8,128)(2,1)S(1)}, f32[256,256]{1,0:T(8,128)S(1)}) custom-call(f32[8,128]{1,0:T(8,128)S(1)} %copy-done.2, bf16[256,1024]{1,0:T(8,128)(2,1)S(1)} %get-tuple-element.33.first_ref, bf16[1024,256]{1,0:T(8,128)(2,1)S(1)} %get-tuple-element.34.second_ref, bf16[1040,128]{1,0:T(8,128)(2,1)S(1)} %collective-permute-done.5.low_ref, ...), custom_call_target="tpu_custom_call" | custom-call | flops 1 | bytes 1 | tf_op jit(solution)/shard_map/pallas_call | solution.py:38
  32.5 1.5 %collective-permute-start.9 = (bf16[256,256]{1,0:T(8,128)(2,1)S(1)}, bf16[256,256]{1,0:T(8,128)(2,1)S(1)}, u32[]{:S(2)}, u32[]{:S(2)}) collective-permute-start(bf16[256,256]{1,0:T(8,128)(2,1)S(1)} %get-tuple-element.37.amp_ref.after_ref.refs_0_), channel_id=1, source_target_pairs={{0,8},{8,0},{16,24},{24,16},{1,9},{9,1},{17,25},{25,17},{2,10},{10... | collective-permute-start | bytes 393224 | tf_op jit(solution)/shard_map/ppermute | solution.py:90
  33.9 1.5 %collective-permute-start.10 = (bf16[256,256]{1,0:T(8,128)(2,1)S(1)}, bf16[256,256]{1,0:T(8,128)(2,1)S(1)}, u32[]{:S(2)}, u32[]{:S(2)}) collective-permute-start(bf16[256,256]{1,0:T(8,128)(2,1)S(1)} %get-tuple-element.37.amp_ref.after_ref.refs_0_), channel_id=1, source_target_pairs={{0,16},{8,24},{16,0},{24,8},{1,17},{9,25},{17,1},{25,9},{2,18},{10... | collective-permute-start | bytes 393224 | tf_op jit(solution)/shard_map/ppermute | solution.py:90
  35.5 0.6 %collective-permute-start.11 = (bf16[256,256]{1,0:T(8,128)(2,1)S(1)}, bf16[256,256]{1,0:T(8,128)(2,1)S(1)}, u32[]{:S(2)}, u32[]{:S(2)}) collective-permute-start(bf16[256,256]{1,0:T(8,128)(2,1)S(1)} %get-tuple-element.37.amp_ref.after_ref.refs_0_), channel_id=1, source_target_pairs={{0,24},{8,16},{16,8},{24,0},{1,25},{9,17},{17,9},{25,1},{2,26},{10... | collective-permute-start | bytes 393224 | tf_op jit(solution)/shard_map/ppermute | solution.py:90
  36.0 0.4 shard_map.122
  36.4 3.3 %collective-permute-start.16 = (bf16[272,256]{1,0:T(8,128)(2,1)S(1)}, bf16[272,256]{1,0:T(8,128)(2,1)S(1)}, u32[]{:S(2)}, u32[]{:S(2)}) collective-permute-start(bf16[272,256]{1,0:T(8,128)(2,1)S(1)} %get-tuple-element.49.held_ref), channel_id=1, source_target_pairs={{0,8},{1,9},{2,10},{3,11},{4,12},{5,13},{6,14},{7,15}} | collective-permute-start | bytes 417800 | tf_op jit(solution)/shard_map/ppermute | solution.py:448
  39.8 0.0 collective-permute-done.12.x_ref
  39.8 0.0 collective-permute-done.9.refs_1_
  39.8 0.0 copy-start.3
  39.8 0.0 collective-permute-done.10.refs_0_.refs_2_
  39.8 1.5 %collective-permute-done.11.refs_1_.refs_3_ = bf16[256,256]{1,0:T(8,128)(2,1)S(1)} collective-permute-done((bf16[256,256]{1,0:T(8,128)(2,1)S(1)}, bf16[256,256]{1,0:T(8,128)(2,1)S(1)}, u32[]{:S(2)}, u32[]{:S(2)}) %collective-permute-start.11) | collective-permute-done | bytes 131104 | tf_op jit(solution)/shard_map/ppermute | solution.py:90
  41.3 0.0 collective-permute-start.13
  41.3 1.0 %collective-permute-done.16.come_ref.refs_0_ = bf16[272,256]{1,0:T(8,128)(2,1)S(1)} collective-permute-done((bf16[272,256]{1,0:T(8,128)(2,1)S(1)}, bf16[272,256]{1,0:T(8,128)(2,1)S(1)}, u32[]{:S(2)}, u32[]{:S(2)}) %collective-permute-start.16) | collective-permute-done | bytes 139296 | tf_op jit(solution)/shard_map/ppermute | solution.py:448
  42.3 3.2 %collective-permute-start.17 = (bf16[272,256]{1,0:T(8,128)(2,1)S(1)}, bf16[272,256]{1,0:T(8,128)(2,1)S(1)}, u32[]{:S(2)}, u32[]{:S(2)}) collective-permute-start(bf16[272,256]{1,0:T(8,128)(2,1)S(1)} %shard_map.128), channel_id=1, source_target_pairs={{0,16},{8,24},{1,17},{9,25},{2,18},{10,26},{3,19},{11,27},{4,20},{... | collective-permute-start | bytes 417800 | tf_op jit(solution)/shard_map/ppermute | solution.py:448
  45.6 0.1 collective-permute-start.14
  45.7 0.5 %collective-permute-start.15 = (bf16[256,256]{1,0:T(8,128)(2,1)S(1)}, bf16[256,256]{1,0:T(8,128)(2,1)S(1)}, u32[]{:S(2)}, u32[]{:S(2)}) collective-permute-start(bf16[256,256]{1,0:T(8,128)(2,1)S(1)} %get-tuple-element.48), channel_id=1, source_target_pairs={{0,1},{1,0},{2,3},{3,2},{4,5},{5,4},{6,7},{7,6},{8,9},{9,8},{10,11... | collective-permute-start | bytes 393224 | tf_op jit(solution)/shard_map/ppermute | solution.py:76
  46.2 1.5 %shard_map.129 = (bf16[2,256,256]{2,1,0:T(8,128)(2,1)}, bf16[2,512,256]{2,1,0:T(8,128)(2,1)}) custom-call(f32[8,128]{1,0:T(8,128)S(1)} %copy-done.2, bf16[256,256]{1,0:T(8,128)(2,1)S(1)} %get-tuple-element.45.refs_4_.after_ref), custom_call_target="tpu_custom_call" | custom-call | flops 1 | bytes 1 | tf_op jit(solution)/shard_map/pallas_call | solution.py:38
  47.7 0.0 copy-done.3
  47.7 0.4 collective-permute-done.17.refs_1_
  48.1 0.0 collective-permute-done.14.ci_ref
  48.1 0.0 collective-permute-done.15.cei_ref
  48.1 0.0 collective-permute-done.13.co_ref
  48.1 0.2 shard_map.130
  (7 shorter events, 0.1 us)
Async XLA Ops:
  0.6 20.4 %collective-permute-start.4 = (bf16[2,1024,512]{2,1,0:T(8,128)(2,1)}, bf16[2,1024,512]{2,1,0:T(8,128)(2,1)S(1)}, u32[]{:S(2)}, u32[]{:S(2)}) collective-permute-start(bf16[2,1024,512]{2,1,0:T(8,128)(2,1)} %three_ref.1), channel_id=1, source_target_pairs={{0,1},{1,0},{2,3},{3,2},{4,5},{5,4},{6,7},{7,6},{8,9},{9,8},{10,11... | collective-permute-start | bytes 6291464 | tf_op jit(solution)/shard_map/ppermute | solution.py:76
  1.1 21.9 %collective-permute-start = (bf16[4,512,256]{2,1,0:T(8,128)(2,1)}, bf16[4,512,256]{2,1,0:T(8,128)(2,1)S(1)}, u32[]{:S(2)}, u32[]{:S(2)}) collective-permute-start(bf16[4,512,256]{2,1,0:T(8,128)(2,1)} %coeff_ref.11), channel_id=1, source_target_pairs={{0,1},{1,0},{2,3},{3,2},{4,5},{5,4},{6,7},{7,6},{8,9},{9,8},{10,11... | collective-permute-start | bytes 3145736 | tf_op jit(solution)/shard_map/ppermute | solution.py:76
  1.2 17.5 %collective-permute-start.1 = (bf16[4,256,256]{2,1,0:T(8,128)(2,1)}, bf16[4,256,256]{2,1,0:T(8,128)(2,1)S(1)}, u32[]{:S(2)}, u32[]{:S(2)}) collective-permute-start(bf16[4,256,256]{2,1,0:T(8,128)(2,1)} %amps_ref.5), channel_id=1, source_target_pairs={{0,1},{1,0},{2,3},{3,2},{4,5},{5,4},{6,7},{7,6},{8,9},{9,8},{10,11... | collective-permute-start | bytes 1572872 | tf_op jit(solution)/shard_map/ppermute | solution.py:76
  3.7 8.4 %collective-permute-start.2 = (bf16[528,128]{1,0:T(8,128)(2,1)}, bf16[528,128]{1,0:T(8,128)(2,1)S(1)}, u32[]{:S(2)}, u32[]{:S(2)}) collective-permute-start(bf16[528,128]{1,0:T(8,128)(2,1)} %get-tuple-element.28), channel_id=1, source_target_pairs={{0,7},{1,2},{2,1},{3,4},{4,3},{5,6},{6,5},{7,0},{8,15},{9,10},{10,... | collective-permute-start | bytes 405512 | tf_op jit(solution)/shard_map/ppermute | solution.py:79
  8.5 7.4 %collective-permute-start.3 = (bf16[512,128]{1,0:T(8,128)(2,1)}, bf16[512,128]{1,0:T(8,128)(2,1)S(1)}, u32[]{:S(2)}, u32[]{:S(2)}) collective-permute-start(bf16[512,128]{1,0:T(8,128)(2,1)} %get-tuple-element.29), channel_id=1, source_target_pairs={{0,7},{1,2},{2,1},{3,4},{4,3},{5,6},{6,5},{7,0},{8,15},{9,10},{10,... | collective-permute-start | bytes 393224 | tf_op jit(solution)/shard_map/ppermute | solution.py:79
  8.6 0.7 %copy-start.2 = (f32[8,128]{1,0:T(8,128)S(1)}, f32[8,128]{1,0:T(8,128)}, u32[]{:S(2)}) copy-start(f32[8,128]{1,0:T(8,128)} %get-tuple-element.27.after_ref.nums) | copy-start | bytes 12292
  10.8 7.0 %copy-start = (bf16[4,512,256]{2,1,0:T(8,128)(2,1)S(1)}, bf16[4,512,256]{2,1,0:T(8,128)(2,1)}, u32[]{:S(2)}) copy-start(bf16[4,512,256]{2,1,0:T(8,128)(2,1)} %coeff_ref.11) | copy-start | bytes 3145732
  10.8 7.0 %copy-start.1 = (bf16[4,256,256]{2,1,0:T(8,128)(2,1)S(1)}, bf16[4,256,256]{2,1,0:T(8,128)(2,1)}, u32[]{:S(2)}) copy-start(bf16[4,256,256]{2,1,0:T(8,128)(2,1)} %amps_ref.5) | copy-start | bytes 1572868
  12.7 8.4 %copy-start.6 = (bf16[528,128]{1,0:T(8,128)(2,1)S(1)}, bf16[528,128]{1,0:T(8,128)(2,1)}, u32[]{:S(2)}) copy-start(bf16[528,128]{1,0:T(8,128)(2,1)} %get-tuple-element.28) | copy-start | bytes 405508
  12.7 19.1 %collective-permute-start.5 = (bf16[1040,128]{1,0:T(8,128)(2,1)S(1)}, bf16[1040,128]{1,0:T(8,128)(2,1)S(1)}, u32[]{:S(2)}, u32[]{:S(2)}) collective-permute-start(bf16[1040,128]{1,0:T(8,128)(2,1)S(1)} %shard_map.115.after_ref), channel_id=1, source_target_pairs={{0,7},{1,2},{2,1},{3,4},{4,3},{5,6},{6,5},{7,0},{8,15},{9,10},{10,... | collective-permute-start | bytes 798728 | tf_op jit(solution)/shard_map/ppermute | solution.py:79
  16.4 15.4 %collective-permute-start.6 = (bf16[1024,128]{1,0:T(8,128)(2,1)S(1)}, bf16[1024,128]{1,0:T(8,128)(2,1)S(1)}, u32[]{:S(2)}, u32[]{:S(2)}) collective-permute-start(bf16[1024,128]{1,0:T(8,128)(2,1)S(1)} %shard_map.116.after_ref), channel_id=1, source_target_pairs={{0,7},{1,2},{2,1},{3,4},{4,3},{5,6},{6,5},{7,0},{8,15},{9,10},{10,... | collective-permute-start | bytes 786440 | tf_op jit(solution)/shard_map/ppermute | solution.py:79
  18.8 6.9 %copy-start.4 = (f32[4,256]{1,0:T(4,128)S(1)}, f32[4,256]{1,0:T(4,128)}, u32[]{:S(2)}) copy-start(f32[4,256]{1,0:T(4,128)} %eps_ref.1) | copy-start | bytes 12292
  18.8 13.0 %collective-permute-start.7 = (bf16[272,256]{1,0:T(8,128)(2,1)S(1)}, bf16[272,256]{1,0:T(8,128)(2,1)S(1)}, u32[]{:S(2)}, u32[]{:S(2)}) collective-permute-start(bf16[272,256]{1,0:T(8,128)(2,1)S(1)} %get-tuple-element.30.after_ref), channel_id=1, source_target_pairs={{0,7},{1,2},{2,1},{3,4},{4,3},{5,6},{6,5},{7,0},{8,15},{9,10},{10,... | collective-permute-start | bytes 417800 | tf_op jit(solution)/shard_map/ppermute | solution.py:79
  21.0 1.4 %copy-start.5 = (bf16[2,1024,512]{2,1,0:T(8,128)(2,1)}, bf16[2,1024,512]{2,1,0:T(8,128)(2,1)S(1)}, u32[]{:S(2)}) copy-start(bf16[2,1024,512]{2,1,0:T(8,128)(2,1)S(1)} %collective-permute-done.4.three_in_ref) | copy-start | bytes 6291460
  21.0 6.1 %collective-permute-start.8 = (bf16[528,128]{1,0:T(8,128)(2,1)S(1)}, bf16[528,128]{1,0:T(8,128)(2,1)S(1)}, u32[]{:S(2)}, u32[]{:S(2)}) collective-permute-start(bf16[528,128]{1,0:T(8,128)(2,1)S(1)} %copy-done.6), channel_id=1, source_target_pairs={{0,1},{1,0},{2,3},{3,2},{4,5},{5,4},{6,7},{7,6},{8,9},{9,8},{10,11... | collective-permute-start | bytes 405512 | tf_op jit(solution)/shard_map/ppermute | solution.py:76
  23.0 16.7 %collective-permute-start.12 = (bf16[512,256]{1,0:T(8,128)(2,1)S(1)}, bf16[512,256]{1,0:T(8,128)(2,1)S(1)}, u32[]{:S(2)}, u32[]{:S(2)}) collective-permute-start(bf16[512,256]{1,0:T(8,128)(2,1)S(1)} %get-tuple-element.44), channel_id=1, source_target_pairs={{0,7},{1,2},{2,1},{3,4},{4,3},{5,6},{6,5},{7,0},{8,15},{9,10},{10,... | collective-permute-start | bytes 786440 | tf_op jit(solution)/shard_map/ppermute | solution.py:79
  32.5 7.3 %collective-permute-start.9 = (bf16[256,256]{1,0:T(8,128)(2,1)S(1)}, bf16[256,256]{1,0:T(8,128)(2,1)S(1)}, u32[]{:S(2)}, u32[]{:S(2)}) collective-permute-start(bf16[256,256]{1,0:T(8,128)(2,1)S(1)} %get-tuple-element.37.amp_ref.after_ref.refs_0_), channel_id=1, source_target_pairs={{0,8},{8,0},{16,24},{24,16},{1,9},{9,1},{17,25},{25,17},{2,10},{10... | collective-permute-start | bytes 393224 | tf_op jit(solution)/shard_map/ppermute | solution.py:90
  33.9 5.9 %collective-permute-start.10 = (bf16[256,256]{1,0:T(8,128)(2,1)S(1)}, bf16[256,256]{1,0:T(8,128)(2,1)S(1)}, u32[]{:S(2)}, u32[]{:S(2)}) collective-permute-start(bf16[256,256]{1,0:T(8,128)(2,1)S(1)} %get-tuple-element.37.amp_ref.after_ref.refs_0_), channel_id=1, source_target_pairs={{0,16},{8,24},{16,0},{24,8},{1,17},{9,25},{17,1},{25,9},{2,18},{10... | collective-permute-start | bytes 393224 | tf_op jit(solution)/shard_map/ppermute | solution.py:90
  35.5 5.9 %collective-permute-start.11 = (bf16[256,256]{1,0:T(8,128)(2,1)S(1)}, bf16[256,256]{1,0:T(8,128)(2,1)S(1)}, u32[]{:S(2)}, u32[]{:S(2)}) collective-permute-start(bf16[256,256]{1,0:T(8,128)(2,1)S(1)} %get-tuple-element.37.amp_ref.after_ref.refs_0_), channel_id=1, source_target_pairs={{0,24},{8,16},{16,8},{24,0},{1,25},{9,17},{17,9},{25,1},{2,26},{10... | collective-permute-start | bytes 393224 | tf_op jit(solution)/shard_map/ppermute | solution.py:90
  36.4 5.9 %collective-permute-start.16 = (bf16[272,256]{1,0:T(8,128)(2,1)S(1)}, bf16[272,256]{1,0:T(8,128)(2,1)S(1)}, u32[]{:S(2)}, u32[]{:S(2)}) collective-permute-start(bf16[272,256]{1,0:T(8,128)(2,1)S(1)} %get-tuple-element.49.held_ref), channel_id=1, source_target_pairs={{0,8},{1,9},{2,10},{3,11},{4,12},{5,13},{6,14},{7,15}} | collective-permute-start | bytes 417800 | tf_op jit(solution)/shard_map/ppermute | solution.py:448
  39.8 7.9 %copy-start.3 = (f32[8,128]{1,0:T(8,128)S(1)}, f32[8,128]{1,0:T(8,128)}, u32[]{:S(2)}) copy-start(f32[8,128]{1,0:T(8,128)} %get-tuple-element.27.after_ref.nums) | copy-start | bytes 12292
  41.3 6.8 %collective-permute-start.13 = (bf16[2,256,256]{2,1,0:T(8,128)(2,1)S(1)}, bf16[2,256,256]{2,1,0:T(8,128)(2,1)S(1)}, u32[]{:S(2)}, u32[]{:S(2)}) collective-permute-start(bf16[2,256,256]{2,1,0:T(8,128)(2,1)S(1)} %shard_map.125.refs_4_), channel_id=1, source_target_pairs={{0,1},{1,0},{2,3},{3,2},{4,5},{5,4},{6,7},{7,6},{8,15},{9,10},{10,... | collective-permute-start | bytes 786440 | tf_op jit(solution)/shard_map/ppermute | solution.py:87
  42.3 5.8 %collective-permute-start.17 = (bf16[272,256]{1,0:T(8,128)(2,1)S(1)}, bf16[272,256]{1,0:T(8,128)(2,1)S(1)}, u32[]{:S(2)}, u32[]{:S(2)}) collective-permute-start(bf16[272,256]{1,0:T(8,128)(2,1)S(1)} %shard_map.128), channel_id=1, source_target_pairs={{0,16},{8,24},{1,17},{9,25},{2,18},{10,26},{3,19},{11,27},{4,20},{... | collective-permute-start | bytes 417800 | tf_op jit(solution)/shard_map/ppermute | solution.py:448
  45.6 2.5 %collective-permute-start.14 = (bf16[256,256]{1,0:T(8,128)(2,1)S(1)}, bf16[256,256]{1,0:T(8,128)(2,1)S(1)}, u32[]{:S(2)}, u32[]{:S(2)}) collective-permute-start(bf16[256,256]{1,0:T(8,128)(2,1)S(1)} %get-tuple-element.45.refs_4_.after_ref), channel_id=1, source_target_pairs={{0,1},{1,0},{2,3},{3,2},{4,5},{5,4},{6,7},{7,6},{8,9},{9,8},{10,11... | collective-permute-start | bytes 393224 | tf_op jit(solution)/shard_map/ppermute | solution.py:76
  45.7 2.5 %collective-permute-start.15 = (bf16[256,256]{1,0:T(8,128)(2,1)S(1)}, bf16[256,256]{1,0:T(8,128)(2,1)S(1)}, u32[]{:S(2)}, u32[]{:S(2)}) collective-permute-start(bf16[256,256]{1,0:T(8,128)(2,1)S(1)} %get-tuple-element.48), channel_id=1, source_target_pairs={{0,1},{1,0},{2,3},{3,2},{4,5},{5,4},{6,7},{7,6},{8,9},{9,8},{10,11... | collective-permute-start | bytes 393224 | tf_op jit(solution)/shard_map/ppermute | solution.py:76
